TPU v7x, 32 devices: a whole 2x2x4 slice. The times are simulated.
32 devices in a mesh: groups: 2 (over y), seq: 4 (over z), head: 4 (over x, core).
Axes of the slice: x: 2, y: 2, z: 4, core: 2. Of those that a mesh axis runs over, the one named last changes fastest.
Arguments:
- tokens: bfloat16 [8192, 1024], P(('groups', 'seq')), parts along dimension 0, may hold values from -16 to 16
- w_query: bfloat16 [1024, 1024], P(None, 'head'), may hold values from -0.1875 to 0.1875
- w_key: bfloat16 [1024, 1024], P(None, 'head'), may hold values from -0.1875 to 0.1875
- w_value: bfloat16 [1024, 1024], P(None, 'head'), may hold values from -0.1875 to 0.1875
- w_out: bfloat16 [1024, 1024], P(None, 'head'), may hold values from -0.1875 to 0.1875
- cotangent: bfloat16 [8192, 1024], P(('groups', 'seq')), parts along dimension 0, may hold values from -6 to 6
Outputs:
- mixed: bfloat16 [8192, 1024], P(('groups', 'seq'), 'head'), parts along dimension 0
- tokens_grad: bfloat16 [8192, 1024], P(('groups', 'seq'), 'head'), parts along dimension 0
- query_grad: bfloat16 [2048, 1024], P('groups', 'head'), parts along dimension 0
- key_grad: bfloat16 [2048, 1024], P('groups', 'head'), parts along dimension 0
- value_grad: bfloat16 [2048, 1024], P('groups', 'head'), parts along dimension 0
- out_grad: bfloat16 [2048, 1024], P('groups', 'head'), parts along dimension 0
There are 2 independent parts, one for each index of `groups`. A program takes and returns all parts, laid end to end along the dimension named above; an argument that names none is the same for every part. Nothing has to cross between parts.
All inputs are finite; a program needn't handle non-finite values.
Results may differ from a plain program's by a relative error of at most 0.024.
The roundings to bfloat16 on the way count: a program that leaves them out, or rounds other values in their place, can miss the bound.
Values may be sent and summed in bfloat16 or wider, within the bound.
No kernel may reach another device: no remote copies, remote signals or barrier semaphores. Data moves between devices by JAX's collectives and lax.ppermute only.
A program may use at most 64 MiB of HBM per device.

v0:
```python
import math

import jax
import jax.numpy as jnp
from jax import lax
from jax.sharding import PartitionSpec as P

HEAD_DIM = 128
BLOCK = 128


def partner(block, axis, bit):
    count = lax.axis_size(axis)
    route = []
    for low in range(count):
        high = low | 1 << bit
        if high != low and high < count:
            route += [(low, high), (high, low)]
    return lax.ppermute(block, axis, route)


def coarsen(values):
    wide = values.astype(jnp.float32)
    paired = wide.reshape(wide.shape[:-2] + (wide.shape[-2] // 2, 2, wide.shape[-1]))
    return ((paired[..., 0, :] + paired[..., 1, :]) * 0.5).astype(jnp.bfloat16)


def spread(grads):
    return jnp.repeat(grads, 2, axis=-2) * 0.5


def sibling_blocks(level, block_rows, reach):
    head_count, level_rows, head_width = level.shape
    segments = level_rows // block_rows
    flipped = level.reshape(head_count, segments // 2, 2, block_rows, head_width)[:, :, ::-1]
    flipped = flipped.reshape(head_count, segments, block_rows, head_width)
    return jnp.repeat(flipped, reach, axis=1)


def fold_back(grads, reach):
    head_count, blocks, block_rows, head_width = grads.shape
    segments = blocks // reach
    summed = grads.reshape(head_count, segments, reach, block_rows, head_width).sum(axis=2)
    summed = summed.reshape(head_count, segments // 2, 2, block_rows, head_width)[:, :, ::-1]
    return summed.reshape(head_count, segments * block_rows, head_width)


def ordered(mine, other, my_bit):
    first = jnp.where(my_bit == 0, mine, other)
    second = jnp.where(my_bit == 0, other, mine)
    return jnp.concatenate([first, second], axis=1)


def split_half(grads, my_bit, block_rows):
    first = grads[:, :block_rows]
    second = grads[:, block_rows:]
    return (jnp.where(my_bit == 0, first, second), jnp.where(my_bit == 0, second, first))


def project(left, weight):
    return lax.dot_general(
        left, weight, (((1,), (1,)), ((), ())), preferred_element_type=jnp.float32
    )


def contract_rows(left, right):
    return lax.dot_general(
        left, right, (((0,), (0,)), ((), ())), preferred_element_type=jnp.float32
    )


def per_device(tokens, w_query, w_key, w_value, w_out, cotangent):
    tok_rows = tokens.shape[0]
    inner_width = w_query.shape[1]
    head_count = inner_width // HEAD_DIM
    block_rows = BLOCK
    blocks = tok_rows // block_rows
    local_levels = blocks.bit_length() - 1
    seq_bits = lax.axis_size("seq").bit_length() - 1
    position = lax.axis_index("seq")
    score_scale = 1.0 / math.sqrt(HEAD_DIM)

    def heads_of(matrix):
        return matrix.reshape(tok_rows, head_count, HEAD_DIM).transpose(1, 0, 2)

    def flatten(stack):
        return (
            stack.reshape(head_count, tok_rows, HEAD_DIM)
            .transpose(1, 0, 2)
            .reshape(tok_rows, inner_width)
        )

    query = heads_of(
        jnp.dot(tokens, w_query, preferred_element_type=jnp.float32).astype(jnp.bfloat16)
    )
    key_heads = heads_of(
        jnp.dot(tokens, w_key, preferred_element_type=jnp.float32).astype(jnp.bfloat16)
    )
    value_heads = heads_of(
        jnp.dot(tokens, w_value, preferred_element_type=jnp.float32).astype(jnp.bfloat16)
    )
    key_levels = [key_heads]
    value_levels = [value_heads]
    for level_index in range(local_levels):
        key_levels.append(coarsen(key_levels[-1]))
        value_levels.append(coarsen(value_levels[-1]))
    own_key = key_levels[-1]
    own_value = value_levels[-1]
    far_keys = []
    far_values = []
    for bit_index in range(seq_bits):
        sib_key, sib_value = partner((own_key, own_value), "seq", bit_index)
        far_keys.append(sib_key)
        far_values.append(sib_value)
        if bit_index + 1 < seq_bits:
            my_bit = jnp.bitwise_and(jnp.right_shift(position, bit_index), 1)
            own_key = coarsen(ordered(own_key, sib_key, my_bit))
            own_value = coarsen(ordered(own_value, sib_value, my_bit))
    near_key = jnp.concatenate(
        [key_heads.reshape(head_count, blocks, block_rows, HEAD_DIM)]
        + [sibling_blocks(key_levels[i], block_rows, 2**i) for i in range(local_levels)],
        axis=2,
    )
    near_value = jnp.concatenate(
        [value_heads.reshape(head_count, blocks, block_rows, HEAD_DIM)]
        + [sibling_blocks(value_levels[i], block_rows, 2**i) for i in range(local_levels)],
        axis=2,
    )
    far_key = jnp.concatenate(far_keys, axis=1)
    far_value = jnp.concatenate(far_values, axis=1)
    bias_near = jnp.concatenate(
        [jnp.zeros((block_rows,), jnp.float32)]
        + [jnp.full((block_rows,), i * math.log(2.0), jnp.float32) for i in range(local_levels)]
    )
    bias_far = jnp.concatenate(
        [
            jnp.full((block_rows,), (local_levels + i) * math.log(2.0), jnp.float32)
            for i in range(seq_bits)
        ]
    )
    q_blocks = query.reshape(head_count, blocks, block_rows, HEAD_DIM)
    score_near = (
        jnp.einsum("hnqd,hnkd->hnqk", q_blocks, near_key, preferred_element_type=jnp.float32)
        * score_scale
        + bias_near
    )
    score_far = (
        jnp.einsum("hnqd,hkd->hnqk", q_blocks, far_key, preferred_element_type=jnp.float32)
        * score_scale
        + bias_far
    )
    row_max = jnp.maximum(jnp.max(score_near, axis=-1), jnp.max(score_far, axis=-1))[..., None]
    expo_near = jnp.exp(score_near - row_max)
    expo_far = jnp.exp(score_far - row_max)
    denominator = (jnp.sum(expo_near, axis=-1) + jnp.sum(expo_far, axis=-1))[..., None]
    prob_near = expo_near / denominator
    prob_far = expo_far / denominator
    probs_near_b = prob_near.astype(jnp.bfloat16)
    probs_far_b = prob_far.astype(jnp.bfloat16)
    attended = (
        jnp.einsum("hnqk,hnkd->hnqd", probs_near_b, near_value, preferred_element_type=jnp.float32)
        + jnp.einsum("hnqk,hkd->hnqd", probs_far_b, far_value, preferred_element_type=jnp.float32)
    ).astype(jnp.bfloat16)
    attended_flat = flatten(attended)
    mixed_part = project(attended_flat, w_out)
    mixed = lax.psum_scatter(
        mixed_part.astype(jnp.bfloat16), "head", scatter_dimension=1, tiled=True
    )
    grad_flat = jnp.dot(cotangent, w_out, preferred_element_type=jnp.float32).astype(jnp.bfloat16)
    out_term = contract_rows(cotangent, attended_flat)
    g_blocks = heads_of(grad_flat).reshape(head_count, blocks, block_rows, HEAD_DIM)
    row_delta = jnp.sum(g_blocks.astype(jnp.float32) * attended.astype(jnp.float32), axis=-1)[
        ..., None
    ]
    dprob_near = jnp.einsum(
        "hnqd,hnkd->hnqk", g_blocks, near_value, preferred_element_type=jnp.float32
    )
    dprob_far = jnp.einsum(
        "hnqd,hkd->hnqk", g_blocks, far_value, preferred_element_type=jnp.float32
    )
    grads_near = (prob_near * (dprob_near - row_delta) * score_scale).astype(jnp.bfloat16)
    grads_far = (prob_far * (dprob_far - row_delta) * score_scale).astype(jnp.bfloat16)
    dquery = (
        jnp.einsum("hnqk,hnkd->hnqd", grads_near, near_key, preferred_element_type=jnp.float32)
        + jnp.einsum("hnqk,hkd->hnqd", grads_far, far_key, preferred_element_type=jnp.float32)
    ).astype(jnp.bfloat16)
    dkey_near = jnp.einsum(
        "hnqk,hnqd->hnkd", grads_near, q_blocks, preferred_element_type=jnp.float32
    )
    dkey_far = jnp.einsum("hnqk,hnqd->hkd", grads_far, q_blocks, preferred_element_type=jnp.float32)
    dvalue_near = jnp.einsum(
        "hnqk,hnqd->hnkd", probs_near_b, g_blocks, preferred_element_type=jnp.float32
    )
    dvalue_far = jnp.einsum(
        "hnqk,hnqd->hkd", probs_far_b, g_blocks, preferred_element_type=jnp.float32
    )
    upper_key = None
    upper_value = None
    for bit_index in reversed(range(seq_bits)):
        low = bit_index * block_rows
        carry_key = dkey_far[:, low : low + block_rows]
        carry_value = dvalue_far[:, low : low + block_rows]
        my_bit = jnp.bitwise_and(jnp.right_shift(position, bit_index), 1)
        if upper_key is not None:
            own_part_key, sib_part_key = split_half(spread(upper_key), my_bit, block_rows)
            own_part_value, sib_part_value = split_half(spread(upper_value), my_bit, block_rows)
            carry_key = carry_key + sib_part_key
            carry_value = carry_value + sib_part_value
        back_key, back_value = (
            partner(carry_key.astype(jnp.bfloat16), "seq", bit_index).astype(carry_key.dtype),
            partner(carry_value.astype(jnp.bfloat16), "seq", bit_index).astype(carry_value.dtype),
        )
        if upper_key is not None:
            back_key = back_key + own_part_key
            back_value = back_value + own_part_value
        upper_key, upper_value = (back_key, back_value)
    for level_index in reversed(range(local_levels)):
        low = (level_index + 1) * block_rows
        upper_key = fold_back(dkey_near[:, :, low : low + block_rows], 2**level_index) + spread(
            upper_key
        )
        upper_value = fold_back(
            dvalue_near[:, :, low : low + block_rows], 2**level_index
        ) + spread(upper_value)
    dkey = (
        dkey_near[:, :, :block_rows].reshape(head_count, tok_rows, HEAD_DIM) + upper_key
    ).astype(jnp.bfloat16)
    dvalue = (
        dvalue_near[:, :, :block_rows].reshape(head_count, tok_rows, HEAD_DIM) + upper_value
    ).astype(jnp.bfloat16)
    dquery_flat = flatten(dquery)
    dkey_flat = flatten(dkey)
    dvalue_flat = flatten(dvalue)
    grad_part = (
        project(dquery_flat, w_query) + project(dkey_flat, w_key) + project(dvalue_flat, w_value)
    )
    tokens_grad = lax.psum_scatter(
        grad_part.astype(jnp.bfloat16), "head", scatter_dimension=1, tiled=True
    )
    query_term = contract_rows(tokens, dquery_flat)
    key_term = contract_rows(tokens, dkey_flat)
    value_term = contract_rows(tokens, dvalue_flat)
    query_sum, key_sum, value_sum, out_sum = (
        lax.psum(query_term.astype(jnp.bfloat16), "seq").astype(jnp.float32),
        lax.psum(key_term.astype(jnp.bfloat16), "seq").astype(jnp.float32),
        lax.psum(value_term.astype(jnp.bfloat16), "seq").astype(jnp.float32),
        lax.psum(out_term.astype(jnp.bfloat16), "seq").astype(jnp.float32),
    )
    return (
        mixed,
        tokens_grad,
        query_sum.astype(jnp.bfloat16),
        key_sum.astype(jnp.bfloat16),
        value_sum.astype(jnp.bfloat16),
        out_sum.astype(jnp.bfloat16),
    )


def solution(mesh):
    return jax.shard_map(
        per_device,
        mesh=mesh,
        in_specs=(
            P(("groups", "seq"), None),
            P(None, "head"),
            P(None, "head"),
            P(None, "head"),
            P(None, "head"),
            P(("groups", "seq"), None),
        ),
        out_specs=(
            P(("groups", "seq"), "head"),
            P(("groups", "seq"), "head"),
            P("groups", "head"),
            P("groups", "head"),
            P("groups", "head"),
            P("groups", "head"),
        ),
        check_vma=False,
    )
```

profile of v0, /device:TPU:0, one launch (start us, length us, event | category | flops | bytes accessed | tf_op | source)
XLA Modules:
  0.0 227.5 jit_solution(3100217319720804188)
XLA Ops:
  8.1 1.5 copy-done
  9.6 1.8 convolution_convert_fusion.6
  12.1 1.6 fusion.61
  14.3 3.1 %collective-permute-start.2 = (bf16[2,128,128]{2,1,0:T(8,128)(2,1)S(1)}, bf16[2,128,128]{2,1,0:T(8,128)(2,1)}, u32[]{:S(2)}, u32[]{:S(2)}) collective-permute-start(bf16[2,128,128]{2,1,0:T(8,128)(2,1)S(1)} %fusion.41), channel_id=1, source_target_pairs={{0,4},{4,0},{8,12},{12,8},{1,5},{5,1},{9,13},{13,9},{2,6},{6,2},{1... | collective-permute-start | bytes 196616 | tf_op jit(solution)/shard_map/ppermute | solution.py:19
  17.4 1.6 convolution_convert_fusion.7
  19.0 1.3 copy.63
  20.7 1.6 fusion.59
  24.3 2.6 %convolution_convert_fusion.8 = bf16[1024,256]{0,1:T(8,128)(2,1)} fusion(bf16[1024,1024]{1,0:T(8,128)(2,1)S(1)} %copy-done, bf16[1024,256]{1,0:T(8,128)(2,1)} %param.7), kind=kOutput, calls=%fused_computation.25 | convolution fusion | flops 537133056 | bytes 3145728 | tf_op jit(solution)/shard_map/dot_general | solution.py:94
  26.9 1.3 copy.62
  28.2 1.9 rev.32
  31.0 3.2 %convolution_convert_fusion.5 = bf16[1024,256]{0,1:T(8,128)(2,1)} fusion(bf16[1024,1024]{1,0:T(8,128)(2,1)} %param.11, bf16[1024,256]{1,0:T(8,128)(2,1)} %param.10), kind=kOutput, calls=%fused_computation.22 | convolution fusion | flops 537133056 | bytes 3145728 | tf_op jit(solution)/shard_map/dot_general | solution.py:169
  34.2 2.0 copy.74
  36.9 1.8 copy.96
  41.3 1.8 copy.94
  43.1 1.7 rev.33
  46.8 2.3 %fusion = (f32[2,8,128]{2,1,0:T(8,128)S(1)}, f32[2,8,128,512]{3,2,1,0:T(8,128)S(1)}) fusion(f32[512]{0:T(512)S(1)} %copy-done.29, bf16[2,8,128,128]{3,2,1,0:T(8,128)(2,1)S(1)} %bitcast.192, bf16[2,8,128,128]{3,2,1,0:T(8,128)(2,1)S(1)} %bitcast.243, bf16[2,8,128,128]{3,2,1,0:T(8,128)(2,1)S(1)} %bitcast.249, bf16[2,8,128,128]{3,2,1,0:T(8,128)(2,1)} %bitcast.258, ...), kind=kOutput, calls=%fused_computation.4 | convolution fusion | flops 279967744 | bytes 6825984 | tf_op jit(solution)/shard_map/hnqd,hnkd->hnqk/dot_general | solution.py:143
  51.3 3.1 %collective-permute-start.1 = (bf16[2,128,128]{2,1,0:T(8,128)(2,1)S(1)}, bf16[2,128,128]{2,1,0:T(8,128)(2,1)S(1)}, u32[]{:S(2)}, u32[]{:S(2)}) collective-permute-start(bf16[2,128,128]{2,1,0:T(8,128)(2,1)S(1)} %fusion.40), channel_id=1, source_target_pairs={{0,8},{8,0},{4,12},{12,4},{1,9},{9,1},{5,13},{13,5},{2,10},{10,2},... | collective-permute-start | bytes 196616 | tf_op jit(solution)/shard_map/ppermute | solution.py:19
  54.5 2.5 %collective-permute-done.1 = bf16[2,128,128]{2,1,0:T(8,128)(2,1)S(1)} collective-permute-done((bf16[2,128,128]{2,1,0:T(8,128)(2,1)S(1)}, bf16[2,128,128]{2,1,0:T(8,128)(2,1)S(1)}, u32[]{:S(2)}, u32[]{:S(2)}) %collective-permute-start.1) | collective-permute-done | bytes 65568 | tf_op jit(solution)/shard_map/ppermute | solution.py:19
  58.4 1.2 fusion.2
  59.6 3.4 %fusion.16 = f32[2,8,512,128]{3,2,1,0:T(8,128)} fusion(bf16[2,8,128,128]{3,2,1,0:T(8,128)(2,1)S(1)} %bitcast.253, f32[2,8,128,512]{3,2,1,0:T(8,128)S(1)} %get-tuple-element.57, f32[2,8,128]{2,1,0:T(8,128)S(1)} %add.147, f32[2,8,128]{2,1,0:T(8,128)S(1)} %max.7, f32[512]{0:T(512)S(1)} %copy-done.29), kind=kOutput, calls=%fused_computation.41 | convolution fusion | flops 273678336 | bytes 8931328 | tf_op jit(solution)/shard_map/hnqk,hnqd->hnkd/dot_general | solution.py:191
  63.3 1.3 fusion.18
  64.6 1.2 convolution_bitcast_fusion
  65.8 2.9 %multiply_reduce_fusion = (f32[2,8,128]{2,1,0:T(8,128)S(1)}, bf16[2,8,128,128]{3,2,1,0:T(8,128)(2,1)}) fusion(bf16[2,8,128,128]{3,2,1,0:T(8,128)(2,1)S(1)} %bitcast.255, f32[2,8,128,128]{3,2,1,0:T(8,128)S(1)} %fusion.18, bf16[2,128,128]{2,1,0:T(8,128)(2,1)S(1)} %collective-permute-done.3, bf16[2,128,128]{2,1,0:T(8,128)(2,1)} %collective-permute-done.2, ...), kind=kOutput, calls=%fused_computation.40 | convolution fusion | flops 138672128 | bytes 4350976 | tf_op jit(solution)/shard_map/hnqk,hkd->hnqd/dot_general | solution.py:162
  68.7 1.9 multiply_convert_fusion
  71.6 2.7 %fusion.70 = f32[2,8,512,128]{3,2,1,0:T(8,128)} fusion(bf16[2,8,128,512]{3,2,1,0:T(8,128)(2,1)S(1)} %multiply_convert_fusion, bf16[2,8,128,128]{3,2,1,0:T(8,128)(2,1)S(1)} %bitcast.194), kind=kOutput, calls=%fused_computation.117 | convolution fusion | flops 268435456 | bytes 6815744 | tf_op jit(solution)/shard_map/hnqk,hnqd->hnkd/dot_general | solution.py:187
  75.0 2.6 %collective-permute-start.6 = (bf16[2,128,128]{2,1,0:T(8,128)(2,1)}, bf16[2,128,128]{2,1,0:T(8,128)(2,1)S(1)}, u32[]{:S(2)}, u32[]{:S(2)}) collective-permute-start(bf16[2,128,128]{2,1,0:T(8,128)(2,1)} %slice.210), channel_id=1, source_target_pairs={{0,8},{8,0},{4,12},{12,4},{1,9},{9,1},{5,13},{13,5},{2,10},{10,2},... | collective-permute-start | bytes 196616 | tf_op jit(solution)/shard_map/ppermute | solution.py:19
  77.5 2.2 multiply_convert_fusion.1
  82.7 4.1 %fusion.63 = (f32[2,8,128,128]{3,2,1,0:T(8,128)}, f32[2,8,128,128]{3,2,1,0:T(8,128)}, f32[2,8,128,128]{3,2,1,0:T(8,128)}, f32[2,8,128,128]{3,2,1,0:T(8,128)S(1)}) fusion(f32[2,8,512,128]{3,2,1,0:T(8,128)} %fusion.16), kind=kLoop, calls=%fused_computation.110 | loop fusion | bytes 8388608 | tf_op jit(solution)/shard_map/slice | solution.py:229
  87.8 1.5 fusion.11
  89.3 2.0 fusion.64
  91.4 1.5 fusion.8
  92.9 1.3 reduce_sum.77
  94.9 2.1 reduce_sum.76
  97.1 1.9 rev.41
  100.0 1.3 reduce_sum.75
  101.3 1.3 reduce_sum.74
  104.2 1.3 rev.38
  105.7 3.3 %collective-permute-start.7 = (bf16[2,128,128]{2,1,0:T(8,128)(2,1)S(1)}, bf16[2,128,128]{2,1,0:T(8,128)(2,1)S(1)}, u32[]{:S(2)}, u32[]{:S(2)}) collective-permute-start(bf16[2,128,128]{2,1,0:T(8,128)(2,1)S(1)} %fusion.36), channel_id=1, source_target_pairs={{0,4},{4,0},{8,12},{12,8},{1,5},{5,1},{9,13},{13,9},{2,6},{6,2},{1... | collective-permute-start | bytes 196616 | tf_op jit(solution)/shard_map/ppermute | solution.py:19
  113.9 2.0 copy.81
  115.9 2.6 %fusion.10 = bf16[1024,256]{0,1:T(8,128)(2,1)} fusion(bf16[1024,256]{0,1:T(8,128)(2,1)} %bitcast.218, bf16[1024,1024]{1,0:T(8,128)(2,1)S(1)} %copy-done), kind=kOutput, calls=%fused_computation.30 | convolution fusion | flops 537133056 | bytes 3145728 | tf_op jit(solution)/shard_map/dot_general | solution.py:67
  120.9 1.2 copy.78
  122.2 1.5 fusion.9
  123.8 3.4 %convolution_convert_fusion = bf16[1024,1024]{1,0:T(8,128)(2,1)} fusion(bf16[1024,256]{0,1:T(8,128)(2,1)} %bitcast.228, bf16[1024,256]{1,0:T(8,128)(2,1)} %param.10), kind=kOutput, calls=%fused_computation.12 | convolution fusion | flops 537919488 | bytes 3145728 | tf_op jit(solution)/shard_map/dot_general | solution.py:61
  127.2 1.9 fusion.69
  130.3 2.1 add_convert_fusion
  132.4 81.5 %all-reduce.3.cloned.1.call-done = (bf16[1024,256]{0,1:T(8,128)(2,1)}, bf16[1024,256]{0,1:T(8,128)(2,1)}, bf16[1024,256]{0,1:T(8,128)(2,1)}, bf16[1024,256]{0,1:T(8,128)(2,1)}) async-done(((bf16[1024,256]{0,1:T(8,128)(2,1)}, bf16[1024,256]{0,1:T(8,128)(2,1)}, bf16[1024,256]{0,1:T(8,128)(2,1)}, bf16[1024,256]{0,1:T(8,128)(2,1)}), (bf16[1024,256]{0,1:T(8,128)(2,1)}, bf16[1024,256]{0,1:T(8,128)(2,1)}, ...) | async-done | bytes 2097168 | tf_op jit(solution)/shard_map/psum | solution.py:244
  213.9 2.1 copy.82
  216.0 2.0 copy.83
  (145 shorter events, 33.2 us)
Async XLA Ops:
  8.0 1.6 copy-start
  8.0 205.9 %all-reduce.3.cloned.1.call-start = ((), (), s32[]{:S(2)}) async-start(), calls=%async_computation.4 | async-start | bytes 4194304 | tf_op jit(solution)/shard_map/psum | solution.py:244
  12.0 5.4 %copy-start.16 = (bf16[1024,256]{1,0:T(8,128)(2,1)S(1)}, bf16[1024,256]{1,0:T(8,128)(2,1)}, u32[]{:S(2)}) copy-start(bf16[1024,256]{1,0:T(8,128)(2,1)} %param.8) | copy-start | bytes 1572868
  14.3 34.8 %collective-permute-start.2 = (bf16[2,128,128]{2,1,0:T(8,128)(2,1)S(1)}, bf16[2,128,128]{2,1,0:T(8,128)(2,1)}, u32[]{:S(2)}, u32[]{:S(2)}) collective-permute-start(bf16[2,128,128]{2,1,0:T(8,128)(2,1)S(1)} %fusion.41), channel_id=1, source_target_pairs={{0,4},{4,0},{8,12},{12,8},{1,5},{5,1},{9,13},{13,9},{2,6},{6,2},{1... | collective-permute-start | bytes 196616 | tf_op jit(solution)/shard_map/ppermute | solution.py:19
  20.3 3.1 %copy-start.2 = (bf16[1024,2,128]{2,0,1:T(8,128)(2,1)}, bf16[1024,2,128]{2,0,1:T(8,128)(2,1)S(1)}, u32[]{:S(2)}) copy-start(bf16[1024,2,128]{2,0,1:T(8,128)(2,1)S(1)} %copy.63) | copy-start | bytes 1572868
  24.3 25.9 %collective-permute-start = (bf16[2,128,128]{2,1,0:T(8,128)(2,1)}, bf16[2,128,128]{2,1,0:T(8,128)(2,1)S(1)}, u32[]{:S(2)}, u32[]{:S(2)}) collective-permute-start(bf16[2,128,128]{2,1,0:T(8,128)(2,1)} %fusion.39), channel_id=1, source_target_pairs={{0,4},{4,0},{8,12},{12,8},{1,5},{5,1},{9,13},{13,9},{2,6},{6,2},{1... | collective-permute-start | bytes 196616 | tf_op jit(solution)/shard_map/ppermute | solution.py:19
  38.7 8.1 %copy-start.29 = (f32[512]{0:T(512)S(1)}, f32[512]{0:T(512)}, u32[]{:S(2)}) copy-start(f32[512]{0:T(512)} %constant.12.clone.1) | copy-start | bytes 6148
  46.8 2.3 %copy-start.19 = (bf16[2,256,1,128]{3,1,2,0:T(8,128)(2,1)S(1)}, bf16[2,256,1,128]{3,1,2,0:T(8,128)(2,1)}, u32[]{:S(2)}) copy-start(bf16[2,256,1,128]{3,1,2,0:T(8,128)(2,1)} %copy.97) | copy-start | bytes 393220
  49.1 7.9 %copy-start.28 = (f32[256]{0:T(256)S(1)}, f32[256]{0:T(256)}, u32[]{:S(2)}) copy-start(f32[256]{0:T(256)} %constant.9.clone.1) | copy-start | bytes 3076
  51.3 5.7 %collective-permute-start.1 = (bf16[2,128,128]{2,1,0:T(8,128)(2,1)S(1)}, bf16[2,128,128]{2,1,0:T(8,128)(2,1)S(1)}, u32[]{:S(2)}, u32[]{:S(2)}) collective-permute-start(bf16[2,128,128]{2,1,0:T(8,128)(2,1)S(1)} %fusion.40), channel_id=1, source_target_pairs={{0,8},{8,0},{4,12},{12,4},{1,9},{9,1},{5,13},{13,5},{2,10},{10,2},... | collective-permute-start | bytes 196616 | tf_op jit(solution)/shard_map/ppermute | solution.py:19
  54.4 11.4 %collective-permute-start.3 = (bf16[2,128,128]{2,1,0:T(8,128)(2,1)S(1)}, bf16[2,128,128]{2,1,0:T(8,128)(2,1)S(1)}, u32[]{:S(2)}, u32[]{:S(2)}) collective-permute-start(bf16[2,128,128]{2,1,0:T(8,128)(2,1)S(1)} %fusion.42), channel_id=1, source_target_pairs={{0,8},{8,0},{4,12},{12,4},{1,9},{9,1},{5,13},{13,5},{2,10},{10,2},... | collective-permute-start | bytes 196616 | tf_op jit(solution)/shard_map/ppermute | solution.py:19
  58.4 1.2 copy-start.20
  59.6 3.7 %copy-start.22 = (bf16[2,4,2,128,128]{4,3,2,1,0:T(8,128)(2,1)S(1)}, bf16[2,4,2,128,128]{4,3,2,1,0:T(8,128)(2,1)}, u32[]{:S(2)}) copy-start(bf16[2,4,2,128,128]{4,3,2,1,0:T(8,128)(2,1)} %rev.35) | copy-start | bytes 1572868
  65.8 8.5 %copy-start.26 = (f32[2,256,128]{2,1,0:T(8,128)}, f32[2,256,128]{2,1,0:T(8,128)S(1)}, u32[]{:S(2)}) copy-start(f32[2,256,128]{2,1,0:T(8,128)S(1)} %convolution_bitcast_fusion) | copy-start | bytes 786436
  68.7 2.0 copy-start.3
  68.7 2.0 copy-start.21
  75.0 30.6 %collective-permute-start.6 = (bf16[2,128,128]{2,1,0:T(8,128)(2,1)}, bf16[2,128,128]{2,1,0:T(8,128)(2,1)S(1)}, u32[]{:S(2)}, u32[]{:S(2)}) collective-permute-start(bf16[2,128,128]{2,1,0:T(8,128)(2,1)} %slice.210), channel_id=1, source_target_pairs={{0,8},{8,0},{4,12},{12,4},{1,9},{9,1},{5,13},{13,5},{2,10},{10,2},... | collective-permute-start | bytes 196616 | tf_op jit(solution)/shard_map/ppermute | solution.py:19
  80.2 6.6 %copy-start.15 = (f32[2,256,128]{2,1,0:T(8,128)}, f32[2,256,128]{2,1,0:T(8,128)S(1)}, u32[]{:S(2)}) copy-start(f32[2,256,128]{2,1,0:T(8,128)S(1)} %convolution_bitcast_fusion.1) | copy-start | bytes 786436
  80.2 1.5 copy-start.25
  82.7 5.1 %copy-start.12 = (bf16[2,1024,128]{1,2,0:T(8,128)(2,1)S(1)}, bf16[2,1024,128]{1,2,0:T(8,128)(2,1)}, u32[]{:S(2)}) copy-start(bf16[2,1024,128]{1,2,0:T(8,128)(2,1)} %copy.73) | copy-start | bytes 1572868
  82.7 5.1 %copy-start.30 = (bf16[1024,1024]{1,0:T(8,128)(2,1)S(1)}, bf16[1024,1024]{1,0:T(8,128)(2,1)}, u32[]{:S(2)}) copy-start(bf16[1024,1024]{1,0:T(8,128)(2,1)} %param.11) | copy-start | bytes 6291460
  82.7 6.6 %copy-start.1 = (f32[2,8,512,128]{3,2,1,0:T(8,128)S(1)}, f32[2,8,512,128]{3,2,1,0:T(8,128)}, u32[]{:S(2)}) copy-start(f32[2,8,512,128]{3,2,1,0:T(8,128)} %fusion.70) | copy-start | bytes 12582916
  87.5 21.5 %collective-permute-start.4 = (bf16[2,128,128]{2,1,0:T(8,128)(2,1)}, bf16[2,128,128]{2,1,0:T(8,128)(2,1)S(1)}, u32[]{:S(2)}, u32[]{:S(2)}) collective-permute-start(bf16[2,128,128]{2,1,0:T(8,128)(2,1)} %slice.211), channel_id=1, source_target_pairs={{0,8},{8,0},{4,12},{12,4},{1,9},{9,1},{5,13},{13,5},{2,10},{10,2},... | collective-permute-start | bytes 196616 | tf_op jit(solution)/shard_map/ppermute | solution.py:19
  89.3 2.1 copy-start.7
  102.7 3.0 %copy-start.27 = (f32[2,256,128]{2,1,0:T(8,128)S(1)}, f32[2,256,128]{2,1,0:T(8,128)}, u32[]{:S(2)}) copy-start(f32[2,256,128]{2,1,0:T(8,128)} %copy-done.26) | copy-start | bytes 786436
  105.5 5.8 %copy-start.14 = (f32[2,2,128,128]{3,2,1,0:T(8,128)S(1)}, f32[2,2,128,128]{3,2,1,0:T(8,128)}, u32[]{:S(2)}) copy-start(f32[2,2,128,128]{3,2,1,0:T(8,128)} %reverse.7) | copy-start | bytes 786436
  105.6 6.1 %copy-start.11 = (f32[2,2,2,128,128]{4,3,2,1,0:T(8,128)S(1)}, f32[2,2,2,128,128]{4,3,2,1,0:T(8,128)}, u32[]{:S(2)}) copy-start(f32[2,2,2,128,128]{4,3,2,1,0:T(8,128)} %rev.41) | copy-start | bytes 1572868
  105.7 5.5 %collective-permute-start.7 = (bf16[2,128,128]{2,1,0:T(8,128)(2,1)S(1)}, bf16[2,128,128]{2,1,0:T(8,128)(2,1)S(1)}, u32[]{:S(2)}, u32[]{:S(2)}) collective-permute-start(bf16[2,128,128]{2,1,0:T(8,128)(2,1)S(1)} %fusion.36), channel_id=1, source_target_pairs={{0,4},{4,0},{8,12},{12,8},{1,5},{5,1},{9,13},{13,9},{2,6},{6,2},{1... | collective-permute-start | bytes 196616 | tf_op jit(solution)/shard_map/ppermute | solution.py:19
  110.0 8.5 %collective-permute-start.5 = (bf16[2,128,128]{2,1,0:T(8,128)(2,1)S(1)}, bf16[2,128,128]{2,1,0:T(8,128)(2,1)S(1)}, u32[]{:S(2)}, u32[]{:S(2)}) collective-permute-start(bf16[2,128,128]{2,1,0:T(8,128)(2,1)S(1)} %fusion.37), channel_id=1, source_target_pairs={{0,4},{4,0},{8,12},{12,8},{1,5},{5,1},{9,13},{13,9},{2,6},{6,2},{1... | collective-permute-start | bytes 196616 | tf_op jit(solution)/shard_map/ppermute | solution.py:19
  111.4 1.2 copy-start.4
  111.4 1.5 copy-start.6
  115.9 2.8 %copy-start.13 = (f32[2,2,128,128]{3,2,1,0:T(8,128)S(1)}, f32[2,2,128,128]{3,2,1,0:T(8,128)}, u32[]{:S(2)}) copy-start(f32[2,2,128,128]{3,2,1,0:T(8,128)} %reverse.6) | copy-start | bytes 786436
  115.9 3.0 %copy-start.9 = (f32[2,2,2,128,128]{4,3,2,1,0:T(8,128)S(1)}, f32[2,2,2,128,128]{4,3,2,1,0:T(8,128)}, u32[]{:S(2)}) copy-start(f32[2,2,2,128,128]{4,3,2,1,0:T(8,128)} %rev.39) | copy-start | bytes 1572868
  118.7 1.2 copy-start.5
  123.7 3.5 %copy-start.8 = (bf16[2,1024,128]{1,2,0:T(8,128)(2,1)S(1)}, bf16[2,1024,128]{1,2,0:T(8,128)(2,1)}, u32[]{:S(2)}) copy-start(bf16[2,1024,128]{1,2,0:T(8,128)(2,1)} %copy.75) | copy-start | bytes 1572868
  123.7 96.3 %reduce-scatter.3.cloned.1.call-start = ((), (), s32[]{:S(2)}) async-start(), calls=%async_computation.2 | async-start | bytes 2621440 | tf_op jit(solution)/shard_map/reduce_scatter | solution.py:166
  127.2 92.9 %reduce-scatter.5.cloned.1.call-start = ((), (), s32[]{:S(2)}) async-start(), calls=%async_computation.3 | async-start | bytes 2621440 | tf_op jit(solution)/shard_map/reduce_scatter | solution.py:237
  127.2 1.9 copy-start.17
  129.1 1.0 copy-start.10
  129.1 1.2 copy-start.18
  213.9 4.2 %copy-start.24 = (bf16[1024,256]{0,1:T(8,128)(2,1)S(1)}, bf16[1024,256]{0,1:T(8,128)(2,1)}, u32[]{:S(2)}) copy-start(bf16[1024,256]{0,1:T(8,128)(2,1)} %get-tuple-element.26) | copy-start | bytes 1572868
  213.9 5.2 %copy-start.23 = (bf16[1024,256]{0,1:T(8,128)(2,1)S(1)}, bf16[1024,256]{0,1:T(8,128)(2,1)}, u32[]{:S(2)}) copy-start(bf16[1024,256]{0,1:T(8,128)(2,1)} %get-tuple-element.27) | copy-start | bytes 1572868
Sparse Core Ops, SparseCore 0:
  123.8 89.9 all-reduce.2
Sparse Core Ops, SparseCore 1:
  127.3 33.4 reduce-scatter.2
  163.9 31.4 reduce-scatter.4
where the time goes:
time: 229 us; the launch traced here: 228 us
  waiting for transfers between devices  85.1 us (37%)
  local copies, waits for them, and re-layouts  49.6 us (22%)
  matrix products  44.7 us (20%)
  other arithmetic  19.2 us (8%)
  between operations  16.2 us (7%)
  starting transfers between devices  12.7 us (6%)
    psum x1, waiting for transfers between devices, per_device(): lax.psum(query_term.astype(jnp.bfloat16), 'seq').astype(jnp.float32)  81.5 us
    unnamed x70, local copies, waits for them, and re-layouts  14.9 us
    ppermute x8, starting transfers between devices, partner(): return lax.ppermute(block, axis, route)  12.6 us
    dot_general x4, matrix products, project(): lax.dot_general(left, weight, (((1,), (1,)), ((), ())), preferred_element...  8.04 us
    dot_general x4, matrix products, contract_rows(): lax.dot_general(left, right, (((0,), (0,)), ((), ())), preferred_element_...  7.14 us
    reduce_sum x4, other arithmetic, fold_back(): grads.reshape(head_count, segments, reach, block_rows, head_width)  6.09 us
    rev x4, local copies, waits for them, and re-layouts, sibling_blocks(): level.reshape(head_count, segments // 2, 2, block_rows, head_width)  5.38 us
    rev x4, local copies, waits for them, and re-layouts, fold_back(): summed.reshape(head_count, segments // 2, 2, block_rows, head_width)  5.05 us
  transfers between devices with their start and end apart: 11, of which 3 were waited for; matrix products, arithmetic and copies ran while one was open for 40% of the time, Pallas kernels for 0%

commit v1 on v0

v1 whole, which is shorter than its diff:
```python
import functools
import math

import jax
import jax.numpy as jnp
from jax import lax
from jax.experimental import pallas as pl
from jax.experimental.pallas import tpu as pltpu
from jax.sharding import PartitionSpec as P

HEAD_DIM = 128
BLOCK = 128
BF16 = jnp.bfloat16
F32 = jnp.float32
MIB = 1024 * 1024

NN = (((1,), (0,)), ((), ()))
NT = (((1,), (1,)), ((), ()))
TN = (((0,), (0,)), ((), ()))


def dot(left, right, dims=NN):
    return lax.dot_general(left, right, dims, preferred_element_type=F32)


def params(mib):
    return pltpu.CompilerParams(vmem_limit_bytes=mib * MIB)


def cost(flops, moved, exps=0):
    return pl.CostEstimate(flops=int(flops), bytes_accessed=int(moved), transcendentals=int(exps))


def shape(rows, cols, dtype=BF16):
    return jax.ShapeDtypeStruct((rows, cols), dtype)


def whole(rows, cols):
    return pl.BlockSpec((rows, cols), lambda *_: (0, 0))


def pool_matrix(rows):
    row = lax.broadcasted_iota(jnp.int32, (rows // 2, rows), 0)
    col = lax.broadcasted_iota(jnp.int32, (rows // 2, rows), 1)
    return jnp.where(jnp.right_shift(col, 1) == row, 0.5, 0.0).astype(BF16)


def spread_matrix(rows, step_bits, offset, cols, weight):
    row = lax.broadcasted_iota(jnp.int32, (rows, cols), 0) + offset
    col = lax.broadcasted_iota(jnp.int32, (rows, cols), 1)
    return jnp.where(jnp.right_shift(row, step_bits) == col, weight, 0.0).astype(BF16)


def key_value_body(local_levels, far_levels, tok_ref, wk_ref, wv_ref, *outs):
    k_ref, v_ref = outs[:2]
    mid = outs[2 : 2 + 2 * (local_levels - 1)]
    far = outs[2 + 2 * (local_levels - 1) : -1]
    top_ref = outs[-1]
    step = pl.program_id(0)
    x = tok_ref[...]
    inner = wk_ref.shape[1]
    for which, (w_ref, out_ref) in enumerate(((wk_ref, k_ref), (wv_ref, v_ref))):
        rows = dot(x, w_ref[...]).astype(BF16)
        out_ref[...] = rows
        for i in range(local_levels - 1):
            rows = dot(pool_matrix(rows.shape[0]), rows).astype(BF16)
            mid[2 * i + which][...] = rows
        rows = dot(pool_matrix(rows.shape[0]), rows).astype(BF16)
        count = rows.shape[0]
        place = pl.ds(pl.multiple_of(step * count, count), count)
        top_ref[place, which * inner : (which + 1) * inner] = rows

    @pl.when(step == pl.num_programs(0) - 1)
    def _():
        rows = top_ref[...]
        for i in range(far_levels):
            if i:
                rows = dot(pool_matrix(rows.shape[0]), rows).astype(BF16)
            far[i][...] = rows


def key_value(tokens, w_key, w_value, local_levels, far_levels):
    tok_rows, width = tokens.shape
    inner = w_key.shape[1]
    tile = 2 * BLOCK
    steps = tok_rows // tile
    out_shape = [shape(tok_rows, inner)] * 2
    out_specs = [pl.BlockSpec((tile, inner), lambda i: (i, 0))] * 2
    for i in range(1, local_levels):
        out_shape += [shape(tok_rows >> i, inner)] * 2
        out_specs += [pl.BlockSpec((tile >> i, inner), lambda i: (i, 0))] * 2
    for i in range(far_levels):
        out_shape += [shape(BLOCK >> i, 2 * inner)]
        out_specs += [whole(BLOCK >> i, 2 * inner)]
    return pl.pallas_call(
        functools.partial(key_value_body, local_levels, far_levels),
        grid=(steps,),
        in_specs=[
            pl.BlockSpec((tile, width), lambda i: (i, 0)),
            whole(width, inner),
            whole(width, inner),
        ],
        out_specs=out_specs,
        out_shape=out_shape,
        scratch_shapes=[pltpu.VMEM((BLOCK, 2 * inner), BF16)],
        compiler_params=params(24),
        cost_estimate=cost(4 * tok_rows * width * inner, 2 * tok_rows * width + 8 * width * inner),
    )(tokens, w_key, w_value)


def pair_body(a_ref, b_ref, wa_ref, wb_ref, x_ref, y_ref):
    x_ref[...] = dot(a_ref[...], wa_ref[...]).astype(BF16)
    y_ref[...] = dot(b_ref[...], wb_ref[...]).astype(BF16)


def project_pair(a, b, wa, wb):
    tok_rows, width = a.shape
    inner = wa.shape[1]
    tile = 2 * BLOCK
    rows = pl.BlockSpec((tile, width), lambda i: (i, 0))
    outs = pl.BlockSpec((tile, inner), lambda i: (i, 0))
    return pl.pallas_call(
        pair_body,
        grid=(tok_rows // tile,),
        in_specs=[rows, rows, whole(width, inner), whole(width, inner)],
        out_specs=[outs, outs],
        out_shape=[shape(tok_rows, inner)] * 2,
        compiler_params=params(24),
        cost_estimate=cost(4 * tok_rows * width * inner, 4 * tok_rows * width + 8 * width * inner),
    )(a, b, wa, wb)


def attention_body(local_levels, far_bits, *refs):
    mids = local_levels - 1
    fars = len(far_bits)
    q_ref, g_ref, k_ref, v_ref = refs[:4]
    mid_refs = refs[4 : 4 + 2 * mids]
    far_refs = refs[4 + 2 * mids : 4 + 2 * mids + fars]
    outs = refs[4 + 2 * mids + fars :]
    att_ref, att_t_ref, dq_ref, dq_t_ref, dkv_ref = outs[:5]
    dmid_refs = outs[5 : 5 + mids]
    dfar_refs = outs[5 + mids : 5 + mids + fars]
    acc_ref = outs[-1]
    tok_rows, inner = q_ref.shape
    heads = inner // HEAD_DIM
    pair = 2 * BLOCK
    score_scale = 1.0 / math.sqrt(HEAD_DIM)
    sizes = [pair] + [BLOCK] * mids + [r.shape[0] for r in far_refs]
    biases = [0.0] + [i * math.log(2.0) for i in range(1, local_levels)]
    biases += [(local_levels + bit) * math.log(2.0) for bit in far_bits]
    starts = [sum(sizes[:i]) for i in range(len(sizes))]

    for ref in (*dmid_refs, acc_ref):
        ref[...] = jnp.zeros_like(ref)

    def unit(m, h):
        low = h * HEAD_DIM
        cols = slice(low, low + HEAD_DIM)
        vcols = slice(inner + low, inner + low + HEAD_DIM)
        here = pl.ds(pl.multiple_of(m * pair, pair), pair)
        seats = []
        for i in range(1, local_levels):
            sibling = jnp.bitwise_xor(jnp.right_shift(m, i - 1), 1)
            seats.append(pl.ds(pl.multiple_of(sibling * BLOCK, BLOCK), BLOCK))
        keys = [k_ref[here, cols]]
        values = [v_ref[here, cols]]
        for i in range(mids):
            keys.append(mid_refs[2 * i][seats[i], cols])
            values.append(mid_refs[2 * i + 1][seats[i], cols])
        for ref in far_refs:
            keys.append(ref[:, cols])
            values.append(ref[:, vcols])
        keys = jnp.concatenate(keys, axis=0)
        values = jnp.concatenate(values, axis=0)
        q = q_ref[here, cols]
        g = g_ref[here, cols]
        raw = dot(keys, q, NT)
        scores = jnp.concatenate(
            [
                raw[start : start + size] * score_scale + bias
                for start, size, bias in zip(starts, sizes, biases)
            ],
            axis=0,
        )
        expo = jnp.exp(scores - jnp.max(scores, axis=0, keepdims=True))
        probs = expo * (1.0 / jnp.sum(expo, axis=0, keepdims=True))
        probs_b = probs.astype(BF16)
        att_t = dot(values, probs_b, TN).astype(BF16)
        att_t_ref[cols, here] = att_t
        att_ref[here, cols] = att_t.T
        g_t = g.T
        delta = jnp.sum(g_t.astype(F32) * att_t.astype(F32), axis=0, keepdims=True)
        dprobs = dot(values, g, NT)
        grads = (probs * (dprobs - delta) * score_scale).astype(BF16)
        dq_t = dot(keys, grads, TN).astype(BF16)
        dq_t_ref[cols, here] = dq_t
        dq_ref[here, cols] = dq_t.T
        dk = dot(grads, q)
        dv = dot(probs_b, g)
        for part, where_to in ((dk, cols), (dv, vcols)):
            dkv_ref[here, where_to] = part[:pair]
            for i in range(mids):
                start = starts[1 + i]
                dmid_refs[i][seats[i], where_to] += part[start : start + BLOCK]
            acc_ref[:, where_to] += part[starts[1 + mids] :]

    def step(m, carry):
        for h in range(heads):
            unit(m, h)
        return carry

    lax.fori_loop(0, tok_rows // pair, step, 0)
    base = starts[1 + mids]
    for ref, start, size in zip(dfar_refs, starts[1 + mids :], sizes[1 + mids :]):
        ref[...] = acc_ref[start - base : start - base + size].astype(BF16)


def attention(query, grad, key, value, mids, fars, far_bits, local_levels):
    tok_rows, inner = query.shape
    far_rows = sum(f.shape[0] for f in fars)
    set_rows = (local_levels + 1) * BLOCK + far_rows
    out_shape = [
        shape(tok_rows, inner),
        shape(inner, tok_rows),
        shape(tok_rows, inner),
        shape(inner, tok_rows),
        shape(tok_rows, 2 * inner, F32),
    ]
    out_shape += [shape(tok_rows >> i, 2 * inner, F32) for i in range(1, local_levels)]
    out_shape += [shape(f.shape[0], 2 * inner) for f in fars]
    return pl.pallas_call(
        functools.partial(attention_body, local_levels, far_bits),
        out_shape=out_shape,
        scratch_shapes=[pltpu.VMEM((far_rows, 2 * inner), F32)],
        compiler_params=params(40),
        cost_estimate=cost(
            12 * tok_rows * set_rows * inner, 24 * tok_rows * inner, tok_rows * set_rows * 2
        ),
    )(query, grad, key, value, *mids, *fars)


def term_body(left_ref, right_ref, *out_refs):
    product = dot(left_ref[...], right_ref[...]).astype(BF16).T
    inner = product.shape[1] // len(out_refs)
    for i, ref in enumerate(out_refs):
        ref[...] = product[:, i * inner : (i + 1) * inner]


def weight_terms(left_t, right, count):
    rows, tok_rows = left_t.shape
    width = right.shape[1]
    tile = min(width, 256)
    inner = rows // count
    return pl.pallas_call(
        term_body,
        grid=(width // tile,),
        in_specs=[whole(rows, tok_rows), pl.BlockSpec((tok_rows, tile), lambda i: (0, i))],
        out_specs=[pl.BlockSpec((tile, inner), lambda i: (i, 0))] * count,
        out_shape=[shape(width, inner)] * count,
        compiler_params=params(24),
        cost_estimate=cost(2 * rows * tok_rows * width, 2 * tok_rows * width + 4 * rows * tok_rows),
    )(left_t, right)


def close_body(local_levels, far_bits, dkv_ref, *refs):
    mids = local_levels - 1
    dmid_refs = refs[:mids]
    back_refs = refs[mids : mids + len(far_bits)]
    dk_ref, dv_ref, dkv_t_ref = refs[mids + len(far_bits) :]
    tile = dkv_ref.shape[0]
    offset = pl.program_id(0) * tile
    inner = dk_ref.shape[1]
    total = dkv_ref[...]
    chain = None
    for i in reversed(range(mids)):
        chain = dmid_refs[i][...] if chain is None else dmid_refs[i][...] + chain
        high = chain.astype(BF16)
        low = (chain - high.astype(F32)).astype(BF16)
        rows = chain.shape[0]
        fan = spread_matrix(2 * rows, 1, 0, rows, 0.5)
        chain = dot(fan, high) + dot(fan, low)
    if chain is not None:
        total = total + chain
    for ref, bit in zip(back_refs, far_bits):
        weight = 0.5 ** (local_levels + bit)
        fan = spread_matrix(tile, local_levels + bit, offset, ref.shape[0], weight)
        total = total + dot(fan, ref[...])
    final = total.astype(BF16)
    dk_ref[...] = final[:, :inner]
    dv_ref[...] = final[:, inner:]
    dkv_t_ref[...] = final.T


def close_keys(dkv, dmids, backs, far_bits, local_levels):
    tok_rows, double = dkv.shape
    inner = double // 2
    tile = 2 * BLOCK
    in_specs = [pl.BlockSpec((tile, double), lambda i: (i, 0))]
    in_specs += [pl.BlockSpec((tile >> i, double), lambda i: (i, 0)) for i in range(1, local_levels)]
    in_specs += [whole(*b.shape) for b in backs]
    return pl.pallas_call(
        functools.partial(close_body, local_levels, far_bits),
        grid=(tok_rows // tile,),
        in_specs=in_specs,
        out_specs=[
            pl.BlockSpec((tile, inner), lambda i: (i, 0)),
            pl.BlockSpec((tile, inner), lambda i: (i, 0)),
            pl.BlockSpec((double, tile), lambda i: (0, i)),
        ],
        out_shape=[shape(tok_rows, inner), shape(tok_rows, inner), shape(double, tok_rows)],
        compiler_params=params(24),
        cost_estimate=cost(4 * tok_rows * 256 * double, 20 * tok_rows * double),
    )(dkv, *dmids, *backs)


def out_body(count, *refs):
    total = None
    for i in range(count):
        part = dot(refs[i][...], refs[count + i][...], NT)
        total = part if total is None else total + part
    refs[-1][...] = total.astype(BF16)


def project_out(lefts, weights):
    count = len(lefts)
    tok_rows, inner = lefts[0].shape
    width = weights[0].shape[0]
    tile = 2 * BLOCK
    return pl.pallas_call(
        functools.partial(out_body, count),
        grid=(tok_rows // tile,),
        in_specs=[pl.BlockSpec((tile, inner), lambda i: (i, 0))] * count
        + [whole(width, inner)] * count,
        out_specs=pl.BlockSpec((tile, width), lambda i: (i, 0)),
        out_shape=shape(tok_rows, width),
        compiler_params=params(24),
        cost_estimate=cost(2 * count * tok_rows * inner * width, 2 * tok_rows * width),
    )(*lefts, *weights)


def exchange(block, axis, distance):
    count = lax.axis_size(axis)
    return lax.ppermute(block, axis, [(i, i ^ distance) for i in range(count)])


def add(left, right):
    return (left.astype(F32) + right.astype(F32)).astype(BF16)


def line_sum(block, axis):
    count = lax.axis_size(axis)
    if count < 4:
        return add(block, exchange(block, axis, 1)) if count == 2 else block
    rank = jnp.bitwise_and(lax.axis_index(axis), 3)
    inward, across, outward = [], [], []
    for base in range(0, count, 4):
        inward += [(base, base + 1), (base + 3, base + 2)]
        across += [(base + 1, base + 2), (base + 2, base + 1)]
        outward += [(base + 1, base), (base + 2, base + 3)]
    half = add(block, lax.ppermute(block, axis, inward))
    total = add(half, lax.ppermute(half, axis, across))
    ends = lax.ppermute(total, axis, outward)
    total = jnp.where((rank == 0) | (rank == 3), ends, total)
    distance = 4
    while distance < count:
        total = add(total, exchange(total, axis, distance))
        distance *= 2
    return total


def per_device(tokens, w_query, w_key, w_value, w_out, cotangent):
    tok_rows = tokens.shape[0]
    local_levels = (tok_rows // BLOCK).bit_length() - 1
    count = lax.axis_size("seq")
    far_levels = count.bit_length() - 1
    far_bits = [d.bit_length() - 1 for d in range(1, count)]

    parts = key_value(tokens, w_key, w_value, local_levels, far_levels)
    key, value = parts[:2]
    mids = parts[2 : 2 + 2 * (local_levels - 1)]
    tops = parts[2 + 2 * (local_levels - 1) :]
    fars = [exchange(tops[bit], "seq", d) for d, bit in enumerate(far_bits, 1)]
    query, grad = project_pair(tokens, cotangent, w_query, w_out)
    results = attention(query, grad, key, value, mids, fars, far_bits, local_levels)
    attended, attended_t, dquery, dquery_t, dkv = results[:5]
    dmids = results[5 : 5 + local_levels - 1]
    dfars = results[5 + local_levels - 1 :]
    backs = [exchange(piece, "seq", d) for d, piece in enumerate(dfars, 1)]

    (out_term,) = weight_terms(attended_t, cotangent, 1)
    out_grad = line_sum(out_term, "seq")
    (query_term,) = weight_terms(dquery_t, tokens, 1)
    query_grad = line_sum(query_term, "seq")
    mixed_part = project_out([attended], [w_out])
    mixed = lax.psum_scatter(mixed_part, "head", scatter_dimension=1, tiled=True)

    dkey, dvalue, dkv_t = close_keys(dkv, dmids, backs, far_bits, local_levels)
    key_term, value_term = weight_terms(dkv_t, tokens, 2)
    key_grad = line_sum(key_term, "seq")
    value_grad = line_sum(value_term, "seq")
    grad_part = project_out([dquery, dkey, dvalue], [w_query, w_key, w_value])
    tokens_grad = lax.psum_scatter(grad_part, "head", scatter_dimension=1, tiled=True)
    return mixed, tokens_grad, query_grad, key_grad, value_grad, out_grad


def solution(mesh):
    return jax.shard_map(
        per_device,
        mesh=mesh,
        in_specs=(
            P(("groups", "seq"), None),
            P(None, "head"),
            P(None, "head"),
            P(None, "head"),
            P(None, "head"),
            P(("groups", "seq"), None),
        ),
        out_specs=(
            P(("groups", "seq"), "head"),
            P(("groups", "seq"), "head"),
            P("groups", "head"),
            P("groups", "head"),
            P("groups", "head"),
            P("groups", "head"),
        ),
        check_vma=False,
    )
```

time: 229 us -> 170 us (0.74)
  matrix products: 44.7 us -> 0 us
  local copies, waits for them, and re-layouts: 49.6 us -> 16.9 us
  Pallas kernels: 0 us -> 31.4 us
  starting transfers between devices: 12.7 us -> 26.6 us
  other arithmetic: 19.2 us -> 6.53 us
  waiting for transfers between devices: 85.1 us -> 73.9 us
    psum x1 -> x0, waiting for transfers between devices: 81.5 us -> none  [per_device(): lax.psum(query_term.astype(jnp.bfloat16), 'seq').astype(jnp.float32)]
    ppermute x8 -> x18, waiting for transfers between devices: 3.62 us -> 73.9 us  [the longest x4 39.6 us: line_sum(): ends = lax.ppermute(total, axis, outward)]
    dot_general x24 -> x0, matrix products: 44.7 us -> none  [the longest x4 8.04 us: project(): lax.dot_general(left, weight, (((1,), (1,)), ((), ())), preferred_element...]
    pallas_call x0 -> x9, Pallas kernels: none -> 31.4 us  [the longest x1 10.4 us: attention(): pl.pallas_call(functools.partial(attention_body, local_levels, far_bits),...]
    ppermute x8 -> x18, starting transfers between devices: 12.6 us -> 26.5 us  [the longest x6 10.1 us: exchange(): return lax.ppermute(block, axis, [(i, i ^ distance) for i in range(count)])]
    rev x8 -> x0, local copies, waits for them, and re-layouts: 10.4 us -> none  [the longest x4 5.38 us: sibling_blocks(): level.reshape(head_count, segments // 2, 2, block_rows, head_width)]
    slice x8 -> x0, local copies, waits for them, and re-layouts: 8.19 us -> none  [the longest x1 4.11 us: per_device(): dvalue_near[:, :, :block_rows].reshape(head_count, tok_rows, HEAD_DIM)]
    reduce_sum x6 -> x0, other arithmetic: 8.1 us -> none  [the longest x4 6.09 us: fold_back(): grads.reshape(head_count, segments, reach, block_rows, head_width)]
  transfers between devices with their start and end apart: 11 -> 20, of which waited for: 3 -> 12; matrix products, arithmetic and copies ran while one was open for 40% -> 4% of each run, Pallas kernels for 0% -> 8%
where the time goes in v1:
time: 170 us
  waiting for transfers between devices  73.9 us (43%)
  Pallas kernels  31.4 us (18%)
  starting transfers between devices  26.6 us (16%)
  local copies, waits for them, and re-layouts  16.9 us (10%)
  between operations  14.4 us (8%)
  other arithmetic  6.53 us (4%)
    ppermute x4, waiting for transfers between devices, line_sum(): ends = lax.ppermute(total, axis, outward)  39.6 us
    ppermute x4, waiting for transfers between devices, line_sum(): half = add(block, lax.ppermute(block, axis, inward))  25.9 us
    unnamed x50, local copies, waits for them, and re-layouts  16.9 us
    pallas_call x1, Pallas kernels, attention(): pl.pallas_call(functools.partial(attention_body, local_levels, far_bits),...  10.4 us
    ppermute x6, starting transfers between devices, exchange(): return lax.ppermute(block, axis, [(i, i ^ distance) for i in range(count)])  10.1 us
    ppermute x4, starting transfers between devices, line_sum(): half = add(block, lax.ppermute(block, axis, inward))  8.44 us
    ppermute x6, waiting for transfers between devices, exchange(): return lax.ppermute(block, axis, [(i, i ^ distance) for i in range(count)])  8.32 us
    pallas_call x1, Pallas kernels, key_value(): pl.pallas_call(functools.partial(key_value_body, local_levels, far_levels...  6.25 us
  transfers between devices with their start and end apart: 20, of which 12 were waited for; matrix products, arithmetic and copies ran while one was open for 4% of the time, Pallas kernels for 8%

profile of v1, /device:TPU:0, one launch (start us, length us, event | category | flops | bytes accessed | tf_op | source)
XLA Modules:
  0.0 169.7 jit_solution(9376428807836854845)
XLA Ops:
  7.2 1.7 %copy-done.1 = bf16[1024,1024]{1,0:T(8,128)(2,1)S(1)} copy-done((bf16[1024,1024]{1,0:T(8,128)(2,1)S(1)}, bf16[1024,1024]{1,0:T(8,128)(2,1)}, u32[]{:S(2)}) %copy-start.1) | copy-done | bytes 2097176
  9.0 1.0 copy-done.19
  10.0 1.0 copy-done.21
  11.0 6.3 %shard_map.110 = (bf16[1024,256]{1,0:T(8,128)(2,1)S(1)}, bf16[1024,256]{1,0:T(8,128)(2,1)S(1)}, bf16[512,256]{1,0:T(8,128)(2,1)S(1)}, bf16[512,256]{1,0:T(8,128)...) custom-call(bf16[1024,1024]{1,0:T(8,128)(2,1)S(1)} %copy-done.1, ...), custom_call_target="tpu_custom_call" | custom-call | flops 1073741824 | bytes 4194304 | tf_op jit(solution)/shard_map/pallas_call | solution.py:95
  17.3 3.1 %collective-permute-start = (bf16[128,512]{1,0:T(8,128)(2,1)S(1)}, bf16[128,512]{1,0:T(8,128)(2,1)S(1)}, u32[]{:S(2)}, u32[]{:S(2)}) collective-permute-start(bf16[128,512]{1,0:T(8,128)(2,1)S(1)} %get-tuple-element.39), channel_id=1, source_target_pairs={{0,4},{4,0},{8,12},{12,8},{1,5},{5,1},{9,13},{13,9},{2,6},{6,2},{1... | collective-permute-start | bytes 393224 | tf_op jit(solution)/shard_map/ppermute | solution.py:343
  20.4 2.6 %collective-permute-start.1 = (bf16[64,512]{1,0:T(8,128)(2,1)S(1)}, bf16[64,512]{1,0:T(8,128)(2,1)S(1)}, u32[]{:S(2)}, u32[]{:S(2)}) collective-permute-start(bf16[64,512]{1,0:T(8,128)(2,1)S(1)} %get-tuple-element.40), channel_id=1, source_target_pairs={{0,8},{4,12},{8,0},{12,4},{1,9},{5,13},{9,1},{13,5},{2,10},{6,14},... | collective-permute-start | bytes 196616 | tf_op jit(solution)/shard_map/ppermute | solution.py:343
  23.0 1.8 %shard_map.109 = (bf16[1024,256]{1,0:T(8,128)(2,1)S(1)}, bf16[1024,256]{1,0:T(8,128)(2,1)S(1)}) custom-call(bf16[1024,1024]{1,0:T(8,128)(2,1)S(1)} %copy-done.1, bf16[1024,1024]{1,0:T(8,128)(2,1)S(1)} %copy-done, bf16[1024,256]{1,0:T(8,128)(2,1)S(1)} %copy-done.9, bf16[1024,256]{1,0:T(8,128)(2,1)S(1)} %copy-done.6), custom_call_target="tpu_custom_call" | custom-call | flops 1073741824 | bytes 6291456 | tf_op jit(solution)/shard_map/pallas_call | solution.py:122
  24.8 2.1 %collective-permute-done.1.refs_9_ = bf16[64,512]{1,0:T(8,128)(2,1)S(1)} collective-permute-done((bf16[64,512]{1,0:T(8,128)(2,1)S(1)}, bf16[64,512]{1,0:T(8,128)(2,1)S(1)}, u32[]{:S(2)}, u32[]{:S(2)}) %collective-permute-start.1) | collective-permute-done | bytes 65568 | tf_op jit(solution)/shard_map/ppermute | solution.py:343
  26.9 2.2 %collective-permute-done.2.refs_10_ = bf16[64,512]{1,0:T(8,128)(2,1)S(1)} collective-permute-done((bf16[64,512]{1,0:T(8,128)(2,1)S(1)}, bf16[64,512]{1,0:T(8,128)(2,1)S(1)}, u32[]{:S(2)}, u32[]{:S(2)}) %collective-permute-start.2) | collective-permute-done | bytes 65568 | tf_op jit(solution)/shard_map/ppermute | solution.py:343
  29.1 10.4 %shard_map.111 = (bf16[1024,256]{1,0:T(8,128)(2,1)S(1)}, bf16[256,1024]{1,0:T(8,128)(2,1)S(1)}, bf16[1024,256]{1,0:T(8,128)(2,1)S(1)}, bf16[256,1024]{1,0:T(8,12...) custom-call(bf16[1024,256]{1,0:T(8,128)(2,1)S(1)} %get-tuple-element, ...), custom_call_target="tpu_custom_call" | custom-call | flops 2415919104 | bytes 6291456 | tf_op jit(solution)/shard_map/pallas_call | solution.py:231
  39.6 1.3 copy-done.7
  44.1 1.4 shard_map.112
  45.4 1.3 copy-done.4
  46.8 1.2 collective-permute-start.3
  48.0 1.2 collective-permute-start.4
  49.2 2.1 %collective-permute-start.5 = (bf16[64,512]{1,0:T(8,128)(2,1)S(1)}, bf16[64,512]{1,0:T(8,128)(2,1)S(1)}, u32[]{:S(2)}, u32[]{:S(2)}) collective-permute-start(bf16[64,512]{1,0:T(8,128)(2,1)S(1)} %get-tuple-element.48), channel_id=1, source_target_pairs={{0,12},{4,8},{8,4},{12,0},{1,13},{5,9},{9,5},{13,1},{2,14},{6,10},... | collective-permute-start | bytes 196616 | tf_op jit(solution)/shard_map/ppermute | solution.py:343
  51.3 2.1 %collective-permute-done.4.refs_3_ = bf16[64,512]{1,0:T(8,128)(2,1)S(1)} collective-permute-done((bf16[64,512]{1,0:T(8,128)(2,1)S(1)}, bf16[64,512]{1,0:T(8,128)(2,1)S(1)}, u32[]{:S(2)}, u32[]{:S(2)}) %collective-permute-start.4) | collective-permute-done | bytes 65568 | tf_op jit(solution)/shard_map/ppermute | solution.py:343
  53.4 2.0 %collective-permute-done.5.refs_4_ = bf16[64,512]{1,0:T(8,128)(2,1)S(1)} collective-permute-done((bf16[64,512]{1,0:T(8,128)(2,1)S(1)}, bf16[64,512]{1,0:T(8,128)(2,1)S(1)}, u32[]{:S(2)}, u32[]{:S(2)}) %collective-permute-start.5) | collective-permute-done | bytes 65568 | tf_op jit(solution)/shard_map/ppermute | solution.py:343
  55.3 1.7 copy-done.8
  57.0 1.0 copy-done.12
  58.0 3.2 %shard_map.113 = (bf16[1024,256]{1,0:T(8,128)(2,1)S(1)}, bf16[1024,256]{1,0:T(8,128)(2,1)S(1)}, bf16[512,1024]{1,0:T(8,128)(2,1)S(1)}) custom-call(f32[1024,512]{1,0:T(8,128)S(1)} %copy-done.8, f32[512,512]{1,0:T(8,128)S(1)} %get-tuple-element.44.refs_0_, f32[256,512]{1,0:T(8,128)S(1)} %copy-done.12, bf16[128,512]{1,0:T(8,128)(2,1)S(1)} %collective-permute-done.3.refs_2_, ...), custom_call_target="tpu_custom_call" | custom-call | flops 536870912 | bytes 10485760 | tf_op jit(solution)/shard_map/pallas_call | solution.py:301
  61.2 1.0 copy-done.17
  62.2 2.5 %shard_map.114 = bf16[1024,1024]{1,0:T(8,128)(2,1)S(1)} custom-call(bf16[1024,256]{1,0:T(8,128)(2,1)S(1)} %copy-done.24, bf16[1024,256]{1,0:T(8,128)(2,1)S(1)} %get-tuple-element.49.refs_1_, bf16[1024,256]{1,0:T(8,128)(2,1)S(1)} %get-tuple-element.50.refs_2_, bf16[1024,256]{1,0:T(8,128)(2,1)S(1)} %copy-done.10, bf16[1024,256]{1,0:T(8,128)(2,1)S(1)} %copy-done.20, ...), custom_call_target="tpu_custom_call" | custom-call | flops 1610612736 | bytes 2097152 | tf_op jit(solution)/shard_map/pallas_call | solution.py:329
  64.7 1.3 copy-done.5
  66.1 1.0 copy-done.16
  67.1 1.8 %shard_map.117 = bf16[1024,256]{1,0:T(8,128)(2,1)S(1)} custom-call(bf16[256,1024]{1,0:T(8,128)(2,1)S(1)} %copy-done.16, bf16[1024,1024]{1,0:T(8,128)(2,1)S(1)} %copy-done), custom_call_target="tpu_custom_call" | custom-call | flops 536870912 | bytes 3145728 | tf_op jit(solution)/shard_map/pallas_call | solution.py:254
  68.9 3.7 %collective-permute-start.15 = (bf16[1024,256]{1,0:T(8,128)(2,1)S(1)}, bf16[1024,256]{1,0:T(8,128)(2,1)}, u32[]{:S(2)}, u32[]{:S(2)}) collective-permute-start(bf16[1024,256]{1,0:T(8,128)(2,1)S(1)} %shard_map.117), channel_id=1, source_target_pairs={{0,4},{12,8},{1,5},{13,9},{2,6},{14,10},{3,7},{15,11},{16,20},{28,... | collective-permute-start | bytes 1572872 | tf_op jit(solution)/shard_map/ppermute | solution.py:360
  72.6 1.8 %shard_map.115 = bf16[1024,256]{1,0:T(8,128)(2,1)S(1)} custom-call(bf16[256,1024]{1,0:T(8,128)(2,1)S(1)} %copy-done.14, bf16[1024,1024]{1,0:T(8,128)(2,1)S(1)} %copy-done.2), custom_call_target="tpu_custom_call" | custom-call | flops 536870912 | bytes 3145728 | tf_op jit(solution)/shard_map/pallas_call | solution.py:254
  74.4 2.1 %collective-permute-start.6 = (bf16[1024,256]{1,0:T(8,128)(2,1)S(1)}, bf16[1024,256]{1,0:T(8,128)(2,1)}, u32[]{:S(2)}, u32[]{:S(2)}) collective-permute-start(bf16[1024,256]{1,0:T(8,128)(2,1)S(1)} %shard_map.115), channel_id=1, source_target_pairs={{0,4},{12,8},{1,5},{13,9},{2,6},{14,10},{3,7},{15,11},{16,20},{28,... | collective-permute-start | bytes 1572872 | tf_op jit(solution)/shard_map/ppermute | solution.py:360
  76.5 1.2 copy-done.18
  77.7 2.3 %shard_map.116 = (bf16[1024,256]{1,0:T(8,128)(2,1)S(1)}, bf16[1024,256]{1,0:T(8,128)(2,1)S(1)}) custom-call(bf16[512,1024]{1,0:T(8,128)(2,1)S(1)} %copy-done.18, bf16[1024,1024]{1,0:T(8,128)(2,1)S(1)} %copy-done.3), custom_call_target="tpu_custom_call" | custom-call | flops 1073741824 | bytes 4194304 | tf_op jit(solution)/shard_map/pallas_call | solution.py:254
  80.0 1.3 collective-permute-start.12
  81.4 1.3 collective-permute-start.9
  82.7 1.4 collective-permute-done.15
  84.1 1.2 add_convert_fusion.1
  86.0 9.4 %collective-permute-done.6 = bf16[1024,256]{1,0:T(8,128)(2,1)} collective-permute-done((bf16[1024,256]{1,0:T(8,128)(2,1)S(1)}, bf16[1024,256]{1,0:T(8,128)(2,1)}, u32[]{:S(2)}, u32[]{:S(2)}) %collective-permute-start.6) | collective-permute-done | bytes 524320 | tf_op jit(solution)/shard_map/ppermute | solution.py:360
  95.4 1.2 add_convert_fusion.7
  97.2 9.4 %collective-permute-done.12 = bf16[1024,256]{1,0:T(8,128)(2,1)S(1)} collective-permute-done((bf16[1024,256]{1,0:T(8,128)(2,1)S(1)}, bf16[1024,256]{1,0:T(8,128)(2,1)S(1)}, u32[]{:S(2)}, u32[]{:S(2)}) %collective-permute-start.12) | collective-permute-done | bytes 524320 | tf_op jit(solution)/shard_map/ppermute | solution.py:360
  107.4 5.8 %collective-permute-done.9 = bf16[1024,256]{1,0:T(8,128)(2,1)S(1)} collective-permute-done((bf16[1024,256]{1,0:T(8,128)(2,1)S(1)}, bf16[1024,256]{1,0:T(8,128)(2,1)S(1)}, u32[]{:S(2)}, u32[]{:S(2)}) %collective-permute-start.9) | collective-permute-done | bytes 524320 | tf_op jit(solution)/shard_map/ppermute | solution.py:360
  114.2 1.3 collective-permute-start.17
  115.6 1.3 collective-permute-start.8
  117.1 1.3 collective-permute-start.14
  118.5 1.3 collective-permute-start.11
  119.8 13.7 %collective-permute-done.17 = bf16[1024,256]{1,0:T(8,128)(2,1)S(1)} collective-permute-done((bf16[1024,256]{1,0:T(8,128)(2,1)S(1)}, bf16[1024,256]{1,0:T(8,128)(2,1)S(1)}, u32[]{:S(2)}, u32[]{:S(2)}) %collective-permute-start.17) | collective-permute-done | bytes 524320 | tf_op jit(solution)/shard_map/ppermute | solution.py:362
  133.5 0.8 broadcast_select_fusion
  134.3 10.4 %collective-permute-done.8 = bf16[1024,256]{1,0:T(8,128)(2,1)S(1)} collective-permute-done((bf16[1024,256]{1,0:T(8,128)(2,1)S(1)}, bf16[1024,256]{1,0:T(8,128)(2,1)S(1)}, u32[]{:S(2)}, u32[]{:S(2)}) %collective-permute-start.8) | collective-permute-done | bytes 524320 | tf_op jit(solution)/shard_map/ppermute | solution.py:362
  145.6 10.4 %collective-permute-done.14 = bf16[1024,256]{1,0:T(8,128)(2,1)S(1)} collective-permute-done((bf16[1024,256]{1,0:T(8,128)(2,1)S(1)}, bf16[1024,256]{1,0:T(8,128)(2,1)S(1)}, u32[]{:S(2)}, u32[]{:S(2)}) %collective-permute-start.14) | collective-permute-done | bytes 524320 | tf_op jit(solution)/shard_map/ppermute | solution.py:362
  156.8 5.2 %collective-permute-done.11 = bf16[1024,256]{1,0:T(8,128)(2,1)S(1)} collective-permute-done((bf16[1024,256]{1,0:T(8,128)(2,1)S(1)}, bf16[1024,256]{1,0:T(8,128)(2,1)S(1)}, u32[]{:S(2)}, u32[]{:S(2)}) %collective-permute-start.11) | collective-permute-done | bytes 524320 | tf_op jit(solution)/shard_map/ppermute | solution.py:362
  (65 shorter events, 9.5 us)
Async XLA Ops:
  7.2 15.8 %copy-start = (bf16[1024,1024]{1,0:T(8,128)(2,1)S(1)}, bf16[1024,1024]{1,0:T(8,128)(2,1)}, u32[]{:S(2)}) copy-start(bf16[1024,1024]{1,0:T(8,128)(2,1)} %right_ref.5) | copy-start | bytes 6291460
  7.2 155.7 %reduce-scatter.3.cloned.1.call-start = ((), (), s32[]{:S(2)}) async-start(), calls=%async_computation.2 | async-start | bytes 2621440 | tf_op jit(solution)/shard_map/reduce_scatter | solution.py:395
  7.2 1.7 %copy-start.1 = (bf16[1024,1024]{1,0:T(8,128)(2,1)S(1)}, bf16[1024,1024]{1,0:T(8,128)(2,1)}, u32[]{:S(2)}) copy-start(bf16[1024,1024]{1,0:T(8,128)(2,1)} %right_ref.4) | copy-start | bytes 6291460
  9.0 1.0 copy-start.19
  10.0 1.0 copy-start.21
  11.0 11.9 %copy-start.6 = (bf16[1024,256]{1,0:T(8,128)(2,1)S(1)}, bf16[1024,256]{1,0:T(8,128)(2,1)}, u32[]{:S(2)}) copy-start(bf16[1024,256]{1,0:T(8,128)(2,1)} %refs_1_.1) | copy-start | bytes 1572868
  11.0 12.0 %copy-start.9 = (bf16[1024,256]{1,0:T(8,128)(2,1)S(1)}, bf16[1024,256]{1,0:T(8,128)(2,1)}, u32[]{:S(2)}) copy-start(bf16[1024,256]{1,0:T(8,128)(2,1)} %refs_3_.1) | copy-start | bytes 1572868
  17.3 11.8 %collective-permute-start = (bf16[128,512]{1,0:T(8,128)(2,1)S(1)}, bf16[128,512]{1,0:T(8,128)(2,1)S(1)}, u32[]{:S(2)}, u32[]{:S(2)}) collective-permute-start(bf16[128,512]{1,0:T(8,128)(2,1)S(1)} %get-tuple-element.39), channel_id=1, source_target_pairs={{0,4},{4,0},{8,12},{12,8},{1,5},{5,1},{9,13},{13,9},{2,6},{6,2},{1... | collective-permute-start | bytes 393224 | tf_op jit(solution)/shard_map/ppermute | solution.py:343
  20.4 6.5 %collective-permute-start.1 = (bf16[64,512]{1,0:T(8,128)(2,1)S(1)}, bf16[64,512]{1,0:T(8,128)(2,1)S(1)}, u32[]{:S(2)}, u32[]{:S(2)}) collective-permute-start(bf16[64,512]{1,0:T(8,128)(2,1)S(1)} %get-tuple-element.40), channel_id=1, source_target_pairs={{0,8},{4,12},{8,0},{12,4},{1,9},{5,13},{9,1},{13,5},{2,10},{6,14},... | collective-permute-start | bytes 196616 | tf_op jit(solution)/shard_map/ppermute | solution.py:343
  23.0 6.1 %collective-permute-start.2 = (bf16[64,512]{1,0:T(8,128)(2,1)S(1)}, bf16[64,512]{1,0:T(8,128)(2,1)S(1)}, u32[]{:S(2)}, u32[]{:S(2)}) collective-permute-start(bf16[64,512]{1,0:T(8,128)(2,1)S(1)} %get-tuple-element.40), channel_id=1, source_target_pairs={{0,12},{4,8},{8,4},{12,0},{1,13},{5,9},{9,5},{13,1},{2,14},{6,10},... | collective-permute-start | bytes 196616 | tf_op jit(solution)/shard_map/ppermute | solution.py:343
  39.6 1.3 copy-start.7
  40.9 0.8 copy-start.11
  41.7 0.8 copy-start.13
  42.5 0.8 copy-start.15
  43.3 0.8 copy-start.23
  45.4 1.3 copy-start.4
  46.8 116.0 %reduce-scatter.5.cloned.1.call-start = ((), (), s32[]{:S(2)}) async-start(), calls=%async_computation.3 | async-start | bytes 2621440 | tf_op jit(solution)/shard_map/reduce_scatter | solution.py:402
  46.8 8.5 %collective-permute-start.3 = (bf16[128,512]{1,0:T(8,128)(2,1)S(1)}, bf16[128,512]{1,0:T(8,128)(2,1)S(1)}, u32[]{:S(2)}, u32[]{:S(2)}) collective-permute-start(bf16[128,512]{1,0:T(8,128)(2,1)S(1)} %get-tuple-element.46), channel_id=1, source_target_pairs={{0,4},{4,0},{8,12},{12,8},{1,5},{5,1},{9,13},{13,9},{2,6},{6,2},{1... | collective-permute-start | bytes 393224 | tf_op jit(solution)/shard_map/ppermute | solution.py:343
  48.0 5.3 %collective-permute-start.4 = (bf16[64,512]{1,0:T(8,128)(2,1)S(1)}, bf16[64,512]{1,0:T(8,128)(2,1)S(1)}, u32[]{:S(2)}, u32[]{:S(2)}) collective-permute-start(bf16[64,512]{1,0:T(8,128)(2,1)S(1)} %get-tuple-element.47), channel_id=1, source_target_pairs={{0,8},{4,12},{8,0},{12,4},{1,9},{5,13},{9,1},{13,5},{2,10},{6,14},... | collective-permute-start | bytes 196616 | tf_op jit(solution)/shard_map/ppermute | solution.py:343
  49.2 6.1 %collective-permute-start.5 = (bf16[64,512]{1,0:T(8,128)(2,1)S(1)}, bf16[64,512]{1,0:T(8,128)(2,1)S(1)}, u32[]{:S(2)}, u32[]{:S(2)}) collective-permute-start(bf16[64,512]{1,0:T(8,128)(2,1)S(1)} %get-tuple-element.48), channel_id=1, source_target_pairs={{0,12},{4,8},{8,4},{12,0},{1,13},{5,9},{9,5},{13,1},{2,14},{6,10},... | collective-permute-start | bytes 196616 | tf_op jit(solution)/shard_map/ppermute | solution.py:343
  55.3 1.7 copy-start.8
  57.0 1.0 copy-start.12
  58.0 4.2 %copy-start.10 = (bf16[1024,256]{1,0:T(8,128)(2,1)S(1)}, bf16[1024,256]{1,0:T(8,128)(2,1)}, u32[]{:S(2)}) copy-start(bf16[1024,256]{1,0:T(8,128)(2,1)} %refs_3_.1) | copy-start | bytes 1572868
  58.0 4.2 %copy-start.20 = (bf16[1024,256]{1,0:T(8,128)(2,1)S(1)}, bf16[1024,256]{1,0:T(8,128)(2,1)}, u32[]{:S(2)}) copy-start(bf16[1024,256]{1,0:T(8,128)(2,1)} %refs_4_.1) | copy-start | bytes 1572868
  58.0 4.2 %copy-start.22 = (bf16[1024,256]{1,0:T(8,128)(2,1)S(1)}, bf16[1024,256]{1,0:T(8,128)(2,1)}, u32[]{:S(2)}) copy-start(bf16[1024,256]{1,0:T(8,128)(2,1)} %refs_5_.1) | copy-start | bytes 1572868
  58.0 4.2 %copy-start.24 = (bf16[1024,256]{1,0:T(8,128)(2,1)S(1)}, bf16[1024,256]{1,0:T(8,128)(2,1)}, u32[]{:S(2)}) copy-start(bf16[1024,256]{1,0:T(8,128)(2,1)} %copy-done.23) | copy-start | bytes 1572868
  61.2 1.0 copy-start.17
  64.7 1.3 copy-start.5
  66.0 1.0 copy-start.16
  66.1 6.5 %copy-start.2 = (bf16[1024,1024]{1,0:T(8,128)(2,1)S(1)}, bf16[1024,1024]{1,0:T(8,128)(2,1)}, u32[]{:S(2)}) copy-start(bf16[1024,1024]{1,0:T(8,128)(2,1)} %right_ref.4) | copy-start | bytes 6291460
  66.1 6.5 %copy-start.14 = (bf16[256,1024]{1,0:T(8,128)(2,1)S(1)}, bf16[256,1024]{1,0:T(8,128)(2,1)}, u32[]{:S(2)}) copy-start(bf16[256,1024]{1,0:T(8,128)(2,1)} %copy-done.13) | copy-start | bytes 1572868
  68.9 7.6 %copy-start.3 = (bf16[1024,1024]{1,0:T(8,128)(2,1)S(1)}, bf16[1024,1024]{1,0:T(8,128)(2,1)}, u32[]{:S(2)}) copy-start(bf16[1024,1024]{1,0:T(8,128)(2,1)} %right_ref.4) | copy-start | bytes 6291460
  68.9 15.2 %collective-permute-start.15 = (bf16[1024,256]{1,0:T(8,128)(2,1)S(1)}, bf16[1024,256]{1,0:T(8,128)(2,1)}, u32[]{:S(2)}, u32[]{:S(2)}) collective-permute-start(bf16[1024,256]{1,0:T(8,128)(2,1)S(1)} %shard_map.117), channel_id=1, source_target_pairs={{0,4},{12,8},{1,5},{13,9},{2,6},{14,10},{3,7},{15,11},{16,20},{28,... | collective-permute-start | bytes 1572872 | tf_op jit(solution)/shard_map/ppermute | solution.py:360
  74.4 21.0 %collective-permute-start.6 = (bf16[1024,256]{1,0:T(8,128)(2,1)S(1)}, bf16[1024,256]{1,0:T(8,128)(2,1)}, u32[]{:S(2)}, u32[]{:S(2)}) collective-permute-start(bf16[1024,256]{1,0:T(8,128)(2,1)S(1)} %shard_map.115), channel_id=1, source_target_pairs={{0,4},{12,8},{1,5},{13,9},{2,6},{14,10},{3,7},{15,11},{16,20},{28,... | collective-permute-start | bytes 1572872 | tf_op jit(solution)/shard_map/ppermute | solution.py:360
  76.5 1.2 copy-start.18
  80.0 26.6 %collective-permute-start.12 = (bf16[1024,256]{1,0:T(8,128)(2,1)S(1)}, bf16[1024,256]{1,0:T(8,128)(2,1)S(1)}, u32[]{:S(2)}, u32[]{:S(2)}) collective-permute-start(bf16[1024,256]{1,0:T(8,128)(2,1)S(1)} %get-tuple-element.54), channel_id=1, source_target_pairs={{0,4},{12,8},{1,5},{13,9},{2,6},{14,10},{3,7},{15,11},{16,20},{28,... | collective-permute-start | bytes 1572872 | tf_op jit(solution)/shard_map/ppermute | solution.py:360
  81.4 31.8 %collective-permute-start.9 = (bf16[1024,256]{1,0:T(8,128)(2,1)S(1)}, bf16[1024,256]{1,0:T(8,128)(2,1)S(1)}, u32[]{:S(2)}, u32[]{:S(2)}) collective-permute-start(bf16[1024,256]{1,0:T(8,128)(2,1)S(1)} %get-tuple-element.53), channel_id=1, source_target_pairs={{0,4},{12,8},{1,5},{13,9},{2,6},{14,10},{3,7},{15,11},{16,20},{28,... | collective-permute-start | bytes 1572872 | tf_op jit(solution)/shard_map/ppermute | solution.py:360
  85.3 28.7 %collective-permute-start.16 = (bf16[1024,256]{1,0:T(8,128)(2,1)S(1)}, bf16[1024,256]{1,0:T(8,128)(2,1)S(1)}, u32[]{:S(2)}, u32[]{:S(2)}) collective-permute-start(bf16[1024,256]{1,0:T(8,128)(2,1)S(1)} %add_convert_fusion.1), channel_id=1, source_target_pairs={{4,8},{8,4},{5,9},{9,5},{6,10},{10,6},{7,11},{11,7},{20,24},{24,20... | collective-permute-start | bytes 1572872 | tf_op jit(solution)/shard_map/ppermute | solution.py:361
  96.5 18.9 %collective-permute-start.7 = (bf16[1024,256]{1,0:T(8,128)(2,1)S(1)}, bf16[1024,256]{1,0:T(8,128)(2,1)S(1)}, u32[]{:S(2)}, u32[]{:S(2)}) collective-permute-start(bf16[1024,256]{1,0:T(8,128)(2,1)S(1)} %add_convert_fusion.7), channel_id=1, source_target_pairs={{4,8},{8,4},{5,9},{9,5},{6,10},{10,6},{7,11},{11,7},{20,24},{24,20... | collective-permute-start | bytes 1572872 | tf_op jit(solution)/shard_map/ppermute | solution.py:361
  106.7 10.2 %collective-permute-start.13 = (bf16[1024,256]{1,0:T(8,128)(2,1)S(1)}, bf16[1024,256]{1,0:T(8,128)(2,1)S(1)}, u32[]{:S(2)}, u32[]{:S(2)}) collective-permute-start(bf16[1024,256]{1,0:T(8,128)(2,1)S(1)} %add_convert_fusion.3), channel_id=1, source_target_pairs={{4,8},{8,4},{5,9},{9,5},{6,10},{10,6},{7,11},{11,7},{20,24},{24,20... | collective-permute-start | bytes 1572872 | tf_op jit(solution)/shard_map/ppermute | solution.py:361
  113.3 5.1 %collective-permute-start.10 = (bf16[1024,256]{1,0:T(8,128)(2,1)S(1)}, bf16[1024,256]{1,0:T(8,128)(2,1)S(1)}, u32[]{:S(2)}, u32[]{:S(2)}) collective-permute-start(bf16[1024,256]{1,0:T(8,128)(2,1)S(1)} %add_convert_fusion.5), channel_id=1, source_target_pairs={{4,8},{8,4},{5,9},{9,5},{6,10},{10,6},{7,11},{11,7},{20,24},{24,20... | collective-permute-start | bytes 1572872 | tf_op jit(solution)/shard_map/ppermute | solution.py:361
  114.2 19.3 %collective-permute-start.17 = (bf16[1024,256]{1,0:T(8,128)(2,1)S(1)}, bf16[1024,256]{1,0:T(8,128)(2,1)S(1)}, u32[]{:S(2)}, u32[]{:S(2)}) collective-permute-start(bf16[1024,256]{1,0:T(8,128)(2,1)S(1)} %add_convert_fusion), channel_id=1, source_target_pairs={{4,0},{8,12},{5,1},{9,13},{6,2},{10,14},{7,3},{11,15},{20,16},{24,... | collective-permute-start | bytes 1572872 | tf_op jit(solution)/shard_map/ppermute | solution.py:362
  115.6 29.1 %collective-permute-start.8 = (bf16[1024,256]{1,0:T(8,128)(2,1)S(1)}, bf16[1024,256]{1,0:T(8,128)(2,1)S(1)}, u32[]{:S(2)}, u32[]{:S(2)}) collective-permute-start(bf16[1024,256]{1,0:T(8,128)(2,1)S(1)} %add_convert_fusion.6), channel_id=1, source_target_pairs={{4,0},{8,12},{5,1},{9,13},{6,2},{10,14},{7,3},{11,15},{20,16},{24,... | collective-permute-start | bytes 1572872 | tf_op jit(solution)/shard_map/ppermute | solution.py:362
  117.1 38.9 %collective-permute-start.14 = (bf16[1024,256]{1,0:T(8,128)(2,1)S(1)}, bf16[1024,256]{1,0:T(8,128)(2,1)S(1)}, u32[]{:S(2)}, u32[]{:S(2)}) collective-permute-start(bf16[1024,256]{1,0:T(8,128)(2,1)S(1)} %add_convert_fusion.2), channel_id=1, source_target_pairs={{4,0},{8,12},{5,1},{9,13},{6,2},{10,14},{7,3},{11,15},{20,16},{24,... | collective-permute-start | bytes 1572872 | tf_op jit(solution)/shard_map/ppermute | solution.py:362
  118.5 43.5 %collective-permute-start.11 = (bf16[1024,256]{1,0:T(8,128)(2,1)S(1)}, bf16[1024,256]{1,0:T(8,128)(2,1)S(1)}, u32[]{:S(2)}, u32[]{:S(2)}) collective-permute-start(bf16[1024,256]{1,0:T(8,128)(2,1)S(1)} %add_convert_fusion.4), channel_id=1, source_target_pairs={{4,0},{8,12},{5,1},{9,13},{6,2},{10,14},{7,3},{11,15},{20,16},{24,... | collective-permute-start | bytes 1572872 | tf_op jit(solution)/shard_map/ppermute | solution.py:362
Sparse Core Ops, SparseCore 0:
  46.9 30.7 reduce-scatter.2
  81.0 31.4 reduce-scatter.4

commit v2 on v1

v2 whole, which is shorter than its diff:
```python
import functools
import math

import jax
import jax.numpy as jnp
from jax import lax
from jax.experimental import pallas as pl
from jax.experimental.pallas import tpu as pltpu
from jax.sharding import PartitionSpec as P

HEAD_DIM = 128
BLOCK = 128
BF16 = jnp.bfloat16
F32 = jnp.float32
MIB = 1024 * 1024

NN = (((1,), (0,)), ((), ()))
NT = (((1,), (1,)), ((), ()))
TN = (((0,), (0,)), ((), ()))


def dot(left, right, dims=NN):
    return lax.dot_general(left, right, dims, preferred_element_type=F32)


def params():
    return pltpu.CompilerParams(vmem_limit_bytes=56 * MIB)


def cost(flops, moved, exps=0):
    return pl.CostEstimate(flops=int(flops), bytes_accessed=int(moved), transcendentals=int(exps))


def shape(rows, cols, dtype=BF16):
    return jax.ShapeDtypeStruct((rows, cols), dtype)


def whole(rows, cols):
    return pl.BlockSpec((rows, cols), lambda *_: (0, 0))


def pool_matrix(rows):
    row = lax.broadcasted_iota(jnp.int32, (rows // 2, rows), 0)
    col = lax.broadcasted_iota(jnp.int32, (rows // 2, rows), 1)
    return jnp.where(jnp.right_shift(col, 1) == row, 0.5, 0.0).astype(BF16)


def spread_matrix(rows, step_bits, offset, cols, weight):
    row = lax.broadcasted_iota(jnp.int32, (rows, cols), 0) + offset
    col = lax.broadcasted_iota(jnp.int32, (rows, cols), 1)
    return jnp.where(jnp.right_shift(row, step_bits) == col, weight, 0.0).astype(BF16)


def key_value_body(local_levels, far_levels, tok_ref, wk_ref, wv_ref, *outs):
    kv_ref = outs[0]
    mid = outs[1:local_levels]
    far = outs[local_levels:-1]
    top_ref = outs[-1]
    step = pl.program_id(0)
    part = 2 * BLOCK
    parts = tok_ref.shape[0] // part
    for p in range(parts):
        x = tok_ref[p * part : (p + 1) * part, :]
        rows = jnp.concatenate([dot(x, wk_ref[...]), dot(x, wv_ref[...])], axis=1).astype(BF16)
        kv_ref[p * part : (p + 1) * part, :] = rows
        for ref in mid:
            rows = dot(pool_matrix(rows.shape[0]), rows).astype(BF16)
            ref[p * rows.shape[0] : (p + 1) * rows.shape[0], :] = rows
        rows = dot(pool_matrix(rows.shape[0]), rows).astype(BF16)
        count = rows.shape[0]
        top_ref[pl.ds(pl.multiple_of((step * parts + p) * count, count), count), :] = rows

    @pl.when(step == pl.num_programs(0) - 1)
    def _():
        rows = top_ref[...]
        for i in range(far_levels):
            if i:
                rows = dot(pool_matrix(rows.shape[0]), rows).astype(BF16)
            far[i][...] = rows


def key_value(tokens, w_key, w_value, local_levels, far_levels):
    tok_rows, width = tokens.shape
    inner = w_key.shape[1]
    tile = 4 * BLOCK
    out_shape, out_specs = [], []
    for i in range(local_levels):
        out_shape += [shape(tok_rows >> i, 2 * inner)]
        out_specs += [pl.BlockSpec((tile >> i, 2 * inner), lambda i: (i, 0))]
    for i in range(far_levels):
        out_shape += [shape(BLOCK >> i, 2 * inner)]
        out_specs += [whole(BLOCK >> i, 2 * inner)]
    return pl.pallas_call(
        functools.partial(key_value_body, local_levels, far_levels),
        grid=(tok_rows // tile,),
        in_specs=[
            pl.BlockSpec((tile, width), lambda i: (i, 0)),
            whole(width, inner),
            whole(width, inner),
        ],
        out_specs=out_specs,
        out_shape=out_shape,
        scratch_shapes=[pltpu.VMEM((BLOCK, 2 * inner), BF16)],
        compiler_params=params(),
        cost_estimate=cost(4 * tok_rows * width * inner, 2 * tok_rows * width + 8 * width * inner),
    )(tokens, w_key, w_value)


def pair_body(a_ref, b_ref, wa_ref, wb_ref, x_ref, y_ref):
    x_ref[...] = dot(a_ref[...], wa_ref[...]).astype(BF16)
    y_ref[...] = dot(b_ref[...], wb_ref[...]).astype(BF16)


def project_pair(a, b, wa, wb):
    tok_rows, width = a.shape
    inner = wa.shape[1]
    tile = 2 * BLOCK
    rows = pl.BlockSpec((tile, width), lambda i: (i, 0))
    outs = pl.BlockSpec((tile, inner), lambda i: (i, 0))
    return pl.pallas_call(
        pair_body,
        grid=(tok_rows // tile,),
        in_specs=[rows, rows, whole(width, inner), whole(width, inner)],
        out_specs=[outs, outs],
        out_shape=[shape(tok_rows, inner)] * 2,
        compiler_params=params(),
        cost_estimate=cost(4 * tok_rows * width * inner, 4 * tok_rows * width + 8 * width * inner),
    )(a, b, wa, wb)


def attention_body(local_levels, far_bits, *refs):
    mids = local_levels - 1
    fars = len(far_bits)
    q_ref, g_ref, kv_ref = refs[:3]
    mid_refs = refs[3 : 3 + mids]
    far_refs = refs[3 + mids : 3 + mids + fars]
    outs = refs[3 + mids + fars :]
    att_ref, att_t_ref, dq_ref, dq_t_ref, dkv_ref = outs[:5]
    dmid_refs = outs[5 : 5 + mids]
    dfar_refs = outs[5 + mids : 5 + mids + fars]
    acc_ref = outs[-1]
    inner = q_ref.shape[1]
    heads = inner // HEAD_DIM
    pair = 2 * BLOCK
    m = pl.program_id(0)
    score_scale = 1.0 / math.sqrt(HEAD_DIM)
    sizes = [pair] + [BLOCK] * mids + [r.shape[0] for r in far_refs]
    biases = [0.0] + [i * math.log(2.0) for i in range(1, local_levels)]
    biases += [(local_levels + bit) * math.log(2.0) for bit in far_bits]
    starts = [sum(sizes[:i]) for i in range(len(sizes))]
    seats = []
    for i in range(1, local_levels):
        sibling = jnp.bitwise_xor(jnp.right_shift(m, i - 1), 1)
        seats.append(pl.ds(pl.multiple_of(sibling * BLOCK, BLOCK), BLOCK))

    @pl.when(m == 0)
    def _():
        for ref in (*dmid_refs, acc_ref):
            ref[...] = jnp.zeros_like(ref)

    def rows_of(cols):
        rows = [kv_ref[:, cols]]
        rows += [ref[seat, cols] for ref, seat in zip(mid_refs, seats)]
        rows += [ref[:, cols] for ref in far_refs]
        return jnp.concatenate(rows, axis=0)

    for h in range(heads):
        low = h * HEAD_DIM
        cols = slice(low, low + HEAD_DIM)
        vcols = slice(inner + low, inner + low + HEAD_DIM)
        keys = rows_of(cols)
        values = rows_of(vcols)
        q = q_ref[:, cols]
        g = g_ref[:, cols]
        raw = dot(keys, q, NT)
        scores = jnp.concatenate(
            [
                raw[start : start + size] * score_scale + bias
                for start, size, bias in zip(starts, sizes, biases)
            ],
            axis=0,
        )
        expo = jnp.exp(scores - jnp.max(scores, axis=0, keepdims=True))
        probs = expo * (1.0 / jnp.sum(expo, axis=0, keepdims=True))
        probs_b = probs.astype(BF16)
        att_t = dot(values, probs_b, TN).astype(BF16)
        att_t_ref[cols, :] = att_t
        att_ref[:, cols] = att_t.T
        delta = jnp.sum(g.T.astype(F32) * att_t.astype(F32), axis=0, keepdims=True)
        dprobs = dot(values, g, NT)
        grads = (probs * (dprobs - delta) * score_scale).astype(BF16)
        dq_t = dot(keys, grads, TN).astype(BF16)
        dq_t_ref[cols, :] = dq_t
        dq_ref[:, cols] = dq_t.T
        for part, place in ((dot(grads, q), cols), (dot(probs_b, g), vcols)):
            dkv_ref[:, place] = part[:pair]
            for i in range(mids):
                start = starts[1 + i]
                dmid_refs[i][seats[i], place] += part[start : start + BLOCK]
            acc_ref[:, place] += part[starts[1 + mids] :]

    @pl.when(m == pl.num_programs(0) - 1)
    def _():
        base = starts[1 + mids]
        for ref, start, size in zip(dfar_refs, starts[1 + mids :], sizes[1 + mids :]):
            ref[...] = acc_ref[start - base : start - base + size].astype(BF16)


def attention(query, grad, levels, fars, far_bits):
    tok_rows, inner = query.shape
    local_levels = len(levels)
    far_rows = sum(f.shape[0] for f in fars)
    set_rows = (local_levels + 1) * BLOCK + far_rows
    pair = 2 * BLOCK
    rows = pl.BlockSpec((pair, inner), lambda i: (i, 0))
    cols = pl.BlockSpec((inner, pair), lambda i: (0, i))
    both = pl.BlockSpec((pair, 2 * inner), lambda i: (i, 0))
    others = [*levels[1:], *fars]
    out_shape = [
        shape(tok_rows, inner),
        shape(inner, tok_rows),
        shape(tok_rows, inner),
        shape(inner, tok_rows),
        shape(tok_rows, 2 * inner, F32),
    ]
    out_shape += [shape(*level.shape, F32) for level in levels[1:]]
    out_shape += [shape(*f.shape) for f in fars]
    return pl.pallas_call(
        functools.partial(attention_body, local_levels, far_bits),
        grid=(tok_rows // pair,),
        in_specs=[rows, rows, both] + [whole(*x.shape) for x in others],
        out_specs=[rows, cols, rows, cols, both] + [whole(*x.shape) for x in others],
        out_shape=out_shape,
        scratch_shapes=[pltpu.VMEM((far_rows, 2 * inner), F32)],
        compiler_params=params(),
        cost_estimate=cost(
            12 * tok_rows * set_rows * inner, 24 * tok_rows * inner, tok_rows * set_rows * 2
        ),
    )(query, grad, *levels, *fars)


def term_body(left_ref, right_ref, out_ref):
    out_ref[...] = dot(left_ref[...], right_ref[...]).astype(BF16).T


def weight_terms(left_t, right, inner, which, part, parts):
    tok_rows = left_t.shape[1]
    width = right.shape[1] // parts
    tile = 256
    steps = width // tile
    return pl.pallas_call(
        term_body,
        grid=(steps,),
        in_specs=[
            pl.BlockSpec((inner, tok_rows), lambda i: (which, 0)),
            pl.BlockSpec((tok_rows, tile), lambda i: (0, part * steps + i)),
        ],
        out_specs=pl.BlockSpec((tile, inner), lambda i: (i, 0)),
        out_shape=shape(width, inner),
        compiler_params=params(),
        cost_estimate=cost(2 * inner * tok_rows * width, 2 * tok_rows * (width + inner)),
    )(left_t, right)


def close_body(local_levels, far_bits, dkv_ref, *refs):
    mids = local_levels - 1
    dmid_refs = refs[:mids]
    back_refs = refs[mids : mids + len(far_bits)]
    dk_ref, dv_ref, dkv_t_ref = refs[mids + len(far_bits) :]
    tile = dkv_ref.shape[0]
    offset = pl.program_id(0) * tile
    inner = dk_ref.shape[1]
    total = dkv_ref[...]
    chain = None
    for i in reversed(range(mids)):
        chain = dmid_refs[i][...] if chain is None else dmid_refs[i][...] + chain
        high = chain.astype(BF16)
        low = (chain - high.astype(F32)).astype(BF16)
        rows = chain.shape[0]
        fan = spread_matrix(2 * rows, 1, 0, rows, 0.5)
        chain = dot(fan, high) + dot(fan, low)
    if chain is not None:
        total = total + chain
    for ref, bit in zip(back_refs, far_bits):
        weight = 0.5 ** (local_levels + bit)
        fan = spread_matrix(tile, local_levels + bit, offset, ref.shape[0], weight)
        total = total + dot(fan, ref[...])
    final = total.astype(BF16)
    dk_ref[...] = final[:, :inner]
    dv_ref[...] = final[:, inner:]
    dkv_t_ref[...] = final.T


def close_keys(dkv, dmids, backs, far_bits, local_levels):
    tok_rows, double = dkv.shape
    inner = double // 2
    tile = 2 * BLOCK
    in_specs = [pl.BlockSpec((tile, double), lambda i: (i, 0))]
    in_specs += [pl.BlockSpec((tile >> i, double), lambda i: (i, 0)) for i in range(1, local_levels)]
    in_specs += [whole(*b.shape) for b in backs]
    return pl.pallas_call(
        functools.partial(close_body, local_levels, far_bits),
        grid=(tok_rows // tile,),
        in_specs=in_specs,
        out_specs=[
            pl.BlockSpec((tile, inner), lambda i: (i, 0)),
            pl.BlockSpec((tile, inner), lambda i: (i, 0)),
            pl.BlockSpec((double, tile), lambda i: (0, i)),
        ],
        out_shape=[shape(tok_rows, inner), shape(tok_rows, inner), shape(double, tok_rows)],
        compiler_params=params(),
        cost_estimate=cost(4 * tok_rows * 256 * double, 20 * tok_rows * double),
    )(dkv, *dmids, *backs)


def out_body(count, *refs):
    total = None
    for i in range(count):
        part = dot(refs[i][...], refs[count + i][...], NT)
        total = part if total is None else total + part
    refs[-1][...] = total.astype(BF16)


def project_out(lefts, weights):
    count = len(lefts)
    tok_rows, inner = lefts[0].shape
    width = weights[0].shape[0]
    tile = 2 * BLOCK
    return pl.pallas_call(
        functools.partial(out_body, count),
        grid=(tok_rows // tile,),
        in_specs=[pl.BlockSpec((tile, inner), lambda i: (i, 0))] * count
        + [whole(width, inner)] * count,
        out_specs=pl.BlockSpec((tile, width), lambda i: (i, 0)),
        out_shape=shape(tok_rows, width),
        compiler_params=params(),
        cost_estimate=cost(2 * count * tok_rows * inner * width, 2 * tok_rows * width),
    )(*lefts, *weights)


def exchange(block, axis, distance):
    count = lax.axis_size(axis)
    return lax.ppermute(block, axis, [(i, i ^ distance) for i in range(count)])


def add(left, right):
    return (left.astype(F32) + right.astype(F32)).astype(BF16)


def combine_body(own_ref, into_ref, half_ref, across_ref, next_ref, total_ref):
    next_ref[...] = (own_ref[...].astype(F32) + into_ref[...].astype(F32)).astype(BF16)
    total_ref[...] = (half_ref[...].astype(F32) + across_ref[...].astype(F32)).astype(BF16)


def combine(own, into, half, across):
    return pl.pallas_call(
        combine_body,
        out_shape=[shape(*own.shape), shape(*half.shape)],
        compiler_params=pltpu.CompilerParams(vmem_limit_bytes=8 * MIB),
        cost_estimate=cost(2 * own.size, 12 * own.size),
    )(own, into, half, across)


def line_sums(chunks, axis):
    count = lax.axis_size(axis)
    if count < 4:
        return [add(c, exchange(c, axis, 1)) if count == 2 else c for c in chunks]
    rank = jnp.bitwise_and(lax.axis_index(axis), 3)
    at_end = (rank == 0) | (rank == 3)
    inward, across, outward = [], [], []
    for base in range(0, count, 4):
        inward += [(base, base + 1), (base + 3, base + 2)]
        across += [(base + 1, base + 2), (base + 2, base + 1)]
        outward += [(base + 1, base), (base + 2, base + 3)]
    lag = 2
    halves, crossed, totals, sums = [], [], [], []
    for k in range(len(chunks) + lag):
        if k < len(chunks):
            into = lax.ppermute(chunks[k], axis, inward)
        if k < lag:
            halves.append(add(chunks[k], into))
        elif k < len(chunks):
            half, total = combine(chunks[k], into, halves[k - lag], crossed[k - lag])
            halves.append(half)
            totals.append(total)
        else:
            totals.append(add(halves[k - lag], crossed[k - lag]))
        if k < len(chunks):
            crossed.append(lax.ppermute(halves[k], axis, across))
    for total in totals:
        ends = lax.ppermute(total, axis, outward)
        result = jnp.where(at_end, ends, total)
        distance = 4
        while distance < count:
            result = add(result, exchange(result, axis, distance))
            distance *= 2
        sums.append(result)
    return sums


def per_device(tokens, w_query, w_key, w_value, w_out, cotangent):
    tok_rows = tokens.shape[0]
    inner = w_query.shape[1]
    local_levels = (tok_rows // BLOCK).bit_length() - 1
    count = lax.axis_size("seq")
    far_levels = count.bit_length() - 1
    far_bits = [d.bit_length() - 1 for d in range(1, count)]

    parts = key_value(tokens, w_key, w_value, local_levels, far_levels)
    levels = parts[:local_levels]
    tops = parts[local_levels:]
    fars = [exchange(tops[bit], "seq", d) for d, bit in enumerate(far_bits, 1)]
    query, grad = project_pair(tokens, cotangent, w_query, w_out)
    results = attention(query, grad, levels, fars, far_bits)
    attended, attended_t, dquery, dquery_t, dkv = results[:5]
    dmids = results[5 : 5 + local_levels - 1]
    dfars = results[5 + local_levels - 1 :]
    backs = [exchange(piece, "seq", d) for d, piece in enumerate(dfars, 1)]
    mixed_part = project_out([attended], [w_out])
    mixed = lax.psum_scatter(mixed_part, "head", scatter_dimension=1, tiled=True)
    dkey, dvalue, dkv_t = close_keys(dkv, dmids, backs, far_bits, local_levels)
    grad_part = project_out([dquery, dkey, dvalue], [w_query, w_key, w_value])
    tokens_grad = lax.psum_scatter(grad_part, "head", scatter_dimension=1, tiled=True)

    pieces = 2
    chunks = []
    for left, which, right in (
        (attended_t, 0, cotangent),
        (dquery_t, 0, tokens),
        (dkv_t, 0, tokens),
        (dkv_t, 1, tokens),
    ):
        chunks += [weight_terms(left, right, inner, which, p, pieces) for p in range(pieces)]
    sums = line_sums(chunks, "seq")
    out_grad, query_grad, key_grad, value_grad = (
        jnp.concatenate(sums[i : i + pieces], axis=0) for i in range(0, len(sums), pieces)
    )
    return mixed, tokens_grad, query_grad, key_grad, value_grad, out_grad


def solution(mesh):
    return jax.shard_map(
        per_device,
        mesh=mesh,
        in_specs=(
            P(("groups", "seq"), None),
            P(None, "head"),
            P(None, "head"),
            P(None, "head"),
            P(None, "head"),
            P(("groups", "seq"), None),
        ),
        out_specs=(
            P(("groups", "seq"), "head"),
            P(("groups", "seq"), "head"),
            P("groups", "head"),
            P("groups", "head"),
            P("groups", "head"),
            P("groups", "head"),
        ),
        check_vma=False,
    )
```

time: 170 us -> 159 us (0.935)
  waiting for transfers between devices: 73.9 us -> 26.6 us
  Pallas kernels: 31.4 us -> 62.1 us
  starting transfers between devices: 26.6 us -> 49.5 us
  local copies, waits for them, and re-layouts: 16.9 us -> 1.38 us
  other arithmetic: 6.53 us -> 3.81 us
    ppermute x12 -> x24, waiting for transfers between devices: 65.5 us -> 25.2 us  [the longest x8 22.4 us: line_sums(): ends = lax.ppermute(total, axis, outward)]
    ppermute x12 -> x24, starting transfers between devices: 16.4 us -> 39.3 us  [the longest x8 23.3 us: line_sums(): into = lax.ppermute(chunks[k], axis, inward)]
    pallas_call x3 -> x14, Pallas kernels: 5.87 us -> 21.8 us  [the longest x8 21 us: weight_terms(): pl.pallas_call(term_body, grid=(steps,), in_specs=[pl.BlockSpec((inner, t...]
    unnamed x50 -> x34, local copies, waits for them, and re-layouts: 16.9 us -> 1.38 us
    ppermute x6, waiting for transfers between devices: 8.32 us -> 1.33 us  [exchange(): return lax.ppermute(block, axis, [(i, i ^ distance) for i in range(count)])]
    pallas_call x2, Pallas kernels: 3.81 us -> 9.89 us  [project_out(): pl.pallas_call(functools.partial(out_body, count), grid=(tok_rows // tile...]
    concatenate x0 -> x4, other arithmetic: none -> 3.31 us  [per_device(): jnp.concatenate(sums[i:i + pieces], axis=0)]
    pallas_call x1, Pallas kernels: 1.8 us -> 5.09 us  [project_pair(): pl.pallas_call(pair_body, grid=(tok_rows // tile,), in_specs=[rows, rows,...]
  transfers between devices with their start and end apart: 20 -> 32, of which waited for: 12 -> 9; matrix products, arithmetic and copies ran while one was open for 4% -> 2% of each run, Pallas kernels for 8% -> 24%
where the time goes in v2:
time: 159 us; the launch traced here: 158 us
  Pallas kernels  62.1 us (39%)
  starting transfers between devices  49.5 us (31%)
  waiting for transfers between devices  26.6 us (17%)
  between operations  14.6 us (9%)
  other arithmetic  3.81 us (2%)
    ppermute x8, starting transfers between devices, line_sums(): into = lax.ppermute(chunks[k], axis, inward)  23.3 us
    ppermute x8, waiting for transfers between devices, line_sums(): ends = lax.ppermute(total, axis, outward)  22.4 us
    pallas_call x8, Pallas kernels, weight_terms(): pl.pallas_call(term_body, grid=(steps,), in_specs=[pl.BlockSpec((inner, t...  21 us
    pallas_call x1, Pallas kernels, attention(): pl.pallas_call(functools.partial(attention_body, local_levels, far_bits),...  13.7 us
    ppermute x8, starting transfers between devices, line_sums(): ends = lax.ppermute(total, axis, outward)  10.5 us
    ppermute x6, starting transfers between devices, exchange(): return lax.ppermute(block, axis, [(i, i ^ distance) for i in range(count)])  10.1 us
    pallas_call x2, Pallas kernels, project_out(): pl.pallas_call(functools.partial(out_body, count), grid=(tok_rows // tile...  9.89 us
    pallas_call x1, Pallas kernels, key_value(): pl.pallas_call(functools.partial(key_value_body, local_levels, far_levels...  5.9 us
  transfers between devices with their start and end apart: 32, of which 9 were waited for; matrix products, arithmetic and copies ran while one was open for 2% of the time, Pallas kernels for 24%

profile of v2, /device:TPU:0, one launch (start us, length us, event | category | flops | bytes accessed | tf_op | source)
XLA Modules:
  0.0 157.9 jit_solution(6612537542684217683)
XLA Ops:
  7.2 5.9 %shard_map.110 = (bf16[1024,512]{1,0:T(8,128)(2,1)}, bf16[512,512]{1,0:T(8,128)(2,1)}, bf16[256,512]{1,0:T(8,128)(2,1)}, bf16[128,512]{1,0:T(8,128)(2,1)}, bf16[64,512]{1,0:T(8,128)(2,1)}) custom-call(bf16[1024,1024]{1,0:T(8,128)(2,1)} %right_ref.15, bf16[1024,256]{1,0:T(8,128)(2,1)} %refs_4_.1, bf16[1024,256]{1,0:T(8,128)(2,1)} %refs_5_.1), custom_call_target="tpu_custom_call" | custom-call | flops 1073741824 | bytes 4194304 | tf_op jit(solution)/shard_map/pallas_call | solution.py:93
  13.1 3.1 %collective-permute-start = (bf16[128,512]{1,0:T(8,128)(2,1)}, bf16[128,512]{1,0:T(8,128)(2,1)S(1)}, u32[]{:S(2)}, u32[]{:S(2)}) collective-permute-start(bf16[128,512]{1,0:T(8,128)(2,1)} %get-tuple-element.43), channel_id=1, source_target_pairs={{0,4},{4,0},{8,12},{12,8},{1,5},{5,1},{9,13},{13,9},{2,6},{6,2},{1... | collective-permute-start | bytes 393224 | tf_op jit(solution)/shard_map/ppermute | solution.py:343
  16.2 2.6 %collective-permute-start.1 = (bf16[64,512]{1,0:T(8,128)(2,1)}, bf16[64,512]{1,0:T(8,128)(2,1)S(1)}, u32[]{:S(2)}, u32[]{:S(2)}) collective-permute-start(bf16[64,512]{1,0:T(8,128)(2,1)} %get-tuple-element.44), channel_id=1, source_target_pairs={{0,8},{4,12},{8,0},{12,4},{1,9},{5,13},{9,1},{13,5},{2,10},{6,14},... | collective-permute-start | bytes 196616 | tf_op jit(solution)/shard_map/ppermute | solution.py:343
  18.8 5.1 %shard_map.109 = (bf16[1024,256]{1,0:T(8,128)(2,1)}, bf16[1024,256]{1,0:T(8,128)(2,1)}) custom-call(bf16[1024,1024]{1,0:T(8,128)(2,1)} %right_ref.15, bf16[1024,1024]{1,0:T(8,128)(2,1)} %right_ref.13, bf16[1024,256]{1,0:T(8,128)(2,1)} %refs_3_.1, bf16[1024,256]{1,0:T(8,128)(2,1)} %refs_1_.1), custom_call_target="tpu_custom_call" | custom-call | flops 1073741824 | bytes 6291456 | tf_op jit(solution)/shard_map/pallas_call | solution.py:120
  23.9 1.2 collective-permute-done.2.refs_7_
  25.8 13.7 %shard_map.111 = (bf16[1024,256]{1,0:T(8,128)(2,1)}, bf16[256,1024]{1,0:T(8,128)(2,1)}, bf16[1024,256]{1,0:T(8,128)(2,1)}, bf16[256,1024]{1,0:T(8,128)(2,1)}, f3...) custom-call(bf16[1024,256]{1,0:T(8,128)(2,1)} %get-tuple-element.38., ...), custom_call_target="tpu_custom_call" | custom-call | flops 2415919104 | bytes 6291456 | tf_op jit(solution)/shard_map/pallas_call | solution.py:228
  39.5 4.4 %shard_map.112 = bf16[1024,1024]{1,0:T(8,128)(2,1)} custom-call(bf16[1024,256]{1,0:T(8,128)(2,1)} %get-tuple-element.45.refs_0_, bf16[1024,256]{1,0:T(8,128)(2,1)} %refs_1_.1), custom_call_target="tpu_custom_call" | custom-call | flops 536870912 | bytes 2097152 | tf_op jit(solution)/shard_map/pallas_call | solution.py:329
  44.0 1.2 collective-permute-start.3
  45.2 2.0 %collective-permute-start.4 = (bf16[64,512]{1,0:T(8,128)(2,1)S(1)}, bf16[64,512]{1,0:T(8,128)(2,1)S(1)}, u32[]{:S(2)}, u32[]{:S(2)}) collective-permute-start(bf16[64,512]{1,0:T(8,128)(2,1)S(1)} %copy-done.14), channel_id=1, source_target_pairs={{0,8},{4,12},{8,0},{12,4},{1,9},{5,13},{9,1},{13,5},{2,10},{6,14},... | collective-permute-start | bytes 196616 | tf_op jit(solution)/shard_map/ppermute | solution.py:343
  47.2 1.2 collective-permute-start.5
  48.4 2.6 %shard_map.117 = bf16[512,256]{1,0:T(8,128)(2,1)} custom-call(bf16[256,1024]{1,0:T(8,128)(2,1)} %get-tuple-element.57.left_ref, bf16[1024,1024]{1,0:T(8,128)(2,1)} %right_ref.13), custom_call_target="tpu_custom_call" | custom-call | flops 268435456 | bytes 1572864 | tf_op jit(solution)/shard_map/pallas_call | solution.py:251
  51.1 2.1 %collective-permute-start.8 = (bf16[512,256]{1,0:T(8,128)(2,1)}, bf16[512,256]{1,0:T(8,128)(2,1)S(1)}, u32[]{:S(2)}, u32[]{:S(2)}) collective-permute-start(bf16[512,256]{1,0:T(8,128)(2,1)} %shard_map.117), channel_id=1, source_target_pairs={{0,4},{12,8},{1,5},{13,9},{2,6},{14,10},{3,7},{15,11},{16,20},{28,... | collective-permute-start | bytes 786440 | tf_op jit(solution)/shard_map/ppermute | solution.py:379
  54.0 5.7 %shard_map.113 = (bf16[1024,256]{1,0:T(8,128)(2,1)}, bf16[1024,256]{1,0:T(8,128)(2,1)}, bf16[512,1024]{1,0:T(8,128)(2,1)}) custom-call(f32[1024,512]{1,0:T(8,128)} %get-tuple-element.47.dkv_ref, f32[512,512]{1,0:T(8,128)} %get-tuple-element.48.refs_0_, f32[256,512]{1,0:T(8,128)} %get-tuple-element.49.refs_1_, bf16[128,512]{1,0:T(8,128)(2,1)} %copy-done.8, ...), custom_call_target="tpu_custom_call" | custom-call | flops 536870912 | bytes 10485760 | tf_op jit(solution)/shard_map/pallas_call | solution.py:301
  59.7 5.5 %shard_map.114 = bf16[1024,1024]{1,0:T(8,128)(2,1)} custom-call(bf16[1024,256]{1,0:T(8,128)(2,1)} %get-tuple-element.46.refs_0_, bf16[1024,256]{1,0:T(8,128)(2,1)} %get-tuple-element.53.refs_1_, bf16[1024,256]{1,0:T(8,128)(2,1)} %get-tuple-element.54.refs_2_, bf16[1024,256]{1,0:T(8,128)(2,1)} %refs_3_.1, bf16[1024,256]{1,0:T(8,128)(2,1)} %refs_4_.1, ...), custom_call_target="tpu_custom_call" | custom-call | flops 1610612736 | bytes 2097152 | tf_op jit(solution)/shard_map/pallas_call | solution.py:329
  65.2 2.6 %shard_map.116.own_ref = bf16[512,256]{1,0:T(8,128)(2,1)} custom-call(bf16[256,1024]{1,0:T(8,128)(2,1)} %get-tuple-element.56.left_ref, bf16[1024,1024]{1,0:T(8,128)(2,1)} %right_ref.15), custom_call_target="tpu_custom_call" | custom-call | flops 268435456 | bytes 1572864 | tf_op jit(solution)/shard_map/pallas_call | solution.py:251
  67.9 1.9 %collective-permute-start.7 = (bf16[512,256]{1,0:T(8,128)(2,1)}, bf16[512,256]{1,0:T(8,128)(2,1)S(1)}, u32[]{:S(2)}, u32[]{:S(2)}) collective-permute-start(bf16[512,256]{1,0:T(8,128)(2,1)} %shard_map.116.own_ref), channel_id=1, source_target_pairs={{0,4},{12,8},{1,5},{13,9},{2,6},{14,10},{3,7},{15,11},{16,20},{28,... | collective-permute-start | bytes 786440 | tf_op jit(solution)/shard_map/ppermute | solution.py:379
  69.7 2.6 %shard_map.122 = bf16[512,256]{1,0:T(8,128)(2,1)} custom-call(bf16[256,1024]{1,0:T(8,128)(2,1)} %get-tuple-element.57.left_ref, bf16[1024,1024]{1,0:T(8,128)(2,1)} %right_ref.13), custom_call_target="tpu_custom_call" | custom-call | flops 268435456 | bytes 1572864 | tf_op jit(solution)/shard_map/pallas_call | solution.py:251
  72.4 1.4 collective-permute-start.14
  73.8 2.6 %shard_map.121.own_ref = bf16[512,256]{1,0:T(8,128)(2,1)} custom-call(bf16[256,1024]{1,0:T(8,128)(2,1)} %get-tuple-element.56.left_ref, bf16[1024,1024]{1,0:T(8,128)(2,1)} %right_ref.15), custom_call_target="tpu_custom_call" | custom-call | flops 268435456 | bytes 1572864 | tf_op jit(solution)/shard_map/pallas_call | solution.py:251
  76.4 1.3 collective-permute-start.13
  78.5 2.7 %collective-permute-done.14 = bf16[512,256]{1,0:T(8,128)(2,1)S(1)} collective-permute-done((bf16[512,256]{1,0:T(8,128)(2,1)}, bf16[512,256]{1,0:T(8,128)(2,1)S(1)}, u32[]{:S(2)}, u32[]{:S(2)}) %collective-permute-start.14) | collective-permute-done | bytes 262176 | tf_op jit(solution)/shard_map/ppermute | solution.py:379
  82.0 2.6 %shard_map.115.own_ref = bf16[512,256]{1,0:T(8,128)(2,1)} custom-call(bf16[512,1024]{1,0:T(8,128)(2,1)} %get-tuple-element.55.left_ref, bf16[1024,1024]{1,0:T(8,128)(2,1)} %right_ref.15), custom_call_target="tpu_custom_call" | custom-call | flops 268435456 | bytes 1572864 | tf_op jit(solution)/shard_map/pallas_call | solution.py:251
  84.6 8.2 %collective-permute-start.6 = (bf16[512,256]{1,0:T(8,128)(2,1)}, bf16[512,256]{1,0:T(8,128)(2,1)S(1)}, u32[]{:S(2)}, u32[]{:S(2)}) collective-permute-start(bf16[512,256]{1,0:T(8,128)(2,1)} %shard_map.115.own_ref), channel_id=1, source_target_pairs={{0,4},{12,8},{1,5},{13,9},{2,6},{14,10},{3,7},{15,11},{16,20},{28,... | collective-permute-start | bytes 786440 | tf_op jit(solution)/shard_map/ppermute | solution.py:379
  92.9 2.6 %shard_map.120.own_ref = bf16[512,256]{1,0:T(8,128)(2,1)} custom-call(bf16[512,1024]{1,0:T(8,128)(2,1)} %get-tuple-element.55.left_ref, bf16[1024,1024]{1,0:T(8,128)(2,1)} %right_ref.15), custom_call_target="tpu_custom_call" | custom-call | flops 268435456 | bytes 1572864 | tf_op jit(solution)/shard_map/pallas_call | solution.py:251
  95.5 1.3 collective-permute-start.12
  98.5 1.3 collective-permute-start.28
  99.8 2.6 %shard_map.125.own_ref = bf16[512,256]{1,0:T(8,128)(2,1)} custom-call(bf16[512,1024]{1,0:T(8,128)(2,1)} %get-tuple-element.55.left_ref, bf16[1024,1024]{1,0:T(8,128)(2,1)} %right_ref.15), custom_call_target="tpu_custom_call" | custom-call | flops 268435456 | bytes 1572864 | tf_op jit(solution)/shard_map/pallas_call | solution.py:251
  102.4 1.4 collective-permute-start.29
  103.9 2.6 %shard_map.127.own_ref = bf16[512,256]{1,0:T(8,128)(2,1)} custom-call(bf16[512,1024]{1,0:T(8,128)(2,1)} %get-tuple-element.55.left_ref, bf16[1024,1024]{1,0:T(8,128)(2,1)} %right_ref.15), custom_call_target="tpu_custom_call" | custom-call | flops 268435456 | bytes 1572864 | tf_op jit(solution)/shard_map/pallas_call | solution.py:251
  106.5 5.8 %collective-permute-start.18 = (bf16[512,256]{1,0:T(8,128)(2,1)S(1)}, bf16[512,256]{1,0:T(8,128)(2,1)S(1)}, u32[]{:S(2)}, u32[]{:S(2)}) collective-permute-start(bf16[512,256]{1,0:T(8,128)(2,1)S(1)} %copy-done.3), channel_id=1, source_target_pairs={{0,4},{12,8},{1,5},{13,9},{2,6},{14,10},{3,7},{15,11},{16,20},{28,... | collective-permute-start | bytes 786440 | tf_op jit(solution)/shard_map/ppermute | solution.py:379
  112.4 1.3 collective-permute-start.21
  114.6 0.8 collective-permute-start.22
  115.5 1.3 collective-permute-start.11
  116.8 1.3 collective-permute-start.17
  118.1 0.8 pad_maximum_fusion.3
  120.6 1.3 collective-permute-start.20
  121.9 3.7 %collective-permute-done.11 = bf16[512,256]{1,0:T(8,128)(2,1)S(1)} collective-permute-done((bf16[512,256]{1,0:T(8,128)(2,1)S(1)}, bf16[512,256]{1,0:T(8,128)(2,1)S(1)}, u32[]{:S(2)}, u32[]{:S(2)}) %collective-permute-start.11) | collective-permute-done | bytes 262176 | tf_op jit(solution)/shard_map/ppermute | solution.py:391
  125.6 1.3 collective-permute-start.23
  126.9 4.3 %collective-permute-done.17 = bf16[512,256]{1,0:T(8,128)(2,1)S(1)} collective-permute-done((bf16[512,256]{1,0:T(8,128)(2,1)S(1)}, bf16[512,256]{1,0:T(8,128)(2,1)S(1)}, u32[]{:S(2)}, u32[]{:S(2)}) %collective-permute-start.17) | collective-permute-done | bytes 262176 | tf_op jit(solution)/shard_map/ppermute | solution.py:391
  131.2 0.8 pad_maximum_fusion
  132.1 1.3 collective-permute-start.25
  133.5 1.3 collective-permute-start.27
  134.8 4.1 %collective-permute-done.20 = bf16[512,256]{1,0:T(8,128)(2,1)S(1)} collective-permute-done((bf16[512,256]{1,0:T(8,128)(2,1)S(1)}, bf16[512,256]{1,0:T(8,128)(2,1)S(1)}, u32[]{:S(2)}, u32[]{:S(2)}) %collective-permute-start.20) | collective-permute-done | bytes 262176 | tf_op jit(solution)/shard_map/ppermute | solution.py:391
  138.9 5.6 %collective-permute-done.23 = bf16[512,256]{1,0:T(8,128)(2,1)S(1)} collective-permute-done((bf16[512,256]{1,0:T(8,128)(2,1)S(1)}, bf16[512,256]{1,0:T(8,128)(2,1)S(1)}, u32[]{:S(2)}, u32[]{:S(2)}) %collective-permute-start.23) | collective-permute-done | bytes 262176 | tf_op jit(solution)/shard_map/ppermute | solution.py:391
  144.5 0.8 pad_maximum_fusion.1
  145.4 2.1 %collective-permute-done.25 = bf16[512,256]{1,0:T(8,128)(2,1)S(1)} collective-permute-done((bf16[512,256]{1,0:T(8,128)(2,1)S(1)}, bf16[512,256]{1,0:T(8,128)(2,1)S(1)}, u32[]{:S(2)}, u32[]{:S(2)}) %collective-permute-start.25) | collective-permute-done | bytes 262176 | tf_op jit(solution)/shard_map/ppermute | solution.py:391
  147.5 2.8 %collective-permute-done.27 = bf16[512,256]{1,0:T(8,128)(2,1)S(1)} collective-permute-done((bf16[512,256]{1,0:T(8,128)(2,1)S(1)}, bf16[512,256]{1,0:T(8,128)(2,1)S(1)}, u32[]{:S(2)}, u32[]{:S(2)}) %collective-permute-start.27) | collective-permute-done | bytes 262176 | tf_op jit(solution)/shard_map/ppermute | solution.py:391
  150.3 0.8 pad_maximum_fusion.2
  (88 shorter events, 7.6 us)
Async XLA Ops:
  7.2 143.9 %reduce-scatter.3.cloned.1.call-start = ((), (), s32[]{:S(2)}) async-start(), calls=%async_computation.2 | async-start | bytes 2621440 | tf_op jit(solution)/shard_map/reduce_scatter | solution.py:420
  13.1 12.0 %collective-permute-start = (bf16[128,512]{1,0:T(8,128)(2,1)}, bf16[128,512]{1,0:T(8,128)(2,1)S(1)}, u32[]{:S(2)}, u32[]{:S(2)}) collective-permute-start(bf16[128,512]{1,0:T(8,128)(2,1)} %get-tuple-element.43), channel_id=1, source_target_pairs={{0,4},{4,0},{8,12},{12,8},{1,5},{5,1},{9,13},{13,9},{2,6},{6,2},{1... | collective-permute-start | bytes 393224 | tf_op jit(solution)/shard_map/ppermute | solution.py:343
  16.2 7.7 %collective-permute-start.1 = (bf16[64,512]{1,0:T(8,128)(2,1)}, bf16[64,512]{1,0:T(8,128)(2,1)S(1)}, u32[]{:S(2)}, u32[]{:S(2)}) collective-permute-start(bf16[64,512]{1,0:T(8,128)(2,1)} %get-tuple-element.44), channel_id=1, source_target_pairs={{0,8},{4,12},{8,0},{12,4},{1,9},{5,13},{9,1},{13,5},{2,10},{6,14},... | collective-permute-start | bytes 196616 | tf_op jit(solution)/shard_map/ppermute | solution.py:343
  18.8 6.3 %collective-permute-start.2 = (bf16[64,512]{1,0:T(8,128)(2,1)}, bf16[64,512]{1,0:T(8,128)(2,1)S(1)}, u32[]{:S(2)}, u32[]{:S(2)}) collective-permute-start(bf16[64,512]{1,0:T(8,128)(2,1)} %get-tuple-element.44), channel_id=1, source_target_pairs={{0,12},{4,8},{8,4},{12,0},{1,13},{5,9},{9,5},{13,1},{2,14},{6,10},... | collective-permute-start | bytes 196616 | tf_op jit(solution)/shard_map/ppermute | solution.py:343
  23.9 1.2 copy-start.15
  25.1 0.7 copy-start.12
  39.5 4.5 %copy-start.11 = (bf16[128,512]{1,0:T(8,128)(2,1)S(1)}, bf16[128,512]{1,0:T(8,128)(2,1)}, u32[]{:S(2)}) copy-start(bf16[128,512]{1,0:T(8,128)(2,1)} %get-tuple-element.50) | copy-start | bytes 393220
  39.5 5.6 %copy-start.14 = (bf16[64,512]{1,0:T(8,128)(2,1)S(1)}, bf16[64,512]{1,0:T(8,128)(2,1)}, u32[]{:S(2)}) copy-start(bf16[64,512]{1,0:T(8,128)(2,1)} %get-tuple-element.51) | copy-start | bytes 196612
  39.5 7.7 %copy-start.13 = (bf16[64,512]{1,0:T(8,128)(2,1)S(1)}, bf16[64,512]{1,0:T(8,128)(2,1)}, u32[]{:S(2)}) copy-start(bf16[64,512]{1,0:T(8,128)(2,1)} %get-tuple-element.52) | copy-start | bytes 196612
  43.9 107.2 %reduce-scatter.5.cloned.1.call-start = ((), (), s32[]{:S(2)}) async-start(), calls=%async_computation.3 | async-start | bytes 2621440 | tf_op jit(solution)/shard_map/reduce_scatter | solution.py:423
  44.0 9.3 %collective-permute-start.3 = (bf16[128,512]{1,0:T(8,128)(2,1)S(1)}, bf16[128,512]{1,0:T(8,128)(2,1)S(1)}, u32[]{:S(2)}, u32[]{:S(2)}) collective-permute-start(bf16[128,512]{1,0:T(8,128)(2,1)S(1)} %copy-done.11), channel_id=1, source_target_pairs={{0,4},{4,0},{8,12},{12,8},{1,5},{5,1},{9,13},{13,9},{2,6},{6,2},{1... | collective-permute-start | bytes 393224 | tf_op jit(solution)/shard_map/ppermute | solution.py:343
  45.2 8.0 %collective-permute-start.4 = (bf16[64,512]{1,0:T(8,128)(2,1)S(1)}, bf16[64,512]{1,0:T(8,128)(2,1)S(1)}, u32[]{:S(2)}, u32[]{:S(2)}) collective-permute-start(bf16[64,512]{1,0:T(8,128)(2,1)S(1)} %copy-done.14), channel_id=1, source_target_pairs={{0,8},{4,12},{8,0},{12,4},{1,9},{5,13},{9,1},{13,5},{2,10},{6,14},... | collective-permute-start | bytes 196616 | tf_op jit(solution)/shard_map/ppermute | solution.py:343
  47.2 6.1 %collective-permute-start.5 = (bf16[64,512]{1,0:T(8,128)(2,1)S(1)}, bf16[64,512]{1,0:T(8,128)(2,1)S(1)}, u32[]{:S(2)}, u32[]{:S(2)}) collective-permute-start(bf16[64,512]{1,0:T(8,128)(2,1)S(1)} %copy-done.13), channel_id=1, source_target_pairs={{0,12},{4,8},{8,4},{12,0},{1,13},{5,9},{9,5},{13,1},{2,14},{6,10},... | collective-permute-start | bytes 196616 | tf_op jit(solution)/shard_map/ppermute | solution.py:343
  51.1 26.7 %collective-permute-start.8 = (bf16[512,256]{1,0:T(8,128)(2,1)}, bf16[512,256]{1,0:T(8,128)(2,1)S(1)}, u32[]{:S(2)}, u32[]{:S(2)}) collective-permute-start(bf16[512,256]{1,0:T(8,128)(2,1)} %shard_map.117), channel_id=1, source_target_pairs={{0,4},{12,8},{1,5},{13,9},{2,6},{14,10},{3,7},{15,11},{16,20},{28,... | collective-permute-start | bytes 786440 | tf_op jit(solution)/shard_map/ppermute | solution.py:379
  53.2 0.6 copy-start.9
  53.3 0.6 copy-start.10
  53.3 0.7 copy-start.8
  67.9 27.6 %collective-permute-start.7 = (bf16[512,256]{1,0:T(8,128)(2,1)}, bf16[512,256]{1,0:T(8,128)(2,1)S(1)}, u32[]{:S(2)}, u32[]{:S(2)}) collective-permute-start(bf16[512,256]{1,0:T(8,128)(2,1)} %shard_map.116.own_ref), channel_id=1, source_target_pairs={{0,4},{12,8},{1,5},{13,9},{2,6},{14,10},{3,7},{15,11},{16,20},{28,... | collective-permute-start | bytes 786440 | tf_op jit(solution)/shard_map/ppermute | solution.py:379
  72.4 5.4 %copy-start.6 = (bf16[512,256]{1,0:T(8,128)(2,1)S(1)}, bf16[512,256]{1,0:T(8,128)(2,1)}, u32[]{:S(2)}) copy-start(bf16[512,256]{1,0:T(8,128)(2,1)} %shard_map.117) | copy-start | bytes 786436
  72.4 8.9 %copy-start.7 = (bf16[512,256]{1,0:T(8,128)(2,1)S(1)}, bf16[512,256]{1,0:T(8,128)(2,1)}, u32[]{:S(2)}) copy-start(bf16[512,256]{1,0:T(8,128)(2,1)} %shard_map.122) | copy-start | bytes 786436
  72.4 8.8 %collective-permute-start.14 = (bf16[512,256]{1,0:T(8,128)(2,1)}, bf16[512,256]{1,0:T(8,128)(2,1)S(1)}, u32[]{:S(2)}, u32[]{:S(2)}) collective-permute-start(bf16[512,256]{1,0:T(8,128)(2,1)} %shard_map.122), channel_id=1, source_target_pairs={{0,4},{12,8},{1,5},{13,9},{2,6},{14,10},{3,7},{15,11},{16,20},{28,... | collective-permute-start | bytes 786440 | tf_op jit(solution)/shard_map/ppermute | solution.py:379
  76.4 21.2 %collective-permute-start.13 = (bf16[512,256]{1,0:T(8,128)(2,1)}, bf16[512,256]{1,0:T(8,128)(2,1)S(1)}, u32[]{:S(2)}, u32[]{:S(2)}) collective-permute-start(bf16[512,256]{1,0:T(8,128)(2,1)} %shard_map.121.own_ref), channel_id=1, source_target_pairs={{0,4},{12,8},{1,5},{13,9},{2,6},{14,10},{3,7},{15,11},{16,20},{28,... | collective-permute-start | bytes 786440 | tf_op jit(solution)/shard_map/ppermute | solution.py:379
  77.8 19.0 %collective-permute-start.9 = (bf16[512,256]{1,0:T(8,128)(2,1)S(1)}, bf16[512,256]{1,0:T(8,128)(2,1)S(1)}, u32[]{:S(2)}, u32[]{:S(2)}) collective-permute-start(bf16[512,256]{1,0:T(8,128)(2,1)S(1)} %add_convert_fusion.3.half_ref), channel_id=1, source_target_pairs={{4,8},{8,4},{5,9},{9,5},{6,10},{10,6},{7,11},{11,7},{20,24},{24,20... | collective-permute-start | bytes 786440 | tf_op jit(solution)/shard_map/ppermute | solution.py:389
  81.3 16.3 %collective-permute-start.15 = (bf16[512,256]{1,0:T(8,128)(2,1)S(1)}, bf16[512,256]{1,0:T(8,128)(2,1)S(1)}, u32[]{:S(2)}, u32[]{:S(2)}) collective-permute-start(bf16[512,256]{1,0:T(8,128)(2,1)S(1)} %add_convert_fusion.2.half_ref), channel_id=1, source_target_pairs={{4,8},{8,4},{5,9},{9,5},{6,10},{10,6},{7,11},{11,7},{20,24},{24,20... | collective-permute-start | bytes 786440 | tf_op jit(solution)/shard_map/ppermute | solution.py:389
  84.6 12.2 %copy-start.5 = (bf16[512,256]{1,0:T(8,128)(2,1)S(1)}, bf16[512,256]{1,0:T(8,128)(2,1)}, u32[]{:S(2)}) copy-start(bf16[512,256]{1,0:T(8,128)(2,1)} %shard_map.116.own_ref) | copy-start | bytes 786436
  84.6 13.0 %copy-start.4 = (bf16[512,256]{1,0:T(8,128)(2,1)S(1)}, bf16[512,256]{1,0:T(8,128)(2,1)}, u32[]{:S(2)}) copy-start(bf16[512,256]{1,0:T(8,128)(2,1)} %shard_map.121.own_ref) | copy-start | bytes 786436
  84.6 17.8 %collective-permute-start.6 = (bf16[512,256]{1,0:T(8,128)(2,1)}, bf16[512,256]{1,0:T(8,128)(2,1)S(1)}, u32[]{:S(2)}, u32[]{:S(2)}) collective-permute-start(bf16[512,256]{1,0:T(8,128)(2,1)} %shard_map.115.own_ref), channel_id=1, source_target_pairs={{0,4},{12,8},{1,5},{13,9},{2,6},{14,10},{3,7},{15,11},{16,20},{28,... | collective-permute-start | bytes 786440 | tf_op jit(solution)/shard_map/ppermute | solution.py:379
  95.5 16.9 %collective-permute-start.12 = (bf16[512,256]{1,0:T(8,128)(2,1)}, bf16[512,256]{1,0:T(8,128)(2,1)S(1)}, u32[]{:S(2)}, u32[]{:S(2)}) collective-permute-start(bf16[512,256]{1,0:T(8,128)(2,1)} %shard_map.120.own_ref), channel_id=1, source_target_pairs={{0,4},{12,8},{1,5},{13,9},{2,6},{14,10},{3,7},{15,11},{16,20},{28,... | collective-permute-start | bytes 786440 | tf_op jit(solution)/shard_map/ppermute | solution.py:379
  96.9 9.6 %collective-permute-start.10 = (bf16[512,256]{1,0:T(8,128)(2,1)S(1)}, bf16[512,256]{1,0:T(8,128)(2,1)S(1)}, u32[]{:S(2)}, u32[]{:S(2)}) collective-permute-start(bf16[512,256]{1,0:T(8,128)(2,1)S(1)} %get-tuple-element.58.half_ref), channel_id=1, source_target_pairs={{4,8},{8,4},{5,9},{9,5},{6,10},{10,6},{7,11},{11,7},{20,24},{24,20... | collective-permute-start | bytes 786440 | tf_op jit(solution)/shard_map/ppermute | solution.py:389
  97.8 16.0 %collective-permute-start.16 = (bf16[512,256]{1,0:T(8,128)(2,1)S(1)}, bf16[512,256]{1,0:T(8,128)(2,1)S(1)}, u32[]{:S(2)}, u32[]{:S(2)}) collective-permute-start(bf16[512,256]{1,0:T(8,128)(2,1)S(1)} %get-tuple-element.60.half_ref), channel_id=1, source_target_pairs={{4,8},{8,4},{5,9},{9,5},{6,10},{10,6},{7,11},{11,7},{20,24},{24,20... | collective-permute-start | bytes 786440 | tf_op jit(solution)/shard_map/ppermute | solution.py:389
  98.5 16.1 %collective-permute-start.28 = (bf16[512,256]{1,0:T(8,128)(2,1)S(1)}, bf16[512,256]{1,0:T(8,128)(2,1)S(1)}, u32[]{:S(2)}, u32[]{:S(2)}) collective-permute-start(bf16[512,256]{1,0:T(8,128)(2,1)S(1)} %get-tuple-element.68), channel_id=1, source_target_pairs={{4,0},{8,12},{5,1},{9,13},{6,2},{10,14},{7,3},{11,15},{20,16},{24,... | collective-permute-start | bytes 786440 | tf_op jit(solution)/shard_map/ppermute | solution.py:391
  102.4 4.1 %copy-start.3 = (bf16[512,256]{1,0:T(8,128)(2,1)S(1)}, bf16[512,256]{1,0:T(8,128)(2,1)}, u32[]{:S(2)}) copy-start(bf16[512,256]{1,0:T(8,128)(2,1)} %shard_map.125.own_ref) | copy-start | bytes 786436
  102.4 9.9 %copy-start.2 = (bf16[512,256]{1,0:T(8,128)(2,1)S(1)}, bf16[512,256]{1,0:T(8,128)(2,1)}, u32[]{:S(2)}) copy-start(bf16[512,256]{1,0:T(8,128)(2,1)} %shard_map.115.own_ref) | copy-start | bytes 786436
  102.4 12.0 %copy-start = (bf16[512,256]{1,0:T(8,128)(2,1)S(1)}, bf16[512,256]{1,0:T(8,128)(2,1)}, u32[]{:S(2)}) copy-start(bf16[512,256]{1,0:T(8,128)(2,1)} %shard_map.120.own_ref) | copy-start | bytes 786436
  102.4 13.0 %collective-permute-start.29 = (bf16[512,256]{1,0:T(8,128)(2,1)S(1)}, bf16[512,256]{1,0:T(8,128)(2,1)S(1)}, u32[]{:S(2)}, u32[]{:S(2)}) collective-permute-start(bf16[512,256]{1,0:T(8,128)(2,1)S(1)} %get-tuple-element.69), channel_id=1, source_target_pairs={{4,0},{8,12},{5,1},{9,13},{6,2},{10,14},{7,3},{11,15},{20,16},{24,... | collective-permute-start | bytes 786440 | tf_op jit(solution)/shard_map/ppermute | solution.py:391
  106.5 10.3 %collective-permute-start.18 = (bf16[512,256]{1,0:T(8,128)(2,1)S(1)}, bf16[512,256]{1,0:T(8,128)(2,1)S(1)}, u32[]{:S(2)}, u32[]{:S(2)}) collective-permute-start(bf16[512,256]{1,0:T(8,128)(2,1)S(1)} %copy-done.3), channel_id=1, source_target_pairs={{0,4},{12,8},{1,5},{13,9},{2,6},{14,10},{3,7},{15,11},{16,20},{28,... | collective-permute-start | bytes 786440 | tf_op jit(solution)/shard_map/ppermute | solution.py:379
  112.4 7.3 %collective-permute-start.21 = (bf16[512,256]{1,0:T(8,128)(2,1)}, bf16[512,256]{1,0:T(8,128)(2,1)S(1)}, u32[]{:S(2)}, u32[]{:S(2)}) collective-permute-start(bf16[512,256]{1,0:T(8,128)(2,1)} %shard_map.127.own_ref), channel_id=1, source_target_pairs={{0,4},{12,8},{1,5},{13,9},{2,6},{14,10},{3,7},{15,11},{16,20},{28,... | collective-permute-start | bytes 786440 | tf_op jit(solution)/shard_map/ppermute | solution.py:379
  113.8 5.2 %collective-permute-start.19 = (bf16[512,256]{1,0:T(8,128)(2,1)S(1)}, bf16[512,256]{1,0:T(8,128)(2,1)S(1)}, u32[]{:S(2)}, u32[]{:S(2)}) collective-permute-start(bf16[512,256]{1,0:T(8,128)(2,1)S(1)} %get-tuple-element.62.half_ref), channel_id=1, source_target_pairs={{4,8},{8,4},{5,9},{9,5},{6,10},{10,6},{7,11},{11,7},{20,24},{24,20... | collective-permute-start | bytes 786440 | tf_op jit(solution)/shard_map/ppermute | solution.py:389
  114.6 5.2 %copy-start.1 = (bf16[512,256]{1,0:T(8,128)(2,1)S(1)}, bf16[512,256]{1,0:T(8,128)(2,1)}, u32[]{:S(2)}) copy-start(bf16[512,256]{1,0:T(8,128)(2,1)} %shard_map.127.own_ref) | copy-start | bytes 786436
  114.6 5.2 %collective-permute-start.22 = (bf16[512,256]{1,0:T(8,128)(2,1)S(1)}, bf16[512,256]{1,0:T(8,128)(2,1)S(1)}, u32[]{:S(2)}, u32[]{:S(2)}) collective-permute-start(bf16[512,256]{1,0:T(8,128)(2,1)S(1)} %get-tuple-element.64.half_ref), channel_id=1, source_target_pairs={{4,8},{8,4},{5,9},{9,5},{6,10},{10,6},{7,11},{11,7},{20,24},{24,20... | collective-permute-start | bytes 786440 | tf_op jit(solution)/shard_map/ppermute | solution.py:389
  115.5 10.1 %collective-permute-start.11 = (bf16[512,256]{1,0:T(8,128)(2,1)S(1)}, bf16[512,256]{1,0:T(8,128)(2,1)S(1)}, u32[]{:S(2)}, u32[]{:S(2)}) collective-permute-start(bf16[512,256]{1,0:T(8,128)(2,1)S(1)} %get-tuple-element.59), channel_id=1, source_target_pairs={{4,0},{8,12},{5,1},{9,13},{6,2},{10,14},{7,3},{11,15},{20,16},{24,... | collective-permute-start | bytes 786440 | tf_op jit(solution)/shard_map/ppermute | solution.py:391
  116.8 14.4 %collective-permute-start.17 = (bf16[512,256]{1,0:T(8,128)(2,1)S(1)}, bf16[512,256]{1,0:T(8,128)(2,1)S(1)}, u32[]{:S(2)}, u32[]{:S(2)}) collective-permute-start(bf16[512,256]{1,0:T(8,128)(2,1)S(1)} %get-tuple-element.61), channel_id=1, source_target_pairs={{4,0},{8,12},{5,1},{9,13},{6,2},{10,14},{7,3},{11,15},{20,16},{24,... | collective-permute-start | bytes 786440 | tf_op jit(solution)/shard_map/ppermute | solution.py:391
  119.1 13.0 %collective-permute-start.24 = (bf16[512,256]{1,0:T(8,128)(2,1)S(1)}, bf16[512,256]{1,0:T(8,128)(2,1)S(1)}, u32[]{:S(2)}, u32[]{:S(2)}) collective-permute-start(bf16[512,256]{1,0:T(8,128)(2,1)S(1)} %get-tuple-element.66), channel_id=1, source_target_pairs={{4,8},{8,4},{5,9},{9,5},{6,10},{10,6},{7,11},{11,7},{20,24},{24,20... | collective-permute-start | bytes 786440 | tf_op jit(solution)/shard_map/ppermute | solution.py:389
  119.9 13.5 %collective-permute-start.26 = (bf16[512,256]{1,0:T(8,128)(2,1)S(1)}, bf16[512,256]{1,0:T(8,128)(2,1)S(1)}, u32[]{:S(2)}, u32[]{:S(2)}) collective-permute-start(bf16[512,256]{1,0:T(8,128)(2,1)S(1)} %get-tuple-element.67), channel_id=1, source_target_pairs={{4,8},{8,4},{5,9},{9,5},{6,10},{10,6},{7,11},{11,7},{20,24},{24,20... | collective-permute-start | bytes 786440 | tf_op jit(solution)/shard_map/ppermute | solution.py:389
  120.6 18.3 %collective-permute-start.20 = (bf16[512,256]{1,0:T(8,128)(2,1)S(1)}, bf16[512,256]{1,0:T(8,128)(2,1)S(1)}, u32[]{:S(2)}, u32[]{:S(2)}) collective-permute-start(bf16[512,256]{1,0:T(8,128)(2,1)S(1)} %get-tuple-element.63), channel_id=1, source_target_pairs={{4,0},{8,12},{5,1},{9,13},{6,2},{10,14},{7,3},{11,15},{20,16},{24,... | collective-permute-start | bytes 786440 | tf_op jit(solution)/shard_map/ppermute | solution.py:391
  125.6 18.9 %collective-permute-start.23 = (bf16[512,256]{1,0:T(8,128)(2,1)S(1)}, bf16[512,256]{1,0:T(8,128)(2,1)S(1)}, u32[]{:S(2)}, u32[]{:S(2)}) collective-permute-start(bf16[512,256]{1,0:T(8,128)(2,1)S(1)} %get-tuple-element.65), channel_id=1, source_target_pairs={{4,0},{8,12},{5,1},{9,13},{6,2},{10,14},{7,3},{11,15},{20,16},{24,... | collective-permute-start | bytes 786440 | tf_op jit(solution)/shard_map/ppermute | solution.py:391
  132.1 15.3 %collective-permute-start.25 = (bf16[512,256]{1,0:T(8,128)(2,1)S(1)}, bf16[512,256]{1,0:T(8,128)(2,1)S(1)}, u32[]{:S(2)}, u32[]{:S(2)}) collective-permute-start(bf16[512,256]{1,0:T(8,128)(2,1)S(1)} %add_convert_fusion.1), channel_id=1, source_target_pairs={{4,0},{8,12},{5,1},{9,13},{6,2},{10,14},{7,3},{11,15},{20,16},{24,... | collective-permute-start | bytes 786440 | tf_op jit(solution)/shard_map/ppermute | solution.py:391
  133.5 16.7 %collective-permute-start.27 = (bf16[512,256]{1,0:T(8,128)(2,1)S(1)}, bf16[512,256]{1,0:T(8,128)(2,1)S(1)}, u32[]{:S(2)}, u32[]{:S(2)}) collective-permute-start(bf16[512,256]{1,0:T(8,128)(2,1)S(1)} %add_convert_fusion), channel_id=1, source_target_pairs={{4,0},{8,12},{5,1},{9,13},{6,2},{10,14},{7,3},{11,15},{20,16},{24,... | collective-permute-start | bytes 786440 | tf_op jit(solution)/shard_map/ppermute | solution.py:391
  (1 other events, 0.6 us)
Sparse Core Ops, SparseCore 0:
  44.0 31.6 reduce-scatter.2
  79.0 31.4 reduce-scatter.4

commit v3 on v2

v3 whole, which is shorter than its diff:
```python
import functools
import math

import jax
import jax.numpy as jnp
from jax import lax
from jax.experimental import pallas as pl
from jax.experimental.pallas import tpu as pltpu
from jax.sharding import PartitionSpec as P

HEAD_DIM = 128
BLOCK = 128
BF16 = jnp.bfloat16
F32 = jnp.float32
MIB = 1024 * 1024

NN = (((1,), (0,)), ((), ()))
NT = (((1,), (1,)), ((), ()))
TN = (((0,), (0,)), ((), ()))


def dot(left, right, dims=NN):
    return lax.dot_general(left, right, dims, preferred_element_type=F32)


def params(mib):
    return pltpu.CompilerParams(vmem_limit_bytes=mib * MIB)


def cost(flops, moved, exps=0):
    return pl.CostEstimate(flops=int(flops), bytes_accessed=int(moved), transcendentals=int(exps))


def shape(rows, cols, dtype=BF16):
    return jax.ShapeDtypeStruct((rows, cols), dtype)


def whole(rows, cols):
    return pl.BlockSpec((rows, cols), lambda *_: (0, 0))


def pool_matrix(rows):
    row = lax.broadcasted_iota(jnp.int32, (rows // 2, rows), 0)
    col = lax.broadcasted_iota(jnp.int32, (rows // 2, rows), 1)
    return jnp.where(jnp.right_shift(col, 1) == row, 0.5, 0.0).astype(BF16)


def spread_matrix(rows, step_bits, offset, cols, weight):
    row = lax.broadcasted_iota(jnp.int32, (rows, cols), 0) + offset
    col = lax.broadcasted_iota(jnp.int32, (rows, cols), 1)
    return jnp.where(jnp.right_shift(row, step_bits) == col, weight, 0.0).astype(BF16)


def key_value_body(local_levels, far_levels, parts, tok_hbm, wk_hbm, wv_hbm, *refs):
    kv_ref = refs[0]
    mid = refs[1:local_levels]
    far = refs[local_levels : local_levels + far_levels]
    tok_ref, wk_ref, wv_ref, sems = refs[local_levels + far_levels :]
    part = tok_ref.shape[0] // parts
    copies = [
        pltpu.make_async_copy(wk_hbm, wk_ref, sems.at[0]),
        pltpu.make_async_copy(wv_hbm, wv_ref, sems.at[1]),
    ]
    for p in range(parts):
        rows = pl.ds(p * part, part)
        copies.append(pltpu.make_async_copy(tok_hbm.at[rows], tok_ref.at[rows], sems.at[2 + p]))
    for copy in (copies[2], *copies[:2], *copies[3:]):
        copy.start()
    copies[0].wait()
    copies[1].wait()
    tops = []
    for p in range(parts):
        copies[2 + p].wait()
        x = tok_ref[p * part : (p + 1) * part, :]
        rows = jnp.concatenate([dot(x, wk_ref[...]), dot(x, wv_ref[...])], axis=1).astype(BF16)
        kv_ref[p * part : (p + 1) * part, :] = rows
        for ref in mid:
            rows = dot(pool_matrix(rows.shape[0]), rows).astype(BF16)
            ref[p * rows.shape[0] : (p + 1) * rows.shape[0], :] = rows
        tops.append(dot(pool_matrix(rows.shape[0]), rows).astype(BF16))
    rows = jnp.concatenate(tops, axis=0)
    for i in range(far_levels):
        if i:
            rows = dot(pool_matrix(rows.shape[0]), rows).astype(BF16)
        far[i][...] = rows


def key_value(tokens, w_key, w_value, local_levels, far_levels):
    tok_rows, width = tokens.shape
    inner = w_key.shape[1]
    parts = tok_rows // (2 * BLOCK)
    out_shape = [shape(tok_rows >> i, 2 * inner) for i in range(local_levels)]
    out_shape += [shape(BLOCK >> i, 2 * inner) for i in range(far_levels)]
    return pl.pallas_call(
        functools.partial(key_value_body, local_levels, far_levels, parts),
        in_specs=[pl.BlockSpec(memory_space=pl.ANY)] * 3,
        out_shape=out_shape,
        scratch_shapes=[
            pltpu.VMEM((tok_rows, width), BF16),
            pltpu.VMEM((width, inner), BF16),
            pltpu.VMEM((width, inner), BF16),
            pltpu.SemaphoreType.DMA((parts + 2,)),
        ],
        compiler_params=params(56),
        cost_estimate=cost(4 * tok_rows * width * inner, 2 * tok_rows * width + 8 * width * inner),
    )(tokens, w_key, w_value)


def pair_body(a_ref, b_ref, wa_ref, wb_ref, x_ref, y_ref):
    x_ref[...] = dot(a_ref[...], wa_ref[...]).astype(BF16)
    y_ref[...] = dot(b_ref[...], wb_ref[...]).astype(BF16)


def project_pair(a, b, wa, wb):
    tok_rows, width = a.shape
    inner = wa.shape[1]
    return pl.pallas_call(
        pair_body,
        out_shape=[shape(tok_rows, inner)] * 2,
        compiler_params=params(8),
        cost_estimate=cost(4 * tok_rows * width * inner, 4 * tok_rows * width + 8 * width * inner),
    )(a, b, wa, wb)


class KeySet:
    def __init__(self, far_rows, far_bits, local_levels):
        mids = local_levels - 1
        self.sizes = [2 * BLOCK] + [BLOCK] * mids + list(far_rows)
        self.bounds = [sum(self.sizes[:i]) for i in range(len(self.sizes) + 1)]
        steps = [0] + list(range(1, local_levels)) + [local_levels + b for b in far_bits]
        self.biases = [float(step) for step in steps]
        self.mids = mids
        self.far_start = self.bounds[1 + mids]
        self.factor = math.log2(math.e) / math.sqrt(HEAD_DIM)

    def here(self, m):
        return pl.ds(pl.multiple_of(m * 2 * BLOCK, 2 * BLOCK), 2 * BLOCK)

    def seats(self, m):
        for i in range(self.mids):
            sibling = jnp.bitwise_xor(jnp.right_shift(m, i), 1)
            yield pl.ds(pl.multiple_of(sibling * BLOCK, BLOCK), BLOCK)

    def rows(self, m, kv_ref, mid_refs, far_refs, cols):
        rows = [kv_ref[self.here(m), cols]]
        rows += [ref[seat, cols] for ref, seat in zip(mid_refs, self.seats(m))]
        rows += [ref[:, cols] for ref in far_refs]
        return jnp.concatenate(rows, axis=0)

    def pieces(self, array):
        return [array[a:b] for a, b in zip(self.bounds, self.bounds[1:])]

    def top(self, raw):
        tops = [
            jnp.max(piece, axis=0, keepdims=True) * self.factor + bias
            for piece, bias in zip(self.pieces(raw), self.biases)
        ]
        return functools.reduce(jnp.maximum, tops)

    def powers(self, raw, top):
        return jnp.concatenate(
            [
                jnp.exp2(piece * self.factor + (bias - top))
                for piece, bias in zip(self.pieces(raw), self.biases)
            ],
            axis=0,
        )


def forward_body(local_levels, far_bits, *refs):
    mids = local_levels - 1
    fars = len(far_bits)
    q_ref, kv_ref = refs[:2]
    mid_refs = refs[2 : 2 + mids]
    far_refs = refs[2 + mids : 2 + mids + fars]
    att_ref, att_t_ref, stat_ref = refs[2 + mids + fars :]
    tok_rows, inner = q_ref.shape
    heads = inner // HEAD_DIM
    keyset = KeySet([r.shape[0] for r in far_refs], far_bits, local_levels)

    def step(m, carry):
        here = keyset.here(m)
        for h in range(heads):
            cols = slice(h * HEAD_DIM, (h + 1) * HEAD_DIM)
            vcols = slice(inner + h * HEAD_DIM, inner + (h + 1) * HEAD_DIM)
            keys = keyset.rows(m, kv_ref, mid_refs, far_refs, cols)
            values = keyset.rows(m, kv_ref, mid_refs, far_refs, vcols)
            raw = dot(keys, q_ref[here, cols], NT)
            top = keyset.top(raw)
            expo = keyset.powers(raw, top)
            inverse = 1.0 / jnp.sum(expo, axis=0, keepdims=True)
            att_t = dot(values, (expo * inverse).astype(BF16), TN).astype(BF16)
            att_t_ref[cols, here] = att_t
            att_ref[here, cols] = att_t.T
            stat_ref[h : h + 1, here] = top
            stat_ref[heads + h : heads + h + 1, here] = inverse
        return carry

    lax.fori_loop(0, tok_rows // (2 * BLOCK), step, 0)


def forward(query, levels, fars, far_bits):
    tok_rows, inner = query.shape
    heads = inner // HEAD_DIM
    set_rows = (len(levels) + 1) * BLOCK + sum(f.shape[0] for f in fars)
    return pl.pallas_call(
        functools.partial(forward_body, len(levels), far_bits),
        out_shape=[
            shape(tok_rows, inner),
            shape(inner, tok_rows),
            shape(2 * heads, tok_rows, F32),
        ],
        compiler_params=params(12),
        cost_estimate=cost(
            4 * tok_rows * set_rows * inner, 12 * tok_rows * inner, tok_rows * set_rows * 2
        ),
    )(query, *levels, *fars)


def backward_body(local_levels, far_bits, *refs):
    mids = local_levels - 1
    fars = len(far_bits)
    q_ref, g_ref, att_t_ref, stat_ref, kv_ref = refs[:5]
    mid_refs = refs[5 : 5 + mids]
    far_refs = refs[5 + mids : 5 + mids + fars]
    outs = refs[5 + mids + fars :]
    dq_ref, dq_t_ref, dkv_ref = outs[:3]
    dmid_refs = outs[3 : 3 + mids]
    dfar_refs = outs[3 + mids : 3 + mids + fars]
    acc_ref = outs[-1]
    tok_rows, inner = q_ref.shape
    heads = inner // HEAD_DIM
    score_scale = 1.0 / math.sqrt(HEAD_DIM)
    keyset = KeySet([r.shape[0] for r in far_refs], far_bits, local_levels)

    for ref in (*dmid_refs, acc_ref):
        ref[...] = jnp.zeros_like(ref)

    def step(m, carry):
        here = keyset.here(m)
        for h in range(heads):
            cols = slice(h * HEAD_DIM, (h + 1) * HEAD_DIM)
            vcols = slice(inner + h * HEAD_DIM, inner + (h + 1) * HEAD_DIM)
            keys = keyset.rows(m, kv_ref, mid_refs, far_refs, cols)
            values = keyset.rows(m, kv_ref, mid_refs, far_refs, vcols)
            q = q_ref[here, cols]
            g = g_ref[here, cols]
            top = stat_ref[h : h + 1, here]
            inverse = stat_ref[heads + h : heads + h + 1, here]
            probs = keyset.powers(dot(keys, q, NT), top) * inverse
            att_t = att_t_ref[cols, here].astype(F32)
            delta = jnp.sum(g.T.astype(F32) * att_t, axis=0, keepdims=True)
            grads = (probs * (dot(values, g, NT) - delta) * score_scale).astype(BF16)
            dq_t = dot(keys, grads, TN).astype(BF16)
            dq_t_ref[cols, here] = dq_t
            dq_ref[here, cols] = dq_t.T
            for part, place in ((dot(grads, q), cols), (dot(probs.astype(BF16), g), vcols)):
                own, *sides = keyset.pieces(part)
                dkv_ref[here, place] = own
                for ref, seat, side in zip(dmid_refs, keyset.seats(m), sides):
                    ref[seat, place] += side
                acc_ref[:, place] += part[keyset.far_start :]
        return carry

    lax.fori_loop(0, tok_rows // (2 * BLOCK), step, 0)
    low = 0
    for ref in dfar_refs:
        ref[...] = acc_ref[low : low + ref.shape[0]].astype(BF16)
        low += ref.shape[0]


def backward(query, grad, attended_t, stats, levels, fars, far_bits):
    tok_rows, inner = query.shape
    far_rows = sum(f.shape[0] for f in fars)
    set_rows = (len(levels) + 1) * BLOCK + far_rows
    return pl.pallas_call(
        functools.partial(backward_body, len(levels), far_bits),
        out_shape=[shape(tok_rows, inner), shape(inner, tok_rows)]
        + [shape(*level.shape, F32) for level in levels]
        + [shape(*f.shape) for f in fars],
        scratch_shapes=[pltpu.VMEM((far_rows, 2 * inner), F32)],
        compiler_params=params(16),
        cost_estimate=cost(
            10 * tok_rows * set_rows * inner, 24 * tok_rows * inner, tok_rows * set_rows * 2
        ),
    )(query, grad, attended_t, stats, *levels, *fars)


def term_body(which, low, left_ref, right_ref, out_ref):
    width, inner = out_ref.shape
    left = left_ref[which * inner : (which + 1) * inner, :]
    out_ref[...] = dot(left, right_ref[:, low : low + width]).astype(BF16).T


def weight_terms(left_t, right, inner, which, part, parts):
    tok_rows = left_t.shape[1]
    width = right.shape[1] // parts
    return pl.pallas_call(
        functools.partial(term_body, which, part * width),
        out_shape=shape(width, inner),
        compiler_params=params(6),
        cost_estimate=cost(2 * inner * tok_rows * width, 2 * tok_rows * (width + inner)),
    )(left_t, right)


def close_body(local_levels, far_bits, dkv_ref, *refs):
    mids = local_levels - 1
    dmid_refs = refs[:mids]
    back_refs = refs[mids : mids + len(far_bits)]
    dk_ref, dv_ref, dkv_t_ref = refs[mids + len(far_bits) :]
    inner = dk_ref.shape[1]
    tile = 2 * BLOCK
    for t in range(dkv_ref.shape[0] // tile):
        here = slice(t * tile, (t + 1) * tile)
        chain = None
        for i in reversed(range(mids)):
            rows = tile >> (i + 1)
            part = dmid_refs[i][t * rows : (t + 1) * rows, :]
            chain = part if chain is None else part + chain
            high = chain.astype(BF16)
            low = (chain - high.astype(F32)).astype(BF16)
            fan = spread_matrix(2 * rows, 1, 0, rows, 0.5)
            chain = dot(fan, high) + dot(fan, low)
        total = dkv_ref[here, :]
        if chain is not None:
            total = total + chain
        for ref, bit in zip(back_refs, far_bits):
            weight = 0.5 ** (local_levels + bit)
            fan = spread_matrix(tile, local_levels + bit, t * tile, ref.shape[0], weight)
            total = total + dot(fan, ref[...])
        final = total.astype(BF16)
        dk_ref[here, :] = final[:, :inner]
        dv_ref[here, :] = final[:, inner:]
        dkv_t_ref[:, here] = final.T


def close_keys(dkv, dmids, backs, far_bits, local_levels):
    tok_rows, double = dkv.shape
    inner = double // 2
    return pl.pallas_call(
        functools.partial(close_body, local_levels, far_bits),
        out_shape=[shape(tok_rows, inner), shape(tok_rows, inner), shape(double, tok_rows)],
        compiler_params=params(8),
        cost_estimate=cost(4 * tok_rows * 256 * double, 20 * tok_rows * double),
    )(dkv, *dmids, *backs)


def out_body(left_ref, weight_ref, out_ref):
    out_ref[...] = dot(left_ref[...], weight_ref[...], NT).astype(BF16)


def project_out(left, weight):
    tok_rows, inner = left.shape
    width = weight.shape[0]
    return pl.pallas_call(
        out_body,
        out_shape=shape(tok_rows, width),
        compiler_params=params(8),
        cost_estimate=cost(2 * tok_rows * inner * width, 2 * tok_rows * width),
    )(left, weight)


def split_body(count, parts, rank_ref, *refs):
    lefts, weights = refs[:count], refs[count : 2 * count]
    outs = refs[2 * count :]
    width = weights[0].shape[0] // parts
    for r in range(parts):
        owner = jnp.bitwise_xor(rank_ref[0], r)
        rows = pl.ds(pl.multiple_of(owner * width, width), width)
        total = None
        for left, weight in zip(lefts, weights):
            product = dot(left[...], weight[rows, :], NT)
            total = product if total is None else total + product
        place = r // 2 * width
        outs[r % 2][:, place : place + width] = total.astype(BF16)


def project_split(lefts, weights, axis):
    count = len(lefts)
    parts = lax.axis_size(axis)
    tok_rows, inner = lefts[0].shape
    width = weights[0].shape[0]
    rank = jnp.reshape(lax.axis_index(axis), (1,)).astype(jnp.int32)
    return pl.pallas_call(
        functools.partial(split_body, count, parts),
        in_specs=[pl.BlockSpec(memory_space=pltpu.SMEM)]
        + [pl.BlockSpec(memory_space=pltpu.VMEM)] * (2 * count),
        out_shape=[shape(tok_rows, width // 2)] * 2,
        compiler_params=params(8),
        cost_estimate=cost(2 * count * tok_rows * inner * width, 2 * tok_rows * width),
    )(rank, *lefts, *weights)


def exchange(block, axis, distance):
    count = lax.axis_size(axis)
    return lax.ppermute(block, axis, [(i, i ^ distance) for i in range(count)])


def add(left, right):
    return (left.astype(F32) + right.astype(F32)).astype(BF16)


def scatter_sum(keep, send, axis):
    parts = lax.axis_size(axis) // 2
    width = keep.shape[1] // parts
    pieces = [keep[:, i * width : (i + 1) * width] for i in range(parts)]
    distance = 1
    while True:
        into = exchange(send, axis, distance)
        for i in reversed(range(len(pieces))):
            pieces[i] = add(pieces[i], into[:, i * width : (i + 1) * width])
        if len(pieces) == 1:
            return pieces[0]
        away = pieces[1::2]
        send = away[0] if len(away) == 1 else jnp.concatenate(away, axis=1)
        pieces = pieces[0::2]
        distance *= 2


def combine_body(own_ref, into_ref, half_ref, across_ref, next_ref, total_ref):
    next_ref[...] = (own_ref[...].astype(F32) + into_ref[...].astype(F32)).astype(BF16)
    total_ref[...] = (half_ref[...].astype(F32) + across_ref[...].astype(F32)).astype(BF16)


def combine(own, into, half, across):
    return pl.pallas_call(
        combine_body,
        out_shape=[shape(*own.shape), shape(*half.shape)],
        compiler_params=pltpu.CompilerParams(vmem_limit_bytes=8 * MIB),
        cost_estimate=cost(2 * own.size, 12 * own.size),
    )(own, into, half, across)


def line_sums(chunks, axis):
    count = lax.axis_size(axis)
    if count < 4:
        return [add(c, exchange(c, axis, 1)) if count == 2 else c for c in chunks]
    rank = jnp.bitwise_and(lax.axis_index(axis), 3)
    at_end = (rank == 0) | (rank == 3)
    inward, across, outward = [], [], []
    for base in range(0, count, 4):
        inward += [(base, base + 1), (base + 3, base + 2)]
        across += [(base + 1, base + 2), (base + 2, base + 1)]
        outward += [(base + 1, base), (base + 2, base + 3)]
    lag = 2
    halves, crossed, totals, sums = [], [], [], []
    for k in range(len(chunks) + lag):
        if k < len(chunks):
            into = lax.ppermute(chunks[k], axis, inward)
        if k < lag:
            halves.append(add(chunks[k], into))
        elif k < len(chunks):
            half, total = combine(chunks[k], into, halves[k - lag], crossed[k - lag])
            halves.append(half)
            totals.append(total)
        else:
            totals.append(add(halves[k - lag], crossed[k - lag]))
        if k < len(chunks):
            crossed.append(lax.ppermute(halves[k], axis, across))
    for total in totals:
        ends = lax.ppermute(total, axis, outward)
        result = jnp.where(at_end, ends, total)
        distance = 4
        while distance < count:
            result = add(result, exchange(result, axis, distance))
            distance *= 2
        sums.append(result)
    return sums


def per_device(tokens, w_query, w_key, w_value, w_out, cotangent):
    tok_rows = tokens.shape[0]
    inner = w_query.shape[1]
    local_levels = (tok_rows // BLOCK).bit_length() - 1
    count = lax.axis_size("seq")
    far_levels = count.bit_length() - 1
    far_bits = [d.bit_length() - 1 for d in range(1, count)]

    parts = key_value(tokens, w_key, w_value, local_levels, far_levels)
    levels = parts[:local_levels]
    tops = parts[local_levels:]
    fars = [exchange(tops[bit], "seq", d) for d, bit in enumerate(far_bits, 1)]
    query, grad = project_pair(tokens, cotangent, w_query, w_out)
    attended, attended_t, stats = forward(query, levels, fars, far_bits)
    results = backward(query, grad, attended_t, stats, levels, fars, far_bits)
    dquery, dquery_t, dkv = results[:3]
    dmids = results[3 : 3 + local_levels - 1]
    dfars = results[3 + local_levels - 1 :]
    backs = [exchange(piece, "seq", d) for d, piece in enumerate(dfars, 1)]
    mixed_part = project_out(attended, w_out)
    mixed = lax.psum_scatter(mixed_part, "head", scatter_dimension=1, tiled=True)
    dkey, dvalue, dkv_t = close_keys(dkv, dmids, backs, far_bits, local_levels)
    keep, send = project_split([dquery, dkey, dvalue], [w_query, w_key, w_value], "head")
    tokens_grad = scatter_sum(keep, send, "head")

    pieces = 2
    chunks = []
    for left, which, right in (
        (attended_t, 0, cotangent),
        (dquery_t, 0, tokens),
        (dkv_t, 0, tokens),
        (dkv_t, 1, tokens),
    ):
        chunks += [weight_terms(left, right, inner, which, p, pieces) for p in range(pieces)]
    sums = line_sums(chunks, "seq")
    out_grad, query_grad, key_grad, value_grad = (
        jnp.concatenate(sums[i : i + pieces], axis=0) for i in range(0, len(sums), pieces)
    )
    return mixed, tokens_grad, query_grad, key_grad, value_grad, out_grad


def solution(mesh):
    return jax.shard_map(
        per_device,
        mesh=mesh,
        in_specs=(
            P(("groups", "seq"), None),
            P(None, "head"),
            P(None, "head"),
            P(None, "head"),
            P(None, "head"),
            P(("groups", "seq"), None),
        ),
        out_specs=(
            P(("groups", "seq"), "head"),
            P(("groups", "seq"), "head"),
            P("groups", "head"),
            P("groups", "head"),
            P("groups", "head"),
            P("groups", "head"),
        ),
        check_vma=False,
    )
```

time: 159 us -> 163 us (1.025)
  Pallas kernels: 62.1 us -> 37.3 us
  starting transfers between devices: 49.5 us -> 64.1 us
  local copies, waits for them, and re-layouts: 1.38 us -> 11.3 us
  other arithmetic: 3.81 us -> 6.85 us
    pallas_call x13 -> x14, Pallas kernels: 55.5 us -> 25.6 us  [the longest x8 6.54 us: weight_terms(): pl.pallas_call(functools.partial(term_body, which, part * width), out_sha...]
    ppermute x8, starting transfers between devices: 23.3 us -> 37.6 us  [line_sums(): into = lax.ppermute(chunks[k], axis, inward)]
    unnamed x34 -> x62, local copies, waits for them, and re-layouts: 1.38 us -> 11.3 us
    pallas_call x6, Pallas kernels: 0.74 us -> 5.69 us  [combine(): pl.pallas_call(combine_body, out_shape=[shape(*own.shape), shape(*half.sh...]
    ppermute x8, waiting for transfers between devices: 2.72 us -> 0.44 us  [line_sums(): into = lax.ppermute(chunks[k], axis, inward)]
    ppermute x6 -> x8, waiting for transfers between devices: 1.33 us -> 3.46 us  [exchange(): return lax.ppermute(block, axis, [(i, i ^ distance) for i in range(count)])]
    convert_element_type x4 -> x6, other arithmetic: 0.26 us -> 2.34 us  [add(): return (left.astype(F32) + right.astype(F32)).astype(BF16)]
    ppermute x6 -> x8, starting transfers between devices: 10.1 us -> 9.18 us  [exchange(): return lax.ppermute(block, axis, [(i, i ^ distance) for i in range(count)])]
  transfers between devices with their start and end apart: 32 -> 33, of which waited for: 9 -> 8; matrix products, arithmetic and copies ran while one was open for 2% -> 4% of each run, Pallas kernels for 24% -> 15%
where the time goes in v3:
time: 163 us; the launch traced here: 162 us
  starting transfers between devices  64.1 us (39%)
  Pallas kernels  37.3 us (23%)
  waiting for transfers between devices  27.7 us (17%)
  between operations  14.7 us (9%)
  local copies, waits for them, and re-layouts  11.3 us (7%)
  other arithmetic  6.85 us (4%)
    ppermute x8, starting transfers between devices, line_sums(): into = lax.ppermute(chunks[k], axis, inward)  37.6 us
    ppermute x8, waiting for transfers between devices, line_sums(): ends = lax.ppermute(total, axis, outward)  23.7 us
    unnamed x62, local copies, waits for them, and re-layouts  11.3 us
    ppermute x8, starting transfers between devices, line_sums(): ends = lax.ppermute(total, axis, outward)  10.5 us
    ppermute x8, starting transfers between devices, exchange(): return lax.ppermute(block, axis, [(i, i ^ distance) for i in range(count)])  9.18 us
    ppermute x8, starting transfers between devices, line_sums(): crossed.append(lax.ppermute(halves[k], axis, across))  6.79 us
    pallas_call x8, Pallas kernels, weight_terms(): pl.pallas_call(functools.partial(term_body, which, part * width), out_sha...  6.54 us
    pallas_call x1, Pallas kernels, backward(): pl.pallas_call(functools.partial(backward_body, len(levels), far_bits), o...  6.09 us
  transfers between devices with their start and end apart: 33, of which 8 were waited for; matrix products, arithmetic and copies ran while one was open for 4% of the time, Pallas kernels for 15%

profile of v3, /device:TPU:0, one launch (start us, length us, event | category | flops | bytes accessed | tf_op | source)
XLA Modules:
  0.0 161.9 jit_solution(13174250203234167823)
XLA Ops:
  7.2 6.0 %shard_map.110 = (bf16[1024,512]{1,0:T(8,128)(2,1)}, bf16[512,512]{1,0:T(8,128)(2,1)}, bf16[256,512]{1,0:T(8,128)(2,1)}, bf16[128,512]{1,0:T(8,128)(2,1)}, bf16[64,512]{1,0:T(8,128)(2,1)}) custom-call(bf16[1024,1024]{1,0:T(8,128)(2,1)} %right_ref.15, bf16[1024,256]{1,0:T(8,128)(2,1)} %refs_4_.1, bf16[1024,256]{1,0:T(8,128)(2,1)} %refs_5_.1), custom_call_target="tpu_custom_call" | custom-call | flops 1073741824 | bytes 4194304 | tf_op jit(solution)/shard_map/pallas_call | solution.py:94
  13.3 3.1 %collective-permute-start = (bf16[128,512]{1,0:T(8,128)(2,1)}, bf16[128,512]{1,0:T(8,128)(2,1)S(1)}, u32[]{:S(2)}, u32[]{:S(2)}) collective-permute-start(bf16[128,512]{1,0:T(8,128)(2,1)} %get-tuple-element.45), channel_id=1, source_target_pairs={{0,4},{4,0},{8,12},{12,8},{1,5},{5,1},{9,13},{13,9},{2,6},{6,2},{1... | collective-permute-start | bytes 393224 | tf_op jit(solution)/shard_map/ppermute | solution.py:396
  16.3 2.6 %collective-permute-start.1 = (bf16[64,512]{1,0:T(8,128)(2,1)}, bf16[64,512]{1,0:T(8,128)(2,1)S(1)}, u32[]{:S(2)}, u32[]{:S(2)}) collective-permute-start(bf16[64,512]{1,0:T(8,128)(2,1)} %get-tuple-element.46), channel_id=1, source_target_pairs={{0,8},{4,12},{8,0},{12,4},{1,9},{5,13},{9,1},{13,5},{2,10},{6,14},... | collective-permute-start | bytes 196616 | tf_op jit(solution)/shard_map/ppermute | solution.py:396
  19.0 1.6 copy-done.1
  20.6 1.2 shard_map.109
  21.8 1.3 collective-permute-done.1.refs_5_.refs_8_
  23.1 2.2 %collective-permute-done.2.refs_6_.refs_9_ = bf16[64,512]{1,0:T(8,128)(2,1)S(1)} collective-permute-done((bf16[64,512]{1,0:T(8,128)(2,1)}, bf16[64,512]{1,0:T(8,128)(2,1)S(1)}, u32[]{:S(2)}, u32[]{:S(2)}) %collective-permute-start.2) | collective-permute-done | bytes 65568 | tf_op jit(solution)/shard_map/ppermute | solution.py:396
  25.3 5.9 %shard_map.111 = (bf16[1024,256]{1,0:T(8,128)(2,1)S(1)}, bf16[256,1024]{1,0:T(8,128)(2,1)S(1)}, f32[4,1024]{1,0:T(4,128)S(1)}) custom-call(bf16[1024,256]{1,0:T(8,128)(2,1)S(1)} %get-tuple-element.41.refs_0_, bf16[1024,512]{1,0:T(8,128)(2,1)S(1)} %copy-done.26, bf16[512,512]{1,0:T(8,128)(2,1)S(1)} %copy-done.27, bf16[256,512]{1,0:T(8,128)(2,1)S(1)} %copy-done.28, ...), custom_call_target="tpu_custom_call" | custom-call | flops 805306368 | bytes 3145728 | tf_op jit(solution)/shard_map/pallas_call | solution.py:206
  31.7 3.7 %collective-permute-start.10 = (bf16[512,256]{1,0:T(8,128)(2,1)S(1)}, bf16[512,256]{1,0:T(8,128)(2,1)}, u32[]{:S(2)}, u32[]{:S(2)}) collective-permute-start(bf16[512,256]{1,0:T(8,128)(2,1)S(1)} %shard_map.118), channel_id=1, source_target_pairs={{0,4},{12,8},{1,5},{13,9},{2,6},{14,10},{3,7},{15,11},{16,20},{28,... | collective-permute-start | bytes 786440 | tf_op jit(solution)/shard_map/ppermute | solution.py:449
  35.4 6.1 %shard_map.113 = (bf16[1024,256]{1,0:T(8,128)(2,1)S(1)}, bf16[256,1024]{1,0:T(8,128)(2,1)S(1)}, f32[1024,512]{1,0:T(8,128)S(1)}, f32[512,512]{1,0:T(8,128)S(1)},...) custom-call(bf16[1024,256]{1,0:T(8,128)(2,1)S(1)} %get-tuple-element.41.r, ...), custom_call_target="tpu_custom_call" | custom-call | flops 2013265920 | bytes 6291456 | tf_op jit(solution)/shard_map/pallas_call | solution.py:276
  41.5 1.0 copy-done.10
  44.1 1.6 shard_map.117.own_ref
  45.7 4.3 %collective-permute-start.9 = (bf16[512,256]{1,0:T(8,128)(2,1)}, bf16[512,256]{1,0:T(8,128)(2,1)}, u32[]{:S(2)}, u32[]{:S(2)}) collective-permute-start(bf16[512,256]{1,0:T(8,128)(2,1)} %shard_map.117.own_ref), channel_id=1, source_target_pairs={{0,4},{12,8},{1,5},{13,9},{2,6},{14,10},{3,7},{15,11},{16,20},{28,... | collective-permute-start | bytes 786440 | tf_op jit(solution)/shard_map/ppermute | solution.py:449
  50.0 1.9 %collective-permute-start.5 = (bf16[64,512]{1,0:T(8,128)(2,1)}, bf16[64,512]{1,0:T(8,128)(2,1)}, u32[]{:S(2)}, u32[]{:S(2)}) collective-permute-start(bf16[64,512]{1,0:T(8,128)(2,1)} %get-tuple-element.57), channel_id=1, source_target_pairs={{0,12},{4,8},{8,4},{12,0},{1,13},{5,9},{9,5},{13,1},{2,14},{6,10},... | collective-permute-start | bytes 196616 | tf_op jit(solution)/shard_map/ppermute | solution.py:396
  52.6 1.3 copy-done.4
  53.9 1.0 copy-done.9
  55.5 1.1 copy-done.3
  57.1 3.7 %collective-permute-start.15 = (bf16[512,256]{1,0:T(8,128)(2,1)S(1)}, bf16[512,256]{1,0:T(8,128)(2,1)S(1)}, u32[]{:S(2)}, u32[]{:S(2)}) collective-permute-start(bf16[512,256]{1,0:T(8,128)(2,1)S(1)} %shard_map.122.own_ref), channel_id=1, source_target_pairs={{0,4},{12,8},{1,5},{13,9},{2,6},{14,10},{3,7},{15,11},{16,20},{28,... | collective-permute-start | bytes 786440 | tf_op jit(solution)/shard_map/ppermute | solution.py:449
  60.8 1.3 collective-permute-start.16
  62.1 3.3 %shard_map.114 = (bf16[1024,256]{1,0:T(8,128)(2,1)S(1)}, bf16[1024,256]{1,0:T(8,128)(2,1)S(1)}, bf16[512,1024]{1,0:T(8,128)(2,1)S(1)}) custom-call(f32[1024,512]{1,0:T(8,128)S(1)} %copy-done.7, f32[512,512]{1,0:T(8,128)S(1)} %copy-done.11, f32[256,512]{1,0:T(8,128)S(1)} %copy-done.17, bf16[128,512]{1,0:T(8,128)(2,1)S(1)} %collective-permute-done.3.refs_2_, ...), custom_call_target="tpu_custom_call" | custom-call | flops 536870912 | bytes 10485760 | tf_op jit(solution)/shard_map/pallas_call | solution.py:340
  67.0 1.0 add_convert_fusion.6.half_ref
  68.7 1.2 shard_map.116.own_ref
  70.0 1.4 collective-permute-start.17
  71.4 5.7 %collective-permute-start.8 = (bf16[512,256]{1,0:T(8,128)(2,1)}, bf16[512,256]{1,0:T(8,128)(2,1)}, u32[]{:S(2)}, u32[]{:S(2)}) collective-permute-start(bf16[512,256]{1,0:T(8,128)(2,1)} %shard_map.116.own_ref), channel_id=1, source_target_pairs={{0,4},{12,8},{1,5},{13,9},{2,6},{14,10},{3,7},{15,11},{16,20},{28,... | collective-permute-start | bytes 786440 | tf_op jit(solution)/shard_map/ppermute | solution.py:449
  77.1 1.9 %shard_map.119 = (bf16[512,256]{1,0:T(8,128)(2,1)}, bf16[512,256]{1,0:T(8,128)(2,1)}) custom-call(bf16[512,256]{1,0:T(8,128)(2,1)} %shard_map.117.own_ref, bf16[512,256]{1,0:T(8,128)(2,1)} %collective-permute-done.9.into_ref, bf16[512,256]{1,0:T(8,128)(2,1)S(1)} %add_convert_fusion.6.half_ref, bf16[512,256]{1,0:T(8,128)(2,1)S(1)} %collective-permute-done.11.across_ref), custom_call_target="tpu_custom_call" | custom-call | flops 262144 | bytes 1572864 | tf_op jit(solution)/shard_map/pallas_call | solution.py:426
  79.0 1.4 collective-permute-start.12
  80.4 1.2 shard_map.121.own_ref
  81.6 4.8 %collective-permute-start.14 = (bf16[512,256]{1,0:T(8,128)(2,1)}, bf16[512,256]{1,0:T(8,128)(2,1)}, u32[]{:S(2)}, u32[]{:S(2)}) collective-permute-start(bf16[512,256]{1,0:T(8,128)(2,1)} %shard_map.121.own_ref), channel_id=1, source_target_pairs={{0,4},{12,8},{1,5},{13,9},{2,6},{14,10},{3,7},{15,11},{16,20},{28,... | collective-permute-start | bytes 786440 | tf_op jit(solution)/shard_map/ppermute | solution.py:449
  87.1 1.5 collective-permute-start.30
  90.5 1.8 %shard_map.115 = (bf16[1024,512]{1,0:T(8,128)(2,1)S(1)}, bf16[1024,512]{1,0:T(8,128)(2,1)S(1)}) custom-call(s32[1]{0:T(128)} %bitcast.rank_ref, bf16[1024,256]{1,0:T(8,128)(2,1)S(1)} %copy-done.30, bf16[1024,256]{1,0:T(8,128)(2,1)S(1)} %copy-done.23, bf16[1024,256]{1,0:T(8,128)(2,1)S(1)} %copy-done.25, bf16[1024,256]{1,0:T(8,128)(2,1)S(1)} %copy-done.15, ...), custom_call_target="tpu_custom_call" | custom-call | flops 1610612736 | bytes 2097152 | tf_op jit(solution)/shard_map/pallas_call | solution.py:384
  92.4 5.1 %collective-permute-start.20 = (bf16[512,256]{1,0:T(8,128)(2,1)S(1)}, bf16[512,256]{1,0:T(8,128)(2,1)S(1)}, u32[]{:S(2)}, u32[]{:S(2)}) collective-permute-start(bf16[512,256]{1,0:T(8,128)(2,1)S(1)} %shard_map.126.own_ref), channel_id=1, source_target_pairs={{0,4},{12,8},{1,5},{13,9},{2,6},{14,10},{3,7},{15,11},{16,20},{28,... | collective-permute-start | bytes 786440 | tf_op jit(solution)/shard_map/ppermute | solution.py:449
  97.5 1.1 shard_map.124
  98.5 1.3 collective-permute-start.31
  101.1 1.3 shard_map.120
  104.2 9.1 %collective-permute-start.23 = (bf16[512,256]{1,0:T(8,128)(2,1)S(1)}, bf16[512,256]{1,0:T(8,128)(2,1)S(1)}, u32[]{:S(2)}, u32[]{:S(2)}) collective-permute-start(bf16[512,256]{1,0:T(8,128)(2,1)S(1)} %shard_map.128.own_ref), channel_id=1, source_target_pairs={{0,4},{12,8},{1,5},{13,9},{2,6},{14,10},{3,7},{15,11},{16,20},{28,... | collective-permute-start | bytes 786440 | tf_op jit(solution)/shard_map/ppermute | solution.py:449
  113.2 1.2 shard_map.125
  115.1 1.3 collective-permute-start.13
  116.4 1.3 collective-permute-start.19
  120.6 5.6 %collective-permute-done.13 = bf16[512,256]{1,0:T(8,128)(2,1)S(1)} collective-permute-done((bf16[512,256]{1,0:T(8,128)(2,1)S(1)}, bf16[512,256]{1,0:T(8,128)(2,1)S(1)}, u32[]{:S(2)}, u32[]{:S(2)}) %collective-permute-start.13) | collective-permute-done | bytes 262176 | tf_op jit(solution)/shard_map/ppermute | solution.py:461
  126.2 1.3 collective-permute-start.22
  127.5 4.3 %collective-permute-done.19 = bf16[512,256]{1,0:T(8,128)(2,1)S(1)} collective-permute-done((bf16[512,256]{1,0:T(8,128)(2,1)S(1)}, bf16[512,256]{1,0:T(8,128)(2,1)S(1)}, u32[]{:S(2)}, u32[]{:S(2)}) %collective-permute-start.19) | collective-permute-done | bytes 262176 | tf_op jit(solution)/shard_map/ppermute | solution.py:461
  131.8 1.3 collective-permute-start.25
  134.1 1.5 collective-permute-start.7
  135.7 1.3 collective-permute-start.27
  137.1 1.3 collective-permute-start.29
  138.5 4.6 %collective-permute-done.25 = bf16[512,256]{1,0:T(8,128)(2,1)S(1)} collective-permute-done((bf16[512,256]{1,0:T(8,128)(2,1)S(1)}, bf16[512,256]{1,0:T(8,128)(2,1)S(1)}, u32[]{:S(2)}, u32[]{:S(2)}) %collective-permute-start.25) | collective-permute-done | bytes 262176 | tf_op jit(solution)/shard_map/ppermute | solution.py:461
  143.9 4.8 %collective-permute-done.27 = bf16[512,256]{1,0:T(8,128)(2,1)S(1)} collective-permute-done((bf16[512,256]{1,0:T(8,128)(2,1)S(1)}, bf16[512,256]{1,0:T(8,128)(2,1)S(1)}, u32[]{:S(2)}, u32[]{:S(2)}) %collective-permute-start.27) | collective-permute-done | bytes 262176 | tf_op jit(solution)/shard_map/ppermute | solution.py:461
  148.7 4.5 %collective-permute-done.29 = bf16[512,256]{1,0:T(8,128)(2,1)S(1)} collective-permute-done((bf16[512,256]{1,0:T(8,128)(2,1)S(1)}, bf16[512,256]{1,0:T(8,128)(2,1)S(1)}, u32[]{:S(2)}, u32[]{:S(2)}) %collective-permute-start.29) | collective-permute-done | bytes 262176 | tf_op jit(solution)/shard_map/ppermute | solution.py:461
  (120 shorter events, 19.3 us)
Async XLA Ops:
  7.2 11.8 %copy-start = (bf16[1024,1024]{1,0:T(8,128)(2,1)S(1)}, bf16[1024,1024]{1,0:T(8,128)(2,1)}, u32[]{:S(2)}) copy-start(bf16[1024,1024]{1,0:T(8,128)(2,1)} %right_ref.15) | copy-start | bytes 6291460
  7.2 11.8 %copy-start.5 = (bf16[1024,256]{1,0:T(8,128)(2,1)S(1)}, bf16[1024,256]{1,0:T(8,128)(2,1)}, u32[]{:S(2)}) copy-start(bf16[1024,256]{1,0:T(8,128)(2,1)} %weight_ref.1) | copy-start | bytes 1572868
  7.2 11.8 %copy-start.14 = (bf16[1024,256]{1,0:T(8,128)(2,1)S(1)}, bf16[1024,256]{1,0:T(8,128)(2,1)}, u32[]{:S(2)}) copy-start(bf16[1024,256]{1,0:T(8,128)(2,1)} %refs_3_.1) | copy-start | bytes 1572868
  7.2 147.9 %reduce-scatter.2.cloned.1.call-start = ((), (), s32[]{:S(2)}) async-start(), calls=%async_computation.1 | async-start | bytes 2621440 | tf_op jit(solution)/shard_map/reduce_scatter | solution.py:491
  13.3 12.0 %collective-permute-start = (bf16[128,512]{1,0:T(8,128)(2,1)}, bf16[128,512]{1,0:T(8,128)(2,1)S(1)}, u32[]{:S(2)}, u32[]{:S(2)}) collective-permute-start(bf16[128,512]{1,0:T(8,128)(2,1)} %get-tuple-element.45), channel_id=1, source_target_pairs={{0,4},{4,0},{8,12},{12,8},{1,5},{5,1},{9,13},{13,9},{2,6},{6,2},{1... | collective-permute-start | bytes 393224 | tf_op jit(solution)/shard_map/ppermute | solution.py:396
  16.3 6.7 %collective-permute-start.1 = (bf16[64,512]{1,0:T(8,128)(2,1)}, bf16[64,512]{1,0:T(8,128)(2,1)S(1)}, u32[]{:S(2)}, u32[]{:S(2)}) collective-permute-start(bf16[64,512]{1,0:T(8,128)(2,1)} %get-tuple-element.46), channel_id=1, source_target_pairs={{0,8},{4,12},{8,0},{12,4},{1,9},{5,13},{9,1},{13,5},{2,10},{6,14},... | collective-permute-start | bytes 196616 | tf_op jit(solution)/shard_map/ppermute | solution.py:396
  18.9 6.3 %collective-permute-start.2 = (bf16[64,512]{1,0:T(8,128)(2,1)}, bf16[64,512]{1,0:T(8,128)(2,1)S(1)}, u32[]{:S(2)}, u32[]{:S(2)}) collective-permute-start(bf16[64,512]{1,0:T(8,128)(2,1)} %get-tuple-element.46), channel_id=1, source_target_pairs={{0,12},{4,8},{8,4},{12,0},{1,13},{5,9},{9,5},{13,1},{2,14},{6,10},... | collective-permute-start | bytes 196616 | tf_op jit(solution)/shard_map/ppermute | solution.py:396
  20.6 4.7 %copy-start.26 = (bf16[1024,512]{1,0:T(8,128)(2,1)S(1)}, bf16[1024,512]{1,0:T(8,128)(2,1)}, u32[]{:S(2)}) copy-start(bf16[1024,512]{1,0:T(8,128)(2,1)} %get-tuple-element.42.refs_1_.refs_4_) | copy-start | bytes 3145732
  20.6 4.7 %copy-start.27 = (bf16[512,512]{1,0:T(8,128)(2,1)S(1)}, bf16[512,512]{1,0:T(8,128)(2,1)}, u32[]{:S(2)}) copy-start(bf16[512,512]{1,0:T(8,128)(2,1)} %get-tuple-element.43.refs_2_.refs_5_) | copy-start | bytes 1572868
  20.6 4.7 %copy-start.28 = (bf16[256,512]{1,0:T(8,128)(2,1)S(1)}, bf16[256,512]{1,0:T(8,128)(2,1)}, u32[]{:S(2)}) copy-start(bf16[256,512]{1,0:T(8,128)(2,1)} %get-tuple-element.44.refs_3_.refs_6_) | copy-start | bytes 786436
  21.8 9.4 %copy-start.2 = (bf16[1024,1024]{1,0:T(8,128)(2,1)S(1)}, bf16[1024,1024]{1,0:T(8,128)(2,1)}, u32[]{:S(2)}) copy-start(bf16[1024,1024]{1,0:T(8,128)(2,1)} %right_ref.13) | copy-start | bytes 6291460
  31.7 35.3 %collective-permute-start.10 = (bf16[512,256]{1,0:T(8,128)(2,1)S(1)}, bf16[512,256]{1,0:T(8,128)(2,1)}, u32[]{:S(2)}, u32[]{:S(2)}) collective-permute-start(bf16[512,256]{1,0:T(8,128)(2,1)S(1)} %shard_map.118), channel_id=1, source_target_pairs={{0,4},{12,8},{1,5},{13,9},{2,6},{14,10},{3,7},{15,11},{16,20},{28,... | collective-permute-start | bytes 786440 | tf_op jit(solution)/shard_map/ppermute | solution.py:449
  44.1 7.7 %copy-start.6 = (f32[1024,512]{1,0:T(8,128)}, f32[1024,512]{1,0:T(8,128)S(1)}, u32[]{:S(2)}) copy-start(f32[1024,512]{1,0:T(8,128)S(1)} %get-tuple-element.52.dkv_ref) | copy-start | bytes 6291460
  44.1 7.7 %copy-start.8 = (bf16[256,1024]{1,0:T(8,128)(2,1)}, bf16[256,1024]{1,0:T(8,128)(2,1)S(1)}, u32[]{:S(2)}) copy-start(bf16[256,1024]{1,0:T(8,128)(2,1)S(1)} %get-tuple-element.63.left_ref) | copy-start | bytes 1572868
  44.1 17.9 %collective-permute-start.3 = (bf16[128,512]{1,0:T(8,128)(2,1)}, bf16[128,512]{1,0:T(8,128)(2,1)S(1)}, u32[]{:S(2)}, u32[]{:S(2)}) collective-permute-start(bf16[128,512]{1,0:T(8,128)(2,1)} %get-tuple-element.55), channel_id=1, source_target_pairs={{0,4},{4,0},{8,12},{12,8},{1,5},{5,1},{9,13},{13,9},{2,6},{6,2},{1... | collective-permute-start | bytes 393224 | tf_op jit(solution)/shard_map/ppermute | solution.py:396
  45.7 31.4 %collective-permute-start.9 = (bf16[512,256]{1,0:T(8,128)(2,1)}, bf16[512,256]{1,0:T(8,128)(2,1)}, u32[]{:S(2)}, u32[]{:S(2)}) collective-permute-start(bf16[512,256]{1,0:T(8,128)(2,1)} %shard_map.117.own_ref), channel_id=1, source_target_pairs={{0,4},{12,8},{1,5},{13,9},{2,6},{14,10},{3,7},{15,11},{16,20},{28,... | collective-permute-start | bytes 786440 | tf_op jit(solution)/shard_map/ppermute | solution.py:449
  50.0 7.1 %collective-permute-start.4 = (bf16[64,512]{1,0:T(8,128)(2,1)}, bf16[64,512]{1,0:T(8,128)(2,1)}, u32[]{:S(2)}, u32[]{:S(2)}) collective-permute-start(bf16[64,512]{1,0:T(8,128)(2,1)} %get-tuple-element.56), channel_id=1, source_target_pairs={{0,8},{4,12},{8,0},{12,4},{1,9},{5,13},{9,1},{13,5},{2,10},{6,14},... | collective-permute-start | bytes 196616 | tf_op jit(solution)/shard_map/ppermute | solution.py:396
  50.0 10.8 %collective-permute-start.5 = (bf16[64,512]{1,0:T(8,128)(2,1)}, bf16[64,512]{1,0:T(8,128)(2,1)}, u32[]{:S(2)}, u32[]{:S(2)}) collective-permute-start(bf16[64,512]{1,0:T(8,128)(2,1)} %get-tuple-element.57), channel_id=1, source_target_pairs={{0,12},{4,8},{8,4},{12,0},{1,13},{5,9},{9,5},{13,1},{2,14},{6,10},... | collective-permute-start | bytes 196616 | tf_op jit(solution)/shard_map/ppermute | solution.py:396
  55.0 7.1 %copy-start.11 = (f32[512,512]{1,0:T(8,128)S(1)}, f32[512,512]{1,0:T(8,128)}, u32[]{:S(2)}) copy-start(f32[512,512]{1,0:T(8,128)} %copy-done.10) | copy-start | bytes 3145732
  56.5 8.9 %copy-start.12 = (bf16[512,256]{1,0:T(8,128)(2,1)}, bf16[512,256]{1,0:T(8,128)(2,1)S(1)}, u32[]{:S(2)}) copy-start(bf16[512,256]{1,0:T(8,128)(2,1)S(1)} %shard_map.122.own_ref) | copy-start | bytes 786436
  56.5 5.5 %copy-start.7 = (f32[1024,512]{1,0:T(8,128)S(1)}, f32[1024,512]{1,0:T(8,128)}, u32[]{:S(2)}) copy-start(f32[1024,512]{1,0:T(8,128)} %copy-done.6) | copy-start | bytes 6291460
  56.5 5.5 %copy-start.17 = (f32[256,512]{1,0:T(8,128)S(1)}, f32[256,512]{1,0:T(8,128)}, u32[]{:S(2)}) copy-start(f32[256,512]{1,0:T(8,128)} %copy-done.16) | copy-start | bytes 1572868
  57.1 29.3 %collective-permute-start.15 = (bf16[512,256]{1,0:T(8,128)(2,1)S(1)}, bf16[512,256]{1,0:T(8,128)(2,1)S(1)}, u32[]{:S(2)}, u32[]{:S(2)}) collective-permute-start(bf16[512,256]{1,0:T(8,128)(2,1)S(1)} %shard_map.122.own_ref), channel_id=1, source_target_pairs={{0,4},{12,8},{1,5},{13,9},{2,6},{14,10},{3,7},{15,11},{16,20},{28,... | collective-permute-start | bytes 786440 | tf_op jit(solution)/shard_map/ppermute | solution.py:449
  60.8 9.2 %collective-permute-start.16 = (bf16[512,256]{1,0:T(8,128)(2,1)S(1)}, bf16[512,256]{1,0:T(8,128)(2,1)S(1)}, u32[]{:S(2)}, u32[]{:S(2)}) collective-permute-start(bf16[512,256]{1,0:T(8,128)(2,1)S(1)} %shard_map.123), channel_id=1, source_target_pairs={{0,4},{12,8},{1,5},{13,9},{2,6},{14,10},{3,7},{15,11},{16,20},{28,... | collective-permute-start | bytes 786440 | tf_op jit(solution)/shard_map/ppermute | solution.py:449
  68.0 9.1 %collective-permute-start.11 = (bf16[512,256]{1,0:T(8,128)(2,1)S(1)}, bf16[512,256]{1,0:T(8,128)(2,1)S(1)}, u32[]{:S(2)}, u32[]{:S(2)}) collective-permute-start(bf16[512,256]{1,0:T(8,128)(2,1)S(1)} %add_convert_fusion.6.half_ref), channel_id=1, source_target_pairs={{4,8},{8,4},{5,9},{9,5},{6,10},{10,6},{7,11},{11,7},{20,24},{24,20... | collective-permute-start | bytes 786440 | tf_op jit(solution)/shard_map/ppermute | solution.py:459
  70.0 22.4 %collective-permute-start.17 = (bf16[512,256]{1,0:T(8,128)(2,1)S(1)}, bf16[512,256]{1,0:T(8,128)(2,1)}, u32[]{:S(2)}, u32[]{:S(2)}) collective-permute-start(bf16[512,256]{1,0:T(8,128)(2,1)S(1)} %add_convert_fusion.5.half_ref), channel_id=1, source_target_pairs={{4,8},{8,4},{5,9},{9,5},{6,10},{10,6},{7,11},{11,7},{20,24},{24,20... | collective-permute-start | bytes 786440 | tf_op jit(solution)/shard_map/ppermute | solution.py:459
  71.4 27.1 %collective-permute-start.8 = (bf16[512,256]{1,0:T(8,128)(2,1)}, bf16[512,256]{1,0:T(8,128)(2,1)}, u32[]{:S(2)}, u32[]{:S(2)}) collective-permute-start(bf16[512,256]{1,0:T(8,128)(2,1)} %shard_map.116.own_ref), channel_id=1, source_target_pairs={{0,4},{12,8},{1,5},{13,9},{2,6},{14,10},{3,7},{15,11},{16,20},{28,... | collective-permute-start | bytes 786440 | tf_op jit(solution)/shard_map/ppermute | solution.py:449
  79.0 20.8 %collective-permute-start.12 = (bf16[512,256]{1,0:T(8,128)(2,1)}, bf16[512,256]{1,0:T(8,128)(2,1)}, u32[]{:S(2)}, u32[]{:S(2)}) collective-permute-start(bf16[512,256]{1,0:T(8,128)(2,1)} %get-tuple-element.64.half_ref), channel_id=1, source_target_pairs={{4,8},{8,4},{5,9},{9,5},{6,10},{10,6},{7,11},{11,7},{20,24},{24,20... | collective-permute-start | bytes 786440 | tf_op jit(solution)/shard_map/ppermute | solution.py:459
  81.6 20.8 %collective-permute-start.14 = (bf16[512,256]{1,0:T(8,128)(2,1)}, bf16[512,256]{1,0:T(8,128)(2,1)}, u32[]{:S(2)}, u32[]{:S(2)}) collective-permute-start(bf16[512,256]{1,0:T(8,128)(2,1)} %shard_map.121.own_ref), channel_id=1, source_target_pairs={{0,4},{12,8},{1,5},{13,9},{2,6},{14,10},{3,7},{15,11},{16,20},{28,... | collective-permute-start | bytes 786440 | tf_op jit(solution)/shard_map/ppermute | solution.py:449
  87.1 15.3 %collective-permute-start.30 = (bf16[512,256]{1,0:T(8,128)(2,1)}, bf16[512,256]{1,0:T(8,128)(2,1)}, u32[]{:S(2)}, u32[]{:S(2)}) collective-permute-start(bf16[512,256]{1,0:T(8,128)(2,1)} %get-tuple-element.74), channel_id=1, source_target_pairs={{4,0},{8,12},{5,1},{9,13},{6,2},{10,14},{7,3},{11,15},{20,16},{24,... | collective-permute-start | bytes 786440 | tf_op jit(solution)/shard_map/ppermute | solution.py:461
  90.5 6.9 %copy-start.13 = (bf16[512,256]{1,0:T(8,128)(2,1)S(1)}, bf16[512,256]{1,0:T(8,128)(2,1)}, u32[]{:S(2)}) copy-start(bf16[512,256]{1,0:T(8,128)(2,1)} %copy-done.12) | copy-start | bytes 786436
  90.5 6.9 %copy-start.19 = (bf16[512,256]{1,0:T(8,128)(2,1)S(1)}, bf16[512,256]{1,0:T(8,128)(2,1)}, u32[]{:S(2)}) copy-start(bf16[512,256]{1,0:T(8,128)(2,1)} %copy-done.18) | copy-start | bytes 786436
  92.4 22.0 %collective-permute-start.20 = (bf16[512,256]{1,0:T(8,128)(2,1)S(1)}, bf16[512,256]{1,0:T(8,128)(2,1)S(1)}, u32[]{:S(2)}, u32[]{:S(2)}) collective-permute-start(bf16[512,256]{1,0:T(8,128)(2,1)S(1)} %shard_map.126.own_ref), channel_id=1, source_target_pairs={{0,4},{12,8},{1,5},{13,9},{2,6},{14,10},{3,7},{15,11},{16,20},{28,... | collective-permute-start | bytes 786440 | tf_op jit(solution)/shard_map/ppermute | solution.py:449
  98.5 16.6 %collective-permute-start.31 = (bf16[512,256]{1,0:T(8,128)(2,1)S(1)}, bf16[512,256]{1,0:T(8,128)(2,1)S(1)}, u32[]{:S(2)}, u32[]{:S(2)}) collective-permute-start(bf16[512,256]{1,0:T(8,128)(2,1)S(1)} %get-tuple-element.75), channel_id=1, source_target_pairs={{4,0},{8,12},{5,1},{9,13},{6,2},{10,14},{7,3},{11,15},{20,16},{24,... | collective-permute-start | bytes 786440 | tf_op jit(solution)/shard_map/ppermute | solution.py:461
  99.8 4.3 %collective-permute-start.18 = (bf16[512,256]{1,0:T(8,128)(2,1)S(1)}, bf16[512,256]{1,0:T(8,128)(2,1)S(1)}, u32[]{:S(2)}, u32[]{:S(2)}) collective-permute-start(bf16[512,256]{1,0:T(8,128)(2,1)S(1)} %get-tuple-element.66.half_ref), channel_id=1, source_target_pairs={{4,8},{8,4},{5,9},{9,5},{6,10},{10,6},{7,11},{11,7},{20,24},{24,20... | collective-permute-start | bytes 786440 | tf_op jit(solution)/shard_map/ppermute | solution.py:459
  102.4 31.6 %collective-permute-start.6 = (bf16[1024,512]{1,0:T(8,128)(2,1)S(1)}, bf16[1024,512]{1,0:T(8,128)(2,1)S(1)}, u32[]{:S(2)}, u32[]{:S(2)}) collective-permute-start(bf16[1024,512]{1,0:T(8,128)(2,1)S(1)} %get-tuple-element.61), channel_id=1, source_target_pairs={{0,1},{1,0},{2,3},{3,2},{4,5},{5,4},{6,7},{7,6},{8,9},{9,8},{10,11... | collective-permute-start | bytes 3145736 | tf_op jit(solution)/shard_map/ppermute | solution.py:396
  102.5 14.0 %collective-permute-start.21 = (bf16[512,256]{1,0:T(8,128)(2,1)S(1)}, bf16[512,256]{1,0:T(8,128)(2,1)S(1)}, u32[]{:S(2)}, u32[]{:S(2)}) collective-permute-start(bf16[512,256]{1,0:T(8,128)(2,1)S(1)} %get-tuple-element.68.half_ref), channel_id=1, source_target_pairs={{4,8},{8,4},{5,9},{9,5},{6,10},{10,6},{7,11},{11,7},{20,24},{24,20... | collective-permute-start | bytes 786440 | tf_op jit(solution)/shard_map/ppermute | solution.py:459
  104.2 15.0 %collective-permute-start.23 = (bf16[512,256]{1,0:T(8,128)(2,1)S(1)}, bf16[512,256]{1,0:T(8,128)(2,1)S(1)}, u32[]{:S(2)}, u32[]{:S(2)}) collective-permute-start(bf16[512,256]{1,0:T(8,128)(2,1)S(1)} %shard_map.128.own_ref), channel_id=1, source_target_pairs={{0,4},{12,8},{1,5},{13,9},{2,6},{14,10},{3,7},{15,11},{16,20},{28,... | collective-permute-start | bytes 786440 | tf_op jit(solution)/shard_map/ppermute | solution.py:449
  114.4 5.4 %collective-permute-start.24 = (bf16[512,256]{1,0:T(8,128)(2,1)S(1)}, bf16[512,256]{1,0:T(8,128)(2,1)S(1)}, u32[]{:S(2)}, u32[]{:S(2)}) collective-permute-start(bf16[512,256]{1,0:T(8,128)(2,1)S(1)} %get-tuple-element.70.half_ref), channel_id=1, source_target_pairs={{4,8},{8,4},{5,9},{9,5},{6,10},{10,6},{7,11},{11,7},{20,24},{24,20... | collective-permute-start | bytes 786440 | tf_op jit(solution)/shard_map/ppermute | solution.py:459
  115.1 11.1 %collective-permute-start.13 = (bf16[512,256]{1,0:T(8,128)(2,1)S(1)}, bf16[512,256]{1,0:T(8,128)(2,1)S(1)}, u32[]{:S(2)}, u32[]{:S(2)}) collective-permute-start(bf16[512,256]{1,0:T(8,128)(2,1)S(1)} %get-tuple-element.65), channel_id=1, source_target_pairs={{4,0},{8,12},{5,1},{9,13},{6,2},{10,14},{7,3},{11,15},{20,16},{24,... | collective-permute-start | bytes 786440 | tf_op jit(solution)/shard_map/ppermute | solution.py:461
  116.4 15.3 %collective-permute-start.19 = (bf16[512,256]{1,0:T(8,128)(2,1)S(1)}, bf16[512,256]{1,0:T(8,128)(2,1)S(1)}, u32[]{:S(2)}, u32[]{:S(2)}) collective-permute-start(bf16[512,256]{1,0:T(8,128)(2,1)S(1)} %get-tuple-element.67), channel_id=1, source_target_pairs={{4,0},{8,12},{5,1},{9,13},{6,2},{10,14},{7,3},{11,15},{20,16},{24,... | collective-permute-start | bytes 786440 | tf_op jit(solution)/shard_map/ppermute | solution.py:461
  119.1 16.5 %collective-permute-start.26 = (bf16[512,256]{1,0:T(8,128)(2,1)S(1)}, bf16[512,256]{1,0:T(8,128)(2,1)S(1)}, u32[]{:S(2)}, u32[]{:S(2)}) collective-permute-start(bf16[512,256]{1,0:T(8,128)(2,1)S(1)} %get-tuple-element.72), channel_id=1, source_target_pairs={{4,8},{8,4},{5,9},{9,5},{6,10},{10,6},{7,11},{11,7},{20,24},{24,20... | collective-permute-start | bytes 786440 | tf_op jit(solution)/shard_map/ppermute | solution.py:459
  119.9 17.1 %collective-permute-start.28 = (bf16[512,256]{1,0:T(8,128)(2,1)S(1)}, bf16[512,256]{1,0:T(8,128)(2,1)S(1)}, u32[]{:S(2)}, u32[]{:S(2)}) collective-permute-start(bf16[512,256]{1,0:T(8,128)(2,1)S(1)} %get-tuple-element.73), channel_id=1, source_target_pairs={{4,8},{8,4},{5,9},{9,5},{6,10},{10,6},{7,11},{11,7},{20,24},{24,20... | collective-permute-start | bytes 786440 | tf_op jit(solution)/shard_map/ppermute | solution.py:459
  126.2 12.2 %collective-permute-start.22 = (bf16[512,256]{1,0:T(8,128)(2,1)S(1)}, bf16[512,256]{1,0:T(8,128)(2,1)S(1)}, u32[]{:S(2)}, u32[]{:S(2)}) collective-permute-start(bf16[512,256]{1,0:T(8,128)(2,1)S(1)} %get-tuple-element.69), channel_id=1, source_target_pairs={{4,0},{8,12},{5,1},{9,13},{6,2},{10,14},{7,3},{11,15},{20,16},{24,... | collective-permute-start | bytes 786440 | tf_op jit(solution)/shard_map/ppermute | solution.py:461
  131.8 11.2 %collective-permute-start.25 = (bf16[512,256]{1,0:T(8,128)(2,1)S(1)}, bf16[512,256]{1,0:T(8,128)(2,1)S(1)}, u32[]{:S(2)}, u32[]{:S(2)}) collective-permute-start(bf16[512,256]{1,0:T(8,128)(2,1)S(1)} %get-tuple-element.71), channel_id=1, source_target_pairs={{4,0},{8,12},{5,1},{9,13},{6,2},{10,14},{7,3},{11,15},{20,16},{24,... | collective-permute-start | bytes 786440 | tf_op jit(solution)/shard_map/ppermute | solution.py:461
  134.1 20.0 %collective-permute-start.7 = (bf16[1024,256]{1,0:T(8,128)(2,1)S(1)}, bf16[1024,256]{1,0:T(8,128)(2,1)S(1)}, u32[]{:S(2)}, u32[]{:S(2)}) collective-permute-start(bf16[1024,256]{1,0:T(8,128)(2,1)S(1)} %add_convert_fusion.1), channel_id=1, source_target_pairs={{0,2},{1,3},{2,0},{3,1},{4,6},{5,7},{6,4},{7,5},{8,10},{9,11},{10,... | collective-permute-start | bytes 1572872 | tf_op jit(solution)/shard_map/ppermute | solution.py:396
  135.7 12.9 %collective-permute-start.27 = (bf16[512,256]{1,0:T(8,128)(2,1)S(1)}, bf16[512,256]{1,0:T(8,128)(2,1)S(1)}, u32[]{:S(2)}, u32[]{:S(2)}) collective-permute-start(bf16[512,256]{1,0:T(8,128)(2,1)S(1)} %add_convert_fusion.4), channel_id=1, source_target_pairs={{4,0},{8,12},{5,1},{9,13},{6,2},{10,14},{7,3},{11,15},{20,16},{24,... | collective-permute-start | bytes 786440 | tf_op jit(solution)/shard_map/ppermute | solution.py:461
  137.1 16.1 %collective-permute-start.29 = (bf16[512,256]{1,0:T(8,128)(2,1)S(1)}, bf16[512,256]{1,0:T(8,128)(2,1)S(1)}, u32[]{:S(2)}, u32[]{:S(2)}) collective-permute-start(bf16[512,256]{1,0:T(8,128)(2,1)S(1)} %add_convert_fusion.3), channel_id=1, source_target_pairs={{4,0},{8,12},{5,1},{9,13},{6,2},{10,14},{7,3},{11,15},{20,16},{24,... | collective-permute-start | bytes 786440 | tf_op jit(solution)/shard_map/ppermute | solution.py:461
  (16 other events, 19.0 us)
Sparse Core Ops, SparseCore 0:
  54.1 31.0 reduce-scatter.1

commit v4 on v3

--- a/solution.py
+++ b/solution.py
@@ -31,6 +31,17 @@
     return pl.CostEstimate(flops=int(flops), bytes_accessed=int(moved), transcendentals=int(exps))
 
 
+def run(body, ready, after=(), in_specs=None, **options):
+    count, extra = len(ready), len(after)
+
+    def kernel(*refs):
+        body(*refs[:count], *refs[count + extra :])
+
+    in_specs = in_specs or [pl.BlockSpec(memory_space=pltpu.VMEM)] * count
+    in_specs = in_specs + [pl.BlockSpec(memory_space=pl.ANY)] * extra
+    return pl.pallas_call(kernel, in_specs=in_specs, **options)(*ready, *after)
+
+
 def shape(rows, cols, dtype=BF16):
     return jax.ShapeDtypeStruct((rows, cols), dtype)
 
@@ -51,75 +62,96 @@
     return jnp.where(jnp.right_shift(row, step_bits) == col, weight, 0.0).astype(BF16)
 
 
-def key_value_body(local_levels, far_levels, parts, tok_hbm, wk_hbm, wv_hbm, *refs):
-    kv_ref = refs[0]
-    mid = refs[1:local_levels]
-    far = refs[local_levels : local_levels + far_levels]
-    tok_ref, wk_ref, wv_ref, sems = refs[local_levels + far_levels :]
+def key_value_body(local_levels, far_levels, parts, tok_hbm, wk_hbm, wv_hbm, wq_hbm, *refs):
+    count = local_levels + 1
+    out_hbm = refs[:count]
+    far = refs[count : count + far_levels]
+    refs = refs[count + far_levels :]
+    tok_ref, wk_ref, wv_ref, wq_ref = refs[:4]
+    held = refs[4 : 4 + count]
+    in_sems, out_sems = refs[4 + count :]
     part = tok_ref.shape[0] // parts
-    copies = [
-        pltpu.make_async_copy(wk_hbm, wk_ref, sems.at[0]),
-        pltpu.make_async_copy(wv_hbm, wv_ref, sems.at[1]),
-    ]
+
+    def fetch(source, target, i):
+        copy = pltpu.make_async_copy(source, target, in_sems.at[i])
+        copy.start()
+        return copy
+
+    def flush(i):
+        copy = pltpu.make_async_copy(held[i], out_hbm[i], out_sems.at[i])
+        copy.start()
+        return copy
+
+    weights = [fetch(wk_hbm, wk_ref, 0), fetch(wv_hbm, wv_ref, 1)]
+    tiles = []
     for p in range(parts):
         rows = pl.ds(p * part, part)
-        copies.append(pltpu.make_async_copy(tok_hbm.at[rows], tok_ref.at[rows], sems.at[2 + p]))
-    for copy in (copies[2], *copies[:2], *copies[3:]):
-        copy.start()
-    copies[0].wait()
-    copies[1].wait()
-    tops = []
+        tiles.append(fetch(tok_hbm.at[rows], tok_ref.at[rows], 3 + p))
+    weights.append(fetch(wq_hbm, wq_ref, 2))
+    kv_ref, q_ref = held[0], held[-1]
+    weights[0].wait()
+    weights[1].wait()
     for p in range(parts):
-        copies[2 + p].wait()
-        x = tok_ref[p * part : (p + 1) * part, :]
-        rows = jnp.concatenate([dot(x, wk_ref[...]), dot(x, wv_ref[...])], axis=1).astype(BF16)
-        kv_ref[p * part : (p + 1) * part, :] = rows
-        for ref in mid:
-            rows = dot(pool_matrix(rows.shape[0]), rows).astype(BF16)
-            ref[p * rows.shape[0] : (p + 1) * rows.shape[0], :] = rows
-        tops.append(dot(pool_matrix(rows.shape[0]), rows).astype(BF16))
-    rows = jnp.concatenate(tops, axis=0)
+        tiles[p].wait()
+        here = slice(p * part, (p + 1) * part)
+        x = tok_ref[here, :]
+        both = jnp.concatenate([dot(x, wk_ref[...]), dot(x, wv_ref[...])], axis=1)
+        kv_ref[here, :] = both.astype(BF16)
+    flushes = [flush(0)]
+    weights[2].wait()
+    q_ref[...] = dot(tok_ref[...], wq_ref[...]).astype(BF16)
+    pool = pool_matrix(part)
+    source = kv_ref
+    for i in range(1, local_levels):
+        rows = source.shape[0]
+        for low in range(0, rows, part):
+            held[i][low // 2 : (low + part) // 2, :] = dot(pool, source[low : low + part, :]).astype(BF16)
+        flushes.append(flush(i))
+        source = held[i]
+    flushes.append(flush(count - 1))
+    rows = dot(pool, source[...]).astype(BF16)
     for i in range(far_levels):
         if i:
             rows = dot(pool_matrix(rows.shape[0]), rows).astype(BF16)
         far[i][...] = rows
-
-
-def key_value(tokens, w_key, w_value, local_levels, far_levels):
+    for copy in flushes:
+        copy.wait()
+
+
+def key_value(tokens, w_key, w_value, w_query, local_levels, far_levels):
     tok_rows, width = tokens.shape
     inner = w_key.shape[1]
     parts = tok_rows // (2 * BLOCK)
-    out_shape = [shape(tok_rows >> i, 2 * inner) for i in range(local_levels)]
-    out_shape += [shape(BLOCK >> i, 2 * inner) for i in range(far_levels)]
+    held = [(tok_rows >> i, 2 * inner) for i in range(local_levels)] + [(tok_rows, inner)]
+    tops = [(BLOCK >> i, 2 * inner) for i in range(far_levels)]
     return pl.pallas_call(
         functools.partial(key_value_body, local_levels, far_levels, parts),
-        in_specs=[pl.BlockSpec(memory_space=pl.ANY)] * 3,
-        out_shape=out_shape,
-        scratch_shapes=[
-            pltpu.VMEM((tok_rows, width), BF16),
-            pltpu.VMEM((width, inner), BF16),
-            pltpu.VMEM((width, inner), BF16),
-            pltpu.SemaphoreType.DMA((parts + 2,)),
-        ],
+        in_specs=[pl.BlockSpec(memory_space=pl.ANY)] * 4,
+        out_specs=[pl.BlockSpec(memory_space=pl.ANY)] * len(held)
+        + [pl.BlockSpec(memory_space=pltpu.VMEM)] * len(tops),
+        out_shape=[shape(*dims) for dims in held + tops],
+        scratch_shapes=[pltpu.VMEM((tok_rows, width), BF16)]
+        + [pltpu.VMEM((width, inner), BF16)] * 3
+        + [pltpu.VMEM(dims, BF16) for dims in held]
+        + [pltpu.SemaphoreType.DMA((parts + 3,)), pltpu.SemaphoreType.DMA((len(held),))],
         compiler_params=params(56),
-        cost_estimate=cost(4 * tok_rows * width * inner, 2 * tok_rows * width + 8 * width * inner),
-    )(tokens, w_key, w_value)
-
-
-def pair_body(a_ref, b_ref, wa_ref, wb_ref, x_ref, y_ref):
-    x_ref[...] = dot(a_ref[...], wa_ref[...]).astype(BF16)
-    y_ref[...] = dot(b_ref[...], wb_ref[...]).astype(BF16)
-
-
-def project_pair(a, b, wa, wb):
-    tok_rows, width = a.shape
-    inner = wa.shape[1]
+        cost_estimate=cost(6 * tok_rows * width * inner, 2 * tok_rows * width + 12 * width * inner),
+    )(tokens, w_key, w_value, w_query)
+
+
+def project_body(left_ref, weight_ref, out_ref):
+    out_ref[...] = dot(left_ref[...], weight_ref[...]).astype(BF16)
+
+
+def project(left, weight):
+    tok_rows, width = left.shape
+    inner = weight.shape[1]
     return pl.pallas_call(
-        pair_body,
-        out_shape=[shape(tok_rows, inner)] * 2,
-        compiler_params=params(8),
-        cost_estimate=cost(4 * tok_rows * width * inner, 4 * tok_rows * width + 8 * width * inner),
-    )(a, b, wa, wb)
+        project_body,
+        out_shape=shape(tok_rows, inner),
+        compiler_params=params(4),
+        cost_estimate=cost(2 * tok_rows * width * inner, 2 * tok_rows * width + 4 * width * inner),
+    )(left, weight)
 
 
 class KeySet:
@@ -210,7 +242,7 @@
             shape(inner, tok_rows),
             shape(2 * heads, tok_rows, F32),
         ],
-        compiler_params=params(12),
+        compiler_params=params(8),
         cost_estimate=cost(
             4 * tok_rows * set_rows * inner, 12 * tok_rows * inner, tok_rows * set_rows * 2
         ),
@@ -225,8 +257,8 @@
     far_refs = refs[5 + mids : 5 + mids + fars]
     outs = refs[5 + mids + fars :]
     dq_ref, dq_t_ref, dkv_ref = outs[:3]
-    dmid_refs = outs[3 : 3 + mids]
-    dfar_refs = outs[3 + mids : 3 + mids + fars]
+    dfar_refs = outs[3 : 3 + fars]
+    dmid_refs = outs[3 + fars : 3 + fars + mids]
     acc_ref = outs[-1]
     tok_rows, inner = q_ref.shape
     heads = inner // HEAD_DIM
@@ -267,23 +299,35 @@
     for ref in dfar_refs:
         ref[...] = acc_ref[low : low + ref.shape[0]].astype(BF16)
         low += ref.shape[0]
-
-
-def backward(query, grad, attended_t, stats, levels, fars, far_bits):
+    fan = spread_matrix(2 * BLOCK, 1, 0, BLOCK, 0.5)
+    targets = (dkv_ref, *dmid_refs)
+    for i in reversed(range(mids)):
+        for t in range(dmid_refs[i].shape[0] // BLOCK):
+            part = dmid_refs[i][t * BLOCK : (t + 1) * BLOCK, :]
+            high = part.astype(BF16)
+            low = (part - high.astype(F32)).astype(BF16)
+            rows = slice(2 * t * BLOCK, 2 * (t + 1) * BLOCK)
+            targets[i][rows, :] += dot(fan, high) + dot(fan, low)
+
+
+def backward(query, grad, attended_t, stats, levels, fars, far_bits, after):
     tok_rows, inner = query.shape
     far_rows = sum(f.shape[0] for f in fars)
     set_rows = (len(levels) + 1) * BLOCK + far_rows
-    return pl.pallas_call(
+    return run(
         functools.partial(backward_body, len(levels), far_bits),
+        [query, grad, attended_t, stats, *levels, *fars],
+        after,
         out_shape=[shape(tok_rows, inner), shape(inner, tok_rows)]
-        + [shape(*level.shape, F32) for level in levels]
+        + [shape(tok_rows, 2 * inner, F32)]
         + [shape(*f.shape) for f in fars],
-        scratch_shapes=[pltpu.VMEM((far_rows, 2 * inner), F32)],
-        compiler_params=params(16),
+        scratch_shapes=[pltpu.VMEM(level.shape, F32) for level in levels[1:]]
+        + [pltpu.VMEM((far_rows, 2 * inner), F32)],
+        compiler_params=params(10),
         cost_estimate=cost(
             10 * tok_rows * set_rows * inner, 24 * tok_rows * inner, tok_rows * set_rows * 2
         ),
-    )(query, grad, attended_t, stats, *levels, *fars)
+    )
 
 
 def term_body(which, low, left_ref, right_ref, out_ref):
@@ -292,38 +336,27 @@
     out_ref[...] = dot(left, right_ref[:, low : low + width]).astype(BF16).T
 
 
-def weight_terms(left_t, right, inner, which, part, parts):
+def weight_terms(left_t, right, inner, which, part, parts, after):
     tok_rows = left_t.shape[1]
     width = right.shape[1] // parts
-    return pl.pallas_call(
+    return run(
         functools.partial(term_body, which, part * width),
+        [left_t, right],
+        after,
         out_shape=shape(width, inner),
-        compiler_params=params(6),
+        compiler_params=params(3),
         cost_estimate=cost(2 * inner * tok_rows * width, 2 * tok_rows * (width + inner)),
-    )(left_t, right)
+    )
 
 
 def close_body(local_levels, far_bits, dkv_ref, *refs):
-    mids = local_levels - 1
-    dmid_refs = refs[:mids]
-    back_refs = refs[mids : mids + len(far_bits)]
-    dk_ref, dv_ref, dkv_t_ref = refs[mids + len(far_bits) :]
+    back_refs = refs[: len(far_bits)]
+    dk_ref, dv_ref, dkv_t_ref = refs[len(far_bits) :]
     inner = dk_ref.shape[1]
     tile = 2 * BLOCK
     for t in range(dkv_ref.shape[0] // tile):
         here = slice(t * tile, (t + 1) * tile)
-        chain = None
-        for i in reversed(range(mids)):
-            rows = tile >> (i + 1)
-            part = dmid_refs[i][t * rows : (t + 1) * rows, :]
-            chain = part if chain is None else part + chain
-            high = chain.astype(BF16)
-            low = (chain - high.astype(F32)).astype(BF16)
-            fan = spread_matrix(2 * rows, 1, 0, rows, 0.5)
-            chain = dot(fan, high) + dot(fan, low)
         total = dkv_ref[here, :]
-        if chain is not None:
-            total = total + chain
         for ref, bit in zip(back_refs, far_bits):
             weight = 0.5 ** (local_levels + bit)
             fan = spread_matrix(tile, local_levels + bit, t * tile, ref.shape[0], weight)
@@ -334,30 +367,17 @@
         dkv_t_ref[:, here] = final.T
 
 
-def close_keys(dkv, dmids, backs, far_bits, local_levels):
+def close_keys(dkv, backs, far_bits, local_levels, after):
     tok_rows, double = dkv.shape
     inner = double // 2
-    return pl.pallas_call(
+    return run(
         functools.partial(close_body, local_levels, far_bits),
+        [dkv, *backs],
+        after,
         out_shape=[shape(tok_rows, inner), shape(tok_rows, inner), shape(double, tok_rows)],
-        compiler_params=params(8),
-        cost_estimate=cost(4 * tok_rows * 256 * double, 20 * tok_rows * double),
-    )(dkv, *dmids, *backs)
-
-
-def out_body(left_ref, weight_ref, out_ref):
-    out_ref[...] = dot(left_ref[...], weight_ref[...], NT).astype(BF16)
-
-
-def project_out(left, weight):
-    tok_rows, inner = left.shape
-    width = weight.shape[0]
-    return pl.pallas_call(
-        out_body,
-        out_shape=shape(tok_rows, width),
-        compiler_params=params(8),
-        cost_estimate=cost(2 * tok_rows * inner * width, 2 * tok_rows * width),
-    )(left, weight)
+        compiler_params=params(5),
+        cost_estimate=cost(2 * tok_rows * 256 * double, 12 * tok_rows * double),
+    )
 
 
 def split_body(count, parts, rank_ref, *refs):
@@ -375,20 +395,22 @@
         outs[r % 2][:, place : place + width] = total.astype(BF16)
 
 
-def project_split(lefts, weights, axis):
+def project_split(lefts, weights, axis, after):
     count = len(lefts)
     parts = lax.axis_size(axis)
     tok_rows, inner = lefts[0].shape
     width = weights[0].shape[0]
     rank = jnp.reshape(lax.axis_index(axis), (1,)).astype(jnp.int32)
-    return pl.pallas_call(
+    return run(
         functools.partial(split_body, count, parts),
+        [rank, *lefts, *weights],
+        after,
         in_specs=[pl.BlockSpec(memory_space=pltpu.SMEM)]
         + [pl.BlockSpec(memory_space=pltpu.VMEM)] * (2 * count),
         out_shape=[shape(tok_rows, width // 2)] * 2,
-        compiler_params=params(8),
+        compiler_params=params(5),
         cost_estimate=cost(2 * count * tok_rows * inner * width, 2 * tok_rows * width),
-    )(rank, *lefts, *weights)
+    )
 
 
 def exchange(block, axis, distance):
@@ -417,55 +439,49 @@
         distance *= 2
 
 
-def combine_body(own_ref, into_ref, half_ref, across_ref, next_ref, total_ref):
-    next_ref[...] = (own_ref[...].astype(F32) + into_ref[...].astype(F32)).astype(BF16)
-    total_ref[...] = (half_ref[...].astype(F32) + across_ref[...].astype(F32)).astype(BF16)
-
-
-def combine(own, into, half, across):
-    return pl.pallas_call(
-        combine_body,
-        out_shape=[shape(*own.shape), shape(*half.shape)],
-        compiler_params=pltpu.CompilerParams(vmem_limit_bytes=8 * MIB),
-        cost_estimate=cost(2 * own.size, 12 * own.size),
-    )(own, into, half, across)
-
-
-def line_sums(chunks, axis):
-    count = lax.axis_size(axis)
-    if count < 4:
-        return [add(c, exchange(c, axis, 1)) if count == 2 else c for c in chunks]
-    rank = jnp.bitwise_and(lax.axis_index(axis), 3)
-    at_end = (rank == 0) | (rank == 3)
-    inward, across, outward = [], [], []
-    for base in range(0, count, 4):
-        inward += [(base, base + 1), (base + 3, base + 2)]
-        across += [(base + 1, base + 2), (base + 2, base + 1)]
-        outward += [(base + 1, base), (base + 2, base + 3)]
-    lag = 2
-    halves, crossed, totals, sums = [], [], [], []
-    for k in range(len(chunks) + lag):
-        if k < len(chunks):
-            into = lax.ppermute(chunks[k], axis, inward)
-        if k < lag:
-            halves.append(add(chunks[k], into))
-        elif k < len(chunks):
-            half, total = combine(chunks[k], into, halves[k - lag], crossed[k - lag])
-            halves.append(half)
-            totals.append(total)
-        else:
-            totals.append(add(halves[k - lag], crossed[k - lag]))
-        if k < len(chunks):
-            crossed.append(lax.ppermute(halves[k], axis, across))
-    for total in totals:
-        ends = lax.ppermute(total, axis, outward)
-        result = jnp.where(at_end, ends, total)
+class Line:
+    lag = 3
+
+    def __init__(self, axis):
+        self.axis = axis
+        self.count = lax.axis_size(axis)
+        rank = jnp.bitwise_and(lax.axis_index(axis), 3)
+        self.at_end = (rank == 0) | (rank == 3)
+        self.across = []
+        for low in range(0, self.count, 4):
+            self.across += [(low, low), (low + 1, low + 2), (low + 2, low + 1), (low + 3, low + 3)]
+        self.halves, self.totals, self.sums = [], [], []
+
+    def push(self, chunk):
+        if self.count < 4:
+            total = add(chunk, exchange(chunk, self.axis, 1)) if self.count == 2 else chunk
+            self.halves.append(total)
+            self.totals.append(total)
+            self.sums.append(total)
+            return
+        k = len(self.totals)
+        send = chunk
+        if k >= self.lag:
+            send = jnp.where(self.at_end, chunk, self.totals[k - self.lag])
+        into = exchange(send, self.axis, 1)
+        if k >= self.lag:
+            self.receive(into)
+        half = add(chunk, into)
+        self.halves.append(half)
+        self.totals.append(add(half, lax.ppermute(half, self.axis, self.across)))
+
+    def receive(self, into):
+        result = jnp.where(self.at_end, into, self.totals[len(self.sums)])
         distance = 4
-        while distance < count:
-            result = add(result, exchange(result, axis, distance))
+        while distance < self.count:
+            result = add(result, exchange(result, self.axis, distance))
             distance *= 2
-        sums.append(result)
-    return sums
+        self.sums.append(result)
+
+    def finish(self):
+        while len(self.sums) < len(self.totals):
+            self.receive(exchange(self.totals[len(self.sums)], self.axis, 1))
+        return self.sums
 
 
 def per_device(tokens, w_query, w_key, w_value, w_out, cotangent):
@@ -476,33 +492,37 @@
     far_levels = count.bit_length() - 1
     far_bits = [d.bit_length() - 1 for d in range(1, count)]
 
-    parts = key_value(tokens, w_key, w_value, local_levels, far_levels)
-    levels = parts[:local_levels]
-    tops = parts[local_levels:]
+    parts = key_value(tokens, w_key, w_value, w_query, local_levels, far_levels)
+    levels, query, tops = parts[:local_levels], parts[local_levels], parts[local_levels + 1 :]
     fars = [exchange(tops[bit], "seq", d) for d, bit in enumerate(far_bits, 1)]
-    query, grad = project_pair(tokens, cotangent, w_query, w_out)
+    grad = project(cotangent, w_out)
     attended, attended_t, stats = forward(query, levels, fars, far_bits)
-    results = backward(query, grad, attended_t, stats, levels, fars, far_bits)
-    dquery, dquery_t, dkv = results[:3]
-    dmids = results[3 : 3 + local_levels - 1]
-    dfars = results[3 + local_levels - 1 :]
+    pieces = 2
+    line = Line("seq")
+
+    def push_terms(left, which, right, after):
+        for p in range(pieces):
+            chunk = weight_terms(left, right, inner, which, p, pieces, after)
+            line.push(chunk)
+            after = [chunk]
+        return after
+
+    after = push_terms(attended_t, 0, cotangent, [])
+    dquery, dquery_t, dkv, *dfars = backward(
+        query, grad, attended_t, stats, levels, fars, far_bits, after
+    )
     backs = [exchange(piece, "seq", d) for d, piece in enumerate(dfars, 1)]
-    mixed_part = project_out(attended, w_out)
-    mixed = lax.psum_scatter(mixed_part, "head", scatter_dimension=1, tiled=True)
-    dkey, dvalue, dkv_t = close_keys(dkv, dmids, backs, far_bits, local_levels)
-    keep, send = project_split([dquery, dkey, dvalue], [w_query, w_key, w_value], "head")
-    tokens_grad = scatter_sum(keep, send, "head")
-
-    pieces = 2
-    chunks = []
-    for left, which, right in (
-        (attended_t, 0, cotangent),
-        (dquery_t, 0, tokens),
-        (dkv_t, 0, tokens),
-        (dkv_t, 1, tokens),
-    ):
-        chunks += [weight_terms(left, right, inner, which, p, pieces) for p in range(pieces)]
-    sums = line_sums(chunks, "seq")
+    after = push_terms(dquery_t, 0, tokens, [line.halves[0]])
+    parts = project_split([attended], [w_out], "head", after)
+    mixed = scatter_sum(*parts, "head")
+    dkey, dvalue, dkv_t = close_keys(
+        dkv, backs, far_bits, local_levels, [parts[0], line.halves[1]]
+    )
+    after = push_terms(dkv_t, 0, tokens, [line.totals[0]])
+    after = push_terms(dkv_t, 1, tokens, after)
+    parts = project_split([dquery, dkey, dvalue], [w_query, w_key, w_value], "head", after)
+    tokens_grad = scatter_sum(*parts, "head")
+    sums = line.finish()
     out_grad, query_grad, key_grad, value_grad = (
         jnp.concatenate(sums[i : i + pieces], axis=0) for i in range(0, len(sums), pieces)
     )

time: 163 us -> 115 us (0.71)
  between operations: 14.7 us -> 1.14 us
  Pallas kernels: 37.3 us -> 26.4 us
  waiting for transfers between devices: 27.7 us -> 16.8 us
  starting transfers between devices: 64.1 us -> 57.3 us
  local copies, waits for them, and re-layouts: 11.3 us -> 5.14 us
    ppermute x24 -> x8, starting transfers between devices: 54.9 us -> 5.6 us  [push(): self.totals.append(add(half, lax.ppermute(half, self.axis, self.across)))]
    ppermute x8 -> x21, starting transfers between devices: 9.18 us -> 51.7 us  [exchange(): return lax.ppermute(block, axis, [(i, i ^ distance) for i in range(count)])]
    ppermute x24 -> x8, waiting for transfers between devices: 24.2 us -> 0.02 us  [push(): self.totals.append(add(half, lax.ppermute(half, self.axis, self.across)))]
    ppermute x8 -> x21, waiting for transfers between devices: 3.46 us -> 16.8 us  [exchange(): return lax.ppermute(block, axis, [(i, i ^ distance) for i in range(count)])]
    pallas_call x19 -> x13, Pallas kernels: 25.4 us -> 14.8 us  [the longest x12 14.1 us: run(): return pl.pallas_call(kernel, in_specs=in_specs, **options)(*ready, *after)]
    unnamed x62 -> x28, local copies, waits for them, and re-layouts: 11.3 us -> 5.14 us
  transfers between devices with their start and end apart: 33 -> 29, of which waited for: 8 -> 7; matrix products, arithmetic and copies ran while one was open for 4% -> 6% of each run, Pallas kernels for 15% -> 13%
where the time goes in v4:
time: 115 us; the launch traced here: 114 us
  starting transfers between devices  57.3 us (50%)
  Pallas kernels  26.4 us (23%)
  waiting for transfers between devices  16.8 us (15%)
  other arithmetic  7.33 us (6%)
  local copies, waits for them, and re-layouts  5.14 us (4%)
    ppermute x21, starting transfers between devices, exchange(): return lax.ppermute(block, axis, [(i, i ^ distance) for i in range(count)])  51.7 us
    ppermute x21, waiting for transfers between devices, exchange(): return lax.ppermute(block, axis, [(i, i ^ distance) for i in range(count)])  16.8 us
    pallas_call x12, Pallas kernels, run(): return pl.pallas_call(kernel, in_specs=in_specs, **options)(*ready, *after)  14.1 us
    pallas_call x1, Pallas kernels, forward(): pl.pallas_call(functools.partial(forward_body, len(levels), far_bits), ou...  5.88 us
    pallas_call x1, Pallas kernels, key_value(): pl.pallas_call(functools.partial(key_value_body, local_levels, far_levels...  5.67 us
    ppermute x8, starting transfers between devices, push(): self.totals.append(add(half, lax.ppermute(half, self.axis, self.across)))  5.6 us
    unnamed x28, local copies, waits for them, and re-layouts  5.14 us
    concatenate x4, other arithmetic, per_device(): jnp.concatenate(sums[i:i + pieces], axis=0)  3.31 us
  transfers between devices with their start and end apart: 29, of which 7 were waited for; matrix products, arithmetic and copies ran while one was open for 6% of the time, Pallas kernels for 13%

profile of v4, /device:TPU:0, one launch (start us, length us, event | category | flops | bytes accessed | tf_op | source)
XLA Modules:
  0.0 114.0 jit_solution(6291056285487533920)
XLA Ops:
  0.6 5.7 %shard_map.109 = (bf16[1024,512]{1,0:T(8,128)(2,1)}, bf16[512,512]{1,0:T(8,128)(2,1)}, bf16[256,512]{1,0:T(8,128)(2,1)}, bf16[1024,256]{1,0:T(8,128)(2,1)}, bf16...) custom-call(bf16[1024,1024]{1,0:T(8,128)(2,1)} %refs_1_.15, bf16[1024,256]{1,0:T(8,128)(2,1)} %refs_5_.1, ...), custom_call_target="tpu_custom_call" | custom-call | flops 1610612736 | bytes 5242880 | tf_op jit(solution)/shard_map/pallas_call | solution.py:127
  6.3 3.1 %collective-permute-start = (bf16[128,512]{1,0:T(8,128)(2,1)}, bf16[128,512]{1,0:T(8,128)(2,1)S(1)}, u32[]{:S(2)}, u32[]{:S(2)}) collective-permute-start(bf16[128,512]{1,0:T(8,128)(2,1)} %get-tuple-element.32), channel_id=1, source_target_pairs={{0,4},{4,0},{8,12},{12,8},{1,5},{5,1},{9,13},{13,9},{2,6},{6,2},{1... | collective-permute-start | bytes 393224 | tf_op jit(solution)/shard_map/ppermute | solution.py:418
  9.4 2.6 %collective-permute-start.1 = (bf16[64,512]{1,0:T(8,128)(2,1)}, bf16[64,512]{1,0:T(8,128)(2,1)S(1)}, u32[]{:S(2)}, u32[]{:S(2)}) collective-permute-start(bf16[64,512]{1,0:T(8,128)(2,1)} %get-tuple-element.33), channel_id=1, source_target_pairs={{0,8},{4,12},{8,0},{12,4},{1,9},{5,13},{9,1},{13,5},{2,10},{6,14},... | collective-permute-start | bytes 196616 | tf_op jit(solution)/shard_map/ppermute | solution.py:418
  12.0 4.1 %collective-permute-done.1.refs_5_.refs_8_ = bf16[64,512]{1,0:T(8,128)(2,1)S(1)} collective-permute-done((bf16[64,512]{1,0:T(8,128)(2,1)}, bf16[64,512]{1,0:T(8,128)(2,1)S(1)}, u32[]{:S(2)}, u32[]{:S(2)}) %collective-permute-start.1) | collective-permute-done | bytes 65568 | tf_op jit(solution)/shard_map/ppermute | solution.py:418
  16.1 2.2 %collective-permute-done.2.refs_6_.refs_9_ = bf16[64,512]{1,0:T(8,128)(2,1)S(1)} collective-permute-done((bf16[64,512]{1,0:T(8,128)(2,1)}, bf16[64,512]{1,0:T(8,128)(2,1)S(1)}, u32[]{:S(2)}, u32[]{:S(2)}) %collective-permute-start.2) | collective-permute-done | bytes 65568 | tf_op jit(solution)/shard_map/ppermute | solution.py:418
  18.3 1.2 %copy-done.6 = bf16[1024,512]{1,0:T(8,128)(2,1)S(1)} copy-done((bf16[1024,512]{1,0:T(8,128)(2,1)S(1)}, bf16[1024,512]{1,0:T(8,128)(2,1)}, u32[]{:S(2)}) %copy-start.6) | copy-done | bytes 1048600
  19.6 1.0 copy-done.8
  20.6 1.0 copy-done.10
  21.6 0.9 copy-done.12
  22.6 5.9 %shard_map.110 = (bf16[1024,256]{1,0:T(8,128)(2,1)S(1)}, bf16[256,1024]{1,0:T(8,128)(2,1)S(1)}, f32[4,1024]{1,0:T(4,128)S(1)}) custom-call(bf16[1024,256]{1,0:T(8,128)(2,1)S(1)} %copy-done.10, bf16[1024,512]{1,0:T(8,128)(2,1)S(1)} %copy-done.6, bf16[512,512]{1,0:T(8,128)(2,1)S(1)} %copy-done.8, bf16[256,512]{1,0:T(8,128)(2,1)S(1)} %copy-done.12, ...), custom_call_target="tpu_custom_call" | custom-call | flops 805306368 | bytes 3145728 | tf_op jit(solution)/shard_map/pallas_call | solution.py:238
  29.0 1.2 %collective-permute-start.3 = (bf16[512,256]{1,0:T(8,128)(2,1)S(1)}, bf16[512,256]{1,0:T(8,128)(2,1)S(1)}, u32[]{:S(2)}, u32[]{:S(2)}) collective-permute-start(bf16[512,256]{1,0:T(8,128)(2,1)S(1)} %shard_map.112.refs_2_), channel_id=1, source_target_pairs={{0,4},{4,0},{8,12},{12,8},{1,5},{5,1},{9,13},{13,9},{2,6},{6,2},{1... | collective-permute-start | bytes 786440 | tf_op jit(solution)/shard_map/ppermute | solution.py:418
  30.2 0.7 shard_map.111.refs_1_
  31.5 1.0 collective-permute-start.9
  32.5 6.4 %shard_map.114 = (bf16[1024,256]{1,0:T(8,128)(2,1)S(1)}, bf16[256,1024]{1,0:T(8,128)(2,1)S(1)}, f32[1024,512]{1,0:T(8,128)S(1)}, bf16[128,512]{1,0:T(8,128)(2,1)...) custom-call(bf16[1024,256]{1,0:T(8,128)(2,1)S(1)} %copy-done.11, ...), custom_call_target="tpu_custom_call" | custom-call | flops 2013265920 | bytes 6291456 | tf_op jit(solution)/shard_map/pallas_call | solution.py:42
  38.9 1.2 %collective-permute-start.6 = (bf16[128,512]{1,0:T(8,128)(2,1)S(1)}, bf16[128,512]{1,0:T(8,128)(2,1)S(1)}, u32[]{:S(2)}, u32[]{:S(2)}) collective-permute-start(bf16[128,512]{1,0:T(8,128)(2,1)S(1)} %get-tuple-element.42), channel_id=1, source_target_pairs={{0,4},{4,0},{8,12},{12,8},{1,5},{5,1},{9,13},{13,9},{2,6},{6,2},{1... | collective-permute-start | bytes 393224 | tf_op jit(solution)/shard_map/ppermute | solution.py:418
  40.1 1.3 %collective-permute-start.7 = (bf16[64,512]{1,0:T(8,128)(2,1)S(1)}, bf16[64,512]{1,0:T(8,128)(2,1)S(1)}, u32[]{:S(2)}, u32[]{:S(2)}) collective-permute-start(bf16[64,512]{1,0:T(8,128)(2,1)S(1)} %get-tuple-element.43), channel_id=1, source_target_pairs={{0,8},{4,12},{8,0},{12,4},{1,9},{5,13},{9,1},{13,5},{2,10},{6,14},... | collective-permute-start | bytes 196616 | tf_op jit(solution)/shard_map/ppermute | solution.py:418
  41.4 1.9 %collective-permute-start.8 = (bf16[64,512]{1,0:T(8,128)(2,1)S(1)}, bf16[64,512]{1,0:T(8,128)(2,1)S(1)}, u32[]{:S(2)}, u32[]{:S(2)}) collective-permute-start(bf16[64,512]{1,0:T(8,128)(2,1)S(1)} %get-tuple-element.44), channel_id=1, source_target_pairs={{0,12},{4,8},{8,4},{12,0},{1,13},{5,9},{9,5},{13,1},{2,14},{6,10},... | collective-permute-start | bytes 196616 | tf_op jit(solution)/shard_map/ppermute | solution.py:418
  43.4 0.7 collective-permute-start.10
  44.6 0.7 collective-permute-done.9
  45.3 1.8 %collective-permute-start.13 = (bf16[512,256]{1,0:T(8,128)(2,1)S(1)}, bf16[512,256]{1,0:T(8,128)(2,1)S(1)}, u32[]{:S(2)}, u32[]{:S(2)}) collective-permute-start(bf16[512,256]{1,0:T(8,128)(2,1)S(1)} %shard_map.115.refs_2_), channel_id=1, source_target_pairs={{0,4},{4,0},{8,12},{12,8},{1,5},{5,1},{9,13},{13,9},{2,6},{6,2},{1... | collective-permute-start | bytes 786440 | tf_op jit(solution)/shard_map/ppermute | solution.py:418
  47.7 0.7 shard_map.117
  48.6 0.9 collective-permute-start.19
  49.4 1.0 shard_map.118
  53.6 1.8 %shard_map.123 = (bf16[1024,512]{1,0:T(8,128)(2,1)S(1)}, bf16[1024,512]{1,0:T(8,128)(2,1)S(1)}) custom-call(s32[1]{0:T(128)} %bitcast.refs_0_, bf16[1024,256]{1,0:T(8,128)(2,1)S(1)} %get-tuple-element.40.refs_1_, bf16[1024,256]{1,0:T(8,128)(2,1)S(1)} %get-tuple-element.45.refs_2_, bf16[1024,256]{1,0:T(8,128)(2,1)S(1)} %get-tuple-element.46.refs_3_, ...), custom_call_target="tpu_custom_call" | custom-call | flops 1610612736 | bytes 2097152 | tf_op jit(solution)/shard_map/pallas_call | solution.py:42
  55.9 3.3 %collective-permute-start.16 = (bf16[512,256]{1,0:T(8,128)(2,1)S(1)}, bf16[512,256]{1,0:T(8,128)(2,1)S(1)}, u32[]{:S(2)}, u32[]{:S(2)}) collective-permute-start(bf16[512,256]{1,0:T(8,128)(2,1)S(1)} %get-tuple-element.50), channel_id=1, source_target_pairs={{0,4},{4,0},{8,12},{12,8},{1,5},{5,1},{9,13},{13,9},{2,6},{6,2},{1... | collective-permute-start | bytes 786440 | tf_op jit(solution)/shard_map/ppermute | solution.py:418
  59.3 0.7 collective-permute-start.14
  60.1 3.0 %collective-permute-start.20 = (bf16[512,256]{1,0:T(8,128)(2,1)S(1)}, bf16[512,256]{1,0:T(8,128)(2,1)S(1)}, u32[]{:S(2)}, u32[]{:S(2)}) collective-permute-start(bf16[512,256]{1,0:T(8,128)(2,1)S(1)} %broadcast_select_fusion.7), channel_id=1, source_target_pairs={{0,4},{4,0},{8,12},{12,8},{1,5},{5,1},{9,13},{13,9},{2,6},{6,2},{1... | collective-permute-start | bytes 786440 | tf_op jit(solution)/shard_map/ppermute | solution.py:418
  63.1 3.3 %collective-permute-done.16 = bf16[512,256]{1,0:T(8,128)(2,1)S(1)} collective-permute-done((bf16[512,256]{1,0:T(8,128)(2,1)S(1)}, bf16[512,256]{1,0:T(8,128)(2,1)S(1)}, u32[]{:S(2)}, u32[]{:S(2)}) %collective-permute-start.16) | collective-permute-done | bytes 262176 | tf_op jit(solution)/shard_map/ppermute | solution.py:418
  66.5 0.7 collective-permute-start.17
  67.3 4.9 %collective-permute-start.15 = (bf16[512,256]{1,0:T(8,128)(2,1)S(1)}, bf16[512,256]{1,0:T(8,128)(2,1)S(1)}, u32[]{:S(2)}, u32[]{:S(2)}) collective-permute-start(bf16[512,256]{1,0:T(8,128)(2,1)S(1)} %broadcast_select_fusion.12), channel_id=1, source_target_pairs={{0,4},{4,0},{8,12},{12,8},{1,5},{5,1},{9,13},{13,9},{2,6},{6,2},{1... | collective-permute-start | bytes 786440 | tf_op jit(solution)/shard_map/ppermute | solution.py:418
  72.3 0.7 collective-permute-start.21
  73.1 0.8 pad_maximum_fusion.3
  74.0 4.7 %collective-permute-start.18 = (bf16[512,256]{1,0:T(8,128)(2,1)S(1)}, bf16[512,256]{1,0:T(8,128)(2,1)S(1)}, u32[]{:S(2)}, u32[]{:S(2)}) collective-permute-start(bf16[512,256]{1,0:T(8,128)(2,1)S(1)} %broadcast_select_fusion.9), channel_id=1, source_target_pairs={{0,4},{4,0},{8,12},{12,8},{1,5},{5,1},{9,13},{13,9},{2,6},{6,2},{1... | collective-permute-start | bytes 786440 | tf_op jit(solution)/shard_map/ppermute | solution.py:418
  78.9 0.7 collective-permute-start.23
  79.7 4.5 %collective-permute-start.22 = (bf16[512,256]{1,0:T(8,128)(2,1)S(1)}, bf16[512,256]{1,0:T(8,128)(2,1)S(1)}, u32[]{:S(2)}, u32[]{:S(2)}) collective-permute-start(bf16[512,256]{1,0:T(8,128)(2,1)S(1)} %broadcast_select_fusion.6), channel_id=1, source_target_pairs={{0,4},{4,0},{8,12},{12,8},{1,5},{5,1},{9,13},{13,9},{2,6},{6,2},{1... | collective-permute-start | bytes 786440 | tf_op jit(solution)/shard_map/ppermute | solution.py:418
  84.4 1.6 %collective-permute-start.5 = (bf16[1024,256]{1,0:T(8,128)(2,1)S(1)}, bf16[1024,256]{1,0:T(8,128)(2,1)S(1)}, u32[]{:S(2)}, u32[]{:S(2)}) collective-permute-start(bf16[1024,256]{1,0:T(8,128)(2,1)S(1)} %add_convert_fusion.4), channel_id=1, source_target_pairs={{0,2},{1,3},{2,0},{3,1},{4,6},{5,7},{6,4},{7,5},{8,10},{9,11},{10,... | collective-permute-start | bytes 1572872 | tf_op jit(solution)/shard_map/ppermute | solution.py:418
  86.0 3.1 %collective-permute-start.24 = (bf16[512,256]{1,0:T(8,128)(2,1)S(1)}, bf16[512,256]{1,0:T(8,128)(2,1)S(1)}, u32[]{:S(2)}, u32[]{:S(2)}) collective-permute-start(bf16[512,256]{1,0:T(8,128)(2,1)S(1)} %add_convert_fusion.10), channel_id=1, source_target_pairs={{0,4},{4,0},{8,12},{12,8},{1,5},{5,1},{9,13},{13,9},{2,6},{6,2},{1... | collective-permute-start | bytes 786440 | tf_op jit(solution)/shard_map/ppermute | solution.py:418
  89.1 1.8 %collective-permute-done.22 = bf16[512,256]{1,0:T(8,128)(2,1)S(1)} collective-permute-done((bf16[512,256]{1,0:T(8,128)(2,1)S(1)}, bf16[512,256]{1,0:T(8,128)(2,1)S(1)}, u32[]{:S(2)}, u32[]{:S(2)}) %collective-permute-start.22) | collective-permute-done | bytes 262176 | tf_op jit(solution)/shard_map/ppermute | solution.py:418
  92.6 0.8 pad_maximum_fusion
  93.7 1.6 %collective-permute-start.12 = (bf16[1024,256]{1,0:T(8,128)(2,1)S(1)}, bf16[1024,256]{1,0:T(8,128)(2,1)S(1)}, u32[]{:S(2)}, u32[]{:S(2)}) collective-permute-start(bf16[1024,256]{1,0:T(8,128)(2,1)S(1)} %add_convert_fusion.1), channel_id=1, source_target_pairs={{0,2},{1,3},{2,0},{3,1},{4,6},{5,7},{6,4},{7,5},{8,10},{9,11},{10,... | collective-permute-start | bytes 1572872 | tf_op jit(solution)/shard_map/ppermute | solution.py:418
  95.3 7.6 %collective-permute-start.28 = (bf16[512,256]{1,0:T(8,128)(2,1)S(1)}, bf16[512,256]{1,0:T(8,128)(2,1)S(1)}, u32[]{:S(2)}, u32[]{:S(2)}) collective-permute-start(bf16[512,256]{1,0:T(8,128)(2,1)S(1)} %add_convert_fusion.6), channel_id=1, source_target_pairs={{0,4},{4,0},{8,12},{12,8},{1,5},{5,1},{9,13},{13,9},{2,6},{6,2},{1... | collective-permute-start | bytes 786440 | tf_op jit(solution)/shard_map/ppermute | solution.py:418
  103.0 2.7 %collective-permute-start.26 = (bf16[512,256]{1,0:T(8,128)(2,1)S(1)}, bf16[512,256]{1,0:T(8,128)(2,1)S(1)}, u32[]{:S(2)}, u32[]{:S(2)}) collective-permute-start(bf16[512,256]{1,0:T(8,128)(2,1)S(1)} %add_convert_fusion.8), channel_id=1, source_target_pairs={{0,4},{4,0},{8,12},{12,8},{1,5},{5,1},{9,13},{13,9},{2,6},{6,2},{1... | collective-permute-start | bytes 786440 | tf_op jit(solution)/shard_map/ppermute | solution.py:418
  105.8 0.8 pad_maximum_fusion.1
  106.6 1.8 %collective-permute-done.28 = bf16[512,256]{1,0:T(8,128)(2,1)S(1)} collective-permute-done((bf16[512,256]{1,0:T(8,128)(2,1)S(1)}, bf16[512,256]{1,0:T(8,128)(2,1)S(1)}, u32[]{:S(2)}, u32[]{:S(2)}) %collective-permute-start.28) | collective-permute-done | bytes 262176 | tf_op jit(solution)/shard_map/ppermute | solution.py:418
  108.4 2.8 %collective-permute-done.26 = bf16[512,256]{1,0:T(8,128)(2,1)S(1)} collective-permute-done((bf16[512,256]{1,0:T(8,128)(2,1)S(1)}, bf16[512,256]{1,0:T(8,128)(2,1)S(1)}, u32[]{:S(2)}, u32[]{:S(2)}) %collective-permute-start.26) | collective-permute-done | bytes 262176 | tf_op jit(solution)/shard_map/ppermute | solution.py:418
  111.2 0.8 pad_maximum_fusion.2
  112.1 1.0 add_convert_fusion.3
  113.1 1.0 add_convert_fusion
  (85 shorter events, 9.1 us)
Async XLA Ops:
  6.3 22.2 %copy-start.1 = (bf16[1024,1024]{1,0:T(8,128)(2,1)S(1)}, bf16[1024,1024]{1,0:T(8,128)(2,1)}, u32[]{:S(2)}) copy-start(bf16[1024,1024]{1,0:T(8,128)(2,1)} %refs_1_.9) | copy-start | bytes 6291460
  6.3 12.0 %collective-permute-start = (bf16[128,512]{1,0:T(8,128)(2,1)}, bf16[128,512]{1,0:T(8,128)(2,1)S(1)}, u32[]{:S(2)}, u32[]{:S(2)}) collective-permute-start(bf16[128,512]{1,0:T(8,128)(2,1)} %get-tuple-element.32), channel_id=1, source_target_pairs={{0,4},{4,0},{8,12},{12,8},{1,5},{5,1},{9,13},{13,9},{2,6},{6,2},{1... | collective-permute-start | bytes 393224 | tf_op jit(solution)/shard_map/ppermute | solution.py:418
  9.4 6.7 %collective-permute-start.1 = (bf16[64,512]{1,0:T(8,128)(2,1)}, bf16[64,512]{1,0:T(8,128)(2,1)S(1)}, u32[]{:S(2)}, u32[]{:S(2)}) collective-permute-start(bf16[64,512]{1,0:T(8,128)(2,1)} %get-tuple-element.33), channel_id=1, source_target_pairs={{0,8},{4,12},{8,0},{12,4},{1,9},{5,13},{9,1},{13,5},{2,10},{6,14},... | collective-permute-start | bytes 196616 | tf_op jit(solution)/shard_map/ppermute | solution.py:418
  12.0 6.3 %collective-permute-start.2 = (bf16[64,512]{1,0:T(8,128)(2,1)}, bf16[64,512]{1,0:T(8,128)(2,1)S(1)}, u32[]{:S(2)}, u32[]{:S(2)}) collective-permute-start(bf16[64,512]{1,0:T(8,128)(2,1)} %get-tuple-element.33), channel_id=1, source_target_pairs={{0,12},{4,8},{8,4},{12,0},{1,13},{5,9},{9,5},{13,1},{2,14},{6,10},... | collective-permute-start | bytes 196616 | tf_op jit(solution)/shard_map/ppermute | solution.py:418
  18.3 1.2 %copy-start.6 = (bf16[1024,512]{1,0:T(8,128)(2,1)S(1)}, bf16[1024,512]{1,0:T(8,128)(2,1)}, u32[]{:S(2)}) copy-start(bf16[1024,512]{1,0:T(8,128)(2,1)} %get-tuple-element.29.refs_1_.refs_4_) | copy-start | bytes 3145732
  19.6 1.0 copy-start.8
  20.6 1.0 copy-start.10
  21.6 0.9 copy-start.12
  28.5 1.7 %copy-start.2 = (bf16[1024,256]{1,0:T(8,128)(2,1)S(1)}, bf16[1024,256]{1,0:T(8,128)(2,1)}, u32[]{:S(2)}) copy-start(bf16[1024,256]{1,0:T(8,128)(2,1)} %refs_2_.1) | copy-start | bytes 1572868
  29.0 14.3 %collective-permute-start.3 = (bf16[512,256]{1,0:T(8,128)(2,1)S(1)}, bf16[512,256]{1,0:T(8,128)(2,1)S(1)}, u32[]{:S(2)}, u32[]{:S(2)}) collective-permute-start(bf16[512,256]{1,0:T(8,128)(2,1)S(1)} %shard_map.112.refs_2_), channel_id=1, source_target_pairs={{0,4},{4,0},{8,12},{12,8},{1,5},{5,1},{9,13},{13,9},{2,6},{6,2},{1... | collective-permute-start | bytes 786440 | tf_op jit(solution)/shard_map/ppermute | solution.py:418
  30.9 1.5 %copy-start.7 = (bf16[1024,512]{1,0:T(8,128)(2,1)S(1)}, bf16[1024,512]{1,0:T(8,128)(2,1)}, u32[]{:S(2)}) copy-start(bf16[1024,512]{1,0:T(8,128)(2,1)} %get-tuple-element.29.refs_1_.refs_4_) | copy-start | bytes 3145732
  30.9 1.5 %copy-start.9 = (bf16[512,512]{1,0:T(8,128)(2,1)S(1)}, bf16[512,512]{1,0:T(8,128)(2,1)}, u32[]{:S(2)}) copy-start(bf16[512,512]{1,0:T(8,128)(2,1)} %get-tuple-element.30.refs_2_.refs_5_) | copy-start | bytes 1572868
  30.9 1.5 %copy-start.11 = (bf16[1024,256]{1,0:T(8,128)(2,1)S(1)}, bf16[1024,256]{1,0:T(8,128)(2,1)}, u32[]{:S(2)}) copy-start(bf16[1024,256]{1,0:T(8,128)(2,1)} %get-tuple-element.28.refs_0_) | copy-start | bytes 1572868
  31.0 1.5 %copy-start.13 = (bf16[256,512]{1,0:T(8,128)(2,1)S(1)}, bf16[256,512]{1,0:T(8,128)(2,1)}, u32[]{:S(2)}) copy-start(bf16[256,512]{1,0:T(8,128)(2,1)} %get-tuple-element.31.refs_3_.refs_6_) | copy-start | bytes 786436
  31.5 13.9 %collective-permute-start.9 = (bf16[512,256]{1,0:T(8,128)(2,1)S(1)}, bf16[512,256]{1,0:T(8,128)(2,1)S(1)}, u32[]{:S(2)}, u32[]{:S(2)}) collective-permute-start(bf16[512,256]{1,0:T(8,128)(2,1)S(1)} %shard_map.113.refs_10_), channel_id=1, source_target_pairs={{0,4},{4,0},{8,12},{12,8},{1,5},{5,1},{9,13},{13,9},{2,6},{6,2},{1... | collective-permute-start | bytes 786440 | tf_op jit(solution)/shard_map/ppermute | solution.py:418
  32.5 11.6 %copy-start = (bf16[1024,1024]{1,0:T(8,128)(2,1)S(1)}, bf16[1024,1024]{1,0:T(8,128)(2,1)}, u32[]{:S(2)}) copy-start(bf16[1024,1024]{1,0:T(8,128)(2,1)} %refs_1_.15) | copy-start | bytes 6291460
  38.9 10.5 %collective-permute-start.6 = (bf16[128,512]{1,0:T(8,128)(2,1)S(1)}, bf16[128,512]{1,0:T(8,128)(2,1)S(1)}, u32[]{:S(2)}, u32[]{:S(2)}) collective-permute-start(bf16[128,512]{1,0:T(8,128)(2,1)S(1)} %get-tuple-element.42), channel_id=1, source_target_pairs={{0,4},{4,0},{8,12},{12,8},{1,5},{5,1},{9,13},{13,9},{2,6},{6,2},{1... | collective-permute-start | bytes 393224 | tf_op jit(solution)/shard_map/ppermute | solution.py:418
  40.1 8.4 %collective-permute-start.7 = (bf16[64,512]{1,0:T(8,128)(2,1)S(1)}, bf16[64,512]{1,0:T(8,128)(2,1)S(1)}, u32[]{:S(2)}, u32[]{:S(2)}) collective-permute-start(bf16[64,512]{1,0:T(8,128)(2,1)S(1)} %get-tuple-element.43), channel_id=1, source_target_pairs={{0,8},{4,12},{8,0},{12,4},{1,9},{5,13},{9,1},{13,5},{2,10},{6,14},... | collective-permute-start | bytes 196616 | tf_op jit(solution)/shard_map/ppermute | solution.py:418
  41.4 7.1 %collective-permute-start.8 = (bf16[64,512]{1,0:T(8,128)(2,1)S(1)}, bf16[64,512]{1,0:T(8,128)(2,1)S(1)}, u32[]{:S(2)}, u32[]{:S(2)}) collective-permute-start(bf16[64,512]{1,0:T(8,128)(2,1)S(1)} %get-tuple-element.44), channel_id=1, source_target_pairs={{0,12},{4,8},{8,4},{12,0},{1,13},{5,9},{9,5},{13,1},{2,14},{6,10},... | collective-permute-start | bytes 196616 | tf_op jit(solution)/shard_map/ppermute | solution.py:418
  43.4 7.1 %collective-permute-start.10 = (bf16[512,256]{1,0:T(8,128)(2,1)S(1)}, bf16[512,256]{1,0:T(8,128)(2,1)S(1)}, u32[]{:S(2)}, u32[]{:S(2)}) collective-permute-start(bf16[512,256]{1,0:T(8,128)(2,1)S(1)} %add_convert_fusion.21.refs_2_), channel_id=1, source_target_pairs={{0,0},{4,8},{8,4},{12,12},{1,1},{5,9},{9,5},{13,13},{2,2},{6,10},{... | collective-permute-start | bytes 786440 | tf_op jit(solution)/shard_map/ppermute | solution.py:471
  45.3 13.9 %collective-permute-start.13 = (bf16[512,256]{1,0:T(8,128)(2,1)S(1)}, bf16[512,256]{1,0:T(8,128)(2,1)S(1)}, u32[]{:S(2)}, u32[]{:S(2)}) collective-permute-start(bf16[512,256]{1,0:T(8,128)(2,1)S(1)} %shard_map.115.refs_2_), channel_id=1, source_target_pairs={{0,4},{4,0},{8,12},{12,8},{1,5},{5,1},{9,13},{13,9},{2,6},{6,2},{1... | collective-permute-start | bytes 786440 | tf_op jit(solution)/shard_map/ppermute | solution.py:418
  48.5 35.8 %collective-permute-start.4 = (bf16[1024,512]{1,0:T(8,128)(2,1)S(1)}, bf16[1024,512]{1,0:T(8,128)(2,1)S(1)}, u32[]{:S(2)}, u32[]{:S(2)}) collective-permute-start(bf16[1024,512]{1,0:T(8,128)(2,1)S(1)} %get-tuple-element.39), channel_id=1, source_target_pairs={{0,1},{1,0},{2,3},{3,2},{4,5},{5,4},{6,7},{7,6},{8,9},{9,8},{10,11... | collective-permute-start | bytes 3145736 | tf_op jit(solution)/shard_map/ppermute | solution.py:418
  48.6 11.5 %collective-permute-start.19 = (bf16[512,256]{1,0:T(8,128)(2,1)S(1)}, bf16[512,256]{1,0:T(8,128)(2,1)S(1)}, u32[]{:S(2)}, u32[]{:S(2)}) collective-permute-start(bf16[512,256]{1,0:T(8,128)(2,1)S(1)} %add_convert_fusion.20.refs_5_), channel_id=1, source_target_pairs={{0,0},{4,8},{8,4},{12,12},{1,1},{5,9},{9,5},{13,13},{2,2},{6,10},{... | collective-permute-start | bytes 786440 | tf_op jit(solution)/shard_map/ppermute | solution.py:471
  52.2 1.0 copy-start.3
  52.2 1.2 %copy-start.4 = (bf16[1024,256]{1,0:T(8,128)(2,1)S(1)}, bf16[1024,256]{1,0:T(8,128)(2,1)}, u32[]{:S(2)}) copy-start(bf16[1024,256]{1,0:T(8,128)(2,1)} %refs_6_.1) | copy-start | bytes 1572868
  52.2 1.3 %copy-start.5 = (bf16[1024,256]{1,0:T(8,128)(2,1)S(1)}, bf16[1024,256]{1,0:T(8,128)(2,1)}, u32[]{:S(2)}) copy-start(bf16[1024,256]{1,0:T(8,128)(2,1)} %refs_4_.1) | copy-start | bytes 1572868
  55.4 38.1 %collective-permute-start.11 = (bf16[1024,512]{1,0:T(8,128)(2,1)S(1)}, bf16[1024,512]{1,0:T(8,128)(2,1)S(1)}, u32[]{:S(2)}, u32[]{:S(2)}) collective-permute-start(bf16[1024,512]{1,0:T(8,128)(2,1)S(1)} %get-tuple-element.49), channel_id=1, source_target_pairs={{0,1},{1,0},{2,3},{3,2},{4,5},{5,4},{6,7},{7,6},{8,9},{9,8},{10,11... | collective-permute-start | bytes 3145736 | tf_op jit(solution)/shard_map/ppermute | solution.py:418
  55.9 10.5 %collective-permute-start.16 = (bf16[512,256]{1,0:T(8,128)(2,1)S(1)}, bf16[512,256]{1,0:T(8,128)(2,1)S(1)}, u32[]{:S(2)}, u32[]{:S(2)}) collective-permute-start(bf16[512,256]{1,0:T(8,128)(2,1)S(1)} %get-tuple-element.50), channel_id=1, source_target_pairs={{0,4},{4,0},{8,12},{12,8},{1,5},{5,1},{9,13},{13,9},{2,6},{6,2},{1... | collective-permute-start | bytes 786440 | tf_op jit(solution)/shard_map/ppermute | solution.py:418
  59.3 7.8 %collective-permute-start.14 = (bf16[512,256]{1,0:T(8,128)(2,1)S(1)}, bf16[512,256]{1,0:T(8,128)(2,1)S(1)}, u32[]{:S(2)}, u32[]{:S(2)}) collective-permute-start(bf16[512,256]{1,0:T(8,128)(2,1)S(1)} %add_convert_fusion.18), channel_id=1, source_target_pairs={{0,0},{4,8},{8,4},{12,12},{1,1},{5,9},{9,5},{13,13},{2,2},{6,10},{... | collective-permute-start | bytes 786440 | tf_op jit(solution)/shard_map/ppermute | solution.py:471
  60.1 12.0 %collective-permute-start.20 = (bf16[512,256]{1,0:T(8,128)(2,1)S(1)}, bf16[512,256]{1,0:T(8,128)(2,1)S(1)}, u32[]{:S(2)}, u32[]{:S(2)}) collective-permute-start(bf16[512,256]{1,0:T(8,128)(2,1)S(1)} %broadcast_select_fusion.7), channel_id=1, source_target_pairs={{0,4},{4,0},{8,12},{12,8},{1,5},{5,1},{9,13},{13,9},{2,6},{6,2},{1... | collective-permute-start | bytes 786440 | tf_op jit(solution)/shard_map/ppermute | solution.py:418
  66.5 7.4 %collective-permute-start.17 = (bf16[512,256]{1,0:T(8,128)(2,1)S(1)}, bf16[512,256]{1,0:T(8,128)(2,1)S(1)}, u32[]{:S(2)}, u32[]{:S(2)}) collective-permute-start(bf16[512,256]{1,0:T(8,128)(2,1)S(1)} %add_convert_fusion.16), channel_id=1, source_target_pairs={{0,0},{4,8},{8,4},{12,12},{1,1},{5,9},{9,5},{13,13},{2,2},{6,10},{... | collective-permute-start | bytes 786440 | tf_op jit(solution)/shard_map/ppermute | solution.py:471
  67.3 11.5 %collective-permute-start.15 = (bf16[512,256]{1,0:T(8,128)(2,1)S(1)}, bf16[512,256]{1,0:T(8,128)(2,1)S(1)}, u32[]{:S(2)}, u32[]{:S(2)}) collective-permute-start(bf16[512,256]{1,0:T(8,128)(2,1)S(1)} %broadcast_select_fusion.12), channel_id=1, source_target_pairs={{0,4},{4,0},{8,12},{12,8},{1,5},{5,1},{9,13},{13,9},{2,6},{6,2},{1... | collective-permute-start | bytes 786440 | tf_op jit(solution)/shard_map/ppermute | solution.py:418
  72.3 7.3 %collective-permute-start.21 = (bf16[512,256]{1,0:T(8,128)(2,1)S(1)}, bf16[512,256]{1,0:T(8,128)(2,1)S(1)}, u32[]{:S(2)}, u32[]{:S(2)}) collective-permute-start(bf16[512,256]{1,0:T(8,128)(2,1)S(1)} %add_convert_fusion.13), channel_id=1, source_target_pairs={{0,0},{4,8},{8,4},{12,12},{1,1},{5,9},{9,5},{13,13},{2,2},{6,10},{... | collective-permute-start | bytes 786440 | tf_op jit(solution)/shard_map/ppermute | solution.py:471
  74.0 17.7 %collective-permute-start.18 = (bf16[512,256]{1,0:T(8,128)(2,1)S(1)}, bf16[512,256]{1,0:T(8,128)(2,1)S(1)}, u32[]{:S(2)}, u32[]{:S(2)}) collective-permute-start(bf16[512,256]{1,0:T(8,128)(2,1)S(1)} %broadcast_select_fusion.9), channel_id=1, source_target_pairs={{0,4},{4,0},{8,12},{12,8},{1,5},{5,1},{9,13},{13,9},{2,6},{6,2},{1... | collective-permute-start | bytes 786440 | tf_op jit(solution)/shard_map/ppermute | solution.py:418
  78.9 7.1 %collective-permute-start.23 = (bf16[512,256]{1,0:T(8,128)(2,1)S(1)}, bf16[512,256]{1,0:T(8,128)(2,1)S(1)}, u32[]{:S(2)}, u32[]{:S(2)}) collective-permute-start(bf16[512,256]{1,0:T(8,128)(2,1)S(1)} %add_convert_fusion.11), channel_id=1, source_target_pairs={{0,0},{4,8},{8,4},{12,12},{1,1},{5,9},{9,5},{13,13},{2,2},{6,10},{... | collective-permute-start | bytes 786440 | tf_op jit(solution)/shard_map/ppermute | solution.py:471
  79.7 11.3 %collective-permute-start.22 = (bf16[512,256]{1,0:T(8,128)(2,1)S(1)}, bf16[512,256]{1,0:T(8,128)(2,1)S(1)}, u32[]{:S(2)}, u32[]{:S(2)}) collective-permute-start(bf16[512,256]{1,0:T(8,128)(2,1)S(1)} %broadcast_select_fusion.6), channel_id=1, source_target_pairs={{0,4},{4,0},{8,12},{12,8},{1,5},{5,1},{9,13},{13,9},{2,6},{6,2},{1... | collective-permute-start | bytes 786440 | tf_op jit(solution)/shard_map/ppermute | solution.py:418
  84.4 27.7 %collective-permute-start.5 = (bf16[1024,256]{1,0:T(8,128)(2,1)S(1)}, bf16[1024,256]{1,0:T(8,128)(2,1)S(1)}, u32[]{:S(2)}, u32[]{:S(2)}) collective-permute-start(bf16[1024,256]{1,0:T(8,128)(2,1)S(1)} %add_convert_fusion.4), channel_id=1, source_target_pairs={{0,2},{1,3},{2,0},{3,1},{4,6},{5,7},{6,4},{7,5},{8,10},{9,11},{10,... | collective-permute-start | bytes 1572872 | tf_op jit(solution)/shard_map/ppermute | solution.py:418
  86.0 19.7 %collective-permute-start.24 = (bf16[512,256]{1,0:T(8,128)(2,1)S(1)}, bf16[512,256]{1,0:T(8,128)(2,1)S(1)}, u32[]{:S(2)}, u32[]{:S(2)}) collective-permute-start(bf16[512,256]{1,0:T(8,128)(2,1)S(1)} %add_convert_fusion.10), channel_id=1, source_target_pairs={{0,4},{4,0},{8,12},{12,8},{1,5},{5,1},{9,13},{13,9},{2,6},{6,2},{1... | collective-permute-start | bytes 786440 | tf_op jit(solution)/shard_map/ppermute | solution.py:418
  91.0 4.2 %collective-permute-start.27 = (bf16[512,256]{1,0:T(8,128)(2,1)S(1)}, bf16[512,256]{1,0:T(8,128)(2,1)S(1)}, u32[]{:S(2)}, u32[]{:S(2)}) collective-permute-start(bf16[512,256]{1,0:T(8,128)(2,1)S(1)} %add_convert_fusion.7), channel_id=1, source_target_pairs={{0,0},{4,8},{8,4},{12,12},{1,1},{5,9},{9,5},{13,13},{2,2},{6,10},{... | collective-permute-start | bytes 786440 | tf_op jit(solution)/shard_map/ppermute | solution.py:471
  91.8 11.1 %collective-permute-start.25 = (bf16[512,256]{1,0:T(8,128)(2,1)S(1)}, bf16[512,256]{1,0:T(8,128)(2,1)S(1)}, u32[]{:S(2)}, u32[]{:S(2)}) collective-permute-start(bf16[512,256]{1,0:T(8,128)(2,1)S(1)} %add_convert_fusion.9), channel_id=1, source_target_pairs={{0,0},{4,8},{8,4},{12,12},{1,1},{5,9},{9,5},{13,13},{2,2},{6,10},{... | collective-permute-start | bytes 786440 | tf_op jit(solution)/shard_map/ppermute | solution.py:471
  93.7 19.4 %collective-permute-start.12 = (bf16[1024,256]{1,0:T(8,128)(2,1)S(1)}, bf16[1024,256]{1,0:T(8,128)(2,1)S(1)}, u32[]{:S(2)}, u32[]{:S(2)}) collective-permute-start(bf16[1024,256]{1,0:T(8,128)(2,1)S(1)} %add_convert_fusion.1), channel_id=1, source_target_pairs={{0,2},{1,3},{2,0},{3,1},{4,6},{5,7},{6,4},{7,5},{8,10},{9,11},{10,... | collective-permute-start | bytes 1572872 | tf_op jit(solution)/shard_map/ppermute | solution.py:418
  95.3 13.1 %collective-permute-start.28 = (bf16[512,256]{1,0:T(8,128)(2,1)S(1)}, bf16[512,256]{1,0:T(8,128)(2,1)S(1)}, u32[]{:S(2)}, u32[]{:S(2)}) collective-permute-start(bf16[512,256]{1,0:T(8,128)(2,1)S(1)} %add_convert_fusion.6), channel_id=1, source_target_pairs={{0,4},{4,0},{8,12},{12,8},{1,5},{5,1},{9,13},{13,9},{2,6},{6,2},{1... | collective-permute-start | bytes 786440 | tf_op jit(solution)/shard_map/ppermute | solution.py:418
  103.0 8.2 %collective-permute-start.26 = (bf16[512,256]{1,0:T(8,128)(2,1)S(1)}, bf16[512,256]{1,0:T(8,128)(2,1)S(1)}, u32[]{:S(2)}, u32[]{:S(2)}) collective-permute-start(bf16[512,256]{1,0:T(8,128)(2,1)S(1)} %add_convert_fusion.8), channel_id=1, source_target_pairs={{0,4},{4,0},{8,12},{12,8},{1,5},{5,1},{9,13},{13,9},{2,6},{6,2},{1... | collective-permute-start | bytes 786440 | tf_op jit(solution)/shard_map/ppermute | solution.py:418

commit v5 on v4

--- a/solution.py
+++ b/solution.py
@@ -62,14 +62,13 @@
     return jnp.where(jnp.right_shift(row, step_bits) == col, weight, 0.0).astype(BF16)
 
 
-def key_value_body(local_levels, far_levels, parts, tok_hbm, wk_hbm, wv_hbm, wq_hbm, *refs):
-    count = local_levels + 1
-    out_hbm = refs[:count]
-    far = refs[count : count + far_levels]
-    refs = refs[count + far_levels :]
-    tok_ref, wk_ref, wv_ref, wq_ref = refs[:4]
-    held = refs[4 : 4 + count]
-    in_sems, out_sems = refs[4 + count :]
+def key_value_body(local_levels, far_levels, parts, tok_hbm, wk_hbm, wv_hbm, *refs):
+    out_hbm = refs[:local_levels]
+    far = refs[local_levels : local_levels + far_levels]
+    refs = refs[local_levels + far_levels :]
+    tok_ref, wk_ref, wv_ref = refs[:3]
+    levels = refs[3 : 3 + local_levels]
+    in_sems, out_sems = refs[3 + local_levels :]
     part = tok_ref.shape[0] // parts
 
     def fetch(source, target, i):
@@ -78,7 +77,7 @@
         return copy
 
     def flush(i):
-        copy = pltpu.make_async_copy(held[i], out_hbm[i], out_sems.at[i])
+        copy = pltpu.make_async_copy(levels[i], out_hbm[i], out_sems.at[i])
         copy.start()
         return copy
 
@@ -86,30 +85,24 @@
     tiles = []
     for p in range(parts):
         rows = pl.ds(p * part, part)
-        tiles.append(fetch(tok_hbm.at[rows], tok_ref.at[rows], 3 + p))
-    weights.append(fetch(wq_hbm, wq_ref, 2))
-    kv_ref, q_ref = held[0], held[-1]
-    weights[0].wait()
-    weights[1].wait()
+        tiles.append(fetch(tok_hbm.at[rows], tok_ref.at[rows], 2 + p))
+    for copy in weights:
+        copy.wait()
     for p in range(parts):
         tiles[p].wait()
         here = slice(p * part, (p + 1) * part)
         x = tok_ref[here, :]
         both = jnp.concatenate([dot(x, wk_ref[...]), dot(x, wv_ref[...])], axis=1)
-        kv_ref[here, :] = both.astype(BF16)
+        levels[0][here, :] = both.astype(BF16)
     flushes = [flush(0)]
-    weights[2].wait()
-    q_ref[...] = dot(tok_ref[...], wq_ref[...]).astype(BF16)
     pool = pool_matrix(part)
-    source = kv_ref
     for i in range(1, local_levels):
-        rows = source.shape[0]
-        for low in range(0, rows, part):
-            held[i][low // 2 : (low + part) // 2, :] = dot(pool, source[low : low + part, :]).astype(BF16)
+        source = levels[i - 1]
+        for low in range(0, source.shape[0], part):
+            mean = dot(pool, source[low : low + part, :])
+            levels[i][low // 2 : (low + part) // 2, :] = mean.astype(BF16)
         flushes.append(flush(i))
-        source = held[i]
-    flushes.append(flush(count - 1))
-    rows = dot(pool, source[...]).astype(BF16)
+    rows = dot(pool, levels[-1][...]).astype(BF16)
     for i in range(far_levels):
         if i:
             rows = dot(pool_matrix(rows.shape[0]), rows).astype(BF16)
@@ -118,40 +111,42 @@
         copy.wait()
 
 
-def key_value(tokens, w_key, w_value, w_query, local_levels, far_levels):
+def key_value(tokens, w_key, w_value, local_levels, far_levels):
     tok_rows, width = tokens.shape
     inner = w_key.shape[1]
     parts = tok_rows // (2 * BLOCK)
-    held = [(tok_rows >> i, 2 * inner) for i in range(local_levels)] + [(tok_rows, inner)]
+    held = [(tok_rows >> i, 2 * inner) for i in range(local_levels)]
     tops = [(BLOCK >> i, 2 * inner) for i in range(far_levels)]
     return pl.pallas_call(
         functools.partial(key_value_body, local_levels, far_levels, parts),
-        in_specs=[pl.BlockSpec(memory_space=pl.ANY)] * 4,
+        in_specs=[pl.BlockSpec(memory_space=pl.ANY)] * 3,
         out_specs=[pl.BlockSpec(memory_space=pl.ANY)] * len(held)
         + [pl.BlockSpec(memory_space=pltpu.VMEM)] * len(tops),
         out_shape=[shape(*dims) for dims in held + tops],
         scratch_shapes=[pltpu.VMEM((tok_rows, width), BF16)]
-        + [pltpu.VMEM((width, inner), BF16)] * 3
+        + [pltpu.VMEM((width, inner), BF16)] * 2
         + [pltpu.VMEM(dims, BF16) for dims in held]
-        + [pltpu.SemaphoreType.DMA((parts + 3,)), pltpu.SemaphoreType.DMA((len(held),))],
+        + [pltpu.SemaphoreType.DMA((parts + 2,)), pltpu.SemaphoreType.DMA((len(held),))],
         compiler_params=params(56),
-        cost_estimate=cost(6 * tok_rows * width * inner, 2 * tok_rows * width + 12 * width * inner),
-    )(tokens, w_key, w_value, w_query)
+        cost_estimate=cost(4 * tok_rows * width * inner, 2 * tok_rows * width + 8 * width * inner),
+    )(tokens, w_key, w_value)
 
 
 def project_body(left_ref, weight_ref, out_ref):
     out_ref[...] = dot(left_ref[...], weight_ref[...]).astype(BF16)
 
 
-def project(left, weight):
+def project(left, weight, after=()):
     tok_rows, width = left.shape
     inner = weight.shape[1]
-    return pl.pallas_call(
+    return run(
         project_body,
+        [left, weight],
+        after,
         out_shape=shape(tok_rows, inner),
         compiler_params=params(4),
         cost_estimate=cost(2 * tok_rows * width * inner, 2 * tok_rows * width + 4 * width * inner),
-    )(left, weight)
+    )
 
 
 class KeySet:
@@ -173,89 +168,148 @@
             sibling = jnp.bitwise_xor(jnp.right_shift(m, i), 1)
             yield pl.ds(pl.multiple_of(sibling * BLOCK, BLOCK), BLOCK)
 
-    def rows(self, m, kv_ref, mid_refs, far_refs, cols):
-        rows = [kv_ref[self.here(m), cols]]
-        rows += [ref[seat, cols] for ref, seat in zip(mid_refs, self.seats(m))]
-        rows += [ref[:, cols] for ref in far_refs]
-        return jnp.concatenate(rows, axis=0)
-
-    def pieces(self, array):
-        return [array[a:b] for a, b in zip(self.bounds, self.bounds[1:])]
-
-    def top(self, raw):
+    def near(self, m, level_refs, cols):
+        rows = [level_refs[0][self.here(m), cols]]
+        rows += [ref[seat, cols] for ref, seat in zip(level_refs[1:], self.seats(m))]
+        return rows
+
+    def far(self, far_refs, cols):
+        return [ref[:, cols] for ref in far_refs]
+
+    def pieces(self, array, first=0, count=None):
+        base = self.bounds[first]
+        ends = self.bounds[first:] if count is None else self.bounds[first : first + count + 1]
+        return [array[a - base : b - base] for a, b in zip(ends, ends[1:])]
+
+    def top(self, pieces, first=0):
         tops = [
             jnp.max(piece, axis=0, keepdims=True) * self.factor + bias
-            for piece, bias in zip(self.pieces(raw), self.biases)
+            for piece, bias in zip(pieces, self.biases[first:])
         ]
         return functools.reduce(jnp.maximum, tops)
 
-    def powers(self, raw, top):
+    def powers(self, pieces, top, first=0):
         return jnp.concatenate(
             [
                 jnp.exp2(piece * self.factor + (bias - top))
-                for piece, bias in zip(self.pieces(raw), self.biases)
+                for piece, bias in zip(pieces, self.biases[first:])
             ],
             axis=0,
         )
 
 
+def head_columns(h, inner):
+    low = h * HEAD_DIM
+    return slice(low, low + HEAD_DIM), slice(inner + low, inner + low + HEAD_DIM)
+
+
+def near_body(local_levels, q_ref, *refs):
+    level_refs = refs[:local_levels]
+    power_ref, stat_ref = refs[local_levels:]
+    tok_rows, inner = q_ref.shape
+    heads = inner // HEAD_DIM
+    keyset = KeySet([], [], local_levels)
+    rows = keyset.far_start
+
+    def step(m, carry):
+        here = keyset.here(m)
+        for h in range(heads):
+            cols, _ = head_columns(h, inner)
+            keys = jnp.concatenate(keyset.near(m, level_refs, cols), axis=0)
+            pieces = keyset.pieces(dot(keys, q_ref[here, cols], NT))
+            top = keyset.top(pieces)
+            powers = keyset.powers(pieces, top)
+            stat_ref[h : h + 1, here] = top
+            stat_ref[heads + h : heads + h + 1, here] = jnp.sum(powers, axis=0, keepdims=True)
+            power_ref[pl.ds(pl.multiple_of((m * heads + h) * rows, rows), rows), :] = powers
+        return carry
+
+    lax.fori_loop(0, tok_rows // (2 * BLOCK), step, 0)
+
+
+def near_powers(query, levels):
+    tok_rows, inner = query.shape
+    heads = inner // HEAD_DIM
+    pairs = tok_rows // (2 * BLOCK)
+    rows = (len(levels) + 1) * BLOCK
+    return run(
+        functools.partial(near_body, len(levels)),
+        [query, *levels],
+        out_shape=[shape(pairs * heads * rows, 2 * BLOCK, F32), shape(2 * heads, tok_rows, F32)],
+        compiler_params=params(6),
+        cost_estimate=cost(2 * tok_rows * rows * inner, 12 * tok_rows * inner, tok_rows * rows * 2),
+    )
+
+
 def forward_body(local_levels, far_bits, *refs):
-    mids = local_levels - 1
     fars = len(far_bits)
-    q_ref, kv_ref = refs[:2]
-    mid_refs = refs[2 : 2 + mids]
-    far_refs = refs[2 + mids : 2 + mids + fars]
-    att_ref, att_t_ref, stat_ref = refs[2 + mids + fars :]
+    q_ref, power_ref, near_ref = refs[:3]
+    level_refs = refs[3 : 3 + local_levels]
+    far_refs = refs[3 + local_levels : 3 + local_levels + fars]
+    att_ref, att_t_ref, stat_ref = refs[3 + local_levels + fars :]
     tok_rows, inner = q_ref.shape
     heads = inner // HEAD_DIM
     keyset = KeySet([r.shape[0] for r in far_refs], far_bits, local_levels)
+    rows = keyset.far_start
 
     def step(m, carry):
         here = keyset.here(m)
         for h in range(heads):
-            cols = slice(h * HEAD_DIM, (h + 1) * HEAD_DIM)
-            vcols = slice(inner + h * HEAD_DIM, inner + (h + 1) * HEAD_DIM)
-            keys = keyset.rows(m, kv_ref, mid_refs, far_refs, cols)
-            values = keyset.rows(m, kv_ref, mid_refs, far_refs, vcols)
-            raw = dot(keys, q_ref[here, cols], NT)
-            top = keyset.top(raw)
-            expo = keyset.powers(raw, top)
-            inverse = 1.0 / jnp.sum(expo, axis=0, keepdims=True)
-            att_t = dot(values, (expo * inverse).astype(BF16), TN).astype(BF16)
+            cols, vcols = head_columns(h, inner)
+            second = heads + h
+            keys = jnp.concatenate(keyset.far(far_refs, cols), axis=0)
+            values = keyset.near(m, level_refs, vcols) + keyset.far(far_refs, vcols)
+            values = jnp.concatenate(values, axis=0)
+            first = local_levels
+            pieces = keyset.pieces(dot(keys, q_ref[here, cols], NT), first)
+            near_top = near_ref[h : h + 1, here]
+            top = jnp.maximum(near_top, keyset.top(pieces, first))
+            shrink = jnp.exp2(near_top - top)
+            powers = keyset.powers(pieces, top, first)
+            total = near_ref[second : second + 1, here] * shrink
+            total = total + jnp.sum(powers, axis=0, keepdims=True)
+            inverse = 1.0 / total
+            place = pl.ds(pl.multiple_of((m * heads + h) * rows, rows), rows)
+            near_probs = (power_ref[place, :] * (shrink * inverse)).astype(BF16)
+            far_probs = (powers * inverse).astype(BF16)
+            probs_b = jnp.concatenate([near_probs, far_probs], axis=0)
+            att_t = dot(values, probs_b, TN).astype(BF16)
             att_t_ref[cols, here] = att_t
             att_ref[here, cols] = att_t.T
             stat_ref[h : h + 1, here] = top
-            stat_ref[heads + h : heads + h + 1, here] = inverse
+            stat_ref[second : second + 1, here] = inverse
         return carry
 
     lax.fori_loop(0, tok_rows // (2 * BLOCK), step, 0)
 
 
-def forward(query, levels, fars, far_bits):
+def forward(query, powers, near, levels, fars, far_bits, after):
     tok_rows, inner = query.shape
     heads = inner // HEAD_DIM
     set_rows = (len(levels) + 1) * BLOCK + sum(f.shape[0] for f in fars)
-    return pl.pallas_call(
+    return run(
         functools.partial(forward_body, len(levels), far_bits),
+        [query, powers, near, *levels, *fars],
+        after,
         out_shape=[
             shape(tok_rows, inner),
             shape(inner, tok_rows),
             shape(2 * heads, tok_rows, F32),
         ],
-        compiler_params=params(8),
+        compiler_params=params(6),
         cost_estimate=cost(
-            4 * tok_rows * set_rows * inner, 12 * tok_rows * inner, tok_rows * set_rows * 2
+            3 * tok_rows * set_rows * inner, 12 * tok_rows * inner, tok_rows * set_rows
         ),
-    )(query, *levels, *fars)
+    )
 
 
 def backward_body(local_levels, far_bits, *refs):
     mids = local_levels - 1
     fars = len(far_bits)
-    q_ref, g_ref, att_t_ref, stat_ref, kv_ref = refs[:5]
-    mid_refs = refs[5 : 5 + mids]
-    far_refs = refs[5 + mids : 5 + mids + fars]
-    outs = refs[5 + mids + fars :]
+    q_ref, g_ref, att_t_ref, stat_ref = refs[:4]
+    level_refs = refs[4 : 4 + local_levels]
+    far_refs = refs[4 + local_levels : 4 + local_levels + fars]
+    outs = refs[4 + local_levels + fars :]
     dq_ref, dq_t_ref, dkv_ref = outs[:3]
     dfar_refs = outs[3 : 3 + fars]
     dmid_refs = outs[3 + fars : 3 + fars + mids]
@@ -271,15 +325,16 @@
     def step(m, carry):
         here = keyset.here(m)
         for h in range(heads):
-            cols = slice(h * HEAD_DIM, (h + 1) * HEAD_DIM)
-            vcols = slice(inner + h * HEAD_DIM, inner + (h + 1) * HEAD_DIM)
-            keys = keyset.rows(m, kv_ref, mid_refs, far_refs, cols)
-            values = keyset.rows(m, kv_ref, mid_refs, far_refs, vcols)
+            cols, vcols = head_columns(h, inner)
+            keys, values = (
+                jnp.concatenate(keyset.near(m, level_refs, c) + keyset.far(far_refs, c), axis=0)
+                for c in (cols, vcols)
+            )
             q = q_ref[here, cols]
             g = g_ref[here, cols]
             top = stat_ref[h : h + 1, here]
             inverse = stat_ref[heads + h : heads + h + 1, here]
-            probs = keyset.powers(dot(keys, q, NT), top) * inverse
+            probs = keyset.powers(keyset.pieces(dot(keys, q, NT)), top) * inverse
             att_t = att_t_ref[cols, here].astype(F32)
             delta = jnp.sum(g.T.astype(F32) * att_t, axis=0, keepdims=True)
             grads = (probs * (dot(values, g, NT) - delta) * score_scale).astype(BF16)
@@ -439,36 +494,86 @@
         distance *= 2
 
 
+def half_body(chunk_ref, into_ref, out_ref):
+    out_ref[...] = (chunk_ref[...].astype(F32) + into_ref[...].astype(F32)).astype(BF16)
+
+
+def half_sum(chunk, into, after=()):
+    return run(
+        half_body,
+        [chunk, into],
+        after,
+        out_shape=shape(*chunk.shape),
+        compiler_params=params(2),
+        cost_estimate=cost(chunk.size, 6 * chunk.size),
+    )
+
+
+def turn_body(end_ref, half_ref, across_ref, chunk_ref, total_ref, send_ref):
+    total = (half_ref[...].astype(F32) + across_ref[...].astype(F32)).astype(BF16)
+    total_ref[...] = total
+
+    @pl.when(end_ref[0] == 1)
+    def _():
+        send_ref[...] = chunk_ref[...]
+
+    @pl.when(end_ref[0] == 0)
+    def _():
+        send_ref[...] = total
+
+
+def turn(end, half, across, chunk, after=()):
+    return run(
+        turn_body,
+        [end, half, across, chunk],
+        after,
+        in_specs=[pl.BlockSpec(memory_space=pltpu.SMEM)]
+        + [pl.BlockSpec(memory_space=pltpu.VMEM)] * 3,
+        out_shape=[shape(*half.shape)] * 2,
+        compiler_params=params(2),
+        cost_estimate=cost(half.size, 10 * half.size),
+    )
+
+
 class Line:
     lag = 3
 
-    def __init__(self, axis):
+    def __init__(self, axis, other):
+        self.axes = (axis, other)
         self.axis = axis
         self.count = lax.axis_size(axis)
         rank = jnp.bitwise_and(lax.axis_index(axis), 3)
         self.at_end = (rank == 0) | (rank == 3)
+        self.end = jnp.reshape(self.at_end, (1,)).astype(jnp.int32)
+        width = lax.axis_size(other)
         self.across = []
-        for low in range(0, self.count, 4):
-            self.across += [(low, low), (low + 1, low + 2), (low + 2, low + 1), (low + 3, low + 3)]
-        self.halves, self.totals, self.sums = [], [], []
-
-    def push(self, chunk):
+        for place in range(self.count):
+            for seat in range(width):
+                target = (place, seat ^ 1 if width > 1 else seat)
+                if place & 3 in (1, 2):
+                    target = (place ^ 3, seat)
+                self.across.append((place * width + seat, target[0] * width + target[1]))
+        self.chunks, self.halves, self.crossed, self.totals, self.sums = [], [], [], [], []
+
+    def push(self, chunk, after=(), later=()):
+        k = len(self.chunks)
+        self.chunks.append(chunk)
         if self.count < 4:
             total = add(chunk, exchange(chunk, self.axis, 1)) if self.count == 2 else chunk
             self.halves.append(total)
-            self.totals.append(total)
             self.sums.append(total)
             return
-        k = len(self.totals)
         send = chunk
         if k >= self.lag:
-            send = jnp.where(self.at_end, chunk, self.totals[k - self.lag])
+            old = k - self.lag
+            total, send = turn(self.end, self.halves[old], self.crossed[old], chunk, later)
+            self.totals.append(total)
         into = exchange(send, self.axis, 1)
         if k >= self.lag:
             self.receive(into)
-        half = add(chunk, into)
+        half = half_sum(chunk, into, after)
         self.halves.append(half)
-        self.totals.append(add(half, lax.ppermute(half, self.axis, self.across)))
+        self.crossed.append(lax.ppermute(half, self.axes, self.across))
 
     def receive(self, into):
         result = jnp.where(self.at_end, into, self.totals[len(self.sums)])
@@ -478,9 +583,12 @@
             distance *= 2
         self.sums.append(result)
 
-    def finish(self):
-        while len(self.sums) < len(self.totals):
-            self.receive(exchange(self.totals[len(self.sums)], self.axis, 1))
+    def finish(self, last):
+        while len(self.sums) < len(self.chunks):
+            old = len(self.sums)
+            after = last if old == len(self.chunks) - 1 else ()
+            self.totals.append(half_sum(self.halves[old], self.crossed[old], after))
+            self.receive(exchange(self.totals[old], self.axis, 1))
         return self.sums
 
 
@@ -492,37 +600,47 @@
     far_levels = count.bit_length() - 1
     far_bits = [d.bit_length() - 1 for d in range(1, count)]
 
-    parts = key_value(tokens, w_key, w_value, w_query, local_levels, far_levels)
-    levels, query, tops = parts[:local_levels], parts[local_levels], parts[local_levels + 1 :]
+    parts = key_value(tokens, w_key, w_value, local_levels, far_levels)
+    levels, tops = parts[:local_levels], parts[local_levels:]
     fars = [exchange(tops[bit], "seq", d) for d, bit in enumerate(far_bits, 1)]
-    grad = project(cotangent, w_out)
-    attended, attended_t, stats = forward(query, levels, fars, far_bits)
+    query = project(tokens, w_query)
+    powers, near = near_powers(query, levels)
+    grad = project(cotangent, w_out, [near])
+    attended, attended_t, stats = forward(query, powers, near, levels, fars, far_bits, [grad])
     pieces = 2
-    line = Line("seq")
-
-    def push_terms(left, which, right, after):
+    line = Line("seq", "head")
+
+    def terms(left, which, right, after):
+        chunks = []
         for p in range(pieces):
-            chunk = weight_terms(left, right, inner, which, p, pieces, after)
-            line.push(chunk)
-            after = [chunk]
-        return after
-
-    after = push_terms(attended_t, 0, cotangent, [])
+            chunks.append(weight_terms(left, right, inner, which, p, pieces, after))
+            after = chunks[-1:]
+        return chunks
+
+    chunks = terms(attended_t, 0, cotangent, [])
+    line.push(chunks[0])
+    line.push(chunks[1])
     dquery, dquery_t, dkv, *dfars = backward(
-        query, grad, attended_t, stats, levels, fars, far_bits, after
+        query, grad, attended_t, stats, levels, fars, far_bits, chunks
     )
     backs = [exchange(piece, "seq", d) for d, piece in enumerate(dfars, 1)]
-    after = push_terms(dquery_t, 0, tokens, [line.halves[0]])
-    parts = project_split([attended], [w_out], "head", after)
-    mixed = scatter_sum(*parts, "head")
+    chunks = terms(dquery_t, 0, tokens, line.halves[:1])
+    line.push(chunks[0])
+    keep, send = project_split([attended], [w_out], "head", chunks)
+    mixed = scatter_sum(keep, send, "head")
     dkey, dvalue, dkv_t = close_keys(
-        dkv, backs, far_bits, local_levels, [parts[0], line.halves[1]]
-    )
-    after = push_terms(dkv_t, 0, tokens, [line.totals[0]])
-    after = push_terms(dkv_t, 1, tokens, after)
-    parts = project_split([dquery, dkey, dvalue], [w_query, w_key, w_value], "head", after)
-    tokens_grad = scatter_sum(*parts, "head")
-    sums = line.finish()
+        dkv, backs, far_bits, local_levels, [keep, line.halves[1]]
+    )
+    line.push(chunks[1])
+    chunks = terms(dkv_t, 0, tokens, [])
+    line.push(chunks[0])
+    line.push(chunks[1])
+    chunks = terms(dkv_t, 1, tokens, chunks)
+    line.push(chunks[0], [mixed])
+    keep, send = project_split([dquery, dkey, dvalue], [w_query, w_key, w_value], "head", chunks)
+    tokens_grad = scatter_sum(keep, send, "head")
+    line.push(chunks[1])
+    sums = line.finish([tokens_grad])
     out_grad, query_grad, key_grad, value_grad = (
         jnp.concatenate(sums[i : i + pieces], axis=0) for i in range(0, len(sums), pieces)
     )

time: 115 us -> 123 us (1.070)
  waiting for transfers between devices: 16.8 us -> 46 us
  starting transfers between devices: 57.3 us -> 36.6 us
  Pallas kernels: 26.4 us -> 32.8 us
  local copies, waits for them, and re-layouts: 5.14 us -> 1.31 us
  other arithmetic: 7.33 us -> 4.27 us
    ppermute x21, waiting for transfers between devices: 16.8 us -> 46 us  [exchange(): return lax.ppermute(block, axis, [(i, i ^ distance) for i in range(count)])]
    ppermute x21, starting transfers between devices: 51.7 us -> 35.6 us  [exchange(): return lax.ppermute(block, axis, [(i, i ^ distance) for i in range(count)])]
    pallas_call x12 -> x32, Pallas kernels: 14.1 us -> 27.4 us  [run(): return pl.pallas_call(kernel, in_specs=in_specs, **options)(*ready, *after)]
    pallas_call x2 -> x0, Pallas kernels: 6.59 us -> none  [the longest x1 5.88 us: forward(): pl.pallas_call(functools.partial(forward_body, len(levels), far_bits), ou...]
    ppermute x8, starting transfers between devices: 5.6 us -> 1 us  [push(): self.crossed.append(lax.ppermute(half, self.axes, self.across))]
    unnamed x28 -> x40, local copies, waits for them, and re-layouts: 5.14 us -> 1.31 us
    convert_element_type x15 -> x4, other arithmetic: 2.97 us -> 0.68 us  [add(): return (left.astype(F32) + right.astype(F32)).astype(BF16)]
  transfers between devices with their start and end apart: 29 -> 29, of which waited for: 7 -> 11; matrix products, arithmetic and copies ran while one was open for 6% -> 3% of each run, Pallas kernels for 13% -> 19%
where the time goes in v5:
time: 123 us; the launch traced here: 122 us
  waiting for transfers between devices  46 us (37%)
  starting transfers between devices  36.6 us (30%)
  Pallas kernels  32.8 us (27%)
  other arithmetic  4.27 us (3%)
  local copies, waits for them, and re-layouts  1.31 us (1%)
  between operations  1.26 us (1%)
    ppermute x21, waiting for transfers between devices, exchange(): return lax.ppermute(block, axis, [(i, i ^ distance) for i in range(count)])  46 us
    ppermute x21, starting transfers between devices, exchange(): return lax.ppermute(block, axis, [(i, i ^ distance) for i in range(count)])  35.6 us
    pallas_call x32, Pallas kernels, run(): return pl.pallas_call(kernel, in_specs=in_specs, **options)(*ready, *after)  27.4 us
    pallas_call x1, Pallas kernels, key_value(): pl.pallas_call(functools.partial(key_value_body, local_levels, far_levels...  5.45 us
    concatenate x4, other arithmetic, per_device(): jnp.concatenate(sums[i:i + pieces], axis=0)  3.36 us
  transfers between devices with their start and end apart: 29, of which 11 were waited for; matrix products, arithmetic and copies ran while one was open for 3% of the time, Pallas kernels for 19%

profile of v5, /device:TPU:0, one launch (start us, length us, event | category | flops | bytes accessed | tf_op | source)
XLA Modules:
  0.0 122.3 jit_solution(16455032705451459993)
XLA Ops:
  0.7 5.5 %shard_map.110 = (bf16[1024,512]{1,0:T(8,128)(2,1)}, bf16[512,512]{1,0:T(8,128)(2,1)}, bf16[256,512]{1,0:T(8,128)(2,1)}, bf16[128,512]{1,0:T(8,128)(2,1)}, bf16[64,512]{1,0:T(8,128)(2,1)}) custom-call(bf16[1024,1024]{1,0:T(8,128)(2,1)} %refs_1_.19, bf16[1024,256]{1,0:T(8,128)(2,1)} %refs_5_.1, bf16[1024,256]{1,0:T(8,128)(2,1)} %refs_6_.1), custom_call_target="tpu_custom_call" | custom-call | flops 1073741824 | bytes 4194304 | tf_op jit(solution)/shard_map/pallas_call | solution.py:120
  6.1 3.1 %collective-permute-start = (bf16[128,512]{1,0:T(8,128)(2,1)}, bf16[128,512]{1,0:T(8,128)(2,1)S(1)}, u32[]{:S(2)}, u32[]{:S(2)}) collective-permute-start(bf16[128,512]{1,0:T(8,128)(2,1)} %get-tuple-element.44), channel_id=1, source_target_pairs={{0,4},{4,0},{8,12},{12,8},{1,5},{5,1},{9,13},{13,9},{2,6},{6,2},{1... | collective-permute-start | bytes 393224 | tf_op jit(solution)/shard_map/ppermute | solution.py:473
  9.2 2.6 %collective-permute-start.1 = (bf16[64,512]{1,0:T(8,128)(2,1)}, bf16[64,512]{1,0:T(8,128)(2,1)S(1)}, u32[]{:S(2)}, u32[]{:S(2)}) collective-permute-start(bf16[64,512]{1,0:T(8,128)(2,1)} %get-tuple-element.45), channel_id=1, source_target_pairs={{0,8},{4,12},{8,0},{12,4},{1,9},{5,13},{9,1},{13,5},{2,10},{6,14},... | collective-permute-start | bytes 196616 | tf_op jit(solution)/shard_map/ppermute | solution.py:473
  11.8 0.7 shard_map.109.refs_0_
  12.6 2.4 %shard_map.111 = (f32[4096,256]{1,0:T(8,128)S(1)}, f32[4,1024]{1,0:T(4,128)S(1)}) custom-call(bf16[1024,256]{1,0:T(8,128)(2,1)S(1)} %shard_map.109.refs_0_, bf16[1024,512]{1,0:T(8,128)(2,1)S(1)} %copy-done.2, bf16[512,512]{1,0:T(8,128)(2,1)S(1)} %copy-done.3, bf16[256,512]{1,0:T(8,128)(2,1)S(1)} %copy-done.8), custom_call_target="tpu_custom_call" | custom-call | flops 268435456 | bytes 3145728 | tf_op jit(solution)/shard_map/pallas_call | solution.py:42
  15.0 0.7 shard_map.112.refs_9_.refs_1_
  16.0 2.2 %collective-permute-done.2.refs_8_.refs_9_ = bf16[64,512]{1,0:T(8,128)(2,1)S(1)} collective-permute-done((bf16[64,512]{1,0:T(8,128)(2,1)}, bf16[64,512]{1,0:T(8,128)(2,1)S(1)}, u32[]{:S(2)}, u32[]{:S(2)}) %collective-permute-start.2) | collective-permute-done | bytes 65568 | tf_op jit(solution)/shard_map/ppermute | solution.py:473
  18.2 3.9 %shard_map.113 = (bf16[1024,256]{1,0:T(8,128)(2,1)S(1)}, bf16[256,1024]{1,0:T(8,128)(2,1)S(1)}, f32[4,1024]{1,0:T(4,128)S(1)}) custom-call(bf16[1024,256]{1,0:T(8,128)(2,1)S(1)} %shard_map.109.refs_0_, f32[4096,256]{1,0:T(8,128)S(1)} %get-tuple-element.42.refs_1_, f32[4,1024]{1,0:T(4,128)S(1)} %get-tuple-element.43.refs_2_, bf16[1024,512]{1,0:T(8,128)(2,1)S(1)} %copy-done.2, ...), custom_call_target="tpu_custom_call" | custom-call | flops 603979776 | bytes 3145728 | tf_op jit(solution)/shard_map/pallas_call | solution.py:42
  22.1 0.5 shard_map.114.refs_2_.refs_10_.refs_0_
  22.9 1.1 collective-permute-start.3
  24.0 0.5 shard_map.115.refs_11_.refs_0_
  24.5 1.0 collective-permute-start.9
  25.5 7.0 %shard_map.116 = (bf16[1024,256]{1,0:T(8,128)(2,1)S(1)}, bf16[256,1024]{1,0:T(8,128)(2,1)S(1)}, f32[1024,512]{1,0:T(8,128)S(1)}, bf16[128,512]{1,0:T(8,128)(2,1)...) custom-call(bf16[1024,256]{1,0:T(8,128)(2,1)S(1)} %shard_map.109.refs_0_, ...), custom_call_target="tpu_custom_call" | custom-call | flops 2013265920 | bytes 6291456 | tf_op jit(solution)/shard_map/pallas_call | solution.py:42
  32.7 3.0 %collective-permute-done.9.refs_1_ = bf16[512,256]{1,0:T(8,128)(2,1)S(1)} collective-permute-done((bf16[512,256]{1,0:T(8,128)(2,1)S(1)}, bf16[512,256]{1,0:T(8,128)(2,1)S(1)}, u32[]{:S(2)}, u32[]{:S(2)}) %collective-permute-start.9) | collective-permute-done | bytes 262176 | tf_op jit(solution)/shard_map/ppermute | solution.py:473
  35.8 0.5 shard_map.118.refs_2_.refs_3_.refs_0_
  36.3 0.8 collective-permute-start.12
  37.2 1.2 collective-permute-start.7
  38.4 1.8 %collective-permute-start.6 = (bf16[128,512]{1,0:T(8,128)(2,1)}, bf16[128,512]{1,0:T(8,128)(2,1)S(1)}, u32[]{:S(2)}, u32[]{:S(2)}) collective-permute-start(bf16[128,512]{1,0:T(8,128)(2,1)} %get-tuple-element.54), channel_id=1, source_target_pairs={{0,4},{4,0},{8,12},{12,8},{1,5},{5,1},{9,13},{13,9},{2,6},{6,2},{1... | collective-permute-start | bytes 393224 | tf_op jit(solution)/shard_map/ppermute | solution.py:473
  40.2 6.7 %collective-permute-done.7.refs_2_ = bf16[64,512]{1,0:T(8,128)(2,1)} collective-permute-done((bf16[64,512]{1,0:T(8,128)(2,1)}, bf16[64,512]{1,0:T(8,128)(2,1)}, u32[]{:S(2)}, u32[]{:S(2)}) %collective-permute-start.7) | collective-permute-done | bytes 65568 | tf_op jit(solution)/shard_map/ppermute | solution.py:473
  46.9 1.4 %collective-permute-start.8 = (bf16[64,512]{1,0:T(8,128)(2,1)}, bf16[64,512]{1,0:T(8,128)(2,1)S(1)}, u32[]{:S(2)}, u32[]{:S(2)}) collective-permute-start(bf16[64,512]{1,0:T(8,128)(2,1)} %copy-done.17), channel_id=1, source_target_pairs={{0,12},{4,8},{8,4},{12,0},{1,13},{5,9},{9,5},{13,1},{2,14},{6,10},... | collective-permute-start | bytes 196616 | tf_op jit(solution)/shard_map/ppermute | solution.py:473
  48.9 0.7 shard_map.120
  49.6 3.6 %collective-permute-done.8.refs_3_ = bf16[64,512]{1,0:T(8,128)(2,1)S(1)} collective-permute-done((bf16[64,512]{1,0:T(8,128)(2,1)}, bf16[64,512]{1,0:T(8,128)(2,1)S(1)}, u32[]{:S(2)}, u32[]{:S(2)}) %collective-permute-start.8) | collective-permute-done | bytes 65568 | tf_op jit(solution)/shard_map/ppermute | solution.py:473
  53.2 1.9 %shard_map.122 = (bf16[1024,256]{1,0:T(8,128)(2,1)S(1)}, bf16[1024,256]{1,0:T(8,128)(2,1)S(1)}, bf16[512,1024]{1,0:T(8,128)(2,1)S(1)}) custom-call(f32[1024,512]{1,0:T(8,128)S(1)} %copy-done.5, bf16[128,512]{1,0:T(8,128)(2,1)S(1)} %collective-permute-done.6.refs_1_, bf16[64,512]{1,0:T(8,128)(2,1)} %collective-permute-done.7.refs_2_, ...), custom_call_target="tpu_custom_call" | custom-call | flops 268435456 | bytes 6291456 | tf_op jit(solution)/shard_map/pallas_call | solution.py:42
  55.1 0.5 shard_map.123.refs_2_.refs_3_.refs_0_
  55.6 1.0 shard_map.130
  56.7 1.2 shard_map.133
  58.0 2.1 %collective-permute-start.20 = (bf16[512,256]{1,0:T(8,128)(2,1)S(1)}, bf16[512,256]{1,0:T(8,128)(2,1)S(1)}, u32[]{:S(2)}, u32[]{:S(2)}) collective-permute-start(bf16[512,256]{1,0:T(8,128)(2,1)S(1)} %get-tuple-element.67), channel_id=1, source_target_pairs={{0,4},{4,0},{8,12},{12,8},{1,5},{5,1},{9,13},{13,9},{2,6},{6,2},{1... | collective-permute-start | bytes 786440 | tf_op jit(solution)/shard_map/ppermute | solution.py:473
  60.0 1.0 shard_map.128.refs_1_
  61.6 0.5 shard_map.124.refs_3_.refs_0_
  62.1 0.5 shard_map.125.refs_2_.refs_7_.refs_3_.refs_0_
  62.7 0.5 shard_map.126.refs_8_.refs_3_.refs_0_
  64.2 1.8 %shard_map.127 = (bf16[1024,512]{1,0:T(8,128)(2,1)S(1)}, bf16[1024,512]{1,0:T(8,128)(2,1)S(1)}) custom-call(s32[1]{0:T(128)} %bitcast.refs_0_, bf16[1024,256]{1,0:T(8,128)(2,1)S(1)} %copy-done.19, bf16[1024,256]{1,0:T(8,128)(2,1)S(1)} %get-tuple-element.57.refs_2_, bf16[1024,256]{1,0:T(8,128)(2,1)S(1)} %get-tuple-element.58.refs_3_, ...), custom_call_target="tpu_custom_call" | custom-call | flops 1610612736 | bytes 2097152 | tf_op jit(solution)/shard_map/pallas_call | solution.py:42
  67.3 2.5 %collective-permute-start.14 = (bf16[512,256]{1,0:T(8,128)(2,1)S(1)}, bf16[512,256]{1,0:T(8,128)(2,1)S(1)}, u32[]{:S(2)}, u32[]{:S(2)}) collective-permute-start(bf16[512,256]{1,0:T(8,128)(2,1)S(1)} %get-tuple-element.62), channel_id=1, source_target_pairs={{0,4},{4,0},{8,12},{12,8},{1,5},{5,1},{9,13},{13,9},{2,6},{6,2},{1... | collective-permute-start | bytes 786440 | tf_op jit(solution)/shard_map/ppermute | solution.py:473
  69.9 0.8 pad_maximum_fusion.3
  70.8 6.0 %collective-permute-start.18 = (bf16[512,256]{1,0:T(8,128)(2,1)S(1)}, bf16[512,256]{1,0:T(8,128)(2,1)S(1)}, u32[]{:S(2)}, u32[]{:S(2)}) collective-permute-start(bf16[512,256]{1,0:T(8,128)(2,1)S(1)} %get-tuple-element.65), channel_id=1, source_target_pairs={{0,4},{4,0},{8,12},{12,8},{1,5},{5,1},{9,13},{13,9},{2,6},{6,2},{1... | collective-permute-start | bytes 786440 | tf_op jit(solution)/shard_map/ppermute | solution.py:473
  76.9 4.6 %collective-permute-start.22 = (bf16[512,256]{1,0:T(8,128)(2,1)S(1)}, bf16[512,256]{1,0:T(8,128)(2,1)S(1)}, u32[]{:S(2)}, u32[]{:S(2)}) collective-permute-start(bf16[512,256]{1,0:T(8,128)(2,1)S(1)} %get-tuple-element.68), channel_id=1, source_target_pairs={{0,4},{4,0},{8,12},{12,8},{1,5},{5,1},{9,13},{13,9},{2,6},{6,2},{1... | collective-permute-start | bytes 786440 | tf_op jit(solution)/shard_map/ppermute | solution.py:473
  81.9 1.5 %collective-permute-start.5 = (bf16[1024,256]{1,0:T(8,128)(2,1)S(1)}, bf16[1024,256]{1,0:T(8,128)(2,1)S(1)}, u32[]{:S(2)}, u32[]{:S(2)}) collective-permute-start(bf16[1024,256]{1,0:T(8,128)(2,1)S(1)} %add_convert_fusion.4), channel_id=1, source_target_pairs={{0,2},{1,3},{2,0},{3,1},{4,6},{5,7},{6,4},{7,5},{8,10},{9,11},{10,... | collective-permute-start | bytes 1572872 | tf_op jit(solution)/shard_map/ppermute | solution.py:473
  83.6 0.6 collective-permute-start.11
  84.2 3.1 %collective-permute-done.22.refs_1_ = bf16[512,256]{1,0:T(8,128)(2,1)S(1)} collective-permute-done((bf16[512,256]{1,0:T(8,128)(2,1)S(1)}, bf16[512,256]{1,0:T(8,128)(2,1)S(1)}, u32[]{:S(2)}, u32[]{:S(2)}) %collective-permute-start.22) | collective-permute-done | bytes 262176 | tf_op jit(solution)/shard_map/ppermute | solution.py:473
  87.5 2.4 %collective-permute-start.24 = (bf16[512,256]{1,0:T(8,128)(2,1)S(1)}, bf16[512,256]{1,0:T(8,128)(2,1)S(1)}, u32[]{:S(2)}, u32[]{:S(2)}) collective-permute-start(bf16[512,256]{1,0:T(8,128)(2,1)S(1)} %shard_map.137), channel_id=1, source_target_pairs={{0,4},{4,0},{8,12},{12,8},{1,5},{5,1},{9,13},{13,9},{2,6},{6,2},{1... | collective-permute-start | bytes 786440 | tf_op jit(solution)/shard_map/ppermute | solution.py:473
  90.0 6.7 %collective-permute-done.5 = bf16[1024,256]{1,0:T(8,128)(2,1)S(1)} collective-permute-done((bf16[1024,256]{1,0:T(8,128)(2,1)S(1)}, bf16[1024,256]{1,0:T(8,128)(2,1)S(1)}, u32[]{:S(2)}, u32[]{:S(2)}) %collective-permute-start.5) | collective-permute-done | bytes 524320 | tf_op jit(solution)/shard_map/ppermute | solution.py:473
  96.9 0.9 pad_maximum_fusion
  97.9 9.6 %collective-permute-done.11 = bf16[1024,256]{1,0:T(8,128)(2,1)S(1)} collective-permute-done((bf16[1024,256]{1,0:T(8,128)(2,1)S(1)}, bf16[1024,256]{1,0:T(8,128)(2,1)S(1)}, u32[]{:S(2)}, u32[]{:S(2)}) %collective-permute-start.11) | collective-permute-done | bytes 524320 | tf_op jit(solution)/shard_map/ppermute | solution.py:473
  108.0 2.1 %collective-permute-start.26 = (bf16[512,256]{1,0:T(8,128)(2,1)S(1)}, bf16[512,256]{1,0:T(8,128)(2,1)S(1)}, u32[]{:S(2)}, u32[]{:S(2)}) collective-permute-start(bf16[512,256]{1,0:T(8,128)(2,1)S(1)} %shard_map.139), channel_id=1, source_target_pairs={{0,4},{4,0},{8,12},{12,8},{1,5},{5,1},{9,13},{13,9},{2,6},{6,2},{1... | collective-permute-start | bytes 786440 | tf_op jit(solution)/shard_map/ppermute | solution.py:473
  110.1 0.8 pad_maximum_fusion.1
  110.9 6.2 %collective-permute-done.28 = bf16[512,256]{1,0:T(8,128)(2,1)S(1)} collective-permute-done((bf16[512,256]{1,0:T(8,128)(2,1)S(1)}, bf16[512,256]{1,0:T(8,128)(2,1)S(1)}, u32[]{:S(2)}, u32[]{:S(2)}) %collective-permute-start.28) | collective-permute-done | bytes 262176 | tf_op jit(solution)/shard_map/ppermute | solution.py:473
  117.1 4.3 %collective-permute-done.26 = bf16[512,256]{1,0:T(8,128)(2,1)S(1)} collective-permute-done((bf16[512,256]{1,0:T(8,128)(2,1)S(1)}, bf16[512,256]{1,0:T(8,128)(2,1)S(1)}, u32[]{:S(2)}, u32[]{:S(2)}) %collective-permute-start.26) | collective-permute-done | bytes 262176 | tf_op jit(solution)/shard_map/ppermute | solution.py:473
  121.4 0.8 pad_maximum_fusion.2
  (99 shorter events, 6.1 us)
Async XLA Ops:
  0.6 11.2 %copy-start = (bf16[1024,1024]{1,0:T(8,128)(2,1)S(1)}, bf16[1024,1024]{1,0:T(8,128)(2,1)}, u32[]{:S(2)}) copy-start(bf16[1024,1024]{1,0:T(8,128)(2,1)} %refs_1_.19) | copy-start | bytes 6291460
  0.6 11.2 %copy-start.11 = (bf16[1024,256]{1,0:T(8,128)(2,1)S(1)}, bf16[1024,256]{1,0:T(8,128)(2,1)}, u32[]{:S(2)}) copy-start(bf16[1024,256]{1,0:T(8,128)(2,1)} %refs_4_.1) | copy-start | bytes 1572868
  6.1 6.4 %copy-start.2 = (bf16[1024,512]{1,0:T(8,128)(2,1)S(1)}, bf16[1024,512]{1,0:T(8,128)(2,1)}, u32[]{:S(2)}) copy-start(bf16[1024,512]{1,0:T(8,128)(2,1)} %get-tuple-element.39.refs_1_.refs_3_.refs_4_) | copy-start | bytes 3145732
  6.1 6.4 %copy-start.3 = (bf16[512,512]{1,0:T(8,128)(2,1)S(1)}, bf16[512,512]{1,0:T(8,128)(2,1)}, u32[]{:S(2)}) copy-start(bf16[512,512]{1,0:T(8,128)(2,1)} %get-tuple-element.40.refs_2_.refs_4_.refs_5_) | copy-start | bytes 1572868
  6.1 6.4 %copy-start.8 = (bf16[256,512]{1,0:T(8,128)(2,1)S(1)}, bf16[256,512]{1,0:T(8,128)(2,1)}, u32[]{:S(2)}) copy-start(bf16[256,512]{1,0:T(8,128)(2,1)} %get-tuple-element.41.refs_3_.refs_5_.refs_6_) | copy-start | bytes 786436
  6.1 12.0 %collective-permute-start = (bf16[128,512]{1,0:T(8,128)(2,1)}, bf16[128,512]{1,0:T(8,128)(2,1)S(1)}, u32[]{:S(2)}, u32[]{:S(2)}) collective-permute-start(bf16[128,512]{1,0:T(8,128)(2,1)} %get-tuple-element.44), channel_id=1, source_target_pairs={{0,4},{4,0},{8,12},{12,8},{1,5},{5,1},{9,13},{13,9},{2,6},{6,2},{1... | collective-permute-start | bytes 393224 | tf_op jit(solution)/shard_map/ppermute | solution.py:473
  9.2 5.7 %copy-start.1 = (bf16[1024,1024]{1,0:T(8,128)(2,1)S(1)}, bf16[1024,1024]{1,0:T(8,128)(2,1)}, u32[]{:S(2)}) copy-start(bf16[1024,1024]{1,0:T(8,128)(2,1)} %refs_1_.13) | copy-start | bytes 6291460
  9.2 5.7 %copy-start.9 = (bf16[1024,256]{1,0:T(8,128)(2,1)S(1)}, bf16[1024,256]{1,0:T(8,128)(2,1)}, u32[]{:S(2)}) copy-start(bf16[1024,256]{1,0:T(8,128)(2,1)} %refs_2_.1) | copy-start | bytes 1572868
  9.2 6.7 %collective-permute-start.1 = (bf16[64,512]{1,0:T(8,128)(2,1)}, bf16[64,512]{1,0:T(8,128)(2,1)S(1)}, u32[]{:S(2)}, u32[]{:S(2)}) collective-permute-start(bf16[64,512]{1,0:T(8,128)(2,1)} %get-tuple-element.45), channel_id=1, source_target_pairs={{0,8},{4,12},{8,0},{12,4},{1,9},{5,13},{9,1},{13,5},{2,10},{6,14},... | collective-permute-start | bytes 196616 | tf_op jit(solution)/shard_map/ppermute | solution.py:473
  11.8 6.3 %collective-permute-start.2 = (bf16[64,512]{1,0:T(8,128)(2,1)}, bf16[64,512]{1,0:T(8,128)(2,1)S(1)}, u32[]{:S(2)}, u32[]{:S(2)}) collective-permute-start(bf16[64,512]{1,0:T(8,128)(2,1)} %get-tuple-element.45), channel_id=1, source_target_pairs={{0,12},{4,8},{8,4},{12,0},{1,13},{5,9},{9,5},{13,1},{2,14},{6,10},... | collective-permute-start | bytes 196616 | tf_op jit(solution)/shard_map/ppermute | solution.py:473
  22.9 9.6 %collective-permute-start.3 = (bf16[512,256]{1,0:T(8,128)(2,1)S(1)}, bf16[512,256]{1,0:T(8,128)(2,1)S(1)}, u32[]{:S(2)}, u32[]{:S(2)}) collective-permute-start(bf16[512,256]{1,0:T(8,128)(2,1)S(1)} %shard_map.114.refs_2_.refs_10_.refs_0_), channel_id=1, source_target_pairs={{0,4},{4,0},{8,12},{12,8},{1,5},{5,1},{9,13},{13,9},{2,6},{6,2},{1... | collective-permute-start | bytes 786440 | tf_op jit(solution)/shard_map/ppermute | solution.py:473
  24.5 11.1 %collective-permute-start.9 = (bf16[512,256]{1,0:T(8,128)(2,1)S(1)}, bf16[512,256]{1,0:T(8,128)(2,1)S(1)}, u32[]{:S(2)}, u32[]{:S(2)}) collective-permute-start(bf16[512,256]{1,0:T(8,128)(2,1)S(1)} %shard_map.115.refs_11_.refs_0_), channel_id=1, source_target_pairs={{0,4},{4,0},{8,12},{12,8},{1,5},{5,1},{9,13},{13,9},{2,6},{6,2},{1... | collective-permute-start | bytes 786440 | tf_op jit(solution)/shard_map/ppermute | solution.py:473
  32.5 3.8 %copy-start.4 = (f32[1024,512]{1,0:T(8,128)}, f32[1024,512]{1,0:T(8,128)S(1)}, u32[]{:S(2)}) copy-start(f32[1024,512]{1,0:T(8,128)S(1)} %get-tuple-element.53.refs_0_) | copy-start | bytes 6291460
  32.5 3.8 %copy-start.17 = (bf16[64,512]{1,0:T(8,128)(2,1)}, bf16[64,512]{1,0:T(8,128)(2,1)S(1)}, u32[]{:S(2)}) copy-start(bf16[64,512]{1,0:T(8,128)(2,1)S(1)} %get-tuple-element.56) | copy-start | bytes 196612
  32.5 3.8 %copy-start.18 = (bf16[1024,256]{1,0:T(8,128)(2,1)}, bf16[1024,256]{1,0:T(8,128)(2,1)S(1)}, u32[]{:S(2)}) copy-start(bf16[1024,256]{1,0:T(8,128)(2,1)S(1)} %get-tuple-element.52.refs_1_) | copy-start | bytes 1572868
  32.6 23.0 %collective-permute-start.15 = (bf16[512,256]{1,0:T(8,128)(2,1)S(1)}, bf16[512,256]{1,0:T(8,128)(2,1)}, u32[]{:S(2)}, u32[]{:S(2)}) collective-permute-start(bf16[512,256]{1,0:T(8,128)(2,1)S(1)} %shard_map.117.refs_2_.refs_1_), channel_id=1, source_target_pairs={{0,1},{1,0},{2,3},{3,2},{4,8},{5,9},{6,10},{7,11},{8,4},{9,5},{10,... | collective-permute-start | bytes 786440 | tf_op jit(solution)/shard_map/ppermute | solution.py:576
  35.7 21.0 %collective-permute-start.19 = (bf16[512,256]{1,0:T(8,128)(2,1)S(1)}, bf16[512,256]{1,0:T(8,128)(2,1)}, u32[]{:S(2)}, u32[]{:S(2)}) collective-permute-start(bf16[512,256]{1,0:T(8,128)(2,1)S(1)} %shard_map.121.refs_5_.refs_1_), channel_id=1, source_target_pairs={{0,1},{1,0},{2,3},{3,2},{4,8},{5,9},{6,10},{7,11},{8,4},{9,5},{10,... | collective-permute-start | bytes 786440 | tf_op jit(solution)/shard_map/ppermute | solution.py:576
  36.3 23.7 %collective-permute-start.12 = (bf16[512,256]{1,0:T(8,128)(2,1)S(1)}, bf16[512,256]{1,0:T(8,128)(2,1)}, u32[]{:S(2)}, u32[]{:S(2)}) collective-permute-start(bf16[512,256]{1,0:T(8,128)(2,1)S(1)} %shard_map.118.refs_2_.refs_3_.refs_0_), channel_id=1, source_target_pairs={{0,4},{4,0},{8,12},{12,8},{1,5},{5,1},{9,13},{13,9},{2,6},{6,2},{1... | collective-permute-start | bytes 786440 | tf_op jit(solution)/shard_map/ppermute | solution.py:473
  37.2 9.7 %collective-permute-start.7 = (bf16[64,512]{1,0:T(8,128)(2,1)}, bf16[64,512]{1,0:T(8,128)(2,1)}, u32[]{:S(2)}, u32[]{:S(2)}) collective-permute-start(bf16[64,512]{1,0:T(8,128)(2,1)} %get-tuple-element.55), channel_id=1, source_target_pairs={{0,8},{4,12},{8,0},{12,4},{1,9},{5,13},{9,1},{13,5},{2,10},{6,14},... | collective-permute-start | bytes 196616 | tf_op jit(solution)/shard_map/ppermute | solution.py:473
  38.4 14.8 %collective-permute-start.6 = (bf16[128,512]{1,0:T(8,128)(2,1)}, bf16[128,512]{1,0:T(8,128)(2,1)S(1)}, u32[]{:S(2)}, u32[]{:S(2)}) collective-permute-start(bf16[128,512]{1,0:T(8,128)(2,1)} %get-tuple-element.54), channel_id=1, source_target_pairs={{0,4},{4,0},{8,12},{12,8},{1,5},{5,1},{9,13},{13,9},{2,6},{6,2},{1... | collective-permute-start | bytes 393224 | tf_op jit(solution)/shard_map/ppermute | solution.py:473
  40.1 8.7 %copy-start.10 = (bf16[1024,256]{1,0:T(8,128)(2,1)S(1)}, bf16[1024,256]{1,0:T(8,128)(2,1)}, u32[]{:S(2)}) copy-start(bf16[1024,256]{1,0:T(8,128)(2,1)} %refs_2_.1) | copy-start | bytes 1572868
  40.2 8.7 %copy-start.16 = (bf16[1024,256]{1,0:T(8,128)(2,1)S(1)}, bf16[1024,256]{1,0:T(8,128)(2,1)}, u32[]{:S(2)}) copy-start(bf16[1024,256]{1,0:T(8,128)(2,1)} %copy-done.15) | copy-start | bytes 1572868
  46.9 6.3 %copy-start.5 = (f32[1024,512]{1,0:T(8,128)S(1)}, f32[1024,512]{1,0:T(8,128)}, u32[]{:S(2)}) copy-start(f32[1024,512]{1,0:T(8,128)} %copy-done.4) | copy-start | bytes 6291460
  46.9 6.3 %collective-permute-start.8 = (bf16[64,512]{1,0:T(8,128)(2,1)}, bf16[64,512]{1,0:T(8,128)(2,1)S(1)}, u32[]{:S(2)}, u32[]{:S(2)}) collective-permute-start(bf16[64,512]{1,0:T(8,128)(2,1)} %copy-done.17), channel_id=1, source_target_pairs={{0,12},{4,8},{8,4},{12,0},{1,13},{5,9},{9,5},{13,1},{2,14},{6,10},... | collective-permute-start | bytes 196616 | tf_op jit(solution)/shard_map/ppermute | solution.py:473
  56.6 9.5 %collective-permute-start.16 = (bf16[512,256]{1,0:T(8,128)(2,1)S(1)}, bf16[512,256]{1,0:T(8,128)(2,1)S(1)}, u32[]{:S(2)}, u32[]{:S(2)}) collective-permute-start(bf16[512,256]{1,0:T(8,128)(2,1)S(1)} %get-tuple-element.64), channel_id=1, source_target_pairs={{0,4},{4,0},{8,12},{12,8},{1,5},{5,1},{9,13},{13,9},{2,6},{6,2},{1... | collective-permute-start | bytes 786440 | tf_op jit(solution)/shard_map/ppermute | solution.py:473
  58.0 9.1 %collective-permute-start.20 = (bf16[512,256]{1,0:T(8,128)(2,1)S(1)}, bf16[512,256]{1,0:T(8,128)(2,1)S(1)}, u32[]{:S(2)}, u32[]{:S(2)}) collective-permute-start(bf16[512,256]{1,0:T(8,128)(2,1)S(1)} %get-tuple-element.67), channel_id=1, source_target_pairs={{0,4},{4,0},{8,12},{12,8},{1,5},{5,1},{9,13},{13,9},{2,6},{6,2},{1... | collective-permute-start | bytes 786440 | tf_op jit(solution)/shard_map/ppermute | solution.py:473
  61.0 6.2 %collective-permute-start.13 = (bf16[512,256]{1,0:T(8,128)(2,1)S(1)}, bf16[512,256]{1,0:T(8,128)(2,1)S(1)}, u32[]{:S(2)}, u32[]{:S(2)}) collective-permute-start(bf16[512,256]{1,0:T(8,128)(2,1)S(1)} %shard_map.128.refs_1_), channel_id=1, source_target_pairs={{0,1},{1,0},{2,3},{3,2},{4,8},{5,9},{6,10},{7,11},{8,4},{9,5},{10,... | collective-permute-start | bytes 786440 | tf_op jit(solution)/shard_map/ppermute | solution.py:576
  61.1 20.6 %collective-permute-start.4 = (bf16[1024,512]{1,0:T(8,128)(2,1)S(1)}, bf16[1024,512]{1,0:T(8,128)(2,1)S(1)}, u32[]{:S(2)}, u32[]{:S(2)}) collective-permute-start(bf16[1024,512]{1,0:T(8,128)(2,1)S(1)} %get-tuple-element.51), channel_id=1, source_target_pairs={{0,1},{1,0},{2,3},{3,2},{4,5},{5,4},{6,7},{7,6},{8,9},{9,8},{10,11... | collective-permute-start | bytes 3145736 | tf_op jit(solution)/shard_map/ppermute | solution.py:473
  62.6 1.0 copy-start.12
  62.7 1.2 copy-start.13
  62.7 1.3 %copy-start.14 = (bf16[1024,256]{1,0:T(8,128)(2,1)S(1)}, bf16[1024,256]{1,0:T(8,128)(2,1)}, u32[]{:S(2)}) copy-start(bf16[1024,256]{1,0:T(8,128)(2,1)} %refs_6_.1) | copy-start | bytes 1572868
  62.7 1.5 %copy-start.19 = (bf16[1024,256]{1,0:T(8,128)(2,1)S(1)}, bf16[1024,256]{1,0:T(8,128)(2,1)}, u32[]{:S(2)}) copy-start(bf16[1024,256]{1,0:T(8,128)(2,1)} %copy-done.18) | copy-start | bytes 1572868
  66.0 17.4 %collective-permute-start.10 = (bf16[1024,512]{1,0:T(8,128)(2,1)S(1)}, bf16[1024,512]{1,0:T(8,128)(2,1)S(1)}, u32[]{:S(2)}, u32[]{:S(2)}) collective-permute-start(bf16[1024,512]{1,0:T(8,128)(2,1)S(1)} %get-tuple-element.61), channel_id=1, source_target_pairs={{0,1},{1,0},{2,3},{3,2},{4,5},{5,4},{6,7},{7,6},{8,9},{9,8},{10,11... | collective-permute-start | bytes 3145736 | tf_op jit(solution)/shard_map/ppermute | solution.py:473
  66.2 4.5 %collective-permute-start.17 = (bf16[512,256]{1,0:T(8,128)(2,1)S(1)}, bf16[512,256]{1,0:T(8,128)(2,1)S(1)}, u32[]{:S(2)}, u32[]{:S(2)}) collective-permute-start(bf16[512,256]{1,0:T(8,128)(2,1)S(1)} %shard_map.131.refs_1_), channel_id=1, source_target_pairs={{0,1},{1,0},{2,3},{3,2},{4,8},{5,9},{6,10},{7,11},{8,4},{9,5},{10,... | collective-permute-start | bytes 786440 | tf_op jit(solution)/shard_map/ppermute | solution.py:576
  67.1 9.7 %collective-permute-start.21 = (bf16[512,256]{1,0:T(8,128)(2,1)S(1)}, bf16[512,256]{1,0:T(8,128)(2,1)S(1)}, u32[]{:S(2)}, u32[]{:S(2)}) collective-permute-start(bf16[512,256]{1,0:T(8,128)(2,1)S(1)} %shard_map.134.refs_1_), channel_id=1, source_target_pairs={{0,1},{1,0},{2,3},{3,2},{4,8},{5,9},{6,10},{7,11},{8,4},{9,5},{10,... | collective-permute-start | bytes 786440 | tf_op jit(solution)/shard_map/ppermute | solution.py:576
  67.3 14.2 %collective-permute-start.14 = (bf16[512,256]{1,0:T(8,128)(2,1)S(1)}, bf16[512,256]{1,0:T(8,128)(2,1)S(1)}, u32[]{:S(2)}, u32[]{:S(2)}) collective-permute-start(bf16[512,256]{1,0:T(8,128)(2,1)S(1)} %get-tuple-element.62), channel_id=1, source_target_pairs={{0,4},{4,0},{8,12},{12,8},{1,5},{5,1},{9,13},{13,9},{2,6},{6,2},{1... | collective-permute-start | bytes 786440 | tf_op jit(solution)/shard_map/ppermute | solution.py:473
  70.8 19.1 %collective-permute-start.18 = (bf16[512,256]{1,0:T(8,128)(2,1)S(1)}, bf16[512,256]{1,0:T(8,128)(2,1)S(1)}, u32[]{:S(2)}, u32[]{:S(2)}) collective-permute-start(bf16[512,256]{1,0:T(8,128)(2,1)S(1)} %get-tuple-element.65), channel_id=1, source_target_pairs={{0,4},{4,0},{8,12},{12,8},{1,5},{5,1},{9,13},{13,9},{2,6},{6,2},{1... | collective-permute-start | bytes 786440 | tf_op jit(solution)/shard_map/ppermute | solution.py:473
  76.9 10.4 %collective-permute-start.22 = (bf16[512,256]{1,0:T(8,128)(2,1)S(1)}, bf16[512,256]{1,0:T(8,128)(2,1)S(1)}, u32[]{:S(2)}, u32[]{:S(2)}) collective-permute-start(bf16[512,256]{1,0:T(8,128)(2,1)S(1)} %get-tuple-element.68), channel_id=1, source_target_pairs={{0,4},{4,0},{8,12},{12,8},{1,5},{5,1},{9,13},{13,9},{2,6},{6,2},{1... | collective-permute-start | bytes 786440 | tf_op jit(solution)/shard_map/ppermute | solution.py:473
  81.6 5.8 %collective-permute-start.23 = (bf16[512,256]{1,0:T(8,128)(2,1)S(1)}, bf16[512,256]{1,0:T(8,128)(2,1)S(1)}, u32[]{:S(2)}, u32[]{:S(2)}) collective-permute-start(bf16[512,256]{1,0:T(8,128)(2,1)S(1)} %shard_map.136.refs_0_), channel_id=1, source_target_pairs={{0,1},{1,0},{2,3},{3,2},{4,8},{5,9},{6,10},{7,11},{8,4},{9,5},{10,... | collective-permute-start | bytes 786440 | tf_op jit(solution)/shard_map/ppermute | solution.py:576
  81.9 14.8 %collective-permute-start.5 = (bf16[1024,256]{1,0:T(8,128)(2,1)S(1)}, bf16[1024,256]{1,0:T(8,128)(2,1)S(1)}, u32[]{:S(2)}, u32[]{:S(2)}) collective-permute-start(bf16[1024,256]{1,0:T(8,128)(2,1)S(1)} %add_convert_fusion.4), channel_id=1, source_target_pairs={{0,2},{1,3},{2,0},{3,1},{4,6},{5,7},{6,4},{7,5},{8,10},{9,11},{10,... | collective-permute-start | bytes 1572872 | tf_op jit(solution)/shard_map/ppermute | solution.py:473
  83.6 23.9 %collective-permute-start.11 = (bf16[1024,256]{1,0:T(8,128)(2,1)S(1)}, bf16[1024,256]{1,0:T(8,128)(2,1)S(1)}, u32[]{:S(2)}, u32[]{:S(2)}) collective-permute-start(bf16[1024,256]{1,0:T(8,128)(2,1)S(1)} %add_convert_fusion.1), channel_id=1, source_target_pairs={{0,2},{1,3},{2,0},{3,1},{4,6},{5,7},{6,4},{7,5},{8,10},{9,11},{10,... | collective-permute-start | bytes 1572872 | tf_op jit(solution)/shard_map/ppermute | solution.py:473
  87.4 20.4 %collective-permute-start.27 = (bf16[512,256]{1,0:T(8,128)(2,1)S(1)}, bf16[512,256]{1,0:T(8,128)(2,1)S(1)}, u32[]{:S(2)}, u32[]{:S(2)}) collective-permute-start(bf16[512,256]{1,0:T(8,128)(2,1)S(1)} %shard_map.140.refs_0_), channel_id=1, source_target_pairs={{0,1},{1,0},{2,3},{3,2},{4,8},{5,9},{6,10},{7,11},{8,4},{9,5},{10,... | collective-permute-start | bytes 786440 | tf_op jit(solution)/shard_map/ppermute | solution.py:576
  87.5 20.4 %collective-permute-start.24 = (bf16[512,256]{1,0:T(8,128)(2,1)S(1)}, bf16[512,256]{1,0:T(8,128)(2,1)S(1)}, u32[]{:S(2)}, u32[]{:S(2)}) collective-permute-start(bf16[512,256]{1,0:T(8,128)(2,1)S(1)} %shard_map.137), channel_id=1, source_target_pairs={{0,4},{4,0},{8,12},{12,8},{1,5},{5,1},{9,13},{13,9},{2,6},{6,2},{1... | collective-permute-start | bytes 786440 | tf_op jit(solution)/shard_map/ppermute | solution.py:473
  96.9 10.8 %copy-start.6 = (bf16[1024,256]{1,0:T(8,128)(2,1)}, bf16[1024,256]{1,0:T(8,128)(2,1)S(1)}, u32[]{:S(2)}) copy-start(bf16[1024,256]{1,0:T(8,128)(2,1)S(1)} %add_convert_fusion.3.refs_2_) | copy-start | bytes 1572868
  97.8 10.1 %collective-permute-start.25 = (bf16[512,256]{1,0:T(8,128)(2,1)S(1)}, bf16[512,256]{1,0:T(8,128)(2,1)S(1)}, u32[]{:S(2)}, u32[]{:S(2)}) collective-permute-start(bf16[512,256]{1,0:T(8,128)(2,1)S(1)} %shard_map.138.refs_0_), channel_id=1, source_target_pairs={{0,1},{1,0},{2,3},{3,2},{4,8},{5,9},{6,10},{7,11},{8,4},{9,5},{10,... | collective-permute-start | bytes 786440 | tf_op jit(solution)/shard_map/ppermute | solution.py:576
  107.7 9.4 %copy-start.7 = (bf16[1024,256]{1,0:T(8,128)(2,1)}, bf16[1024,256]{1,0:T(8,128)(2,1)S(1)}, u32[]{:S(2)}) copy-start(bf16[1024,256]{1,0:T(8,128)(2,1)S(1)} %add_convert_fusion.refs_2_) | copy-start | bytes 1572868
  107.8 9.3 %collective-permute-start.28 = (bf16[512,256]{1,0:T(8,128)(2,1)S(1)}, bf16[512,256]{1,0:T(8,128)(2,1)S(1)}, u32[]{:S(2)}, u32[]{:S(2)}) collective-permute-start(bf16[512,256]{1,0:T(8,128)(2,1)S(1)} %shard_map.141), channel_id=1, source_target_pairs={{0,4},{4,0},{8,12},{12,8},{1,5},{5,1},{9,13},{13,9},{2,6},{6,2},{1... | collective-permute-start | bytes 786440 | tf_op jit(solution)/shard_map/ppermute | solution.py:473
  108.0 13.4 %collective-permute-start.26 = (bf16[512,256]{1,0:T(8,128)(2,1)S(1)}, bf16[512,256]{1,0:T(8,128)(2,1)S(1)}, u32[]{:S(2)}, u32[]{:S(2)}) collective-permute-start(bf16[512,256]{1,0:T(8,128)(2,1)S(1)} %shard_map.139), channel_id=1, source_target_pairs={{0,4},{4,0},{8,12},{12,8},{1,5},{5,1},{9,13},{13,9},{2,6},{6,2},{1... | collective-permute-start | bytes 786440 | tf_op jit(solution)/shard_map/ppermute | solution.py:473
  (1 other events, 0.8 us)

commit v6 on v5

--- a/solution.py
+++ b/solution.py
@@ -27,8 +27,8 @@
     return pltpu.CompilerParams(vmem_limit_bytes=mib * MIB)
 
 
-def cost(flops, moved, exps=0):
-    return pl.CostEstimate(flops=int(flops), bytes_accessed=int(moved), transcendentals=int(exps))
+def cost(microseconds):
+    return pl.CostEstimate(flops=int(microseconds * 1150e6) + 1, bytes_accessed=1, transcendentals=0)
 
 
 def run(body, ready, after=(), in_specs=None, **options):
@@ -128,7 +128,7 @@
         + [pltpu.VMEM(dims, BF16) for dims in held]
         + [pltpu.SemaphoreType.DMA((parts + 2,)), pltpu.SemaphoreType.DMA((len(held),))],
         compiler_params=params(56),
-        cost_estimate=cost(4 * tok_rows * width * inner, 2 * tok_rows * width + 8 * width * inner),
+        cost_estimate=cost(5.0),
     )(tokens, w_key, w_value)
 
 
@@ -136,7 +136,7 @@
     out_ref[...] = dot(left_ref[...], weight_ref[...]).astype(BF16)
 
 
-def project(left, weight, after=()):
+def project(left, weight, after):
     tok_rows, width = left.shape
     inner = weight.shape[1]
     return run(
@@ -145,7 +145,7 @@
         after,
         out_shape=shape(tok_rows, inner),
         compiler_params=params(4),
-        cost_estimate=cost(2 * tok_rows * width * inner, 2 * tok_rows * width + 4 * width * inner),
+        cost_estimate=cost(0.7),
     )
 
 
@@ -227,7 +227,7 @@
     lax.fori_loop(0, tok_rows // (2 * BLOCK), step, 0)
 
 
-def near_powers(query, levels):
+def near_powers(query, levels, after):
     tok_rows, inner = query.shape
     heads = inner // HEAD_DIM
     pairs = tok_rows // (2 * BLOCK)
@@ -235,9 +235,10 @@
     return run(
         functools.partial(near_body, len(levels)),
         [query, *levels],
+        after,
         out_shape=[shape(pairs * heads * rows, 2 * BLOCK, F32), shape(2 * heads, tok_rows, F32)],
         compiler_params=params(6),
-        cost_estimate=cost(2 * tok_rows * rows * inner, 12 * tok_rows * inner, tok_rows * rows * 2),
+        cost_estimate=cost(2.3),
     )
 
 
@@ -297,23 +298,22 @@
             shape(2 * heads, tok_rows, F32),
         ],
         compiler_params=params(6),
-        cost_estimate=cost(
-            3 * tok_rows * set_rows * inner, 12 * tok_rows * inner, tok_rows * set_rows
-        ),
-    )
-
-
-def backward_body(local_levels, far_bits, *refs):
+        cost_estimate=cost(4.0),
+    )
+
+
+def backward_body(local_levels, far_bits, pieces, *refs):
     mids = local_levels - 1
     fars = len(far_bits)
-    q_ref, g_ref, att_t_ref, stat_ref = refs[:4]
-    level_refs = refs[4 : 4 + local_levels]
-    far_refs = refs[4 + local_levels : 4 + local_levels + fars]
-    outs = refs[4 + local_levels + fars :]
-    dq_ref, dq_t_ref, dkv_ref = outs[:3]
-    dfar_refs = outs[3 : 3 + fars]
-    dmid_refs = outs[3 + fars : 3 + fars + mids]
-    acc_ref = outs[-1]
+    q_ref, g_ref, att_t_ref, stat_ref, tok_ref = refs[:5]
+    level_refs = refs[5 : 5 + local_levels]
+    far_refs = refs[5 + local_levels : 5 + local_levels + fars]
+    outs = refs[5 + local_levels + fars :]
+    dq_ref, dkv_ref = outs[:2]
+    term_refs = outs[2 : 2 + pieces]
+    dfar_refs = outs[2 + pieces : 1 + pieces + fars]
+    dmid_refs = outs[1 + pieces + fars : 1 + pieces + fars + mids]
+    dq_t_ref, acc_ref = outs[-2:]
     tok_rows, inner = q_ref.shape
     heads = inner // HEAD_DIM
     score_scale = 1.0 / math.sqrt(HEAD_DIM)
@@ -350,10 +350,17 @@
         return carry
 
     lax.fori_loop(0, tok_rows // (2 * BLOCK), step, 0)
-    low = 0
+    width = term_refs[-1].shape[0]
+    first = acc_ref[:BLOCK].astype(BF16)
+    term_refs[0][width : width + BLOCK, :] = first[:, :inner]
+    term_refs[0][width + BLOCK :, :] = first[:, inner:]
+    low = BLOCK
     for ref in dfar_refs:
         ref[...] = acc_ref[low : low + ref.shape[0]].astype(BF16)
         low += ref.shape[0]
+    for i, ref in enumerate(term_refs):
+        part = dot(dq_t_ref[...], tok_ref[:, i * width : (i + 1) * width])
+        ref[:width, :] = part.astype(BF16).T
     fan = spread_matrix(2 * BLOCK, 1, 0, BLOCK, 0.5)
     targets = (dkv_ref, *dmid_refs)
     for i in reversed(range(mids)):
@@ -365,23 +372,22 @@
             targets[i][rows, :] += dot(fan, high) + dot(fan, low)
 
 
-def backward(query, grad, attended_t, stats, levels, fars, far_bits, after):
+def backward(query, grad, attended_t, stats, tokens, levels, fars, far_bits, pieces, after):
     tok_rows, inner = query.shape
     far_rows = sum(f.shape[0] for f in fars)
     set_rows = (len(levels) + 1) * BLOCK + far_rows
     return run(
-        functools.partial(backward_body, len(levels), far_bits),
-        [query, grad, attended_t, stats, *levels, *fars],
-        after,
-        out_shape=[shape(tok_rows, inner), shape(inner, tok_rows)]
-        + [shape(tok_rows, 2 * inner, F32)]
-        + [shape(*f.shape) for f in fars],
+        functools.partial(backward_body, len(levels), far_bits, pieces),
+        [query, grad, attended_t, stats, tokens, *levels, *fars],
+        after,
+        out_shape=[shape(tok_rows, inner), shape(tok_rows, 2 * inner, F32)]
+        + [shape(tokens.shape[1] // pieces + 2 * BLOCK, inner)]
+        + [shape(tokens.shape[1] // pieces, inner)] * (pieces - 1)
+        + [shape(*f.shape) for f in fars[1:]],
         scratch_shapes=[pltpu.VMEM(level.shape, F32) for level in levels[1:]]
-        + [pltpu.VMEM((far_rows, 2 * inner), F32)],
+        + [pltpu.VMEM((inner, tok_rows), BF16), pltpu.VMEM((far_rows, 2 * inner), F32)],
         compiler_params=params(10),
-        cost_estimate=cost(
-            10 * tok_rows * set_rows * inner, 24 * tok_rows * inner, tok_rows * set_rows * 2
-        ),
+        cost_estimate=cost(8.0),
     )
 
 
@@ -400,22 +406,25 @@
         after,
         out_shape=shape(width, inner),
         compiler_params=params(3),
-        cost_estimate=cost(2 * inner * tok_rows * width, 2 * tok_rows * (width + inner)),
+        cost_estimate=cost(0.5),
     )
 
 
 def close_body(local_levels, far_bits, dkv_ref, *refs):
-    back_refs = refs[: len(far_bits)]
+    joined_ref, *back_refs = refs[: len(far_bits)]
     dk_ref, dv_ref, dkv_t_ref = refs[len(far_bits) :]
     inner = dk_ref.shape[1]
     tile = 2 * BLOCK
+    low = joined_ref.shape[0] - 2 * BLOCK
+    joined = [joined_ref[low : low + BLOCK, :], joined_ref[low + BLOCK :, :]]
+    backs = [jnp.concatenate(joined, axis=1)] + [ref[...] for ref in back_refs]
     for t in range(dkv_ref.shape[0] // tile):
         here = slice(t * tile, (t + 1) * tile)
         total = dkv_ref[here, :]
-        for ref, bit in zip(back_refs, far_bits):
+        for back, bit in zip(backs, far_bits):
             weight = 0.5 ** (local_levels + bit)
-            fan = spread_matrix(tile, local_levels + bit, t * tile, ref.shape[0], weight)
-            total = total + dot(fan, ref[...])
+            fan = spread_matrix(tile, local_levels + bit, t * tile, back.shape[0], weight)
+            total = total + dot(fan, back)
         final = total.astype(BF16)
         dk_ref[here, :] = final[:, :inner]
         dv_ref[here, :] = final[:, inner:]
@@ -431,7 +440,7 @@
         after,
         out_shape=[shape(tok_rows, inner), shape(tok_rows, inner), shape(double, tok_rows)],
         compiler_params=params(5),
-        cost_estimate=cost(2 * tok_rows * 256 * double, 12 * tok_rows * double),
+        cost_estimate=cost(1.8),
     )
 
 
@@ -464,7 +473,7 @@
         + [pl.BlockSpec(memory_space=pltpu.VMEM)] * (2 * count),
         out_shape=[shape(tok_rows, width // 2)] * 2,
         compiler_params=params(5),
-        cost_estimate=cost(2 * count * tok_rows * inner * width, 2 * tok_rows * width),
+        cost_estimate=cost(1.0),
     )
 
 
@@ -477,35 +486,59 @@
     return (left.astype(F32) + right.astype(F32)).astype(BF16)
 
 
-def scatter_sum(keep, send, axis):
-    parts = lax.axis_size(axis) // 2
-    width = keep.shape[1] // parts
-    pieces = [keep[:, i * width : (i + 1) * width] for i in range(parts)]
-    distance = 1
-    while True:
-        into = exchange(send, axis, distance)
-        for i in reversed(range(len(pieces))):
-            pieces[i] = add(pieces[i], into[:, i * width : (i + 1) * width])
-        if len(pieces) == 1:
-            return pieces[0]
-        away = pieces[1::2]
-        send = away[0] if len(away) == 1 else jnp.concatenate(away, axis=1)
-        pieces = pieces[0::2]
-        distance *= 2
-
-
-def half_body(chunk_ref, into_ref, out_ref):
-    out_ref[...] = (chunk_ref[...].astype(F32) + into_ref[...].astype(F32)).astype(BF16)
-
-
-def half_sum(chunk, into, after=()):
-    return run(
-        half_body,
+def term_half_body(chunk_ref, into_ref, out_ref):
+    rows = slice(0, out_ref.shape[0])
+    out_ref[...] = (chunk_ref[rows, :].astype(F32) + into_ref[rows, :].astype(F32)).astype(BF16)
+
+
+def half_sum(chunk, into, rows, after):
+    return run(
+        term_half_body,
         [chunk, into],
         after,
-        out_shape=shape(*chunk.shape),
-        compiler_params=params(2),
-        cost_estimate=cost(chunk.size, 6 * chunk.size),
+        out_shape=shape(rows, chunk.shape[1]),
+        compiler_params=params(3),
+        cost_estimate=cost(0.1),
+    )
+
+
+def pair_half_body(chunk_ref, into_ref, *out_refs):
+    rows = out_refs[0].shape[0]
+    for i, ref in enumerate(out_refs):
+        here = slice(i * rows, (i + 1) * rows)
+        ref[...] = (chunk_ref[here, :].astype(F32) + into_ref[here, :].astype(F32)).astype(BF16)
+
+
+def half_sums(chunk, into, count, after):
+    rows = chunk.shape[0] // count
+    return run(
+        pair_half_body,
+        [chunk, into],
+        after,
+        out_shape=[shape(rows, chunk.shape[1])] * count,
+        compiler_params=params(3),
+        cost_estimate=cost(0.2),
+    )
+
+
+def scatter_body(pieces, keep_ref, into_ref, even_ref, odd_ref):
+    width = keep_ref.shape[1] // pieces
+    for i in range(pieces):
+        here = slice(i * width, (i + 1) * width)
+        place = slice(i // 2 * width, (i // 2 + 1) * width)
+        total = keep_ref[:, here].astype(F32) + into_ref[:, here].astype(F32)
+        (even_ref, odd_ref)[i % 2][:, place] = total.astype(BF16)
+
+
+def scatter_step(keep, into, pieces, after):
+    rows, width = keep.shape
+    return run(
+        functools.partial(scatter_body, pieces),
+        [keep, into],
+        after,
+        out_shape=[shape(rows, width // 2)] * 2,
+        compiler_params=params(4),
+        cost_estimate=cost(0.2),
     )
 
 
@@ -522,7 +555,7 @@
         send_ref[...] = total
 
 
-def turn(end, half, across, chunk, after=()):
+def turn(end, half, across, chunk, after):
     return run(
         turn_body,
         [end, half, across, chunk],
@@ -531,20 +564,60 @@
         + [pl.BlockSpec(memory_space=pltpu.VMEM)] * 3,
         out_shape=[shape(*half.shape)] * 2,
         compiler_params=params(2),
-        cost_estimate=cost(half.size, 10 * half.size),
+        cost_estimate=cost(0.1),
+    )
+
+
+def output_body(count, end_ref, *refs):
+    totals, ends, out_ref = refs[:count], refs[count : 2 * count], refs[-1]
+    rows = totals[0].shape[0]
+
+    for flag, sources in ((0, totals), (1, ends)):
+
+        @pl.when(end_ref[0] == flag)
+        def _():
+            for i, ref in enumerate(sources):
+                out_ref[i * rows : (i + 1) * rows, :] = ref[...]
+
+
+def output(end, totals, ends, after):
+    count = len(totals)
+    rows, width = totals[0].shape
+    return run(
+        functools.partial(output_body, count),
+        [end, *totals, *ends],
+        after,
+        in_specs=[pl.BlockSpec(memory_space=pltpu.SMEM)]
+        + [pl.BlockSpec(memory_space=pltpu.VMEM)] * (2 * count),
+        out_shape=shape(count * rows, width),
+        compiler_params=params(4),
+        cost_estimate=cost(0.9),
+    )
+
+
+def relay_body(source_ref, target_ref):
+    target_ref[...] = source_ref[...]
+
+
+def relay(block, after):
+    return run(
+        relay_body,
+        [block],
+        after,
+        out_shape=shape(*block.shape),
+        compiler_params=params(3),
+        cost_estimate=cost(0.2),
     )
 
 
 class Line:
     lag = 3
 
-    def __init__(self, axis, other):
-        self.axes = (axis, other)
-        self.axis = axis
+    def __init__(self, axis, other, step):
+        self.axis, self.axes, self.step = axis, (axis, other), step
         self.count = lax.axis_size(axis)
         rank = jnp.bitwise_and(lax.axis_index(axis), 3)
-        self.at_end = (rank == 0) | (rank == 3)
-        self.end = jnp.reshape(self.at_end, (1,)).astype(jnp.int32)
+        self.end = jnp.reshape((rank == 0) | (rank == 3), (1,)).astype(jnp.int32)
         width = lax.axis_size(other)
         self.across = []
         for place in range(self.count):
@@ -553,43 +626,69 @@
                 if place & 3 in (1, 2):
                     target = (place ^ 3, seat)
                 self.across.append((place * width + seat, target[0] * width + target[1]))
-        self.chunks, self.halves, self.crossed, self.totals, self.sums = [], [], [], [], []
-
-    def push(self, chunk, after=(), later=()):
-        k = len(self.chunks)
+        self.chunks, self.into, self.halves, self.crossed, self.totals = [], [], [], [], []
+
+    def enter(self, chunk):
         self.chunks.append(chunk)
-        if self.count < 4:
-            total = add(chunk, exchange(chunk, self.axis, 1)) if self.count == 2 else chunk
-            self.halves.append(total)
-            self.sums.append(total)
-            return
-        send = chunk
-        if k >= self.lag:
-            old = k - self.lag
-            total, send = turn(self.end, self.halves[old], self.crossed[old], chunk, later)
-            self.totals.append(total)
-        into = exchange(send, self.axis, 1)
-        if k >= self.lag:
-            self.receive(into)
-        half = half_sum(chunk, into, after)
+        self.into.append(exchange(chunk, self.axis, 1))
+
+    def enter_whole(self, whole, count):
+        self.whole = whole, exchange(whole, self.axis, 1), count
+        self.chunks += [None] * count
+        self.into += [None] * count
+
+    def meet_whole(self):
+        for half in self.step(half_sums, *self.whole):
+            self.halves.append(half)
+            self.crossed.append(lax.ppermute(half, self.axes, self.across))
+
+    def meet(self, rows):
+        k = len(self.halves)
+        half = self.step(half_sum, self.chunks[k], self.into[k], rows)
         self.halves.append(half)
         self.crossed.append(lax.ppermute(half, self.axes, self.across))
 
-    def receive(self, into):
-        result = jnp.where(self.at_end, into, self.totals[len(self.sums)])
+    def turn(self, chunk):
+        old = len(self.totals)
+        total, send = self.step(turn, self.end, self.halves[old], self.crossed[old], chunk)
+        self.totals.append(total)
+        self.chunks.append(chunk)
+        self.into.append(exchange(send, self.axis, 1))
+
+    def leave(self):
+        old = len(self.totals)
+        half = self.halves[old]
+        total = self.step(half_sum, half, self.crossed[old], half.shape[0])
+        self.totals.append(total)
+        self.into.append(exchange(total, self.axis, 1))
+
+    def output(self, first, count):
+        ends = self.into[first + self.lag : first + self.lag + count]
+        result = self.step(output, self.end, self.totals[first : first + count], ends)
         distance = 4
         while distance < self.count:
             result = add(result, exchange(result, self.axis, distance))
             distance *= 2
-        self.sums.append(result)
-
-    def finish(self, last):
-        while len(self.sums) < len(self.chunks):
-            old = len(self.sums)
-            after = last if old == len(self.chunks) - 1 else ()
-            self.totals.append(half_sum(self.halves[old], self.crossed[old], after))
-            self.receive(exchange(self.totals[old], self.axis, 1))
-        return self.sums
+        return result
+
+
+class Scatter:
+    def __init__(self, parts, axis, step):
+        self.axis, self.step = axis, step
+        self.pieces = lax.axis_size(axis) // 2
+        self.keep, send = parts
+        self.distance = 1
+        self.into = exchange(send, axis, 1)
+
+    def advance(self):
+        while self.pieces > 1:
+            self.keep, send = self.step(scatter_step, self.keep, self.into, self.pieces)
+            self.distance *= 2
+            self.pieces //= 2
+            self.into = exchange(send, self.axis, self.distance)
+
+    def result(self):
+        return self.step(half_sum, self.keep, self.into, self.keep.shape[0])
 
 
 def per_device(tokens, w_query, w_key, w_value, w_out, cotangent):
@@ -600,50 +699,64 @@
     far_levels = count.bit_length() - 1
     far_bits = [d.bit_length() - 1 for d in range(1, count)]
 
+    last = []
+
+    def step(kernel, *operands):
+        made = kernel(*operands, list(last))
+        last[:] = made[:1] if isinstance(made, (list, tuple)) else [made]
+        return made
+
     parts = key_value(tokens, w_key, w_value, local_levels, far_levels)
     levels, tops = parts[:local_levels], parts[local_levels:]
     fars = [exchange(tops[bit], "seq", d) for d, bit in enumerate(far_bits, 1)]
-    query = project(tokens, w_query)
-    powers, near = near_powers(query, levels)
-    grad = project(cotangent, w_out, [near])
-    attended, attended_t, stats = forward(query, powers, near, levels, fars, far_bits, [grad])
+    query = step(project, tokens, w_query)
+    powers, near = step(near_powers, query, levels)
+    grad = step(project, cotangent, w_out)
+    attended, attended_t, stats = step(forward, query, powers, near, levels, fars, far_bits)
+
+    line = Line("seq", "head", step)
     pieces = 2
-    line = Line("seq", "head")
-
-    def terms(left, which, right, after):
-        chunks = []
-        for p in range(pieces):
-            chunks.append(weight_terms(left, right, inner, which, p, pieces, after))
-            after = chunks[-1:]
-        return chunks
-
-    chunks = terms(attended_t, 0, cotangent, [])
-    line.push(chunks[0])
-    line.push(chunks[1])
-    dquery, dquery_t, dkv, *dfars = backward(
-        query, grad, attended_t, stats, levels, fars, far_bits, chunks
-    )
-    backs = [exchange(piece, "seq", d) for d, piece in enumerate(dfars, 1)]
-    chunks = terms(dquery_t, 0, tokens, line.halves[:1])
-    line.push(chunks[0])
-    keep, send = project_split([attended], [w_out], "head", chunks)
-    mixed = scatter_sum(keep, send, "head")
-    dkey, dvalue, dkv_t = close_keys(
-        dkv, backs, far_bits, local_levels, [keep, line.halves[1]]
-    )
-    line.push(chunks[1])
-    chunks = terms(dkv_t, 0, tokens, [])
-    line.push(chunks[0])
-    line.push(chunks[1])
-    chunks = terms(dkv_t, 1, tokens, chunks)
-    line.push(chunks[0], [mixed])
-    keep, send = project_split([dquery, dkey, dvalue], [w_query, w_key, w_value], "head", chunks)
-    tokens_grad = scatter_sum(keep, send, "head")
-    line.push(chunks[1])
-    sums = line.finish([tokens_grad])
-    out_grad, query_grad, key_grad, value_grad = (
-        jnp.concatenate(sums[i : i + pieces], axis=0) for i in range(0, len(sums), pieces)
-    )
+    rows = tokens.shape[1] // pieces
+    line.enter_whole(step(weight_terms, attended_t, cotangent, inner, 0, 0, 1), pieces)
+    dquery, dkv, query_first, query_second, *away = step(
+        backward, query, grad, attended_t, stats, tokens, levels, fars, far_bits, pieces
+    )
+    line.enter(query_first)
+    backs = [exchange(piece, "seq", d) for d, piece in enumerate(away, 2)]
+    line.meet_whole()
+    line.turn(query_second)
+    dkey, dvalue, dkv_t = step(
+        close_keys, dkv, [line.into[2], *backs], far_bits, local_levels
+    )
+    key_first = step(weight_terms, dkv_t, tokens, inner, 0, 0, pieces)
+    line.meet(rows)
+    line.turn(key_first)
+    line.meet(rows)
+    parts = step(project_split, [attended], [w_out], "head")
+    mixed = Scatter(parts, "head", step)
+    key_second = step(weight_terms, dkv_t, tokens, inner, 0, 1, pieces)
+    value_first = step(weight_terms, dkv_t, tokens, inner, 1, 0, pieces)
+    value_second = step(weight_terms, dkv_t, tokens, inner, 1, 1, pieces)
+    keep, send = step(project_split, [dquery, dkey, dvalue], [w_query, w_key, w_value], "head")
+    line.turn(key_second)
+    line.meet(rows)
+    tokens_grad = Scatter([keep, step(relay, send)], "head", step)
+    line.turn(value_first)
+    line.meet(rows)
+    mixed.advance()
+    line.turn(value_second)
+    tokens_grad.advance()
+    out_grad = line.output(0, pieces)
+    line.meet(rows)
+    line.leave()
+    query_grad = line.output(2, pieces)
+    line.meet(rows)
+    mixed = mixed.result()
+    line.leave()
+    line.leave()
+    tokens_grad = tokens_grad.result()
+    key_grad = line.output(4, pieces)
+    value_grad = line.output(6, pieces)
     return mixed, tokens_grad, query_grad, key_grad, value_grad, out_grad
 
 

time: 123 us -> 110 us (0.89)
  waiting for transfers between devices: 46 us -> 16 us
  starting transfers between devices: 36.6 us -> 45.7 us
  local copies, waits for them, and re-layouts: 1.31 us -> 9.88 us
  Pallas kernels: 32.8 us -> 37.1 us
  other arithmetic: 4.27 us -> 0 us
    ppermute x21 -> x19, waiting for transfers between devices: 46 us -> 14.8 us  [exchange(): return lax.ppermute(block, axis, [(i, i ^ distance) for i in range(count)])]
    ppermute x21 -> x19, starting transfers between devices: 35.6 us -> 45.4 us  [exchange(): return lax.ppermute(block, axis, [(i, i ^ distance) for i in range(count)])]
    unnamed x40 -> x46, local copies, waits for them, and re-layouts: 1.31 us -> 9.88 us
    pallas_call x32 -> x37, Pallas kernels: 27.4 us -> 31.6 us  [run(): return pl.pallas_call(kernel, in_specs=in_specs, **options)(*ready, *after)]
    concatenate x4 -> x0, other arithmetic: 3.36 us -> none  [per_device(): jnp.concatenate(sums[i:i + pieces], axis=0)]
  transfers between devices with their start and end apart: 29 -> 27, of which waited for: 11 -> 9; matrix products, arithmetic and copies ran while one was open for 3% -> 0% of each run, Pallas kernels for 19% -> 24%
where the time goes in v6:
time: 110 us
  starting transfers between devices  45.7 us (42%)
  Pallas kernels  37.1 us (34%)
  waiting for transfers between devices  16 us (15%)
  local copies, waits for them, and re-layouts  9.88 us (9%)
  between operations  1.12 us (1%)
    ppermute x19, starting transfers between devices, exchange(): return lax.ppermute(block, axis, [(i, i ^ distance) for i in range(count)])  45.4 us
    pallas_call x37, Pallas kernels, run(): return pl.pallas_call(kernel, in_specs=in_specs, **options)(*ready, *after)  31.6 us
    ppermute x19, waiting for transfers between devices, exchange(): return lax.ppermute(block, axis, [(i, i ^ distance) for i in range(count)])  14.8 us
    unnamed x46, local copies, waits for them, and re-layouts  9.88 us
    pallas_call x1, Pallas kernels, key_value(): pl.pallas_call(functools.partial(key_value_body, local_levels, far_levels...  5.45 us
  transfers between devices with their start and end apart: 27, of which 9 were waited for; matrix products, arithmetic and copies ran while one was open for 0% of the time, Pallas kernels for 24%

profile of v6, /device:TPU:0, one launch (start us, length us, event | category | flops | bytes accessed | tf_op | source)
XLA Modules:
  0.0 109.8 jit_solution(75309560379068938)
XLA Ops:
  0.7 5.5 %shard_map.110 = (bf16[1024,512]{1,0:T(8,128)(2,1)}, bf16[512,512]{1,0:T(8,128)(2,1)}, bf16[256,512]{1,0:T(8,128)(2,1)}, bf16[128,512]{1,0:T(8,128)(2,1)}, bf16[64,512]{1,0:T(8,128)(2,1)}) custom-call(bf16[1024,1024]{1,0:T(8,128)(2,1)} %refs_1_.13, bf16[1024,256]{1,0:T(8,128)(2,1)} %refs_5_.1, bf16[1024,256]{1,0:T(8,128)(2,1)} %refs_6_.1), custom_call_target="tpu_custom_call" | custom-call | flops 5750000128 | bytes 1 | tf_op jit(solution)/shard_map/pallas_call | solution.py:120
  6.1 4.1 %collective-permute-start.1 = (bf16[64,512]{1,0:T(8,128)(2,1)}, bf16[64,512]{1,0:T(8,128)(2,1)S(1)}, u32[]{:S(2)}, u32[]{:S(2)}) collective-permute-start(bf16[64,512]{1,0:T(8,128)(2,1)} %get-tuple-element.51), channel_id=1, source_target_pairs={{0,8},{4,12},{8,0},{12,4},{1,9},{5,13},{9,1},{13,5},{2,10},{6,14},... | collective-permute-start | bytes 196616 | tf_op jit(solution)/shard_map/ppermute | solution.py:482
  10.3 1.3 %collective-permute-start.2 = (bf16[64,512]{1,0:T(8,128)(2,1)}, bf16[64,512]{1,0:T(8,128)(2,1)S(1)}, u32[]{:S(2)}, u32[]{:S(2)}) collective-permute-start(bf16[64,512]{1,0:T(8,128)(2,1)} %get-tuple-element.51), channel_id=1, source_target_pairs={{0,12},{4,8},{8,4},{12,0},{1,13},{5,9},{9,5},{13,1},{2,14},{6,10},... | collective-permute-start | bytes 196616 | tf_op jit(solution)/shard_map/ppermute | solution.py:482
  11.8 0.7 shard_map.109.refs_0_.refs_4_
  12.6 2.3 %shard_map.111 = (f32[4096,256]{1,0:T(8,128)S(1)}, f32[4,1024]{1,0:T(4,128)S(1)}) custom-call(bf16[1024,256]{1,0:T(8,128)(2,1)S(1)} %shard_map.109.refs_0_.refs_4_, bf16[1024,512]{1,0:T(8,128)(2,1)S(1)} %copy-done.20, bf16[512,512]{1,0:T(8,128)(2,1)S(1)} %copy-done.21, bf16[256,512]{1,0:T(8,128)(2,1)S(1)} %copy-done.22, ...), custom_call_target="tpu_custom_call" | custom-call | flops 2644999936 | bytes 1 | tf_op jit(solution)/shard_map/pallas_call | solution.py:42
  15.0 0.7 shard_map.112.refs_9_.refs_1_
  15.7 1.6 %collective-permute-done.2.refs_8_.refs_10_ = bf16[64,512]{1,0:T(8,128)(2,1)S(1)} collective-permute-done((bf16[64,512]{1,0:T(8,128)(2,1)}, bf16[64,512]{1,0:T(8,128)(2,1)S(1)}, u32[]{:S(2)}, u32[]{:S(2)}) %collective-permute-start.2) | collective-permute-done | bytes 65568 | tf_op jit(solution)/shard_map/ppermute | solution.py:482
  18.0 3.9 %shard_map.113 = (bf16[1024,256]{1,0:T(8,128)(2,1)S(1)}, bf16[256,1024]{1,0:T(8,128)(2,1)S(1)}, f32[4,1024]{1,0:T(4,128)S(1)}) custom-call(bf16[1024,256]{1,0:T(8,128)(2,1)S(1)} %shard_map.109.refs_0_.refs_4_, f32[4096,256]{1,0:T(8,128)S(1)} %get-tuple-element.48.refs_2_.refs_1_, f32[4,1024]{1,0:T(4,128)S(1)} %get-tuple-element.49.refs_2_, ...), custom_call_target="tpu_custom_call" | custom-call | flops 4600000000 | bytes 1 | tf_op jit(solution)/shard_map/pallas_call | solution.py:42
  21.9 0.8 shard_map.114.refs_11_.refs_0_
  22.7 1.0 collective-permute-start.3
  23.7 7.5 %shard_map.115 = (bf16[1024,256]{1,0:T(8,128)(2,1)S(1)}, f32[1024,512]{1,0:T(8,128)S(1)}, bf16[768,256]{1,0:T(8,128)(2,1)S(1)}, bf16[512,256]{1,0:T(8,128)(2,1)S...) custom-call(bf16[1024,256]{1,0:T(8,128)(2,1)S(1)} %shard_map.109.refs_0_.refs_4_, ...), custom_call_target="tpu_custom_call" | custom-call | flops 9200000000 | bytes 1 | tf_op jit(solution)/shard_map/pallas_call | solution.py:42
  31.2 1.3 %copy-done.18 = f32[1024,512]{1,0:T(8,128)} copy-done((f32[1024,512]{1,0:T(8,128)}, f32[1024,512]{1,0:T(8,128)S(1)}, u32[]{:S(2)}) %copy-start.18) | copy-done | bytes 2097176
  32.5 1.1 %collective-permute-start.7 = (bf16[768,256]{1,0:T(8,128)(2,1)S(1)}, bf16[768,256]{1,0:T(8,128)(2,1)}, u32[]{:S(2)}, u32[]{:S(2)}) collective-permute-start(bf16[768,256]{1,0:T(8,128)(2,1)S(1)} %get-tuple-element.61.refs_0_), channel_id=1, source_target_pairs={{0,4},{4,0},{8,12},{12,8},{1,5},{5,1},{9,13},{13,9},{2,6},{6,2},{1... | collective-permute-start | bytes 1179656 | tf_op jit(solution)/shard_map/ppermute | solution.py:482
  33.6 2.9 %collective-permute-done.3.refs_1_ = bf16[1024,256]{1,0:T(8,128)(2,1)S(1)} collective-permute-done((bf16[1024,256]{1,0:T(8,128)(2,1)S(1)}, bf16[1024,256]{1,0:T(8,128)(2,1)S(1)}, u32[]{:S(2)}, u32[]{:S(2)}) %collective-permute-start.3) | collective-permute-done | bytes 524320 | tf_op jit(solution)/shard_map/ppermute | solution.py:482
  36.7 0.7 copy-done.13
  37.4 3.4 %collective-permute-start.8 = (bf16[64,512]{1,0:T(8,128)(2,1)}, bf16[64,512]{1,0:T(8,128)(2,1)}, u32[]{:S(2)}, u32[]{:S(2)}) collective-permute-start(bf16[64,512]{1,0:T(8,128)(2,1)} %get-tuple-element.62), channel_id=1, source_target_pairs={{0,8},{4,12},{8,0},{12,4},{1,9},{5,13},{9,1},{13,5},{2,10},{6,14},... | collective-permute-start | bytes 196616 | tf_op jit(solution)/shard_map/ppermute | solution.py:482
  40.8 1.8 %collective-permute-start.9 = (bf16[64,512]{1,0:T(8,128)(2,1)}, bf16[64,512]{1,0:T(8,128)(2,1)}, u32[]{:S(2)}, u32[]{:S(2)}) collective-permute-start(bf16[64,512]{1,0:T(8,128)(2,1)} %get-tuple-element.63), channel_id=1, source_target_pairs={{0,12},{4,8},{8,4},{12,0},{1,13},{5,9},{9,5},{13,1},{2,14},{6,10},... | collective-permute-start | bytes 196616 | tf_op jit(solution)/shard_map/ppermute | solution.py:482
  42.7 1.0 shard_map.117
  43.7 5.5 %collective-permute-start.5 = (bf16[512,256]{1,0:T(8,128)(2,1)S(1)}, bf16[512,256]{1,0:T(8,128)(2,1)S(1)}, u32[]{:S(2)}, u32[]{:S(2)}) collective-permute-start(bf16[512,256]{1,0:T(8,128)(2,1)S(1)} %get-tuple-element.58), channel_id=1, source_target_pairs={{0,4},{4,0},{8,12},{12,8},{1,5},{5,1},{9,13},{13,9},{2,6},{6,2},{1... | collective-permute-start | bytes 786440 | tf_op jit(solution)/shard_map/ppermute | solution.py:482
  49.2 0.7 collective-permute-done.8.refs_2_
  49.9 1.6 %copy-done.19 = f32[1024,512]{1,0:T(8,128)S(1)} copy-done((f32[1024,512]{1,0:T(8,128)S(1)}, f32[1024,512]{1,0:T(8,128)}, u32[]{:S(2)}) %copy-start.19) | copy-done | bytes 2097176
  51.5 2.1 %shard_map.118 = (bf16[1024,256]{1,0:T(8,128)(2,1)S(1)}, bf16[1024,256]{1,0:T(8,128)(2,1)S(1)}, bf16[512,1024]{1,0:T(8,128)(2,1)S(1)}) custom-call(f32[1024,512]{1,0:T(8,128)S(1)} %copy-done.19, bf16[768,256]{1,0:T(8,128)(2,1)} %collective-permute-done.7.refs_1_, bf16[64,512]{1,0:T(8,128)(2,1)} %collective-permute-done.8.refs_2_, ...), custom_call_target="tpu_custom_call" | custom-call | flops 2070000000 | bytes 1 | tf_op jit(solution)/shard_map/pallas_call | solution.py:42
  54.1 1.1 %shard_map.120.refs_4_.refs_1_ = bf16[512,256]{1,0:T(8,128)(2,1)S(1)} custom-call(bf16[768,256]{1,0:T(8,128)(2,1)S(1)} %get-tuple-element.61.refs_0_, bf16[768,256]{1,0:T(8,128)(2,1)} %collective-permute-done.7.refs_1_, bf16[512,256]{1,0:T(8,128)(2,1)S(1)} %shard_map.119.refs_2_.refs_3_.refs_0_), custom_call_target="tpu_custom_call" | custom-call | flops 115000000 | bytes 1 | tf_op jit(solution)/shard_map/pallas_call | solution.py:42
  55.6 3.8 %collective-permute-start.14 = (bf16[512,256]{1,0:T(8,128)(2,1)S(1)}, bf16[512,256]{1,0:T(8,128)(2,1)S(1)}, u32[]{:S(2)}, u32[]{:S(2)}) collective-permute-start(bf16[512,256]{1,0:T(8,128)(2,1)S(1)} %get-tuple-element.74), channel_id=1, source_target_pairs={{0,4},{4,0},{8,12},{12,8},{1,5},{5,1},{9,13},{13,9},{2,6},{6,2},{1... | collective-permute-start | bytes 786440 | tf_op jit(solution)/shard_map/ppermute | solution.py:482
  59.5 0.7 shard_map.123
  62.9 1.8 %shard_map.127 = (bf16[1024,512]{1,0:T(8,128)(2,1)S(1)}, bf16[1024,512]{1,0:T(8,128)(2,1)S(1)}) custom-call(s32[1]{0:T(128)} %bitcast.refs_0_, bf16[1024,256]{1,0:T(8,128)(2,1)S(1)} %copy-done.7, bf16[1024,256]{1,0:T(8,128)(2,1)S(1)} %get-tuple-element.66.refs_2_, bf16[1024,256]{1,0:T(8,128)(2,1)S(1)} %get-tuple-element.70.refs_3_, ...), custom_call_target="tpu_custom_call" | custom-call | flops 1150000000 | bytes 1 | tf_op jit(solution)/shard_map/pallas_call | solution.py:42
  65.6 1.4 %collective-permute-start.12 = (bf16[512,256]{1,0:T(8,128)(2,1)S(1)}, bf16[512,256]{1,0:T(8,128)(2,1)S(1)}, u32[]{:S(2)}, u32[]{:S(2)}) collective-permute-start(bf16[512,256]{1,0:T(8,128)(2,1)S(1)} %get-tuple-element.72), channel_id=1, source_target_pairs={{0,4},{4,0},{8,12},{12,8},{1,5},{5,1},{9,13},{13,9},{2,6},{6,2},{1... | collective-permute-start | bytes 786440 | tf_op jit(solution)/shard_map/ppermute | solution.py:482
  67.0 1.2 %collective-permute-done.13.refs_2_ = bf16[512,256]{1,0:T(8,128)(2,1)S(1)} collective-permute-done((bf16[512,256]{1,0:T(8,128)(2,1)S(1)}, bf16[512,256]{1,0:T(8,128)(2,1)S(1)}, u32[]{:S(2)}, u32[]{:S(2)}) %collective-permute-start.13) | collective-permute-done | bytes 262176 | tf_op jit(solution)/shard_map/ppermute | solution.py:649
  68.3 7.0 %collective-permute-start.18 = (bf16[512,256]{1,0:T(8,128)(2,1)S(1)}, bf16[512,256]{1,0:T(8,128)(2,1)S(1)}, u32[]{:S(2)}, u32[]{:S(2)}) collective-permute-start(bf16[512,256]{1,0:T(8,128)(2,1)S(1)} %get-tuple-element.80), channel_id=1, source_target_pairs={{0,4},{4,0},{8,12},{12,8},{1,5},{5,1},{9,13},{13,9},{2,6},{6,2},{1... | collective-permute-start | bytes 786440 | tf_op jit(solution)/shard_map/ppermute | solution.py:482
  75.7 1.4 %collective-permute-start.15 = (bf16[1024,256]{1,0:T(8,128)(2,1)S(1)}, bf16[1024,256]{1,0:T(8,128)(2,1)S(1)}, u32[]{:S(2)}, u32[]{:S(2)}) collective-permute-start(bf16[1024,256]{1,0:T(8,128)(2,1)S(1)} %get-tuple-element.78), channel_id=1, source_target_pairs={{0,2},{1,3},{2,0},{3,1},{4,6},{5,7},{6,4},{7,5},{8,10},{9,11},{10,... | collective-permute-start | bytes 1572872 | tf_op jit(solution)/shard_map/ppermute | solution.py:482
  77.2 3.7 %collective-permute-start.17 = (bf16[512,256]{1,0:T(8,128)(2,1)S(1)}, bf16[512,256]{1,0:T(8,128)(2,1)S(1)}, u32[]{:S(2)}, u32[]{:S(2)}) collective-permute-start(bf16[512,256]{1,0:T(8,128)(2,1)S(1)} %get-tuple-element.79), channel_id=1, source_target_pairs={{0,4},{4,0},{8,12},{12,8},{1,5},{5,1},{9,13},{13,9},{2,6},{6,2},{1... | collective-permute-start | bytes 786440 | tf_op jit(solution)/shard_map/ppermute | solution.py:482
  81.2 0.8 shard_map.136.refs_2_
  82.1 1.0 copy-done.9
  83.2 1.4 %collective-permute-start.21 = (bf16[1024,256]{1,0:T(8,128)(2,1)S(1)}, bf16[1024,256]{1,0:T(8,128)(2,1)S(1)}, u32[]{:S(2)}, u32[]{:S(2)}) collective-permute-start(bf16[1024,256]{1,0:T(8,128)(2,1)S(1)} %get-tuple-element.83), channel_id=1, source_target_pairs={{0,2},{1,3},{2,0},{3,1},{4,6},{5,7},{6,4},{7,5},{8,10},{9,11},{10,... | collective-permute-start | bytes 1572872 | tf_op jit(solution)/shard_map/ppermute | solution.py:482
  84.7 0.8 shard_map.139.refs_2_
  85.5 1.1 %collective-permute-done.17.refs_1_.refs_3_ = bf16[512,256]{1,0:T(8,128)(2,1)S(1)} collective-permute-done((bf16[512,256]{1,0:T(8,128)(2,1)S(1)}, bf16[512,256]{1,0:T(8,128)(2,1)S(1)}, u32[]{:S(2)}, u32[]{:S(2)}) %collective-permute-start.17) | collective-permute-done | bytes 262176 | tf_op jit(solution)/shard_map/ppermute | solution.py:482
  86.6 1.0 copy-done.10
  87.8 2.7 %collective-permute-start.24 = (bf16[512,256]{1,0:T(8,128)(2,1)S(1)}, bf16[512,256]{1,0:T(8,128)(2,1)S(1)}, u32[]{:S(2)}, u32[]{:S(2)}) collective-permute-start(bf16[512,256]{1,0:T(8,128)(2,1)S(1)} %shard_map.138.refs_5_.refs_2_), channel_id=1, source_target_pairs={{0,4},{4,0},{8,12},{12,8},{1,5},{5,1},{9,13},{13,9},{2,6},{6,2},{1... | collective-permute-start | bytes 786440 | tf_op jit(solution)/shard_map/ppermute | solution.py:482
  90.5 0.9 shard_map.141.refs_2_
  91.4 1.0 copy-done.2
  92.6 4.7 %collective-permute-start.26 = (bf16[512,256]{1,0:T(8,128)(2,1)S(1)}, bf16[512,256]{1,0:T(8,128)(2,1)S(1)}, u32[]{:S(2)}, u32[]{:S(2)}) collective-permute-start(bf16[512,256]{1,0:T(8,128)(2,1)S(1)} %shard_map.143.refs_2_), channel_id=1, source_target_pairs={{0,4},{4,0},{8,12},{12,8},{1,5},{5,1},{9,13},{13,9},{2,6},{6,2},{1... | collective-permute-start | bytes 786440 | tf_op jit(solution)/shard_map/ppermute | solution.py:482
  97.4 3.9 %collective-permute-done.21.refs_1_ = bf16[1024,256]{1,0:T(8,128)(2,1)S(1)} collective-permute-done((bf16[1024,256]{1,0:T(8,128)(2,1)S(1)}, bf16[1024,256]{1,0:T(8,128)(2,1)S(1)}, u32[]{:S(2)}, u32[]{:S(2)}) %collective-permute-start.21) | collective-permute-done | bytes 524320 | tf_op jit(solution)/shard_map/ppermute | solution.py:482
  101.4 0.9 shard_map.144.refs_5_
  102.3 1.0 copy-done.8
  103.3 0.8 shard_map.145.refs_5_
  104.6 3.4 %collective-permute-done.25.refs_3_ = bf16[512,256]{1,0:T(8,128)(2,1)S(1)} collective-permute-done((bf16[512,256]{1,0:T(8,128)(2,1)S(1)}, bf16[512,256]{1,0:T(8,128)(2,1)S(1)}, u32[]{:S(2)}, u32[]{:S(2)}) %collective-permute-start.25) | collective-permute-done | bytes 262176 | tf_op jit(solution)/shard_map/ppermute | solution.py:482
  107.9 1.0 copy-done.17
  109.0 0.8 shard_map.146
  (90 shorter events, 7.2 us)
Async XLA Ops:
  0.6 11.2 %copy-start = (bf16[1024,1024]{1,0:T(8,128)(2,1)S(1)}, bf16[1024,1024]{1,0:T(8,128)(2,1)}, u32[]{:S(2)}) copy-start(bf16[1024,1024]{1,0:T(8,128)(2,1)} %refs_1_.13) | copy-start | bytes 6291460
  0.6 11.2 %copy-start.11 = (bf16[1024,256]{1,0:T(8,128)(2,1)S(1)}, bf16[1024,256]{1,0:T(8,128)(2,1)}, u32[]{:S(2)}) copy-start(bf16[1024,256]{1,0:T(8,128)(2,1)} %refs_4_.3) | copy-start | bytes 1572868
  6.1 6.4 %copy-start.20 = (bf16[1024,512]{1,0:T(8,128)(2,1)S(1)}, bf16[1024,512]{1,0:T(8,128)(2,1)}, u32[]{:S(2)}) copy-start(bf16[1024,512]{1,0:T(8,128)(2,1)} %get-tuple-element.45.refs_1_.refs_3_.refs_5_) | copy-start | bytes 3145732
  6.1 6.4 %copy-start.21 = (bf16[512,512]{1,0:T(8,128)(2,1)S(1)}, bf16[512,512]{1,0:T(8,128)(2,1)}, u32[]{:S(2)}) copy-start(bf16[512,512]{1,0:T(8,128)(2,1)} %get-tuple-element.46.refs_2_.refs_4_.refs_6_) | copy-start | bytes 1572868
  6.1 6.4 %copy-start.22 = (bf16[256,512]{1,0:T(8,128)(2,1)S(1)}, bf16[256,512]{1,0:T(8,128)(2,1)}, u32[]{:S(2)}) copy-start(bf16[256,512]{1,0:T(8,128)(2,1)} %get-tuple-element.47.refs_3_.refs_5_.refs_7_) | copy-start | bytes 786436
  6.1 9.5 %collective-permute-start.1 = (bf16[64,512]{1,0:T(8,128)(2,1)}, bf16[64,512]{1,0:T(8,128)(2,1)S(1)}, u32[]{:S(2)}, u32[]{:S(2)}) collective-permute-start(bf16[64,512]{1,0:T(8,128)(2,1)} %get-tuple-element.51), channel_id=1, source_target_pairs={{0,8},{4,12},{8,0},{12,4},{1,9},{5,13},{9,1},{13,5},{2,10},{6,14},... | collective-permute-start | bytes 196616 | tf_op jit(solution)/shard_map/ppermute | solution.py:482
  10.3 7.1 %collective-permute-start.2 = (bf16[64,512]{1,0:T(8,128)(2,1)}, bf16[64,512]{1,0:T(8,128)(2,1)S(1)}, u32[]{:S(2)}, u32[]{:S(2)}) collective-permute-start(bf16[64,512]{1,0:T(8,128)(2,1)} %get-tuple-element.51), channel_id=1, source_target_pairs={{0,12},{4,8},{8,4},{12,0},{1,13},{5,9},{9,5},{13,1},{2,14},{6,10},... | collective-permute-start | bytes 196616 | tf_op jit(solution)/shard_map/ppermute | solution.py:482
  11.6 6.4 %collective-permute-start = (bf16[128,512]{1,0:T(8,128)(2,1)}, bf16[128,512]{1,0:T(8,128)(2,1)S(1)}, u32[]{:S(2)}, u32[]{:S(2)}) collective-permute-start(bf16[128,512]{1,0:T(8,128)(2,1)} %get-tuple-element.50), channel_id=1, source_target_pairs={{0,4},{4,0},{8,12},{12,8},{1,5},{5,1},{9,13},{13,9},{2,6},{6,2},{1... | collective-permute-start | bytes 393224 | tf_op jit(solution)/shard_map/ppermute | solution.py:482
  12.6 2.4 %copy-start.1 = (bf16[1024,1024]{1,0:T(8,128)(2,1)S(1)}, bf16[1024,1024]{1,0:T(8,128)(2,1)}, u32[]{:S(2)}) copy-start(bf16[1024,1024]{1,0:T(8,128)(2,1)} %refs_1_.9) | copy-start | bytes 6291460
  12.6 2.4 %copy-start.3 = (bf16[1024,256]{1,0:T(8,128)(2,1)S(1)}, bf16[1024,256]{1,0:T(8,128)(2,1)}, u32[]{:S(2)}) copy-start(bf16[1024,256]{1,0:T(8,128)(2,1)} %refs_2_.1) | copy-start | bytes 1572868
  21.9 1.8 %copy-start.4 = (bf16[1024,256]{1,0:T(8,128)(2,1)}, bf16[1024,256]{1,0:T(8,128)(2,1)S(1)}, u32[]{:S(2)}) copy-start(bf16[1024,256]{1,0:T(8,128)(2,1)S(1)} %get-tuple-element.52.refs_2_.refs_1_) | copy-start | bytes 1572868
  22.7 13.9 %collective-permute-start.3 = (bf16[1024,256]{1,0:T(8,128)(2,1)S(1)}, bf16[1024,256]{1,0:T(8,128)(2,1)S(1)}, u32[]{:S(2)}, u32[]{:S(2)}) collective-permute-start(bf16[1024,256]{1,0:T(8,128)(2,1)S(1)} %shard_map.114.refs_11_.refs_0_), channel_id=1, source_target_pairs={{0,4},{4,0},{8,12},{12,8},{1,5},{5,1},{9,13},{13,9},{2,6},{6,2},{1... | collective-permute-start | bytes 1572872 | tf_op jit(solution)/shard_map/ppermute | solution.py:482
  31.2 1.3 %copy-start.18 = (f32[1024,512]{1,0:T(8,128)}, f32[1024,512]{1,0:T(8,128)S(1)}, u32[]{:S(2)}) copy-start(f32[1024,512]{1,0:T(8,128)S(1)} %get-tuple-element.60.refs_0_) | copy-start | bytes 6291460
  32.5 4.1 %copy-start.6 = (bf16[1024,256]{1,0:T(8,128)(2,1)}, bf16[1024,256]{1,0:T(8,128)(2,1)S(1)}, u32[]{:S(2)}) copy-start(bf16[1024,256]{1,0:T(8,128)(2,1)S(1)} %get-tuple-element.56.refs_2_.refs_1_) | copy-start | bytes 1572868
  32.5 17.4 %collective-permute-start.7 = (bf16[768,256]{1,0:T(8,128)(2,1)S(1)}, bf16[768,256]{1,0:T(8,128)(2,1)}, u32[]{:S(2)}, u32[]{:S(2)}) collective-permute-start(bf16[768,256]{1,0:T(8,128)(2,1)S(1)} %get-tuple-element.61.refs_0_), channel_id=1, source_target_pairs={{0,4},{4,0},{8,12},{12,8},{1,5},{5,1},{9,13},{13,9},{2,6},{6,2},{1... | collective-permute-start | bytes 1179656 | tf_op jit(solution)/shard_map/ppermute | solution.py:482
  37.4 5.3 %collective-permute-start.4 = (bf16[512,256]{1,0:T(8,128)(2,1)S(1)}, bf16[512,256]{1,0:T(8,128)(2,1)}, u32[]{:S(2)}, u32[]{:S(2)}) collective-permute-start(bf16[512,256]{1,0:T(8,128)(2,1)S(1)} %get-tuple-element.57.refs_1_.refs_4_), channel_id=1, source_target_pairs={{0,1},{1,0},{2,3},{3,2},{4,8},{5,9},{6,10},{7,11},{8,4},{9,5},{10,... | collective-permute-start | bytes 786440 | tf_op jit(solution)/shard_map/ppermute | solution.py:643
  37.4 12.5 %collective-permute-start.8 = (bf16[64,512]{1,0:T(8,128)(2,1)}, bf16[64,512]{1,0:T(8,128)(2,1)}, u32[]{:S(2)}, u32[]{:S(2)}) collective-permute-start(bf16[64,512]{1,0:T(8,128)(2,1)} %get-tuple-element.62), channel_id=1, source_target_pairs={{0,8},{4,12},{8,0},{12,4},{1,9},{5,13},{9,1},{13,5},{2,10},{6,14},... | collective-permute-start | bytes 196616 | tf_op jit(solution)/shard_map/ppermute | solution.py:482
  40.8 9.1 %collective-permute-start.9 = (bf16[64,512]{1,0:T(8,128)(2,1)}, bf16[64,512]{1,0:T(8,128)(2,1)}, u32[]{:S(2)}, u32[]{:S(2)}) collective-permute-start(bf16[64,512]{1,0:T(8,128)(2,1)} %get-tuple-element.63), channel_id=1, source_target_pairs={{0,12},{4,8},{8,4},{12,0},{1,13},{5,9},{9,5},{13,1},{2,14},{6,10},... | collective-permute-start | bytes 196616 | tf_op jit(solution)/shard_map/ppermute | solution.py:482
  42.7 12.7 %collective-permute-start.6 = (bf16[512,256]{1,0:T(8,128)(2,1)}, bf16[512,256]{1,0:T(8,128)(2,1)S(1)}, u32[]{:S(2)}, u32[]{:S(2)}) collective-permute-start(bf16[512,256]{1,0:T(8,128)(2,1)} %copy-done.13), channel_id=1, source_target_pairs={{0,1},{1,0},{2,3},{3,2},{4,8},{5,9},{6,10},{7,11},{8,4},{9,5},{10,... | collective-permute-start | bytes 786440 | tf_op jit(solution)/shard_map/ppermute | solution.py:643
  43.7 15.7 %collective-permute-start.5 = (bf16[512,256]{1,0:T(8,128)(2,1)S(1)}, bf16[512,256]{1,0:T(8,128)(2,1)S(1)}, u32[]{:S(2)}, u32[]{:S(2)}) collective-permute-start(bf16[512,256]{1,0:T(8,128)(2,1)S(1)} %get-tuple-element.58), channel_id=1, source_target_pairs={{0,4},{4,0},{8,12},{12,8},{1,5},{5,1},{9,13},{13,9},{2,6},{6,2},{1... | collective-permute-start | bytes 786440 | tf_op jit(solution)/shard_map/ppermute | solution.py:482
  49.9 1.6 %copy-start.19 = (f32[1024,512]{1,0:T(8,128)S(1)}, f32[1024,512]{1,0:T(8,128)}, u32[]{:S(2)}) copy-start(f32[1024,512]{1,0:T(8,128)} %copy-done.18) | copy-start | bytes 6291460
  53.6 1.8 %copy-start.14 = (bf16[512,256]{1,0:T(8,128)(2,1)S(1)}, bf16[512,256]{1,0:T(8,128)(2,1)}, u32[]{:S(2)}) copy-start(bf16[512,256]{1,0:T(8,128)(2,1)} %copy-done.13) | copy-start | bytes 786436
  54.1 5.4 %copy-start.5 = (bf16[1024,256]{1,0:T(8,128)(2,1)S(1)}, bf16[1024,256]{1,0:T(8,128)(2,1)}, u32[]{:S(2)}) copy-start(bf16[1024,256]{1,0:T(8,128)(2,1)} %copy-done.4) | copy-start | bytes 1572868
  55.3 9.5 %collective-permute-start.11 = (bf16[512,256]{1,0:T(8,128)(2,1)S(1)}, bf16[512,256]{1,0:T(8,128)(2,1)S(1)}, u32[]{:S(2)}, u32[]{:S(2)}) collective-permute-start(bf16[512,256]{1,0:T(8,128)(2,1)S(1)} %shard_map.120.refs_4_.refs_1_), channel_id=1, source_target_pairs={{0,1},{1,0},{2,3},{3,2},{4,8},{5,9},{6,10},{7,11},{8,4},{9,5},{10,... | collective-permute-start | bytes 786440 | tf_op jit(solution)/shard_map/ppermute | solution.py:649
  55.6 9.2 %collective-permute-start.14 = (bf16[512,256]{1,0:T(8,128)(2,1)S(1)}, bf16[512,256]{1,0:T(8,128)(2,1)S(1)}, u32[]{:S(2)}, u32[]{:S(2)}) collective-permute-start(bf16[512,256]{1,0:T(8,128)(2,1)S(1)} %get-tuple-element.74), channel_id=1, source_target_pairs={{0,4},{4,0},{8,12},{12,8},{1,5},{5,1},{9,13},{13,9},{2,6},{6,2},{1... | collective-permute-start | bytes 786440 | tf_op jit(solution)/shard_map/ppermute | solution.py:482
  60.2 15.2 %collective-permute-start.10 = (bf16[1024,512]{1,0:T(8,128)(2,1)S(1)}, bf16[1024,512]{1,0:T(8,128)(2,1)S(1)}, u32[]{:S(2)}, u32[]{:S(2)}) collective-permute-start(bf16[1024,512]{1,0:T(8,128)(2,1)S(1)} %get-tuple-element.69), channel_id=1, source_target_pairs={{0,1},{1,0},{2,3},{3,2},{4,5},{5,4},{6,7},{7,6},{8,9},{9,8},{10,11... | collective-permute-start | bytes 3145736 | tf_op jit(solution)/shard_map/ppermute | solution.py:482
  61.4 1.0 copy-start.7
  61.4 1.2 %copy-start.12 = (bf16[1024,256]{1,0:T(8,128)(2,1)S(1)}, bf16[1024,256]{1,0:T(8,128)(2,1)}, u32[]{:S(2)}) copy-start(bf16[1024,256]{1,0:T(8,128)(2,1)} %refs_4_.3) | copy-start | bytes 1572868
  61.4 1.3 %copy-start.15 = (bf16[1024,256]{1,0:T(8,128)(2,1)S(1)}, bf16[1024,256]{1,0:T(8,128)(2,1)}, u32[]{:S(2)}) copy-start(bf16[1024,256]{1,0:T(8,128)(2,1)} %refs_5_.1) | copy-start | bytes 1572868
  61.4 1.5 %copy-start.16 = (bf16[1024,256]{1,0:T(8,128)(2,1)S(1)}, bf16[1024,256]{1,0:T(8,128)(2,1)}, u32[]{:S(2)}) copy-start(bf16[1024,256]{1,0:T(8,128)(2,1)} %refs_6_.1) | copy-start | bytes 1572868
  65.0 16.0 %collective-permute-start.20 = (bf16[1024,512]{1,0:T(8,128)(2,1)S(1)}, bf16[1024,512]{1,0:T(8,128)(2,1)S(1)}, u32[]{:S(2)}, u32[]{:S(2)}) collective-permute-start(bf16[1024,512]{1,0:T(8,128)(2,1)S(1)} %shard_map.130.refs_4_), channel_id=1, source_target_pairs={{0,1},{1,0},{2,3},{3,2},{4,5},{5,4},{6,7},{7,6},{8,9},{9,8},{10,11... | collective-permute-start | bytes 3145736 | tf_op jit(solution)/shard_map/ppermute | solution.py:482
  65.6 2.7 %collective-permute-start.13 = (bf16[512,256]{1,0:T(8,128)(2,1)S(1)}, bf16[512,256]{1,0:T(8,128)(2,1)S(1)}, u32[]{:S(2)}, u32[]{:S(2)}) collective-permute-start(bf16[512,256]{1,0:T(8,128)(2,1)S(1)} %shard_map.122.refs_3_.refs_1_), channel_id=1, source_target_pairs={{0,1},{1,0},{2,3},{3,2},{4,8},{5,9},{6,10},{7,11},{8,4},{9,5},{10,... | collective-permute-start | bytes 786440 | tf_op jit(solution)/shard_map/ppermute | solution.py:649
  65.6 9.7 %collective-permute-start.12 = (bf16[512,256]{1,0:T(8,128)(2,1)S(1)}, bf16[512,256]{1,0:T(8,128)(2,1)S(1)}, u32[]{:S(2)}, u32[]{:S(2)}) collective-permute-start(bf16[512,256]{1,0:T(8,128)(2,1)S(1)} %get-tuple-element.72), channel_id=1, source_target_pairs={{0,4},{4,0},{8,12},{12,8},{1,5},{5,1},{9,13},{13,9},{2,6},{6,2},{1... | collective-permute-start | bytes 786440 | tf_op jit(solution)/shard_map/ppermute | solution.py:482
  67.0 10.1 %collective-permute-start.16 = (bf16[512,256]{1,0:T(8,128)(2,1)S(1)}, bf16[512,256]{1,0:T(8,128)(2,1)S(1)}, u32[]{:S(2)}, u32[]{:S(2)}) collective-permute-start(bf16[512,256]{1,0:T(8,128)(2,1)S(1)} %shard_map.129.refs_1_), channel_id=1, source_target_pairs={{0,1},{1,0},{2,3},{3,2},{4,8},{5,9},{6,10},{7,11},{8,4},{9,5},{10,... | collective-permute-start | bytes 786440 | tf_op jit(solution)/shard_map/ppermute | solution.py:649
  68.3 13.7 %collective-permute-start.18 = (bf16[512,256]{1,0:T(8,128)(2,1)S(1)}, bf16[512,256]{1,0:T(8,128)(2,1)S(1)}, u32[]{:S(2)}, u32[]{:S(2)}) collective-permute-start(bf16[512,256]{1,0:T(8,128)(2,1)S(1)} %get-tuple-element.80), channel_id=1, source_target_pairs={{0,4},{4,0},{8,12},{12,8},{1,5},{5,1},{9,13},{13,9},{2,6},{6,2},{1... | collective-permute-start | bytes 786440 | tf_op jit(solution)/shard_map/ppermute | solution.py:482
  75.4 9.2 %collective-permute-start.19 = (bf16[512,256]{1,0:T(8,128)(2,1)S(1)}, bf16[512,256]{1,0:T(8,128)(2,1)S(1)}, u32[]{:S(2)}, u32[]{:S(2)}) collective-permute-start(bf16[512,256]{1,0:T(8,128)(2,1)S(1)} %shard_map.132.refs_2_.refs_0_), channel_id=1, source_target_pairs={{0,1},{1,0},{2,3},{3,2},{4,8},{5,9},{6,10},{7,11},{8,4},{9,5},{10,... | collective-permute-start | bytes 786440 | tf_op jit(solution)/shard_map/ppermute | solution.py:649
  75.7 14.8 %collective-permute-start.15 = (bf16[1024,256]{1,0:T(8,128)(2,1)S(1)}, bf16[1024,256]{1,0:T(8,128)(2,1)S(1)}, u32[]{:S(2)}, u32[]{:S(2)}) collective-permute-start(bf16[1024,256]{1,0:T(8,128)(2,1)S(1)} %get-tuple-element.78), channel_id=1, source_target_pairs={{0,2},{1,3},{2,0},{3,1},{4,6},{5,7},{6,4},{7,5},{8,10},{9,11},{10,... | collective-permute-start | bytes 1572872 | tf_op jit(solution)/shard_map/ppermute | solution.py:482
  77.2 9.4 %collective-permute-start.17 = (bf16[512,256]{1,0:T(8,128)(2,1)S(1)}, bf16[512,256]{1,0:T(8,128)(2,1)S(1)}, u32[]{:S(2)}, u32[]{:S(2)}) collective-permute-start(bf16[512,256]{1,0:T(8,128)(2,1)S(1)} %get-tuple-element.79), channel_id=1, source_target_pairs={{0,4},{4,0},{8,12},{12,8},{1,5},{5,1},{9,13},{13,9},{2,6},{6,2},{1... | collective-permute-start | bytes 786440 | tf_op jit(solution)/shard_map/ppermute | solution.py:482
  82.0 1.0 copy-start.9
  83.2 8.3 %collective-permute-start.23 = (bf16[512,256]{1,0:T(8,128)(2,1)S(1)}, bf16[512,256]{1,0:T(8,128)(2,1)S(1)}, u32[]{:S(2)}, u32[]{:S(2)}) collective-permute-start(bf16[512,256]{1,0:T(8,128)(2,1)S(1)} %shard_map.137.refs_2_.refs_0_), channel_id=1, source_target_pairs={{0,1},{1,0},{2,3},{3,2},{4,8},{5,9},{6,10},{7,11},{8,4},{9,5},{10,... | collective-permute-start | bytes 786440 | tf_op jit(solution)/shard_map/ppermute | solution.py:649
  83.2 18.1 %collective-permute-start.21 = (bf16[1024,256]{1,0:T(8,128)(2,1)S(1)}, bf16[1024,256]{1,0:T(8,128)(2,1)S(1)}, u32[]{:S(2)}, u32[]{:S(2)}) collective-permute-start(bf16[1024,256]{1,0:T(8,128)(2,1)S(1)} %get-tuple-element.83), channel_id=1, source_target_pairs={{0,2},{1,3},{2,0},{3,1},{4,6},{5,7},{6,4},{7,5},{8,10},{9,11},{10,... | collective-permute-start | bytes 1572872 | tf_op jit(solution)/shard_map/ppermute | solution.py:482
  86.6 1.0 copy-start.10
  87.7 4.8 %collective-permute-start.22 = (bf16[512,256]{1,0:T(8,128)(2,1)S(1)}, bf16[512,256]{1,0:T(8,128)(2,1)S(1)}, u32[]{:S(2)}, u32[]{:S(2)}) collective-permute-start(bf16[512,256]{1,0:T(8,128)(2,1)S(1)} %shard_map.140.refs_2_.refs_0_), channel_id=1, source_target_pairs={{0,1},{1,0},{2,3},{3,2},{4,8},{5,9},{6,10},{7,11},{8,4},{9,5},{10,... | collective-permute-start | bytes 786440 | tf_op jit(solution)/shard_map/ppermute | solution.py:649
  87.8 14.5 %collective-permute-start.24 = (bf16[512,256]{1,0:T(8,128)(2,1)S(1)}, bf16[512,256]{1,0:T(8,128)(2,1)S(1)}, u32[]{:S(2)}, u32[]{:S(2)}) collective-permute-start(bf16[512,256]{1,0:T(8,128)(2,1)S(1)} %shard_map.138.refs_5_.refs_2_), channel_id=1, source_target_pairs={{0,4},{4,0},{8,12},{12,8},{1,5},{5,1},{9,13},{13,9},{2,6},{6,2},{1... | collective-permute-start | bytes 786440 | tf_op jit(solution)/shard_map/ppermute | solution.py:482
  91.4 1.0 copy-start.2
  92.6 11.9 %collective-permute-start.26 = (bf16[512,256]{1,0:T(8,128)(2,1)S(1)}, bf16[512,256]{1,0:T(8,128)(2,1)S(1)}, u32[]{:S(2)}, u32[]{:S(2)}) collective-permute-start(bf16[512,256]{1,0:T(8,128)(2,1)S(1)} %shard_map.143.refs_2_), channel_id=1, source_target_pairs={{0,4},{4,0},{8,12},{12,8},{1,5},{5,1},{9,13},{13,9},{2,6},{6,2},{1... | collective-permute-start | bytes 786440 | tf_op jit(solution)/shard_map/ppermute | solution.py:482
  97.3 10.6 %collective-permute-start.25 = (bf16[512,256]{1,0:T(8,128)(2,1)S(1)}, bf16[512,256]{1,0:T(8,128)(2,1)S(1)}, u32[]{:S(2)}, u32[]{:S(2)}) collective-permute-start(bf16[512,256]{1,0:T(8,128)(2,1)S(1)} %shard_map.142.refs_2_.refs_1_), channel_id=1, source_target_pairs={{0,4},{4,0},{8,12},{12,8},{1,5},{5,1},{9,13},{13,9},{2,6},{6,2},{1... | collective-permute-start | bytes 786440 | tf_op jit(solution)/shard_map/ppermute | solution.py:482
  102.3 1.0 copy-start.8
  (2 other events, 1.7 us)

commit v7 on v6

--- a/solution.py
+++ b/solution.py
@@ -111,14 +111,16 @@
         copy.wait()
 
 
-def key_value(tokens, w_key, w_value, local_levels, far_levels):
+def key_value(tokens, w_key, w_value, local_levels, far_levels, after):
     tok_rows, width = tokens.shape
     inner = w_key.shape[1]
     parts = tok_rows // (2 * BLOCK)
     held = [(tok_rows >> i, 2 * inner) for i in range(local_levels)]
     tops = [(BLOCK >> i, 2 * inner) for i in range(far_levels)]
-    return pl.pallas_call(
+    return run(
         functools.partial(key_value_body, local_levels, far_levels, parts),
+        [tokens, w_key, w_value],
+        after,
         in_specs=[pl.BlockSpec(memory_space=pl.ANY)] * 3,
         out_specs=[pl.BlockSpec(memory_space=pl.ANY)] * len(held)
         + [pl.BlockSpec(memory_space=pltpu.VMEM)] * len(tops),
@@ -129,7 +131,7 @@
         + [pltpu.SemaphoreType.DMA((parts + 2,)), pltpu.SemaphoreType.DMA((len(held),))],
         compiler_params=params(56),
         cost_estimate=cost(5.0),
-    )(tokens, w_key, w_value)
+    )
 
 
 def project_body(left_ref, weight_ref, out_ref):
@@ -459,12 +461,11 @@
         outs[r % 2][:, place : place + width] = total.astype(BF16)
 
 
-def project_split(lefts, weights, axis, after):
+def project_split(rank, lefts, weights, axis, after):
     count = len(lefts)
     parts = lax.axis_size(axis)
     tok_rows, inner = lefts[0].shape
     width = weights[0].shape[0]
-    rank = jnp.reshape(lax.axis_index(axis), (1,)).astype(jnp.int32)
     return run(
         functools.partial(split_body, count, parts),
         [rank, *lefts, *weights],
@@ -530,6 +531,22 @@
         (even_ref, odd_ref)[i % 2][:, place] = total.astype(BF16)
 
 
+def last_body(left_ref, right_ref, token_ref, out_ref):
+    token_ref[...] = jnp.zeros_like(token_ref)
+    out_ref[...] = (left_ref[...].astype(F32) + right_ref[...].astype(F32)).astype(BF16)
+
+
+def last_sum(left, right, after):
+    return run(
+        last_body,
+        [left, right],
+        after,
+        out_shape=[shape(8, 128, F32), shape(*left.shape)],
+        compiler_params=params(3),
+        cost_estimate=cost(0.9),
+    )
+
+
 def scatter_step(keep, into, pieces, after):
     rows, width = keep.shape
     return run(
@@ -569,7 +586,8 @@
 
 
 def output_body(count, end_ref, *refs):
-    totals, ends, out_ref = refs[:count], refs[count : 2 * count], refs[-1]
+    totals, ends, (token_ref, out_ref) = refs[:count], refs[count : 2 * count], refs[2 * count :]
+    token_ref[...] = jnp.zeros_like(token_ref)
     rows = totals[0].shape[0]
 
     for flag, sources in ((0, totals), (1, ends)):
@@ -589,7 +607,7 @@
         after,
         in_specs=[pl.BlockSpec(memory_space=pltpu.SMEM)]
         + [pl.BlockSpec(memory_space=pltpu.VMEM)] * (2 * count),
-        out_shape=shape(count * rows, width),
+        out_shape=[shape(8, 128, F32), shape(count * rows, width)],
         compiler_params=params(4),
         cost_estimate=cost(0.9),
     )
@@ -613,11 +631,10 @@
 class Line:
     lag = 3
 
-    def __init__(self, axis, other, step):
+    def __init__(self, axis, other, end, step):
         self.axis, self.axes, self.step = axis, (axis, other), step
         self.count = lax.axis_size(axis)
-        rank = jnp.bitwise_and(lax.axis_index(axis), 3)
-        self.end = jnp.reshape((rank == 0) | (rank == 3), (1,)).astype(jnp.int32)
+        self.end = end
         width = lax.axis_size(other)
         self.across = []
         for place in range(self.count):
@@ -664,7 +681,7 @@
 
     def output(self, first, count):
         ends = self.into[first + self.lag : first + self.lag + count]
-        result = self.step(output, self.end, self.totals[first : first + count], ends)
+        _, result = self.step(output, self.end, self.totals[first : first + count], ends)
         distance = 4
         while distance < self.count:
             result = add(result, exchange(result, self.axis, distance))
@@ -688,7 +705,7 @@
             self.into = exchange(send, self.axis, self.distance)
 
     def result(self):
-        return self.step(half_sum, self.keep, self.into, self.keep.shape[0])
+        return self.step(last_sum, self.keep, self.into)[1]
 
 
 def per_device(tokens, w_query, w_key, w_value, w_out, cotangent):
@@ -706,7 +723,10 @@
         last[:] = made[:1] if isinstance(made, (list, tuple)) else [made]
         return made
 
-    parts = key_value(tokens, w_key, w_value, local_levels, far_levels)
+    place = jnp.bitwise_and(lax.axis_index("seq"), 3)
+    end = jnp.reshape((place == 0) | (place == 3), (1,)).astype(jnp.int32)
+    rank = jnp.reshape(lax.axis_index("head"), (1,)).astype(jnp.int32)
+    parts = key_value(tokens, w_key, w_value, local_levels, far_levels, [end, rank])
     levels, tops = parts[:local_levels], parts[local_levels:]
     fars = [exchange(tops[bit], "seq", d) for d, bit in enumerate(far_bits, 1)]
     query = step(project, tokens, w_query)
@@ -714,7 +734,7 @@
     grad = step(project, cotangent, w_out)
     attended, attended_t, stats = step(forward, query, powers, near, levels, fars, far_bits)
 
-    line = Line("seq", "head", step)
+    line = Line("seq", "head", end, step)
     pieces = 2
     rows = tokens.shape[1] // pieces
     line.enter_whole(step(weight_terms, attended_t, cotangent, inner, 0, 0, 1), pieces)
@@ -732,30 +752,30 @@
     line.meet(rows)
     line.turn(key_first)
     line.meet(rows)
-    parts = step(project_split, [attended], [w_out], "head")
+    parts = step(project_split, rank, [attended], [w_out], "head")
     mixed = Scatter(parts, "head", step)
     key_second = step(weight_terms, dkv_t, tokens, inner, 0, 1, pieces)
     value_first = step(weight_terms, dkv_t, tokens, inner, 1, 0, pieces)
     value_second = step(weight_terms, dkv_t, tokens, inner, 1, 1, pieces)
-    keep, send = step(project_split, [dquery, dkey, dvalue], [w_query, w_key, w_value], "head")
+    keep, send = step(project_split, rank, [dquery, dkey, dvalue], [w_query, w_key, w_value], "head")
     line.turn(key_second)
     line.meet(rows)
     tokens_grad = Scatter([keep, step(relay, send)], "head", step)
     line.turn(value_first)
+    mixed.advance()
     line.meet(rows)
-    mixed.advance()
     line.turn(value_second)
     tokens_grad.advance()
+    line.meet(rows)
     out_grad = line.output(0, pieces)
+    line.leave()
     line.meet(rows)
+    query_grad = line.output(2, pieces)
     line.leave()
-    query_grad = line.output(2, pieces)
-    line.meet(rows)
     mixed = mixed.result()
-    line.leave()
+    key_grad = line.output(4, pieces)
     line.leave()
     tokens_grad = tokens_grad.result()
-    key_grad = line.output(4, pieces)
     value_grad = line.output(6, pieces)
     return mixed, tokens_grad, query_grad, key_grad, value_grad, out_grad
 

time: 110 us -> 104 us (0.945)
  local copies, waits for them, and re-layouts: 9.88 us -> 0.71 us
  starting transfers between devices: 45.7 us -> 52.9 us
  Pallas kernels: 37.1 us -> 33.4 us
    unnamed x46 -> x18, local copies, waits for them, and re-layouts: 9.88 us -> 0.71 us
    ppermute x19, starting transfers between devices: 45.4 us -> 52.4 us  [exchange(): return lax.ppermute(block, axis, [(i, i ^ distance) for i in range(count)])]
    pallas_call x1 -> x0, Pallas kernels: 5.45 us -> none  [key_value(): pl.pallas_call(functools.partial(key_value_body, local_levels, far_levels...]
    pallas_call x37 -> x38, Pallas kernels: 31.6 us -> 33.4 us  [run(): return pl.pallas_call(kernel, in_specs=in_specs, **options)(*ready, *after)]
  transfers between devices with their start and end apart: 27 -> 27, of which waited for: 9 -> 7; matrix products, arithmetic and copies ran while one was open for 0% -> 0% of each run, Pallas kernels for 24% -> 22%
where the time goes in v7:
time: 104 us; the launch traced here: 103 us
  starting transfers between devices  52.9 us (51%)
  Pallas kernels  33.4 us (32%)
  waiting for transfers between devices  15.4 us (15%)
  between operations  1.07 us (1%)
    ppermute x19, starting transfers between devices, exchange(): return lax.ppermute(block, axis, [(i, i ^ distance) for i in range(count)])  52.4 us
    pallas_call x38, Pallas kernels, run(): return pl.pallas_call(kernel, in_specs=in_specs, **options)(*ready, *after)  33.4 us
    ppermute x19, waiting for transfers between devices, exchange(): return lax.ppermute(block, axis, [(i, i ^ distance) for i in range(count)])  14.7 us
  transfers between devices with their start and end apart: 27, of which 7 were waited for; matrix products, arithmetic and copies ran while one was open for 0% of the time, Pallas kernels for 22%

profile of v7, /device:TPU:0, one launch (start us, length us, event | category | flops | bytes accessed | tf_op | source)
XLA Modules:
  0.0 103.5 jit_solution(15339119879443328523)
XLA Ops:
  0.7 5.3 %shard_map.110 = (bf16[1024,512]{1,0:T(8,128)(2,1)}, bf16[512,512]{1,0:T(8,128)(2,1)}, bf16[256,512]{1,0:T(8,128)(2,1)}, bf16[128,512]{1,0:T(8,128)(2,1)}, bf16[64,512]{1,0:T(8,128)(2,1)}) custom-call(bf16[1024,1024]{1,0:T(8,128)(2,1)} %refs_1_.15, bf16[1024,256]{1,0:T(8,128)(2,1)} %refs_5_.1, bf16[1024,256]{1,0:T(8,128)(2,1)} %refs_6_.1, ...), custom_call_target="tpu_custom_call" | custom-call | flops 5750000128 | bytes 1 | tf_op jit(solution)/shard_map/pallas_call | solution.py:42
  6.0 4.1 %collective-permute-start.1 = (bf16[64,512]{1,0:T(8,128)(2,1)}, bf16[64,512]{1,0:T(8,128)(2,1)S(1)}, u32[]{:S(2)}, u32[]{:S(2)}) collective-permute-start(bf16[64,512]{1,0:T(8,128)(2,1)} %get-tuple-element.62), channel_id=1, source_target_pairs={{0,8},{4,12},{8,0},{12,4},{1,9},{5,13},{9,1},{13,5},{2,10},{6,14},... | collective-permute-start | bytes 196616 | tf_op jit(solution)/shard_map/ppermute | solution.py:483
  10.1 1.3 %collective-permute-start.2 = (bf16[64,512]{1,0:T(8,128)(2,1)}, bf16[64,512]{1,0:T(8,128)(2,1)S(1)}, u32[]{:S(2)}, u32[]{:S(2)}) collective-permute-start(bf16[64,512]{1,0:T(8,128)(2,1)} %get-tuple-element.62), channel_id=1, source_target_pairs={{0,12},{4,8},{8,4},{12,0},{1,13},{5,9},{9,5},{13,1},{2,14},{6,10},... | collective-permute-start | bytes 196616 | tf_op jit(solution)/shard_map/ppermute | solution.py:483
  11.7 0.7 shard_map.109.refs_0_.refs_4_
  12.5 2.3 %shard_map.111 = (f32[4096,256]{1,0:T(8,128)S(1)}, f32[4,1024]{1,0:T(4,128)S(1)}) custom-call(bf16[1024,256]{1,0:T(8,128)(2,1)S(1)} %shard_map.109.refs_0_.refs_4_, bf16[1024,512]{1,0:T(8,128)(2,1)S(1)} %copy-done.6, bf16[512,512]{1,0:T(8,128)(2,1)S(1)} %copy-done.7, bf16[256,512]{1,0:T(8,128)(2,1)S(1)} %copy-done.8, ...), custom_call_target="tpu_custom_call" | custom-call | flops 2644999936 | bytes 1 | tf_op jit(solution)/shard_map/pallas_call | solution.py:42
  14.9 0.7 shard_map.112.refs_9_.refs_1_
  15.6 1.5 %collective-permute-done.2.refs_8_.refs_10_ = bf16[64,512]{1,0:T(8,128)(2,1)S(1)} collective-permute-done((bf16[64,512]{1,0:T(8,128)(2,1)}, bf16[64,512]{1,0:T(8,128)(2,1)S(1)}, u32[]{:S(2)}, u32[]{:S(2)}) %collective-permute-start.2) | collective-permute-done | bytes 65568 | tf_op jit(solution)/shard_map/ppermute | solution.py:483
  17.1 0.8 collective-permute-done.refs_6_.refs_8_
  17.9 3.9 %shard_map.113 = (bf16[1024,256]{1,0:T(8,128)(2,1)S(1)}, bf16[256,1024]{1,0:T(8,128)(2,1)S(1)}, f32[4,1024]{1,0:T(4,128)S(1)}) custom-call(bf16[1024,256]{1,0:T(8,128)(2,1)S(1)} %shard_map.109.refs_0_.refs_4_, f32[4096,256]{1,0:T(8,128)S(1)} %get-tuple-element.59.refs_2_.refs_1_, f32[4,1024]{1,0:T(4,128)S(1)} %get-tuple-element.60.refs_2_, ...), custom_call_target="tpu_custom_call" | custom-call | flops 4600000000 | bytes 1 | tf_op jit(solution)/shard_map/pallas_call | solution.py:42
  21.8 0.8 shard_map.114.refs_11_.refs_0_
  22.6 1.0 collective-permute-start.3
  23.5 6.9 %shard_map.115 = (bf16[1024,256]{1,0:T(8,128)(2,1)S(1)}, f32[1024,512]{1,0:T(8,128)S(1)}, bf16[768,256]{1,0:T(8,128)(2,1)S(1)}, bf16[512,256]{1,0:T(8,128)(2,1)S...) custom-call(bf16[1024,256]{1,0:T(8,128)(2,1)S(1)} %shard_map.109.refs_0_.refs_4_, ...), custom_call_target="tpu_custom_call" | custom-call | flops 9200000000 | bytes 1 | tf_op jit(solution)/shard_map/pallas_call | solution.py:42
  30.5 1.2 %collective-permute-start.7 = (bf16[768,256]{1,0:T(8,128)(2,1)S(1)}, bf16[768,256]{1,0:T(8,128)(2,1)S(1)}, u32[]{:S(2)}, u32[]{:S(2)}) collective-permute-start(bf16[768,256]{1,0:T(8,128)(2,1)S(1)} %get-tuple-element.72.refs_0_), channel_id=1, source_target_pairs={{0,4},{4,0},{8,12},{12,8},{1,5},{5,1},{9,13},{13,9},{2,6},{6,2},{1... | collective-permute-start | bytes 1179656 | tf_op jit(solution)/shard_map/ppermute | solution.py:483
  31.7 5.8 %collective-permute-done.3.refs_1_ = bf16[1024,256]{1,0:T(8,128)(2,1)S(1)} collective-permute-done((bf16[1024,256]{1,0:T(8,128)(2,1)S(1)}, bf16[1024,256]{1,0:T(8,128)(2,1)S(1)}, u32[]{:S(2)}, u32[]{:S(2)}) %collective-permute-start.3) | collective-permute-done | bytes 524320 | tf_op jit(solution)/shard_map/ppermute | solution.py:483
  37.7 2.4 %collective-permute-start.8 = (bf16[64,512]{1,0:T(8,128)(2,1)S(1)}, bf16[64,512]{1,0:T(8,128)(2,1)S(1)}, u32[]{:S(2)}, u32[]{:S(2)}) collective-permute-start(bf16[64,512]{1,0:T(8,128)(2,1)S(1)} %get-tuple-element.73), channel_id=1, source_target_pairs={{0,8},{4,12},{8,0},{12,4},{1,9},{5,13},{9,1},{13,5},{2,10},{6,14},... | collective-permute-start | bytes 196616 | tf_op jit(solution)/shard_map/ppermute | solution.py:483
  40.1 2.3 %collective-permute-start.9 = (bf16[64,512]{1,0:T(8,128)(2,1)S(1)}, bf16[64,512]{1,0:T(8,128)(2,1)S(1)}, u32[]{:S(2)}, u32[]{:S(2)}) collective-permute-start(bf16[64,512]{1,0:T(8,128)(2,1)S(1)} %get-tuple-element.74), channel_id=1, source_target_pairs={{0,12},{4,8},{8,4},{12,0},{1,13},{5,9},{9,5},{13,1},{2,14},{6,10},... | collective-permute-start | bytes 196616 | tf_op jit(solution)/shard_map/ppermute | solution.py:483
  42.4 6.9 %collective-permute-start.5 = (bf16[512,256]{1,0:T(8,128)(2,1)S(1)}, bf16[512,256]{1,0:T(8,128)(2,1)S(1)}, u32[]{:S(2)}, u32[]{:S(2)}) collective-permute-start(bf16[512,256]{1,0:T(8,128)(2,1)S(1)} %get-tuple-element.69), channel_id=1, source_target_pairs={{0,4},{4,0},{8,12},{12,8},{1,5},{5,1},{9,13},{13,9},{2,6},{6,2},{1... | collective-permute-start | bytes 786440 | tf_op jit(solution)/shard_map/ppermute | solution.py:483
  49.3 1.3 %collective-permute-done.8.refs_2_ = bf16[64,512]{1,0:T(8,128)(2,1)S(1)} collective-permute-done((bf16[64,512]{1,0:T(8,128)(2,1)S(1)}, bf16[64,512]{1,0:T(8,128)(2,1)S(1)}, u32[]{:S(2)}, u32[]{:S(2)}) %collective-permute-start.8) | collective-permute-done | bytes 65568 | tf_op jit(solution)/shard_map/ppermute | solution.py:483
  50.7 1.0 %shard_map.118 = (bf16[1024,256]{1,0:T(8,128)(2,1)S(1)}, bf16[1024,256]{1,0:T(8,128)(2,1)S(1)}, bf16[512,1024]{1,0:T(8,128)(2,1)S(1)}) custom-call(f32[1024,512]{1,0:T(8,128)S(1)} %get-tuple-element.71.refs_0_, bf16[768,256]{1,0:T(8,128)(2,1)S(1)} %collective-permute-done.7.refs_1_, bf16[64,512]{1,0:T(8,128)(2,1)S(1)} %collective-permute-done.8.refs_2_, ...), custom_call_target="tpu_custom_call" | custom-call | flops 2070000000 | bytes 1 | tf_op jit(solution)/shard_map/pallas_call | solution.py:42
  51.7 0.5 shard_map.119.refs_2_.refs_3_.refs_0_
  52.4 0.3 shard_map.121
  52.7 5.9 %collective-permute-start.12 = (bf16[512,256]{1,0:T(8,128)(2,1)S(1)}, bf16[512,256]{1,0:T(8,128)(2,1)S(1)}, u32[]{:S(2)}, u32[]{:S(2)}) collective-permute-start(bf16[512,256]{1,0:T(8,128)(2,1)S(1)} %get-tuple-element.83), channel_id=1, source_target_pairs={{0,4},{4,0},{8,12},{12,8},{1,5},{5,1},{9,13},{13,9},{2,6},{6,2},{1... | collective-permute-start | bytes 786440 | tf_op jit(solution)/shard_map/ppermute | solution.py:483
  58.6 0.7 shard_map.123
  59.5 0.5 shard_map.124.refs_2_.refs_3_.refs_0_
  60.0 0.5 shard_map.125.refs_2_.refs_3_.refs_0_
  60.5 0.5 shard_map.126.refs_7_.refs_3_.refs_0_
  61.0 0.5 copy-done.4
  61.7 1.8 %shard_map.127 = (bf16[1024,512]{1,0:T(8,128)(2,1)S(1)}, bf16[1024,512]{1,0:T(8,128)(2,1)S(1)}) custom-call(s32[1]{0:T(128)} %bitcast.refs_4_.refs_0_, bf16[1024,256]{1,0:T(8,128)(2,1)S(1)} %get-tuple-element.67.refs_2_.refs_1_, bf16[1024,256]{1,0:T(8,128)(2,1)S(1)} %get-tuple-element.77.refs_2_, bf16[1024,256]{1,0:T(8,128)(2,1)S(1)} %get-tuple-element.81.refs_3_, ...), custom_call_target="tpu_custom_call" | custom-call | flops 1150000000 | bytes 1 | tf_op jit(solution)/shard_map/pallas_call | solution.py:42
  63.8 0.6 collective-permute-start.16
  64.4 1.9 %collective-permute-start.18 = (bf16[512,256]{1,0:T(8,128)(2,1)S(1)}, bf16[512,256]{1,0:T(8,128)(2,1)S(1)}, u32[]{:S(2)}, u32[]{:S(2)}) collective-permute-start(bf16[512,256]{1,0:T(8,128)(2,1)S(1)} %get-tuple-element.90), channel_id=1, source_target_pairs={{0,4},{4,0},{8,12},{12,8},{1,5},{5,1},{9,13},{13,9},{2,6},{6,2},{1... | collective-permute-start | bytes 786440 | tf_op jit(solution)/shard_map/ppermute | solution.py:483
  66.3 0.7 collective-permute-done.11.refs_2_
  67.1 7.4 %collective-permute-start.15 = (bf16[512,256]{1,0:T(8,128)(2,1)S(1)}, bf16[512,256]{1,0:T(8,128)(2,1)S(1)}, u32[]{:S(2)}, u32[]{:S(2)}) collective-permute-start(bf16[512,256]{1,0:T(8,128)(2,1)S(1)} %get-tuple-element.89), channel_id=1, source_target_pairs={{0,4},{4,0},{8,12},{12,8},{1,5},{5,1},{9,13},{13,9},{2,6},{6,2},{1... | collective-permute-start | bytes 786440 | tf_op jit(solution)/shard_map/ppermute | solution.py:483
  74.5 0.2 shard_map.132
  74.7 1.6 %collective-permute-start.14 = (bf16[1024,256]{1,0:T(8,128)(2,1)S(1)}, bf16[1024,256]{1,0:T(8,128)(2,1)S(1)}, u32[]{:S(2)}, u32[]{:S(2)}) collective-permute-start(bf16[1024,256]{1,0:T(8,128)(2,1)S(1)} %get-tuple-element.88), channel_id=1, source_target_pairs={{0,2},{1,3},{2,0},{3,1},{4,6},{5,7},{6,4},{7,5},{8,10},{9,11},{10,... | collective-permute-start | bytes 1572872 | tf_op jit(solution)/shard_map/ppermute | solution.py:483
  76.6 3.6 %collective-permute-start.20 = (bf16[512,256]{1,0:T(8,128)(2,1)S(1)}, bf16[512,256]{1,0:T(8,128)(2,1)S(1)}, u32[]{:S(2)}, u32[]{:S(2)}) collective-permute-start(bf16[512,256]{1,0:T(8,128)(2,1)S(1)} %get-tuple-element.93), channel_id=1, source_target_pairs={{0,4},{4,0},{8,12},{12,8},{1,5},{5,1},{9,13},{13,9},{2,6},{6,2},{1... | collective-permute-start | bytes 786440 | tf_op jit(solution)/shard_map/ppermute | solution.py:483
  80.1 0.2 shard_map.135
  80.5 0.8 shard_map.137
  81.4 4.4 %collective-permute-start.24 = (bf16[512,256]{1,0:T(8,128)(2,1)S(1)}, bf16[512,256]{1,0:T(8,128)(2,1)S(1)}, u32[]{:S(2)}, u32[]{:S(2)}) collective-permute-start(bf16[512,256]{1,0:T(8,128)(2,1)S(1)} %shard_map.138.refs_2_), channel_id=1, source_target_pairs={{0,4},{4,0},{8,12},{12,8},{1,5},{5,1},{9,13},{13,9},{2,6},{6,2},{1... | collective-permute-start | bytes 786440 | tf_op jit(solution)/shard_map/ppermute | solution.py:483
  85.8 1.4 %collective-permute-start.22 = (bf16[1024,256]{1,0:T(8,128)(2,1)S(1)}, bf16[1024,256]{1,0:T(8,128)(2,1)S(1)}, u32[]{:S(2)}, u32[]{:S(2)}) collective-permute-start(bf16[1024,256]{1,0:T(8,128)(2,1)S(1)} %get-tuple-element.97), channel_id=1, source_target_pairs={{0,2},{1,3},{2,0},{3,1},{4,6},{5,7},{6,4},{7,5},{8,10},{9,11},{10,... | collective-permute-start | bytes 1572872 | tf_op jit(solution)/shard_map/ppermute | solution.py:483
  87.3 0.8 shard_map.140
  88.3 3.2 %collective-permute-start.25 = (bf16[512,256]{1,0:T(8,128)(2,1)S(1)}, bf16[512,256]{1,0:T(8,128)(2,1)S(1)}, u32[]{:S(2)}, u32[]{:S(2)}) collective-permute-start(bf16[512,256]{1,0:T(8,128)(2,1)S(1)} %shard_map.141.refs_2_.refs_1_), channel_id=1, source_target_pairs={{0,4},{4,0},{8,12},{12,8},{1,5},{5,1},{9,13},{13,9},{2,6},{6,2},{1... | collective-permute-start | bytes 786440 | tf_op jit(solution)/shard_map/ppermute | solution.py:483
  91.5 0.9 shard_map.142
  92.4 0.8 shard_map.143
  93.3 3.2 %collective-permute-start.26 = (bf16[512,256]{1,0:T(8,128)(2,1)S(1)}, bf16[512,256]{1,0:T(8,128)(2,1)S(1)}, u32[]{:S(2)}, u32[]{:S(2)}) collective-permute-start(bf16[512,256]{1,0:T(8,128)(2,1)S(1)} %shard_map.144.refs_2_), channel_id=1, source_target_pairs={{0,4},{4,0},{8,12},{12,8},{1,5},{5,1},{9,13},{13,9},{2,6},{6,2},{1... | collective-permute-start | bytes 786440 | tf_op jit(solution)/shard_map/ppermute | solution.py:483
  96.5 2.3 %collective-permute-done.22.refs_1_ = bf16[1024,256]{1,0:T(8,128)(2,1)S(1)} collective-permute-done((bf16[1024,256]{1,0:T(8,128)(2,1)S(1)}, bf16[1024,256]{1,0:T(8,128)(2,1)S(1)}, u32[]{:S(2)}, u32[]{:S(2)}) %collective-permute-start.22) | collective-permute-done | bytes 524320 | tf_op jit(solution)/shard_map/ppermute | solution.py:483
  98.8 0.9 shard_map.145
  99.7 2.9 %collective-permute-done.26.refs_4_ = bf16[512,256]{1,0:T(8,128)(2,1)S(1)} collective-permute-done((bf16[512,256]{1,0:T(8,128)(2,1)S(1)}, bf16[512,256]{1,0:T(8,128)(2,1)S(1)}, u32[]{:S(2)}, u32[]{:S(2)}) %collective-permute-start.26) | collective-permute-done | bytes 262176 | tf_op jit(solution)/shard_map/ppermute | solution.py:483
  102.6 0.8 shard_map.146
  (62 shorter events, 2.1 us)
Async XLA Ops:
  0.6 11.1 %copy-start = (bf16[1024,1024]{1,0:T(8,128)(2,1)S(1)}, bf16[1024,1024]{1,0:T(8,128)(2,1)}, u32[]{:S(2)}) copy-start(bf16[1024,1024]{1,0:T(8,128)(2,1)} %refs_1_.15) | copy-start | bytes 6291460
  0.7 11.1 %copy-start.3 = (bf16[1024,256]{1,0:T(8,128)(2,1)S(1)}, bf16[1024,256]{1,0:T(8,128)(2,1)}, u32[]{:S(2)}) copy-start(bf16[1024,256]{1,0:T(8,128)(2,1)} %refs_4_.3) | copy-start | bytes 1572868
  6.0 6.4 %copy-start.6 = (bf16[1024,512]{1,0:T(8,128)(2,1)S(1)}, bf16[1024,512]{1,0:T(8,128)(2,1)}, u32[]{:S(2)}) copy-start(bf16[1024,512]{1,0:T(8,128)(2,1)} %get-tuple-element.56.refs_1_.refs_3_.refs_5_) | copy-start | bytes 3145732
  6.0 6.4 %copy-start.7 = (bf16[512,512]{1,0:T(8,128)(2,1)S(1)}, bf16[512,512]{1,0:T(8,128)(2,1)}, u32[]{:S(2)}) copy-start(bf16[512,512]{1,0:T(8,128)(2,1)} %get-tuple-element.57.refs_2_.refs_4_.refs_6_) | copy-start | bytes 1572868
  6.0 6.4 %copy-start.8 = (bf16[256,512]{1,0:T(8,128)(2,1)S(1)}, bf16[256,512]{1,0:T(8,128)(2,1)}, u32[]{:S(2)}) copy-start(bf16[256,512]{1,0:T(8,128)(2,1)} %get-tuple-element.58.refs_3_.refs_5_.refs_7_) | copy-start | bytes 786436
  6.0 9.5 %collective-permute-start.1 = (bf16[64,512]{1,0:T(8,128)(2,1)}, bf16[64,512]{1,0:T(8,128)(2,1)S(1)}, u32[]{:S(2)}, u32[]{:S(2)}) collective-permute-start(bf16[64,512]{1,0:T(8,128)(2,1)} %get-tuple-element.62), channel_id=1, source_target_pairs={{0,8},{4,12},{8,0},{12,4},{1,9},{5,13},{9,1},{13,5},{2,10},{6,14},... | collective-permute-start | bytes 196616 | tf_op jit(solution)/shard_map/ppermute | solution.py:483
  10.1 7.0 %collective-permute-start.2 = (bf16[64,512]{1,0:T(8,128)(2,1)}, bf16[64,512]{1,0:T(8,128)(2,1)S(1)}, u32[]{:S(2)}, u32[]{:S(2)}) collective-permute-start(bf16[64,512]{1,0:T(8,128)(2,1)} %get-tuple-element.62), channel_id=1, source_target_pairs={{0,12},{4,8},{8,4},{12,0},{1,13},{5,9},{9,5},{13,1},{2,14},{6,10},... | collective-permute-start | bytes 196616 | tf_op jit(solution)/shard_map/ppermute | solution.py:483
  11.5 6.4 %collective-permute-start = (bf16[128,512]{1,0:T(8,128)(2,1)}, bf16[128,512]{1,0:T(8,128)(2,1)S(1)}, u32[]{:S(2)}, u32[]{:S(2)}) collective-permute-start(bf16[128,512]{1,0:T(8,128)(2,1)} %get-tuple-element.61), channel_id=1, source_target_pairs={{0,4},{4,0},{8,12},{12,8},{1,5},{5,1},{9,13},{13,9},{2,6},{6,2},{1... | collective-permute-start | bytes 393224 | tf_op jit(solution)/shard_map/ppermute | solution.py:483
  12.5 2.4 %copy-start.1 = (bf16[1024,1024]{1,0:T(8,128)(2,1)S(1)}, bf16[1024,1024]{1,0:T(8,128)(2,1)}, u32[]{:S(2)}) copy-start(bf16[1024,1024]{1,0:T(8,128)(2,1)} %refs_1_.11) | copy-start | bytes 6291460
  12.5 2.4 %copy-start.2 = (bf16[1024,256]{1,0:T(8,128)(2,1)S(1)}, bf16[1024,256]{1,0:T(8,128)(2,1)}, u32[]{:S(2)}) copy-start(bf16[1024,256]{1,0:T(8,128)(2,1)} %refs_2_.3) | copy-start | bytes 1572868
  22.6 14.9 %collective-permute-start.3 = (bf16[1024,256]{1,0:T(8,128)(2,1)S(1)}, bf16[1024,256]{1,0:T(8,128)(2,1)S(1)}, u32[]{:S(2)}, u32[]{:S(2)}) collective-permute-start(bf16[1024,256]{1,0:T(8,128)(2,1)S(1)} %shard_map.114.refs_11_.refs_0_), channel_id=1, source_target_pairs={{0,4},{4,0},{8,12},{12,8},{1,5},{5,1},{9,13},{13,9},{2,6},{6,2},{1... | collective-permute-start | bytes 1572872 | tf_op jit(solution)/shard_map/ppermute | solution.py:483
  30.5 20.2 %collective-permute-start.7 = (bf16[768,256]{1,0:T(8,128)(2,1)S(1)}, bf16[768,256]{1,0:T(8,128)(2,1)S(1)}, u32[]{:S(2)}, u32[]{:S(2)}) collective-permute-start(bf16[768,256]{1,0:T(8,128)(2,1)S(1)} %get-tuple-element.72.refs_0_), channel_id=1, source_target_pairs={{0,4},{4,0},{8,12},{12,8},{1,5},{5,1},{9,13},{13,9},{2,6},{6,2},{1... | collective-permute-start | bytes 1179656 | tf_op jit(solution)/shard_map/ppermute | solution.py:483
  37.6 4.7 %collective-permute-start.4 = (bf16[512,256]{1,0:T(8,128)(2,1)S(1)}, bf16[512,256]{1,0:T(8,128)(2,1)S(1)}, u32[]{:S(2)}, u32[]{:S(2)}) collective-permute-start(bf16[512,256]{1,0:T(8,128)(2,1)S(1)} %get-tuple-element.68.refs_1_.refs_4_), channel_id=1, source_target_pairs={{0,1},{1,0},{2,3},{3,2},{4,8},{5,9},{6,10},{7,11},{8,4},{9,5},{10,... | collective-permute-start | bytes 786440 | tf_op jit(solution)/shard_map/ppermute | solution.py:660
  37.7 13.0 %collective-permute-start.8 = (bf16[64,512]{1,0:T(8,128)(2,1)S(1)}, bf16[64,512]{1,0:T(8,128)(2,1)S(1)}, u32[]{:S(2)}, u32[]{:S(2)}) collective-permute-start(bf16[64,512]{1,0:T(8,128)(2,1)S(1)} %get-tuple-element.73), channel_id=1, source_target_pairs={{0,8},{4,12},{8,0},{12,4},{1,9},{5,13},{9,1},{13,5},{2,10},{6,14},... | collective-permute-start | bytes 196616 | tf_op jit(solution)/shard_map/ppermute | solution.py:483
  40.1 10.6 %collective-permute-start.9 = (bf16[64,512]{1,0:T(8,128)(2,1)S(1)}, bf16[64,512]{1,0:T(8,128)(2,1)S(1)}, u32[]{:S(2)}, u32[]{:S(2)}) collective-permute-start(bf16[64,512]{1,0:T(8,128)(2,1)S(1)} %get-tuple-element.74), channel_id=1, source_target_pairs={{0,12},{4,8},{8,4},{12,0},{1,13},{5,9},{9,5},{13,1},{2,14},{6,10},... | collective-permute-start | bytes 196616 | tf_op jit(solution)/shard_map/ppermute | solution.py:483
  42.3 10.1 %collective-permute-start.6 = (bf16[512,256]{1,0:T(8,128)(2,1)S(1)}, bf16[512,256]{1,0:T(8,128)(2,1)S(1)}, u32[]{:S(2)}, u32[]{:S(2)}) collective-permute-start(bf16[512,256]{1,0:T(8,128)(2,1)S(1)} %get-tuple-element.70.refs_1_), channel_id=1, source_target_pairs={{0,1},{1,0},{2,3},{3,2},{4,8},{5,9},{6,10},{7,11},{8,4},{9,5},{10,... | collective-permute-start | bytes 786440 | tf_op jit(solution)/shard_map/ppermute | solution.py:660
  42.4 16.2 %collective-permute-start.5 = (bf16[512,256]{1,0:T(8,128)(2,1)S(1)}, bf16[512,256]{1,0:T(8,128)(2,1)S(1)}, u32[]{:S(2)}, u32[]{:S(2)}) collective-permute-start(bf16[512,256]{1,0:T(8,128)(2,1)S(1)} %get-tuple-element.69), channel_id=1, source_target_pairs={{0,4},{4,0},{8,12},{12,8},{1,5},{5,1},{9,13},{13,9},{2,6},{6,2},{1... | collective-permute-start | bytes 786440 | tf_op jit(solution)/shard_map/ppermute | solution.py:483
  52.3 11.3 %collective-permute-start.13 = (bf16[512,256]{1,0:T(8,128)(2,1)S(1)}, bf16[512,256]{1,0:T(8,128)(2,1)S(1)}, u32[]{:S(2)}, u32[]{:S(2)}) collective-permute-start(bf16[512,256]{1,0:T(8,128)(2,1)S(1)} %shard_map.120.refs_4_.refs_1_), channel_id=1, source_target_pairs={{0,1},{1,0},{2,3},{3,2},{4,8},{5,9},{6,10},{7,11},{8,4},{9,5},{10,... | collective-permute-start | bytes 786440 | tf_op jit(solution)/shard_map/ppermute | solution.py:666
  52.7 11.0 %collective-permute-start.12 = (bf16[512,256]{1,0:T(8,128)(2,1)S(1)}, bf16[512,256]{1,0:T(8,128)(2,1)S(1)}, u32[]{:S(2)}, u32[]{:S(2)}) collective-permute-start(bf16[512,256]{1,0:T(8,128)(2,1)S(1)} %get-tuple-element.83), channel_id=1, source_target_pairs={{0,4},{4,0},{8,12},{12,8},{1,5},{5,1},{9,13},{13,9},{2,6},{6,2},{1... | collective-permute-start | bytes 786440 | tf_op jit(solution)/shard_map/ppermute | solution.py:483
  59.4 15.1 %collective-permute-start.10 = (bf16[1024,512]{1,0:T(8,128)(2,1)S(1)}, bf16[1024,512]{1,0:T(8,128)(2,1)S(1)}, u32[]{:S(2)}, u32[]{:S(2)}) collective-permute-start(bf16[1024,512]{1,0:T(8,128)(2,1)S(1)} %get-tuple-element.80), channel_id=1, source_target_pairs={{0,1},{1,0},{2,3},{3,2},{4,5},{5,4},{6,7},{7,6},{8,9},{9,8},{10,11... | collective-permute-start | bytes 3145736 | tf_op jit(solution)/shard_map/ppermute | solution.py:483
  60.5 1.0 %copy-start.4 = (bf16[1024,256]{1,0:T(8,128)(2,1)S(1)}, bf16[1024,256]{1,0:T(8,128)(2,1)}, u32[]{:S(2)}) copy-start(bf16[1024,256]{1,0:T(8,128)(2,1)} %refs_5_.1) | copy-start | bytes 1572868
  60.5 1.2 %copy-start.5 = (bf16[1024,256]{1,0:T(8,128)(2,1)S(1)}, bf16[1024,256]{1,0:T(8,128)(2,1)}, u32[]{:S(2)}) copy-start(bf16[1024,256]{1,0:T(8,128)(2,1)} %refs_6_.1) | copy-start | bytes 1572868
  63.8 16.3 %collective-permute-start.16 = (bf16[1024,512]{1,0:T(8,128)(2,1)S(1)}, bf16[1024,512]{1,0:T(8,128)(2,1)S(1)}, u32[]{:S(2)}, u32[]{:S(2)}) collective-permute-start(bf16[1024,512]{1,0:T(8,128)(2,1)S(1)} %shard_map.130.refs_4_), channel_id=1, source_target_pairs={{0,1},{1,0},{2,3},{3,2},{4,5},{5,4},{6,7},{7,6},{8,9},{9,8},{10,11... | collective-permute-start | bytes 3145736 | tf_op jit(solution)/shard_map/ppermute | solution.py:483
  64.4 2.7 %collective-permute-start.11 = (bf16[512,256]{1,0:T(8,128)(2,1)S(1)}, bf16[512,256]{1,0:T(8,128)(2,1)S(1)}, u32[]{:S(2)}, u32[]{:S(2)}) collective-permute-start(bf16[512,256]{1,0:T(8,128)(2,1)S(1)} %shard_map.122.refs_3_.refs_1_), channel_id=1, source_target_pairs={{0,1},{1,0},{2,3},{3,2},{4,8},{5,9},{6,10},{7,11},{8,4},{9,5},{10,... | collective-permute-start | bytes 786440 | tf_op jit(solution)/shard_map/ppermute | solution.py:666
  64.4 11.9 %collective-permute-start.18 = (bf16[512,256]{1,0:T(8,128)(2,1)S(1)}, bf16[512,256]{1,0:T(8,128)(2,1)S(1)}, u32[]{:S(2)}, u32[]{:S(2)}) collective-permute-start(bf16[512,256]{1,0:T(8,128)(2,1)S(1)} %get-tuple-element.90), channel_id=1, source_target_pairs={{0,4},{4,0},{8,12},{12,8},{1,5},{5,1},{9,13},{13,9},{2,6},{6,2},{1... | collective-permute-start | bytes 786440 | tf_op jit(solution)/shard_map/ppermute | solution.py:483
  66.3 10.1 %collective-permute-start.17 = (bf16[512,256]{1,0:T(8,128)(2,1)S(1)}, bf16[512,256]{1,0:T(8,128)(2,1)S(1)}, u32[]{:S(2)}, u32[]{:S(2)}) collective-permute-start(bf16[512,256]{1,0:T(8,128)(2,1)S(1)} %shard_map.129.refs_1_), channel_id=1, source_target_pairs={{0,1},{1,0},{2,3},{3,2},{4,8},{5,9},{6,10},{7,11},{8,4},{9,5},{10,... | collective-permute-start | bytes 786440 | tf_op jit(solution)/shard_map/ppermute | solution.py:666
  67.1 13.2 %collective-permute-start.15 = (bf16[512,256]{1,0:T(8,128)(2,1)S(1)}, bf16[512,256]{1,0:T(8,128)(2,1)S(1)}, u32[]{:S(2)}, u32[]{:S(2)}) collective-permute-start(bf16[512,256]{1,0:T(8,128)(2,1)S(1)} %get-tuple-element.89), channel_id=1, source_target_pairs={{0,4},{4,0},{8,12},{12,8},{1,5},{5,1},{9,13},{13,9},{2,6},{6,2},{1... | collective-permute-start | bytes 786440 | tf_op jit(solution)/shard_map/ppermute | solution.py:483
  74.7 16.7 %collective-permute-start.14 = (bf16[1024,256]{1,0:T(8,128)(2,1)S(1)}, bf16[1024,256]{1,0:T(8,128)(2,1)S(1)}, u32[]{:S(2)}, u32[]{:S(2)}) collective-permute-start(bf16[1024,256]{1,0:T(8,128)(2,1)S(1)} %get-tuple-element.88), channel_id=1, source_target_pairs={{0,2},{1,3},{2,0},{3,1},{4,6},{5,7},{6,4},{7,5},{8,10},{9,11},{10,... | collective-permute-start | bytes 1572872 | tf_op jit(solution)/shard_map/ppermute | solution.py:483
  76.4 5.0 %collective-permute-start.21 = (bf16[512,256]{1,0:T(8,128)(2,1)S(1)}, bf16[512,256]{1,0:T(8,128)(2,1)S(1)}, u32[]{:S(2)}, u32[]{:S(2)}) collective-permute-start(bf16[512,256]{1,0:T(8,128)(2,1)S(1)} %shard_map.133.refs_4_.refs_0_), channel_id=1, source_target_pairs={{0,1},{1,0},{2,3},{3,2},{4,8},{5,9},{6,10},{7,11},{8,4},{9,5},{10,... | collective-permute-start | bytes 786440 | tf_op jit(solution)/shard_map/ppermute | solution.py:666
  76.6 10.6 %collective-permute-start.20 = (bf16[512,256]{1,0:T(8,128)(2,1)S(1)}, bf16[512,256]{1,0:T(8,128)(2,1)S(1)}, u32[]{:S(2)}, u32[]{:S(2)}) collective-permute-start(bf16[512,256]{1,0:T(8,128)(2,1)S(1)} %get-tuple-element.93), channel_id=1, source_target_pairs={{0,4},{4,0},{8,12},{12,8},{1,5},{5,1},{9,13},{13,9},{2,6},{6,2},{1... | collective-permute-start | bytes 786440 | tf_op jit(solution)/shard_map/ppermute | solution.py:483
  80.4 7.8 %collective-permute-start.19 = (bf16[512,256]{1,0:T(8,128)(2,1)S(1)}, bf16[512,256]{1,0:T(8,128)(2,1)S(1)}, u32[]{:S(2)}, u32[]{:S(2)}) collective-permute-start(bf16[512,256]{1,0:T(8,128)(2,1)S(1)} %shard_map.136.refs_5_.refs_0_), channel_id=1, source_target_pairs={{0,1},{1,0},{2,3},{3,2},{4,8},{5,9},{6,10},{7,11},{8,4},{9,5},{10,... | collective-permute-start | bytes 786440 | tf_op jit(solution)/shard_map/ppermute | solution.py:666
  81.4 10.9 %collective-permute-start.24 = (bf16[512,256]{1,0:T(8,128)(2,1)S(1)}, bf16[512,256]{1,0:T(8,128)(2,1)S(1)}, u32[]{:S(2)}, u32[]{:S(2)}) collective-permute-start(bf16[512,256]{1,0:T(8,128)(2,1)S(1)} %shard_map.138.refs_2_), channel_id=1, source_target_pairs={{0,4},{4,0},{8,12},{12,8},{1,5},{5,1},{9,13},{13,9},{2,6},{6,2},{1... | collective-permute-start | bytes 786440 | tf_op jit(solution)/shard_map/ppermute | solution.py:483
  85.8 13.0 %collective-permute-start.22 = (bf16[1024,256]{1,0:T(8,128)(2,1)S(1)}, bf16[1024,256]{1,0:T(8,128)(2,1)S(1)}, u32[]{:S(2)}, u32[]{:S(2)}) collective-permute-start(bf16[1024,256]{1,0:T(8,128)(2,1)S(1)} %get-tuple-element.97), channel_id=1, source_target_pairs={{0,2},{1,3},{2,0},{3,1},{4,6},{5,7},{6,4},{7,5},{8,10},{9,11},{10,... | collective-permute-start | bytes 1572872 | tf_op jit(solution)/shard_map/ppermute | solution.py:483
  87.3 5.9 %collective-permute-start.23 = (bf16[512,256]{1,0:T(8,128)(2,1)S(1)}, bf16[512,256]{1,0:T(8,128)(2,1)S(1)}, u32[]{:S(2)}, u32[]{:S(2)}) collective-permute-start(bf16[512,256]{1,0:T(8,128)(2,1)S(1)} %shard_map.139.refs_5_.refs_0_), channel_id=1, source_target_pairs={{0,1},{1,0},{2,3},{3,2},{4,8},{5,9},{6,10},{7,11},{8,4},{9,5},{10,... | collective-permute-start | bytes 786440 | tf_op jit(solution)/shard_map/ppermute | solution.py:666
  88.3 11.4 %collective-permute-start.25 = (bf16[512,256]{1,0:T(8,128)(2,1)S(1)}, bf16[512,256]{1,0:T(8,128)(2,1)S(1)}, u32[]{:S(2)}, u32[]{:S(2)}) collective-permute-start(bf16[512,256]{1,0:T(8,128)(2,1)S(1)} %shard_map.141.refs_2_.refs_1_), channel_id=1, source_target_pairs={{0,4},{4,0},{8,12},{12,8},{1,5},{5,1},{9,13},{13,9},{2,6},{6,2},{1... | collective-permute-start | bytes 786440 | tf_op jit(solution)/shard_map/ppermute | solution.py:483
  93.3 9.4 %collective-permute-start.26 = (bf16[512,256]{1,0:T(8,128)(2,1)S(1)}, bf16[512,256]{1,0:T(8,128)(2,1)S(1)}, u32[]{:S(2)}, u32[]{:S(2)}) collective-permute-start(bf16[512,256]{1,0:T(8,128)(2,1)S(1)} %shard_map.144.refs_2_), channel_id=1, source_target_pairs={{0,4},{4,0},{8,12},{12,8},{1,5},{5,1},{9,13},{13,9},{2,6},{6,2},{1... | collective-permute-start | bytes 786440 | tf_op jit(solution)/shard_map/ppermute | solution.py:483

commit v8 on v7

--- a/solution.py
+++ b/solution.py
@@ -503,25 +503,6 @@
     )
 
 
-def pair_half_body(chunk_ref, into_ref, *out_refs):
-    rows = out_refs[0].shape[0]
-    for i, ref in enumerate(out_refs):
-        here = slice(i * rows, (i + 1) * rows)
-        ref[...] = (chunk_ref[here, :].astype(F32) + into_ref[here, :].astype(F32)).astype(BF16)
-
-
-def half_sums(chunk, into, count, after):
-    rows = chunk.shape[0] // count
-    return run(
-        pair_half_body,
-        [chunk, into],
-        after,
-        out_shape=[shape(rows, chunk.shape[1])] * count,
-        compiler_params=params(3),
-        cost_estimate=cost(0.2),
-    )
-
-
 def scatter_body(pieces, keep_ref, into_ref, even_ref, odd_ref):
     width = keep_ref.shape[1] // pieces
     for i in range(pieces):
@@ -649,16 +630,6 @@
         self.chunks.append(chunk)
         self.into.append(exchange(chunk, self.axis, 1))
 
-    def enter_whole(self, whole, count):
-        self.whole = whole, exchange(whole, self.axis, 1), count
-        self.chunks += [None] * count
-        self.into += [None] * count
-
-    def meet_whole(self):
-        for half in self.step(half_sums, *self.whole):
-            self.halves.append(half)
-            self.crossed.append(lax.ppermute(half, self.axes, self.across))
-
     def meet(self, rows):
         k = len(self.halves)
         half = self.step(half_sum, self.chunks[k], self.into[k], rows)
@@ -737,13 +708,15 @@
     line = Line("seq", "head", end, step)
     pieces = 2
     rows = tokens.shape[1] // pieces
-    line.enter_whole(step(weight_terms, attended_t, cotangent, inner, 0, 0, 1), pieces)
+    line.enter(step(weight_terms, attended_t, cotangent, inner, 0, 0, pieces))
+    line.enter(step(weight_terms, attended_t, cotangent, inner, 0, 1, pieces))
     dquery, dkv, query_first, query_second, *away = step(
         backward, query, grad, attended_t, stats, tokens, levels, fars, far_bits, pieces
     )
     line.enter(query_first)
     backs = [exchange(piece, "seq", d) for d, piece in enumerate(away, 2)]
-    line.meet_whole()
+    line.meet(rows)
+    line.meet(rows)
     line.turn(query_second)
     dkey, dvalue, dkv_t = step(
         close_keys, dkv, [line.into[2], *backs], far_bits, local_levels
@@ -760,8 +733,8 @@
     keep, send = step(project_split, rank, [dquery, dkey, dvalue], [w_query, w_key, w_value], "head")
     line.turn(key_second)
     line.meet(rows)
+    line.turn(value_first)
     tokens_grad = Scatter([keep, step(relay, send)], "head", step)
-    line.turn(value_first)
     mixed.advance()
     line.meet(rows)
     line.turn(value_second)

time: 104 us -> 104 us (level)
  waiting for transfers between devices: 15.4 us -> 26.7 us
  starting transfers between devices: 52.9 us -> 42 us
    ppermute x19 -> x20, waiting for transfers between devices: 14.7 us -> 26.7 us  [exchange(): return lax.ppermute(block, axis, [(i, i ^ distance) for i in range(count)])]
    ppermute x19 -> x20, starting transfers between devices: 52.4 us -> 41.4 us  [exchange(): return lax.ppermute(block, axis, [(i, i ^ distance) for i in range(count)])]
    pallas_call x38 -> x40, Pallas kernels: 33.4 us -> 33.7 us  [run(): return pl.pallas_call(kernel, in_specs=in_specs, **options)(*ready, *after)]
  transfers between devices with their start and end apart: 27 -> 28, of which waited for: 7 -> 9; matrix products, arithmetic and copies ran while one was open for 0% -> 0% of each run, Pallas kernels for 22% -> 22%
where the time goes in v8:
time: 104 us
  starting transfers between devices  42 us (40%)
  Pallas kernels  33.7 us (32%)
  waiting for transfers between devices  26.7 us (26%)
  between operations  1.09 us (1%)
    ppermute x20, starting transfers between devices, exchange(): return lax.ppermute(block, axis, [(i, i ^ distance) for i in range(count)])  41.4 us
    pallas_call x40, Pallas kernels, run(): return pl.pallas_call(kernel, in_specs=in_specs, **options)(*ready, *after)  33.7 us
    ppermute x20, waiting for transfers between devices, exchange(): return lax.ppermute(block, axis, [(i, i ^ distance) for i in range(count)])  26.7 us
  transfers between devices with their start and end apart: 28, of which 9 were waited for; matrix products, arithmetic and copies ran while one was open for 0% of the time, Pallas kernels for 22%

profile of v8, /device:TPU:0, one launch (start us, length us, event | category | flops | bytes accessed | tf_op | source)
XLA Modules:
  0.0 104.2 jit_solution(2274077185180584425)
XLA Ops:
  0.7 5.3 %shard_map.110 = (bf16[1024,512]{1,0:T(8,128)(2,1)}, bf16[512,512]{1,0:T(8,128)(2,1)}, bf16[256,512]{1,0:T(8,128)(2,1)}, bf16[128,512]{1,0:T(8,128)(2,1)}, bf16[64,512]{1,0:T(8,128)(2,1)}) custom-call(bf16[1024,1024]{1,0:T(8,128)(2,1)} %refs_1_.17, bf16[1024,256]{1,0:T(8,128)(2,1)} %refs_5_.1, bf16[1024,256]{1,0:T(8,128)(2,1)} %refs_6_.1, ...), custom_call_target="tpu_custom_call" | custom-call | flops 5750000128 | bytes 1 | tf_op jit(solution)/shard_map/pallas_call | solution.py:42
  6.0 4.1 %collective-permute-start.1 = (bf16[64,512]{1,0:T(8,128)(2,1)}, bf16[64,512]{1,0:T(8,128)(2,1)S(1)}, u32[]{:S(2)}, u32[]{:S(2)}) collective-permute-start(bf16[64,512]{1,0:T(8,128)(2,1)} %get-tuple-element.60), channel_id=1, source_target_pairs={{0,8},{4,12},{8,0},{12,4},{1,9},{5,13},{9,1},{13,5},{2,10},{6,14},... | collective-permute-start | bytes 196616 | tf_op jit(solution)/shard_map/ppermute | solution.py:483
  10.1 1.3 %collective-permute-start.2 = (bf16[64,512]{1,0:T(8,128)(2,1)}, bf16[64,512]{1,0:T(8,128)(2,1)S(1)}, u32[]{:S(2)}, u32[]{:S(2)}) collective-permute-start(bf16[64,512]{1,0:T(8,128)(2,1)} %get-tuple-element.60), channel_id=1, source_target_pairs={{0,12},{4,8},{8,4},{12,0},{1,13},{5,9},{9,5},{13,1},{2,14},{6,10},... | collective-permute-start | bytes 196616 | tf_op jit(solution)/shard_map/ppermute | solution.py:483
  11.7 0.7 shard_map.109.refs_0_.refs_4_
  12.5 2.3 %shard_map.111 = (f32[4096,256]{1,0:T(8,128)S(1)}, f32[4,1024]{1,0:T(4,128)S(1)}) custom-call(bf16[1024,256]{1,0:T(8,128)(2,1)S(1)} %shard_map.109.refs_0_.refs_4_, bf16[1024,512]{1,0:T(8,128)(2,1)S(1)} %copy-done.6, bf16[512,512]{1,0:T(8,128)(2,1)S(1)} %copy-done.7, bf16[256,512]{1,0:T(8,128)(2,1)S(1)} %copy-done.8, ...), custom_call_target="tpu_custom_call" | custom-call | flops 2644999936 | bytes 1 | tf_op jit(solution)/shard_map/pallas_call | solution.py:42
  14.9 0.7 shard_map.112.refs_9_.refs_1_
  15.6 1.5 %collective-permute-done.2.refs_8_.refs_10_ = bf16[64,512]{1,0:T(8,128)(2,1)S(1)} collective-permute-done((bf16[64,512]{1,0:T(8,128)(2,1)}, bf16[64,512]{1,0:T(8,128)(2,1)S(1)}, u32[]{:S(2)}, u32[]{:S(2)}) %collective-permute-start.2) | collective-permute-done | bytes 65568 | tf_op jit(solution)/shard_map/ppermute | solution.py:483
  17.1 0.8 collective-permute-done.refs_6_.refs_8_
  17.9 3.9 %shard_map.113 = (bf16[1024,256]{1,0:T(8,128)(2,1)S(1)}, bf16[256,1024]{1,0:T(8,128)(2,1)S(1)}, f32[4,1024]{1,0:T(4,128)S(1)}) custom-call(bf16[1024,256]{1,0:T(8,128)(2,1)S(1)} %shard_map.109.refs_0_.refs_4_, f32[4096,256]{1,0:T(8,128)S(1)} %get-tuple-element.57.refs_2_.refs_1_, f32[4,1024]{1,0:T(4,128)S(1)} %get-tuple-element.58.refs_2_, ...), custom_call_target="tpu_custom_call" | custom-call | flops 4600000000 | bytes 1 | tf_op jit(solution)/shard_map/pallas_call | solution.py:42
  21.8 0.5 shard_map.114.refs_2_.refs_0_
  22.3 0.5 shard_map.115.refs_11_.refs_0_
  22.8 1.0 collective-permute-start.3
  23.8 6.9 %shard_map.116 = (bf16[1024,256]{1,0:T(8,128)(2,1)S(1)}, f32[1024,512]{1,0:T(8,128)S(1)}, bf16[768,256]{1,0:T(8,128)(2,1)S(1)}, bf16[512,256]{1,0:T(8,128)(2,1)S...) custom-call(bf16[1024,256]{1,0:T(8,128)(2,1)S(1)} %shard_map.109.refs_0_.refs_4_, ...), custom_call_target="tpu_custom_call" | custom-call | flops 9200000000 | bytes 1 | tf_op jit(solution)/shard_map/pallas_call | solution.py:42
  30.7 1.2 %collective-permute-start.8 = (bf16[768,256]{1,0:T(8,128)(2,1)S(1)}, bf16[768,256]{1,0:T(8,128)(2,1)S(1)}, u32[]{:S(2)}, u32[]{:S(2)}) collective-permute-start(bf16[768,256]{1,0:T(8,128)(2,1)S(1)} %get-tuple-element.68.refs_0_), channel_id=1, source_target_pairs={{0,4},{4,0},{8,12},{12,8},{1,5},{5,1},{9,13},{13,9},{2,6},{6,2},{1... | collective-permute-start | bytes 1179656 | tf_op jit(solution)/shard_map/ppermute | solution.py:483
  31.9 0.9 collective-permute-start.5
  33.0 2.4 %collective-permute-start.10 = (bf16[64,512]{1,0:T(8,128)(2,1)S(1)}, bf16[64,512]{1,0:T(8,128)(2,1)S(1)}, u32[]{:S(2)}, u32[]{:S(2)}) collective-permute-start(bf16[64,512]{1,0:T(8,128)(2,1)S(1)} %get-tuple-element.70), channel_id=1, source_target_pairs={{0,12},{4,8},{8,4},{12,0},{1,13},{5,9},{9,5},{13,1},{2,14},{6,10},... | collective-permute-start | bytes 196616 | tf_op jit(solution)/shard_map/ppermute | solution.py:483
  35.4 2.4 %collective-permute-start.9 = (bf16[64,512]{1,0:T(8,128)(2,1)S(1)}, bf16[64,512]{1,0:T(8,128)(2,1)S(1)}, u32[]{:S(2)}, u32[]{:S(2)}) collective-permute-start(bf16[64,512]{1,0:T(8,128)(2,1)S(1)} %get-tuple-element.69), channel_id=1, source_target_pairs={{0,8},{4,12},{8,0},{12,4},{1,9},{5,13},{9,1},{13,5},{2,10},{6,14},... | collective-permute-start | bytes 196616 | tf_op jit(solution)/shard_map/ppermute | solution.py:483
  37.8 10.8 %collective-permute-done.5.refs_1_ = bf16[512,256]{1,0:T(8,128)(2,1)S(1)} collective-permute-done((bf16[512,256]{1,0:T(8,128)(2,1)S(1)}, bf16[512,256]{1,0:T(8,128)(2,1)S(1)}, u32[]{:S(2)}, u32[]{:S(2)}) %collective-permute-start.5) | collective-permute-done | bytes 262176 | tf_op jit(solution)/shard_map/ppermute | solution.py:483
  48.9 2.8 %collective-permute-start.6 = (bf16[512,256]{1,0:T(8,128)(2,1)S(1)}, bf16[512,256]{1,0:T(8,128)(2,1)S(1)}, u32[]{:S(2)}, u32[]{:S(2)}) collective-permute-start(bf16[512,256]{1,0:T(8,128)(2,1)S(1)} %get-tuple-element.66), channel_id=1, source_target_pairs={{0,4},{4,0},{8,12},{12,8},{1,5},{5,1},{9,13},{13,9},{2,6},{6,2},{1... | collective-permute-start | bytes 786440 | tf_op jit(solution)/shard_map/ppermute | solution.py:483
  51.7 1.0 shard_map.120
  52.7 0.5 shard_map.121.refs_2_.refs_3_.refs_0_
  53.7 4.1 %collective-permute-start.13 = (bf16[512,256]{1,0:T(8,128)(2,1)S(1)}, bf16[512,256]{1,0:T(8,128)(2,1)S(1)}, u32[]{:S(2)}, u32[]{:S(2)}) collective-permute-start(bf16[512,256]{1,0:T(8,128)(2,1)S(1)} %get-tuple-element.79), channel_id=1, source_target_pairs={{0,4},{4,0},{8,12},{12,8},{1,5},{5,1},{9,13},{13,9},{2,6},{6,2},{1... | collective-permute-start | bytes 786440 | tf_op jit(solution)/shard_map/ppermute | solution.py:483
  57.8 0.5 collective-permute-done.6.refs_1_.refs_3_
  58.4 0.7 shard_map.125
  59.3 0.5 shard_map.126.refs_2_.refs_3_.refs_0_
  59.8 0.6 collective-permute-start.11
  60.4 0.5 shard_map.127.refs_2_.refs_3_.refs_0_
  60.9 0.5 shard_map.128.refs_7_.refs_3_.refs_0_
  62.1 1.8 %shard_map.129 = (bf16[1024,512]{1,0:T(8,128)(2,1)S(1)}, bf16[1024,512]{1,0:T(8,128)(2,1)S(1)}) custom-call(s32[1]{0:T(128)} %bitcast.refs_4_.refs_0_, bf16[1024,256]{1,0:T(8,128)(2,1)S(1)} %get-tuple-element.65.refs_2_.refs_1_, bf16[1024,256]{1,0:T(8,128)(2,1)S(1)} %get-tuple-element.73.refs_2_, bf16[1024,256]{1,0:T(8,128)(2,1)S(1)} %get-tuple-element.77.refs_3_, ...), custom_call_target="tpu_custom_call" | custom-call | flops 1150000000 | bytes 1 | tf_op jit(solution)/shard_map/pallas_call | solution.py:42
  64.4 4.1 %collective-permute-start.19 = (bf16[512,256]{1,0:T(8,128)(2,1)S(1)}, bf16[512,256]{1,0:T(8,128)(2,1)S(1)}, u32[]{:S(2)}, u32[]{:S(2)}) collective-permute-start(bf16[512,256]{1,0:T(8,128)(2,1)S(1)} %get-tuple-element.86), channel_id=1, source_target_pairs={{0,4},{4,0},{8,12},{12,8},{1,5},{5,1},{9,13},{13,9},{2,6},{6,2},{1... | collective-permute-start | bytes 786440 | tf_op jit(solution)/shard_map/ppermute | solution.py:483
  68.6 1.0 collective-permute-start.16
  69.8 1.6 %collective-permute-start.15 = (bf16[1024,256]{1,0:T(8,128)(2,1)S(1)}, bf16[1024,256]{1,0:T(8,128)(2,1)S(1)}, u32[]{:S(2)}, u32[]{:S(2)}) collective-permute-start(bf16[1024,256]{1,0:T(8,128)(2,1)S(1)} %get-tuple-element.84), channel_id=1, source_target_pairs={{0,2},{1,3},{2,0},{3,1},{4,6},{5,7},{6,4},{7,5},{8,10},{9,11},{10,... | collective-permute-start | bytes 1572872 | tf_op jit(solution)/shard_map/ppermute | solution.py:483
  71.3 4.2 %collective-permute-done.19.refs_1_.refs_3_ = bf16[512,256]{1,0:T(8,128)(2,1)S(1)} collective-permute-done((bf16[512,256]{1,0:T(8,128)(2,1)S(1)}, bf16[512,256]{1,0:T(8,128)(2,1)S(1)}, u32[]{:S(2)}, u32[]{:S(2)}) %collective-permute-start.19) | collective-permute-done | bytes 262176 | tf_op jit(solution)/shard_map/ppermute | solution.py:483
  75.8 3.0 %collective-permute-start.21 = (bf16[512,256]{1,0:T(8,128)(2,1)S(1)}, bf16[512,256]{1,0:T(8,128)(2,1)S(1)}, u32[]{:S(2)}, u32[]{:S(2)}) collective-permute-start(bf16[512,256]{1,0:T(8,128)(2,1)S(1)} %get-tuple-element.89), channel_id=1, source_target_pairs={{0,4},{4,0},{8,12},{12,8},{1,5},{5,1},{9,13},{13,9},{2,6},{6,2},{1... | collective-permute-start | bytes 786440 | tf_op jit(solution)/shard_map/ppermute | solution.py:483
  79.1 2.1 %collective-permute-done.16.refs_1_.refs_4_ = bf16[512,256]{1,0:T(8,128)(2,1)S(1)} collective-permute-done((bf16[512,256]{1,0:T(8,128)(2,1)S(1)}, bf16[512,256]{1,0:T(8,128)(2,1)S(1)}, u32[]{:S(2)}, u32[]{:S(2)}) %collective-permute-start.16) | collective-permute-done | bytes 262176 | tf_op jit(solution)/shard_map/ppermute | solution.py:483
  81.3 0.8 shard_map.139
  82.3 3.0 %collective-permute-start.25 = (bf16[512,256]{1,0:T(8,128)(2,1)S(1)}, bf16[512,256]{1,0:T(8,128)(2,1)S(1)}, u32[]{:S(2)}, u32[]{:S(2)}) collective-permute-start(bf16[512,256]{1,0:T(8,128)(2,1)S(1)} %shard_map.140.refs_2_), channel_id=1, source_target_pairs={{0,4},{4,0},{8,12},{12,8},{1,5},{5,1},{9,13},{13,9},{2,6},{6,2},{1... | collective-permute-start | bytes 786440 | tf_op jit(solution)/shard_map/ppermute | solution.py:483
  85.3 1.5 %collective-permute-start.23 = (bf16[1024,256]{1,0:T(8,128)(2,1)S(1)}, bf16[1024,256]{1,0:T(8,128)(2,1)S(1)}, u32[]{:S(2)}, u32[]{:S(2)}) collective-permute-start(bf16[1024,256]{1,0:T(8,128)(2,1)S(1)} %get-tuple-element.93), channel_id=1, source_target_pairs={{0,2},{1,3},{2,0},{3,1},{4,6},{5,7},{6,4},{7,5},{8,10},{9,11},{10,... | collective-permute-start | bytes 1572872 | tf_op jit(solution)/shard_map/ppermute | solution.py:483
  87.0 0.8 shard_map.142
  87.9 3.0 %collective-permute-start.26 = (bf16[512,256]{1,0:T(8,128)(2,1)S(1)}, bf16[512,256]{1,0:T(8,128)(2,1)S(1)}, u32[]{:S(2)}, u32[]{:S(2)}) collective-permute-start(bf16[512,256]{1,0:T(8,128)(2,1)S(1)} %shard_map.143.refs_2_.refs_1_), channel_id=1, source_target_pairs={{0,4},{4,0},{8,12},{12,8},{1,5},{5,1},{9,13},{13,9},{2,6},{6,2},{1... | collective-permute-start | bytes 786440 | tf_op jit(solution)/shard_map/ppermute | solution.py:483
  90.9 0.9 shard_map.144
  91.8 0.7 collective-permute-done.25.refs_4_
  92.5 0.8 shard_map.145
  93.4 3.0 %collective-permute-start.27 = (bf16[512,256]{1,0:T(8,128)(2,1)S(1)}, bf16[512,256]{1,0:T(8,128)(2,1)S(1)}, u32[]{:S(2)}, u32[]{:S(2)}) collective-permute-start(bf16[512,256]{1,0:T(8,128)(2,1)S(1)} %shard_map.146.refs_2_), channel_id=1, source_target_pairs={{0,4},{4,0},{8,12},{12,8},{1,5},{5,1},{9,13},{13,9},{2,6},{6,2},{1... | collective-permute-start | bytes 786440 | tf_op jit(solution)/shard_map/ppermute | solution.py:483
  96.5 1.3 %collective-permute-done.23.refs_1_ = bf16[1024,256]{1,0:T(8,128)(2,1)S(1)} collective-permute-done((bf16[1024,256]{1,0:T(8,128)(2,1)S(1)}, bf16[1024,256]{1,0:T(8,128)(2,1)S(1)}, u32[]{:S(2)}, u32[]{:S(2)}) %collective-permute-start.23) | collective-permute-done | bytes 524320 | tf_op jit(solution)/shard_map/ppermute | solution.py:483
  97.8 0.9 shard_map.147
  98.7 4.7 %collective-permute-done.27.refs_4_ = bf16[512,256]{1,0:T(8,128)(2,1)S(1)} collective-permute-done((bf16[512,256]{1,0:T(8,128)(2,1)S(1)}, bf16[512,256]{1,0:T(8,128)(2,1)S(1)}, u32[]{:S(2)}, u32[]{:S(2)}) %collective-permute-start.27) | collective-permute-done | bytes 262176 | tf_op jit(solution)/shard_map/ppermute | solution.py:483
  103.4 0.8 shard_map.148
  (66 shorter events, 3.7 us)
Async XLA Ops:
  0.6 11.1 %copy-start = (bf16[1024,1024]{1,0:T(8,128)(2,1)S(1)}, bf16[1024,1024]{1,0:T(8,128)(2,1)}, u32[]{:S(2)}) copy-start(bf16[1024,1024]{1,0:T(8,128)(2,1)} %refs_1_.17) | copy-start | bytes 6291460
  0.7 11.1 %copy-start.3 = (bf16[1024,256]{1,0:T(8,128)(2,1)S(1)}, bf16[1024,256]{1,0:T(8,128)(2,1)}, u32[]{:S(2)}) copy-start(bf16[1024,256]{1,0:T(8,128)(2,1)} %refs_4_.3) | copy-start | bytes 1572868
  6.0 6.4 %copy-start.6 = (bf16[1024,512]{1,0:T(8,128)(2,1)S(1)}, bf16[1024,512]{1,0:T(8,128)(2,1)}, u32[]{:S(2)}) copy-start(bf16[1024,512]{1,0:T(8,128)(2,1)} %get-tuple-element.54.refs_1_.refs_3_.refs_5_) | copy-start | bytes 3145732
  6.0 6.4 %copy-start.7 = (bf16[512,512]{1,0:T(8,128)(2,1)S(1)}, bf16[512,512]{1,0:T(8,128)(2,1)}, u32[]{:S(2)}) copy-start(bf16[512,512]{1,0:T(8,128)(2,1)} %get-tuple-element.55.refs_2_.refs_4_.refs_6_) | copy-start | bytes 1572868
  6.0 6.4 %copy-start.8 = (bf16[256,512]{1,0:T(8,128)(2,1)S(1)}, bf16[256,512]{1,0:T(8,128)(2,1)}, u32[]{:S(2)}) copy-start(bf16[256,512]{1,0:T(8,128)(2,1)} %get-tuple-element.56.refs_3_.refs_5_.refs_7_) | copy-start | bytes 786436
  6.0 9.5 %collective-permute-start.1 = (bf16[64,512]{1,0:T(8,128)(2,1)}, bf16[64,512]{1,0:T(8,128)(2,1)S(1)}, u32[]{:S(2)}, u32[]{:S(2)}) collective-permute-start(bf16[64,512]{1,0:T(8,128)(2,1)} %get-tuple-element.60), channel_id=1, source_target_pairs={{0,8},{4,12},{8,0},{12,4},{1,9},{5,13},{9,1},{13,5},{2,10},{6,14},... | collective-permute-start | bytes 196616 | tf_op jit(solution)/shard_map/ppermute | solution.py:483
  10.1 7.0 %collective-permute-start.2 = (bf16[64,512]{1,0:T(8,128)(2,1)}, bf16[64,512]{1,0:T(8,128)(2,1)S(1)}, u32[]{:S(2)}, u32[]{:S(2)}) collective-permute-start(bf16[64,512]{1,0:T(8,128)(2,1)} %get-tuple-element.60), channel_id=1, source_target_pairs={{0,12},{4,8},{8,4},{12,0},{1,13},{5,9},{9,5},{13,1},{2,14},{6,10},... | collective-permute-start | bytes 196616 | tf_op jit(solution)/shard_map/ppermute | solution.py:483
  11.5 6.4 %collective-permute-start = (bf16[128,512]{1,0:T(8,128)(2,1)}, bf16[128,512]{1,0:T(8,128)(2,1)S(1)}, u32[]{:S(2)}, u32[]{:S(2)}) collective-permute-start(bf16[128,512]{1,0:T(8,128)(2,1)} %get-tuple-element.59), channel_id=1, source_target_pairs={{0,4},{4,0},{8,12},{12,8},{1,5},{5,1},{9,13},{13,9},{2,6},{6,2},{1... | collective-permute-start | bytes 393224 | tf_op jit(solution)/shard_map/ppermute | solution.py:483
  12.5 2.4 %copy-start.1 = (bf16[1024,1024]{1,0:T(8,128)(2,1)S(1)}, bf16[1024,1024]{1,0:T(8,128)(2,1)}, u32[]{:S(2)}) copy-start(bf16[1024,1024]{1,0:T(8,128)(2,1)} %refs_1_.13) | copy-start | bytes 6291460
  12.5 2.4 %copy-start.2 = (bf16[1024,256]{1,0:T(8,128)(2,1)S(1)}, bf16[1024,256]{1,0:T(8,128)(2,1)}, u32[]{:S(2)}) copy-start(bf16[1024,256]{1,0:T(8,128)(2,1)} %refs_2_.3) | copy-start | bytes 1572868
  22.8 10.0 %collective-permute-start.3 = (bf16[512,256]{1,0:T(8,128)(2,1)S(1)}, bf16[512,256]{1,0:T(8,128)(2,1)S(1)}, u32[]{:S(2)}, u32[]{:S(2)}) collective-permute-start(bf16[512,256]{1,0:T(8,128)(2,1)S(1)} %shard_map.114.refs_2_.refs_0_), channel_id=1, source_target_pairs={{0,4},{4,0},{8,12},{12,8},{1,5},{5,1},{9,13},{13,9},{2,6},{6,2},{1... | collective-permute-start | bytes 786440 | tf_op jit(solution)/shard_map/ppermute | solution.py:483
  30.7 20.9 %collective-permute-start.8 = (bf16[768,256]{1,0:T(8,128)(2,1)S(1)}, bf16[768,256]{1,0:T(8,128)(2,1)S(1)}, u32[]{:S(2)}, u32[]{:S(2)}) collective-permute-start(bf16[768,256]{1,0:T(8,128)(2,1)S(1)} %get-tuple-element.68.refs_0_), channel_id=1, source_target_pairs={{0,4},{4,0},{8,12},{12,8},{1,5},{5,1},{9,13},{13,9},{2,6},{6,2},{1... | collective-permute-start | bytes 1179656 | tf_op jit(solution)/shard_map/ppermute | solution.py:483
  31.9 16.7 %collective-permute-start.5 = (bf16[512,256]{1,0:T(8,128)(2,1)S(1)}, bf16[512,256]{1,0:T(8,128)(2,1)S(1)}, u32[]{:S(2)}, u32[]{:S(2)}) collective-permute-start(bf16[512,256]{1,0:T(8,128)(2,1)S(1)} %shard_map.115.refs_11_.refs_0_), channel_id=1, source_target_pairs={{0,4},{4,0},{8,12},{12,8},{1,5},{5,1},{9,13},{13,9},{2,6},{6,2},{1... | collective-permute-start | bytes 786440 | tf_op jit(solution)/shard_map/ppermute | solution.py:483
  32.9 15.9 %collective-permute-start.4 = (bf16[512,256]{1,0:T(8,128)(2,1)S(1)}, bf16[512,256]{1,0:T(8,128)(2,1)S(1)}, u32[]{:S(2)}, u32[]{:S(2)}) collective-permute-start(bf16[512,256]{1,0:T(8,128)(2,1)S(1)} %shard_map.117.refs_2_.refs_1_), channel_id=1, source_target_pairs={{0,1},{1,0},{2,3},{3,2},{4,8},{5,9},{6,10},{7,11},{8,4},{9,5},{10,... | collective-permute-start | bytes 786440 | tf_op jit(solution)/shard_map/ppermute | solution.py:637
  33.0 18.7 %collective-permute-start.10 = (bf16[64,512]{1,0:T(8,128)(2,1)S(1)}, bf16[64,512]{1,0:T(8,128)(2,1)S(1)}, u32[]{:S(2)}, u32[]{:S(2)}) collective-permute-start(bf16[64,512]{1,0:T(8,128)(2,1)S(1)} %get-tuple-element.70), channel_id=1, source_target_pairs={{0,12},{4,8},{8,4},{12,0},{1,13},{5,9},{9,5},{13,1},{2,14},{6,10},... | collective-permute-start | bytes 196616 | tf_op jit(solution)/shard_map/ppermute | solution.py:483
  35.4 16.3 %collective-permute-start.9 = (bf16[64,512]{1,0:T(8,128)(2,1)S(1)}, bf16[64,512]{1,0:T(8,128)(2,1)S(1)}, u32[]{:S(2)}, u32[]{:S(2)}) collective-permute-start(bf16[64,512]{1,0:T(8,128)(2,1)S(1)} %get-tuple-element.69), channel_id=1, source_target_pairs={{0,8},{4,12},{8,0},{12,4},{1,9},{5,13},{9,1},{13,5},{2,10},{6,14},... | collective-permute-start | bytes 196616 | tf_op jit(solution)/shard_map/ppermute | solution.py:483
  48.7 4.7 %collective-permute-start.7 = (bf16[512,256]{1,0:T(8,128)(2,1)S(1)}, bf16[512,256]{1,0:T(8,128)(2,1)S(1)}, u32[]{:S(2)}, u32[]{:S(2)}) collective-permute-start(bf16[512,256]{1,0:T(8,128)(2,1)S(1)} %shard_map.118.refs_4_.refs_1_), channel_id=1, source_target_pairs={{0,1},{1,0},{2,3},{3,2},{4,8},{5,9},{6,10},{7,11},{8,4},{9,5},{10,... | collective-permute-start | bytes 786440 | tf_op jit(solution)/shard_map/ppermute | solution.py:637
  48.9 9.5 %collective-permute-start.6 = (bf16[512,256]{1,0:T(8,128)(2,1)S(1)}, bf16[512,256]{1,0:T(8,128)(2,1)S(1)}, u32[]{:S(2)}, u32[]{:S(2)}) collective-permute-start(bf16[512,256]{1,0:T(8,128)(2,1)S(1)} %get-tuple-element.66), channel_id=1, source_target_pairs={{0,4},{4,0},{8,12},{12,8},{1,5},{5,1},{9,13},{13,9},{2,6},{6,2},{1... | collective-permute-start | bytes 786440 | tf_op jit(solution)/shard_map/ppermute | solution.py:483
  53.3 10.6 %collective-permute-start.14 = (bf16[512,256]{1,0:T(8,128)(2,1)S(1)}, bf16[512,256]{1,0:T(8,128)(2,1)S(1)}, u32[]{:S(2)}, u32[]{:S(2)}) collective-permute-start(bf16[512,256]{1,0:T(8,128)(2,1)S(1)} %shard_map.122.refs_4_.refs_1_), channel_id=1, source_target_pairs={{0,1},{1,0},{2,3},{3,2},{4,8},{5,9},{6,10},{7,11},{8,4},{9,5},{10,... | collective-permute-start | bytes 786440 | tf_op jit(solution)/shard_map/ppermute | solution.py:637
  53.7 10.3 %collective-permute-start.13 = (bf16[512,256]{1,0:T(8,128)(2,1)S(1)}, bf16[512,256]{1,0:T(8,128)(2,1)S(1)}, u32[]{:S(2)}, u32[]{:S(2)}) collective-permute-start(bf16[512,256]{1,0:T(8,128)(2,1)S(1)} %get-tuple-element.79), channel_id=1, source_target_pairs={{0,4},{4,0},{8,12},{12,8},{1,5},{5,1},{9,13},{13,9},{2,6},{6,2},{1... | collective-permute-start | bytes 786440 | tf_op jit(solution)/shard_map/ppermute | solution.py:483
  59.2 4.9 %collective-permute-start.12 = (bf16[512,256]{1,0:T(8,128)(2,1)S(1)}, bf16[512,256]{1,0:T(8,128)(2,1)S(1)}, u32[]{:S(2)}, u32[]{:S(2)}) collective-permute-start(bf16[512,256]{1,0:T(8,128)(2,1)S(1)} %shard_map.124.refs_3_.refs_1_), channel_id=1, source_target_pairs={{0,1},{1,0},{2,3},{3,2},{4,8},{5,9},{6,10},{7,11},{8,4},{9,5},{10,... | collective-permute-start | bytes 786440 | tf_op jit(solution)/shard_map/ppermute | solution.py:637
  59.8 9.7 %collective-permute-start.11 = (bf16[1024,512]{1,0:T(8,128)(2,1)S(1)}, bf16[1024,512]{1,0:T(8,128)(2,1)S(1)}, u32[]{:S(2)}, u32[]{:S(2)}) collective-permute-start(bf16[1024,512]{1,0:T(8,128)(2,1)S(1)} %get-tuple-element.76), channel_id=1, source_target_pairs={{0,1},{1,0},{2,3},{3,2},{4,5},{5,4},{6,7},{7,6},{8,9},{9,8},{10,11... | collective-permute-start | bytes 3145736 | tf_op jit(solution)/shard_map/ppermute | solution.py:483
  60.9 1.0 %copy-start.4 = (bf16[1024,256]{1,0:T(8,128)(2,1)S(1)}, bf16[1024,256]{1,0:T(8,128)(2,1)}, u32[]{:S(2)}) copy-start(bf16[1024,256]{1,0:T(8,128)(2,1)} %refs_5_.1) | copy-start | bytes 1572868
  60.9 1.2 %copy-start.5 = (bf16[1024,256]{1,0:T(8,128)(2,1)S(1)}, bf16[1024,256]{1,0:T(8,128)(2,1)}, u32[]{:S(2)}) copy-start(bf16[1024,256]{1,0:T(8,128)(2,1)} %refs_6_.1) | copy-start | bytes 1572868
  64.3 14.6 %collective-permute-start.17 = (bf16[1024,512]{1,0:T(8,128)(2,1)S(1)}, bf16[1024,512]{1,0:T(8,128)(2,1)S(1)}, u32[]{:S(2)}, u32[]{:S(2)}) collective-permute-start(bf16[1024,512]{1,0:T(8,128)(2,1)S(1)} %shard_map.133.refs_2_), channel_id=1, source_target_pairs={{0,1},{1,0},{2,3},{3,2},{4,5},{5,4},{6,7},{7,6},{8,9},{9,8},{10,11... | collective-permute-start | bytes 3145736 | tf_op jit(solution)/shard_map/ppermute | solution.py:483
  64.4 11.2 %collective-permute-start.19 = (bf16[512,256]{1,0:T(8,128)(2,1)S(1)}, bf16[512,256]{1,0:T(8,128)(2,1)S(1)}, u32[]{:S(2)}, u32[]{:S(2)}) collective-permute-start(bf16[512,256]{1,0:T(8,128)(2,1)S(1)} %get-tuple-element.86), channel_id=1, source_target_pairs={{0,4},{4,0},{8,12},{12,8},{1,5},{5,1},{9,13},{13,9},{2,6},{6,2},{1... | collective-permute-start | bytes 786440 | tf_op jit(solution)/shard_map/ppermute | solution.py:483
  68.4 7.3 %collective-permute-start.18 = (bf16[512,256]{1,0:T(8,128)(2,1)S(1)}, bf16[512,256]{1,0:T(8,128)(2,1)S(1)}, u32[]{:S(2)}, u32[]{:S(2)}) collective-permute-start(bf16[512,256]{1,0:T(8,128)(2,1)S(1)} %shard_map.131.refs_4_.refs_1_), channel_id=1, source_target_pairs={{0,1},{1,0},{2,3},{3,2},{4,8},{5,9},{6,10},{7,11},{8,4},{9,5},{10,... | collective-permute-start | bytes 786440 | tf_op jit(solution)/shard_map/ppermute | solution.py:637
  68.6 12.6 %collective-permute-start.16 = (bf16[512,256]{1,0:T(8,128)(2,1)S(1)}, bf16[512,256]{1,0:T(8,128)(2,1)S(1)}, u32[]{:S(2)}, u32[]{:S(2)}) collective-permute-start(bf16[512,256]{1,0:T(8,128)(2,1)S(1)} %get-tuple-element.85), channel_id=1, source_target_pairs={{0,4},{4,0},{8,12},{12,8},{1,5},{5,1},{9,13},{13,9},{2,6},{6,2},{1... | collective-permute-start | bytes 786440 | tf_op jit(solution)/shard_map/ppermute | solution.py:483
  69.8 21.1 %collective-permute-start.15 = (bf16[1024,256]{1,0:T(8,128)(2,1)S(1)}, bf16[1024,256]{1,0:T(8,128)(2,1)S(1)}, u32[]{:S(2)}, u32[]{:S(2)}) collective-permute-start(bf16[1024,256]{1,0:T(8,128)(2,1)S(1)} %get-tuple-element.84), channel_id=1, source_target_pairs={{0,2},{1,3},{2,0},{3,1},{4,6},{5,7},{6,4},{7,5},{8,10},{9,11},{10,... | collective-permute-start | bytes 1572872 | tf_op jit(solution)/shard_map/ppermute | solution.py:483
  75.7 6.5 %collective-permute-start.22 = (bf16[512,256]{1,0:T(8,128)(2,1)S(1)}, bf16[512,256]{1,0:T(8,128)(2,1)S(1)}, u32[]{:S(2)}, u32[]{:S(2)}) collective-permute-start(bf16[512,256]{1,0:T(8,128)(2,1)S(1)} %shard_map.135.refs_4_.refs_0_), channel_id=1, source_target_pairs={{0,1},{1,0},{2,3},{3,2},{4,8},{5,9},{6,10},{7,11},{8,4},{9,5},{10,... | collective-permute-start | bytes 786440 | tf_op jit(solution)/shard_map/ppermute | solution.py:637
  75.8 11.0 %collective-permute-start.21 = (bf16[512,256]{1,0:T(8,128)(2,1)S(1)}, bf16[512,256]{1,0:T(8,128)(2,1)S(1)}, u32[]{:S(2)}, u32[]{:S(2)}) collective-permute-start(bf16[512,256]{1,0:T(8,128)(2,1)S(1)} %get-tuple-element.89), channel_id=1, source_target_pairs={{0,4},{4,0},{8,12},{12,8},{1,5},{5,1},{9,13},{13,9},{2,6},{6,2},{1... | collective-permute-start | bytes 786440 | tf_op jit(solution)/shard_map/ppermute | solution.py:483
  81.3 6.5 %collective-permute-start.20 = (bf16[512,256]{1,0:T(8,128)(2,1)S(1)}, bf16[512,256]{1,0:T(8,128)(2,1)S(1)}, u32[]{:S(2)}, u32[]{:S(2)}) collective-permute-start(bf16[512,256]{1,0:T(8,128)(2,1)S(1)} %shard_map.138.refs_5_.refs_0_), channel_id=1, source_target_pairs={{0,1},{1,0},{2,3},{3,2},{4,8},{5,9},{6,10},{7,11},{8,4},{9,5},{10,... | collective-permute-start | bytes 786440 | tf_op jit(solution)/shard_map/ppermute | solution.py:637
  82.3 10.3 %collective-permute-start.25 = (bf16[512,256]{1,0:T(8,128)(2,1)S(1)}, bf16[512,256]{1,0:T(8,128)(2,1)S(1)}, u32[]{:S(2)}, u32[]{:S(2)}) collective-permute-start(bf16[512,256]{1,0:T(8,128)(2,1)S(1)} %shard_map.140.refs_2_), channel_id=1, source_target_pairs={{0,4},{4,0},{8,12},{12,8},{1,5},{5,1},{9,13},{13,9},{2,6},{6,2},{1... | collective-permute-start | bytes 786440 | tf_op jit(solution)/shard_map/ppermute | solution.py:483
  85.3 12.5 %collective-permute-start.23 = (bf16[1024,256]{1,0:T(8,128)(2,1)S(1)}, bf16[1024,256]{1,0:T(8,128)(2,1)S(1)}, u32[]{:S(2)}, u32[]{:S(2)}) collective-permute-start(bf16[1024,256]{1,0:T(8,128)(2,1)S(1)} %get-tuple-element.93), channel_id=1, source_target_pairs={{0,2},{1,3},{2,0},{3,1},{4,6},{5,7},{6,4},{7,5},{8,10},{9,11},{10,... | collective-permute-start | bytes 1572872 | tf_op jit(solution)/shard_map/ppermute | solution.py:483
  86.9 6.5 %collective-permute-start.24 = (bf16[512,256]{1,0:T(8,128)(2,1)S(1)}, bf16[512,256]{1,0:T(8,128)(2,1)S(1)}, u32[]{:S(2)}, u32[]{:S(2)}) collective-permute-start(bf16[512,256]{1,0:T(8,128)(2,1)S(1)} %shard_map.141.refs_5_.refs_0_), channel_id=1, source_target_pairs={{0,1},{1,0},{2,3},{3,2},{4,8},{5,9},{6,10},{7,11},{8,4},{9,5},{10,... | collective-permute-start | bytes 786440 | tf_op jit(solution)/shard_map/ppermute | solution.py:637
  87.9 10.8 %collective-permute-start.26 = (bf16[512,256]{1,0:T(8,128)(2,1)S(1)}, bf16[512,256]{1,0:T(8,128)(2,1)S(1)}, u32[]{:S(2)}, u32[]{:S(2)}) collective-permute-start(bf16[512,256]{1,0:T(8,128)(2,1)S(1)} %shard_map.143.refs_2_.refs_1_), channel_id=1, source_target_pairs={{0,4},{4,0},{8,12},{12,8},{1,5},{5,1},{9,13},{13,9},{2,6},{6,2},{1... | collective-permute-start | bytes 786440 | tf_op jit(solution)/shard_map/ppermute | solution.py:483
  93.4 10.0 %collective-permute-start.27 = (bf16[512,256]{1,0:T(8,128)(2,1)S(1)}, bf16[512,256]{1,0:T(8,128)(2,1)S(1)}, u32[]{:S(2)}, u32[]{:S(2)}) collective-permute-start(bf16[512,256]{1,0:T(8,128)(2,1)S(1)} %shard_map.146.refs_2_), channel_id=1, source_target_pairs={{0,4},{4,0},{8,12},{12,8},{1,5},{5,1},{9,13},{13,9},{2,6},{6,2},{1... | collective-permute-start | bytes 786440 | tf_op jit(solution)/shard_map/ppermute | solution.py:483

commit v9 on v8

--- a/solution.py
+++ b/solution.py
@@ -408,7 +408,7 @@
         after,
         out_shape=shape(width, inner),
         compiler_params=params(3),
-        cost_estimate=cost(0.5),
+        cost_estimate=cost(0.2),
     )
 
 
@@ -442,7 +442,7 @@
         after,
         out_shape=[shape(tok_rows, inner), shape(tok_rows, inner), shape(double, tok_rows)],
         compiler_params=params(5),
-        cost_estimate=cost(1.8),
+        cost_estimate=cost(0.2),
     )
 
 
@@ -499,7 +499,7 @@
         after,
         out_shape=shape(rows, chunk.shape[1]),
         compiler_params=params(3),
-        cost_estimate=cost(0.1),
+        cost_estimate=cost(3),
     )
 
 
@@ -562,7 +562,7 @@
         + [pl.BlockSpec(memory_space=pltpu.VMEM)] * 3,
         out_shape=[shape(*half.shape)] * 2,
         compiler_params=params(2),
-        cost_estimate=cost(0.1),
+        cost_estimate=cost(3),
     )
 
 
@@ -723,32 +723,32 @@
     )
     key_first = step(weight_terms, dkv_t, tokens, inner, 0, 0, pieces)
     line.meet(rows)
+    parts = step(project_split, rank, [attended], [w_out], "head")
+    mixed = Scatter(parts, "head", step)
     line.turn(key_first)
     line.meet(rows)
-    parts = step(project_split, rank, [attended], [w_out], "head")
-    mixed = Scatter(parts, "head", step)
     key_second = step(weight_terms, dkv_t, tokens, inner, 0, 1, pieces)
+    line.turn(key_second)
     value_first = step(weight_terms, dkv_t, tokens, inner, 1, 0, pieces)
+    keep, send = step(project_split, rank, [dquery, dkey, dvalue], [w_query, w_key, w_value], "head")
+    line.meet(rows)
+    tokens_grad = Scatter([keep, step(relay, send)], "head", step)
+    line.turn(value_first)
+    mixed.advance()
     value_second = step(weight_terms, dkv_t, tokens, inner, 1, 1, pieces)
-    keep, send = step(project_split, rank, [dquery, dkey, dvalue], [w_query, w_key, w_value], "head")
-    line.turn(key_second)
-    line.meet(rows)
-    line.turn(value_first)
-    tokens_grad = Scatter([keep, step(relay, send)], "head", step)
-    mixed.advance()
     line.meet(rows)
     line.turn(value_second)
+    out_grad = line.output(0, pieces)
+    line.meet(rows)
+    mixed = mixed.result()
+    line.leave()
     tokens_grad.advance()
-    line.meet(rows)
-    out_grad = line.output(0, pieces)
-    line.leave()
     line.meet(rows)
     query_grad = line.output(2, pieces)
     line.leave()
-    mixed = mixed.result()
     key_grad = line.output(4, pieces)
+    tokens_grad = tokens_grad.result()
     line.leave()
-    tokens_grad = tokens_grad.result()
     value_grad = line.output(6, pieces)
     return mixed, tokens_grad, query_grad, key_grad, value_grad, out_grad
 

time: 104 us -> 103 us (level)
  starting transfers between devices: 42 us -> 39 us
  waiting for transfers between devices: 26.7 us -> 29.2 us
    ppermute x20, starting transfers between devices: 41.4 us -> 38 us  [exchange(): return lax.ppermute(block, axis, [(i, i ^ distance) for i in range(count)])]
    ppermute x20, waiting for transfers between devices: 26.7 us -> 29.1 us  [exchange(): return lax.ppermute(block, axis, [(i, i ^ distance) for i in range(count)])]
  transfers between devices with their start and end apart: 28 -> 28, of which waited for: 9 -> 11; matrix products, arithmetic and copies ran while one was open for 0% -> 0% of each run, Pallas kernels for 22% -> 22%
where the time goes in v9:
time: 103 us
  starting transfers between devices  39 us (38%)
  Pallas kernels  33.7 us (33%)
  waiting for transfers between devices  29.2 us (28%)
  between operations  1.09 us (1%)
    ppermute x20, starting transfers between devices, exchange(): return lax.ppermute(block, axis, [(i, i ^ distance) for i in range(count)])  38 us
    pallas_call x40, Pallas kernels, run(): return pl.pallas_call(kernel, in_specs=in_specs, **options)(*ready, *after)  33.7 us
    ppermute x20, waiting for transfers between devices, exchange(): return lax.ppermute(block, axis, [(i, i ^ distance) for i in range(count)])  29.1 us
  transfers between devices with their start and end apart: 28, of which 11 were waited for; matrix products, arithmetic and copies ran while one was open for 0% of the time, Pallas kernels for 22%

profile of v9, /device:TPU:0, one launch (start us, length us, event | category | flops | bytes accessed | tf_op | source)
XLA Modules:
  0.0 103.0 jit_solution(17532955350714186846)
XLA Ops:
  0.7 5.3 %shard_map.110 = (bf16[1024,512]{1,0:T(8,128)(2,1)}, bf16[512,512]{1,0:T(8,128)(2,1)}, bf16[256,512]{1,0:T(8,128)(2,1)}, bf16[128,512]{1,0:T(8,128)(2,1)}, bf16[64,512]{1,0:T(8,128)(2,1)}) custom-call(bf16[1024,1024]{1,0:T(8,128)(2,1)} %refs_1_.17, bf16[1024,256]{1,0:T(8,128)(2,1)} %refs_5_.1, bf16[1024,256]{1,0:T(8,128)(2,1)} %refs_6_.1, ...), custom_call_target="tpu_custom_call" | custom-call | flops 5750000128 | bytes 1 | tf_op jit(solution)/shard_map/pallas_call | solution.py:42
  6.0 4.1 %collective-permute-start.1 = (bf16[64,512]{1,0:T(8,128)(2,1)}, bf16[64,512]{1,0:T(8,128)(2,1)S(1)}, u32[]{:S(2)}, u32[]{:S(2)}) collective-permute-start(bf16[64,512]{1,0:T(8,128)(2,1)} %get-tuple-element.60), channel_id=1, source_target_pairs={{0,8},{4,12},{8,0},{12,4},{1,9},{5,13},{9,1},{13,5},{2,10},{6,14},... | collective-permute-start | bytes 196616 | tf_op jit(solution)/shard_map/ppermute | solution.py:483
  10.1 1.3 %collective-permute-start.2 = (bf16[64,512]{1,0:T(8,128)(2,1)}, bf16[64,512]{1,0:T(8,128)(2,1)S(1)}, u32[]{:S(2)}, u32[]{:S(2)}) collective-permute-start(bf16[64,512]{1,0:T(8,128)(2,1)} %get-tuple-element.60), channel_id=1, source_target_pairs={{0,12},{4,8},{8,4},{12,0},{1,13},{5,9},{9,5},{13,1},{2,14},{6,10},... | collective-permute-start | bytes 196616 | tf_op jit(solution)/shard_map/ppermute | solution.py:483
  11.7 0.7 shard_map.109.refs_0_.refs_4_
  12.5 2.3 %shard_map.111 = (f32[4096,256]{1,0:T(8,128)S(1)}, f32[4,1024]{1,0:T(4,128)S(1)}) custom-call(bf16[1024,256]{1,0:T(8,128)(2,1)S(1)} %shard_map.109.refs_0_.refs_4_, bf16[1024,512]{1,0:T(8,128)(2,1)S(1)} %copy-done.6, bf16[512,512]{1,0:T(8,128)(2,1)S(1)} %copy-done.7, bf16[256,512]{1,0:T(8,128)(2,1)S(1)} %copy-done.8, ...), custom_call_target="tpu_custom_call" | custom-call | flops 2644999936 | bytes 1 | tf_op jit(solution)/shard_map/pallas_call | solution.py:42
  14.9 0.7 shard_map.112.refs_9_.refs_1_
  15.6 1.5 %collective-permute-done.2.refs_8_.refs_10_ = bf16[64,512]{1,0:T(8,128)(2,1)S(1)} collective-permute-done((bf16[64,512]{1,0:T(8,128)(2,1)}, bf16[64,512]{1,0:T(8,128)(2,1)S(1)}, u32[]{:S(2)}, u32[]{:S(2)}) %collective-permute-start.2) | collective-permute-done | bytes 65568 | tf_op jit(solution)/shard_map/ppermute | solution.py:483
  17.1 0.8 collective-permute-done.refs_6_.refs_8_
  17.9 3.9 %shard_map.113 = (bf16[1024,256]{1,0:T(8,128)(2,1)S(1)}, bf16[256,1024]{1,0:T(8,128)(2,1)S(1)}, f32[4,1024]{1,0:T(4,128)S(1)}) custom-call(bf16[1024,256]{1,0:T(8,128)(2,1)S(1)} %shard_map.109.refs_0_.refs_4_, f32[4096,256]{1,0:T(8,128)S(1)} %get-tuple-element.57.refs_2_.refs_1_, f32[4,1024]{1,0:T(4,128)S(1)} %get-tuple-element.58.refs_2_, ...), custom_call_target="tpu_custom_call" | custom-call | flops 4600000000 | bytes 1 | tf_op jit(solution)/shard_map/pallas_call | solution.py:42
  21.8 0.5 shard_map.114.refs_2_.refs_0_
  22.3 0.5 shard_map.115.refs_11_.refs_0_
  22.8 1.0 collective-permute-start.6
  23.8 1.1 %collective-permute-start.8 = (bf16[512,256]{1,0:T(8,128)(2,1)S(1)}, bf16[512,256]{1,0:T(8,128)(2,1)S(1)}, u32[]{:S(2)}, u32[]{:S(2)}) collective-permute-start(bf16[512,256]{1,0:T(8,128)(2,1)S(1)} %shard_map.115.refs_11_.refs_0_), channel_id=1, source_target_pairs={{0,4},{4,0},{8,12},{12,8},{1,5},{5,1},{9,13},{13,9},{2,6},{6,2},{1... | collective-permute-start | bytes 786440 | tf_op jit(solution)/shard_map/ppermute | solution.py:483
  24.9 6.9 %shard_map.116 = (bf16[1024,256]{1,0:T(8,128)(2,1)S(1)}, f32[1024,512]{1,0:T(8,128)S(1)}, bf16[768,256]{1,0:T(8,128)(2,1)S(1)}, bf16[512,256]{1,0:T(8,128)(2,1)S...) custom-call(bf16[1024,256]{1,0:T(8,128)(2,1)S(1)} %shard_map.109.refs_0_.refs_4_, ...), custom_call_target="tpu_custom_call" | custom-call | flops 9200000000 | bytes 1 | tf_op jit(solution)/shard_map/pallas_call | solution.py:42
  31.8 1.0 collective-permute-start.3
  32.8 2.8 %collective-permute-start.4 = (bf16[64,512]{1,0:T(8,128)(2,1)S(1)}, bf16[64,512]{1,0:T(8,128)(2,1)S(1)}, u32[]{:S(2)}, u32[]{:S(2)}) collective-permute-start(bf16[64,512]{1,0:T(8,128)(2,1)S(1)} %get-tuple-element.66), channel_id=1, source_target_pairs={{0,8},{4,12},{8,0},{12,4},{1,9},{5,13},{9,1},{13,5},{2,10},{6,14},... | collective-permute-start | bytes 196616 | tf_op jit(solution)/shard_map/ppermute | solution.py:483
  35.7 0.6 collective-permute-start.5
  36.4 2.7 %collective-permute-done.8.refs_1_ = bf16[512,256]{1,0:T(8,128)(2,1)S(1)} collective-permute-done((bf16[512,256]{1,0:T(8,128)(2,1)S(1)}, bf16[512,256]{1,0:T(8,128)(2,1)S(1)}, u32[]{:S(2)}, u32[]{:S(2)}) %collective-permute-start.8) | collective-permute-done | bytes 262176 | tf_op jit(solution)/shard_map/ppermute | solution.py:483
  39.4 8.3 %collective-permute-start.10 = (bf16[512,256]{1,0:T(8,128)(2,1)S(1)}, bf16[512,256]{1,0:T(8,128)(2,1)S(1)}, u32[]{:S(2)}, u32[]{:S(2)}) collective-permute-start(bf16[512,256]{1,0:T(8,128)(2,1)S(1)} %get-tuple-element.75), channel_id=1, source_target_pairs={{0,4},{4,0},{8,12},{12,8},{1,5},{5,1},{9,13},{13,9},{2,6},{6,2},{1... | collective-permute-start | bytes 786440 | tf_op jit(solution)/shard_map/ppermute | solution.py:483
  47.7 2.4 %collective-permute-done.5.refs_3_ = bf16[64,512]{1,0:T(8,128)(2,1)S(1)} collective-permute-done((bf16[64,512]{1,0:T(8,128)(2,1)S(1)}, bf16[64,512]{1,0:T(8,128)(2,1)S(1)}, u32[]{:S(2)}, u32[]{:S(2)}) %collective-permute-start.5) | collective-permute-done | bytes 65568 | tf_op jit(solution)/shard_map/ppermute | solution.py:483
  50.1 1.0 %shard_map.120 = (bf16[1024,256]{1,0:T(8,128)(2,1)S(1)}, bf16[1024,256]{1,0:T(8,128)(2,1)S(1)}, bf16[512,1024]{1,0:T(8,128)(2,1)S(1)}) custom-call(f32[1024,512]{1,0:T(8,128)S(1)} %get-tuple-element.65.refs_0_, bf16[768,256]{1,0:T(8,128)(2,1)S(1)} %collective-permute-done.3.refs_1_, bf16[64,512]{1,0:T(8,128)(2,1)S(1)} %collective-permute-done.4.refs_2_, ...), custom_call_target="tpu_custom_call" | custom-call | flops 230000000 | bytes 1 | tf_op jit(solution)/shard_map/pallas_call | solution.py:42
  51.2 0.5 shard_map.121.refs_2_.refs_3_.refs_0_
  51.8 0.7 shard_map.123
  52.7 2.3 %collective-permute-start.14 = (bf16[512,256]{1,0:T(8,128)(2,1)S(1)}, bf16[512,256]{1,0:T(8,128)(2,1)S(1)}, u32[]{:S(2)}, u32[]{:S(2)}) collective-permute-start(bf16[512,256]{1,0:T(8,128)(2,1)S(1)} %get-tuple-element.80), channel_id=1, source_target_pairs={{0,4},{4,0},{8,12},{12,8},{1,5},{5,1},{9,13},{13,9},{2,6},{6,2},{1... | collective-permute-start | bytes 786440 | tf_op jit(solution)/shard_map/ppermute | solution.py:483
  55.1 0.6 collective-permute-start.12
  55.6 0.5 shard_map.126.refs_3_.refs_4_.refs_0_
  56.5 2.9 %collective-permute-start.18 = (bf16[512,256]{1,0:T(8,128)(2,1)S(1)}, bf16[512,256]{1,0:T(8,128)(2,1)S(1)}, u32[]{:S(2)}, u32[]{:S(2)}) collective-permute-start(bf16[512,256]{1,0:T(8,128)(2,1)S(1)} %get-tuple-element.86), channel_id=1, source_target_pairs={{0,4},{4,0},{8,12},{12,8},{1,5},{5,1},{9,13},{13,9},{2,6},{6,2},{1... | collective-permute-start | bytes 786440 | tf_op jit(solution)/shard_map/ppermute | solution.py:483
  59.4 0.5 shard_map.128.refs_7_.refs_3_.refs_0_
  59.9 1.8 %shard_map.129 = (bf16[1024,512]{1,0:T(8,128)(2,1)S(1)}, bf16[1024,512]{1,0:T(8,128)(2,1)S(1)}) custom-call(s32[1]{0:T(128)} %bitcast.refs_4_.refs_0_, bf16[1024,256]{1,0:T(8,128)(2,1)S(1)} %get-tuple-element.68.refs_2_.refs_1_, bf16[1024,256]{1,0:T(8,128)(2,1)S(1)} %get-tuple-element.72.refs_2_, bf16[1024,256]{1,0:T(8,128)(2,1)S(1)} %get-tuple-element.78.refs_3_, ...), custom_call_target="tpu_custom_call" | custom-call | flops 1150000000 | bytes 1 | tf_op jit(solution)/shard_map/pallas_call | solution.py:42
  62.3 0.6 collective-permute-start.19
  63.0 2.2 %collective-permute-start.16 = (bf16[512,256]{1,0:T(8,128)(2,1)S(1)}, bf16[512,256]{1,0:T(8,128)(2,1)S(1)}, u32[]{:S(2)}, u32[]{:S(2)}) collective-permute-start(bf16[512,256]{1,0:T(8,128)(2,1)S(1)} %get-tuple-element.85), channel_id=1, source_target_pairs={{0,4},{4,0},{8,12},{12,8},{1,5},{5,1},{9,13},{13,9},{2,6},{6,2},{1... | collective-permute-start | bytes 786440 | tf_op jit(solution)/shard_map/ppermute | solution.py:483
  65.4 1.6 %collective-permute-start.15 = (bf16[1024,256]{1,0:T(8,128)(2,1)S(1)}, bf16[1024,256]{1,0:T(8,128)(2,1)S(1)}, u32[]{:S(2)}, u32[]{:S(2)}) collective-permute-start(bf16[1024,256]{1,0:T(8,128)(2,1)S(1)} %get-tuple-element.84), channel_id=1, source_target_pairs={{0,2},{1,3},{2,0},{3,1},{4,6},{5,7},{6,4},{7,5},{8,10},{9,11},{10,... | collective-permute-start | bytes 1572872 | tf_op jit(solution)/shard_map/ppermute | solution.py:483
  67.0 0.5 shard_map.134.refs_2_.refs_3_.refs_0_
  67.9 2.2 %collective-permute-start.22 = (bf16[512,256]{1,0:T(8,128)(2,1)S(1)}, bf16[512,256]{1,0:T(8,128)(2,1)S(1)}, u32[]{:S(2)}, u32[]{:S(2)}) collective-permute-start(bf16[512,256]{1,0:T(8,128)(2,1)S(1)} %get-tuple-element.93), channel_id=1, source_target_pairs={{0,4},{4,0},{8,12},{12,8},{1,5},{5,1},{9,13},{13,9},{2,6},{6,2},{1... | collective-permute-start | bytes 786440 | tf_op jit(solution)/shard_map/ppermute | solution.py:483
  70.1 0.8 shard_map.137
  70.9 2.3 %collective-permute-done.16.refs_1_.refs_4_ = bf16[512,256]{1,0:T(8,128)(2,1)S(1)} collective-permute-done((bf16[512,256]{1,0:T(8,128)(2,1)S(1)}, bf16[512,256]{1,0:T(8,128)(2,1)S(1)}, u32[]{:S(2)}, u32[]{:S(2)}) %collective-permute-start.16) | collective-permute-done | bytes 262176 | tf_op jit(solution)/shard_map/ppermute | solution.py:483
  73.4 6.1 %collective-permute-done.15.refs_1_ = bf16[1024,256]{1,0:T(8,128)(2,1)S(1)} collective-permute-done((bf16[1024,256]{1,0:T(8,128)(2,1)S(1)}, bf16[1024,256]{1,0:T(8,128)(2,1)S(1)}, u32[]{:S(2)}, u32[]{:S(2)}) %collective-permute-start.15) | collective-permute-done | bytes 524320 | tf_op jit(solution)/shard_map/ppermute | solution.py:483
  79.5 0.9 shard_map.139
  81.1 1.6 %collective-permute-start.21 = (bf16[1024,256]{1,0:T(8,128)(2,1)S(1)}, bf16[1024,256]{1,0:T(8,128)(2,1)S(1)}, u32[]{:S(2)}, u32[]{:S(2)}) collective-permute-start(bf16[1024,256]{1,0:T(8,128)(2,1)S(1)} %get-tuple-element.92), channel_id=1, source_target_pairs={{0,2},{1,3},{2,0},{3,1},{4,6},{5,7},{6,4},{7,5},{8,10},{9,11},{10,... | collective-permute-start | bytes 1572872 | tf_op jit(solution)/shard_map/ppermute | solution.py:483
  82.8 0.8 shard_map.143
  83.7 2.4 %collective-permute-start.26 = (bf16[512,256]{1,0:T(8,128)(2,1)S(1)}, bf16[512,256]{1,0:T(8,128)(2,1)S(1)}, u32[]{:S(2)}, u32[]{:S(2)}) collective-permute-start(bf16[512,256]{1,0:T(8,128)(2,1)S(1)} %shard_map.144.refs_5_.refs_1_), channel_id=1, source_target_pairs={{0,4},{4,0},{8,12},{12,8},{1,5},{5,1},{9,13},{13,9},{2,6},{6,2},{1... | collective-permute-start | bytes 786440 | tf_op jit(solution)/shard_map/ppermute | solution.py:483
  86.1 3.3 %collective-permute-done.23.refs_4_ = bf16[512,256]{1,0:T(8,128)(2,1)S(1)} collective-permute-done((bf16[512,256]{1,0:T(8,128)(2,1)S(1)}, bf16[512,256]{1,0:T(8,128)(2,1)S(1)}, u32[]{:S(2)}, u32[]{:S(2)}) %collective-permute-start.23) | collective-permute-done | bytes 262176 | tf_op jit(solution)/shard_map/ppermute | solution.py:483
  89.3 0.8 shard_map.145
  90.2 4.2 %collective-permute-done.21.refs_1_ = bf16[1024,256]{1,0:T(8,128)(2,1)S(1)} collective-permute-done((bf16[1024,256]{1,0:T(8,128)(2,1)S(1)}, bf16[1024,256]{1,0:T(8,128)(2,1)S(1)}, u32[]{:S(2)}, u32[]{:S(2)}) %collective-permute-start.21) | collective-permute-done | bytes 524320 | tf_op jit(solution)/shard_map/ppermute | solution.py:483
  94.4 0.9 shard_map.146
  95.4 1.5 %collective-permute-start.27 = (bf16[512,256]{1,0:T(8,128)(2,1)S(1)}, bf16[512,256]{1,0:T(8,128)(2,1)S(1)}, u32[]{:S(2)}, u32[]{:S(2)}) collective-permute-start(bf16[512,256]{1,0:T(8,128)(2,1)S(1)} %shard_map.147.refs_2_.refs_5_), channel_id=1, source_target_pairs={{0,4},{4,0},{8,12},{12,8},{1,5},{5,1},{9,13},{13,9},{2,6},{6,2},{1... | collective-permute-start | bytes 786440 | tf_op jit(solution)/shard_map/ppermute | solution.py:483
  96.9 5.3 %collective-permute-done.27.refs_4_ = bf16[512,256]{1,0:T(8,128)(2,1)S(1)} collective-permute-done((bf16[512,256]{1,0:T(8,128)(2,1)S(1)}, bf16[512,256]{1,0:T(8,128)(2,1)S(1)}, u32[]{:S(2)}, u32[]{:S(2)}) %collective-permute-start.27) | collective-permute-done | bytes 262176 | tf_op jit(solution)/shard_map/ppermute | solution.py:483
  102.2 0.8 shard_map.148
  (66 shorter events, 3.6 us)
Async XLA Ops:
  0.6 11.1 %copy-start = (bf16[1024,1024]{1,0:T(8,128)(2,1)S(1)}, bf16[1024,1024]{1,0:T(8,128)(2,1)}, u32[]{:S(2)}) copy-start(bf16[1024,1024]{1,0:T(8,128)(2,1)} %refs_1_.17) | copy-start | bytes 6291460
  0.7 11.1 %copy-start.3 = (bf16[1024,256]{1,0:T(8,128)(2,1)S(1)}, bf16[1024,256]{1,0:T(8,128)(2,1)}, u32[]{:S(2)}) copy-start(bf16[1024,256]{1,0:T(8,128)(2,1)} %refs_4_.3) | copy-start | bytes 1572868
  6.0 6.4 %copy-start.6 = (bf16[1024,512]{1,0:T(8,128)(2,1)S(1)}, bf16[1024,512]{1,0:T(8,128)(2,1)}, u32[]{:S(2)}) copy-start(bf16[1024,512]{1,0:T(8,128)(2,1)} %get-tuple-element.54.refs_1_.refs_3_.refs_5_) | copy-start | bytes 3145732
  6.0 6.4 %copy-start.7 = (bf16[512,512]{1,0:T(8,128)(2,1)S(1)}, bf16[512,512]{1,0:T(8,128)(2,1)}, u32[]{:S(2)}) copy-start(bf16[512,512]{1,0:T(8,128)(2,1)} %get-tuple-element.55.refs_2_.refs_4_.refs_6_) | copy-start | bytes 1572868
  6.0 6.4 %copy-start.8 = (bf16[256,512]{1,0:T(8,128)(2,1)S(1)}, bf16[256,512]{1,0:T(8,128)(2,1)}, u32[]{:S(2)}) copy-start(bf16[256,512]{1,0:T(8,128)(2,1)} %get-tuple-element.56.refs_3_.refs_5_.refs_7_) | copy-start | bytes 786436
  6.0 9.5 %collective-permute-start.1 = (bf16[64,512]{1,0:T(8,128)(2,1)}, bf16[64,512]{1,0:T(8,128)(2,1)S(1)}, u32[]{:S(2)}, u32[]{:S(2)}) collective-permute-start(bf16[64,512]{1,0:T(8,128)(2,1)} %get-tuple-element.60), channel_id=1, source_target_pairs={{0,8},{4,12},{8,0},{12,4},{1,9},{5,13},{9,1},{13,5},{2,10},{6,14},... | collective-permute-start | bytes 196616 | tf_op jit(solution)/shard_map/ppermute | solution.py:483
  10.1 7.0 %collective-permute-start.2 = (bf16[64,512]{1,0:T(8,128)(2,1)}, bf16[64,512]{1,0:T(8,128)(2,1)S(1)}, u32[]{:S(2)}, u32[]{:S(2)}) collective-permute-start(bf16[64,512]{1,0:T(8,128)(2,1)} %get-tuple-element.60), channel_id=1, source_target_pairs={{0,12},{4,8},{8,4},{12,0},{1,13},{5,9},{9,5},{13,1},{2,14},{6,10},... | collective-permute-start | bytes 196616 | tf_op jit(solution)/shard_map/ppermute | solution.py:483
  11.5 6.4 %collective-permute-start = (bf16[128,512]{1,0:T(8,128)(2,1)}, bf16[128,512]{1,0:T(8,128)(2,1)S(1)}, u32[]{:S(2)}, u32[]{:S(2)}) collective-permute-start(bf16[128,512]{1,0:T(8,128)(2,1)} %get-tuple-element.59), channel_id=1, source_target_pairs={{0,4},{4,0},{8,12},{12,8},{1,5},{5,1},{9,13},{13,9},{2,6},{6,2},{1... | collective-permute-start | bytes 393224 | tf_op jit(solution)/shard_map/ppermute | solution.py:483
  12.5 2.4 %copy-start.1 = (bf16[1024,1024]{1,0:T(8,128)(2,1)S(1)}, bf16[1024,1024]{1,0:T(8,128)(2,1)}, u32[]{:S(2)}) copy-start(bf16[1024,1024]{1,0:T(8,128)(2,1)} %refs_1_.13) | copy-start | bytes 6291460
  12.5 2.4 %copy-start.2 = (bf16[1024,256]{1,0:T(8,128)(2,1)S(1)}, bf16[1024,256]{1,0:T(8,128)(2,1)}, u32[]{:S(2)}) copy-start(bf16[1024,256]{1,0:T(8,128)(2,1)} %refs_2_.3) | copy-start | bytes 1572868
  22.8 13.5 %collective-permute-start.6 = (bf16[512,256]{1,0:T(8,128)(2,1)S(1)}, bf16[512,256]{1,0:T(8,128)(2,1)S(1)}, u32[]{:S(2)}, u32[]{:S(2)}) collective-permute-start(bf16[512,256]{1,0:T(8,128)(2,1)S(1)} %shard_map.114.refs_2_.refs_0_), channel_id=1, source_target_pairs={{0,4},{4,0},{8,12},{12,8},{1,5},{5,1},{9,13},{13,9},{2,6},{6,2},{1... | collective-permute-start | bytes 786440 | tf_op jit(solution)/shard_map/ppermute | solution.py:483
  23.8 15.3 %collective-permute-start.8 = (bf16[512,256]{1,0:T(8,128)(2,1)S(1)}, bf16[512,256]{1,0:T(8,128)(2,1)S(1)}, u32[]{:S(2)}, u32[]{:S(2)}) collective-permute-start(bf16[512,256]{1,0:T(8,128)(2,1)S(1)} %shard_map.115.refs_11_.refs_0_), channel_id=1, source_target_pairs={{0,4},{4,0},{8,12},{12,8},{1,5},{5,1},{9,13},{13,9},{2,6},{6,2},{1... | collective-permute-start | bytes 786440 | tf_op jit(solution)/shard_map/ppermute | solution.py:483
  31.8 18.3 %collective-permute-start.3 = (bf16[768,256]{1,0:T(8,128)(2,1)S(1)}, bf16[768,256]{1,0:T(8,128)(2,1)S(1)}, u32[]{:S(2)}, u32[]{:S(2)}) collective-permute-start(bf16[768,256]{1,0:T(8,128)(2,1)S(1)} %get-tuple-element.64.refs_0_), channel_id=1, source_target_pairs={{0,4},{4,0},{8,12},{12,8},{1,5},{5,1},{9,13},{13,9},{2,6},{6,2},{1... | collective-permute-start | bytes 1179656 | tf_op jit(solution)/shard_map/ppermute | solution.py:483
  32.8 14.9 %collective-permute-start.4 = (bf16[64,512]{1,0:T(8,128)(2,1)S(1)}, bf16[64,512]{1,0:T(8,128)(2,1)S(1)}, u32[]{:S(2)}, u32[]{:S(2)}) collective-permute-start(bf16[64,512]{1,0:T(8,128)(2,1)S(1)} %get-tuple-element.66), channel_id=1, source_target_pairs={{0,8},{4,12},{8,0},{12,4},{1,9},{5,13},{9,1},{13,5},{2,10},{6,14},... | collective-permute-start | bytes 196616 | tf_op jit(solution)/shard_map/ppermute | solution.py:483
  35.7 14.5 %collective-permute-start.5 = (bf16[64,512]{1,0:T(8,128)(2,1)S(1)}, bf16[64,512]{1,0:T(8,128)(2,1)S(1)}, u32[]{:S(2)}, u32[]{:S(2)}) collective-permute-start(bf16[64,512]{1,0:T(8,128)(2,1)S(1)} %get-tuple-element.67), channel_id=1, source_target_pairs={{0,12},{4,8},{8,4},{12,0},{1,13},{5,9},{9,5},{13,1},{2,14},{6,10},... | collective-permute-start | bytes 196616 | tf_op jit(solution)/shard_map/ppermute | solution.py:483
  36.4 2.9 %collective-permute-start.7 = (bf16[512,256]{1,0:T(8,128)(2,1)S(1)}, bf16[512,256]{1,0:T(8,128)(2,1)S(1)}, u32[]{:S(2)}, u32[]{:S(2)}) collective-permute-start(bf16[512,256]{1,0:T(8,128)(2,1)S(1)} %shard_map.117.refs_2_.refs_1_), channel_id=1, source_target_pairs={{0,1},{1,0},{2,3},{3,2},{4,8},{5,9},{6,10},{7,11},{8,4},{9,5},{10,... | collective-permute-start | bytes 786440 | tf_op jit(solution)/shard_map/ppermute | solution.py:637
  39.2 13.4 %collective-permute-start.11 = (bf16[512,256]{1,0:T(8,128)(2,1)S(1)}, bf16[512,256]{1,0:T(8,128)(2,1)S(1)}, u32[]{:S(2)}, u32[]{:S(2)}) collective-permute-start(bf16[512,256]{1,0:T(8,128)(2,1)S(1)} %shard_map.118.refs_4_.refs_1_), channel_id=1, source_target_pairs={{0,1},{1,0},{2,3},{3,2},{4,8},{5,9},{6,10},{7,11},{8,4},{9,5},{10,... | collective-permute-start | bytes 786440 | tf_op jit(solution)/shard_map/ppermute | solution.py:637
  39.4 15.6 %collective-permute-start.10 = (bf16[512,256]{1,0:T(8,128)(2,1)S(1)}, bf16[512,256]{1,0:T(8,128)(2,1)S(1)}, u32[]{:S(2)}, u32[]{:S(2)}) collective-permute-start(bf16[512,256]{1,0:T(8,128)(2,1)S(1)} %get-tuple-element.75), channel_id=1, source_target_pairs={{0,4},{4,0},{8,12},{12,8},{1,5},{5,1},{9,13},{13,9},{2,6},{6,2},{1... | collective-permute-start | bytes 786440 | tf_op jit(solution)/shard_map/ppermute | solution.py:483
  51.8 4.4 %collective-permute-start.13 = (bf16[512,256]{1,0:T(8,128)(2,1)S(1)}, bf16[512,256]{1,0:T(8,128)(2,1)S(1)}, u32[]{:S(2)}, u32[]{:S(2)}) collective-permute-start(bf16[512,256]{1,0:T(8,128)(2,1)S(1)} %shard_map.122.refs_3_.refs_1_), channel_id=1, source_target_pairs={{0,1},{1,0},{2,3},{3,2},{4,8},{5,9},{6,10},{7,11},{8,4},{9,5},{10,... | collective-permute-start | bytes 786440 | tf_op jit(solution)/shard_map/ppermute | solution.py:637
  52.7 9.4 %collective-permute-start.14 = (bf16[512,256]{1,0:T(8,128)(2,1)S(1)}, bf16[512,256]{1,0:T(8,128)(2,1)S(1)}, u32[]{:S(2)}, u32[]{:S(2)}) collective-permute-start(bf16[512,256]{1,0:T(8,128)(2,1)S(1)} %get-tuple-element.80), channel_id=1, source_target_pairs={{0,4},{4,0},{8,12},{12,8},{1,5},{5,1},{9,13},{13,9},{2,6},{6,2},{1... | collective-permute-start | bytes 786440 | tf_op jit(solution)/shard_map/ppermute | solution.py:483
  55.0 10.2 %collective-permute-start.9 = (bf16[1024,512]{1,0:T(8,128)(2,1)S(1)}, bf16[1024,512]{1,0:T(8,128)(2,1)S(1)}, u32[]{:S(2)}, u32[]{:S(2)}) collective-permute-start(bf16[1024,512]{1,0:T(8,128)(2,1)S(1)} %get-tuple-element.74), channel_id=1, source_target_pairs={{0,1},{1,0},{2,3},{3,2},{4,5},{5,4},{6,7},{7,6},{8,9},{9,8},{10,11... | collective-permute-start | bytes 3145736 | tf_op jit(solution)/shard_map/ppermute | solution.py:483
  55.1 7.8 %collective-permute-start.12 = (bf16[512,256]{1,0:T(8,128)(2,1)S(1)}, bf16[512,256]{1,0:T(8,128)(2,1)S(1)}, u32[]{:S(2)}, u32[]{:S(2)}) collective-permute-start(bf16[512,256]{1,0:T(8,128)(2,1)S(1)} %shard_map.125.refs_2_.refs_1_), channel_id=1, source_target_pairs={{0,1},{1,0},{2,3},{3,2},{4,8},{5,9},{6,10},{7,11},{8,4},{9,5},{10,... | collective-permute-start | bytes 786440 | tf_op jit(solution)/shard_map/ppermute | solution.py:637
  56.4 3.4 %copy-start.4 = (bf16[1024,256]{1,0:T(8,128)(2,1)S(1)}, bf16[1024,256]{1,0:T(8,128)(2,1)}, u32[]{:S(2)}) copy-start(bf16[1024,256]{1,0:T(8,128)(2,1)} %refs_5_.1) | copy-start | bytes 1572868
  56.5 3.4 %copy-start.5 = (bf16[1024,256]{1,0:T(8,128)(2,1)S(1)}, bf16[1024,256]{1,0:T(8,128)(2,1)}, u32[]{:S(2)}) copy-start(bf16[1024,256]{1,0:T(8,128)(2,1)} %refs_6_.1) | copy-start | bytes 1572868
  56.5 11.1 %collective-permute-start.18 = (bf16[512,256]{1,0:T(8,128)(2,1)S(1)}, bf16[512,256]{1,0:T(8,128)(2,1)S(1)}, u32[]{:S(2)}, u32[]{:S(2)}) collective-permute-start(bf16[512,256]{1,0:T(8,128)(2,1)S(1)} %get-tuple-element.86), channel_id=1, source_target_pairs={{0,4},{4,0},{8,12},{12,8},{1,5},{5,1},{9,13},{13,9},{2,6},{6,2},{1... | collective-permute-start | bytes 786440 | tf_op jit(solution)/shard_map/ppermute | solution.py:483
  62.2 5.6 %collective-permute-start.17 = (bf16[512,256]{1,0:T(8,128)(2,1)S(1)}, bf16[512,256]{1,0:T(8,128)(2,1)S(1)}, u32[]{:S(2)}, u32[]{:S(2)}) collective-permute-start(bf16[512,256]{1,0:T(8,128)(2,1)S(1)} %shard_map.130.refs_1_), channel_id=1, source_target_pairs={{0,1},{1,0},{2,3},{3,2},{4,8},{5,9},{6,10},{7,11},{8,4},{9,5},{10,... | collective-permute-start | bytes 786440 | tf_op jit(solution)/shard_map/ppermute | solution.py:637
  62.3 18.5 %collective-permute-start.19 = (bf16[1024,512]{1,0:T(8,128)(2,1)S(1)}, bf16[1024,512]{1,0:T(8,128)(2,1)S(1)}, u32[]{:S(2)}, u32[]{:S(2)}) collective-permute-start(bf16[1024,512]{1,0:T(8,128)(2,1)S(1)} %shard_map.131.refs_4_), channel_id=1, source_target_pairs={{0,1},{1,0},{2,3},{3,2},{4,5},{5,4},{6,7},{7,6},{8,9},{9,8},{10,11... | collective-permute-start | bytes 3145736 | tf_op jit(solution)/shard_map/ppermute | solution.py:483
  63.0 10.2 %collective-permute-start.16 = (bf16[512,256]{1,0:T(8,128)(2,1)S(1)}, bf16[512,256]{1,0:T(8,128)(2,1)S(1)}, u32[]{:S(2)}, u32[]{:S(2)}) collective-permute-start(bf16[512,256]{1,0:T(8,128)(2,1)S(1)} %get-tuple-element.85), channel_id=1, source_target_pairs={{0,4},{4,0},{8,12},{12,8},{1,5},{5,1},{9,13},{13,9},{2,6},{6,2},{1... | collective-permute-start | bytes 786440 | tf_op jit(solution)/shard_map/ppermute | solution.py:483
  65.4 14.1 %collective-permute-start.15 = (bf16[1024,256]{1,0:T(8,128)(2,1)S(1)}, bf16[1024,256]{1,0:T(8,128)(2,1)S(1)}, u32[]{:S(2)}, u32[]{:S(2)}) collective-permute-start(bf16[1024,256]{1,0:T(8,128)(2,1)S(1)} %get-tuple-element.84), channel_id=1, source_target_pairs={{0,2},{1,3},{2,0},{3,1},{4,6},{5,7},{6,4},{7,5},{8,10},{9,11},{10,... | collective-permute-start | bytes 1572872 | tf_op jit(solution)/shard_map/ppermute | solution.py:483
  67.7 12.7 %collective-permute-start.20 = (bf16[512,256]{1,0:T(8,128)(2,1)S(1)}, bf16[512,256]{1,0:T(8,128)(2,1)S(1)}, u32[]{:S(2)}, u32[]{:S(2)}) collective-permute-start(bf16[512,256]{1,0:T(8,128)(2,1)S(1)} %shard_map.135.refs_4_.refs_0_), channel_id=1, source_target_pairs={{0,1},{1,0},{2,3},{3,2},{4,8},{5,9},{6,10},{7,11},{8,4},{9,5},{10,... | collective-permute-start | bytes 786440 | tf_op jit(solution)/shard_map/ppermute | solution.py:637
  67.9 14.8 %collective-permute-start.22 = (bf16[512,256]{1,0:T(8,128)(2,1)S(1)}, bf16[512,256]{1,0:T(8,128)(2,1)S(1)}, u32[]{:S(2)}, u32[]{:S(2)}) collective-permute-start(bf16[512,256]{1,0:T(8,128)(2,1)S(1)} %get-tuple-element.93), channel_id=1, source_target_pairs={{0,4},{4,0},{8,12},{12,8},{1,5},{5,1},{9,13},{13,9},{2,6},{6,2},{1... | collective-permute-start | bytes 786440 | tf_op jit(solution)/shard_map/ppermute | solution.py:483
  73.3 10.4 %collective-permute-start.24 = (bf16[512,256]{1,0:T(8,128)(2,1)S(1)}, bf16[512,256]{1,0:T(8,128)(2,1)S(1)}, u32[]{:S(2)}, u32[]{:S(2)}) collective-permute-start(bf16[512,256]{1,0:T(8,128)(2,1)S(1)} %shard_map.138.refs_2_.refs_0_), channel_id=1, source_target_pairs={{0,1},{1,0},{2,3},{3,2},{4,8},{5,9},{6,10},{7,11},{8,4},{9,5},{10,... | collective-permute-start | bytes 786440 | tf_op jit(solution)/shard_map/ppermute | solution.py:637
  80.5 8.9 %collective-permute-start.23 = (bf16[512,256]{1,0:T(8,128)(2,1)S(1)}, bf16[512,256]{1,0:T(8,128)(2,1)S(1)}, u32[]{:S(2)}, u32[]{:S(2)}) collective-permute-start(bf16[512,256]{1,0:T(8,128)(2,1)S(1)} %shard_map.140.refs_2_), channel_id=1, source_target_pairs={{0,4},{4,0},{8,12},{12,8},{1,5},{5,1},{9,13},{13,9},{2,6},{6,2},{1... | collective-permute-start | bytes 786440 | tf_op jit(solution)/shard_map/ppermute | solution.py:483
  81.1 13.3 %collective-permute-start.21 = (bf16[1024,256]{1,0:T(8,128)(2,1)S(1)}, bf16[1024,256]{1,0:T(8,128)(2,1)S(1)}, u32[]{:S(2)}, u32[]{:S(2)}) collective-permute-start(bf16[1024,256]{1,0:T(8,128)(2,1)S(1)} %get-tuple-element.92), channel_id=1, source_target_pairs={{0,2},{1,3},{2,0},{3,1},{4,6},{5,7},{6,4},{7,5},{8,10},{9,11},{10,... | collective-permute-start | bytes 1572872 | tf_op jit(solution)/shard_map/ppermute | solution.py:483
  82.7 12.6 %collective-permute-start.25 = (bf16[512,256]{1,0:T(8,128)(2,1)S(1)}, bf16[512,256]{1,0:T(8,128)(2,1)S(1)}, u32[]{:S(2)}, u32[]{:S(2)}) collective-permute-start(bf16[512,256]{1,0:T(8,128)(2,1)S(1)} %shard_map.142.refs_5_.refs_0_), channel_id=1, source_target_pairs={{0,1},{1,0},{2,3},{3,2},{4,8},{5,9},{6,10},{7,11},{8,4},{9,5},{10,... | collective-permute-start | bytes 786440 | tf_op jit(solution)/shard_map/ppermute | solution.py:637
  83.7 13.1 %collective-permute-start.26 = (bf16[512,256]{1,0:T(8,128)(2,1)S(1)}, bf16[512,256]{1,0:T(8,128)(2,1)S(1)}, u32[]{:S(2)}, u32[]{:S(2)}) collective-permute-start(bf16[512,256]{1,0:T(8,128)(2,1)S(1)} %shard_map.144.refs_5_.refs_1_), channel_id=1, source_target_pairs={{0,4},{4,0},{8,12},{12,8},{1,5},{5,1},{9,13},{13,9},{2,6},{6,2},{1... | collective-permute-start | bytes 786440 | tf_op jit(solution)/shard_map/ppermute | solution.py:483
  95.4 6.8 %collective-permute-start.27 = (bf16[512,256]{1,0:T(8,128)(2,1)S(1)}, bf16[512,256]{1,0:T(8,128)(2,1)S(1)}, u32[]{:S(2)}, u32[]{:S(2)}) collective-permute-start(bf16[512,256]{1,0:T(8,128)(2,1)S(1)} %shard_map.147.refs_2_.refs_5_), channel_id=1, source_target_pairs={{0,4},{4,0},{8,12},{12,8},{1,5},{5,1},{9,13},{13,9},{2,6},{6,2},{1... | collective-permute-start | bytes 786440 | tf_op jit(solution)/shard_map/ppermute | solution.py:483

commit v10 on v9

--- a/solution.py
+++ b/solution.py
@@ -492,14 +492,14 @@
     out_ref[...] = (chunk_ref[rows, :].astype(F32) + into_ref[rows, :].astype(F32)).astype(BF16)
 
 
-def half_sum(chunk, into, rows, after):
+def half_sum(chunk, into, rows, weight, after):
     return run(
         term_half_body,
         [chunk, into],
         after,
         out_shape=shape(rows, chunk.shape[1]),
         compiler_params=params(3),
-        cost_estimate=cost(3),
+        cost_estimate=cost(weight),
     )
 
 
@@ -553,7 +553,7 @@
         send_ref[...] = total
 
 
-def turn(end, half, across, chunk, after):
+def turn(end, half, across, chunk, weight, after):
     return run(
         turn_body,
         [end, half, across, chunk],
@@ -562,7 +562,7 @@
         + [pl.BlockSpec(memory_space=pltpu.VMEM)] * 3,
         out_shape=[shape(*half.shape)] * 2,
         compiler_params=params(2),
-        cost_estimate=cost(3),
+        cost_estimate=cost(weight),
     )
 
 
@@ -611,6 +611,8 @@
 
 class Line:
     lag = 3
+    half_weights = (3.0, 3.0, 3.0, 2.5, 2.5, 3.0, 3.0, 3.0)
+    turn_weights = (3.0, 2.5, 2.5, 3.0, 3.0, 3.0, 3.0, 3.0)
 
     def __init__(self, axis, other, end, step):
         self.axis, self.axes, self.step = axis, (axis, other), step
@@ -632,13 +634,16 @@
 
     def meet(self, rows):
         k = len(self.halves)
-        half = self.step(half_sum, self.chunks[k], self.into[k], rows)
+        weight = self.half_weights[k]
+        half = self.step(half_sum, self.chunks[k], self.into[k], rows, weight)
         self.halves.append(half)
         self.crossed.append(lax.ppermute(half, self.axes, self.across))
 
     def turn(self, chunk):
         old = len(self.totals)
-        total, send = self.step(turn, self.end, self.halves[old], self.crossed[old], chunk)
+        half, crossed = self.halves[old], self.crossed[old]
+        weight = self.turn_weights[old]
+        total, send = self.step(turn, self.end, half, crossed, chunk, weight)
         self.totals.append(total)
         self.chunks.append(chunk)
         self.into.append(exchange(send, self.axis, 1))
@@ -646,7 +651,8 @@
     def leave(self):
         old = len(self.totals)
         half = self.halves[old]
-        total = self.step(half_sum, half, self.crossed[old], half.shape[0])
+        weight = self.turn_weights[old]
+        total = self.step(half_sum, half, self.crossed[old], half.shape[0], weight)
         self.totals.append(total)
         self.into.append(exchange(total, self.axis, 1))
 
@@ -710,12 +716,15 @@
     rows = tokens.shape[1] // pieces
     line.enter(step(weight_terms, attended_t, cotangent, inner, 0, 0, pieces))
     line.enter(step(weight_terms, attended_t, cotangent, inner, 0, 1, pieces))
+    parts = step(project_split, rank, [attended], [w_out], "head")
+    mixed = Scatter(parts, "head", step)
     dquery, dkv, query_first, query_second, *away = step(
         backward, query, grad, attended_t, stats, tokens, levels, fars, far_bits, pieces
     )
     line.enter(query_first)
     backs = [exchange(piece, "seq", d) for d, piece in enumerate(away, 2)]
     line.meet(rows)
+    mixed.advance()
     line.meet(rows)
     line.turn(query_second)
     dkey, dvalue, dkv_t = step(
@@ -723,8 +732,6 @@
     )
     key_first = step(weight_terms, dkv_t, tokens, inner, 0, 0, pieces)
     line.meet(rows)
-    parts = step(project_split, rank, [attended], [w_out], "head")
-    mixed = Scatter(parts, "head", step)
     line.turn(key_first)
     line.meet(rows)
     key_second = step(weight_terms, dkv_t, tokens, inner, 0, 1, pieces)
@@ -734,21 +741,20 @@
     line.meet(rows)
     tokens_grad = Scatter([keep, step(relay, send)], "head", step)
     line.turn(value_first)
-    mixed.advance()
+    mixed = mixed.result()
     value_second = step(weight_terms, dkv_t, tokens, inner, 1, 1, pieces)
     line.meet(rows)
     line.turn(value_second)
     out_grad = line.output(0, pieces)
     line.meet(rows)
-    mixed = mixed.result()
+    tokens_grad.advance()
     line.leave()
-    tokens_grad.advance()
     line.meet(rows)
     query_grad = line.output(2, pieces)
     line.leave()
     key_grad = line.output(4, pieces)
+    line.leave()
     tokens_grad = tokens_grad.result()
-    line.leave()
     value_grad = line.output(6, pieces)
     return mixed, tokens_grad, query_grad, key_grad, value_grad, out_grad
 

time: 103 us -> 97.7 us (0.949)
  waiting for transfers between devices: 29.2 us -> 12.1 us
  starting transfers between devices: 39 us -> 50.6 us
    ppermute x20, waiting for transfers between devices: 29.1 us -> 11.4 us  [exchange(): return lax.ppermute(block, axis, [(i, i ^ distance) for i in range(count)])]
    ppermute x20, starting transfers between devices: 38 us -> 49.4 us  [exchange(): return lax.ppermute(block, axis, [(i, i ^ distance) for i in range(count)])]
  transfers between devices with their start and end apart: 28 -> 28, of which waited for: 11 -> 7; matrix products, arithmetic and copies ran while one was open for 0% -> 0% of each run, Pallas kernels for 22% -> 23%
where the time goes in v10:
time: 97.7 us; the launch traced here: 97.5 us
  starting transfers between devices  50.6 us (52%)
  Pallas kernels  33.7 us (34%)
  waiting for transfers between devices  12.1 us (12%)
  between operations  1.12 us (1%)
    ppermute x20, starting transfers between devices, exchange(): return lax.ppermute(block, axis, [(i, i ^ distance) for i in range(count)])  49.4 us
    pallas_call x40, Pallas kernels, run(): return pl.pallas_call(kernel, in_specs=in_specs, **options)(*ready, *after)  33.7 us
    ppermute x20, waiting for transfers between devices, exchange(): return lax.ppermute(block, axis, [(i, i ^ distance) for i in range(count)])  11.4 us
  transfers between devices with their start and end apart: 28, of which 7 were waited for; matrix products, arithmetic and copies ran while one was open for 0% of the time, Pallas kernels for 23%

profile of v10, /device:TPU:0, one launch (start us, length us, event | category | flops | bytes accessed | tf_op | source)
XLA Modules:
  0.0 97.5 jit_solution(4589300746504445849)
XLA Ops:
  0.7 5.3 %shard_map.110 = (bf16[1024,512]{1,0:T(8,128)(2,1)}, bf16[512,512]{1,0:T(8,128)(2,1)}, bf16[256,512]{1,0:T(8,128)(2,1)}, bf16[128,512]{1,0:T(8,128)(2,1)}, bf16[64,512]{1,0:T(8,128)(2,1)}) custom-call(bf16[1024,1024]{1,0:T(8,128)(2,1)} %refs_1_.17, bf16[1024,256]{1,0:T(8,128)(2,1)} %refs_5_.1, bf16[1024,256]{1,0:T(8,128)(2,1)} %refs_6_.1, ...), custom_call_target="tpu_custom_call" | custom-call | flops 5750000128 | bytes 1 | tf_op jit(solution)/shard_map/pallas_call | solution.py:42
  6.0 4.1 %collective-permute-start.1 = (bf16[64,512]{1,0:T(8,128)(2,1)}, bf16[64,512]{1,0:T(8,128)(2,1)S(1)}, u32[]{:S(2)}, u32[]{:S(2)}) collective-permute-start(bf16[64,512]{1,0:T(8,128)(2,1)} %get-tuple-element.60), channel_id=1, source_target_pairs={{0,8},{4,12},{8,0},{12,4},{1,9},{5,13},{9,1},{13,5},{2,10},{6,14},... | collective-permute-start | bytes 196616 | tf_op jit(solution)/shard_map/ppermute | solution.py:483
  10.1 1.3 %collective-permute-start.2 = (bf16[64,512]{1,0:T(8,128)(2,1)}, bf16[64,512]{1,0:T(8,128)(2,1)S(1)}, u32[]{:S(2)}, u32[]{:S(2)}) collective-permute-start(bf16[64,512]{1,0:T(8,128)(2,1)} %get-tuple-element.60), channel_id=1, source_target_pairs={{0,12},{4,8},{8,4},{12,0},{1,13},{5,9},{9,5},{13,1},{2,14},{6,10},... | collective-permute-start | bytes 196616 | tf_op jit(solution)/shard_map/ppermute | solution.py:483
  11.7 0.7 shard_map.109.refs_0_.refs_4_
  12.5 2.3 %shard_map.111 = (f32[4096,256]{1,0:T(8,128)S(1)}, f32[4,1024]{1,0:T(4,128)S(1)}) custom-call(bf16[1024,256]{1,0:T(8,128)(2,1)S(1)} %shard_map.109.refs_0_.refs_4_, bf16[1024,512]{1,0:T(8,128)(2,1)S(1)} %copy-done.6, bf16[512,512]{1,0:T(8,128)(2,1)S(1)} %copy-done.7, bf16[256,512]{1,0:T(8,128)(2,1)S(1)} %copy-done.8, ...), custom_call_target="tpu_custom_call" | custom-call | flops 2644999936 | bytes 1 | tf_op jit(solution)/shard_map/pallas_call | solution.py:42
  14.9 0.7 shard_map.112.refs_9_.refs_1_
  15.6 1.5 %collective-permute-done.2.refs_8_.refs_10_ = bf16[64,512]{1,0:T(8,128)(2,1)S(1)} collective-permute-done((bf16[64,512]{1,0:T(8,128)(2,1)}, bf16[64,512]{1,0:T(8,128)(2,1)S(1)}, u32[]{:S(2)}, u32[]{:S(2)}) %collective-permute-start.2) | collective-permute-done | bytes 65568 | tf_op jit(solution)/shard_map/ppermute | solution.py:483
  17.1 0.8 collective-permute-done.refs_6_.refs_8_
  17.9 3.9 %shard_map.113 = (bf16[1024,256]{1,0:T(8,128)(2,1)S(1)}, bf16[256,1024]{1,0:T(8,128)(2,1)S(1)}, f32[4,1024]{1,0:T(4,128)S(1)}) custom-call(bf16[1024,256]{1,0:T(8,128)(2,1)S(1)} %shard_map.109.refs_0_.refs_4_, f32[4096,256]{1,0:T(8,128)S(1)} %get-tuple-element.57.refs_2_.refs_1_, f32[4,1024]{1,0:T(4,128)S(1)} %get-tuple-element.58.refs_2_, ...), custom_call_target="tpu_custom_call" | custom-call | flops 4600000000 | bytes 1 | tf_op jit(solution)/shard_map/pallas_call | solution.py:42
  21.8 0.5 shard_map.114.refs_2_.refs_0_
  22.3 0.5 shard_map.115.refs_3_.refs_0_
  22.8 1.0 %collective-permute-start.4 = (bf16[512,256]{1,0:T(8,128)(2,1)S(1)}, bf16[512,256]{1,0:T(8,128)(2,1)S(1)}, u32[]{:S(2)}, u32[]{:S(2)}) collective-permute-start(bf16[512,256]{1,0:T(8,128)(2,1)S(1)} %shard_map.114.refs_2_.refs_0_), channel_id=1, source_target_pairs={{0,4},{4,0},{8,12},{12,8},{1,5},{5,1},{9,13},{13,9},{2,6},{6,2},{1... | collective-permute-start | bytes 786440 | tf_op jit(solution)/shard_map/ppermute | solution.py:483
  23.8 0.7 shard_map.116
  24.5 1.2 %collective-permute-start.7 = (bf16[512,256]{1,0:T(8,128)(2,1)S(1)}, bf16[512,256]{1,0:T(8,128)(2,1)S(1)}, u32[]{:S(2)}, u32[]{:S(2)}) collective-permute-start(bf16[512,256]{1,0:T(8,128)(2,1)S(1)} %shard_map.115.refs_3_.refs_0_), channel_id=1, source_target_pairs={{0,4},{4,0},{8,12},{12,8},{1,5},{5,1},{9,13},{13,9},{2,6},{6,2},{1... | collective-permute-start | bytes 786440 | tf_op jit(solution)/shard_map/ppermute | solution.py:483
  25.7 6.9 %shard_map.117 = (bf16[1024,256]{1,0:T(8,128)(2,1)S(1)}, f32[1024,512]{1,0:T(8,128)S(1)}, bf16[768,256]{1,0:T(8,128)(2,1)S(1)}, bf16[512,256]{1,0:T(8,128)(2,1)S...) custom-call(bf16[1024,256]{1,0:T(8,128)(2,1)S(1)} %shard_map.109.refs_0_.refs_4_, ...), custom_call_target="tpu_custom_call" | custom-call | flops 9200000000 | bytes 1 | tf_op jit(solution)/shard_map/pallas_call | solution.py:42
  32.7 1.0 %collective-permute-start.10 = (bf16[768,256]{1,0:T(8,128)(2,1)S(1)}, bf16[768,256]{1,0:T(8,128)(2,1)S(1)}, u32[]{:S(2)}, u32[]{:S(2)}) collective-permute-start(bf16[768,256]{1,0:T(8,128)(2,1)S(1)} %get-tuple-element.72.refs_0_), channel_id=1, source_target_pairs={{0,4},{4,0},{8,12},{12,8},{1,5},{5,1},{9,13},{13,9},{2,6},{6,2},{1... | collective-permute-start | bytes 1179656 | tf_op jit(solution)/shard_map/ppermute | solution.py:483
  33.6 2.8 %collective-permute-start.11 = (bf16[64,512]{1,0:T(8,128)(2,1)S(1)}, bf16[64,512]{1,0:T(8,128)(2,1)S(1)}, u32[]{:S(2)}, u32[]{:S(2)}) collective-permute-start(bf16[64,512]{1,0:T(8,128)(2,1)S(1)} %get-tuple-element.73), channel_id=1, source_target_pairs={{0,8},{4,12},{8,0},{12,4},{1,9},{5,13},{9,1},{13,5},{2,10},{6,14},... | collective-permute-start | bytes 196616 | tf_op jit(solution)/shard_map/ppermute | solution.py:483
  36.5 0.6 collective-permute-start.12
  37.6 0.6 collective-permute-start.9
  38.2 0.6 collective-permute-done.6.refs_2_
  38.9 11.2 %collective-permute-start.8 = (bf16[512,256]{1,0:T(8,128)(2,1)S(1)}, bf16[512,256]{1,0:T(8,128)(2,1)S(1)}, u32[]{:S(2)}, u32[]{:S(2)}) collective-permute-start(bf16[512,256]{1,0:T(8,128)(2,1)S(1)} %get-tuple-element.70), channel_id=1, source_target_pairs={{0,4},{4,0},{8,12},{12,8},{1,5},{5,1},{9,13},{13,9},{2,6},{6,2},{1... | collective-permute-start | bytes 786440 | tf_op jit(solution)/shard_map/ppermute | solution.py:483
  50.1 1.0 %shard_map.122 = (bf16[1024,256]{1,0:T(8,128)(2,1)S(1)}, bf16[1024,256]{1,0:T(8,128)(2,1)S(1)}, bf16[512,1024]{1,0:T(8,128)(2,1)S(1)}) custom-call(f32[1024,512]{1,0:T(8,128)S(1)} %get-tuple-element.71.refs_0_, bf16[768,256]{1,0:T(8,128)(2,1)S(1)} %collective-permute-done.10.refs_1_, bf16[64,512]{1,0:T(8,128)(2,1)S(1)} %collective-permute-done.11.refs_2_, ...), custom_call_target="tpu_custom_call" | custom-call | flops 230000000 | bytes 1 | tf_op jit(solution)/shard_map/pallas_call | solution.py:42
  51.1 0.5 shard_map.123.refs_2_.refs_3_.refs_0_
  51.8 1.6 %collective-permute-start.5 = (bf16[1024,256]{1,0:T(8,128)(2,1)S(1)}, bf16[1024,256]{1,0:T(8,128)(2,1)S(1)}, u32[]{:S(2)}, u32[]{:S(2)}) collective-permute-start(bf16[1024,256]{1,0:T(8,128)(2,1)S(1)} %get-tuple-element.68), channel_id=1, source_target_pairs={{0,2},{1,3},{2,0},{3,1},{4,6},{5,7},{6,4},{7,5},{8,10},{9,11},{10,... | collective-permute-start | bytes 1572872 | tf_op jit(solution)/shard_map/ppermute | solution.py:483
  53.5 2.2 %collective-permute-start.15 = (bf16[512,256]{1,0:T(8,128)(2,1)S(1)}, bf16[512,256]{1,0:T(8,128)(2,1)S(1)}, u32[]{:S(2)}, u32[]{:S(2)}) collective-permute-start(bf16[512,256]{1,0:T(8,128)(2,1)S(1)} %get-tuple-element.82), channel_id=1, source_target_pairs={{0,4},{4,0},{8,12},{12,8},{1,5},{5,1},{9,13},{13,9},{2,6},{6,2},{1... | collective-permute-start | bytes 786440 | tf_op jit(solution)/shard_map/ppermute | solution.py:483
  55.9 0.5 shard_map.127.refs_3_.refs_4_.refs_0_
  56.4 0.3 shard_map.128
  56.7 4.8 %collective-permute-start.19 = (bf16[512,256]{1,0:T(8,128)(2,1)S(1)}, bf16[512,256]{1,0:T(8,128)(2,1)S(1)}, u32[]{:S(2)}, u32[]{:S(2)}) collective-permute-start(bf16[512,256]{1,0:T(8,128)(2,1)S(1)} %get-tuple-element.88), channel_id=1, source_target_pairs={{0,4},{4,0},{8,12},{12,8},{1,5},{5,1},{9,13},{13,9},{2,6},{6,2},{1... | collective-permute-start | bytes 786440 | tf_op jit(solution)/shard_map/ppermute | solution.py:483
  61.5 0.5 shard_map.129.refs_7_.refs_3_.refs_0_
  62.1 1.8 %shard_map.130 = (bf16[1024,512]{1,0:T(8,128)(2,1)S(1)}, bf16[1024,512]{1,0:T(8,128)(2,1)S(1)}) custom-call(s32[1]{0:T(128)} %bitcast.refs_4_.refs_0_, bf16[1024,256]{1,0:T(8,128)(2,1)S(1)} %get-tuple-element.66.refs_2_.refs_1_, bf16[1024,256]{1,0:T(8,128)(2,1)S(1)} %get-tuple-element.77.refs_2_, bf16[1024,256]{1,0:T(8,128)(2,1)S(1)} %get-tuple-element.80.refs_3_, ...), custom_call_target="tpu_custom_call" | custom-call | flops 1150000000 | bytes 1 | tf_op jit(solution)/shard_map/pallas_call | solution.py:42
  64.1 0.6 collective-permute-start.16
  64.8 1.6 %collective-permute-start.17 = (bf16[512,256]{1,0:T(8,128)(2,1)S(1)}, bf16[512,256]{1,0:T(8,128)(2,1)S(1)}, u32[]{:S(2)}, u32[]{:S(2)}) collective-permute-start(bf16[512,256]{1,0:T(8,128)(2,1)S(1)} %get-tuple-element.86), channel_id=1, source_target_pairs={{0,4},{4,0},{8,12},{12,8},{1,5},{5,1},{9,13},{13,9},{2,6},{6,2},{1... | collective-permute-start | bytes 786440 | tf_op jit(solution)/shard_map/ppermute | solution.py:483
  66.4 0.9 shard_map.134
  67.3 0.5 shard_map.135.refs_2_.refs_3_.refs_0_
  68.3 4.5 %collective-permute-start.21 = (bf16[512,256]{1,0:T(8,128)(2,1)S(1)}, bf16[512,256]{1,0:T(8,128)(2,1)S(1)}, u32[]{:S(2)}, u32[]{:S(2)}) collective-permute-start(bf16[512,256]{1,0:T(8,128)(2,1)S(1)} %get-tuple-element.93), channel_id=1, source_target_pairs={{0,4},{4,0},{8,12},{12,8},{1,5},{5,1},{9,13},{13,9},{2,6},{6,2},{1... | collective-permute-start | bytes 786440 | tf_op jit(solution)/shard_map/ppermute | solution.py:483
  72.8 0.8 shard_map.138
  73.7 0.4 collective-permute-done.17.refs_1_.refs_4_
  74.5 3.6 %collective-permute-start.24 = (bf16[512,256]{1,0:T(8,128)(2,1)S(1)}, bf16[512,256]{1,0:T(8,128)(2,1)S(1)}, u32[]{:S(2)}, u32[]{:S(2)}) collective-permute-start(bf16[512,256]{1,0:T(8,128)(2,1)S(1)} %shard_map.141.refs_2_), channel_id=1, source_target_pairs={{0,4},{4,0},{8,12},{12,8},{1,5},{5,1},{9,13},{13,9},{2,6},{6,2},{1... | collective-permute-start | bytes 786440 | tf_op jit(solution)/shard_map/ppermute | solution.py:483
  78.1 1.9 %collective-permute-done.21.refs_1_.refs_3_ = bf16[512,256]{1,0:T(8,128)(2,1)S(1)} collective-permute-done((bf16[512,256]{1,0:T(8,128)(2,1)S(1)}, bf16[512,256]{1,0:T(8,128)(2,1)S(1)}, u32[]{:S(2)}, u32[]{:S(2)}) %collective-permute-start.21) | collective-permute-done | bytes 262176 | tf_op jit(solution)/shard_map/ppermute | solution.py:483
  80.1 1.6 %collective-permute-start.20 = (bf16[1024,256]{1,0:T(8,128)(2,1)S(1)}, bf16[1024,256]{1,0:T(8,128)(2,1)S(1)}, u32[]{:S(2)}, u32[]{:S(2)}) collective-permute-start(bf16[1024,256]{1,0:T(8,128)(2,1)S(1)} %get-tuple-element.92), channel_id=1, source_target_pairs={{0,2},{1,3},{2,0},{3,1},{4,6},{5,7},{6,4},{7,5},{8,10},{9,11},{10,... | collective-permute-start | bytes 1572872 | tf_op jit(solution)/shard_map/ppermute | solution.py:483
  81.7 0.8 shard_map.143
  82.6 2.5 %collective-permute-start.26 = (bf16[512,256]{1,0:T(8,128)(2,1)S(1)}, bf16[512,256]{1,0:T(8,128)(2,1)S(1)}, u32[]{:S(2)}, u32[]{:S(2)}) collective-permute-start(bf16[512,256]{1,0:T(8,128)(2,1)S(1)} %shard_map.144.refs_5_.refs_1_), channel_id=1, source_target_pairs={{0,4},{4,0},{8,12},{12,8},{1,5},{5,1},{9,13},{13,9},{2,6},{6,2},{1... | collective-permute-start | bytes 786440 | tf_op jit(solution)/shard_map/ppermute | solution.py:483
  85.1 0.8 shard_map.145
  86.0 2.8 %collective-permute-start.27 = (bf16[512,256]{1,0:T(8,128)(2,1)S(1)}, bf16[512,256]{1,0:T(8,128)(2,1)S(1)}, u32[]{:S(2)}, u32[]{:S(2)}) collective-permute-start(bf16[512,256]{1,0:T(8,128)(2,1)S(1)} %shard_map.146.refs_2_), channel_id=1, source_target_pairs={{0,4},{4,0},{8,12},{12,8},{1,5},{5,1},{9,13},{13,9},{2,6},{6,2},{1... | collective-permute-start | bytes 786440 | tf_op jit(solution)/shard_map/ppermute | solution.py:483
  88.9 5.6 %collective-permute-done.20.refs_1_ = bf16[1024,256]{1,0:T(8,128)(2,1)S(1)} collective-permute-done((bf16[1024,256]{1,0:T(8,128)(2,1)S(1)}, bf16[1024,256]{1,0:T(8,128)(2,1)S(1)}, u32[]{:S(2)}, u32[]{:S(2)}) %collective-permute-start.20) | collective-permute-done | bytes 524320 | tf_op jit(solution)/shard_map/ppermute | solution.py:483
  94.4 0.9 shard_map.147
  95.4 1.3 %collective-permute-done.27.refs_4_ = bf16[512,256]{1,0:T(8,128)(2,1)S(1)} collective-permute-done((bf16[512,256]{1,0:T(8,128)(2,1)S(1)}, bf16[512,256]{1,0:T(8,128)(2,1)S(1)}, u32[]{:S(2)}, u32[]{:S(2)}) %collective-permute-start.27) | collective-permute-done | bytes 262176 | tf_op jit(solution)/shard_map/ppermute | solution.py:483
  96.7 0.8 shard_map.148
  (66 shorter events, 2.6 us)
Async XLA Ops:
  0.6 11.1 %copy-start = (bf16[1024,1024]{1,0:T(8,128)(2,1)S(1)}, bf16[1024,1024]{1,0:T(8,128)(2,1)}, u32[]{:S(2)}) copy-start(bf16[1024,1024]{1,0:T(8,128)(2,1)} %refs_1_.17) | copy-start | bytes 6291460
  0.7 11.1 %copy-start.3 = (bf16[1024,256]{1,0:T(8,128)(2,1)S(1)}, bf16[1024,256]{1,0:T(8,128)(2,1)}, u32[]{:S(2)}) copy-start(bf16[1024,256]{1,0:T(8,128)(2,1)} %refs_4_.3) | copy-start | bytes 1572868
  6.0 6.4 %copy-start.6 = (bf16[1024,512]{1,0:T(8,128)(2,1)S(1)}, bf16[1024,512]{1,0:T(8,128)(2,1)}, u32[]{:S(2)}) copy-start(bf16[1024,512]{1,0:T(8,128)(2,1)} %get-tuple-element.54.refs_1_.refs_3_.refs_5_) | copy-start | bytes 3145732
  6.0 6.4 %copy-start.7 = (bf16[512,512]{1,0:T(8,128)(2,1)S(1)}, bf16[512,512]{1,0:T(8,128)(2,1)}, u32[]{:S(2)}) copy-start(bf16[512,512]{1,0:T(8,128)(2,1)} %get-tuple-element.55.refs_2_.refs_4_.refs_6_) | copy-start | bytes 1572868
  6.0 6.4 %copy-start.8 = (bf16[256,512]{1,0:T(8,128)(2,1)S(1)}, bf16[256,512]{1,0:T(8,128)(2,1)}, u32[]{:S(2)}) copy-start(bf16[256,512]{1,0:T(8,128)(2,1)} %get-tuple-element.56.refs_3_.refs_5_.refs_7_) | copy-start | bytes 786436
  6.0 9.5 %collective-permute-start.1 = (bf16[64,512]{1,0:T(8,128)(2,1)}, bf16[64,512]{1,0:T(8,128)(2,1)S(1)}, u32[]{:S(2)}, u32[]{:S(2)}) collective-permute-start(bf16[64,512]{1,0:T(8,128)(2,1)} %get-tuple-element.60), channel_id=1, source_target_pairs={{0,8},{4,12},{8,0},{12,4},{1,9},{5,13},{9,1},{13,5},{2,10},{6,14},... | collective-permute-start | bytes 196616 | tf_op jit(solution)/shard_map/ppermute | solution.py:483
  10.1 7.0 %collective-permute-start.2 = (bf16[64,512]{1,0:T(8,128)(2,1)}, bf16[64,512]{1,0:T(8,128)(2,1)S(1)}, u32[]{:S(2)}, u32[]{:S(2)}) collective-permute-start(bf16[64,512]{1,0:T(8,128)(2,1)} %get-tuple-element.60), channel_id=1, source_target_pairs={{0,12},{4,8},{8,4},{12,0},{1,13},{5,9},{9,5},{13,1},{2,14},{6,10},... | collective-permute-start | bytes 196616 | tf_op jit(solution)/shard_map/ppermute | solution.py:483
  11.5 6.4 %collective-permute-start = (bf16[128,512]{1,0:T(8,128)(2,1)}, bf16[128,512]{1,0:T(8,128)(2,1)S(1)}, u32[]{:S(2)}, u32[]{:S(2)}) collective-permute-start(bf16[128,512]{1,0:T(8,128)(2,1)} %get-tuple-element.59), channel_id=1, source_target_pairs={{0,4},{4,0},{8,12},{12,8},{1,5},{5,1},{9,13},{13,9},{2,6},{6,2},{1... | collective-permute-start | bytes 393224 | tf_op jit(solution)/shard_map/ppermute | solution.py:483
  12.5 2.4 %copy-start.1 = (bf16[1024,1024]{1,0:T(8,128)(2,1)S(1)}, bf16[1024,1024]{1,0:T(8,128)(2,1)}, u32[]{:S(2)}) copy-start(bf16[1024,1024]{1,0:T(8,128)(2,1)} %refs_1_.13) | copy-start | bytes 6291460
  12.5 2.4 %copy-start.2 = (bf16[1024,256]{1,0:T(8,128)(2,1)S(1)}, bf16[1024,256]{1,0:T(8,128)(2,1)}, u32[]{:S(2)}) copy-start(bf16[1024,256]{1,0:T(8,128)(2,1)} %refs_2_.3) | copy-start | bytes 1572868
  22.8 13.7 %collective-permute-start.4 = (bf16[512,256]{1,0:T(8,128)(2,1)S(1)}, bf16[512,256]{1,0:T(8,128)(2,1)S(1)}, u32[]{:S(2)}, u32[]{:S(2)}) collective-permute-start(bf16[512,256]{1,0:T(8,128)(2,1)S(1)} %shard_map.114.refs_2_.refs_0_), channel_id=1, source_target_pairs={{0,4},{4,0},{8,12},{12,8},{1,5},{5,1},{9,13},{13,9},{2,6},{6,2},{1... | collective-permute-start | bytes 786440 | tf_op jit(solution)/shard_map/ppermute | solution.py:483
  24.5 13.0 %collective-permute-start.7 = (bf16[512,256]{1,0:T(8,128)(2,1)S(1)}, bf16[512,256]{1,0:T(8,128)(2,1)S(1)}, u32[]{:S(2)}, u32[]{:S(2)}) collective-permute-start(bf16[512,256]{1,0:T(8,128)(2,1)S(1)} %shard_map.115.refs_3_.refs_0_), channel_id=1, source_target_pairs={{0,4},{4,0},{8,12},{12,8},{1,5},{5,1},{9,13},{13,9},{2,6},{6,2},{1... | collective-permute-start | bytes 786440 | tf_op jit(solution)/shard_map/ppermute | solution.py:483
  25.7 11.5 %collective-permute-start.3 = (bf16[1024,512]{1,0:T(8,128)(2,1)S(1)}, bf16[1024,512]{1,0:T(8,128)(2,1)S(1)}, u32[]{:S(2)}, u32[]{:S(2)}) collective-permute-start(bf16[1024,512]{1,0:T(8,128)(2,1)S(1)} %get-tuple-element.64), channel_id=1, source_target_pairs={{0,1},{1,0},{2,3},{3,2},{4,5},{5,4},{6,7},{7,6},{8,9},{9,8},{10,11... | collective-permute-start | bytes 3145736 | tf_op jit(solution)/shard_map/ppermute | solution.py:483
  32.7 17.4 %collective-permute-start.10 = (bf16[768,256]{1,0:T(8,128)(2,1)S(1)}, bf16[768,256]{1,0:T(8,128)(2,1)S(1)}, u32[]{:S(2)}, u32[]{:S(2)}) collective-permute-start(bf16[768,256]{1,0:T(8,128)(2,1)S(1)} %get-tuple-element.72.refs_0_), channel_id=1, source_target_pairs={{0,4},{4,0},{8,12},{12,8},{1,5},{5,1},{9,13},{13,9},{2,6},{6,2},{1... | collective-permute-start | bytes 1179656 | tf_op jit(solution)/shard_map/ppermute | solution.py:483
  33.6 16.4 %collective-permute-start.11 = (bf16[64,512]{1,0:T(8,128)(2,1)S(1)}, bf16[64,512]{1,0:T(8,128)(2,1)S(1)}, u32[]{:S(2)}, u32[]{:S(2)}) collective-permute-start(bf16[64,512]{1,0:T(8,128)(2,1)S(1)} %get-tuple-element.73), channel_id=1, source_target_pairs={{0,8},{4,12},{8,0},{12,4},{1,9},{5,13},{9,1},{13,5},{2,10},{6,14},... | collective-permute-start | bytes 196616 | tf_op jit(solution)/shard_map/ppermute | solution.py:483
  36.5 13.6 %collective-permute-start.12 = (bf16[64,512]{1,0:T(8,128)(2,1)S(1)}, bf16[64,512]{1,0:T(8,128)(2,1)S(1)}, u32[]{:S(2)}, u32[]{:S(2)}) collective-permute-start(bf16[64,512]{1,0:T(8,128)(2,1)S(1)} %get-tuple-element.74), channel_id=1, source_target_pairs={{0,12},{4,8},{8,4},{12,0},{1,13},{5,9},{9,5},{13,1},{2,14},{6,10},... | collective-permute-start | bytes 196616 | tf_op jit(solution)/shard_map/ppermute | solution.py:483
  37.2 1.6 %collective-permute-start.6 = (bf16[512,256]{1,0:T(8,128)(2,1)S(1)}, bf16[512,256]{1,0:T(8,128)(2,1)S(1)}, u32[]{:S(2)}, u32[]{:S(2)}) collective-permute-start(bf16[512,256]{1,0:T(8,128)(2,1)S(1)} %shard_map.118.refs_2_.refs_1_), channel_id=1, source_target_pairs={{0,1},{1,0},{2,3},{3,2},{4,8},{5,9},{6,10},{7,11},{8,4},{9,5},{10,... | collective-permute-start | bytes 786440 | tf_op jit(solution)/shard_map/ppermute | solution.py:640
  37.6 15.8 %collective-permute-start.9 = (bf16[512,256]{1,0:T(8,128)(2,1)S(1)}, bf16[512,256]{1,0:T(8,128)(2,1)S(1)}, u32[]{:S(2)}, u32[]{:S(2)}) collective-permute-start(bf16[512,256]{1,0:T(8,128)(2,1)S(1)} %shard_map.120.refs_4_.refs_1_), channel_id=1, source_target_pairs={{0,1},{1,0},{2,3},{3,2},{4,8},{5,9},{6,10},{7,11},{8,4},{9,5},{10,... | collective-permute-start | bytes 786440 | tf_op jit(solution)/shard_map/ppermute | solution.py:640
  38.9 16.8 %collective-permute-start.8 = (bf16[512,256]{1,0:T(8,128)(2,1)S(1)}, bf16[512,256]{1,0:T(8,128)(2,1)S(1)}, u32[]{:S(2)}, u32[]{:S(2)}) collective-permute-start(bf16[512,256]{1,0:T(8,128)(2,1)S(1)} %get-tuple-element.70), channel_id=1, source_target_pairs={{0,4},{4,0},{8,12},{12,8},{1,5},{5,1},{9,13},{13,9},{2,6},{6,2},{1... | collective-permute-start | bytes 786440 | tf_op jit(solution)/shard_map/ppermute | solution.py:483
  51.7 4.7 %collective-permute-start.14 = (bf16[512,256]{1,0:T(8,128)(2,1)S(1)}, bf16[512,256]{1,0:T(8,128)(2,1)S(1)}, u32[]{:S(2)}, u32[]{:S(2)}) collective-permute-start(bf16[512,256]{1,0:T(8,128)(2,1)S(1)} %shard_map.124.refs_4_.refs_1_), channel_id=1, source_target_pairs={{0,1},{1,0},{2,3},{3,2},{4,8},{5,9},{6,10},{7,11},{8,4},{9,5},{10,... | collective-permute-start | bytes 786440 | tf_op jit(solution)/shard_map/ppermute | solution.py:640
  51.8 14.6 %collective-permute-start.5 = (bf16[1024,256]{1,0:T(8,128)(2,1)S(1)}, bf16[1024,256]{1,0:T(8,128)(2,1)S(1)}, u32[]{:S(2)}, u32[]{:S(2)}) collective-permute-start(bf16[1024,256]{1,0:T(8,128)(2,1)S(1)} %get-tuple-element.68), channel_id=1, source_target_pairs={{0,2},{1,3},{2,0},{3,1},{4,6},{5,7},{6,4},{7,5},{8,10},{9,11},{10,... | collective-permute-start | bytes 1572872 | tf_op jit(solution)/shard_map/ppermute | solution.py:483
  53.5 10.4 %collective-permute-start.15 = (bf16[512,256]{1,0:T(8,128)(2,1)S(1)}, bf16[512,256]{1,0:T(8,128)(2,1)S(1)}, u32[]{:S(2)}, u32[]{:S(2)}) collective-permute-start(bf16[512,256]{1,0:T(8,128)(2,1)S(1)} %get-tuple-element.82), channel_id=1, source_target_pairs={{0,4},{4,0},{8,12},{12,8},{1,5},{5,1},{9,13},{13,9},{2,6},{6,2},{1... | collective-permute-start | bytes 786440 | tf_op jit(solution)/shard_map/ppermute | solution.py:483
  55.8 8.9 %collective-permute-start.13 = (bf16[512,256]{1,0:T(8,128)(2,1)S(1)}, bf16[512,256]{1,0:T(8,128)(2,1)S(1)}, u32[]{:S(2)}, u32[]{:S(2)}) collective-permute-start(bf16[512,256]{1,0:T(8,128)(2,1)S(1)} %shard_map.126.refs_2_.refs_1_), channel_id=1, source_target_pairs={{0,1},{1,0},{2,3},{3,2},{4,8},{5,9},{6,10},{7,11},{8,4},{9,5},{10,... | collective-permute-start | bytes 786440 | tf_op jit(solution)/shard_map/ppermute | solution.py:640
  56.7 5.4 %copy-start.4 = (bf16[1024,256]{1,0:T(8,128)(2,1)S(1)}, bf16[1024,256]{1,0:T(8,128)(2,1)}, u32[]{:S(2)}) copy-start(bf16[1024,256]{1,0:T(8,128)(2,1)} %refs_5_.1) | copy-start | bytes 1572868
  56.7 5.4 %copy-start.5 = (bf16[1024,256]{1,0:T(8,128)(2,1)S(1)}, bf16[1024,256]{1,0:T(8,128)(2,1)}, u32[]{:S(2)}) copy-start(bf16[1024,256]{1,0:T(8,128)(2,1)} %refs_6_.1) | copy-start | bytes 1572868
  56.7 11.2 %collective-permute-start.19 = (bf16[512,256]{1,0:T(8,128)(2,1)S(1)}, bf16[512,256]{1,0:T(8,128)(2,1)S(1)}, u32[]{:S(2)}, u32[]{:S(2)}) collective-permute-start(bf16[512,256]{1,0:T(8,128)(2,1)S(1)} %get-tuple-element.88), channel_id=1, source_target_pairs={{0,4},{4,0},{8,12},{12,8},{1,5},{5,1},{9,13},{13,9},{2,6},{6,2},{1... | collective-permute-start | bytes 786440 | tf_op jit(solution)/shard_map/ppermute | solution.py:483
  64.0 4.2 %collective-permute-start.18 = (bf16[512,256]{1,0:T(8,128)(2,1)S(1)}, bf16[512,256]{1,0:T(8,128)(2,1)S(1)}, u32[]{:S(2)}, u32[]{:S(2)}) collective-permute-start(bf16[512,256]{1,0:T(8,128)(2,1)S(1)} %shard_map.131.refs_1_), channel_id=1, source_target_pairs={{0,1},{1,0},{2,3},{3,2},{4,8},{5,9},{6,10},{7,11},{8,4},{9,5},{10,... | collective-permute-start | bytes 786440 | tf_op jit(solution)/shard_map/ppermute | solution.py:640
  64.1 10.0 %collective-permute-start.16 = (bf16[1024,512]{1,0:T(8,128)(2,1)S(1)}, bf16[1024,512]{1,0:T(8,128)(2,1)S(1)}, u32[]{:S(2)}, u32[]{:S(2)}) collective-permute-start(bf16[1024,512]{1,0:T(8,128)(2,1)S(1)} %shard_map.132.refs_4_), channel_id=1, source_target_pairs={{0,1},{1,0},{2,3},{3,2},{4,5},{5,4},{6,7},{7,6},{8,9},{9,8},{10,11... | collective-permute-start | bytes 3145736 | tf_op jit(solution)/shard_map/ppermute | solution.py:483
  64.8 9.2 %collective-permute-start.17 = (bf16[512,256]{1,0:T(8,128)(2,1)S(1)}, bf16[512,256]{1,0:T(8,128)(2,1)S(1)}, u32[]{:S(2)}, u32[]{:S(2)}) collective-permute-start(bf16[512,256]{1,0:T(8,128)(2,1)S(1)} %get-tuple-element.86), channel_id=1, source_target_pairs={{0,4},{4,0},{8,12},{12,8},{1,5},{5,1},{9,13},{13,9},{2,6},{6,2},{1... | collective-permute-start | bytes 786440 | tf_op jit(solution)/shard_map/ppermute | solution.py:483
  68.0 6.5 %collective-permute-start.22 = (bf16[512,256]{1,0:T(8,128)(2,1)S(1)}, bf16[512,256]{1,0:T(8,128)(2,1)S(1)}, u32[]{:S(2)}, u32[]{:S(2)}) collective-permute-start(bf16[512,256]{1,0:T(8,128)(2,1)S(1)} %shard_map.136.refs_4_.refs_0_), channel_id=1, source_target_pairs={{0,1},{1,0},{2,3},{3,2},{4,8},{5,9},{6,10},{7,11},{8,4},{9,5},{10,... | collective-permute-start | bytes 786440 | tf_op jit(solution)/shard_map/ppermute | solution.py:640
  68.3 11.7 %collective-permute-start.21 = (bf16[512,256]{1,0:T(8,128)(2,1)S(1)}, bf16[512,256]{1,0:T(8,128)(2,1)S(1)}, u32[]{:S(2)}, u32[]{:S(2)}) collective-permute-start(bf16[512,256]{1,0:T(8,128)(2,1)S(1)} %get-tuple-element.93), channel_id=1, source_target_pairs={{0,4},{4,0},{8,12},{12,8},{1,5},{5,1},{9,13},{13,9},{2,6},{6,2},{1... | collective-permute-start | bytes 786440 | tf_op jit(solution)/shard_map/ppermute | solution.py:483
  74.1 8.5 %collective-permute-start.25 = (bf16[512,256]{1,0:T(8,128)(2,1)S(1)}, bf16[512,256]{1,0:T(8,128)(2,1)S(1)}, u32[]{:S(2)}, u32[]{:S(2)}) collective-permute-start(bf16[512,256]{1,0:T(8,128)(2,1)S(1)} %shard_map.139.refs_2_.refs_0_), channel_id=1, source_target_pairs={{0,1},{1,0},{2,3},{3,2},{4,8},{5,9},{6,10},{7,11},{8,4},{9,5},{10,... | collective-permute-start | bytes 786440 | tf_op jit(solution)/shard_map/ppermute | solution.py:640
  74.5 10.6 %collective-permute-start.24 = (bf16[512,256]{1,0:T(8,128)(2,1)S(1)}, bf16[512,256]{1,0:T(8,128)(2,1)S(1)}, u32[]{:S(2)}, u32[]{:S(2)}) collective-permute-start(bf16[512,256]{1,0:T(8,128)(2,1)S(1)} %shard_map.141.refs_2_), channel_id=1, source_target_pairs={{0,4},{4,0},{8,12},{12,8},{1,5},{5,1},{9,13},{13,9},{2,6},{6,2},{1... | collective-permute-start | bytes 786440 | tf_op jit(solution)/shard_map/ppermute | solution.py:483
  80.0 5.9 %collective-permute-start.23 = (bf16[512,256]{1,0:T(8,128)(2,1)S(1)}, bf16[512,256]{1,0:T(8,128)(2,1)S(1)}, u32[]{:S(2)}, u32[]{:S(2)}) collective-permute-start(bf16[512,256]{1,0:T(8,128)(2,1)S(1)} %shard_map.142.refs_5_.refs_0_), channel_id=1, source_target_pairs={{0,1},{1,0},{2,3},{3,2},{4,8},{5,9},{6,10},{7,11},{8,4},{9,5},{10,... | collective-permute-start | bytes 786440 | tf_op jit(solution)/shard_map/ppermute | solution.py:640
  80.1 14.3 %collective-permute-start.20 = (bf16[1024,256]{1,0:T(8,128)(2,1)S(1)}, bf16[1024,256]{1,0:T(8,128)(2,1)S(1)}, u32[]{:S(2)}, u32[]{:S(2)}) collective-permute-start(bf16[1024,256]{1,0:T(8,128)(2,1)S(1)} %get-tuple-element.92), channel_id=1, source_target_pairs={{0,2},{1,3},{2,0},{3,1},{4,6},{5,7},{6,4},{7,5},{8,10},{9,11},{10,... | collective-permute-start | bytes 1572872 | tf_op jit(solution)/shard_map/ppermute | solution.py:483
  82.6 12.7 %collective-permute-start.26 = (bf16[512,256]{1,0:T(8,128)(2,1)S(1)}, bf16[512,256]{1,0:T(8,128)(2,1)S(1)}, u32[]{:S(2)}, u32[]{:S(2)}) collective-permute-start(bf16[512,256]{1,0:T(8,128)(2,1)S(1)} %shard_map.144.refs_5_.refs_1_), channel_id=1, source_target_pairs={{0,4},{4,0},{8,12},{12,8},{1,5},{5,1},{9,13},{13,9},{2,6},{6,2},{1... | collective-permute-start | bytes 786440 | tf_op jit(solution)/shard_map/ppermute | solution.py:483
  86.0 10.6 %collective-permute-start.27 = (bf16[512,256]{1,0:T(8,128)(2,1)S(1)}, bf16[512,256]{1,0:T(8,128)(2,1)S(1)}, u32[]{:S(2)}, u32[]{:S(2)}) collective-permute-start(bf16[512,256]{1,0:T(8,128)(2,1)S(1)} %shard_map.146.refs_2_), channel_id=1, source_target_pairs={{0,4},{4,0},{8,12},{12,8},{1,5},{5,1},{9,13},{13,9},{2,6},{6,2},{1... | collective-permute-start | bytes 786440 | tf_op jit(solution)/shard_map/ppermute | solution.py:483

commit v11 on v10

--- a/solution.py
+++ b/solution.py
@@ -304,65 +304,71 @@
     )
 
 
-def backward_body(local_levels, far_bits, pieces, *refs):
+def backward_body(h, heads, local_levels, far_bits, pieces, *refs):
     mids = local_levels - 1
     fars = len(far_bits)
-    q_ref, g_ref, att_t_ref, stat_ref, tok_ref = refs[:5]
-    level_refs = refs[5 : 5 + local_levels]
-    far_refs = refs[5 + local_levels : 5 + local_levels + fars]
-    outs = refs[5 + local_levels + fars :]
-    dq_ref, dkv_ref = outs[:2]
-    term_refs = outs[2 : 2 + pieces]
-    dfar_refs = outs[2 + pieces : 1 + pieces + fars]
-    dmid_refs = outs[1 + pieces + fars : 1 + pieces + fars + mids]
-    dq_t_ref, acc_ref = outs[-2:]
+    closing = h == heads - 1
+    q_ref, g_ref, att_t_ref, stat_ref = refs[:4]
+    level_refs = refs[4 : 4 + local_levels]
+    far_refs = refs[4 + local_levels : 4 + local_levels + fars]
+    refs = refs[4 + local_levels + fars :]
+    if closing:
+        tok_ref, *earlier = refs[: 1 + 3 * h]
+        refs = refs[1 + 3 * h :]
+        dq_ref, dkv_ref = refs[:2]
+        term_refs = refs[2 : 2 + pieces]
+        dfar_refs = refs[2 + pieces : 1 + pieces + fars]
+        scratch = refs[1 + pieces + fars :]
+        dq_t_ref = scratch[-1]
+        place = slice(h * HEAD_DIM, (h + 1) * HEAD_DIM)
+    else:
+        dq_ref, dkv_ref, dq_t_ref, out_ref = refs[:4]
+        scratch = refs[4:]
+        place = slice(0, HEAD_DIM)
+    dmid_refs = scratch[:mids]
+    acc_ref = scratch[mids]
     tok_rows, inner = q_ref.shape
-    heads = inner // HEAD_DIM
     score_scale = 1.0 / math.sqrt(HEAD_DIM)
     keyset = KeySet([r.shape[0] for r in far_refs], far_bits, local_levels)
+    cols, vcols = head_columns(h, inner)
+    parts = (slice(0, HEAD_DIM), slice(HEAD_DIM, 2 * HEAD_DIM))
 
     for ref in (*dmid_refs, acc_ref):
         ref[...] = jnp.zeros_like(ref)
 
-    def step(m, carry):
+    def unit(m):
         here = keyset.here(m)
-        for h in range(heads):
-            cols, vcols = head_columns(h, inner)
-            keys, values = (
-                jnp.concatenate(keyset.near(m, level_refs, c) + keyset.far(far_refs, c), axis=0)
-                for c in (cols, vcols)
-            )
-            q = q_ref[here, cols]
-            g = g_ref[here, cols]
-            top = stat_ref[h : h + 1, here]
-            inverse = stat_ref[heads + h : heads + h + 1, here]
-            probs = keyset.powers(keyset.pieces(dot(keys, q, NT)), top) * inverse
-            att_t = att_t_ref[cols, here].astype(F32)
-            delta = jnp.sum(g.T.astype(F32) * att_t, axis=0, keepdims=True)
-            grads = (probs * (dot(values, g, NT) - delta) * score_scale).astype(BF16)
-            dq_t = dot(keys, grads, TN).astype(BF16)
-            dq_t_ref[cols, here] = dq_t
-            dq_ref[here, cols] = dq_t.T
-            for part, place in ((dot(grads, q), cols), (dot(probs.astype(BF16), g), vcols)):
-                own, *sides = keyset.pieces(part)
-                dkv_ref[here, place] = own
-                for ref, seat, side in zip(dmid_refs, keyset.seats(m), sides):
-                    ref[seat, place] += side
-                acc_ref[:, place] += part[keyset.far_start :]
+        keys, values = (
+            jnp.concatenate(keyset.near(m, level_refs, c) + keyset.far(far_refs, c), axis=0)
+            for c in (cols, vcols)
+        )
+        q = q_ref[here, cols]
+        g = g_ref[here, cols]
+        top = stat_ref[h : h + 1, here]
+        inverse = stat_ref[heads + h : heads + h + 1, here]
+        probs = keyset.powers(keyset.pieces(dot(keys, q, NT)), top) * inverse
+        att_t = att_t_ref[cols, here].astype(F32)
+        delta = jnp.sum(g.T.astype(F32) * att_t, axis=0, keepdims=True)
+        grads = (probs * (dot(values, g, NT) - delta) * score_scale).astype(BF16)
+        dq_t = dot(keys, grads, TN).astype(BF16)
+        dq_t_ref[place, here] = dq_t
+        dq_ref[here, place] = dq_t.T
+        for part, half in zip((dot(grads, q), dot(probs.astype(BF16), g)), parts):
+            own, *sides = keyset.pieces(part)
+            dkv_ref[here, half] = own
+            for ref, seat, side in zip(dmid_refs, keyset.seats(m), sides):
+                ref[seat, half] += side
+            acc_ref[:, half] += part[keyset.far_start :]
+
+    pairs = tok_rows // (2 * BLOCK)
+    stride = 2 if pairs % 2 == 0 else 1
+
+    def step(i, carry):
+        for u in range(stride):
+            unit(i * stride + u)
         return carry
 
-    lax.fori_loop(0, tok_rows // (2 * BLOCK), step, 0)
-    width = term_refs[-1].shape[0]
-    first = acc_ref[:BLOCK].astype(BF16)
-    term_refs[0][width : width + BLOCK, :] = first[:, :inner]
-    term_refs[0][width + BLOCK :, :] = first[:, inner:]
-    low = BLOCK
-    for ref in dfar_refs:
-        ref[...] = acc_ref[low : low + ref.shape[0]].astype(BF16)
-        low += ref.shape[0]
-    for i, ref in enumerate(term_refs):
-        part = dot(dq_t_ref[...], tok_ref[:, i * width : (i + 1) * width])
-        ref[:width, :] = part.astype(BF16).T
+    lax.fori_loop(0, pairs // stride, step, 0)
     fan = spread_matrix(2 * BLOCK, 1, 0, BLOCK, 0.5)
     targets = (dkv_ref, *dmid_refs)
     for i in reversed(range(mids)):
@@ -372,24 +378,75 @@
             low = (part - high.astype(F32)).astype(BF16)
             rows = slice(2 * t * BLOCK, 2 * (t + 1) * BLOCK)
             targets[i][rows, :] += dot(fan, high) + dot(fan, low)
-
-
-def backward(query, grad, attended_t, stats, tokens, levels, fars, far_bits, pieces, after):
+    away = acc_ref[...].astype(BF16)
+    if not closing:
+        out_ref[...] = away
+        return
+    aways = []
+    for e in range(h):
+        dq_e, dq_t_e, away_e = earlier[3 * e : 3 * e + 3]
+        here = slice(e * HEAD_DIM, (e + 1) * HEAD_DIM)
+        dq_ref[:, here] = dq_e[...]
+        dq_t_ref[here, :] = dq_t_e[...]
+        aways.append(away_e[...])
+    aways.append(away)
+    away = jnp.concatenate([x[:, half] for half in parts for x in aways], axis=1)
+    width = term_refs[-1].shape[0]
+    term_refs[0][width : width + BLOCK, :] = away[:BLOCK, :inner]
+    term_refs[0][width + BLOCK :, :] = away[:BLOCK, inner:]
+    low = BLOCK
+    for ref in dfar_refs:
+        ref[...] = away[low : low + ref.shape[0]]
+        low += ref.shape[0]
+    for i, ref in enumerate(term_refs):
+        part = dot(dq_t_ref[...], tok_ref[:, i * width : (i + 1) * width])
+        ref[:width, :] = part.astype(BF16).T
+
+
+def backward_scratch(levels, fars):
+    mids = [pltpu.VMEM((level.shape[0], 2 * HEAD_DIM), F32) for level in levels[1:]]
+    return mids + [pltpu.VMEM((sum(f.shape[0] for f in fars), 2 * HEAD_DIM), F32)]
+
+
+def backward_first(h, query, grad, attended_t, stats, levels, fars, far_bits, after):
     tok_rows, inner = query.shape
-    far_rows = sum(f.shape[0] for f in fars)
-    set_rows = (len(levels) + 1) * BLOCK + far_rows
-    return run(
-        functools.partial(backward_body, len(levels), far_bits, pieces),
-        [query, grad, attended_t, stats, tokens, *levels, *fars],
-        after,
-        out_shape=[shape(tok_rows, inner), shape(tok_rows, 2 * inner, F32)]
+    return run(
+        functools.partial(
+            backward_body, h, inner // HEAD_DIM, len(levels), far_bits, 0
+        ),
+        [query, grad, attended_t, stats, *levels, *fars],
+        after,
+        out_shape=[
+            shape(tok_rows, HEAD_DIM),
+            shape(tok_rows, 2 * HEAD_DIM, F32),
+            shape(HEAD_DIM, tok_rows),
+            shape(sum(f.shape[0] for f in fars), 2 * HEAD_DIM),
+        ],
+        scratch_shapes=backward_scratch(levels, fars),
+        compiler_params=params(10),
+        cost_estimate=cost(4.0),
+    )
+
+
+def backward_last(earlier, query, grad, attended_t, stats, tokens, levels, fars, far_bits, pieces, after):
+    tok_rows, inner = query.shape
+    h = len(earlier)
+    ready = [query, grad, attended_t, stats, *levels, *fars, tokens]
+    for dq, _, dq_t, away in earlier:
+        ready += [dq, dq_t, away]
+    return run(
+        functools.partial(
+            backward_body, h, inner // HEAD_DIM, len(levels), far_bits, pieces
+        ),
+        ready,
+        after,
+        out_shape=[shape(tok_rows, inner), shape(tok_rows, 2 * HEAD_DIM, F32)]
         + [shape(tokens.shape[1] // pieces + 2 * BLOCK, inner)]
         + [shape(tokens.shape[1] // pieces, inner)] * (pieces - 1)
         + [shape(*f.shape) for f in fars[1:]],
-        scratch_shapes=[pltpu.VMEM(level.shape, F32) for level in levels[1:]]
-        + [pltpu.VMEM((inner, tok_rows), BF16), pltpu.VMEM((far_rows, 2 * inner), F32)],
+        scratch_shapes=backward_scratch(levels, fars) + [pltpu.VMEM((inner, tok_rows), BF16)],
         compiler_params=params(10),
-        cost_estimate=cost(8.0),
+        cost_estimate=cost(4.0),
     )
 
 
@@ -412,17 +469,19 @@
     )
 
 
-def close_body(local_levels, far_bits, dkv_ref, *refs):
-    joined_ref, *back_refs = refs[: len(far_bits)]
-    dk_ref, dv_ref, dkv_t_ref = refs[len(far_bits) :]
+def close_body(local_levels, far_bits, heads, *refs):
+    dkv_refs = refs[:heads]
+    joined_ref, *back_refs = refs[heads : heads + len(far_bits)]
+    dk_ref, dv_ref, dkv_t_ref = refs[heads + len(far_bits) :]
     inner = dk_ref.shape[1]
     tile = 2 * BLOCK
     low = joined_ref.shape[0] - 2 * BLOCK
     joined = [joined_ref[low : low + BLOCK, :], joined_ref[low + BLOCK :, :]]
     backs = [jnp.concatenate(joined, axis=1)] + [ref[...] for ref in back_refs]
-    for t in range(dkv_ref.shape[0] // tile):
+    halves = (slice(0, HEAD_DIM), slice(HEAD_DIM, 2 * HEAD_DIM))
+    for t in range(dk_ref.shape[0] // tile):
         here = slice(t * tile, (t + 1) * tile)
-        total = dkv_ref[here, :]
+        total = jnp.concatenate([ref[here, half] for half in halves for ref in dkv_refs], axis=1)
         for back, bit in zip(backs, far_bits):
             weight = 0.5 ** (local_levels + bit)
             fan = spread_matrix(tile, local_levels + bit, t * tile, back.shape[0], weight)
@@ -433,12 +492,13 @@
         dkv_t_ref[:, here] = final.T
 
 
-def close_keys(dkv, backs, far_bits, local_levels, after):
-    tok_rows, double = dkv.shape
-    inner = double // 2
-    return run(
-        functools.partial(close_body, local_levels, far_bits),
-        [dkv, *backs],
+def close_keys(dkvs, backs, far_bits, local_levels, after):
+    tok_rows = dkvs[0].shape[0]
+    inner = len(dkvs) * HEAD_DIM
+    double = 2 * inner
+    return run(
+        functools.partial(close_body, local_levels, far_bits, len(dkvs)),
+        [*dkvs, *backs],
         after,
         out_shape=[shape(tok_rows, inner), shape(tok_rows, inner), shape(double, tok_rows)],
         compiler_params=params(5),
@@ -611,8 +671,8 @@
 
 class Line:
     lag = 3
-    half_weights = (3.0, 3.0, 3.0, 2.5, 2.5, 3.0, 3.0, 3.0)
-    turn_weights = (3.0, 2.5, 2.5, 3.0, 3.0, 3.0, 3.0, 3.0)
+    half_weights = (3.0, 3.0, 2.5, 2.0, 2.5, 3.0, 3.0, 2.0)
+    turn_weights = (3.0, 2.0, 2.0, 3.0, 3.0, 2.0, 2.0, 2.0)
 
     def __init__(self, axis, other, end, step):
         self.axis, self.axes, self.step = axis, (axis, other), step
@@ -715,20 +775,24 @@
     pieces = 2
     rows = tokens.shape[1] // pieces
     line.enter(step(weight_terms, attended_t, cotangent, inner, 0, 0, pieces))
-    line.enter(step(weight_terms, attended_t, cotangent, inner, 0, 1, pieces))
     parts = step(project_split, rank, [attended], [w_out], "head")
     mixed = Scatter(parts, "head", step)
+    earlier = [
+        step(backward_first, h, query, grad, attended_t, stats, levels, fars, far_bits)
+        for h in range(inner // HEAD_DIM - 1)
+    ]
+    line.enter(step(weight_terms, attended_t, cotangent, inner, 0, 1, pieces))
+    line.meet(rows)
+    mixed.advance()
     dquery, dkv, query_first, query_second, *away = step(
-        backward, query, grad, attended_t, stats, tokens, levels, fars, far_bits, pieces
+        backward_last, earlier, query, grad, attended_t, stats, tokens, levels, fars, far_bits, pieces
     )
     line.enter(query_first)
     backs = [exchange(piece, "seq", d) for d, piece in enumerate(away, 2)]
     line.meet(rows)
-    mixed.advance()
-    line.meet(rows)
     line.turn(query_second)
     dkey, dvalue, dkv_t = step(
-        close_keys, dkv, [line.into[2], *backs], far_bits, local_levels
+        close_keys, [made[1] for made in earlier] + [dkv], [line.into[2], *backs], far_bits, local_levels
     )
     key_first = step(weight_terms, dkv_t, tokens, inner, 0, 0, pieces)
     line.meet(rows)

time: 97.7 us -> 102 us (1.044)
  waiting for transfers between devices: 12.1 us -> 29.3 us
  starting transfers between devices: 50.6 us -> 37.7 us
    ppermute x20, waiting for transfers between devices: 11.4 us -> 29.2 us  [exchange(): return lax.ppermute(block, axis, [(i, i ^ distance) for i in range(count)])]
    ppermute x20, starting transfers between devices: 49.4 us -> 37.1 us  [exchange(): return lax.ppermute(block, axis, [(i, i ^ distance) for i in range(count)])]
    pallas_call x40 -> x41, Pallas kernels: 33.7 us -> 34.1 us  [run(): return pl.pallas_call(kernel, in_specs=in_specs, **options)(*ready, *after)]
  transfers between devices with their start and end apart: 28 -> 28, of which waited for: 7 -> 12; matrix products, arithmetic and copies ran while one was open for 0% -> 0% of each run, Pallas kernels for 23% -> 22%
where the time goes in v11:
time: 102 us
  starting transfers between devices  37.7 us (37%)
  Pallas kernels  34.1 us (33%)
  waiting for transfers between devices  29.3 us (29%)
  between operations  1.14 us (1%)
    ppermute x20, starting transfers between devices, exchange(): return lax.ppermute(block, axis, [(i, i ^ distance) for i in range(count)])  37.1 us
    pallas_call x41, Pallas kernels, run(): return pl.pallas_call(kernel, in_specs=in_specs, **options)(*ready, *after)  34.1 us
    ppermute x20, waiting for transfers between devices, exchange(): return lax.ppermute(block, axis, [(i, i ^ distance) for i in range(count)])  29.2 us
  transfers between devices with their start and end apart: 28, of which 12 were waited for; matrix products, arithmetic and copies ran while one was open for 0% of the time, Pallas kernels for 22%

profile of v11, /device:TPU:0, one launch (start us, length us, event | category | flops | bytes accessed | tf_op | source)
XLA Modules:
  0.0 102.2 jit_solution(5682810505130040252)
XLA Ops:
  0.7 5.3 %shard_map.110 = (bf16[1024,512]{1,0:T(8,128)(2,1)}, bf16[512,512]{1,0:T(8,128)(2,1)}, bf16[256,512]{1,0:T(8,128)(2,1)}, bf16[128,512]{1,0:T(8,128)(2,1)}, bf16[64,512]{1,0:T(8,128)(2,1)}) custom-call(bf16[1024,1024]{1,0:T(8,128)(2,1)} %refs_1_.17, bf16[1024,256]{1,0:T(8,128)(2,1)} %refs_5_.1, bf16[1024,256]{1,0:T(8,128)(2,1)} %refs_6_.1, ...), custom_call_target="tpu_custom_call" | custom-call | flops 5750000128 | bytes 1 | tf_op jit(solution)/shard_map/pallas_call | solution.py:42
  6.0 5.1 %collective-permute-start.2 = (bf16[64,512]{1,0:T(8,128)(2,1)}, bf16[64,512]{1,0:T(8,128)(2,1)S(1)}, u32[]{:S(2)}, u32[]{:S(2)}) collective-permute-start(bf16[64,512]{1,0:T(8,128)(2,1)} %get-tuple-element.64), channel_id=1, source_target_pairs={{0,12},{4,8},{8,4},{12,0},{1,13},{5,9},{9,5},{13,1},{2,14},{6,10},... | collective-permute-start | bytes 196616 | tf_op jit(solution)/shard_map/ppermute | solution.py:543
  11.2 0.6 collective-permute-start
  11.8 0.7 shard_map.109.refs_0_.refs_4_
  12.6 2.3 %shard_map.111 = (f32[4096,256]{1,0:T(8,128)S(1)}, f32[4,1024]{1,0:T(4,128)S(1)}) custom-call(bf16[1024,256]{1,0:T(8,128)(2,1)S(1)} %shard_map.109.refs_0_.refs_4_, bf16[1024,512]{1,0:T(8,128)(2,1)S(1)} %copy-done.6, bf16[512,512]{1,0:T(8,128)(2,1)S(1)} %copy-done.7, bf16[256,512]{1,0:T(8,128)(2,1)S(1)} %copy-done.8, ...), custom_call_target="tpu_custom_call" | custom-call | flops 2644999936 | bytes 1 | tf_op jit(solution)/shard_map/pallas_call | solution.py:42
  14.9 0.7 shard_map.112.refs_9_.refs_1_
  15.7 1.4 %collective-permute-done.1.refs_7_.refs_8_ = bf16[64,512]{1,0:T(8,128)(2,1)S(1)} collective-permute-done((bf16[64,512]{1,0:T(8,128)(2,1)}, bf16[64,512]{1,0:T(8,128)(2,1)S(1)}, u32[]{:S(2)}, u32[]{:S(2)}) %collective-permute-start.1) | collective-permute-done | bytes 65568 | tf_op jit(solution)/shard_map/ppermute | solution.py:543
  17.1 0.9 collective-permute-done.refs_6_.refs_7_
  17.9 3.9 %shard_map.113 = (bf16[1024,256]{1,0:T(8,128)(2,1)S(1)}, bf16[256,1024]{1,0:T(8,128)(2,1)S(1)}, f32[4,1024]{1,0:T(4,128)S(1)}) custom-call(bf16[1024,256]{1,0:T(8,128)(2,1)S(1)} %shard_map.109.refs_0_.refs_4_, f32[4096,256]{1,0:T(8,128)S(1)} %get-tuple-element.61.refs_2_.refs_1_, f32[4,1024]{1,0:T(4,128)S(1)} %get-tuple-element.62.refs_2_, ...), custom_call_target="tpu_custom_call" | custom-call | flops 4600000000 | bytes 1 | tf_op jit(solution)/shard_map/pallas_call | solution.py:42
  22.4 0.7 shard_map.115
  23.2 1.6 %collective-permute-start.4 = (bf16[512,256]{1,0:T(8,128)(2,1)S(1)}, bf16[512,256]{1,0:T(8,128)(2,1)S(1)}, u32[]{:S(2)}, u32[]{:S(2)}) collective-permute-start(bf16[512,256]{1,0:T(8,128)(2,1)S(1)} %shard_map.114.refs_3_.refs_0_), channel_id=1, source_target_pairs={{0,4},{4,0},{8,12},{12,8},{1,5},{5,1},{9,13},{13,9},{2,6},{6,2},{1... | collective-permute-start | bytes 786440 | tf_op jit(solution)/shard_map/ppermute | solution.py:543
  24.8 3.4 %shard_map.116 = (bf16[1024,128]{1,0:T(8,128)(2,1)S(1)}, f32[1024,256]{1,0:T(8,128)S(1)}, bf16[128,1024]{1,0:T(8,128)(2,1)S(1)}, bf16[256,256]{1,0:T(8,128)(2,1)S(1)}) custom-call(bf16[1024,256]{1,0:T(8,128)(2,1)S(1)} %shard_map.109.refs_0_.refs_4_, bf16[1024,256]{1,0:T(8,128)(2,1)S(1)} %shard_map.112.refs_9_.refs_1_, ...), custom_call_target="tpu_custom_call" | custom-call | flops 4600000000 | bytes 1 | tf_op jit(solution)/shard_map/pallas_call | solution.py:42
  28.7 0.6 collective-permute-start.7
  29.3 3.0 %collective-permute-done.4.refs_1_ = bf16[512,256]{1,0:T(8,128)(2,1)S(1)} collective-permute-done((bf16[512,256]{1,0:T(8,128)(2,1)S(1)}, bf16[512,256]{1,0:T(8,128)(2,1)S(1)}, u32[]{:S(2)}, u32[]{:S(2)}) %collective-permute-start.4) | collective-permute-done | bytes 262176 | tf_op jit(solution)/shard_map/ppermute | solution.py:543
  32.6 4.0 %shard_map.120 = (bf16[1024,256]{1,0:T(8,128)(2,1)S(1)}, f32[1024,256]{1,0:T(8,128)S(1)}, bf16[768,256]{1,0:T(8,128)(2,1)S(1)}, bf16[512,256]{1,0:T(8,128)(2,1)S...) custom-call(bf16[1024,256]{1,0:T(8,128)(2,1)S(1)} %shard_map.109.refs_0_.refs_4_, ...), custom_call_target="tpu_custom_call" | custom-call | flops 4600000000 | bytes 1 | tf_op jit(solution)/shard_map/pallas_call | solution.py:42
  36.7 3.1 %collective-permute-start.11 = (bf16[64,512]{1,0:T(8,128)(2,1)S(1)}, bf16[64,512]{1,0:T(8,128)(2,1)S(1)}, u32[]{:S(2)}, u32[]{:S(2)}) collective-permute-start(bf16[64,512]{1,0:T(8,128)(2,1)S(1)} %get-tuple-element.81), channel_id=1, source_target_pairs={{0,8},{4,12},{8,0},{12,4},{1,9},{5,13},{9,1},{13,5},{2,10},{6,14},... | collective-permute-start | bytes 196616 | tf_op jit(solution)/shard_map/ppermute | solution.py:543
  39.8 1.3 %collective-permute-start.12 = (bf16[64,512]{1,0:T(8,128)(2,1)S(1)}, bf16[64,512]{1,0:T(8,128)(2,1)S(1)}, u32[]{:S(2)}, u32[]{:S(2)}) collective-permute-start(bf16[64,512]{1,0:T(8,128)(2,1)S(1)} %get-tuple-element.82), channel_id=1, source_target_pairs={{0,12},{4,8},{8,4},{12,0},{1,13},{5,9},{9,5},{13,1},{2,14},{6,10},... | collective-permute-start | bytes 196616 | tf_op jit(solution)/shard_map/ppermute | solution.py:543
  41.5 3.7 %collective-permute-start.8 = (bf16[512,256]{1,0:T(8,128)(2,1)S(1)}, bf16[512,256]{1,0:T(8,128)(2,1)S(1)}, u32[]{:S(2)}, u32[]{:S(2)}) collective-permute-start(bf16[512,256]{1,0:T(8,128)(2,1)S(1)} %get-tuple-element.77), channel_id=1, source_target_pairs={{0,4},{4,0},{8,12},{12,8},{1,5},{5,1},{9,13},{13,9},{2,6},{6,2},{1... | collective-permute-start | bytes 786440 | tf_op jit(solution)/shard_map/ppermute | solution.py:543
  45.2 1.5 %collective-permute-start.5 = (bf16[1024,256]{1,0:T(8,128)(2,1)S(1)}, bf16[1024,256]{1,0:T(8,128)(2,1)S(1)}, u32[]{:S(2)}, u32[]{:S(2)}) collective-permute-start(bf16[1024,256]{1,0:T(8,128)(2,1)S(1)} %get-tuple-element.72), channel_id=1, source_target_pairs={{0,2},{1,3},{2,0},{3,1},{4,6},{5,7},{6,4},{7,5},{8,10},{9,11},{10,... | collective-permute-start | bytes 1572872 | tf_op jit(solution)/shard_map/ppermute | solution.py:543
  46.7 7.1 %collective-permute-done.10.refs_2_.refs_1_ = bf16[768,256]{1,0:T(8,128)(2,1)S(1)} collective-permute-done((bf16[768,256]{1,0:T(8,128)(2,1)S(1)}, bf16[768,256]{1,0:T(8,128)(2,1)S(1)}, u32[]{:S(2)}, u32[]{:S(2)}) %collective-permute-start.10) | collective-permute-done | bytes 393248 | tf_op jit(solution)/shard_map/ppermute | solution.py:543
  53.9 1.0 %shard_map.123 = (bf16[1024,256]{1,0:T(8,128)(2,1)S(1)}, bf16[1024,256]{1,0:T(8,128)(2,1)S(1)}, bf16[512,1024]{1,0:T(8,128)(2,1)S(1)}) custom-call(f32[1024,256]{1,0:T(8,128)S(1)} %get-tuple-element.78.refs_0_, f32[1024,256]{1,0:T(8,128)S(1)} %get-tuple-element.79.refs_1_, bf16[768,256]{1,0:T(8,128)(2,1)S(1)} %collective-permute-done.10.refs_2_.refs_1_, ...), custom_call_target="tpu_custom_call" | custom-call | flops 230000000 | bytes 1 | tf_op jit(solution)/shard_map/pallas_call | solution.py:42
  54.9 0.5 shard_map.124.refs_2_.refs_3_.refs_0_
  55.7 2.7 %collective-permute-done.8.refs_1_.refs_3_ = bf16[512,256]{1,0:T(8,128)(2,1)S(1)} collective-permute-done((bf16[512,256]{1,0:T(8,128)(2,1)S(1)}, bf16[512,256]{1,0:T(8,128)(2,1)S(1)}, u32[]{:S(2)}, u32[]{:S(2)}) %collective-permute-start.8) | collective-permute-done | bytes 262176 | tf_op jit(solution)/shard_map/ppermute | solution.py:543
  58.6 1.5 %collective-permute-start.15 = (bf16[512,256]{1,0:T(8,128)(2,1)S(1)}, bf16[512,256]{1,0:T(8,128)(2,1)S(1)}, u32[]{:S(2)}, u32[]{:S(2)}) collective-permute-start(bf16[512,256]{1,0:T(8,128)(2,1)S(1)} %get-tuple-element.90), channel_id=1, source_target_pairs={{0,4},{4,0},{8,12},{12,8},{1,5},{5,1},{9,13},{13,9},{2,6},{6,2},{1... | collective-permute-start | bytes 786440 | tf_op jit(solution)/shard_map/ppermute | solution.py:543
  60.1 0.5 shard_map.128.refs_3_.refs_4_.refs_0_
  60.7 3.9 %collective-permute-start.19 = (bf16[512,256]{1,0:T(8,128)(2,1)S(1)}, bf16[512,256]{1,0:T(8,128)(2,1)S(1)}, u32[]{:S(2)}, u32[]{:S(2)}) collective-permute-start(bf16[512,256]{1,0:T(8,128)(2,1)S(1)} %get-tuple-element.96), channel_id=1, source_target_pairs={{0,4},{4,0},{8,12},{12,8},{1,5},{5,1},{9,13},{13,9},{2,6},{6,2},{1... | collective-permute-start | bytes 786440 | tf_op jit(solution)/shard_map/ppermute | solution.py:543
  64.6 0.5 shard_map.130.refs_7_.refs_3_.refs_0_
  65.2 1.8 %shard_map.131 = (bf16[1024,512]{1,0:T(8,128)(2,1)S(1)}, bf16[1024,512]{1,0:T(8,128)(2,1)S(1)}) custom-call(s32[1]{0:T(128)} %bitcast.refs_4_.refs_0_, bf16[1024,256]{1,0:T(8,128)(2,1)S(1)} %get-tuple-element.76.refs_2_.refs_1_, bf16[1024,256]{1,0:T(8,128)(2,1)S(1)} %get-tuple-element.85.refs_2_, bf16[1024,256]{1,0:T(8,128)(2,1)S(1)} %get-tuple-element.88.refs_3_, ...), custom_call_target="tpu_custom_call" | custom-call | flops 1150000000 | bytes 1 | tf_op jit(solution)/shard_map/pallas_call | solution.py:42
  67.0 0.7 collective-permute-done.15.refs_1_.refs_4_
  68.0 0.6 collective-permute-start.16
  68.6 2.3 %collective-permute-start.17 = (bf16[512,256]{1,0:T(8,128)(2,1)S(1)}, bf16[512,256]{1,0:T(8,128)(2,1)S(1)}, u32[]{:S(2)}, u32[]{:S(2)}) collective-permute-start(bf16[512,256]{1,0:T(8,128)(2,1)S(1)} %get-tuple-element.94), channel_id=1, source_target_pairs={{0,4},{4,0},{8,12},{12,8},{1,5},{5,1},{9,13},{13,9},{2,6},{6,2},{1... | collective-permute-start | bytes 786440 | tf_op jit(solution)/shard_map/ppermute | solution.py:543
  71.0 0.9 shard_map.135
  71.9 0.5 shard_map.136.refs_2_.refs_3_.refs_0_
  72.4 0.9 collective-permute-done.19.refs_1_.refs_3_
  73.6 2.5 %collective-permute-start.21 = (bf16[512,256]{1,0:T(8,128)(2,1)S(1)}, bf16[512,256]{1,0:T(8,128)(2,1)S(1)}, u32[]{:S(2)}, u32[]{:S(2)}) collective-permute-start(bf16[512,256]{1,0:T(8,128)(2,1)S(1)} %get-tuple-element.101), channel_id=1, source_target_pairs={{0,4},{4,0},{8,12},{12,8},{1,5},{5,1},{9,13},{13,9},{2,6},{6,2},{1... | collective-permute-start | bytes 786440 | tf_op jit(solution)/shard_map/ppermute | solution.py:543
  76.1 0.8 shard_map.139
  76.9 2.0 %collective-permute-done.17.refs_1_.refs_4_ = bf16[512,256]{1,0:T(8,128)(2,1)S(1)} collective-permute-done((bf16[512,256]{1,0:T(8,128)(2,1)S(1)}, bf16[512,256]{1,0:T(8,128)(2,1)S(1)}, u32[]{:S(2)}, u32[]{:S(2)}) %collective-permute-start.17) | collective-permute-done | bytes 262176 | tf_op jit(solution)/shard_map/ppermute | solution.py:543
  79.5 2.1 %collective-permute-start.24 = (bf16[512,256]{1,0:T(8,128)(2,1)S(1)}, bf16[512,256]{1,0:T(8,128)(2,1)S(1)}, u32[]{:S(2)}, u32[]{:S(2)}) collective-permute-start(bf16[512,256]{1,0:T(8,128)(2,1)S(1)} %shard_map.142.refs_2_), channel_id=1, source_target_pairs={{0,4},{4,0},{8,12},{12,8},{1,5},{5,1},{9,13},{13,9},{2,6},{6,2},{1... | collective-permute-start | bytes 786440 | tf_op jit(solution)/shard_map/ppermute | solution.py:543
  81.6 3.0 %collective-permute-done.21.refs_1_.refs_3_ = bf16[512,256]{1,0:T(8,128)(2,1)S(1)} collective-permute-done((bf16[512,256]{1,0:T(8,128)(2,1)S(1)}, bf16[512,256]{1,0:T(8,128)(2,1)S(1)}, u32[]{:S(2)}, u32[]{:S(2)}) %collective-permute-start.21) | collective-permute-done | bytes 262176 | tf_op jit(solution)/shard_map/ppermute | solution.py:543
  84.7 1.7 %collective-permute-start.20 = (bf16[1024,256]{1,0:T(8,128)(2,1)S(1)}, bf16[1024,256]{1,0:T(8,128)(2,1)S(1)}, u32[]{:S(2)}, u32[]{:S(2)}) collective-permute-start(bf16[1024,256]{1,0:T(8,128)(2,1)S(1)} %get-tuple-element.100), channel_id=1, source_target_pairs={{0,2},{1,3},{2,0},{3,1},{4,6},{5,7},{6,4},{7,5},{8,10},{9,11},{10,... | collective-permute-start | bytes 1572872 | tf_op jit(solution)/shard_map/ppermute | solution.py:543
  86.4 0.8 shard_map.144
  87.3 2.1 %collective-permute-start.26 = (bf16[512,256]{1,0:T(8,128)(2,1)S(1)}, bf16[512,256]{1,0:T(8,128)(2,1)S(1)}, u32[]{:S(2)}, u32[]{:S(2)}) collective-permute-start(bf16[512,256]{1,0:T(8,128)(2,1)S(1)} %shard_map.145.refs_5_.refs_1_), channel_id=1, source_target_pairs={{0,4},{4,0},{8,12},{12,8},{1,5},{5,1},{9,13},{13,9},{2,6},{6,2},{1... | collective-permute-start | bytes 786440 | tf_op jit(solution)/shard_map/ppermute | solution.py:543
  89.8 0.8 shard_map.146
  90.7 2.8 %collective-permute-start.27 = (bf16[512,256]{1,0:T(8,128)(2,1)S(1)}, bf16[512,256]{1,0:T(8,128)(2,1)S(1)}, u32[]{:S(2)}, u32[]{:S(2)}) collective-permute-start(bf16[512,256]{1,0:T(8,128)(2,1)S(1)} %shard_map.147.refs_2_), channel_id=1, source_target_pairs={{0,4},{4,0},{8,12},{12,8},{1,5},{5,1},{9,13},{13,9},{2,6},{6,2},{1... | collective-permute-start | bytes 786440 | tf_op jit(solution)/shard_map/ppermute | solution.py:543
  93.5 5.6 %collective-permute-done.20.refs_1_ = bf16[1024,256]{1,0:T(8,128)(2,1)S(1)} collective-permute-done((bf16[1024,256]{1,0:T(8,128)(2,1)S(1)}, bf16[1024,256]{1,0:T(8,128)(2,1)S(1)}, u32[]{:S(2)}, u32[]{:S(2)}) %collective-permute-start.20) | collective-permute-done | bytes 524320 | tf_op jit(solution)/shard_map/ppermute | solution.py:543
  99.1 0.9 shard_map.148
  100.0 1.4 %collective-permute-done.27.refs_4_ = bf16[512,256]{1,0:T(8,128)(2,1)S(1)} collective-permute-done((bf16[512,256]{1,0:T(8,128)(2,1)S(1)}, bf16[512,256]{1,0:T(8,128)(2,1)S(1)}, u32[]{:S(2)}, u32[]{:S(2)}) %collective-permute-start.27) | collective-permute-done | bytes 262176 | tf_op jit(solution)/shard_map/ppermute | solution.py:543
  101.4 0.8 shard_map.149
  (67 shorter events, 4.0 us)
Async XLA Ops:
  0.6 11.2 %copy-start = (bf16[1024,1024]{1,0:T(8,128)(2,1)S(1)}, bf16[1024,1024]{1,0:T(8,128)(2,1)}, u32[]{:S(2)}) copy-start(bf16[1024,1024]{1,0:T(8,128)(2,1)} %refs_1_.17) | copy-start | bytes 6291460
  0.7 11.1 %copy-start.3 = (bf16[1024,256]{1,0:T(8,128)(2,1)S(1)}, bf16[1024,256]{1,0:T(8,128)(2,1)}, u32[]{:S(2)}) copy-start(bf16[1024,256]{1,0:T(8,128)(2,1)} %refs_4_.1) | copy-start | bytes 1572868
  6.0 6.5 %copy-start.6 = (bf16[1024,512]{1,0:T(8,128)(2,1)S(1)}, bf16[1024,512]{1,0:T(8,128)(2,1)}, u32[]{:S(2)}) copy-start(bf16[1024,512]{1,0:T(8,128)(2,1)} %get-tuple-element.58.refs_1_.refs_3_.refs_4_) | copy-start | bytes 3145732
  6.0 6.5 %copy-start.7 = (bf16[512,512]{1,0:T(8,128)(2,1)S(1)}, bf16[512,512]{1,0:T(8,128)(2,1)}, u32[]{:S(2)}) copy-start(bf16[512,512]{1,0:T(8,128)(2,1)} %get-tuple-element.59.refs_2_.refs_4_.refs_5_) | copy-start | bytes 1572868
  6.0 6.5 %copy-start.8 = (bf16[256,512]{1,0:T(8,128)(2,1)S(1)}, bf16[256,512]{1,0:T(8,128)(2,1)}, u32[]{:S(2)}) copy-start(bf16[256,512]{1,0:T(8,128)(2,1)} %get-tuple-element.60.refs_3_.refs_5_.refs_6_) | copy-start | bytes 786436
  6.0 9.6 %collective-permute-start.2 = (bf16[64,512]{1,0:T(8,128)(2,1)}, bf16[64,512]{1,0:T(8,128)(2,1)S(1)}, u32[]{:S(2)}, u32[]{:S(2)}) collective-permute-start(bf16[64,512]{1,0:T(8,128)(2,1)} %get-tuple-element.64), channel_id=1, source_target_pairs={{0,12},{4,8},{8,4},{12,0},{1,13},{5,9},{9,5},{13,1},{2,14},{6,10},... | collective-permute-start | bytes 196616 | tf_op jit(solution)/shard_map/ppermute | solution.py:543
  11.2 5.9 %collective-permute-start.1 = (bf16[64,512]{1,0:T(8,128)(2,1)}, bf16[64,512]{1,0:T(8,128)(2,1)S(1)}, u32[]{:S(2)}, u32[]{:S(2)}) collective-permute-start(bf16[64,512]{1,0:T(8,128)(2,1)} %get-tuple-element.64), channel_id=1, source_target_pairs={{0,8},{4,12},{8,0},{12,4},{1,9},{5,13},{9,1},{13,5},{2,10},{6,14},... | collective-permute-start | bytes 196616 | tf_op jit(solution)/shard_map/ppermute | solution.py:543
  11.2 6.8 %collective-permute-start = (bf16[128,512]{1,0:T(8,128)(2,1)}, bf16[128,512]{1,0:T(8,128)(2,1)S(1)}, u32[]{:S(2)}, u32[]{:S(2)}) collective-permute-start(bf16[128,512]{1,0:T(8,128)(2,1)} %get-tuple-element.63), channel_id=1, source_target_pairs={{0,4},{4,0},{8,12},{12,8},{1,5},{5,1},{9,13},{13,9},{2,6},{6,2},{1... | collective-permute-start | bytes 393224 | tf_op jit(solution)/shard_map/ppermute | solution.py:543
  12.5 2.4 %copy-start.1 = (bf16[1024,1024]{1,0:T(8,128)(2,1)S(1)}, bf16[1024,1024]{1,0:T(8,128)(2,1)}, u32[]{:S(2)}) copy-start(bf16[1024,1024]{1,0:T(8,128)(2,1)} %refs_1_.13) | copy-start | bytes 6291460
  12.6 2.4 %copy-start.2 = (bf16[1024,256]{1,0:T(8,128)(2,1)S(1)}, bf16[1024,256]{1,0:T(8,128)(2,1)}, u32[]{:S(2)}) copy-start(bf16[1024,256]{1,0:T(8,128)(2,1)} %refs_2_.3) | copy-start | bytes 1572868
  23.1 9.3 %collective-permute-start.3 = (bf16[1024,512]{1,0:T(8,128)(2,1)S(1)}, bf16[1024,512]{1,0:T(8,128)(2,1)S(1)}, u32[]{:S(2)}, u32[]{:S(2)}) collective-permute-start(bf16[1024,512]{1,0:T(8,128)(2,1)S(1)} %get-tuple-element.68), channel_id=1, source_target_pairs={{0,1},{1,0},{2,3},{3,2},{4,5},{5,4},{6,7},{7,6},{8,9},{9,8},{10,11... | collective-permute-start | bytes 3145736 | tf_op jit(solution)/shard_map/ppermute | solution.py:543
  23.2 9.1 %collective-permute-start.4 = (bf16[512,256]{1,0:T(8,128)(2,1)S(1)}, bf16[512,256]{1,0:T(8,128)(2,1)S(1)}, u32[]{:S(2)}, u32[]{:S(2)}) collective-permute-start(bf16[512,256]{1,0:T(8,128)(2,1)S(1)} %shard_map.114.refs_3_.refs_0_), channel_id=1, source_target_pairs={{0,4},{4,0},{8,12},{12,8},{1,5},{5,1},{9,13},{13,9},{2,6},{6,2},{1... | collective-permute-start | bytes 786440 | tf_op jit(solution)/shard_map/ppermute | solution.py:543
  28.7 12.4 %collective-permute-start.7 = (bf16[512,256]{1,0:T(8,128)(2,1)S(1)}, bf16[512,256]{1,0:T(8,128)(2,1)S(1)}, u32[]{:S(2)}, u32[]{:S(2)}) collective-permute-start(bf16[512,256]{1,0:T(8,128)(2,1)S(1)} %shard_map.117.refs_2_.refs_0_), channel_id=1, source_target_pairs={{0,4},{4,0},{8,12},{12,8},{1,5},{5,1},{9,13},{13,9},{2,6},{6,2},{1... | collective-permute-start | bytes 786440 | tf_op jit(solution)/shard_map/ppermute | solution.py:543
  32.3 9.0 %collective-permute-start.6 = (bf16[512,256]{1,0:T(8,128)(2,1)S(1)}, bf16[512,256]{1,0:T(8,128)(2,1)S(1)}, u32[]{:S(2)}, u32[]{:S(2)}) collective-permute-start(bf16[512,256]{1,0:T(8,128)(2,1)S(1)} %shard_map.118.refs_2_.refs_1_), channel_id=1, source_target_pairs={{0,1},{1,0},{2,3},{3,2},{4,8},{5,9},{6,10},{7,11},{8,4},{9,5},{10,... | collective-permute-start | bytes 786440 | tf_op jit(solution)/shard_map/ppermute | solution.py:700
  36.7 8.6 %collective-permute-start.11 = (bf16[64,512]{1,0:T(8,128)(2,1)S(1)}, bf16[64,512]{1,0:T(8,128)(2,1)S(1)}, u32[]{:S(2)}, u32[]{:S(2)}) collective-permute-start(bf16[64,512]{1,0:T(8,128)(2,1)S(1)} %get-tuple-element.81), channel_id=1, source_target_pairs={{0,8},{4,12},{8,0},{12,4},{1,9},{5,13},{9,1},{13,5},{2,10},{6,14},... | collective-permute-start | bytes 196616 | tf_op jit(solution)/shard_map/ppermute | solution.py:543
  39.8 6.9 %collective-permute-start.12 = (bf16[64,512]{1,0:T(8,128)(2,1)S(1)}, bf16[64,512]{1,0:T(8,128)(2,1)S(1)}, u32[]{:S(2)}, u32[]{:S(2)}) collective-permute-start(bf16[64,512]{1,0:T(8,128)(2,1)S(1)} %get-tuple-element.82), channel_id=1, source_target_pairs={{0,12},{4,8},{8,4},{12,0},{1,13},{5,9},{9,5},{13,1},{2,14},{6,10},... | collective-permute-start | bytes 196616 | tf_op jit(solution)/shard_map/ppermute | solution.py:543
  41.1 12.8 %collective-permute-start.10 = (bf16[768,256]{1,0:T(8,128)(2,1)S(1)}, bf16[768,256]{1,0:T(8,128)(2,1)S(1)}, u32[]{:S(2)}, u32[]{:S(2)}) collective-permute-start(bf16[768,256]{1,0:T(8,128)(2,1)S(1)} %get-tuple-element.80.refs_0_), channel_id=1, source_target_pairs={{0,4},{4,0},{8,12},{12,8},{1,5},{5,1},{9,13},{13,9},{2,6},{6,2},{1... | collective-permute-start | bytes 1179656 | tf_op jit(solution)/shard_map/ppermute | solution.py:543
  41.2 14.4 %collective-permute-start.9 = (bf16[512,256]{1,0:T(8,128)(2,1)S(1)}, bf16[512,256]{1,0:T(8,128)(2,1)S(1)}, u32[]{:S(2)}, u32[]{:S(2)}) collective-permute-start(bf16[512,256]{1,0:T(8,128)(2,1)S(1)} %shard_map.121.refs_4_.refs_1_), channel_id=1, source_target_pairs={{0,1},{1,0},{2,3},{3,2},{4,8},{5,9},{6,10},{7,11},{8,4},{9,5},{10,... | collective-permute-start | bytes 786440 | tf_op jit(solution)/shard_map/ppermute | solution.py:700
  41.5 16.9 %collective-permute-start.8 = (bf16[512,256]{1,0:T(8,128)(2,1)S(1)}, bf16[512,256]{1,0:T(8,128)(2,1)S(1)}, u32[]{:S(2)}, u32[]{:S(2)}) collective-permute-start(bf16[512,256]{1,0:T(8,128)(2,1)S(1)} %get-tuple-element.77), channel_id=1, source_target_pairs={{0,4},{4,0},{8,12},{12,8},{1,5},{5,1},{9,13},{13,9},{2,6},{6,2},{1... | collective-permute-start | bytes 786440 | tf_op jit(solution)/shard_map/ppermute | solution.py:543
  45.2 25.7 %collective-permute-start.5 = (bf16[1024,256]{1,0:T(8,128)(2,1)S(1)}, bf16[1024,256]{1,0:T(8,128)(2,1)S(1)}, u32[]{:S(2)}, u32[]{:S(2)}) collective-permute-start(bf16[1024,256]{1,0:T(8,128)(2,1)S(1)} %get-tuple-element.72), channel_id=1, source_target_pairs={{0,2},{1,3},{2,0},{3,1},{4,6},{5,7},{6,4},{7,5},{8,10},{9,11},{10,... | collective-permute-start | bytes 1572872 | tf_op jit(solution)/shard_map/ppermute | solution.py:543
  55.5 5.1 %collective-permute-start.14 = (bf16[512,256]{1,0:T(8,128)(2,1)S(1)}, bf16[512,256]{1,0:T(8,128)(2,1)S(1)}, u32[]{:S(2)}, u32[]{:S(2)}) collective-permute-start(bf16[512,256]{1,0:T(8,128)(2,1)S(1)} %shard_map.125.refs_4_.refs_1_), channel_id=1, source_target_pairs={{0,1},{1,0},{2,3},{3,2},{4,8},{5,9},{6,10},{7,11},{8,4},{9,5},{10,... | collective-permute-start | bytes 786440 | tf_op jit(solution)/shard_map/ppermute | solution.py:700
  58.5 10.0 %collective-permute-start.13 = (bf16[512,256]{1,0:T(8,128)(2,1)S(1)}, bf16[512,256]{1,0:T(8,128)(2,1)S(1)}, u32[]{:S(2)}, u32[]{:S(2)}) collective-permute-start(bf16[512,256]{1,0:T(8,128)(2,1)S(1)} %shard_map.127.refs_2_.refs_1_), channel_id=1, source_target_pairs={{0,1},{1,0},{2,3},{3,2},{4,8},{5,9},{6,10},{7,11},{8,4},{9,5},{10,... | collective-permute-start | bytes 786440 | tf_op jit(solution)/shard_map/ppermute | solution.py:700
  58.6 9.2 %collective-permute-start.15 = (bf16[512,256]{1,0:T(8,128)(2,1)S(1)}, bf16[512,256]{1,0:T(8,128)(2,1)S(1)}, u32[]{:S(2)}, u32[]{:S(2)}) collective-permute-start(bf16[512,256]{1,0:T(8,128)(2,1)S(1)} %get-tuple-element.90), channel_id=1, source_target_pairs={{0,4},{4,0},{8,12},{12,8},{1,5},{5,1},{9,13},{13,9},{2,6},{6,2},{1... | collective-permute-start | bytes 786440 | tf_op jit(solution)/shard_map/ppermute | solution.py:543
  60.7 4.4 %copy-start.4 = (bf16[1024,256]{1,0:T(8,128)(2,1)S(1)}, bf16[1024,256]{1,0:T(8,128)(2,1)}, u32[]{:S(2)}) copy-start(bf16[1024,256]{1,0:T(8,128)(2,1)} %refs_5_.1) | copy-start | bytes 1572868
  60.7 4.4 %copy-start.5 = (bf16[1024,256]{1,0:T(8,128)(2,1)S(1)}, bf16[1024,256]{1,0:T(8,128)(2,1)}, u32[]{:S(2)}) copy-start(bf16[1024,256]{1,0:T(8,128)(2,1)} %refs_6_.1) | copy-start | bytes 1572868
  60.7 12.6 %collective-permute-start.19 = (bf16[512,256]{1,0:T(8,128)(2,1)S(1)}, bf16[512,256]{1,0:T(8,128)(2,1)S(1)}, u32[]{:S(2)}, u32[]{:S(2)}) collective-permute-start(bf16[512,256]{1,0:T(8,128)(2,1)S(1)} %get-tuple-element.96), channel_id=1, source_target_pairs={{0,4},{4,0},{8,12},{12,8},{1,5},{5,1},{9,13},{13,9},{2,6},{6,2},{1... | collective-permute-start | bytes 786440 | tf_op jit(solution)/shard_map/ppermute | solution.py:543
  67.8 5.7 %collective-permute-start.18 = (bf16[512,256]{1,0:T(8,128)(2,1)S(1)}, bf16[512,256]{1,0:T(8,128)(2,1)S(1)}, u32[]{:S(2)}, u32[]{:S(2)}) collective-permute-start(bf16[512,256]{1,0:T(8,128)(2,1)S(1)} %shard_map.132.refs_1_), channel_id=1, source_target_pairs={{0,1},{1,0},{2,3},{3,2},{4,8},{5,9},{6,10},{7,11},{8,4},{9,5},{10,... | collective-permute-start | bytes 786440 | tf_op jit(solution)/shard_map/ppermute | solution.py:700
  68.0 11.2 %collective-permute-start.16 = (bf16[1024,512]{1,0:T(8,128)(2,1)S(1)}, bf16[1024,512]{1,0:T(8,128)(2,1)S(1)}, u32[]{:S(2)}, u32[]{:S(2)}) collective-permute-start(bf16[1024,512]{1,0:T(8,128)(2,1)S(1)} %shard_map.133.refs_4_), channel_id=1, source_target_pairs={{0,1},{1,0},{2,3},{3,2},{4,5},{5,4},{6,7},{7,6},{8,9},{9,8},{10,11... | collective-permute-start | bytes 3145736 | tf_op jit(solution)/shard_map/ppermute | solution.py:543
  68.6 10.4 %collective-permute-start.17 = (bf16[512,256]{1,0:T(8,128)(2,1)S(1)}, bf16[512,256]{1,0:T(8,128)(2,1)S(1)}, u32[]{:S(2)}, u32[]{:S(2)}) collective-permute-start(bf16[512,256]{1,0:T(8,128)(2,1)S(1)} %get-tuple-element.94), channel_id=1, source_target_pairs={{0,4},{4,0},{8,12},{12,8},{1,5},{5,1},{9,13},{13,9},{2,6},{6,2},{1... | collective-permute-start | bytes 786440 | tf_op jit(solution)/shard_map/ppermute | solution.py:543
  73.4 6.0 %collective-permute-start.22 = (bf16[512,256]{1,0:T(8,128)(2,1)S(1)}, bf16[512,256]{1,0:T(8,128)(2,1)S(1)}, u32[]{:S(2)}, u32[]{:S(2)}) collective-permute-start(bf16[512,256]{1,0:T(8,128)(2,1)S(1)} %shard_map.137.refs_4_.refs_0_), channel_id=1, source_target_pairs={{0,1},{1,0},{2,3},{3,2},{4,8},{5,9},{6,10},{7,11},{8,4},{9,5},{10,... | collective-permute-start | bytes 786440 | tf_op jit(solution)/shard_map/ppermute | solution.py:700
  73.6 11.0 %collective-permute-start.21 = (bf16[512,256]{1,0:T(8,128)(2,1)S(1)}, bf16[512,256]{1,0:T(8,128)(2,1)S(1)}, u32[]{:S(2)}, u32[]{:S(2)}) collective-permute-start(bf16[512,256]{1,0:T(8,128)(2,1)S(1)} %get-tuple-element.101), channel_id=1, source_target_pairs={{0,4},{4,0},{8,12},{12,8},{1,5},{5,1},{9,13},{13,9},{2,6},{6,2},{1... | collective-permute-start | bytes 786440 | tf_op jit(solution)/shard_map/ppermute | solution.py:543
  79.0 8.2 %collective-permute-start.25 = (bf16[512,256]{1,0:T(8,128)(2,1)S(1)}, bf16[512,256]{1,0:T(8,128)(2,1)S(1)}, u32[]{:S(2)}, u32[]{:S(2)}) collective-permute-start(bf16[512,256]{1,0:T(8,128)(2,1)S(1)} %shard_map.140.refs_2_.refs_0_), channel_id=1, source_target_pairs={{0,1},{1,0},{2,3},{3,2},{4,8},{5,9},{6,10},{7,11},{8,4},{9,5},{10,... | collective-permute-start | bytes 786440 | tf_op jit(solution)/shard_map/ppermute | solution.py:700
  79.5 10.3 %collective-permute-start.24 = (bf16[512,256]{1,0:T(8,128)(2,1)S(1)}, bf16[512,256]{1,0:T(8,128)(2,1)S(1)}, u32[]{:S(2)}, u32[]{:S(2)}) collective-permute-start(bf16[512,256]{1,0:T(8,128)(2,1)S(1)} %shard_map.142.refs_2_), channel_id=1, source_target_pairs={{0,4},{4,0},{8,12},{12,8},{1,5},{5,1},{9,13},{13,9},{2,6},{6,2},{1... | collective-permute-start | bytes 786440 | tf_op jit(solution)/shard_map/ppermute | solution.py:543
  84.7 5.9 %collective-permute-start.23 = (bf16[512,256]{1,0:T(8,128)(2,1)S(1)}, bf16[512,256]{1,0:T(8,128)(2,1)S(1)}, u32[]{:S(2)}, u32[]{:S(2)}) collective-permute-start(bf16[512,256]{1,0:T(8,128)(2,1)S(1)} %shard_map.143.refs_5_.refs_0_), channel_id=1, source_target_pairs={{0,1},{1,0},{2,3},{3,2},{4,8},{5,9},{6,10},{7,11},{8,4},{9,5},{10,... | collective-permute-start | bytes 786440 | tf_op jit(solution)/shard_map/ppermute | solution.py:700
  84.7 14.3 %collective-permute-start.20 = (bf16[1024,256]{1,0:T(8,128)(2,1)S(1)}, bf16[1024,256]{1,0:T(8,128)(2,1)S(1)}, u32[]{:S(2)}, u32[]{:S(2)}) collective-permute-start(bf16[1024,256]{1,0:T(8,128)(2,1)S(1)} %get-tuple-element.100), channel_id=1, source_target_pairs={{0,2},{1,3},{2,0},{3,1},{4,6},{5,7},{6,4},{7,5},{8,10},{9,11},{10,... | collective-permute-start | bytes 1572872 | tf_op jit(solution)/shard_map/ppermute | solution.py:543
  87.3 12.7 %collective-permute-start.26 = (bf16[512,256]{1,0:T(8,128)(2,1)S(1)}, bf16[512,256]{1,0:T(8,128)(2,1)S(1)}, u32[]{:S(2)}, u32[]{:S(2)}) collective-permute-start(bf16[512,256]{1,0:T(8,128)(2,1)S(1)} %shard_map.145.refs_5_.refs_1_), channel_id=1, source_target_pairs={{0,4},{4,0},{8,12},{12,8},{1,5},{5,1},{9,13},{13,9},{2,6},{6,2},{1... | collective-permute-start | bytes 786440 | tf_op jit(solution)/shard_map/ppermute | solution.py:543
  90.7 10.7 %collective-permute-start.27 = (bf16[512,256]{1,0:T(8,128)(2,1)S(1)}, bf16[512,256]{1,0:T(8,128)(2,1)S(1)}, u32[]{:S(2)}, u32[]{:S(2)}) collective-permute-start(bf16[512,256]{1,0:T(8,128)(2,1)S(1)} %shard_map.147.refs_2_), channel_id=1, source_target_pairs={{0,4},{4,0},{8,12},{12,8},{1,5},{5,1},{9,13},{13,9},{2,6},{6,2},{1... | collective-permute-start | bytes 786440 | tf_op jit(solution)/shard_map/ppermute | solution.py:543

commit v12 on v10

--- a/solution.py
+++ b/solution.py
@@ -313,8 +313,8 @@
     outs = refs[5 + local_levels + fars :]
     dq_ref, dkv_ref = outs[:2]
     term_refs = outs[2 : 2 + pieces]
-    dfar_refs = outs[2 + pieces : 1 + pieces + fars]
-    dmid_refs = outs[1 + pieces + fars : 1 + pieces + fars + mids]
+    dfar_refs = outs[2 + pieces : 2 + pieces + fars]
+    dmid_refs = outs[2 + pieces + fars : 2 + pieces + fars + mids]
     dq_t_ref, acc_ref = outs[-2:]
     tok_rows, inner = q_ref.shape
     heads = inner // HEAD_DIM
@@ -353,16 +353,13 @@
 
     lax.fori_loop(0, tok_rows // (2 * BLOCK), step, 0)
     width = term_refs[-1].shape[0]
-    first = acc_ref[:BLOCK].astype(BF16)
-    term_refs[0][width : width + BLOCK, :] = first[:, :inner]
-    term_refs[0][width + BLOCK :, :] = first[:, inner:]
-    low = BLOCK
+    low = 0
     for ref in dfar_refs:
         ref[...] = acc_ref[low : low + ref.shape[0]].astype(BF16)
         low += ref.shape[0]
     for i, ref in enumerate(term_refs):
         part = dot(dq_t_ref[...], tok_ref[:, i * width : (i + 1) * width])
-        ref[:width, :] = part.astype(BF16).T
+        ref[...] = part.astype(BF16).T
     fan = spread_matrix(2 * BLOCK, 1, 0, BLOCK, 0.5)
     targets = (dkv_ref, *dmid_refs)
     for i in reversed(range(mids)):
@@ -383,9 +380,8 @@
         [query, grad, attended_t, stats, tokens, *levels, *fars],
         after,
         out_shape=[shape(tok_rows, inner), shape(tok_rows, 2 * inner, F32)]
-        + [shape(tokens.shape[1] // pieces + 2 * BLOCK, inner)]
-        + [shape(tokens.shape[1] // pieces, inner)] * (pieces - 1)
-        + [shape(*f.shape) for f in fars[1:]],
+        + [shape(tokens.shape[1] // pieces, inner)] * pieces
+        + [shape(*f.shape) for f in fars],
         scratch_shapes=[pltpu.VMEM(level.shape, F32) for level in levels[1:]]
         + [pltpu.VMEM((inner, tok_rows), BF16), pltpu.VMEM((far_rows, 2 * inner), F32)],
         compiler_params=params(10),
@@ -413,13 +409,10 @@
 
 
 def close_body(local_levels, far_bits, dkv_ref, *refs):
-    joined_ref, *back_refs = refs[: len(far_bits)]
+    backs = [ref[...] for ref in refs[: len(far_bits)]]
     dk_ref, dv_ref, dkv_t_ref = refs[len(far_bits) :]
     inner = dk_ref.shape[1]
     tile = 2 * BLOCK
-    low = joined_ref.shape[0] - 2 * BLOCK
-    joined = [joined_ref[low : low + BLOCK, :], joined_ref[low + BLOCK :, :]]
-    backs = [jnp.concatenate(joined, axis=1)] + [ref[...] for ref in back_refs]
     for t in range(dkv_ref.shape[0] // tile):
         here = slice(t * tile, (t + 1) * tile)
         total = dkv_ref[here, :]
@@ -611,8 +604,8 @@
 
 class Line:
     lag = 3
-    half_weights = (3.0, 3.0, 3.0, 2.5, 2.5, 3.0, 3.0, 3.0)
-    turn_weights = (3.0, 2.5, 2.5, 3.0, 3.0, 3.0, 3.0, 3.0)
+    half_weights = (3.0, 3.0, 3.0, 1.0, 1.0, 3.0, 3.0, 0.5)
+    turn_weights = (6.0, 1.0, 1.0, 1.0, 4.0, 2.0, 0.5, 0.5)
 
     def __init__(self, axis, other, end, step):
         self.axis, self.axes, self.step = axis, (axis, other), step
@@ -716,28 +709,26 @@
     rows = tokens.shape[1] // pieces
     line.enter(step(weight_terms, attended_t, cotangent, inner, 0, 0, pieces))
     line.enter(step(weight_terms, attended_t, cotangent, inner, 0, 1, pieces))
+    dquery, dkv, query_first, query_second, *away = step(
+        backward, query, grad, attended_t, stats, tokens, levels, fars, far_bits, pieces
+    )
+    backs = [exchange(piece, "seq", d) for d, piece in enumerate(away, 1)]
+    line.meet(rows)
+    line.meet(rows)
+    dkey, dvalue, dkv_t = step(close_keys, dkv, backs, far_bits, local_levels)
+    line.enter(step(relay, query_first))
     parts = step(project_split, rank, [attended], [w_out], "head")
     mixed = Scatter(parts, "head", step)
-    dquery, dkv, query_first, query_second, *away = step(
-        backward, query, grad, attended_t, stats, tokens, levels, fars, far_bits, pieces
-    )
-    line.enter(query_first)
-    backs = [exchange(piece, "seq", d) for d, piece in enumerate(away, 2)]
+    line.turn(query_second)
+    key_first = step(weight_terms, dkv_t, tokens, inner, 0, 0, pieces)
+    key_second = step(weight_terms, dkv_t, tokens, inner, 0, 1, pieces)
+    keep, send = step(project_split, rank, [dquery, dkey, dvalue], [w_query, w_key, w_value], "head")
     line.meet(rows)
     mixed.advance()
-    line.meet(rows)
-    line.turn(query_second)
-    dkey, dvalue, dkv_t = step(
-        close_keys, dkv, [line.into[2], *backs], far_bits, local_levels
-    )
-    key_first = step(weight_terms, dkv_t, tokens, inner, 0, 0, pieces)
-    line.meet(rows)
     line.turn(key_first)
     line.meet(rows)
-    key_second = step(weight_terms, dkv_t, tokens, inner, 0, 1, pieces)
+    value_first = step(weight_terms, dkv_t, tokens, inner, 1, 0, pieces)
     line.turn(key_second)
-    value_first = step(weight_terms, dkv_t, tokens, inner, 1, 0, pieces)
-    keep, send = step(project_split, rank, [dquery, dkey, dvalue], [w_query, w_key, w_value], "head")
     line.meet(rows)
     tokens_grad = Scatter([keep, step(relay, send)], "head", step)
     line.turn(value_first)

time: 97.7 us -> 98.6 us (level)
  waiting for transfers between devices: 12.1 us -> 30 us
  starting transfers between devices: 50.6 us -> 32.9 us
    ppermute x20 -> x21, waiting for transfers between devices: 11.4 us -> 29.9 us  [exchange(): return lax.ppermute(block, axis, [(i, i ^ distance) for i in range(count)])]
    ppermute x20 -> x21, starting transfers between devices: 49.4 us -> 32.4 us  [exchange(): return lax.ppermute(block, axis, [(i, i ^ distance) for i in range(count)])]
    pallas_call x40 -> x41, Pallas kernels: 33.7 us -> 33.7 us  [run(): return pl.pallas_call(kernel, in_specs=in_specs, **options)(*ready, *after)]
  transfers between devices with their start and end apart: 28 -> 29, of which waited for: 7 -> 16; matrix products, arithmetic and copies ran while one was open for 0% -> 0% of each run, Pallas kernels for 23% -> 23%
where the time goes in v12:
time: 98.6 us; the launch traced here: 98.4 us
  Pallas kernels  33.7 us (34%)
  starting transfers between devices  32.9 us (33%)
  waiting for transfers between devices  30 us (30%)
  between operations  1.12 us (1%)
    pallas_call x41, Pallas kernels, run(): return pl.pallas_call(kernel, in_specs=in_specs, **options)(*ready, *after)  33.7 us
    ppermute x21, starting transfers between devices, exchange(): return lax.ppermute(block, axis, [(i, i ^ distance) for i in range(count)])  32.4 us
    ppermute x21, waiting for transfers between devices, exchange(): return lax.ppermute(block, axis, [(i, i ^ distance) for i in range(count)])  29.9 us
  transfers between devices with their start and end apart: 29, of which 16 were waited for; matrix products, arithmetic and copies ran while one was open for 0% of the time, Pallas kernels for 23%

profile of v12, /device:TPU:0, one launch (start us, length us, event | category | flops | bytes accessed | tf_op | source)
XLA Modules:
  0.0 98.4 jit_solution(4955392394364840087)
XLA Ops:
  0.7 5.3 %shard_map.110 = (bf16[1024,512]{1,0:T(8,128)(2,1)}, bf16[512,512]{1,0:T(8,128)(2,1)}, bf16[256,512]{1,0:T(8,128)(2,1)}, bf16[128,512]{1,0:T(8,128)(2,1)}, bf16[64,512]{1,0:T(8,128)(2,1)}) custom-call(bf16[1024,1024]{1,0:T(8,128)(2,1)} %refs_1_.17, bf16[1024,256]{1,0:T(8,128)(2,1)} %refs_5_.1, bf16[1024,256]{1,0:T(8,128)(2,1)} %refs_6_.1, ...), custom_call_target="tpu_custom_call" | custom-call | flops 5750000128 | bytes 1 | tf_op jit(solution)/shard_map/pallas_call | solution.py:42
  6.0 4.1 %collective-permute-start.1 = (bf16[64,512]{1,0:T(8,128)(2,1)}, bf16[64,512]{1,0:T(8,128)(2,1)S(1)}, u32[]{:S(2)}, u32[]{:S(2)}) collective-permute-start(bf16[64,512]{1,0:T(8,128)(2,1)} %get-tuple-element.61), channel_id=1, source_target_pairs={{0,8},{4,12},{8,0},{12,4},{1,9},{5,13},{9,1},{13,5},{2,10},{6,14},... | collective-permute-start | bytes 196616 | tf_op jit(solution)/shard_map/ppermute | solution.py:476
  10.1 1.3 %collective-permute-start.2 = (bf16[64,512]{1,0:T(8,128)(2,1)}, bf16[64,512]{1,0:T(8,128)(2,1)S(1)}, u32[]{:S(2)}, u32[]{:S(2)}) collective-permute-start(bf16[64,512]{1,0:T(8,128)(2,1)} %get-tuple-element.61), channel_id=1, source_target_pairs={{0,12},{4,8},{8,4},{12,0},{1,13},{5,9},{9,5},{13,1},{2,14},{6,10},... | collective-permute-start | bytes 196616 | tf_op jit(solution)/shard_map/ppermute | solution.py:476
  11.7 0.7 shard_map.109.refs_0_.refs_4_
  12.5 2.3 %shard_map.111 = (f32[4096,256]{1,0:T(8,128)S(1)}, f32[4,1024]{1,0:T(4,128)S(1)}) custom-call(bf16[1024,256]{1,0:T(8,128)(2,1)S(1)} %shard_map.109.refs_0_.refs_4_, bf16[1024,512]{1,0:T(8,128)(2,1)S(1)} %copy-done.6, bf16[512,512]{1,0:T(8,128)(2,1)S(1)} %copy-done.7, bf16[256,512]{1,0:T(8,128)(2,1)S(1)} %copy-done.8, ...), custom_call_target="tpu_custom_call" | custom-call | flops 2644999936 | bytes 1 | tf_op jit(solution)/shard_map/pallas_call | solution.py:42
  14.9 0.7 shard_map.112.refs_9_.refs_1_
  15.6 1.5 %collective-permute-done.2.refs_8_.refs_10_ = bf16[64,512]{1,0:T(8,128)(2,1)S(1)} collective-permute-done((bf16[64,512]{1,0:T(8,128)(2,1)}, bf16[64,512]{1,0:T(8,128)(2,1)S(1)}, u32[]{:S(2)}, u32[]{:S(2)}) %collective-permute-start.2) | collective-permute-done | bytes 65568 | tf_op jit(solution)/shard_map/ppermute | solution.py:476
  17.1 0.8 collective-permute-done.refs_6_.refs_8_
  17.9 3.9 %shard_map.113 = (bf16[1024,256]{1,0:T(8,128)(2,1)S(1)}, bf16[256,1024]{1,0:T(8,128)(2,1)S(1)}, f32[4,1024]{1,0:T(4,128)S(1)}) custom-call(bf16[1024,256]{1,0:T(8,128)(2,1)S(1)} %shard_map.109.refs_0_.refs_4_, f32[4096,256]{1,0:T(8,128)S(1)} %get-tuple-element.58.refs_2_.refs_1_, f32[4,1024]{1,0:T(4,128)S(1)} %get-tuple-element.59.refs_2_, ...), custom_call_target="tpu_custom_call" | custom-call | flops 4600000000 | bytes 1 | tf_op jit(solution)/shard_map/pallas_call | solution.py:42
  22.8 1.0 %collective-permute-start.7 = (bf16[512,256]{1,0:T(8,128)(2,1)S(1)}, bf16[512,256]{1,0:T(8,128)(2,1)S(1)}, u32[]{:S(2)}, u32[]{:S(2)}) collective-permute-start(bf16[512,256]{1,0:T(8,128)(2,1)S(1)} %shard_map.114.refs_2_.refs_0_), channel_id=1, source_target_pairs={{0,4},{4,0},{8,12},{12,8},{1,5},{5,1},{9,13},{13,9},{2,6},{6,2},{1... | collective-permute-start | bytes 786440 | tf_op jit(solution)/shard_map/ppermute | solution.py:476
  23.8 1.1 %collective-permute-start.6 = (bf16[512,256]{1,0:T(8,128)(2,1)S(1)}, bf16[512,256]{1,0:T(8,128)(2,1)S(1)}, u32[]{:S(2)}, u32[]{:S(2)}) collective-permute-start(bf16[512,256]{1,0:T(8,128)(2,1)S(1)} %shard_map.115.refs_11_.refs_0_), channel_id=1, source_target_pairs={{0,4},{4,0},{8,12},{12,8},{1,5},{5,1},{9,13},{13,9},{2,6},{6,2},{1... | collective-permute-start | bytes 786440 | tf_op jit(solution)/shard_map/ppermute | solution.py:476
  24.9 6.9 %shard_map.116 = (bf16[1024,256]{1,0:T(8,128)(2,1)S(1)}, f32[1024,512]{1,0:T(8,128)S(1)}, bf16[512,256]{1,0:T(8,128)(2,1)S(1)}, bf16[512,256]{1,0:T(8,128)(2,1)S...) custom-call(bf16[1024,256]{1,0:T(8,128)(2,1)S(1)} %shard_map.109.refs_0_.refs_4_, ...), custom_call_target="tpu_custom_call" | custom-call | flops 9200000000 | bytes 1 | tf_op jit(solution)/shard_map/pallas_call | solution.py:42
  31.8 1.0 %collective-permute-start.3 = (bf16[128,512]{1,0:T(8,128)(2,1)S(1)}, bf16[128,512]{1,0:T(8,128)(2,1)S(1)}, u32[]{:S(2)}, u32[]{:S(2)}) collective-permute-start(bf16[128,512]{1,0:T(8,128)(2,1)S(1)} %get-tuple-element.67), channel_id=1, source_target_pairs={{0,4},{4,0},{8,12},{12,8},{1,5},{5,1},{9,13},{13,9},{2,6},{6,2},{1... | collective-permute-start | bytes 393224 | tf_op jit(solution)/shard_map/ppermute | solution.py:476
  32.8 2.8 %collective-permute-start.4 = (bf16[64,512]{1,0:T(8,128)(2,1)S(1)}, bf16[64,512]{1,0:T(8,128)(2,1)S(1)}, u32[]{:S(2)}, u32[]{:S(2)}) collective-permute-start(bf16[64,512]{1,0:T(8,128)(2,1)S(1)} %get-tuple-element.68), channel_id=1, source_target_pairs={{0,8},{4,12},{8,0},{12,4},{1,9},{5,13},{9,1},{13,5},{2,10},{6,14},... | collective-permute-start | bytes 196616 | tf_op jit(solution)/shard_map/ppermute | solution.py:476
  35.7 0.6 collective-permute-start.5
  36.4 1.4 %collective-permute-done.6.refs_1_ = bf16[512,256]{1,0:T(8,128)(2,1)S(1)} collective-permute-done((bf16[512,256]{1,0:T(8,128)(2,1)S(1)}, bf16[512,256]{1,0:T(8,128)(2,1)S(1)}, u32[]{:S(2)}, u32[]{:S(2)}) %collective-permute-start.6) | collective-permute-done | bytes 262176 | tf_op jit(solution)/shard_map/ppermute | solution.py:476
  38.0 1.4 %collective-permute-done.4.refs_2_ = bf16[64,512]{1,0:T(8,128)(2,1)S(1)} collective-permute-done((bf16[64,512]{1,0:T(8,128)(2,1)S(1)}, bf16[64,512]{1,0:T(8,128)(2,1)S(1)}, u32[]{:S(2)}, u32[]{:S(2)}) %collective-permute-start.4) | collective-permute-done | bytes 65568 | tf_op jit(solution)/shard_map/ppermute | solution.py:476
  39.4 3.9 %collective-permute-done.5.refs_3_ = bf16[64,512]{1,0:T(8,128)(2,1)S(1)} collective-permute-done((bf16[64,512]{1,0:T(8,128)(2,1)S(1)}, bf16[64,512]{1,0:T(8,128)(2,1)S(1)}, u32[]{:S(2)}, u32[]{:S(2)}) %collective-permute-start.5) | collective-permute-done | bytes 65568 | tf_op jit(solution)/shard_map/ppermute | solution.py:476
  43.3 1.1 %shard_map.119 = (bf16[1024,256]{1,0:T(8,128)(2,1)S(1)}, bf16[1024,256]{1,0:T(8,128)(2,1)S(1)}, bf16[512,1024]{1,0:T(8,128)(2,1)S(1)}) custom-call(f32[1024,512]{1,0:T(8,128)S(1)} %get-tuple-element.66.refs_0_, bf16[128,512]{1,0:T(8,128)(2,1)S(1)} %collective-permute-done.3.refs_1_, bf16[64,512]{1,0:T(8,128)(2,1)S(1)} %collective-permute-done.4.refs_2_, ...), custom_call_target="tpu_custom_call" | custom-call | flops 230000000 | bytes 1 | tf_op jit(solution)/shard_map/pallas_call | solution.py:42
  44.5 0.7 shard_map.121
  45.6 4.0 %collective-permute-start.12 = (bf16[512,256]{1,0:T(8,128)(2,1)S(1)}, bf16[512,256]{1,0:T(8,128)(2,1)S(1)}, u32[]{:S(2)}, u32[]{:S(2)}) collective-permute-start(bf16[512,256]{1,0:T(8,128)(2,1)S(1)} %get-tuple-element.81), channel_id=1, source_target_pairs={{0,4},{4,0},{8,12},{12,8},{1,5},{5,1},{9,13},{13,9},{2,6},{6,2},{1... | collective-permute-start | bytes 786440 | tf_op jit(solution)/shard_map/ppermute | solution.py:476
  50.1 0.5 shard_map.124.refs_7_.refs_3_.refs_0_
  51.3 1.8 %shard_map.125 = (bf16[1024,512]{1,0:T(8,128)(2,1)S(1)}, bf16[1024,512]{1,0:T(8,128)(2,1)S(1)}) custom-call(s32[1]{0:T(128)} %bitcast.refs_4_.refs_0_, bf16[1024,256]{1,0:T(8,128)(2,1)S(1)} %get-tuple-element.70.refs_2_.refs_1_, bf16[1024,256]{1,0:T(8,128)(2,1)S(1)} %get-tuple-element.71.refs_1_.refs_2_, bf16[1024,256]{1,0:T(8,128)(2,1)S(1)} %get-tuple-element.74.refs_3_, ...), custom_call_target="tpu_custom_call" | custom-call | flops 1150000000 | bytes 1 | tf_op jit(solution)/shard_map/pallas_call | solution.py:42
  53.7 1.6 %collective-permute-start.11 = (bf16[1024,256]{1,0:T(8,128)(2,1)S(1)}, bf16[1024,256]{1,0:T(8,128)(2,1)S(1)}, u32[]{:S(2)}, u32[]{:S(2)}) collective-permute-start(bf16[1024,256]{1,0:T(8,128)(2,1)S(1)} %get-tuple-element.80), channel_id=1, source_target_pairs={{0,2},{1,3},{2,0},{3,1},{4,6},{5,7},{6,4},{7,5},{8,10},{9,11},{10,... | collective-permute-start | bytes 1572872 | tf_op jit(solution)/shard_map/ppermute | solution.py:476
  55.4 1.1 %collective-permute-start.15 = (bf16[512,256]{1,0:T(8,128)(2,1)S(1)}, bf16[512,256]{1,0:T(8,128)(2,1)S(1)}, u32[]{:S(2)}, u32[]{:S(2)}) collective-permute-start(bf16[512,256]{1,0:T(8,128)(2,1)S(1)} %get-tuple-element.84), channel_id=1, source_target_pairs={{0,4},{4,0},{8,12},{12,8},{1,5},{5,1},{9,13},{13,9},{2,6},{6,2},{1... | collective-permute-start | bytes 786440 | tf_op jit(solution)/shard_map/ppermute | solution.py:476
  57.6 2.7 %collective-permute-start.20 = (bf16[512,256]{1,0:T(8,128)(2,1)S(1)}, bf16[512,256]{1,0:T(8,128)(2,1)S(1)}, u32[]{:S(2)}, u32[]{:S(2)}) collective-permute-start(bf16[512,256]{1,0:T(8,128)(2,1)S(1)} %get-tuple-element.90), channel_id=1, source_target_pairs={{0,4},{4,0},{8,12},{12,8},{1,5},{5,1},{9,13},{13,9},{2,6},{6,2},{1... | collective-permute-start | bytes 786440 | tf_op jit(solution)/shard_map/ppermute | solution.py:476
  60.2 4.4 %collective-permute-done.15.refs_1_.refs_4_ = bf16[512,256]{1,0:T(8,128)(2,1)S(1)} collective-permute-done((bf16[512,256]{1,0:T(8,128)(2,1)S(1)}, bf16[512,256]{1,0:T(8,128)(2,1)S(1)}, u32[]{:S(2)}, u32[]{:S(2)}) %collective-permute-start.15) | collective-permute-done | bytes 262176 | tf_op jit(solution)/shard_map/ppermute | solution.py:476
  64.8 0.6 collective-permute-start.17
  65.5 1.4 %collective-permute-start.18 = (bf16[512,256]{1,0:T(8,128)(2,1)S(1)}, bf16[512,256]{1,0:T(8,128)(2,1)S(1)}, u32[]{:S(2)}, u32[]{:S(2)}) collective-permute-start(bf16[512,256]{1,0:T(8,128)(2,1)S(1)} %get-tuple-element.88), channel_id=1, source_target_pairs={{0,4},{4,0},{8,12},{12,8},{1,5},{5,1},{9,13},{13,9},{2,6},{6,2},{1... | collective-permute-start | bytes 786440 | tf_op jit(solution)/shard_map/ppermute | solution.py:476
  66.9 1.2 %collective-permute-done.11.refs_1_ = bf16[1024,256]{1,0:T(8,128)(2,1)S(1)} collective-permute-done((bf16[1024,256]{1,0:T(8,128)(2,1)S(1)}, bf16[1024,256]{1,0:T(8,128)(2,1)S(1)}, u32[]{:S(2)}, u32[]{:S(2)}) %collective-permute-start.11) | collective-permute-done | bytes 524320 | tf_op jit(solution)/shard_map/ppermute | solution.py:476
  68.1 0.9 shard_map.135
  69.6 0.7 collective-permute-done.20.refs_1_.refs_3_
  70.5 2.5 %collective-permute-start.22 = (bf16[512,256]{1,0:T(8,128)(2,1)S(1)}, bf16[512,256]{1,0:T(8,128)(2,1)S(1)}, u32[]{:S(2)}, u32[]{:S(2)}) collective-permute-start(bf16[512,256]{1,0:T(8,128)(2,1)S(1)} %get-tuple-element.95), channel_id=1, source_target_pairs={{0,4},{4,0},{8,12},{12,8},{1,5},{5,1},{9,13},{13,9},{2,6},{6,2},{1... | collective-permute-start | bytes 786440 | tf_op jit(solution)/shard_map/ppermute | solution.py:476
  73.0 0.8 shard_map.139
  73.8 2.1 %collective-permute-done.18.refs_1_.refs_4_ = bf16[512,256]{1,0:T(8,128)(2,1)S(1)} collective-permute-done((bf16[512,256]{1,0:T(8,128)(2,1)S(1)}, bf16[512,256]{1,0:T(8,128)(2,1)S(1)}, u32[]{:S(2)}, u32[]{:S(2)}) %collective-permute-start.18) | collective-permute-done | bytes 262176 | tf_op jit(solution)/shard_map/ppermute | solution.py:476
  76.3 1.7 %collective-permute-start.25 = (bf16[512,256]{1,0:T(8,128)(2,1)S(1)}, bf16[512,256]{1,0:T(8,128)(2,1)S(1)}, u32[]{:S(2)}, u32[]{:S(2)}) collective-permute-start(bf16[512,256]{1,0:T(8,128)(2,1)S(1)} %shard_map.142.refs_2_), channel_id=1, source_target_pairs={{0,4},{4,0},{8,12},{12,8},{1,5},{5,1},{9,13},{13,9},{2,6},{6,2},{1... | collective-permute-start | bytes 786440 | tf_op jit(solution)/shard_map/ppermute | solution.py:476
  78.0 1.4 %collective-permute-start.21 = (bf16[1024,256]{1,0:T(8,128)(2,1)S(1)}, bf16[1024,256]{1,0:T(8,128)(2,1)S(1)}, u32[]{:S(2)}, u32[]{:S(2)}) collective-permute-start(bf16[1024,256]{1,0:T(8,128)(2,1)S(1)} %get-tuple-element.94), channel_id=1, source_target_pairs={{0,2},{1,3},{2,0},{3,1},{4,6},{5,7},{6,4},{7,5},{8,10},{9,11},{10,... | collective-permute-start | bytes 1572872 | tf_op jit(solution)/shard_map/ppermute | solution.py:476
  79.4 2.1 %collective-permute-done.22.refs_1_.refs_3_ = bf16[512,256]{1,0:T(8,128)(2,1)S(1)} collective-permute-done((bf16[512,256]{1,0:T(8,128)(2,1)S(1)}, bf16[512,256]{1,0:T(8,128)(2,1)S(1)}, u32[]{:S(2)}, u32[]{:S(2)}) %collective-permute-start.22) | collective-permute-done | bytes 262176 | tf_op jit(solution)/shard_map/ppermute | solution.py:476
  81.6 0.8 shard_map.144
  82.5 1.7 %collective-permute-start.27 = (bf16[512,256]{1,0:T(8,128)(2,1)S(1)}, bf16[512,256]{1,0:T(8,128)(2,1)S(1)}, u32[]{:S(2)}, u32[]{:S(2)}) collective-permute-start(bf16[512,256]{1,0:T(8,128)(2,1)S(1)} %shard_map.145.refs_5_.refs_1_), channel_id=1, source_target_pairs={{0,4},{4,0},{8,12},{12,8},{1,5},{5,1},{9,13},{13,9},{2,6},{6,2},{1... | collective-permute-start | bytes 786440 | tf_op jit(solution)/shard_map/ppermute | solution.py:476
  84.2 2.8 %collective-permute-done.25.refs_4_ = bf16[512,256]{1,0:T(8,128)(2,1)S(1)} collective-permute-done((bf16[512,256]{1,0:T(8,128)(2,1)S(1)}, bf16[512,256]{1,0:T(8,128)(2,1)S(1)}, u32[]{:S(2)}, u32[]{:S(2)}) %collective-permute-start.25) | collective-permute-done | bytes 262176 | tf_op jit(solution)/shard_map/ppermute | solution.py:476
  87.0 0.8 shard_map.146
  87.9 1.6 %collective-permute-start.28 = (bf16[512,256]{1,0:T(8,128)(2,1)S(1)}, bf16[512,256]{1,0:T(8,128)(2,1)S(1)}, u32[]{:S(2)}, u32[]{:S(2)}) collective-permute-start(bf16[512,256]{1,0:T(8,128)(2,1)S(1)} %shard_map.147.refs_2_), channel_id=1, source_target_pairs={{0,4},{4,0},{8,12},{12,8},{1,5},{5,1},{9,13},{13,9},{2,6},{6,2},{1... | collective-permute-start | bytes 786440 | tf_op jit(solution)/shard_map/ppermute | solution.py:476
  89.4 1.4 %collective-permute-done.21.refs_1_ = bf16[1024,256]{1,0:T(8,128)(2,1)S(1)} collective-permute-done((bf16[1024,256]{1,0:T(8,128)(2,1)S(1)}, bf16[1024,256]{1,0:T(8,128)(2,1)S(1)}, u32[]{:S(2)}, u32[]{:S(2)}) %collective-permute-start.21) | collective-permute-done | bytes 524320 | tf_op jit(solution)/shard_map/ppermute | solution.py:476
  90.8 0.9 shard_map.148
  91.7 0.9 collective-permute-done.27.refs_3_
  92.6 5.0 %collective-permute-done.28.refs_4_ = bf16[512,256]{1,0:T(8,128)(2,1)S(1)} collective-permute-done((bf16[512,256]{1,0:T(8,128)(2,1)S(1)}, bf16[512,256]{1,0:T(8,128)(2,1)S(1)}, u32[]{:S(2)}, u32[]{:S(2)}) %collective-permute-start.28) | collective-permute-done | bytes 262176 | tf_op jit(solution)/shard_map/ppermute | solution.py:476
  97.6 0.8 shard_map.149
  (69 shorter events, 6.7 us)
Async XLA Ops:
  0.6 11.1 %copy-start = (bf16[1024,1024]{1,0:T(8,128)(2,1)S(1)}, bf16[1024,1024]{1,0:T(8,128)(2,1)}, u32[]{:S(2)}) copy-start(bf16[1024,1024]{1,0:T(8,128)(2,1)} %refs_1_.17) | copy-start | bytes 6291460
  0.7 11.1 %copy-start.3 = (bf16[1024,256]{1,0:T(8,128)(2,1)S(1)}, bf16[1024,256]{1,0:T(8,128)(2,1)}, u32[]{:S(2)}) copy-start(bf16[1024,256]{1,0:T(8,128)(2,1)} %refs_4_.3) | copy-start | bytes 1572868
  6.0 6.4 %copy-start.6 = (bf16[1024,512]{1,0:T(8,128)(2,1)S(1)}, bf16[1024,512]{1,0:T(8,128)(2,1)}, u32[]{:S(2)}) copy-start(bf16[1024,512]{1,0:T(8,128)(2,1)} %get-tuple-element.55.refs_1_.refs_3_.refs_5_) | copy-start | bytes 3145732
  6.0 6.4 %copy-start.7 = (bf16[512,512]{1,0:T(8,128)(2,1)S(1)}, bf16[512,512]{1,0:T(8,128)(2,1)}, u32[]{:S(2)}) copy-start(bf16[512,512]{1,0:T(8,128)(2,1)} %get-tuple-element.56.refs_2_.refs_4_.refs_6_) | copy-start | bytes 1572868
  6.0 6.4 %copy-start.8 = (bf16[256,512]{1,0:T(8,128)(2,1)S(1)}, bf16[256,512]{1,0:T(8,128)(2,1)}, u32[]{:S(2)}) copy-start(bf16[256,512]{1,0:T(8,128)(2,1)} %get-tuple-element.57.refs_3_.refs_5_.refs_7_) | copy-start | bytes 786436
  6.0 9.5 %collective-permute-start.1 = (bf16[64,512]{1,0:T(8,128)(2,1)}, bf16[64,512]{1,0:T(8,128)(2,1)S(1)}, u32[]{:S(2)}, u32[]{:S(2)}) collective-permute-start(bf16[64,512]{1,0:T(8,128)(2,1)} %get-tuple-element.61), channel_id=1, source_target_pairs={{0,8},{4,12},{8,0},{12,4},{1,9},{5,13},{9,1},{13,5},{2,10},{6,14},... | collective-permute-start | bytes 196616 | tf_op jit(solution)/shard_map/ppermute | solution.py:476
  10.1 7.0 %collective-permute-start.2 = (bf16[64,512]{1,0:T(8,128)(2,1)}, bf16[64,512]{1,0:T(8,128)(2,1)S(1)}, u32[]{:S(2)}, u32[]{:S(2)}) collective-permute-start(bf16[64,512]{1,0:T(8,128)(2,1)} %get-tuple-element.61), channel_id=1, source_target_pairs={{0,12},{4,8},{8,4},{12,0},{1,13},{5,9},{9,5},{13,1},{2,14},{6,10},... | collective-permute-start | bytes 196616 | tf_op jit(solution)/shard_map/ppermute | solution.py:476
  11.5 6.4 %collective-permute-start = (bf16[128,512]{1,0:T(8,128)(2,1)}, bf16[128,512]{1,0:T(8,128)(2,1)S(1)}, u32[]{:S(2)}, u32[]{:S(2)}) collective-permute-start(bf16[128,512]{1,0:T(8,128)(2,1)} %get-tuple-element.60), channel_id=1, source_target_pairs={{0,4},{4,0},{8,12},{12,8},{1,5},{5,1},{9,13},{13,9},{2,6},{6,2},{1... | collective-permute-start | bytes 393224 | tf_op jit(solution)/shard_map/ppermute | solution.py:476
  12.5 2.4 %copy-start.1 = (bf16[1024,1024]{1,0:T(8,128)(2,1)S(1)}, bf16[1024,1024]{1,0:T(8,128)(2,1)}, u32[]{:S(2)}) copy-start(bf16[1024,1024]{1,0:T(8,128)(2,1)} %refs_1_.13) | copy-start | bytes 6291460
  12.5 2.4 %copy-start.2 = (bf16[1024,256]{1,0:T(8,128)(2,1)S(1)}, bf16[1024,256]{1,0:T(8,128)(2,1)}, u32[]{:S(2)}) copy-start(bf16[1024,256]{1,0:T(8,128)(2,1)} %refs_2_.3) | copy-start | bytes 1572868
  22.8 13.5 %collective-permute-start.7 = (bf16[512,256]{1,0:T(8,128)(2,1)S(1)}, bf16[512,256]{1,0:T(8,128)(2,1)S(1)}, u32[]{:S(2)}, u32[]{:S(2)}) collective-permute-start(bf16[512,256]{1,0:T(8,128)(2,1)S(1)} %shard_map.114.refs_2_.refs_0_), channel_id=1, source_target_pairs={{0,4},{4,0},{8,12},{12,8},{1,5},{5,1},{9,13},{13,9},{2,6},{6,2},{1... | collective-permute-start | bytes 786440 | tf_op jit(solution)/shard_map/ppermute | solution.py:476
  23.8 14.1 %collective-permute-start.6 = (bf16[512,256]{1,0:T(8,128)(2,1)S(1)}, bf16[512,256]{1,0:T(8,128)(2,1)S(1)}, u32[]{:S(2)}, u32[]{:S(2)}) collective-permute-start(bf16[512,256]{1,0:T(8,128)(2,1)S(1)} %shard_map.115.refs_11_.refs_0_), channel_id=1, source_target_pairs={{0,4},{4,0},{8,12},{12,8},{1,5},{5,1},{9,13},{13,9},{2,6},{6,2},{1... | collective-permute-start | bytes 786440 | tf_op jit(solution)/shard_map/ppermute | solution.py:476
  31.8 11.5 %collective-permute-start.3 = (bf16[128,512]{1,0:T(8,128)(2,1)S(1)}, bf16[128,512]{1,0:T(8,128)(2,1)S(1)}, u32[]{:S(2)}, u32[]{:S(2)}) collective-permute-start(bf16[128,512]{1,0:T(8,128)(2,1)S(1)} %get-tuple-element.67), channel_id=1, source_target_pairs={{0,4},{4,0},{8,12},{12,8},{1,5},{5,1},{9,13},{13,9},{2,6},{6,2},{1... | collective-permute-start | bytes 393224 | tf_op jit(solution)/shard_map/ppermute | solution.py:476
  32.8 6.6 %collective-permute-start.4 = (bf16[64,512]{1,0:T(8,128)(2,1)S(1)}, bf16[64,512]{1,0:T(8,128)(2,1)S(1)}, u32[]{:S(2)}, u32[]{:S(2)}) collective-permute-start(bf16[64,512]{1,0:T(8,128)(2,1)S(1)} %get-tuple-element.68), channel_id=1, source_target_pairs={{0,8},{4,12},{8,0},{12,4},{1,9},{5,13},{9,1},{13,5},{2,10},{6,14},... | collective-permute-start | bytes 196616 | tf_op jit(solution)/shard_map/ppermute | solution.py:476
  35.7 7.6 %collective-permute-start.5 = (bf16[64,512]{1,0:T(8,128)(2,1)S(1)}, bf16[64,512]{1,0:T(8,128)(2,1)S(1)}, u32[]{:S(2)}, u32[]{:S(2)}) collective-permute-start(bf16[64,512]{1,0:T(8,128)(2,1)S(1)} %get-tuple-element.69), channel_id=1, source_target_pairs={{0,12},{4,8},{8,4},{12,0},{1,13},{5,9},{9,5},{13,1},{2,14},{6,10},... | collective-permute-start | bytes 196616 | tf_op jit(solution)/shard_map/ppermute | solution.py:476
  36.4 8.9 %collective-permute-start.10 = (bf16[512,256]{1,0:T(8,128)(2,1)S(1)}, bf16[512,256]{1,0:T(8,128)(2,1)S(1)}, u32[]{:S(2)}, u32[]{:S(2)}) collective-permute-start(bf16[512,256]{1,0:T(8,128)(2,1)S(1)} %shard_map.117.refs_2_.refs_1_), channel_id=1, source_target_pairs={{0,1},{1,0},{2,3},{3,2},{4,8},{5,9},{6,10},{7,11},{8,4},{9,5},{10,... | collective-permute-start | bytes 786440 | tf_op jit(solution)/shard_map/ppermute | solution.py:633
  37.9 17.3 %collective-permute-start.13 = (bf16[512,256]{1,0:T(8,128)(2,1)S(1)}, bf16[512,256]{1,0:T(8,128)(2,1)S(1)}, u32[]{:S(2)}, u32[]{:S(2)}) collective-permute-start(bf16[512,256]{1,0:T(8,128)(2,1)S(1)} %shard_map.118.refs_4_.refs_1_), channel_id=1, source_target_pairs={{0,1},{1,0},{2,3},{3,2},{4,8},{5,9},{6,10},{7,11},{8,4},{9,5},{10,... | collective-permute-start | bytes 786440 | tf_op jit(solution)/shard_map/ppermute | solution.py:633
  44.4 8.9 %collective-permute-start.9 = (bf16[512,256]{1,0:T(8,128)(2,1)S(1)}, bf16[512,256]{1,0:T(8,128)(2,1)S(1)}, u32[]{:S(2)}, u32[]{:S(2)}) collective-permute-start(bf16[512,256]{1,0:T(8,128)(2,1)S(1)} %shard_map.120.refs_3_.refs_0_), channel_id=1, source_target_pairs={{0,4},{4,0},{8,12},{12,8},{1,5},{5,1},{9,13},{13,9},{2,6},{6,2},{1... | collective-permute-start | bytes 786440 | tf_op jit(solution)/shard_map/ppermute | solution.py:476
  45.2 8.3 %collective-permute-start.8 = (bf16[1024,512]{1,0:T(8,128)(2,1)S(1)}, bf16[1024,512]{1,0:T(8,128)(2,1)S(1)}, u32[]{:S(2)}, u32[]{:S(2)}) collective-permute-start(bf16[1024,512]{1,0:T(8,128)(2,1)S(1)} %get-tuple-element.73), channel_id=1, source_target_pairs={{0,1},{1,0},{2,3},{3,2},{4,5},{5,4},{6,7},{7,6},{8,9},{9,8},{10,11... | collective-permute-start | bytes 3145736 | tf_op jit(solution)/shard_map/ppermute | solution.py:476
  45.6 11.2 %collective-permute-start.12 = (bf16[512,256]{1,0:T(8,128)(2,1)S(1)}, bf16[512,256]{1,0:T(8,128)(2,1)S(1)}, u32[]{:S(2)}, u32[]{:S(2)}) collective-permute-start(bf16[512,256]{1,0:T(8,128)(2,1)S(1)} %get-tuple-element.81), channel_id=1, source_target_pairs={{0,4},{4,0},{8,12},{12,8},{1,5},{5,1},{9,13},{13,9},{2,6},{6,2},{1... | collective-permute-start | bytes 786440 | tf_op jit(solution)/shard_map/ppermute | solution.py:476
  50.1 1.0 %copy-start.4 = (bf16[1024,256]{1,0:T(8,128)(2,1)S(1)}, bf16[1024,256]{1,0:T(8,128)(2,1)}, u32[]{:S(2)}) copy-start(bf16[1024,256]{1,0:T(8,128)(2,1)} %refs_5_.1) | copy-start | bytes 1572868
  50.1 1.2 %copy-start.5 = (bf16[1024,256]{1,0:T(8,128)(2,1)S(1)}, bf16[1024,256]{1,0:T(8,128)(2,1)}, u32[]{:S(2)}) copy-start(bf16[1024,256]{1,0:T(8,128)(2,1)} %refs_6_.1) | copy-start | bytes 1572868
  53.4 4.1 %collective-permute-start.16 = (bf16[512,256]{1,0:T(8,128)(2,1)S(1)}, bf16[512,256]{1,0:T(8,128)(2,1)S(1)}, u32[]{:S(2)}, u32[]{:S(2)}) collective-permute-start(bf16[512,256]{1,0:T(8,128)(2,1)S(1)} %shard_map.126.refs_2_.refs_1_), channel_id=1, source_target_pairs={{0,1},{1,0},{2,3},{3,2},{4,8},{5,9},{6,10},{7,11},{8,4},{9,5},{10,... | collective-permute-start | bytes 786440 | tf_op jit(solution)/shard_map/ppermute | solution.py:633
  53.7 14.4 %collective-permute-start.11 = (bf16[1024,256]{1,0:T(8,128)(2,1)S(1)}, bf16[1024,256]{1,0:T(8,128)(2,1)S(1)}, u32[]{:S(2)}, u32[]{:S(2)}) collective-permute-start(bf16[1024,256]{1,0:T(8,128)(2,1)S(1)} %get-tuple-element.80), channel_id=1, source_target_pairs={{0,2},{1,3},{2,0},{3,1},{4,6},{5,7},{6,4},{7,5},{8,10},{9,11},{10,... | collective-permute-start | bytes 1572872 | tf_op jit(solution)/shard_map/ppermute | solution.py:476
  55.4 9.2 %collective-permute-start.15 = (bf16[512,256]{1,0:T(8,128)(2,1)S(1)}, bf16[512,256]{1,0:T(8,128)(2,1)S(1)}, u32[]{:S(2)}, u32[]{:S(2)}) collective-permute-start(bf16[512,256]{1,0:T(8,128)(2,1)S(1)} %get-tuple-element.84), channel_id=1, source_target_pairs={{0,4},{4,0},{8,12},{12,8},{1,5},{5,1},{9,13},{13,9},{2,6},{6,2},{1... | collective-permute-start | bytes 786440 | tf_op jit(solution)/shard_map/ppermute | solution.py:476
  56.8 8.5 %collective-permute-start.14 = (bf16[512,256]{1,0:T(8,128)(2,1)S(1)}, bf16[512,256]{1,0:T(8,128)(2,1)S(1)}, u32[]{:S(2)}, u32[]{:S(2)}) collective-permute-start(bf16[512,256]{1,0:T(8,128)(2,1)S(1)} %shard_map.129.refs_2_.refs_1_), channel_id=1, source_target_pairs={{0,1},{1,0},{2,3},{3,2},{4,8},{5,9},{6,10},{7,11},{8,4},{9,5},{10,... | collective-permute-start | bytes 786440 | tf_op jit(solution)/shard_map/ppermute | solution.py:633
  57.6 12.7 %collective-permute-start.20 = (bf16[512,256]{1,0:T(8,128)(2,1)S(1)}, bf16[512,256]{1,0:T(8,128)(2,1)S(1)}, u32[]{:S(2)}, u32[]{:S(2)}) collective-permute-start(bf16[512,256]{1,0:T(8,128)(2,1)S(1)} %get-tuple-element.90), channel_id=1, source_target_pairs={{0,4},{4,0},{8,12},{12,8},{1,5},{5,1},{9,13},{13,9},{2,6},{6,2},{1... | collective-permute-start | bytes 786440 | tf_op jit(solution)/shard_map/ppermute | solution.py:476
  64.7 5.7 %collective-permute-start.19 = (bf16[512,256]{1,0:T(8,128)(2,1)S(1)}, bf16[512,256]{1,0:T(8,128)(2,1)S(1)}, u32[]{:S(2)}, u32[]{:S(2)}) collective-permute-start(bf16[512,256]{1,0:T(8,128)(2,1)S(1)} %shard_map.132.refs_1_), channel_id=1, source_target_pairs={{0,1},{1,0},{2,3},{3,2},{4,8},{5,9},{6,10},{7,11},{8,4},{9,5},{10,... | collective-permute-start | bytes 786440 | tf_op jit(solution)/shard_map/ppermute | solution.py:633
  64.8 11.2 %collective-permute-start.17 = (bf16[1024,512]{1,0:T(8,128)(2,1)S(1)}, bf16[1024,512]{1,0:T(8,128)(2,1)S(1)}, u32[]{:S(2)}, u32[]{:S(2)}) collective-permute-start(bf16[1024,512]{1,0:T(8,128)(2,1)S(1)} %shard_map.133.refs_4_), channel_id=1, source_target_pairs={{0,1},{1,0},{2,3},{3,2},{4,5},{5,4},{6,7},{7,6},{8,9},{9,8},{10,11... | collective-permute-start | bytes 3145736 | tf_op jit(solution)/shard_map/ppermute | solution.py:476
  65.5 10.4 %collective-permute-start.18 = (bf16[512,256]{1,0:T(8,128)(2,1)S(1)}, bf16[512,256]{1,0:T(8,128)(2,1)S(1)}, u32[]{:S(2)}, u32[]{:S(2)}) collective-permute-start(bf16[512,256]{1,0:T(8,128)(2,1)S(1)} %get-tuple-element.88), channel_id=1, source_target_pairs={{0,4},{4,0},{8,12},{12,8},{1,5},{5,1},{9,13},{13,9},{2,6},{6,2},{1... | collective-permute-start | bytes 786440 | tf_op jit(solution)/shard_map/ppermute | solution.py:476
  70.3 6.0 %collective-permute-start.23 = (bf16[512,256]{1,0:T(8,128)(2,1)S(1)}, bf16[512,256]{1,0:T(8,128)(2,1)S(1)}, u32[]{:S(2)}, u32[]{:S(2)}) collective-permute-start(bf16[512,256]{1,0:T(8,128)(2,1)S(1)} %shard_map.137.refs_4_.refs_0_), channel_id=1, source_target_pairs={{0,1},{1,0},{2,3},{3,2},{4,8},{5,9},{6,10},{7,11},{8,4},{9,5},{10,... | collective-permute-start | bytes 786440 | tf_op jit(solution)/shard_map/ppermute | solution.py:633
  70.5 11.0 %collective-permute-start.22 = (bf16[512,256]{1,0:T(8,128)(2,1)S(1)}, bf16[512,256]{1,0:T(8,128)(2,1)S(1)}, u32[]{:S(2)}, u32[]{:S(2)}) collective-permute-start(bf16[512,256]{1,0:T(8,128)(2,1)S(1)} %get-tuple-element.95), channel_id=1, source_target_pairs={{0,4},{4,0},{8,12},{12,8},{1,5},{5,1},{9,13},{13,9},{2,6},{6,2},{1... | collective-permute-start | bytes 786440 | tf_op jit(solution)/shard_map/ppermute | solution.py:476
  75.9 6.5 %collective-permute-start.26 = (bf16[512,256]{1,0:T(8,128)(2,1)S(1)}, bf16[512,256]{1,0:T(8,128)(2,1)S(1)}, u32[]{:S(2)}, u32[]{:S(2)}) collective-permute-start(bf16[512,256]{1,0:T(8,128)(2,1)S(1)} %shard_map.140.refs_2_.refs_0_), channel_id=1, source_target_pairs={{0,1},{1,0},{2,3},{3,2},{4,8},{5,9},{6,10},{7,11},{8,4},{9,5},{10,... | collective-permute-start | bytes 786440 | tf_op jit(solution)/shard_map/ppermute | solution.py:633
  76.3 10.6 %collective-permute-start.25 = (bf16[512,256]{1,0:T(8,128)(2,1)S(1)}, bf16[512,256]{1,0:T(8,128)(2,1)S(1)}, u32[]{:S(2)}, u32[]{:S(2)}) collective-permute-start(bf16[512,256]{1,0:T(8,128)(2,1)S(1)} %shard_map.142.refs_2_), channel_id=1, source_target_pairs={{0,4},{4,0},{8,12},{12,8},{1,5},{5,1},{9,13},{13,9},{2,6},{6,2},{1... | collective-permute-start | bytes 786440 | tf_op jit(solution)/shard_map/ppermute | solution.py:476
  78.0 12.8 %collective-permute-start.21 = (bf16[1024,256]{1,0:T(8,128)(2,1)S(1)}, bf16[1024,256]{1,0:T(8,128)(2,1)S(1)}, u32[]{:S(2)}, u32[]{:S(2)}) collective-permute-start(bf16[1024,256]{1,0:T(8,128)(2,1)S(1)} %get-tuple-element.94), channel_id=1, source_target_pairs={{0,2},{1,3},{2,0},{3,1},{4,6},{5,7},{6,4},{7,5},{8,10},{9,11},{10,... | collective-permute-start | bytes 1572872 | tf_op jit(solution)/shard_map/ppermute | solution.py:476
  81.5 6.3 %collective-permute-start.24 = (bf16[512,256]{1,0:T(8,128)(2,1)S(1)}, bf16[512,256]{1,0:T(8,128)(2,1)S(1)}, u32[]{:S(2)}, u32[]{:S(2)}) collective-permute-start(bf16[512,256]{1,0:T(8,128)(2,1)S(1)} %shard_map.143.refs_5_.refs_0_), channel_id=1, source_target_pairs={{0,1},{1,0},{2,3},{3,2},{4,8},{5,9},{6,10},{7,11},{8,4},{9,5},{10,... | collective-permute-start | bytes 786440 | tf_op jit(solution)/shard_map/ppermute | solution.py:633
  82.5 10.1 %collective-permute-start.27 = (bf16[512,256]{1,0:T(8,128)(2,1)S(1)}, bf16[512,256]{1,0:T(8,128)(2,1)S(1)}, u32[]{:S(2)}, u32[]{:S(2)}) collective-permute-start(bf16[512,256]{1,0:T(8,128)(2,1)S(1)} %shard_map.145.refs_5_.refs_1_), channel_id=1, source_target_pairs={{0,4},{4,0},{8,12},{12,8},{1,5},{5,1},{9,13},{13,9},{2,6},{6,2},{1... | collective-permute-start | bytes 786440 | tf_op jit(solution)/shard_map/ppermute | solution.py:476
  87.9 9.7 %collective-permute-start.28 = (bf16[512,256]{1,0:T(8,128)(2,1)S(1)}, bf16[512,256]{1,0:T(8,128)(2,1)S(1)}, u32[]{:S(2)}, u32[]{:S(2)}) collective-permute-start(bf16[512,256]{1,0:T(8,128)(2,1)S(1)} %shard_map.147.refs_2_), channel_id=1, source_target_pairs={{0,4},{4,0},{8,12},{12,8},{1,5},{5,1},{9,13},{13,9},{2,6},{6,2},{1... | collective-permute-start | bytes 786440 | tf_op jit(solution)/shard_map/ppermute | solution.py:476

commit v13 on v12

--- a/solution.py
+++ b/solution.py
@@ -604,8 +604,8 @@
 
 class Line:
     lag = 3
-    half_weights = (3.0, 3.0, 3.0, 1.0, 1.0, 3.0, 3.0, 0.5)
-    turn_weights = (6.0, 1.0, 1.0, 1.0, 4.0, 2.0, 0.5, 0.5)
+    half_weights = (3.0, 3.0, 3.0, 3.0, 3.0, 3.0, 3.0, 0.5)
+    turn_weights = (4.0, 4.0, 3.0, 3.0, 4.0, 2.0, 0.5, 0.5)
 
     def __init__(self, axis, other, end, step):
         self.axis, self.axes, self.step = axis, (axis, other), step
@@ -709,23 +709,23 @@
     rows = tokens.shape[1] // pieces
     line.enter(step(weight_terms, attended_t, cotangent, inner, 0, 0, pieces))
     line.enter(step(weight_terms, attended_t, cotangent, inner, 0, 1, pieces))
+    parts = step(project_split, rank, [attended], [w_out], "head")
+    mixed = Scatter(parts, "head", step)
     dquery, dkv, query_first, query_second, *away = step(
         backward, query, grad, attended_t, stats, tokens, levels, fars, far_bits, pieces
     )
     backs = [exchange(piece, "seq", d) for d, piece in enumerate(away, 1)]
     line.meet(rows)
+    mixed.advance()
     line.meet(rows)
     dkey, dvalue, dkv_t = step(close_keys, dkv, backs, far_bits, local_levels)
     line.enter(step(relay, query_first))
-    parts = step(project_split, rank, [attended], [w_out], "head")
-    mixed = Scatter(parts, "head", step)
+    key_first = step(weight_terms, dkv_t, tokens, inner, 0, 0, pieces)
     line.turn(query_second)
-    key_first = step(weight_terms, dkv_t, tokens, inner, 0, 0, pieces)
     key_second = step(weight_terms, dkv_t, tokens, inner, 0, 1, pieces)
+    line.meet(rows)
+    line.turn(key_first)
     keep, send = step(project_split, rank, [dquery, dkey, dvalue], [w_query, w_key, w_value], "head")
-    line.meet(rows)
-    mixed.advance()
-    line.turn(key_first)
     line.meet(rows)
     value_first = step(weight_terms, dkv_t, tokens, inner, 1, 0, pieces)
     line.turn(key_second)

time: 98.6 us -> 98.4 us (level)
  starting transfers between devices: 32.9 us -> 35.7 us
  waiting for transfers between devices: 30 us -> 27.7 us
    ppermute x21, waiting for transfers between devices: 29.9 us -> 27.7 us  [exchange(): return lax.ppermute(block, axis, [(i, i ^ distance) for i in range(count)])]
    ppermute x21, starting transfers between devices: 32.4 us -> 34.6 us  [exchange(): return lax.ppermute(block, axis, [(i, i ^ distance) for i in range(count)])]
  transfers between devices with their start and end apart: 29 -> 29, of which waited for: 16 -> 14; matrix products, arithmetic and copies ran while one was open for 0% -> 0% of each run, Pallas kernels for 23% -> 23%
where the time goes in v13:
time: 98.4 us; the launch traced here: 98.3 us
  starting transfers between devices  35.7 us (36%)
  Pallas kernels  33.7 us (34%)
  waiting for transfers between devices  27.7 us (28%)
  between operations  1.12 us (1%)
    ppermute x21, starting transfers between devices, exchange(): return lax.ppermute(block, axis, [(i, i ^ distance) for i in range(count)])  34.6 us
    pallas_call x41, Pallas kernels, run(): return pl.pallas_call(kernel, in_specs=in_specs, **options)(*ready, *after)  33.7 us
    ppermute x21, waiting for transfers between devices, exchange(): return lax.ppermute(block, axis, [(i, i ^ distance) for i in range(count)])  27.7 us
  transfers between devices with their start and end apart: 29, of which 14 were waited for; matrix products, arithmetic and copies ran while one was open for 0% of the time, Pallas kernels for 23%

profile of v13, /device:TPU:0, one launch (start us, length us, event | category | flops | bytes accessed | tf_op | source)
XLA Modules:
  0.0 98.3 jit_solution(6103761012996150910)
XLA Ops:
  0.7 5.3 %shard_map.110 = (bf16[1024,512]{1,0:T(8,128)(2,1)}, bf16[512,512]{1,0:T(8,128)(2,1)}, bf16[256,512]{1,0:T(8,128)(2,1)}, bf16[128,512]{1,0:T(8,128)(2,1)}, bf16[64,512]{1,0:T(8,128)(2,1)}) custom-call(bf16[1024,1024]{1,0:T(8,128)(2,1)} %refs_1_.17, bf16[1024,256]{1,0:T(8,128)(2,1)} %refs_5_.1, bf16[1024,256]{1,0:T(8,128)(2,1)} %refs_6_.1, ...), custom_call_target="tpu_custom_call" | custom-call | flops 5750000128 | bytes 1 | tf_op jit(solution)/shard_map/pallas_call | solution.py:42
  6.0 4.1 %collective-permute-start.1 = (bf16[64,512]{1,0:T(8,128)(2,1)}, bf16[64,512]{1,0:T(8,128)(2,1)S(1)}, u32[]{:S(2)}, u32[]{:S(2)}) collective-permute-start(bf16[64,512]{1,0:T(8,128)(2,1)} %get-tuple-element.61), channel_id=1, source_target_pairs={{0,8},{4,12},{8,0},{12,4},{1,9},{5,13},{9,1},{13,5},{2,10},{6,14},... | collective-permute-start | bytes 196616 | tf_op jit(solution)/shard_map/ppermute | solution.py:476
  10.1 1.3 %collective-permute-start.2 = (bf16[64,512]{1,0:T(8,128)(2,1)}, bf16[64,512]{1,0:T(8,128)(2,1)S(1)}, u32[]{:S(2)}, u32[]{:S(2)}) collective-permute-start(bf16[64,512]{1,0:T(8,128)(2,1)} %get-tuple-element.61), channel_id=1, source_target_pairs={{0,12},{4,8},{8,4},{12,0},{1,13},{5,9},{9,5},{13,1},{2,14},{6,10},... | collective-permute-start | bytes 196616 | tf_op jit(solution)/shard_map/ppermute | solution.py:476
  11.7 0.7 shard_map.109.refs_0_.refs_4_
  12.5 2.3 %shard_map.111 = (f32[4096,256]{1,0:T(8,128)S(1)}, f32[4,1024]{1,0:T(4,128)S(1)}) custom-call(bf16[1024,256]{1,0:T(8,128)(2,1)S(1)} %shard_map.109.refs_0_.refs_4_, bf16[1024,512]{1,0:T(8,128)(2,1)S(1)} %copy-done.6, bf16[512,512]{1,0:T(8,128)(2,1)S(1)} %copy-done.7, bf16[256,512]{1,0:T(8,128)(2,1)S(1)} %copy-done.8, ...), custom_call_target="tpu_custom_call" | custom-call | flops 2644999936 | bytes 1 | tf_op jit(solution)/shard_map/pallas_call | solution.py:42
  14.9 0.7 shard_map.112.refs_9_.refs_1_
  15.6 1.5 %collective-permute-done.2.refs_8_.refs_10_ = bf16[64,512]{1,0:T(8,128)(2,1)S(1)} collective-permute-done((bf16[64,512]{1,0:T(8,128)(2,1)}, bf16[64,512]{1,0:T(8,128)(2,1)S(1)}, u32[]{:S(2)}, u32[]{:S(2)}) %collective-permute-start.2) | collective-permute-done | bytes 65568 | tf_op jit(solution)/shard_map/ppermute | solution.py:476
  17.1 0.8 collective-permute-done.refs_6_.refs_8_
  17.9 3.9 %shard_map.113 = (bf16[1024,256]{1,0:T(8,128)(2,1)S(1)}, bf16[256,1024]{1,0:T(8,128)(2,1)S(1)}, f32[4,1024]{1,0:T(4,128)S(1)}) custom-call(bf16[1024,256]{1,0:T(8,128)(2,1)S(1)} %shard_map.109.refs_0_.refs_4_, f32[4096,256]{1,0:T(8,128)S(1)} %get-tuple-element.58.refs_2_.refs_1_, f32[4,1024]{1,0:T(4,128)S(1)} %get-tuple-element.59.refs_2_, ...), custom_call_target="tpu_custom_call" | custom-call | flops 4600000000 | bytes 1 | tf_op jit(solution)/shard_map/pallas_call | solution.py:42
  22.8 1.0 %collective-permute-start.4 = (bf16[512,256]{1,0:T(8,128)(2,1)S(1)}, bf16[512,256]{1,0:T(8,128)(2,1)S(1)}, u32[]{:S(2)}, u32[]{:S(2)}) collective-permute-start(bf16[512,256]{1,0:T(8,128)(2,1)S(1)} %shard_map.114.refs_2_.refs_0_), channel_id=1, source_target_pairs={{0,4},{4,0},{8,12},{12,8},{1,5},{5,1},{9,13},{13,9},{2,6},{6,2},{1... | collective-permute-start | bytes 786440 | tf_op jit(solution)/shard_map/ppermute | solution.py:476
  23.8 0.7 shard_map.116
  24.5 1.2 %collective-permute-start.10 = (bf16[512,256]{1,0:T(8,128)(2,1)S(1)}, bf16[512,256]{1,0:T(8,128)(2,1)S(1)}, u32[]{:S(2)}, u32[]{:S(2)}) collective-permute-start(bf16[512,256]{1,0:T(8,128)(2,1)S(1)} %shard_map.115.refs_3_.refs_0_), channel_id=1, source_target_pairs={{0,4},{4,0},{8,12},{12,8},{1,5},{5,1},{9,13},{13,9},{2,6},{6,2},{1... | collective-permute-start | bytes 786440 | tf_op jit(solution)/shard_map/ppermute | solution.py:476
  25.7 6.9 %shard_map.117 = (bf16[1024,256]{1,0:T(8,128)(2,1)S(1)}, f32[1024,512]{1,0:T(8,128)S(1)}, bf16[512,256]{1,0:T(8,128)(2,1)S(1)}, bf16[512,256]{1,0:T(8,128)(2,1)S...) custom-call(bf16[1024,256]{1,0:T(8,128)(2,1)S(1)} %shard_map.109.refs_0_.refs_4_, ...), custom_call_target="tpu_custom_call" | custom-call | flops 9200000000 | bytes 1 | tf_op jit(solution)/shard_map/pallas_call | solution.py:42
  32.7 1.0 %collective-permute-start.7 = (bf16[128,512]{1,0:T(8,128)(2,1)S(1)}, bf16[128,512]{1,0:T(8,128)(2,1)S(1)}, u32[]{:S(2)}, u32[]{:S(2)}) collective-permute-start(bf16[128,512]{1,0:T(8,128)(2,1)S(1)} %get-tuple-element.72), channel_id=1, source_target_pairs={{0,4},{4,0},{8,12},{12,8},{1,5},{5,1},{9,13},{13,9},{2,6},{6,2},{1... | collective-permute-start | bytes 393224 | tf_op jit(solution)/shard_map/ppermute | solution.py:476
  33.6 2.8 %collective-permute-start.8 = (bf16[64,512]{1,0:T(8,128)(2,1)S(1)}, bf16[64,512]{1,0:T(8,128)(2,1)S(1)}, u32[]{:S(2)}, u32[]{:S(2)}) collective-permute-start(bf16[64,512]{1,0:T(8,128)(2,1)S(1)} %get-tuple-element.73), channel_id=1, source_target_pairs={{0,8},{4,12},{8,0},{12,4},{1,9},{5,13},{9,1},{13,5},{2,10},{6,14},... | collective-permute-start | bytes 196616 | tf_op jit(solution)/shard_map/ppermute | solution.py:476
  36.5 0.6 collective-permute-start.9
  38.2 1.1 %collective-permute-done.8.refs_2_ = bf16[64,512]{1,0:T(8,128)(2,1)S(1)} collective-permute-done((bf16[64,512]{1,0:T(8,128)(2,1)S(1)}, bf16[64,512]{1,0:T(8,128)(2,1)S(1)}, u32[]{:S(2)}, u32[]{:S(2)}) %collective-permute-start.8) | collective-permute-done | bytes 65568 | tf_op jit(solution)/shard_map/ppermute | solution.py:476
  39.2 4.0 %collective-permute-done.9.refs_3_ = bf16[64,512]{1,0:T(8,128)(2,1)S(1)} collective-permute-done((bf16[64,512]{1,0:T(8,128)(2,1)S(1)}, bf16[64,512]{1,0:T(8,128)(2,1)S(1)}, u32[]{:S(2)}, u32[]{:S(2)}) %collective-permute-start.9) | collective-permute-done | bytes 65568 | tf_op jit(solution)/shard_map/ppermute | solution.py:476
  43.3 1.0 %shard_map.121 = (bf16[1024,256]{1,0:T(8,128)(2,1)S(1)}, bf16[1024,256]{1,0:T(8,128)(2,1)S(1)}, bf16[512,1024]{1,0:T(8,128)(2,1)S(1)}) custom-call(f32[1024,512]{1,0:T(8,128)S(1)} %get-tuple-element.71.refs_0_, bf16[128,512]{1,0:T(8,128)(2,1)S(1)} %collective-permute-done.7.refs_1_, bf16[64,512]{1,0:T(8,128)(2,1)S(1)} %collective-permute-done.8.refs_2_, ...), custom_call_target="tpu_custom_call" | custom-call | flops 230000000 | bytes 1 | tf_op jit(solution)/shard_map/pallas_call | solution.py:42
  44.4 1.1 %collective-permute-start.13 = (bf16[512,256]{1,0:T(8,128)(2,1)S(1)}, bf16[512,256]{1,0:T(8,128)(2,1)S(1)}, u32[]{:S(2)}, u32[]{:S(2)}) collective-permute-start(bf16[512,256]{1,0:T(8,128)(2,1)S(1)} %shard_map.122.refs_2_.refs_0_), channel_id=1, source_target_pairs={{0,4},{4,0},{8,12},{12,8},{1,5},{5,1},{9,13},{13,9},{2,6},{6,2},{1... | collective-permute-start | bytes 786440 | tf_op jit(solution)/shard_map/ppermute | solution.py:476
  46.1 4.0 %collective-permute-start.11 = (bf16[512,256]{1,0:T(8,128)(2,1)S(1)}, bf16[512,256]{1,0:T(8,128)(2,1)S(1)}, u32[]{:S(2)}, u32[]{:S(2)}) collective-permute-start(bf16[512,256]{1,0:T(8,128)(2,1)S(1)} %get-tuple-element.78), channel_id=1, source_target_pairs={{0,4},{4,0},{8,12},{12,8},{1,5},{5,1},{9,13},{13,9},{2,6},{6,2},{1... | collective-permute-start | bytes 786440 | tf_op jit(solution)/shard_map/ppermute | solution.py:476
  50.1 1.5 %collective-permute-start.5 = (bf16[1024,256]{1,0:T(8,128)(2,1)S(1)}, bf16[1024,256]{1,0:T(8,128)(2,1)S(1)}, u32[]{:S(2)}, u32[]{:S(2)}) collective-permute-start(bf16[1024,256]{1,0:T(8,128)(2,1)S(1)} %get-tuple-element.69), channel_id=1, source_target_pairs={{0,2},{1,3},{2,0},{3,1},{4,6},{5,7},{6,4},{7,5},{8,10},{9,11},{10,... | collective-permute-start | bytes 1572872 | tf_op jit(solution)/shard_map/ppermute | solution.py:476
  52.1 1.5 %collective-permute-done.13.refs_1_ = bf16[512,256]{1,0:T(8,128)(2,1)S(1)} collective-permute-done((bf16[512,256]{1,0:T(8,128)(2,1)S(1)}, bf16[512,256]{1,0:T(8,128)(2,1)S(1)}, u32[]{:S(2)}, u32[]{:S(2)}) %collective-permute-start.13) | collective-permute-done | bytes 262176 | tf_op jit(solution)/shard_map/ppermute | solution.py:476
  54.1 1.8 %collective-permute-start.15 = (bf16[512,256]{1,0:T(8,128)(2,1)S(1)}, bf16[512,256]{1,0:T(8,128)(2,1)S(1)}, u32[]{:S(2)}, u32[]{:S(2)}) collective-permute-start(bf16[512,256]{1,0:T(8,128)(2,1)S(1)} %get-tuple-element.84), channel_id=1, source_target_pairs={{0,4},{4,0},{8,12},{12,8},{1,5},{5,1},{9,13},{13,9},{2,6},{6,2},{1... | collective-permute-start | bytes 786440 | tf_op jit(solution)/shard_map/ppermute | solution.py:476
  55.9 1.8 %shard_map.128 = (bf16[1024,512]{1,0:T(8,128)(2,1)S(1)}, bf16[1024,512]{1,0:T(8,128)(2,1)S(1)}) custom-call(s32[1]{0:T(128)} %bitcast.refs_4_.refs_0_, bf16[1024,256]{1,0:T(8,128)(2,1)S(1)} %get-tuple-element.67.refs_2_.refs_1_, bf16[1024,256]{1,0:T(8,128)(2,1)S(1)} %get-tuple-element.77.refs_1_.refs_2_, bf16[1024,256]{1,0:T(8,128)(2,1)S(1)} %get-tuple-element.79.refs_3_, ...), custom_call_target="tpu_custom_call" | custom-call | flops 1150000000 | bytes 1 | tf_op jit(solution)/shard_map/pallas_call | solution.py:42
  57.7 1.2 %collective-permute-done.11.refs_1_.refs_3_ = bf16[512,256]{1,0:T(8,128)(2,1)S(1)} collective-permute-done((bf16[512,256]{1,0:T(8,128)(2,1)S(1)}, bf16[512,256]{1,0:T(8,128)(2,1)S(1)}, u32[]{:S(2)}, u32[]{:S(2)}) %collective-permute-start.11) | collective-permute-done | bytes 262176 | tf_op jit(solution)/shard_map/ppermute | solution.py:476
  59.7 1.9 %collective-permute-start.20 = (bf16[512,256]{1,0:T(8,128)(2,1)S(1)}, bf16[512,256]{1,0:T(8,128)(2,1)S(1)}, u32[]{:S(2)}, u32[]{:S(2)}) collective-permute-start(bf16[512,256]{1,0:T(8,128)(2,1)S(1)} %get-tuple-element.90), channel_id=1, source_target_pairs={{0,4},{4,0},{8,12},{12,8},{1,5},{5,1},{9,13},{13,9},{2,6},{6,2},{1... | collective-permute-start | bytes 786440 | tf_op jit(solution)/shard_map/ppermute | solution.py:476
  61.6 2.9 %collective-permute-done.15.refs_1_.refs_4_ = bf16[512,256]{1,0:T(8,128)(2,1)S(1)} collective-permute-done((bf16[512,256]{1,0:T(8,128)(2,1)S(1)}, bf16[512,256]{1,0:T(8,128)(2,1)S(1)}, u32[]{:S(2)}, u32[]{:S(2)}) %collective-permute-start.15) | collective-permute-done | bytes 262176 | tf_op jit(solution)/shard_map/ppermute | solution.py:476
  64.7 0.6 collective-permute-start.17
  65.4 2.0 %collective-permute-start.18 = (bf16[512,256]{1,0:T(8,128)(2,1)S(1)}, bf16[512,256]{1,0:T(8,128)(2,1)S(1)}, u32[]{:S(2)}, u32[]{:S(2)}) collective-permute-start(bf16[512,256]{1,0:T(8,128)(2,1)S(1)} %get-tuple-element.88), channel_id=1, source_target_pairs={{0,4},{4,0},{8,12},{12,8},{1,5},{5,1},{9,13},{13,9},{2,6},{6,2},{1... | collective-permute-start | bytes 786440 | tf_op jit(solution)/shard_map/ppermute | solution.py:476
  67.4 0.9 shard_map.135
  68.9 1.2 %collective-permute-done.20.refs_1_.refs_3_ = bf16[512,256]{1,0:T(8,128)(2,1)S(1)} collective-permute-done((bf16[512,256]{1,0:T(8,128)(2,1)S(1)}, bf16[512,256]{1,0:T(8,128)(2,1)S(1)}, u32[]{:S(2)}, u32[]{:S(2)}) %collective-permute-start.20) | collective-permute-done | bytes 262176 | tf_op jit(solution)/shard_map/ppermute | solution.py:476
  70.4 2.3 %collective-permute-start.22 = (bf16[512,256]{1,0:T(8,128)(2,1)S(1)}, bf16[512,256]{1,0:T(8,128)(2,1)S(1)}, u32[]{:S(2)}, u32[]{:S(2)}) collective-permute-start(bf16[512,256]{1,0:T(8,128)(2,1)S(1)} %get-tuple-element.95), channel_id=1, source_target_pairs={{0,4},{4,0},{8,12},{12,8},{1,5},{5,1},{9,13},{13,9},{2,6},{6,2},{1... | collective-permute-start | bytes 786440 | tf_op jit(solution)/shard_map/ppermute | solution.py:476
  72.8 0.8 shard_map.139
  73.6 2.2 %collective-permute-done.18.refs_1_.refs_4_ = bf16[512,256]{1,0:T(8,128)(2,1)S(1)} collective-permute-done((bf16[512,256]{1,0:T(8,128)(2,1)S(1)}, bf16[512,256]{1,0:T(8,128)(2,1)S(1)}, u32[]{:S(2)}, u32[]{:S(2)}) %collective-permute-start.18) | collective-permute-done | bytes 262176 | tf_op jit(solution)/shard_map/ppermute | solution.py:476
  76.2 2.0 %collective-permute-start.25 = (bf16[512,256]{1,0:T(8,128)(2,1)S(1)}, bf16[512,256]{1,0:T(8,128)(2,1)S(1)}, u32[]{:S(2)}, u32[]{:S(2)}) collective-permute-start(bf16[512,256]{1,0:T(8,128)(2,1)S(1)} %shard_map.142.refs_2_), channel_id=1, source_target_pairs={{0,4},{4,0},{8,12},{12,8},{1,5},{5,1},{9,13},{13,9},{2,6},{6,2},{1... | collective-permute-start | bytes 786440 | tf_op jit(solution)/shard_map/ppermute | solution.py:476
  78.3 1.5 %collective-permute-start.21 = (bf16[1024,256]{1,0:T(8,128)(2,1)S(1)}, bf16[1024,256]{1,0:T(8,128)(2,1)S(1)}, u32[]{:S(2)}, u32[]{:S(2)}) collective-permute-start(bf16[1024,256]{1,0:T(8,128)(2,1)S(1)} %get-tuple-element.94), channel_id=1, source_target_pairs={{0,2},{1,3},{2,0},{3,1},{4,6},{5,7},{6,4},{7,5},{8,10},{9,11},{10,... | collective-permute-start | bytes 1572872 | tf_op jit(solution)/shard_map/ppermute | solution.py:476
  79.7 1.6 %collective-permute-done.22.refs_1_.refs_3_ = bf16[512,256]{1,0:T(8,128)(2,1)S(1)} collective-permute-done((bf16[512,256]{1,0:T(8,128)(2,1)S(1)}, bf16[512,256]{1,0:T(8,128)(2,1)S(1)}, u32[]{:S(2)}, u32[]{:S(2)}) %collective-permute-start.22) | collective-permute-done | bytes 262176 | tf_op jit(solution)/shard_map/ppermute | solution.py:476
  81.5 0.8 shard_map.144
  82.4 2.0 %collective-permute-start.27 = (bf16[512,256]{1,0:T(8,128)(2,1)S(1)}, bf16[512,256]{1,0:T(8,128)(2,1)S(1)}, u32[]{:S(2)}, u32[]{:S(2)}) collective-permute-start(bf16[512,256]{1,0:T(8,128)(2,1)S(1)} %shard_map.145.refs_5_.refs_1_), channel_id=1, source_target_pairs={{0,4},{4,0},{8,12},{12,8},{1,5},{5,1},{9,13},{13,9},{2,6},{6,2},{1... | collective-permute-start | bytes 786440 | tf_op jit(solution)/shard_map/ppermute | solution.py:476
  84.4 2.3 %collective-permute-done.25.refs_4_ = bf16[512,256]{1,0:T(8,128)(2,1)S(1)} collective-permute-done((bf16[512,256]{1,0:T(8,128)(2,1)S(1)}, bf16[512,256]{1,0:T(8,128)(2,1)S(1)}, u32[]{:S(2)}, u32[]{:S(2)}) %collective-permute-start.25) | collective-permute-done | bytes 262176 | tf_op jit(solution)/shard_map/ppermute | solution.py:476
  86.7 0.8 shard_map.146
  87.6 1.6 %collective-permute-start.28 = (bf16[512,256]{1,0:T(8,128)(2,1)S(1)}, bf16[512,256]{1,0:T(8,128)(2,1)S(1)}, u32[]{:S(2)}, u32[]{:S(2)}) collective-permute-start(bf16[512,256]{1,0:T(8,128)(2,1)S(1)} %shard_map.147.refs_2_), channel_id=1, source_target_pairs={{0,4},{4,0},{8,12},{12,8},{1,5},{5,1},{9,13},{13,9},{2,6},{6,2},{1... | collective-permute-start | bytes 786440 | tf_op jit(solution)/shard_map/ppermute | solution.py:476
  89.2 1.5 %collective-permute-done.21.refs_1_ = bf16[1024,256]{1,0:T(8,128)(2,1)S(1)} collective-permute-done((bf16[1024,256]{1,0:T(8,128)(2,1)S(1)}, bf16[1024,256]{1,0:T(8,128)(2,1)S(1)}, u32[]{:S(2)}, u32[]{:S(2)}) %collective-permute-start.21) | collective-permute-done | bytes 524320 | tf_op jit(solution)/shard_map/ppermute | solution.py:476
  90.7 0.9 shard_map.148
  91.6 0.7 collective-permute-done.27.refs_3_
  92.4 5.1 %collective-permute-done.28.refs_4_ = bf16[512,256]{1,0:T(8,128)(2,1)S(1)} collective-permute-done((bf16[512,256]{1,0:T(8,128)(2,1)S(1)}, bf16[512,256]{1,0:T(8,128)(2,1)S(1)}, u32[]{:S(2)}, u32[]{:S(2)}) %collective-permute-start.28) | collective-permute-done | bytes 262176 | tf_op jit(solution)/shard_map/ppermute | solution.py:476
  97.4 0.8 shard_map.149
  (69 shorter events, 6.4 us)
Async XLA Ops:
  0.6 11.1 %copy-start = (bf16[1024,1024]{1,0:T(8,128)(2,1)S(1)}, bf16[1024,1024]{1,0:T(8,128)(2,1)}, u32[]{:S(2)}) copy-start(bf16[1024,1024]{1,0:T(8,128)(2,1)} %refs_1_.17) | copy-start | bytes 6291460
  0.7 11.1 %copy-start.3 = (bf16[1024,256]{1,0:T(8,128)(2,1)S(1)}, bf16[1024,256]{1,0:T(8,128)(2,1)}, u32[]{:S(2)}) copy-start(bf16[1024,256]{1,0:T(8,128)(2,1)} %refs_4_.3) | copy-start | bytes 1572868
  6.0 6.4 %copy-start.6 = (bf16[1024,512]{1,0:T(8,128)(2,1)S(1)}, bf16[1024,512]{1,0:T(8,128)(2,1)}, u32[]{:S(2)}) copy-start(bf16[1024,512]{1,0:T(8,128)(2,1)} %get-tuple-element.55.refs_1_.refs_3_.refs_5_) | copy-start | bytes 3145732
  6.0 6.4 %copy-start.7 = (bf16[512,512]{1,0:T(8,128)(2,1)S(1)}, bf16[512,512]{1,0:T(8,128)(2,1)}, u32[]{:S(2)}) copy-start(bf16[512,512]{1,0:T(8,128)(2,1)} %get-tuple-element.56.refs_2_.refs_4_.refs_6_) | copy-start | bytes 1572868
  6.0 6.4 %copy-start.8 = (bf16[256,512]{1,0:T(8,128)(2,1)S(1)}, bf16[256,512]{1,0:T(8,128)(2,1)}, u32[]{:S(2)}) copy-start(bf16[256,512]{1,0:T(8,128)(2,1)} %get-tuple-element.57.refs_3_.refs_5_.refs_7_) | copy-start | bytes 786436
  6.0 9.5 %collective-permute-start.1 = (bf16[64,512]{1,0:T(8,128)(2,1)}, bf16[64,512]{1,0:T(8,128)(2,1)S(1)}, u32[]{:S(2)}, u32[]{:S(2)}) collective-permute-start(bf16[64,512]{1,0:T(8,128)(2,1)} %get-tuple-element.61), channel_id=1, source_target_pairs={{0,8},{4,12},{8,0},{12,4},{1,9},{5,13},{9,1},{13,5},{2,10},{6,14},... | collective-permute-start | bytes 196616 | tf_op jit(solution)/shard_map/ppermute | solution.py:476
  10.1 7.0 %collective-permute-start.2 = (bf16[64,512]{1,0:T(8,128)(2,1)}, bf16[64,512]{1,0:T(8,128)(2,1)S(1)}, u32[]{:S(2)}, u32[]{:S(2)}) collective-permute-start(bf16[64,512]{1,0:T(8,128)(2,1)} %get-tuple-element.61), channel_id=1, source_target_pairs={{0,12},{4,8},{8,4},{12,0},{1,13},{5,9},{9,5},{13,1},{2,14},{6,10},... | collective-permute-start | bytes 196616 | tf_op jit(solution)/shard_map/ppermute | solution.py:476
  11.5 6.4 %collective-permute-start = (bf16[128,512]{1,0:T(8,128)(2,1)}, bf16[128,512]{1,0:T(8,128)(2,1)S(1)}, u32[]{:S(2)}, u32[]{:S(2)}) collective-permute-start(bf16[128,512]{1,0:T(8,128)(2,1)} %get-tuple-element.60), channel_id=1, source_target_pairs={{0,4},{4,0},{8,12},{12,8},{1,5},{5,1},{9,13},{13,9},{2,6},{6,2},{1... | collective-permute-start | bytes 393224 | tf_op jit(solution)/shard_map/ppermute | solution.py:476
  12.5 2.4 %copy-start.1 = (bf16[1024,1024]{1,0:T(8,128)(2,1)S(1)}, bf16[1024,1024]{1,0:T(8,128)(2,1)}, u32[]{:S(2)}) copy-start(bf16[1024,1024]{1,0:T(8,128)(2,1)} %refs_1_.13) | copy-start | bytes 6291460
  12.5 2.4 %copy-start.2 = (bf16[1024,256]{1,0:T(8,128)(2,1)S(1)}, bf16[1024,256]{1,0:T(8,128)(2,1)}, u32[]{:S(2)}) copy-start(bf16[1024,256]{1,0:T(8,128)(2,1)} %refs_2_.3) | copy-start | bytes 1572868
  22.8 13.7 %collective-permute-start.4 = (bf16[512,256]{1,0:T(8,128)(2,1)S(1)}, bf16[512,256]{1,0:T(8,128)(2,1)S(1)}, u32[]{:S(2)}, u32[]{:S(2)}) collective-permute-start(bf16[512,256]{1,0:T(8,128)(2,1)S(1)} %shard_map.114.refs_2_.refs_0_), channel_id=1, source_target_pairs={{0,4},{4,0},{8,12},{12,8},{1,5},{5,1},{9,13},{13,9},{2,6},{6,2},{1... | collective-permute-start | bytes 786440 | tf_op jit(solution)/shard_map/ppermute | solution.py:476
  24.5 13.0 %collective-permute-start.10 = (bf16[512,256]{1,0:T(8,128)(2,1)S(1)}, bf16[512,256]{1,0:T(8,128)(2,1)S(1)}, u32[]{:S(2)}, u32[]{:S(2)}) collective-permute-start(bf16[512,256]{1,0:T(8,128)(2,1)S(1)} %shard_map.115.refs_3_.refs_0_), channel_id=1, source_target_pairs={{0,4},{4,0},{8,12},{12,8},{1,5},{5,1},{9,13},{13,9},{2,6},{6,2},{1... | collective-permute-start | bytes 786440 | tf_op jit(solution)/shard_map/ppermute | solution.py:476
  25.7 11.5 %collective-permute-start.3 = (bf16[1024,512]{1,0:T(8,128)(2,1)S(1)}, bf16[1024,512]{1,0:T(8,128)(2,1)S(1)}, u32[]{:S(2)}, u32[]{:S(2)}) collective-permute-start(bf16[1024,512]{1,0:T(8,128)(2,1)S(1)} %get-tuple-element.65), channel_id=1, source_target_pairs={{0,1},{1,0},{2,3},{3,2},{4,5},{5,4},{6,7},{7,6},{8,9},{9,8},{10,11... | collective-permute-start | bytes 3145736 | tf_op jit(solution)/shard_map/ppermute | solution.py:476
  32.7 10.6 %collective-permute-start.7 = (bf16[128,512]{1,0:T(8,128)(2,1)S(1)}, bf16[128,512]{1,0:T(8,128)(2,1)S(1)}, u32[]{:S(2)}, u32[]{:S(2)}) collective-permute-start(bf16[128,512]{1,0:T(8,128)(2,1)S(1)} %get-tuple-element.72), channel_id=1, source_target_pairs={{0,4},{4,0},{8,12},{12,8},{1,5},{5,1},{9,13},{13,9},{2,6},{6,2},{1... | collective-permute-start | bytes 393224 | tf_op jit(solution)/shard_map/ppermute | solution.py:476
  33.6 5.6 %collective-permute-start.8 = (bf16[64,512]{1,0:T(8,128)(2,1)S(1)}, bf16[64,512]{1,0:T(8,128)(2,1)S(1)}, u32[]{:S(2)}, u32[]{:S(2)}) collective-permute-start(bf16[64,512]{1,0:T(8,128)(2,1)S(1)} %get-tuple-element.73), channel_id=1, source_target_pairs={{0,8},{4,12},{8,0},{12,4},{1,9},{5,13},{9,1},{13,5},{2,10},{6,14},... | collective-permute-start | bytes 196616 | tf_op jit(solution)/shard_map/ppermute | solution.py:476
  36.5 6.8 %collective-permute-start.9 = (bf16[64,512]{1,0:T(8,128)(2,1)S(1)}, bf16[64,512]{1,0:T(8,128)(2,1)S(1)}, u32[]{:S(2)}, u32[]{:S(2)}) collective-permute-start(bf16[64,512]{1,0:T(8,128)(2,1)S(1)} %get-tuple-element.74), channel_id=1, source_target_pairs={{0,12},{4,8},{8,4},{12,0},{1,13},{5,9},{9,5},{13,1},{2,14},{6,10},... | collective-permute-start | bytes 196616 | tf_op jit(solution)/shard_map/ppermute | solution.py:476
  37.2 8.8 %collective-permute-start.6 = (bf16[512,256]{1,0:T(8,128)(2,1)S(1)}, bf16[512,256]{1,0:T(8,128)(2,1)S(1)}, u32[]{:S(2)}, u32[]{:S(2)}) collective-permute-start(bf16[512,256]{1,0:T(8,128)(2,1)S(1)} %shard_map.118.refs_2_.refs_1_), channel_id=1, source_target_pairs={{0,1},{1,0},{2,3},{3,2},{4,8},{5,9},{6,10},{7,11},{8,4},{9,5},{10,... | collective-permute-start | bytes 786440 | tf_op jit(solution)/shard_map/ppermute | solution.py:633
  37.6 16.2 %collective-permute-start.12 = (bf16[512,256]{1,0:T(8,128)(2,1)S(1)}, bf16[512,256]{1,0:T(8,128)(2,1)S(1)}, u32[]{:S(2)}, u32[]{:S(2)}) collective-permute-start(bf16[512,256]{1,0:T(8,128)(2,1)S(1)} %shard_map.120.refs_4_.refs_1_), channel_id=1, source_target_pairs={{0,1},{1,0},{2,3},{3,2},{4,8},{5,9},{6,10},{7,11},{8,4},{9,5},{10,... | collective-permute-start | bytes 786440 | tf_op jit(solution)/shard_map/ppermute | solution.py:633
  44.4 9.3 %collective-permute-start.13 = (bf16[512,256]{1,0:T(8,128)(2,1)S(1)}, bf16[512,256]{1,0:T(8,128)(2,1)S(1)}, u32[]{:S(2)}, u32[]{:S(2)}) collective-permute-start(bf16[512,256]{1,0:T(8,128)(2,1)S(1)} %shard_map.122.refs_2_.refs_0_), channel_id=1, source_target_pairs={{0,4},{4,0},{8,12},{12,8},{1,5},{5,1},{9,13},{13,9},{2,6},{6,2},{1... | collective-permute-start | bytes 786440 | tf_op jit(solution)/shard_map/ppermute | solution.py:476
  46.1 12.8 %collective-permute-start.11 = (bf16[512,256]{1,0:T(8,128)(2,1)S(1)}, bf16[512,256]{1,0:T(8,128)(2,1)S(1)}, u32[]{:S(2)}, u32[]{:S(2)}) collective-permute-start(bf16[512,256]{1,0:T(8,128)(2,1)S(1)} %get-tuple-element.78), channel_id=1, source_target_pairs={{0,4},{4,0},{8,12},{12,8},{1,5},{5,1},{9,13},{13,9},{2,6},{6,2},{1... | collective-permute-start | bytes 786440 | tf_op jit(solution)/shard_map/ppermute | solution.py:476
  50.1 17.3 %collective-permute-start.5 = (bf16[1024,256]{1,0:T(8,128)(2,1)S(1)}, bf16[1024,256]{1,0:T(8,128)(2,1)S(1)}, u32[]{:S(2)}, u32[]{:S(2)}) collective-permute-start(bf16[1024,256]{1,0:T(8,128)(2,1)S(1)} %get-tuple-element.69), channel_id=1, source_target_pairs={{0,2},{1,3},{2,0},{3,1},{4,6},{5,7},{6,4},{7,5},{8,10},{9,11},{10,... | collective-permute-start | bytes 1572872 | tf_op jit(solution)/shard_map/ppermute | solution.py:476
  53.7 2.2 %copy-start.4 = (bf16[1024,256]{1,0:T(8,128)(2,1)S(1)}, bf16[1024,256]{1,0:T(8,128)(2,1)}, u32[]{:S(2)}) copy-start(bf16[1024,256]{1,0:T(8,128)(2,1)} %refs_5_.1) | copy-start | bytes 1572868
  53.7 2.2 %copy-start.5 = (bf16[1024,256]{1,0:T(8,128)(2,1)S(1)}, bf16[1024,256]{1,0:T(8,128)(2,1)}, u32[]{:S(2)}) copy-start(bf16[1024,256]{1,0:T(8,128)(2,1)} %refs_6_.1) | copy-start | bytes 1572868
  53.7 5.9 %collective-permute-start.16 = (bf16[512,256]{1,0:T(8,128)(2,1)S(1)}, bf16[512,256]{1,0:T(8,128)(2,1)S(1)}, u32[]{:S(2)}, u32[]{:S(2)}) collective-permute-start(bf16[512,256]{1,0:T(8,128)(2,1)S(1)} %shard_map.126.refs_4_.refs_1_), channel_id=1, source_target_pairs={{0,1},{1,0},{2,3},{3,2},{4,8},{5,9},{6,10},{7,11},{8,4},{9,5},{10,... | collective-permute-start | bytes 786440 | tf_op jit(solution)/shard_map/ppermute | solution.py:633
  54.1 10.4 %collective-permute-start.15 = (bf16[512,256]{1,0:T(8,128)(2,1)S(1)}, bf16[512,256]{1,0:T(8,128)(2,1)S(1)}, u32[]{:S(2)}, u32[]{:S(2)}) collective-permute-start(bf16[512,256]{1,0:T(8,128)(2,1)S(1)} %get-tuple-element.84), channel_id=1, source_target_pairs={{0,4},{4,0},{8,12},{12,8},{1,5},{5,1},{9,13},{13,9},{2,6},{6,2},{1... | collective-permute-start | bytes 786440 | tf_op jit(solution)/shard_map/ppermute | solution.py:476
  59.0 6.3 %collective-permute-start.14 = (bf16[512,256]{1,0:T(8,128)(2,1)S(1)}, bf16[512,256]{1,0:T(8,128)(2,1)S(1)}, u32[]{:S(2)}, u32[]{:S(2)}) collective-permute-start(bf16[512,256]{1,0:T(8,128)(2,1)S(1)} %shard_map.129.refs_2_.refs_1_), channel_id=1, source_target_pairs={{0,1},{1,0},{2,3},{3,2},{4,8},{5,9},{6,10},{7,11},{8,4},{9,5},{10,... | collective-permute-start | bytes 786440 | tf_op jit(solution)/shard_map/ppermute | solution.py:633
  59.7 10.5 %collective-permute-start.20 = (bf16[512,256]{1,0:T(8,128)(2,1)S(1)}, bf16[512,256]{1,0:T(8,128)(2,1)S(1)}, u32[]{:S(2)}, u32[]{:S(2)}) collective-permute-start(bf16[512,256]{1,0:T(8,128)(2,1)S(1)} %get-tuple-element.90), channel_id=1, source_target_pairs={{0,4},{4,0},{8,12},{12,8},{1,5},{5,1},{9,13},{13,9},{2,6},{6,2},{1... | collective-permute-start | bytes 786440 | tf_op jit(solution)/shard_map/ppermute | solution.py:476
  64.6 5.7 %collective-permute-start.19 = (bf16[512,256]{1,0:T(8,128)(2,1)S(1)}, bf16[512,256]{1,0:T(8,128)(2,1)S(1)}, u32[]{:S(2)}, u32[]{:S(2)}) collective-permute-start(bf16[512,256]{1,0:T(8,128)(2,1)S(1)} %shard_map.132.refs_1_), channel_id=1, source_target_pairs={{0,1},{1,0},{2,3},{3,2},{4,8},{5,9},{6,10},{7,11},{8,4},{9,5},{10,... | collective-permute-start | bytes 786440 | tf_op jit(solution)/shard_map/ppermute | solution.py:633
  64.7 11.2 %collective-permute-start.17 = (bf16[1024,512]{1,0:T(8,128)(2,1)S(1)}, bf16[1024,512]{1,0:T(8,128)(2,1)S(1)}, u32[]{:S(2)}, u32[]{:S(2)}) collective-permute-start(bf16[1024,512]{1,0:T(8,128)(2,1)S(1)} %shard_map.133.refs_4_), channel_id=1, source_target_pairs={{0,1},{1,0},{2,3},{3,2},{4,5},{5,4},{6,7},{7,6},{8,9},{9,8},{10,11... | collective-permute-start | bytes 3145736 | tf_op jit(solution)/shard_map/ppermute | solution.py:476
  65.4 10.4 %collective-permute-start.18 = (bf16[512,256]{1,0:T(8,128)(2,1)S(1)}, bf16[512,256]{1,0:T(8,128)(2,1)S(1)}, u32[]{:S(2)}, u32[]{:S(2)}) collective-permute-start(bf16[512,256]{1,0:T(8,128)(2,1)S(1)} %get-tuple-element.88), channel_id=1, source_target_pairs={{0,4},{4,0},{8,12},{12,8},{1,5},{5,1},{9,13},{13,9},{2,6},{6,2},{1... | collective-permute-start | bytes 786440 | tf_op jit(solution)/shard_map/ppermute | solution.py:476
  70.2 6.0 %collective-permute-start.23 = (bf16[512,256]{1,0:T(8,128)(2,1)S(1)}, bf16[512,256]{1,0:T(8,128)(2,1)S(1)}, u32[]{:S(2)}, u32[]{:S(2)}) collective-permute-start(bf16[512,256]{1,0:T(8,128)(2,1)S(1)} %shard_map.137.refs_4_.refs_0_), channel_id=1, source_target_pairs={{0,1},{1,0},{2,3},{3,2},{4,8},{5,9},{6,10},{7,11},{8,4},{9,5},{10,... | collective-permute-start | bytes 786440 | tf_op jit(solution)/shard_map/ppermute | solution.py:633
  70.4 11.0 %collective-permute-start.22 = (bf16[512,256]{1,0:T(8,128)(2,1)S(1)}, bf16[512,256]{1,0:T(8,128)(2,1)S(1)}, u32[]{:S(2)}, u32[]{:S(2)}) collective-permute-start(bf16[512,256]{1,0:T(8,128)(2,1)S(1)} %get-tuple-element.95), channel_id=1, source_target_pairs={{0,4},{4,0},{8,12},{12,8},{1,5},{5,1},{9,13},{13,9},{2,6},{6,2},{1... | collective-permute-start | bytes 786440 | tf_op jit(solution)/shard_map/ppermute | solution.py:476
  75.8 6.5 %collective-permute-start.26 = (bf16[512,256]{1,0:T(8,128)(2,1)S(1)}, bf16[512,256]{1,0:T(8,128)(2,1)S(1)}, u32[]{:S(2)}, u32[]{:S(2)}) collective-permute-start(bf16[512,256]{1,0:T(8,128)(2,1)S(1)} %shard_map.140.refs_2_.refs_0_), channel_id=1, source_target_pairs={{0,1},{1,0},{2,3},{3,2},{4,8},{5,9},{6,10},{7,11},{8,4},{9,5},{10,... | collective-permute-start | bytes 786440 | tf_op jit(solution)/shard_map/ppermute | solution.py:633
  76.2 10.5 %collective-permute-start.25 = (bf16[512,256]{1,0:T(8,128)(2,1)S(1)}, bf16[512,256]{1,0:T(8,128)(2,1)S(1)}, u32[]{:S(2)}, u32[]{:S(2)}) collective-permute-start(bf16[512,256]{1,0:T(8,128)(2,1)S(1)} %shard_map.142.refs_2_), channel_id=1, source_target_pairs={{0,4},{4,0},{8,12},{12,8},{1,5},{5,1},{9,13},{13,9},{2,6},{6,2},{1... | collective-permute-start | bytes 786440 | tf_op jit(solution)/shard_map/ppermute | solution.py:476
  78.3 12.4 %collective-permute-start.21 = (bf16[1024,256]{1,0:T(8,128)(2,1)S(1)}, bf16[1024,256]{1,0:T(8,128)(2,1)S(1)}, u32[]{:S(2)}, u32[]{:S(2)}) collective-permute-start(bf16[1024,256]{1,0:T(8,128)(2,1)S(1)} %get-tuple-element.94), channel_id=1, source_target_pairs={{0,2},{1,3},{2,0},{3,1},{4,6},{5,7},{6,4},{7,5},{8,10},{9,11},{10,... | collective-permute-start | bytes 1572872 | tf_op jit(solution)/shard_map/ppermute | solution.py:476
  81.4 6.1 %collective-permute-start.24 = (bf16[512,256]{1,0:T(8,128)(2,1)S(1)}, bf16[512,256]{1,0:T(8,128)(2,1)S(1)}, u32[]{:S(2)}, u32[]{:S(2)}) collective-permute-start(bf16[512,256]{1,0:T(8,128)(2,1)S(1)} %shard_map.143.refs_5_.refs_0_), channel_id=1, source_target_pairs={{0,1},{1,0},{2,3},{3,2},{4,8},{5,9},{6,10},{7,11},{8,4},{9,5},{10,... | collective-permute-start | bytes 786440 | tf_op jit(solution)/shard_map/ppermute | solution.py:633
  82.4 9.9 %collective-permute-start.27 = (bf16[512,256]{1,0:T(8,128)(2,1)S(1)}, bf16[512,256]{1,0:T(8,128)(2,1)S(1)}, u32[]{:S(2)}, u32[]{:S(2)}) collective-permute-start(bf16[512,256]{1,0:T(8,128)(2,1)S(1)} %shard_map.145.refs_5_.refs_1_), channel_id=1, source_target_pairs={{0,4},{4,0},{8,12},{12,8},{1,5},{5,1},{9,13},{13,9},{2,6},{6,2},{1... | collective-permute-start | bytes 786440 | tf_op jit(solution)/shard_map/ppermute | solution.py:476
  87.6 9.8 %collective-permute-start.28 = (bf16[512,256]{1,0:T(8,128)(2,1)S(1)}, bf16[512,256]{1,0:T(8,128)(2,1)S(1)}, u32[]{:S(2)}, u32[]{:S(2)}) collective-permute-start(bf16[512,256]{1,0:T(8,128)(2,1)S(1)} %shard_map.147.refs_2_), channel_id=1, source_target_pairs={{0,4},{4,0},{8,12},{12,8},{1,5},{5,1},{9,13},{13,9},{2,6},{6,2},{1... | collective-permute-start | bytes 786440 | tf_op jit(solution)/shard_map/ppermute | solution.py:476

commit v14 on v11

--- a/solution.py
+++ b/solution.py
@@ -317,8 +317,8 @@
         refs = refs[1 + 3 * h :]
         dq_ref, dkv_ref = refs[:2]
         term_refs = refs[2 : 2 + pieces]
-        dfar_refs = refs[2 + pieces : 1 + pieces + fars]
-        scratch = refs[1 + pieces + fars :]
+        dfar_refs = refs[2 + pieces : 2 + pieces + fars]
+        scratch = refs[2 + pieces + fars :]
         dq_t_ref = scratch[-1]
         place = slice(h * HEAD_DIM, (h + 1) * HEAD_DIM)
     else:
@@ -391,16 +391,14 @@
         aways.append(away_e[...])
     aways.append(away)
     away = jnp.concatenate([x[:, half] for half in parts for x in aways], axis=1)
-    width = term_refs[-1].shape[0]
-    term_refs[0][width : width + BLOCK, :] = away[:BLOCK, :inner]
-    term_refs[0][width + BLOCK :, :] = away[:BLOCK, inner:]
-    low = BLOCK
+    width = term_refs[0].shape[0]
+    low = 0
     for ref in dfar_refs:
         ref[...] = away[low : low + ref.shape[0]]
         low += ref.shape[0]
     for i, ref in enumerate(term_refs):
         part = dot(dq_t_ref[...], tok_ref[:, i * width : (i + 1) * width])
-        ref[:width, :] = part.astype(BF16).T
+        ref[...] = part.astype(BF16).T
 
 
 def backward_scratch(levels, fars):
@@ -441,9 +439,8 @@
         ready,
         after,
         out_shape=[shape(tok_rows, inner), shape(tok_rows, 2 * HEAD_DIM, F32)]
-        + [shape(tokens.shape[1] // pieces + 2 * BLOCK, inner)]
-        + [shape(tokens.shape[1] // pieces, inner)] * (pieces - 1)
-        + [shape(*f.shape) for f in fars[1:]],
+        + [shape(tokens.shape[1] // pieces, inner)] * pieces
+        + [shape(*f.shape) for f in fars],
         scratch_shapes=backward_scratch(levels, fars) + [pltpu.VMEM((inner, tok_rows), BF16)],
         compiler_params=params(10),
         cost_estimate=cost(4.0),
@@ -471,13 +468,10 @@
 
 def close_body(local_levels, far_bits, heads, *refs):
     dkv_refs = refs[:heads]
-    joined_ref, *back_refs = refs[heads : heads + len(far_bits)]
+    backs = [ref[...] for ref in refs[heads : heads + len(far_bits)]]
     dk_ref, dv_ref, dkv_t_ref = refs[heads + len(far_bits) :]
     inner = dk_ref.shape[1]
     tile = 2 * BLOCK
-    low = joined_ref.shape[0] - 2 * BLOCK
-    joined = [joined_ref[low : low + BLOCK, :], joined_ref[low + BLOCK :, :]]
-    backs = [jnp.concatenate(joined, axis=1)] + [ref[...] for ref in back_refs]
     halves = (slice(0, HEAD_DIM), slice(HEAD_DIM, 2 * HEAD_DIM))
     for t in range(dk_ref.shape[0] // tile):
         here = slice(t * tile, (t + 1) * tile)
@@ -671,8 +665,8 @@
 
 class Line:
     lag = 3
-    half_weights = (3.0, 3.0, 2.5, 2.0, 2.5, 3.0, 3.0, 2.0)
-    turn_weights = (3.0, 2.0, 2.0, 3.0, 3.0, 2.0, 2.0, 2.0)
+    half_weights = (3.0, 5.0, 3.0, 3.0, 3.0, 3.0, 3.0, 0.5)
+    turn_weights = (4.0, 4.0, 3.0, 3.0, 4.0, 2.0, 0.5, 0.5)
 
     def __init__(self, axis, other, end, step):
         self.axis, self.axes, self.step = axis, (axis, other), step
@@ -775,33 +769,32 @@
     pieces = 2
     rows = tokens.shape[1] // pieces
     line.enter(step(weight_terms, attended_t, cotangent, inner, 0, 0, pieces))
-    parts = step(project_split, rank, [attended], [w_out], "head")
-    mixed = Scatter(parts, "head", step)
     earlier = [
         step(backward_first, h, query, grad, attended_t, stats, levels, fars, far_bits)
         for h in range(inner // HEAD_DIM - 1)
     ]
     line.enter(step(weight_terms, attended_t, cotangent, inner, 0, 1, pieces))
     line.meet(rows)
-    mixed.advance()
+    parts = step(project_split, rank, [attended], [w_out], "head")
+    mixed = Scatter(parts, "head", step)
     dquery, dkv, query_first, query_second, *away = step(
         backward_last, earlier, query, grad, attended_t, stats, tokens, levels, fars, far_bits, pieces
     )
-    line.enter(query_first)
-    backs = [exchange(piece, "seq", d) for d, piece in enumerate(away, 2)]
+    dkvs = [made[1] for made in earlier] + [dkv]
+    backs = [exchange(piece, "seq", d) for d, piece in enumerate(away, 1)]
     line.meet(rows)
+    mixed.advance()
+    line.enter(step(relay, query_first))
     line.turn(query_second)
-    dkey, dvalue, dkv_t = step(
-        close_keys, [made[1] for made in earlier] + [dkv], [line.into[2], *backs], far_bits, local_levels
-    )
+    dkey, dvalue, dkv_t = step(close_keys, dkvs, backs, far_bits, local_levels)
     key_first = step(weight_terms, dkv_t, tokens, inner, 0, 0, pieces)
+    key_second = step(weight_terms, dkv_t, tokens, inner, 0, 1, pieces)
     line.meet(rows)
     line.turn(key_first)
+    keep, send = step(project_split, rank, [dquery, dkey, dvalue], [w_query, w_key, w_value], "head")
     line.meet(rows)
-    key_second = step(weight_terms, dkv_t, tokens, inner, 0, 1, pieces)
+    value_first = step(weight_terms, dkv_t, tokens, inner, 1, 0, pieces)
     line.turn(key_second)
-    value_first = step(weight_terms, dkv_t, tokens, inner, 1, 0, pieces)
-    keep, send = step(project_split, rank, [dquery, dkey, dvalue], [w_query, w_key, w_value], "head")
     line.meet(rows)
     tokens_grad = Scatter([keep, step(relay, send)], "head", step)
     line.turn(value_first)

time: 102 us -> 99 us (0.971)
  starting transfers between devices: 37.7 us -> 32.9 us
  waiting for transfers between devices: 29.3 us -> 30.7 us
    ppermute x20 -> x21, starting transfers between devices: 37.1 us -> 32.2 us  [exchange(): return lax.ppermute(block, axis, [(i, i ^ distance) for i in range(count)])]
    ppermute x20 -> x21, waiting for transfers between devices: 29.2 us -> 30.6 us  [exchange(): return lax.ppermute(block, axis, [(i, i ^ distance) for i in range(count)])]
    pallas_call x41 -> x42, Pallas kernels: 34.1 us -> 34.1 us  [run(): return pl.pallas_call(kernel, in_specs=in_specs, **options)(*ready, *after)]
  transfers between devices with their start and end apart: 28 -> 29, of which waited for: 12 -> 14; matrix products, arithmetic and copies ran while one was open for 0% -> 0% of each run, Pallas kernels for 22% -> 23%
where the time goes in v14:
time: 99 us; the launch traced here: 98.8 us
  Pallas kernels  34.1 us (34%)
  starting transfers between devices  32.9 us (33%)
  waiting for transfers between devices  30.7 us (31%)
  between operations  1.13 us (1%)
    pallas_call x42, Pallas kernels, run(): return pl.pallas_call(kernel, in_specs=in_specs, **options)(*ready, *after)  34.1 us
    ppermute x21, starting transfers between devices, exchange(): return lax.ppermute(block, axis, [(i, i ^ distance) for i in range(count)])  32.2 us
    ppermute x21, waiting for transfers between devices, exchange(): return lax.ppermute(block, axis, [(i, i ^ distance) for i in range(count)])  30.6 us
  transfers between devices with their start and end apart: 29, of which 14 were waited for; matrix products, arithmetic and copies ran while one was open for 0% of the time, Pallas kernels for 23%

profile of v14, /device:TPU:0, one launch (start us, length us, event | category | flops | bytes accessed | tf_op | source)
XLA Modules:
  0.0 98.8 jit_solution(17476773510288568417)
XLA Ops:
  0.7 5.3 %shard_map.110 = (bf16[1024,512]{1,0:T(8,128)(2,1)}, bf16[512,512]{1,0:T(8,128)(2,1)}, bf16[256,512]{1,0:T(8,128)(2,1)}, bf16[128,512]{1,0:T(8,128)(2,1)}, bf16[64,512]{1,0:T(8,128)(2,1)}) custom-call(bf16[1024,1024]{1,0:T(8,128)(2,1)} %refs_1_.17, bf16[1024,256]{1,0:T(8,128)(2,1)} %refs_5_.1, bf16[1024,256]{1,0:T(8,128)(2,1)} %refs_6_.1, ...), custom_call_target="tpu_custom_call" | custom-call | flops 5750000128 | bytes 1 | tf_op jit(solution)/shard_map/pallas_call | solution.py:42
  6.0 4.1 %collective-permute-start.1 = (bf16[64,512]{1,0:T(8,128)(2,1)}, bf16[64,512]{1,0:T(8,128)(2,1)S(1)}, u32[]{:S(2)}, u32[]{:S(2)}) collective-permute-start(bf16[64,512]{1,0:T(8,128)(2,1)} %get-tuple-element.65), channel_id=1, source_target_pairs={{0,8},{4,12},{8,0},{12,4},{1,9},{5,13},{9,1},{13,5},{2,10},{6,14},... | collective-permute-start | bytes 196616 | tf_op jit(solution)/shard_map/ppermute | solution.py:537
  10.1 1.3 %collective-permute-start.2 = (bf16[64,512]{1,0:T(8,128)(2,1)}, bf16[64,512]{1,0:T(8,128)(2,1)S(1)}, u32[]{:S(2)}, u32[]{:S(2)}) collective-permute-start(bf16[64,512]{1,0:T(8,128)(2,1)} %get-tuple-element.65), channel_id=1, source_target_pairs={{0,12},{4,8},{8,4},{12,0},{1,13},{5,9},{9,5},{13,1},{2,14},{6,10},... | collective-permute-start | bytes 196616 | tf_op jit(solution)/shard_map/ppermute | solution.py:537
  11.7 0.7 shard_map.109.refs_0_.refs_4_
  12.5 2.3 %shard_map.111 = (f32[4096,256]{1,0:T(8,128)S(1)}, f32[4,1024]{1,0:T(4,128)S(1)}) custom-call(bf16[1024,256]{1,0:T(8,128)(2,1)S(1)} %shard_map.109.refs_0_.refs_4_, bf16[1024,512]{1,0:T(8,128)(2,1)S(1)} %copy-done.6, bf16[512,512]{1,0:T(8,128)(2,1)S(1)} %copy-done.7, bf16[256,512]{1,0:T(8,128)(2,1)S(1)} %copy-done.8, ...), custom_call_target="tpu_custom_call" | custom-call | flops 2644999936 | bytes 1 | tf_op jit(solution)/shard_map/pallas_call | solution.py:42
  14.8 0.7 shard_map.112.refs_9_.refs_1_
  15.6 1.5 %collective-permute-done.2.refs_8_.refs_9_ = bf16[64,512]{1,0:T(8,128)(2,1)S(1)} collective-permute-done((bf16[64,512]{1,0:T(8,128)(2,1)}, bf16[64,512]{1,0:T(8,128)(2,1)S(1)}, u32[]{:S(2)}, u32[]{:S(2)}) %collective-permute-start.2) | collective-permute-done | bytes 65568 | tf_op jit(solution)/shard_map/ppermute | solution.py:537
  17.1 0.8 collective-permute-done.refs_6_.refs_7_
  17.9 3.9 %shard_map.113 = (bf16[1024,256]{1,0:T(8,128)(2,1)S(1)}, bf16[256,1024]{1,0:T(8,128)(2,1)S(1)}, f32[4,1024]{1,0:T(4,128)S(1)}) custom-call(bf16[1024,256]{1,0:T(8,128)(2,1)S(1)} %shard_map.109.refs_0_.refs_4_, f32[4096,256]{1,0:T(8,128)S(1)} %get-tuple-element.62.refs_2_.refs_1_, f32[4,1024]{1,0:T(4,128)S(1)} %get-tuple-element.63.refs_2_, ...), custom_call_target="tpu_custom_call" | custom-call | flops 4600000000 | bytes 1 | tf_op jit(solution)/shard_map/pallas_call | solution.py:42
  22.3 1.0 collective-permute-start.3
  23.3 3.4 %shard_map.115 = (bf16[1024,128]{1,0:T(8,128)(2,1)S(1)}, f32[1024,256]{1,0:T(8,128)S(1)}, bf16[128,1024]{1,0:T(8,128)(2,1)S(1)}, bf16[256,256]{1,0:T(8,128)(2,1)S(1)}) custom-call(bf16[1024,256]{1,0:T(8,128)(2,1)S(1)} %shard_map.109.refs_0_.refs_4_, bf16[1024,256]{1,0:T(8,128)(2,1)S(1)} %shard_map.112.refs_9_.refs_1_, ...), custom_call_target="tpu_custom_call" | custom-call | flops 4600000000 | bytes 1 | tf_op jit(solution)/shard_map/pallas_call | solution.py:42
  27.2 2.2 %collective-permute-done.3.refs_1_ = bf16[512,256]{1,0:T(8,128)(2,1)S(1)} collective-permute-done((bf16[512,256]{1,0:T(8,128)(2,1)S(1)}, bf16[512,256]{1,0:T(8,128)(2,1)S(1)}, u32[]{:S(2)}, u32[]{:S(2)}) %collective-permute-start.3) | collective-permute-done | bytes 262176 | tf_op jit(solution)/shard_map/ppermute | solution.py:537
  29.4 0.7 shard_map.118
  30.2 1.6 %collective-permute-start.5 = (bf16[512,256]{1,0:T(8,128)(2,1)S(1)}, bf16[512,256]{1,0:T(8,128)(2,1)S(1)}, u32[]{:S(2)}, u32[]{:S(2)}) collective-permute-start(bf16[512,256]{1,0:T(8,128)(2,1)S(1)} %shard_map.116.refs_2_.refs_0_), channel_id=1, source_target_pairs={{0,4},{4,0},{8,12},{12,8},{1,5},{5,1},{9,13},{13,9},{2,6},{6,2},{1... | collective-permute-start | bytes 786440 | tf_op jit(solution)/shard_map/ppermute | solution.py:537
  32.0 4.0 %shard_map.119 = (bf16[1024,256]{1,0:T(8,128)(2,1)S(1)}, f32[1024,256]{1,0:T(8,128)S(1)}, bf16[512,256]{1,0:T(8,128)(2,1)S(1)}, bf16[512,256]{1,0:T(8,128)(2,1)S...) custom-call(bf16[1024,256]{1,0:T(8,128)(2,1)S(1)} %shard_map.109.refs_0_.refs_4_, ...), custom_call_target="tpu_custom_call" | custom-call | flops 4600000000 | bytes 1 | tf_op jit(solution)/shard_map/pallas_call | solution.py:42
  36.0 3.4 %collective-permute-start.9 = (bf16[128,512]{1,0:T(8,128)(2,1)S(1)}, bf16[128,512]{1,0:T(8,128)(2,1)S(1)}, u32[]{:S(2)}, u32[]{:S(2)}) collective-permute-start(bf16[128,512]{1,0:T(8,128)(2,1)S(1)} %get-tuple-element.82), channel_id=1, source_target_pairs={{0,4},{4,0},{8,12},{12,8},{1,5},{5,1},{9,13},{13,9},{2,6},{6,2},{1... | collective-permute-start | bytes 393224 | tf_op jit(solution)/shard_map/ppermute | solution.py:537
  39.4 3.9 %collective-permute-start.11 = (bf16[64,512]{1,0:T(8,128)(2,1)S(1)}, bf16[64,512]{1,0:T(8,128)(2,1)S(1)}, u32[]{:S(2)}, u32[]{:S(2)}) collective-permute-start(bf16[64,512]{1,0:T(8,128)(2,1)S(1)} %get-tuple-element.84), channel_id=1, source_target_pairs={{0,12},{4,8},{8,4},{12,0},{1,13},{5,9},{9,5},{13,1},{2,14},{6,10},... | collective-permute-start | bytes 196616 | tf_op jit(solution)/shard_map/ppermute | solution.py:537
  44.0 3.7 %collective-permute-done.10.refs_3_ = bf16[64,512]{1,0:T(8,128)(2,1)S(1)} collective-permute-done((bf16[64,512]{1,0:T(8,128)(2,1)S(1)}, bf16[64,512]{1,0:T(8,128)(2,1)S(1)}, u32[]{:S(2)}, u32[]{:S(2)}) %collective-permute-start.10) | collective-permute-done | bytes 65568 | tf_op jit(solution)/shard_map/ppermute | solution.py:537
  47.8 1.5 %collective-permute-start.6 = (bf16[1024,256]{1,0:T(8,128)(2,1)S(1)}, bf16[1024,256]{1,0:T(8,128)(2,1)S(1)}, u32[]{:S(2)}, u32[]{:S(2)}) collective-permute-start(bf16[1024,256]{1,0:T(8,128)(2,1)S(1)} %get-tuple-element.76), channel_id=1, source_target_pairs={{0,2},{1,3},{2,0},{3,1},{4,6},{5,7},{6,4},{7,5},{8,10},{9,11},{10,... | collective-permute-start | bytes 1572872 | tf_op jit(solution)/shard_map/ppermute | solution.py:537
  49.2 1.0 %shard_map.124 = (bf16[1024,256]{1,0:T(8,128)(2,1)S(1)}, bf16[1024,256]{1,0:T(8,128)(2,1)S(1)}, bf16[512,1024]{1,0:T(8,128)(2,1)S(1)}) custom-call(f32[1024,256]{1,0:T(8,128)S(1)} %get-tuple-element.80.refs_0_, f32[1024,256]{1,0:T(8,128)S(1)} %get-tuple-element.81.refs_1_, bf16[128,512]{1,0:T(8,128)(2,1)S(1)} %collective-permute-done.9.refs_2_, ...), custom_call_target="tpu_custom_call" | custom-call | flops 230000000 | bytes 1 | tf_op jit(solution)/shard_map/pallas_call | solution.py:42
  50.3 0.5 shard_map.125.refs_2_.refs_3_.refs_0_
  51.4 1.8 %collective-permute-done.13.refs_1_ = bf16[512,256]{1,0:T(8,128)(2,1)S(1)} collective-permute-done((bf16[512,256]{1,0:T(8,128)(2,1)S(1)}, bf16[512,256]{1,0:T(8,128)(2,1)S(1)}, u32[]{:S(2)}, u32[]{:S(2)}) %collective-permute-start.13) | collective-permute-done | bytes 262176 | tf_op jit(solution)/shard_map/ppermute | solution.py:537
  53.5 1.4 %collective-permute-start.15 = (bf16[512,256]{1,0:T(8,128)(2,1)S(1)}, bf16[512,256]{1,0:T(8,128)(2,1)S(1)}, u32[]{:S(2)}, u32[]{:S(2)}) collective-permute-start(bf16[512,256]{1,0:T(8,128)(2,1)S(1)} %get-tuple-element.92), channel_id=1, source_target_pairs={{0,4},{4,0},{8,12},{12,8},{1,5},{5,1},{9,13},{13,9},{2,6},{6,2},{1... | collective-permute-start | bytes 786440 | tf_op jit(solution)/shard_map/ppermute | solution.py:537
  54.9 1.8 %shard_map.129 = (bf16[1024,512]{1,0:T(8,128)(2,1)S(1)}, bf16[1024,512]{1,0:T(8,128)(2,1)S(1)}) custom-call(s32[1]{0:T(128)} %bitcast.refs_4_.refs_0_, bf16[1024,256]{1,0:T(8,128)(2,1)S(1)} %get-tuple-element.74.refs_2_.refs_1_, bf16[1024,256]{1,0:T(8,128)(2,1)S(1)} %get-tuple-element.86.refs_2_, bf16[1024,256]{1,0:T(8,128)(2,1)S(1)} %get-tuple-element.87.refs_3_, ...), custom_call_target="tpu_custom_call" | custom-call | flops 1150000000 | bytes 1 | tf_op jit(solution)/shard_map/pallas_call | solution.py:42
  56.7 2.1 %collective-permute-done.8.refs_1_.refs_3_ = bf16[512,256]{1,0:T(8,128)(2,1)S(1)} collective-permute-done((bf16[512,256]{1,0:T(8,128)(2,1)S(1)}, bf16[512,256]{1,0:T(8,128)(2,1)S(1)}, u32[]{:S(2)}, u32[]{:S(2)}) %collective-permute-start.8) | collective-permute-done | bytes 262176 | tf_op jit(solution)/shard_map/ppermute | solution.py:537
  59.6 1.8 %collective-permute-start.20 = (bf16[512,256]{1,0:T(8,128)(2,1)S(1)}, bf16[512,256]{1,0:T(8,128)(2,1)S(1)}, u32[]{:S(2)}, u32[]{:S(2)}) collective-permute-start(bf16[512,256]{1,0:T(8,128)(2,1)S(1)} %get-tuple-element.98), channel_id=1, source_target_pairs={{0,4},{4,0},{8,12},{12,8},{1,5},{5,1},{9,13},{13,9},{2,6},{6,2},{1... | collective-permute-start | bytes 786440 | tf_op jit(solution)/shard_map/ppermute | solution.py:537
  61.4 3.1 %collective-permute-done.15.refs_1_.refs_4_ = bf16[512,256]{1,0:T(8,128)(2,1)S(1)} collective-permute-done((bf16[512,256]{1,0:T(8,128)(2,1)S(1)}, bf16[512,256]{1,0:T(8,128)(2,1)S(1)}, u32[]{:S(2)}, u32[]{:S(2)}) %collective-permute-start.15) | collective-permute-done | bytes 262176 | tf_op jit(solution)/shard_map/ppermute | solution.py:537
  64.6 0.6 collective-permute-start.17
  65.3 1.7 %collective-permute-start.18 = (bf16[512,256]{1,0:T(8,128)(2,1)S(1)}, bf16[512,256]{1,0:T(8,128)(2,1)S(1)}, u32[]{:S(2)}, u32[]{:S(2)}) collective-permute-start(bf16[512,256]{1,0:T(8,128)(2,1)S(1)} %get-tuple-element.96), channel_id=1, source_target_pairs={{0,4},{4,0},{8,12},{12,8},{1,5},{5,1},{9,13},{13,9},{2,6},{6,2},{1... | collective-permute-start | bytes 786440 | tf_op jit(solution)/shard_map/ppermute | solution.py:537
  67.0 0.9 shard_map.136
  67.9 0.5 shard_map.137.refs_2_.refs_3_.refs_0_
  68.4 1.6 %collective-permute-done.20.refs_1_.refs_3_ = bf16[512,256]{1,0:T(8,128)(2,1)S(1)} collective-permute-done((bf16[512,256]{1,0:T(8,128)(2,1)S(1)}, bf16[512,256]{1,0:T(8,128)(2,1)S(1)}, u32[]{:S(2)}, u32[]{:S(2)}) %collective-permute-start.20) | collective-permute-done | bytes 262176 | tf_op jit(solution)/shard_map/ppermute | solution.py:537
  70.3 2.5 %collective-permute-start.22 = (bf16[512,256]{1,0:T(8,128)(2,1)S(1)}, bf16[512,256]{1,0:T(8,128)(2,1)S(1)}, u32[]{:S(2)}, u32[]{:S(2)}) collective-permute-start(bf16[512,256]{1,0:T(8,128)(2,1)S(1)} %get-tuple-element.103), channel_id=1, source_target_pairs={{0,4},{4,0},{8,12},{12,8},{1,5},{5,1},{9,13},{13,9},{2,6},{6,2},{1... | collective-permute-start | bytes 786440 | tf_op jit(solution)/shard_map/ppermute | solution.py:537
  72.8 0.8 shard_map.140
  73.6 2.0 %collective-permute-done.18.refs_1_.refs_4_ = bf16[512,256]{1,0:T(8,128)(2,1)S(1)} collective-permute-done((bf16[512,256]{1,0:T(8,128)(2,1)S(1)}, bf16[512,256]{1,0:T(8,128)(2,1)S(1)}, u32[]{:S(2)}, u32[]{:S(2)}) %collective-permute-start.18) | collective-permute-done | bytes 262176 | tf_op jit(solution)/shard_map/ppermute | solution.py:537
  76.1 2.3 %collective-permute-start.25 = (bf16[512,256]{1,0:T(8,128)(2,1)S(1)}, bf16[512,256]{1,0:T(8,128)(2,1)S(1)}, u32[]{:S(2)}, u32[]{:S(2)}) collective-permute-start(bf16[512,256]{1,0:T(8,128)(2,1)S(1)} %shard_map.143.refs_2_), channel_id=1, source_target_pairs={{0,4},{4,0},{8,12},{12,8},{1,5},{5,1},{9,13},{13,9},{2,6},{6,2},{1... | collective-permute-start | bytes 786440 | tf_op jit(solution)/shard_map/ppermute | solution.py:537
  78.4 1.5 %collective-permute-start.21 = (bf16[1024,256]{1,0:T(8,128)(2,1)S(1)}, bf16[1024,256]{1,0:T(8,128)(2,1)S(1)}, u32[]{:S(2)}, u32[]{:S(2)}) collective-permute-start(bf16[1024,256]{1,0:T(8,128)(2,1)S(1)} %get-tuple-element.102), channel_id=1, source_target_pairs={{0,2},{1,3},{2,0},{3,1},{4,6},{5,7},{6,4},{7,5},{8,10},{9,11},{10,... | collective-permute-start | bytes 1572872 | tf_op jit(solution)/shard_map/ppermute | solution.py:537
  79.9 1.4 %collective-permute-done.22.refs_1_.refs_3_ = bf16[512,256]{1,0:T(8,128)(2,1)S(1)} collective-permute-done((bf16[512,256]{1,0:T(8,128)(2,1)S(1)}, bf16[512,256]{1,0:T(8,128)(2,1)S(1)}, u32[]{:S(2)}, u32[]{:S(2)}) %collective-permute-start.22) | collective-permute-done | bytes 262176 | tf_op jit(solution)/shard_map/ppermute | solution.py:537
  81.4 0.8 shard_map.145
  82.3 1.7 %collective-permute-start.27 = (bf16[512,256]{1,0:T(8,128)(2,1)S(1)}, bf16[512,256]{1,0:T(8,128)(2,1)S(1)}, u32[]{:S(2)}, u32[]{:S(2)}) collective-permute-start(bf16[512,256]{1,0:T(8,128)(2,1)S(1)} %shard_map.146.refs_5_.refs_1_), channel_id=1, source_target_pairs={{0,4},{4,0},{8,12},{12,8},{1,5},{5,1},{9,13},{13,9},{2,6},{6,2},{1... | collective-permute-start | bytes 786440 | tf_op jit(solution)/shard_map/ppermute | solution.py:537
  84.0 2.9 %collective-permute-done.25.refs_4_ = bf16[512,256]{1,0:T(8,128)(2,1)S(1)} collective-permute-done((bf16[512,256]{1,0:T(8,128)(2,1)S(1)}, bf16[512,256]{1,0:T(8,128)(2,1)S(1)}, u32[]{:S(2)}, u32[]{:S(2)}) %collective-permute-start.25) | collective-permute-done | bytes 262176 | tf_op jit(solution)/shard_map/ppermute | solution.py:537
  86.9 0.8 shard_map.147
  87.8 1.6 %collective-permute-start.28 = (bf16[512,256]{1,0:T(8,128)(2,1)S(1)}, bf16[512,256]{1,0:T(8,128)(2,1)S(1)}, u32[]{:S(2)}, u32[]{:S(2)}) collective-permute-start(bf16[512,256]{1,0:T(8,128)(2,1)S(1)} %shard_map.148.refs_2_), channel_id=1, source_target_pairs={{0,4},{4,0},{8,12},{12,8},{1,5},{5,1},{9,13},{13,9},{2,6},{6,2},{1... | collective-permute-start | bytes 786440 | tf_op jit(solution)/shard_map/ppermute | solution.py:537
  89.4 1.2 %collective-permute-done.21.refs_1_ = bf16[1024,256]{1,0:T(8,128)(2,1)S(1)} collective-permute-done((bf16[1024,256]{1,0:T(8,128)(2,1)S(1)}, bf16[1024,256]{1,0:T(8,128)(2,1)S(1)}, u32[]{:S(2)}, u32[]{:S(2)}) %collective-permute-start.21) | collective-permute-done | bytes 524320 | tf_op jit(solution)/shard_map/ppermute | solution.py:537
  90.6 0.9 shard_map.149
  91.5 1.0 %collective-permute-done.27.refs_3_ = bf16[512,256]{1,0:T(8,128)(2,1)S(1)} collective-permute-done((bf16[512,256]{1,0:T(8,128)(2,1)S(1)}, bf16[512,256]{1,0:T(8,128)(2,1)S(1)}, u32[]{:S(2)}, u32[]{:S(2)}) %collective-permute-start.27) | collective-permute-done | bytes 262176 | tf_op jit(solution)/shard_map/ppermute | solution.py:537
  92.5 5.5 %collective-permute-done.28.refs_4_ = bf16[512,256]{1,0:T(8,128)(2,1)S(1)} collective-permute-done((bf16[512,256]{1,0:T(8,128)(2,1)S(1)}, bf16[512,256]{1,0:T(8,128)(2,1)S(1)}, u32[]{:S(2)}, u32[]{:S(2)}) %collective-permute-start.28) | collective-permute-done | bytes 262176 | tf_op jit(solution)/shard_map/ppermute | solution.py:537
  98.0 0.8 shard_map.150
  (70 shorter events, 5.1 us)
Async XLA Ops:
  0.6 11.1 %copy-start = (bf16[1024,1024]{1,0:T(8,128)(2,1)S(1)}, bf16[1024,1024]{1,0:T(8,128)(2,1)}, u32[]{:S(2)}) copy-start(bf16[1024,1024]{1,0:T(8,128)(2,1)} %refs_1_.17) | copy-start | bytes 6291460
  0.7 11.1 %copy-start.3 = (bf16[1024,256]{1,0:T(8,128)(2,1)S(1)}, bf16[1024,256]{1,0:T(8,128)(2,1)}, u32[]{:S(2)}) copy-start(bf16[1024,256]{1,0:T(8,128)(2,1)} %refs_4_.1) | copy-start | bytes 1572868
  6.0 6.4 %copy-start.6 = (bf16[1024,512]{1,0:T(8,128)(2,1)S(1)}, bf16[1024,512]{1,0:T(8,128)(2,1)}, u32[]{:S(2)}) copy-start(bf16[1024,512]{1,0:T(8,128)(2,1)} %get-tuple-element.59.refs_1_.refs_3_.refs_4_) | copy-start | bytes 3145732
  6.0 6.4 %copy-start.7 = (bf16[512,512]{1,0:T(8,128)(2,1)S(1)}, bf16[512,512]{1,0:T(8,128)(2,1)}, u32[]{:S(2)}) copy-start(bf16[512,512]{1,0:T(8,128)(2,1)} %get-tuple-element.60.refs_2_.refs_4_.refs_5_) | copy-start | bytes 1572868
  6.0 6.4 %copy-start.8 = (bf16[256,512]{1,0:T(8,128)(2,1)S(1)}, bf16[256,512]{1,0:T(8,128)(2,1)}, u32[]{:S(2)}) copy-start(bf16[256,512]{1,0:T(8,128)(2,1)} %get-tuple-element.61.refs_3_.refs_5_.refs_6_) | copy-start | bytes 786436
  6.0 9.5 %collective-permute-start.1 = (bf16[64,512]{1,0:T(8,128)(2,1)}, bf16[64,512]{1,0:T(8,128)(2,1)S(1)}, u32[]{:S(2)}, u32[]{:S(2)}) collective-permute-start(bf16[64,512]{1,0:T(8,128)(2,1)} %get-tuple-element.65), channel_id=1, source_target_pairs={{0,8},{4,12},{8,0},{12,4},{1,9},{5,13},{9,1},{13,5},{2,10},{6,14},... | collective-permute-start | bytes 196616 | tf_op jit(solution)/shard_map/ppermute | solution.py:537
  10.1 7.0 %collective-permute-start.2 = (bf16[64,512]{1,0:T(8,128)(2,1)}, bf16[64,512]{1,0:T(8,128)(2,1)S(1)}, u32[]{:S(2)}, u32[]{:S(2)}) collective-permute-start(bf16[64,512]{1,0:T(8,128)(2,1)} %get-tuple-element.65), channel_id=1, source_target_pairs={{0,12},{4,8},{8,4},{12,0},{1,13},{5,9},{9,5},{13,1},{2,14},{6,10},... | collective-permute-start | bytes 196616 | tf_op jit(solution)/shard_map/ppermute | solution.py:537
  11.5 6.4 %collective-permute-start = (bf16[128,512]{1,0:T(8,128)(2,1)}, bf16[128,512]{1,0:T(8,128)(2,1)S(1)}, u32[]{:S(2)}, u32[]{:S(2)}) collective-permute-start(bf16[128,512]{1,0:T(8,128)(2,1)} %get-tuple-element.64), channel_id=1, source_target_pairs={{0,4},{4,0},{8,12},{12,8},{1,5},{5,1},{9,13},{13,9},{2,6},{6,2},{1... | collective-permute-start | bytes 393224 | tf_op jit(solution)/shard_map/ppermute | solution.py:537
  12.5 2.4 %copy-start.1 = (bf16[1024,1024]{1,0:T(8,128)(2,1)S(1)}, bf16[1024,1024]{1,0:T(8,128)(2,1)}, u32[]{:S(2)}) copy-start(bf16[1024,1024]{1,0:T(8,128)(2,1)} %refs_1_.13) | copy-start | bytes 6291460
  12.5 2.4 %copy-start.2 = (bf16[1024,256]{1,0:T(8,128)(2,1)S(1)}, bf16[1024,256]{1,0:T(8,128)(2,1)}, u32[]{:S(2)}) copy-start(bf16[1024,256]{1,0:T(8,128)(2,1)} %refs_2_.3) | copy-start | bytes 1572868
  22.3 7.1 %collective-permute-start.3 = (bf16[512,256]{1,0:T(8,128)(2,1)S(1)}, bf16[512,256]{1,0:T(8,128)(2,1)S(1)}, u32[]{:S(2)}, u32[]{:S(2)}) collective-permute-start(bf16[512,256]{1,0:T(8,128)(2,1)S(1)} %shard_map.114.refs_10_.refs_0_), channel_id=1, source_target_pairs={{0,4},{4,0},{8,12},{12,8},{1,5},{5,1},{9,13},{13,9},{2,6},{6,2},{1... | collective-permute-start | bytes 786440 | tf_op jit(solution)/shard_map/ppermute | solution.py:537
  30.2 13.2 %collective-permute-start.4 = (bf16[1024,512]{1,0:T(8,128)(2,1)S(1)}, bf16[1024,512]{1,0:T(8,128)(2,1)S(1)}, u32[]{:S(2)}, u32[]{:S(2)}) collective-permute-start(bf16[1024,512]{1,0:T(8,128)(2,1)S(1)} %get-tuple-element.71), channel_id=1, source_target_pairs={{0,1},{1,0},{2,3},{3,2},{4,5},{5,4},{6,7},{7,6},{8,9},{9,8},{10,11... | collective-permute-start | bytes 3145736 | tf_op jit(solution)/shard_map/ppermute | solution.py:537
  30.2 9.1 %collective-permute-start.5 = (bf16[512,256]{1,0:T(8,128)(2,1)S(1)}, bf16[512,256]{1,0:T(8,128)(2,1)S(1)}, u32[]{:S(2)}, u32[]{:S(2)}) collective-permute-start(bf16[512,256]{1,0:T(8,128)(2,1)S(1)} %shard_map.116.refs_2_.refs_0_), channel_id=1, source_target_pairs={{0,4},{4,0},{8,12},{12,8},{1,5},{5,1},{9,13},{13,9},{2,6},{6,2},{1... | collective-permute-start | bytes 786440 | tf_op jit(solution)/shard_map/ppermute | solution.py:537
  31.8 11.9 %collective-permute-start.7 = (bf16[512,256]{1,0:T(8,128)(2,1)S(1)}, bf16[512,256]{1,0:T(8,128)(2,1)S(1)}, u32[]{:S(2)}, u32[]{:S(2)}) collective-permute-start(bf16[512,256]{1,0:T(8,128)(2,1)S(1)} %shard_map.117.refs_3_.refs_1_), channel_id=1, source_target_pairs={{0,1},{1,0},{2,3},{3,2},{4,8},{5,9},{6,10},{7,11},{8,4},{9,5},{10,... | collective-permute-start | bytes 786440 | tf_op jit(solution)/shard_map/ppermute | solution.py:694
  36.0 13.3 %collective-permute-start.9 = (bf16[128,512]{1,0:T(8,128)(2,1)S(1)}, bf16[128,512]{1,0:T(8,128)(2,1)S(1)}, u32[]{:S(2)}, u32[]{:S(2)}) collective-permute-start(bf16[128,512]{1,0:T(8,128)(2,1)S(1)} %get-tuple-element.82), channel_id=1, source_target_pairs={{0,4},{4,0},{8,12},{12,8},{1,5},{5,1},{9,13},{13,9},{2,6},{6,2},{1... | collective-permute-start | bytes 393224 | tf_op jit(solution)/shard_map/ppermute | solution.py:537
  39.3 8.4 %collective-permute-start.10 = (bf16[64,512]{1,0:T(8,128)(2,1)S(1)}, bf16[64,512]{1,0:T(8,128)(2,1)S(1)}, u32[]{:S(2)}, u32[]{:S(2)}) collective-permute-start(bf16[64,512]{1,0:T(8,128)(2,1)S(1)} %get-tuple-element.83), channel_id=1, source_target_pairs={{0,8},{4,12},{8,0},{12,4},{1,9},{5,13},{9,1},{13,5},{2,10},{6,14},... | collective-permute-start | bytes 196616 | tf_op jit(solution)/shard_map/ppermute | solution.py:537
  39.4 8.4 %collective-permute-start.11 = (bf16[64,512]{1,0:T(8,128)(2,1)S(1)}, bf16[64,512]{1,0:T(8,128)(2,1)S(1)}, u32[]{:S(2)}, u32[]{:S(2)}) collective-permute-start(bf16[64,512]{1,0:T(8,128)(2,1)S(1)} %get-tuple-element.84), channel_id=1, source_target_pairs={{0,12},{4,8},{8,4},{12,0},{1,13},{5,9},{9,5},{13,1},{2,14},{6,10},... | collective-permute-start | bytes 196616 | tf_op jit(solution)/shard_map/ppermute | solution.py:537
  43.3 10.0 %collective-permute-start.12 = (bf16[512,256]{1,0:T(8,128)(2,1)S(1)}, bf16[512,256]{1,0:T(8,128)(2,1)S(1)}, u32[]{:S(2)}, u32[]{:S(2)}) collective-permute-start(bf16[512,256]{1,0:T(8,128)(2,1)S(1)} %shard_map.120.refs_2_.refs_1_), channel_id=1, source_target_pairs={{0,1},{1,0},{2,3},{3,2},{4,8},{5,9},{6,10},{7,11},{8,4},{9,5},{10,... | collective-permute-start | bytes 786440 | tf_op jit(solution)/shard_map/ppermute | solution.py:694
  43.7 9.5 %collective-permute-start.13 = (bf16[512,256]{1,0:T(8,128)(2,1)S(1)}, bf16[512,256]{1,0:T(8,128)(2,1)S(1)}, u32[]{:S(2)}, u32[]{:S(2)}) collective-permute-start(bf16[512,256]{1,0:T(8,128)(2,1)S(1)} %shard_map.122.refs_4_.refs_0_), channel_id=1, source_target_pairs={{0,4},{4,0},{8,12},{12,8},{1,5},{5,1},{9,13},{13,9},{2,6},{6,2},{1... | collective-permute-start | bytes 786440 | tf_op jit(solution)/shard_map/ppermute | solution.py:537
  47.7 11.1 %collective-permute-start.8 = (bf16[512,256]{1,0:T(8,128)(2,1)S(1)}, bf16[512,256]{1,0:T(8,128)(2,1)S(1)}, u32[]{:S(2)}, u32[]{:S(2)}) collective-permute-start(bf16[512,256]{1,0:T(8,128)(2,1)S(1)} %get-tuple-element.79), channel_id=1, source_target_pairs={{0,4},{4,0},{8,12},{12,8},{1,5},{5,1},{9,13},{13,9},{2,6},{6,2},{1... | collective-permute-start | bytes 786440 | tf_op jit(solution)/shard_map/ppermute | solution.py:537
  47.8 19.2 %collective-permute-start.6 = (bf16[1024,256]{1,0:T(8,128)(2,1)S(1)}, bf16[1024,256]{1,0:T(8,128)(2,1)S(1)}, u32[]{:S(2)}, u32[]{:S(2)}) collective-permute-start(bf16[1024,256]{1,0:T(8,128)(2,1)S(1)} %get-tuple-element.76), channel_id=1, source_target_pairs={{0,2},{1,3},{2,0},{3,1},{4,6},{5,7},{6,4},{7,5},{8,10},{9,11},{10,... | collective-permute-start | bytes 1572872 | tf_op jit(solution)/shard_map/ppermute | solution.py:537
  53.2 1.7 %copy-start.4 = (bf16[1024,256]{1,0:T(8,128)(2,1)S(1)}, bf16[1024,256]{1,0:T(8,128)(2,1)}, u32[]{:S(2)}) copy-start(bf16[1024,256]{1,0:T(8,128)(2,1)} %refs_5_.1) | copy-start | bytes 1572868
  53.3 1.7 %copy-start.5 = (bf16[1024,256]{1,0:T(8,128)(2,1)S(1)}, bf16[1024,256]{1,0:T(8,128)(2,1)}, u32[]{:S(2)}) copy-start(bf16[1024,256]{1,0:T(8,128)(2,1)} %refs_6_.1) | copy-start | bytes 1572868
  53.3 6.2 %collective-permute-start.16 = (bf16[512,256]{1,0:T(8,128)(2,1)S(1)}, bf16[512,256]{1,0:T(8,128)(2,1)S(1)}, u32[]{:S(2)}, u32[]{:S(2)}) collective-permute-start(bf16[512,256]{1,0:T(8,128)(2,1)S(1)} %shard_map.127.refs_4_.refs_1_), channel_id=1, source_target_pairs={{0,1},{1,0},{2,3},{3,2},{4,8},{5,9},{6,10},{7,11},{8,4},{9,5},{10,... | collective-permute-start | bytes 786440 | tf_op jit(solution)/shard_map/ppermute | solution.py:694
  53.5 11.0 %collective-permute-start.15 = (bf16[512,256]{1,0:T(8,128)(2,1)S(1)}, bf16[512,256]{1,0:T(8,128)(2,1)S(1)}, u32[]{:S(2)}, u32[]{:S(2)}) collective-permute-start(bf16[512,256]{1,0:T(8,128)(2,1)S(1)} %get-tuple-element.92), channel_id=1, source_target_pairs={{0,4},{4,0},{8,12},{12,8},{1,5},{5,1},{9,13},{13,9},{2,6},{6,2},{1... | collective-permute-start | bytes 786440 | tf_op jit(solution)/shard_map/ppermute | solution.py:537
  58.9 6.3 %collective-permute-start.14 = (bf16[512,256]{1,0:T(8,128)(2,1)S(1)}, bf16[512,256]{1,0:T(8,128)(2,1)S(1)}, u32[]{:S(2)}, u32[]{:S(2)}) collective-permute-start(bf16[512,256]{1,0:T(8,128)(2,1)S(1)} %shard_map.130.refs_2_.refs_1_), channel_id=1, source_target_pairs={{0,1},{1,0},{2,3},{3,2},{4,8},{5,9},{6,10},{7,11},{8,4},{9,5},{10,... | collective-permute-start | bytes 786440 | tf_op jit(solution)/shard_map/ppermute | solution.py:694
  59.6 10.5 %collective-permute-start.20 = (bf16[512,256]{1,0:T(8,128)(2,1)S(1)}, bf16[512,256]{1,0:T(8,128)(2,1)S(1)}, u32[]{:S(2)}, u32[]{:S(2)}) collective-permute-start(bf16[512,256]{1,0:T(8,128)(2,1)S(1)} %get-tuple-element.98), channel_id=1, source_target_pairs={{0,4},{4,0},{8,12},{12,8},{1,5},{5,1},{9,13},{13,9},{2,6},{6,2},{1... | collective-permute-start | bytes 786440 | tf_op jit(solution)/shard_map/ppermute | solution.py:537
  64.5 5.7 %collective-permute-start.19 = (bf16[512,256]{1,0:T(8,128)(2,1)S(1)}, bf16[512,256]{1,0:T(8,128)(2,1)S(1)}, u32[]{:S(2)}, u32[]{:S(2)}) collective-permute-start(bf16[512,256]{1,0:T(8,128)(2,1)S(1)} %shard_map.133.refs_1_), channel_id=1, source_target_pairs={{0,1},{1,0},{2,3},{3,2},{4,8},{5,9},{6,10},{7,11},{8,4},{9,5},{10,... | collective-permute-start | bytes 786440 | tf_op jit(solution)/shard_map/ppermute | solution.py:694
  64.6 11.2 %collective-permute-start.17 = (bf16[1024,512]{1,0:T(8,128)(2,1)S(1)}, bf16[1024,512]{1,0:T(8,128)(2,1)S(1)}, u32[]{:S(2)}, u32[]{:S(2)}) collective-permute-start(bf16[1024,512]{1,0:T(8,128)(2,1)S(1)} %shard_map.134.refs_4_), channel_id=1, source_target_pairs={{0,1},{1,0},{2,3},{3,2},{4,5},{5,4},{6,7},{7,6},{8,9},{9,8},{10,11... | collective-permute-start | bytes 3145736 | tf_op jit(solution)/shard_map/ppermute | solution.py:537
  65.3 10.4 %collective-permute-start.18 = (bf16[512,256]{1,0:T(8,128)(2,1)S(1)}, bf16[512,256]{1,0:T(8,128)(2,1)S(1)}, u32[]{:S(2)}, u32[]{:S(2)}) collective-permute-start(bf16[512,256]{1,0:T(8,128)(2,1)S(1)} %get-tuple-element.96), channel_id=1, source_target_pairs={{0,4},{4,0},{8,12},{12,8},{1,5},{5,1},{9,13},{13,9},{2,6},{6,2},{1... | collective-permute-start | bytes 786440 | tf_op jit(solution)/shard_map/ppermute | solution.py:537
  70.1 6.0 %collective-permute-start.23 = (bf16[512,256]{1,0:T(8,128)(2,1)S(1)}, bf16[512,256]{1,0:T(8,128)(2,1)S(1)}, u32[]{:S(2)}, u32[]{:S(2)}) collective-permute-start(bf16[512,256]{1,0:T(8,128)(2,1)S(1)} %shard_map.138.refs_4_.refs_0_), channel_id=1, source_target_pairs={{0,1},{1,0},{2,3},{3,2},{4,8},{5,9},{6,10},{7,11},{8,4},{9,5},{10,... | collective-permute-start | bytes 786440 | tf_op jit(solution)/shard_map/ppermute | solution.py:694
  70.3 11.0 %collective-permute-start.22 = (bf16[512,256]{1,0:T(8,128)(2,1)S(1)}, bf16[512,256]{1,0:T(8,128)(2,1)S(1)}, u32[]{:S(2)}, u32[]{:S(2)}) collective-permute-start(bf16[512,256]{1,0:T(8,128)(2,1)S(1)} %get-tuple-element.103), channel_id=1, source_target_pairs={{0,4},{4,0},{8,12},{12,8},{1,5},{5,1},{9,13},{13,9},{2,6},{6,2},{1... | collective-permute-start | bytes 786440 | tf_op jit(solution)/shard_map/ppermute | solution.py:537
  75.7 6.5 %collective-permute-start.26 = (bf16[512,256]{1,0:T(8,128)(2,1)S(1)}, bf16[512,256]{1,0:T(8,128)(2,1)S(1)}, u32[]{:S(2)}, u32[]{:S(2)}) collective-permute-start(bf16[512,256]{1,0:T(8,128)(2,1)S(1)} %shard_map.141.refs_2_.refs_0_), channel_id=1, source_target_pairs={{0,1},{1,0},{2,3},{3,2},{4,8},{5,9},{6,10},{7,11},{8,4},{9,5},{10,... | collective-permute-start | bytes 786440 | tf_op jit(solution)/shard_map/ppermute | solution.py:694
  76.1 10.8 %collective-permute-start.25 = (bf16[512,256]{1,0:T(8,128)(2,1)S(1)}, bf16[512,256]{1,0:T(8,128)(2,1)S(1)}, u32[]{:S(2)}, u32[]{:S(2)}) collective-permute-start(bf16[512,256]{1,0:T(8,128)(2,1)S(1)} %shard_map.143.refs_2_), channel_id=1, source_target_pairs={{0,4},{4,0},{8,12},{12,8},{1,5},{5,1},{9,13},{13,9},{2,6},{6,2},{1... | collective-permute-start | bytes 786440 | tf_op jit(solution)/shard_map/ppermute | solution.py:537
  78.4 12.2 %collective-permute-start.21 = (bf16[1024,256]{1,0:T(8,128)(2,1)S(1)}, bf16[1024,256]{1,0:T(8,128)(2,1)S(1)}, u32[]{:S(2)}, u32[]{:S(2)}) collective-permute-start(bf16[1024,256]{1,0:T(8,128)(2,1)S(1)} %get-tuple-element.102), channel_id=1, source_target_pairs={{0,2},{1,3},{2,0},{3,1},{4,6},{5,7},{6,4},{7,5},{8,10},{9,11},{10,... | collective-permute-start | bytes 1572872 | tf_op jit(solution)/shard_map/ppermute | solution.py:537
  81.3 6.4 %collective-permute-start.24 = (bf16[512,256]{1,0:T(8,128)(2,1)S(1)}, bf16[512,256]{1,0:T(8,128)(2,1)S(1)}, u32[]{:S(2)}, u32[]{:S(2)}) collective-permute-start(bf16[512,256]{1,0:T(8,128)(2,1)S(1)} %shard_map.144.refs_5_.refs_0_), channel_id=1, source_target_pairs={{0,1},{1,0},{2,3},{3,2},{4,8},{5,9},{6,10},{7,11},{8,4},{9,5},{10,... | collective-permute-start | bytes 786440 | tf_op jit(solution)/shard_map/ppermute | solution.py:694
  82.3 10.2 %collective-permute-start.27 = (bf16[512,256]{1,0:T(8,128)(2,1)S(1)}, bf16[512,256]{1,0:T(8,128)(2,1)S(1)}, u32[]{:S(2)}, u32[]{:S(2)}) collective-permute-start(bf16[512,256]{1,0:T(8,128)(2,1)S(1)} %shard_map.146.refs_5_.refs_1_), channel_id=1, source_target_pairs={{0,4},{4,0},{8,12},{12,8},{1,5},{5,1},{9,13},{13,9},{2,6},{6,2},{1... | collective-permute-start | bytes 786440 | tf_op jit(solution)/shard_map/ppermute | solution.py:537
  87.8 10.2 %collective-permute-start.28 = (bf16[512,256]{1,0:T(8,128)(2,1)S(1)}, bf16[512,256]{1,0:T(8,128)(2,1)S(1)}, u32[]{:S(2)}, u32[]{:S(2)}) collective-permute-start(bf16[512,256]{1,0:T(8,128)(2,1)S(1)} %shard_map.148.refs_2_), channel_id=1, source_target_pairs={{0,4},{4,0},{8,12},{12,8},{1,5},{5,1},{9,13},{13,9},{2,6},{6,2},{1... | collective-permute-start | bytes 786440 | tf_op jit(solution)/shard_map/ppermute | solution.py:537

commit v15 on v13

--- a/solution.py
+++ b/solution.py
@@ -602,6 +602,23 @@
     )
 
 
+def relay_all_body(*refs):
+    count = len(refs) // 2
+    for source, target in zip(refs[:count], refs[count:]):
+        target[...] = source[...]
+
+
+def relay_all(blocks, after):
+    return run(
+        relay_all_body,
+        list(blocks),
+        after,
+        out_shape=[shape(*block.shape) for block in blocks],
+        compiler_params=params(3),
+        cost_estimate=cost(0.2),
+    )
+
+
 class Line:
     lag = 3
     half_weights = (3.0, 3.0, 3.0, 3.0, 3.0, 3.0, 3.0, 0.5)
@@ -714,9 +731,10 @@
     dquery, dkv, query_first, query_second, *away = step(
         backward, query, grad, attended_t, stats, tokens, levels, fars, far_bits, pieces
     )
-    backs = [exchange(piece, "seq", d) for d, piece in enumerate(away, 1)]
     line.meet(rows)
     mixed.advance()
+    away = step(relay_all, away)
+    backs = [exchange(piece, "seq", d) for d, piece in enumerate(away, 1)]
     line.meet(rows)
     dkey, dvalue, dkv_t = step(close_keys, dkv, backs, far_bits, local_levels)
     line.enter(step(relay, query_first))

time: 98.4 us -> 102 us (1.037)
  starting transfers between devices: 35.7 us -> 39.7 us
    ppermute x21, starting transfers between devices: 34.6 us -> 38.6 us  [exchange(): return lax.ppermute(block, axis, [(i, i ^ distance) for i in range(count)])]
    pallas_call x41 -> x42, Pallas kernels: 33.7 us -> 33.7 us  [run(): return pl.pallas_call(kernel, in_specs=in_specs, **options)(*ready, *after)]
  transfers between devices with their start and end apart: 29 -> 29, of which waited for: 14 -> 11; matrix products, arithmetic and copies ran while one was open for 0% -> 0% of each run, Pallas kernels for 23% -> 22%
where the time goes in v15:
time: 102 us
  starting transfers between devices  39.7 us (39%)
  Pallas kernels  33.7 us (33%)
  waiting for transfers between devices  27.6 us (27%)
  between operations  1.13 us (1%)
    ppermute x21, starting transfers between devices, exchange(): return lax.ppermute(block, axis, [(i, i ^ distance) for i in range(count)])  38.6 us
    pallas_call x42, Pallas kernels, run(): return pl.pallas_call(kernel, in_specs=in_specs, **options)(*ready, *after)  33.7 us
    ppermute x21, waiting for transfers between devices, exchange(): return lax.ppermute(block, axis, [(i, i ^ distance) for i in range(count)])  27.5 us
  transfers between devices with their start and end apart: 29, of which 11 were waited for; matrix products, arithmetic and copies ran while one was open for 0% of the time, Pallas kernels for 22%

profile of v15, /device:TPU:0, one launch (start us, length us, event | category | flops | bytes accessed | tf_op | source)
XLA Modules:
  0.0 102.2 jit_solution(4307079143965802895)
XLA Ops:
  0.7 5.3 %shard_map.110 = (bf16[1024,512]{1,0:T(8,128)(2,1)}, bf16[512,512]{1,0:T(8,128)(2,1)}, bf16[256,512]{1,0:T(8,128)(2,1)}, bf16[128,512]{1,0:T(8,128)(2,1)}, bf16[64,512]{1,0:T(8,128)(2,1)}) custom-call(bf16[1024,1024]{1,0:T(8,128)(2,1)} %refs_1_.17, bf16[1024,256]{1,0:T(8,128)(2,1)} %refs_5_.1, bf16[1024,256]{1,0:T(8,128)(2,1)} %refs_6_.1, ...), custom_call_target="tpu_custom_call" | custom-call | flops 5750000128 | bytes 1 | tf_op jit(solution)/shard_map/pallas_call | solution.py:42
  6.0 4.1 %collective-permute-start.1 = (bf16[64,512]{1,0:T(8,128)(2,1)}, bf16[64,512]{1,0:T(8,128)(2,1)S(1)}, u32[]{:S(2)}, u32[]{:S(2)}) collective-permute-start(bf16[64,512]{1,0:T(8,128)(2,1)} %get-tuple-element.64), channel_id=1, source_target_pairs={{0,8},{4,12},{8,0},{12,4},{1,9},{5,13},{9,1},{13,5},{2,10},{6,14},... | collective-permute-start | bytes 196616 | tf_op jit(solution)/shard_map/ppermute | solution.py:476
  10.1 1.3 %collective-permute-start.2 = (bf16[64,512]{1,0:T(8,128)(2,1)}, bf16[64,512]{1,0:T(8,128)(2,1)S(1)}, u32[]{:S(2)}, u32[]{:S(2)}) collective-permute-start(bf16[64,512]{1,0:T(8,128)(2,1)} %get-tuple-element.64), channel_id=1, source_target_pairs={{0,12},{4,8},{8,4},{12,0},{1,13},{5,9},{9,5},{13,1},{2,14},{6,10},... | collective-permute-start | bytes 196616 | tf_op jit(solution)/shard_map/ppermute | solution.py:476
  11.7 0.7 shard_map.109.refs_0_.refs_4_
  12.5 2.3 %shard_map.111 = (f32[4096,256]{1,0:T(8,128)S(1)}, f32[4,1024]{1,0:T(4,128)S(1)}) custom-call(bf16[1024,256]{1,0:T(8,128)(2,1)S(1)} %shard_map.109.refs_0_.refs_4_, bf16[1024,512]{1,0:T(8,128)(2,1)S(1)} %copy-done.6, bf16[512,512]{1,0:T(8,128)(2,1)S(1)} %copy-done.7, bf16[256,512]{1,0:T(8,128)(2,1)S(1)} %copy-done.8, ...), custom_call_target="tpu_custom_call" | custom-call | flops 2644999936 | bytes 1 | tf_op jit(solution)/shard_map/pallas_call | solution.py:42
  14.9 0.7 shard_map.112.refs_9_.refs_1_
  15.6 1.5 %collective-permute-done.2.refs_8_.refs_10_ = bf16[64,512]{1,0:T(8,128)(2,1)S(1)} collective-permute-done((bf16[64,512]{1,0:T(8,128)(2,1)}, bf16[64,512]{1,0:T(8,128)(2,1)S(1)}, u32[]{:S(2)}, u32[]{:S(2)}) %collective-permute-start.2) | collective-permute-done | bytes 65568 | tf_op jit(solution)/shard_map/ppermute | solution.py:476
  17.1 0.8 collective-permute-done.refs_6_.refs_8_
  17.9 3.9 %shard_map.113 = (bf16[1024,256]{1,0:T(8,128)(2,1)S(1)}, bf16[256,1024]{1,0:T(8,128)(2,1)S(1)}, f32[4,1024]{1,0:T(4,128)S(1)}) custom-call(bf16[1024,256]{1,0:T(8,128)(2,1)S(1)} %shard_map.109.refs_0_.refs_4_, f32[4096,256]{1,0:T(8,128)S(1)} %get-tuple-element.61.refs_2_.refs_1_, f32[4,1024]{1,0:T(4,128)S(1)} %get-tuple-element.62.refs_2_, ...), custom_call_target="tpu_custom_call" | custom-call | flops 4600000000 | bytes 1 | tf_op jit(solution)/shard_map/pallas_call | solution.py:42
  22.8 1.0 collective-permute-start.4
  23.8 0.7 shard_map.116
  24.5 1.2 %collective-permute-start.10 = (bf16[512,256]{1,0:T(8,128)(2,1)S(1)}, bf16[512,256]{1,0:T(8,128)(2,1)S(1)}, u32[]{:S(2)}, u32[]{:S(2)}) collective-permute-start(bf16[512,256]{1,0:T(8,128)(2,1)S(1)} %shard_map.115.refs_3_.refs_0_), channel_id=1, source_target_pairs={{0,4},{4,0},{8,12},{12,8},{1,5},{5,1},{9,13},{13,9},{2,6},{6,2},{1... | collective-permute-start | bytes 786440 | tf_op jit(solution)/shard_map/ppermute | solution.py:476
  25.7 6.9 %shard_map.117 = (bf16[1024,256]{1,0:T(8,128)(2,1)S(1)}, f32[1024,512]{1,0:T(8,128)S(1)}, bf16[512,256]{1,0:T(8,128)(2,1)S(1)}, bf16[512,256]{1,0:T(8,128)(2,1)S...) custom-call(bf16[1024,256]{1,0:T(8,128)(2,1)S(1)} %shard_map.109.refs_0_.refs_4_, ...), custom_call_target="tpu_custom_call" | custom-call | flops 9200000000 | bytes 1 | tf_op jit(solution)/shard_map/pallas_call | solution.py:42
  32.7 0.6 collective-permute-start.6
  33.6 2.0 %collective-permute-start.7 = (bf16[128,512]{1,0:T(8,128)(2,1)S(1)}, bf16[128,512]{1,0:T(8,128)(2,1)S(1)}, u32[]{:S(2)}, u32[]{:S(2)}) collective-permute-start(bf16[128,512]{1,0:T(8,128)(2,1)S(1)} %get-tuple-element.78.refs_2_), channel_id=1, source_target_pairs={{0,4},{4,0},{8,12},{12,8},{1,5},{5,1},{9,13},{13,9},{2,6},{6,2},{1... | collective-permute-start | bytes 393224 | tf_op jit(solution)/shard_map/ppermute | solution.py:476
  35.5 1.9 %collective-permute-start.8 = (bf16[64,512]{1,0:T(8,128)(2,1)S(1)}, bf16[64,512]{1,0:T(8,128)(2,1)S(1)}, u32[]{:S(2)}, u32[]{:S(2)}) collective-permute-start(bf16[64,512]{1,0:T(8,128)(2,1)S(1)} %get-tuple-element.79), channel_id=1, source_target_pairs={{0,8},{4,12},{8,0},{12,4},{1,9},{5,13},{9,1},{13,5},{2,10},{6,14},... | collective-permute-start | bytes 196616 | tf_op jit(solution)/shard_map/ppermute | solution.py:476
  37.4 0.6 collective-permute-start.9
  38.2 8.3 %collective-permute-done.8.refs_2_ = bf16[64,512]{1,0:T(8,128)(2,1)S(1)} collective-permute-done((bf16[64,512]{1,0:T(8,128)(2,1)S(1)}, bf16[64,512]{1,0:T(8,128)(2,1)S(1)}, u32[]{:S(2)}, u32[]{:S(2)}) %collective-permute-start.8) | collective-permute-done | bytes 65568 | tf_op jit(solution)/shard_map/ppermute | solution.py:476
  46.5 1.5 %collective-permute-start.5 = (bf16[1024,256]{1,0:T(8,128)(2,1)S(1)}, bf16[1024,256]{1,0:T(8,128)(2,1)S(1)}, u32[]{:S(2)}, u32[]{:S(2)}) collective-permute-start(bf16[1024,256]{1,0:T(8,128)(2,1)S(1)} %get-tuple-element.72), channel_id=1, source_target_pairs={{0,2},{1,3},{2,0},{3,1},{4,6},{5,7},{6,4},{7,5},{8,10},{9,11},{10,... | collective-permute-start | bytes 1572872 | tf_op jit(solution)/shard_map/ppermute | solution.py:476
  48.0 1.0 %shard_map.122 = (bf16[1024,256]{1,0:T(8,128)(2,1)S(1)}, bf16[1024,256]{1,0:T(8,128)(2,1)S(1)}, bf16[512,1024]{1,0:T(8,128)(2,1)S(1)}) custom-call(f32[1024,512]{1,0:T(8,128)S(1)} %get-tuple-element.74.refs_0_, bf16[128,512]{1,0:T(8,128)(2,1)S(1)} %collective-permute-done.7.refs_1_, bf16[64,512]{1,0:T(8,128)(2,1)S(1)} %collective-permute-done.8.refs_2_, ...), custom_call_target="tpu_custom_call" | custom-call | flops 230000000 | bytes 1 | tf_op jit(solution)/shard_map/pallas_call | solution.py:42
  49.0 0.5 collective-permute-start.13
  49.6 0.5 shard_map.124.refs_4_.refs_3_.refs_0_
  50.2 1.6 %collective-permute-start.11 = (bf16[512,256]{1,0:T(8,128)(2,1)S(1)}, bf16[512,256]{1,0:T(8,128)(2,1)S(1)}, u32[]{:S(2)}, u32[]{:S(2)}) collective-permute-start(bf16[512,256]{1,0:T(8,128)(2,1)S(1)} %get-tuple-element.84), channel_id=1, source_target_pairs={{0,4},{4,0},{8,12},{12,8},{1,5},{5,1},{9,13},{13,9},{2,6},{6,2},{1... | collective-permute-start | bytes 786440 | tf_op jit(solution)/shard_map/ppermute | solution.py:476
  52.4 6.0 %collective-permute-done.13.refs_1_ = bf16[512,256]{1,0:T(8,128)(2,1)S(1)} collective-permute-done((bf16[512,256]{1,0:T(8,128)(2,1)S(1)}, bf16[512,256]{1,0:T(8,128)(2,1)S(1)}, u32[]{:S(2)}, u32[]{:S(2)}) %collective-permute-start.13) | collective-permute-done | bytes 262176 | tf_op jit(solution)/shard_map/ppermute | solution.py:476
  58.8 2.0 %collective-permute-start.15 = (bf16[512,256]{1,0:T(8,128)(2,1)S(1)}, bf16[512,256]{1,0:T(8,128)(2,1)S(1)}, u32[]{:S(2)}, u32[]{:S(2)}) collective-permute-start(bf16[512,256]{1,0:T(8,128)(2,1)S(1)} %get-tuple-element.90), channel_id=1, source_target_pairs={{0,4},{4,0},{8,12},{12,8},{1,5},{5,1},{9,13},{13,9},{2,6},{6,2},{1... | collective-permute-start | bytes 786440 | tf_op jit(solution)/shard_map/ppermute | solution.py:476
  60.8 1.8 %shard_map.129 = (bf16[1024,512]{1,0:T(8,128)(2,1)S(1)}, bf16[1024,512]{1,0:T(8,128)(2,1)S(1)}) custom-call(s32[1]{0:T(128)} %bitcast.refs_4_.refs_0_, bf16[1024,256]{1,0:T(8,128)(2,1)S(1)} %get-tuple-element.70.refs_2_.refs_1_, bf16[1024,256]{1,0:T(8,128)(2,1)S(1)} %get-tuple-element.83.refs_1_.refs_2_, bf16[1024,256]{1,0:T(8,128)(2,1)S(1)} %get-tuple-element.85.refs_3_, ...), custom_call_target="tpu_custom_call" | custom-call | flops 1150000000 | bytes 1 | tf_op jit(solution)/shard_map/pallas_call | solution.py:42
  62.8 0.5 shard_map.131.refs_4_.refs_3_.refs_0_
  63.4 2.1 %collective-permute-start.20 = (bf16[512,256]{1,0:T(8,128)(2,1)S(1)}, bf16[512,256]{1,0:T(8,128)(2,1)S(1)}, u32[]{:S(2)}, u32[]{:S(2)}) collective-permute-start(bf16[512,256]{1,0:T(8,128)(2,1)S(1)} %get-tuple-element.96), channel_id=1, source_target_pairs={{0,4},{4,0},{8,12},{12,8},{1,5},{5,1},{9,13},{13,9},{2,6},{6,2},{1... | collective-permute-start | bytes 786440 | tf_op jit(solution)/shard_map/ppermute | solution.py:476
  65.5 2.5 %collective-permute-done.15.refs_1_.refs_4_ = bf16[512,256]{1,0:T(8,128)(2,1)S(1)} collective-permute-done((bf16[512,256]{1,0:T(8,128)(2,1)S(1)}, bf16[512,256]{1,0:T(8,128)(2,1)S(1)}, u32[]{:S(2)}, u32[]{:S(2)}) %collective-permute-start.15) | collective-permute-done | bytes 262176 | tf_op jit(solution)/shard_map/ppermute | solution.py:476
  68.2 0.6 collective-permute-start.17
  68.9 3.7 %collective-permute-start.18 = (bf16[512,256]{1,0:T(8,128)(2,1)S(1)}, bf16[512,256]{1,0:T(8,128)(2,1)S(1)}, u32[]{:S(2)}, u32[]{:S(2)}) collective-permute-start(bf16[512,256]{1,0:T(8,128)(2,1)S(1)} %get-tuple-element.94), channel_id=1, source_target_pairs={{0,4},{4,0},{8,12},{12,8},{1,5},{5,1},{9,13},{13,9},{2,6},{6,2},{1... | collective-permute-start | bytes 786440 | tf_op jit(solution)/shard_map/ppermute | solution.py:476
  72.5 0.9 shard_map.136
  73.5 0.5 shard_map.137.refs_2_.refs_3_.refs_0_
  74.3 3.6 %collective-permute-start.22 = (bf16[512,256]{1,0:T(8,128)(2,1)S(1)}, bf16[512,256]{1,0:T(8,128)(2,1)S(1)}, u32[]{:S(2)}, u32[]{:S(2)}) collective-permute-start(bf16[512,256]{1,0:T(8,128)(2,1)S(1)} %get-tuple-element.101), channel_id=1, source_target_pairs={{0,4},{4,0},{8,12},{12,8},{1,5},{5,1},{9,13},{13,9},{2,6},{6,2},{1... | collective-permute-start | bytes 786440 | tf_op jit(solution)/shard_map/ppermute | solution.py:476
  77.9 0.8 shard_map.140
  78.7 1.0 %collective-permute-done.18.refs_1_.refs_4_ = bf16[512,256]{1,0:T(8,128)(2,1)S(1)} collective-permute-done((bf16[512,256]{1,0:T(8,128)(2,1)S(1)}, bf16[512,256]{1,0:T(8,128)(2,1)S(1)}, u32[]{:S(2)}, u32[]{:S(2)}) %collective-permute-start.18) | collective-permute-done | bytes 262176 | tf_op jit(solution)/shard_map/ppermute | solution.py:476
  80.2 3.4 %collective-permute-start.25 = (bf16[512,256]{1,0:T(8,128)(2,1)S(1)}, bf16[512,256]{1,0:T(8,128)(2,1)S(1)}, u32[]{:S(2)}, u32[]{:S(2)}) collective-permute-start(bf16[512,256]{1,0:T(8,128)(2,1)S(1)} %shard_map.143.refs_2_), channel_id=1, source_target_pairs={{0,4},{4,0},{8,12},{12,8},{1,5},{5,1},{9,13},{13,9},{2,6},{6,2},{1... | collective-permute-start | bytes 786440 | tf_op jit(solution)/shard_map/ppermute | solution.py:476
  83.6 1.3 %collective-permute-start.21 = (bf16[1024,256]{1,0:T(8,128)(2,1)S(1)}, bf16[1024,256]{1,0:T(8,128)(2,1)S(1)}, u32[]{:S(2)}, u32[]{:S(2)}) collective-permute-start(bf16[1024,256]{1,0:T(8,128)(2,1)S(1)} %get-tuple-element.100), channel_id=1, source_target_pairs={{0,2},{1,3},{2,0},{3,1},{4,6},{5,7},{6,4},{7,5},{8,10},{9,11},{10,... | collective-permute-start | bytes 1572872 | tf_op jit(solution)/shard_map/ppermute | solution.py:476
  85.5 0.8 shard_map.145
  86.4 3.6 %collective-permute-start.27 = (bf16[512,256]{1,0:T(8,128)(2,1)S(1)}, bf16[512,256]{1,0:T(8,128)(2,1)S(1)}, u32[]{:S(2)}, u32[]{:S(2)}) collective-permute-start(bf16[512,256]{1,0:T(8,128)(2,1)S(1)} %shard_map.146.refs_5_.refs_1_), channel_id=1, source_target_pairs={{0,4},{4,0},{8,12},{12,8},{1,5},{5,1},{9,13},{13,9},{2,6},{6,2},{1... | collective-permute-start | bytes 786440 | tf_op jit(solution)/shard_map/ppermute | solution.py:476
  90.0 0.5 collective-permute-done.25.refs_4_
  90.6 0.8 shard_map.147
  91.5 2.4 %collective-permute-start.28 = (bf16[512,256]{1,0:T(8,128)(2,1)S(1)}, bf16[512,256]{1,0:T(8,128)(2,1)S(1)}, u32[]{:S(2)}, u32[]{:S(2)}) collective-permute-start(bf16[512,256]{1,0:T(8,128)(2,1)S(1)} %shard_map.148.refs_2_), channel_id=1, source_target_pairs={{0,4},{4,0},{8,12},{12,8},{1,5},{5,1},{9,13},{13,9},{2,6},{6,2},{1... | collective-permute-start | bytes 786440 | tf_op jit(solution)/shard_map/ppermute | solution.py:476
  93.9 1.5 %collective-permute-done.21.refs_1_ = bf16[1024,256]{1,0:T(8,128)(2,1)S(1)} collective-permute-done((bf16[1024,256]{1,0:T(8,128)(2,1)S(1)}, bf16[1024,256]{1,0:T(8,128)(2,1)S(1)}, u32[]{:S(2)}, u32[]{:S(2)}) %collective-permute-start.21) | collective-permute-done | bytes 524320 | tf_op jit(solution)/shard_map/ppermute | solution.py:476
  95.4 0.9 shard_map.149
  96.3 1.0 collective-permute-done.27.refs_3_
  97.3 4.1 %collective-permute-done.28.refs_4_ = bf16[512,256]{1,0:T(8,128)(2,1)S(1)} collective-permute-done((bf16[512,256]{1,0:T(8,128)(2,1)S(1)}, bf16[512,256]{1,0:T(8,128)(2,1)S(1)}, u32[]{:S(2)}, u32[]{:S(2)}) %collective-permute-start.28) | collective-permute-done | bytes 262176 | tf_op jit(solution)/shard_map/ppermute | solution.py:476
  101.3 0.8 shard_map.150
  (70 shorter events, 4.7 us)
Async XLA Ops:
  0.6 11.1 %copy-start = (bf16[1024,1024]{1,0:T(8,128)(2,1)S(1)}, bf16[1024,1024]{1,0:T(8,128)(2,1)}, u32[]{:S(2)}) copy-start(bf16[1024,1024]{1,0:T(8,128)(2,1)} %refs_1_.17) | copy-start | bytes 6291460
  0.7 11.1 %copy-start.3 = (bf16[1024,256]{1,0:T(8,128)(2,1)S(1)}, bf16[1024,256]{1,0:T(8,128)(2,1)}, u32[]{:S(2)}) copy-start(bf16[1024,256]{1,0:T(8,128)(2,1)} %refs_4_.3) | copy-start | bytes 1572868
  6.0 6.4 %copy-start.6 = (bf16[1024,512]{1,0:T(8,128)(2,1)S(1)}, bf16[1024,512]{1,0:T(8,128)(2,1)}, u32[]{:S(2)}) copy-start(bf16[1024,512]{1,0:T(8,128)(2,1)} %get-tuple-element.58.refs_1_.refs_3_.refs_5_) | copy-start | bytes 3145732
  6.0 6.4 %copy-start.7 = (bf16[512,512]{1,0:T(8,128)(2,1)S(1)}, bf16[512,512]{1,0:T(8,128)(2,1)}, u32[]{:S(2)}) copy-start(bf16[512,512]{1,0:T(8,128)(2,1)} %get-tuple-element.59.refs_2_.refs_4_.refs_6_) | copy-start | bytes 1572868
  6.0 6.4 %copy-start.8 = (bf16[256,512]{1,0:T(8,128)(2,1)S(1)}, bf16[256,512]{1,0:T(8,128)(2,1)}, u32[]{:S(2)}) copy-start(bf16[256,512]{1,0:T(8,128)(2,1)} %get-tuple-element.60.refs_3_.refs_5_.refs_7_) | copy-start | bytes 786436
  6.0 9.5 %collective-permute-start.1 = (bf16[64,512]{1,0:T(8,128)(2,1)}, bf16[64,512]{1,0:T(8,128)(2,1)S(1)}, u32[]{:S(2)}, u32[]{:S(2)}) collective-permute-start(bf16[64,512]{1,0:T(8,128)(2,1)} %get-tuple-element.64), channel_id=1, source_target_pairs={{0,8},{4,12},{8,0},{12,4},{1,9},{5,13},{9,1},{13,5},{2,10},{6,14},... | collective-permute-start | bytes 196616 | tf_op jit(solution)/shard_map/ppermute | solution.py:476
  10.1 7.0 %collective-permute-start.2 = (bf16[64,512]{1,0:T(8,128)(2,1)}, bf16[64,512]{1,0:T(8,128)(2,1)S(1)}, u32[]{:S(2)}, u32[]{:S(2)}) collective-permute-start(bf16[64,512]{1,0:T(8,128)(2,1)} %get-tuple-element.64), channel_id=1, source_target_pairs={{0,12},{4,8},{8,4},{12,0},{1,13},{5,9},{9,5},{13,1},{2,14},{6,10},... | collective-permute-start | bytes 196616 | tf_op jit(solution)/shard_map/ppermute | solution.py:476
  11.5 6.4 %collective-permute-start = (bf16[128,512]{1,0:T(8,128)(2,1)}, bf16[128,512]{1,0:T(8,128)(2,1)S(1)}, u32[]{:S(2)}, u32[]{:S(2)}) collective-permute-start(bf16[128,512]{1,0:T(8,128)(2,1)} %get-tuple-element.63), channel_id=1, source_target_pairs={{0,4},{4,0},{8,12},{12,8},{1,5},{5,1},{9,13},{13,9},{2,6},{6,2},{1... | collective-permute-start | bytes 393224 | tf_op jit(solution)/shard_map/ppermute | solution.py:476
  12.5 2.4 %copy-start.1 = (bf16[1024,1024]{1,0:T(8,128)(2,1)S(1)}, bf16[1024,1024]{1,0:T(8,128)(2,1)}, u32[]{:S(2)}) copy-start(bf16[1024,1024]{1,0:T(8,128)(2,1)} %refs_1_.13) | copy-start | bytes 6291460
  12.5 2.4 %copy-start.2 = (bf16[1024,256]{1,0:T(8,128)(2,1)S(1)}, bf16[1024,256]{1,0:T(8,128)(2,1)}, u32[]{:S(2)}) copy-start(bf16[1024,256]{1,0:T(8,128)(2,1)} %refs_2_.3) | copy-start | bytes 1572868
  22.8 9.9 %collective-permute-start.4 = (bf16[512,256]{1,0:T(8,128)(2,1)S(1)}, bf16[512,256]{1,0:T(8,128)(2,1)S(1)}, u32[]{:S(2)}, u32[]{:S(2)}) collective-permute-start(bf16[512,256]{1,0:T(8,128)(2,1)S(1)} %shard_map.114.refs_2_.refs_0_), channel_id=1, source_target_pairs={{0,4},{4,0},{8,12},{12,8},{1,5},{5,1},{9,13},{13,9},{2,6},{6,2},{1... | collective-permute-start | bytes 786440 | tf_op jit(solution)/shard_map/ppermute | solution.py:476
  24.5 13.5 %collective-permute-start.10 = (bf16[512,256]{1,0:T(8,128)(2,1)S(1)}, bf16[512,256]{1,0:T(8,128)(2,1)S(1)}, u32[]{:S(2)}, u32[]{:S(2)}) collective-permute-start(bf16[512,256]{1,0:T(8,128)(2,1)S(1)} %shard_map.115.refs_3_.refs_0_), channel_id=1, source_target_pairs={{0,4},{4,0},{8,12},{12,8},{1,5},{5,1},{9,13},{13,9},{2,6},{6,2},{1... | collective-permute-start | bytes 786440 | tf_op jit(solution)/shard_map/ppermute | solution.py:476
  25.7 7.6 %collective-permute-start.3 = (bf16[1024,512]{1,0:T(8,128)(2,1)S(1)}, bf16[1024,512]{1,0:T(8,128)(2,1)S(1)}, u32[]{:S(2)}, u32[]{:S(2)}) collective-permute-start(bf16[1024,512]{1,0:T(8,128)(2,1)S(1)} %get-tuple-element.68), channel_id=1, source_target_pairs={{0,1},{1,0},{2,3},{3,2},{4,5},{5,4},{6,7},{7,6},{8,9},{9,8},{10,11... | collective-permute-start | bytes 3145736 | tf_op jit(solution)/shard_map/ppermute | solution.py:476
  32.7 17.4 %collective-permute-start.6 = (bf16[512,256]{1,0:T(8,128)(2,1)S(1)}, bf16[512,256]{1,0:T(8,128)(2,1)S(1)}, u32[]{:S(2)}, u32[]{:S(2)}) collective-permute-start(bf16[512,256]{1,0:T(8,128)(2,1)S(1)} %shard_map.118.refs_2_.refs_1_), channel_id=1, source_target_pairs={{0,1},{1,0},{2,3},{3,2},{4,8},{5,9},{6,10},{7,11},{8,4},{9,5},{10,... | collective-permute-start | bytes 786440 | tf_op jit(solution)/shard_map/ppermute | solution.py:650
  33.6 14.4 %collective-permute-start.7 = (bf16[128,512]{1,0:T(8,128)(2,1)S(1)}, bf16[128,512]{1,0:T(8,128)(2,1)S(1)}, u32[]{:S(2)}, u32[]{:S(2)}) collective-permute-start(bf16[128,512]{1,0:T(8,128)(2,1)S(1)} %get-tuple-element.78.refs_2_), channel_id=1, source_target_pairs={{0,4},{4,0},{8,12},{12,8},{1,5},{5,1},{9,13},{13,9},{2,6},{6,2},{1... | collective-permute-start | bytes 393224 | tf_op jit(solution)/shard_map/ppermute | solution.py:476
  35.5 10.9 %collective-permute-start.8 = (bf16[64,512]{1,0:T(8,128)(2,1)S(1)}, bf16[64,512]{1,0:T(8,128)(2,1)S(1)}, u32[]{:S(2)}, u32[]{:S(2)}) collective-permute-start(bf16[64,512]{1,0:T(8,128)(2,1)S(1)} %get-tuple-element.79), channel_id=1, source_target_pairs={{0,8},{4,12},{8,0},{12,4},{1,9},{5,13},{9,1},{13,5},{2,10},{6,14},... | collective-permute-start | bytes 196616 | tf_op jit(solution)/shard_map/ppermute | solution.py:476
  37.4 10.6 %collective-permute-start.9 = (bf16[64,512]{1,0:T(8,128)(2,1)S(1)}, bf16[64,512]{1,0:T(8,128)(2,1)S(1)}, u32[]{:S(2)}, u32[]{:S(2)}) collective-permute-start(bf16[64,512]{1,0:T(8,128)(2,1)S(1)} %get-tuple-element.80), channel_id=1, source_target_pairs={{0,12},{4,8},{8,4},{12,0},{1,13},{5,9},{9,5},{13,1},{2,14},{6,10},... | collective-permute-start | bytes 196616 | tf_op jit(solution)/shard_map/ppermute | solution.py:476
  38.1 20.4 %collective-permute-start.12 = (bf16[512,256]{1,0:T(8,128)(2,1)S(1)}, bf16[512,256]{1,0:T(8,128)(2,1)S(1)}, u32[]{:S(2)}, u32[]{:S(2)}) collective-permute-start(bf16[512,256]{1,0:T(8,128)(2,1)S(1)} %shard_map.121.refs_4_.refs_1_), channel_id=1, source_target_pairs={{0,1},{1,0},{2,3},{3,2},{4,8},{5,9},{6,10},{7,11},{8,4},{9,5},{10,... | collective-permute-start | bytes 786440 | tf_op jit(solution)/shard_map/ppermute | solution.py:650
  46.5 26.1 %collective-permute-start.5 = (bf16[1024,256]{1,0:T(8,128)(2,1)S(1)}, bf16[1024,256]{1,0:T(8,128)(2,1)S(1)}, u32[]{:S(2)}, u32[]{:S(2)}) collective-permute-start(bf16[1024,256]{1,0:T(8,128)(2,1)S(1)} %get-tuple-element.72), channel_id=1, source_target_pairs={{0,2},{1,3},{2,0},{3,1},{4,6},{5,7},{6,4},{7,5},{8,10},{9,11},{10,... | collective-permute-start | bytes 1572872 | tf_op jit(solution)/shard_map/ppermute | solution.py:476
  49.0 9.3 %collective-permute-start.13 = (bf16[512,256]{1,0:T(8,128)(2,1)S(1)}, bf16[512,256]{1,0:T(8,128)(2,1)S(1)}, u32[]{:S(2)}, u32[]{:S(2)}) collective-permute-start(bf16[512,256]{1,0:T(8,128)(2,1)S(1)} %shard_map.123.refs_2_.refs_0_), channel_id=1, source_target_pairs={{0,4},{4,0},{8,12},{12,8},{1,5},{5,1},{9,13},{13,9},{2,6},{6,2},{1... | collective-permute-start | bytes 786440 | tf_op jit(solution)/shard_map/ppermute | solution.py:476
  50.2 12.4 %collective-permute-start.11 = (bf16[512,256]{1,0:T(8,128)(2,1)S(1)}, bf16[512,256]{1,0:T(8,128)(2,1)S(1)}, u32[]{:S(2)}, u32[]{:S(2)}) collective-permute-start(bf16[512,256]{1,0:T(8,128)(2,1)S(1)} %get-tuple-element.84), channel_id=1, source_target_pairs={{0,4},{4,0},{8,12},{12,8},{1,5},{5,1},{9,13},{13,9},{2,6},{6,2},{1... | collective-permute-start | bytes 786440 | tf_op jit(solution)/shard_map/ppermute | solution.py:476
  58.4 2.4 %copy-start.4 = (bf16[1024,256]{1,0:T(8,128)(2,1)S(1)}, bf16[1024,256]{1,0:T(8,128)(2,1)}, u32[]{:S(2)}) copy-start(bf16[1024,256]{1,0:T(8,128)(2,1)} %refs_5_.1) | copy-start | bytes 1572868
  58.4 2.4 %copy-start.5 = (bf16[1024,256]{1,0:T(8,128)(2,1)S(1)}, bf16[1024,256]{1,0:T(8,128)(2,1)}, u32[]{:S(2)}) copy-start(bf16[1024,256]{1,0:T(8,128)(2,1)} %refs_6_.1) | copy-start | bytes 1572868
  58.4 4.9 %collective-permute-start.16 = (bf16[512,256]{1,0:T(8,128)(2,1)S(1)}, bf16[512,256]{1,0:T(8,128)(2,1)S(1)}, u32[]{:S(2)}, u32[]{:S(2)}) collective-permute-start(bf16[512,256]{1,0:T(8,128)(2,1)S(1)} %shard_map.127.refs_4_.refs_1_), channel_id=1, source_target_pairs={{0,1},{1,0},{2,3},{3,2},{4,8},{5,9},{6,10},{7,11},{8,4},{9,5},{10,... | collective-permute-start | bytes 786440 | tf_op jit(solution)/shard_map/ppermute | solution.py:650
  58.8 9.2 %collective-permute-start.15 = (bf16[512,256]{1,0:T(8,128)(2,1)S(1)}, bf16[512,256]{1,0:T(8,128)(2,1)S(1)}, u32[]{:S(2)}, u32[]{:S(2)}) collective-permute-start(bf16[512,256]{1,0:T(8,128)(2,1)S(1)} %get-tuple-element.90), channel_id=1, source_target_pairs={{0,4},{4,0},{8,12},{12,8},{1,5},{5,1},{9,13},{13,9},{2,6},{6,2},{1... | collective-permute-start | bytes 786440 | tf_op jit(solution)/shard_map/ppermute | solution.py:476
  62.7 6.0 %collective-permute-start.14 = (bf16[512,256]{1,0:T(8,128)(2,1)S(1)}, bf16[512,256]{1,0:T(8,128)(2,1)S(1)}, u32[]{:S(2)}, u32[]{:S(2)}) collective-permute-start(bf16[512,256]{1,0:T(8,128)(2,1)S(1)} %shard_map.130.refs_2_.refs_1_), channel_id=1, source_target_pairs={{0,1},{1,0},{2,3},{3,2},{4,8},{5,9},{6,10},{7,11},{8,4},{9,5},{10,... | collective-permute-start | bytes 786440 | tf_op jit(solution)/shard_map/ppermute | solution.py:650
  63.4 10.5 %collective-permute-start.20 = (bf16[512,256]{1,0:T(8,128)(2,1)S(1)}, bf16[512,256]{1,0:T(8,128)(2,1)S(1)}, u32[]{:S(2)}, u32[]{:S(2)}) collective-permute-start(bf16[512,256]{1,0:T(8,128)(2,1)S(1)} %get-tuple-element.96), channel_id=1, source_target_pairs={{0,4},{4,0},{8,12},{12,8},{1,5},{5,1},{9,13},{13,9},{2,6},{6,2},{1... | collective-permute-start | bytes 786440 | tf_op jit(solution)/shard_map/ppermute | solution.py:476
  68.1 6.1 %collective-permute-start.19 = (bf16[512,256]{1,0:T(8,128)(2,1)S(1)}, bf16[512,256]{1,0:T(8,128)(2,1)S(1)}, u32[]{:S(2)}, u32[]{:S(2)}) collective-permute-start(bf16[512,256]{1,0:T(8,128)(2,1)S(1)} %shard_map.133.refs_1_), channel_id=1, source_target_pairs={{0,1},{1,0},{2,3},{3,2},{4,8},{5,9},{6,10},{7,11},{8,4},{9,5},{10,... | collective-permute-start | bytes 786440 | tf_op jit(solution)/shard_map/ppermute | solution.py:650
  68.2 11.7 %collective-permute-start.17 = (bf16[1024,512]{1,0:T(8,128)(2,1)S(1)}, bf16[1024,512]{1,0:T(8,128)(2,1)S(1)}, u32[]{:S(2)}, u32[]{:S(2)}) collective-permute-start(bf16[1024,512]{1,0:T(8,128)(2,1)S(1)} %shard_map.134.refs_4_), channel_id=1, source_target_pairs={{0,1},{1,0},{2,3},{3,2},{4,5},{5,4},{6,7},{7,6},{8,9},{9,8},{10,11... | collective-permute-start | bytes 3145736 | tf_op jit(solution)/shard_map/ppermute | solution.py:476
  68.9 10.9 %collective-permute-start.18 = (bf16[512,256]{1,0:T(8,128)(2,1)S(1)}, bf16[512,256]{1,0:T(8,128)(2,1)S(1)}, u32[]{:S(2)}, u32[]{:S(2)}) collective-permute-start(bf16[512,256]{1,0:T(8,128)(2,1)S(1)} %get-tuple-element.94), channel_id=1, source_target_pairs={{0,4},{4,0},{8,12},{12,8},{1,5},{5,1},{9,13},{13,9},{2,6},{6,2},{1... | collective-permute-start | bytes 786440 | tf_op jit(solution)/shard_map/ppermute | solution.py:476
  74.1 6.1 %collective-permute-start.23 = (bf16[512,256]{1,0:T(8,128)(2,1)S(1)}, bf16[512,256]{1,0:T(8,128)(2,1)S(1)}, u32[]{:S(2)}, u32[]{:S(2)}) collective-permute-start(bf16[512,256]{1,0:T(8,128)(2,1)S(1)} %shard_map.138.refs_4_.refs_0_), channel_id=1, source_target_pairs={{0,1},{1,0},{2,3},{3,2},{4,8},{5,9},{6,10},{7,11},{8,4},{9,5},{10,... | collective-permute-start | bytes 786440 | tf_op jit(solution)/shard_map/ppermute | solution.py:650
  74.3 11.1 %collective-permute-start.22 = (bf16[512,256]{1,0:T(8,128)(2,1)S(1)}, bf16[512,256]{1,0:T(8,128)(2,1)S(1)}, u32[]{:S(2)}, u32[]{:S(2)}) collective-permute-start(bf16[512,256]{1,0:T(8,128)(2,1)S(1)} %get-tuple-element.101), channel_id=1, source_target_pairs={{0,4},{4,0},{8,12},{12,8},{1,5},{5,1},{9,13},{13,9},{2,6},{6,2},{1... | collective-permute-start | bytes 786440 | tf_op jit(solution)/shard_map/ppermute | solution.py:476
  79.8 6.5 %collective-permute-start.26 = (bf16[512,256]{1,0:T(8,128)(2,1)S(1)}, bf16[512,256]{1,0:T(8,128)(2,1)S(1)}, u32[]{:S(2)}, u32[]{:S(2)}) collective-permute-start(bf16[512,256]{1,0:T(8,128)(2,1)S(1)} %shard_map.141.refs_2_.refs_0_), channel_id=1, source_target_pairs={{0,1},{1,0},{2,3},{3,2},{4,8},{5,9},{6,10},{7,11},{8,4},{9,5},{10,... | collective-permute-start | bytes 786440 | tf_op jit(solution)/shard_map/ppermute | solution.py:650
  80.2 10.3 %collective-permute-start.25 = (bf16[512,256]{1,0:T(8,128)(2,1)S(1)}, bf16[512,256]{1,0:T(8,128)(2,1)S(1)}, u32[]{:S(2)}, u32[]{:S(2)}) collective-permute-start(bf16[512,256]{1,0:T(8,128)(2,1)S(1)} %shard_map.143.refs_2_), channel_id=1, source_target_pairs={{0,4},{4,0},{8,12},{12,8},{1,5},{5,1},{9,13},{13,9},{2,6},{6,2},{1... | collective-permute-start | bytes 786440 | tf_op jit(solution)/shard_map/ppermute | solution.py:476
  83.6 11.7 %collective-permute-start.21 = (bf16[1024,256]{1,0:T(8,128)(2,1)S(1)}, bf16[1024,256]{1,0:T(8,128)(2,1)S(1)}, u32[]{:S(2)}, u32[]{:S(2)}) collective-permute-start(bf16[1024,256]{1,0:T(8,128)(2,1)S(1)} %get-tuple-element.100), channel_id=1, source_target_pairs={{0,2},{1,3},{2,0},{3,1},{4,6},{5,7},{6,4},{7,5},{8,10},{9,11},{10,... | collective-permute-start | bytes 1572872 | tf_op jit(solution)/shard_map/ppermute | solution.py:476
  85.4 6.0 %collective-permute-start.24 = (bf16[512,256]{1,0:T(8,128)(2,1)S(1)}, bf16[512,256]{1,0:T(8,128)(2,1)S(1)}, u32[]{:S(2)}, u32[]{:S(2)}) collective-permute-start(bf16[512,256]{1,0:T(8,128)(2,1)S(1)} %shard_map.144.refs_5_.refs_0_), channel_id=1, source_target_pairs={{0,1},{1,0},{2,3},{3,2},{4,8},{5,9},{6,10},{7,11},{8,4},{9,5},{10,... | collective-permute-start | bytes 786440 | tf_op jit(solution)/shard_map/ppermute | solution.py:650
  86.4 10.8 %collective-permute-start.27 = (bf16[512,256]{1,0:T(8,128)(2,1)S(1)}, bf16[512,256]{1,0:T(8,128)(2,1)S(1)}, u32[]{:S(2)}, u32[]{:S(2)}) collective-permute-start(bf16[512,256]{1,0:T(8,128)(2,1)S(1)} %shard_map.146.refs_5_.refs_1_), channel_id=1, source_target_pairs={{0,4},{4,0},{8,12},{12,8},{1,5},{5,1},{9,13},{13,9},{2,6},{6,2},{1... | collective-permute-start | bytes 786440 | tf_op jit(solution)/shard_map/ppermute | solution.py:476
  91.5 9.9 %collective-permute-start.28 = (bf16[512,256]{1,0:T(8,128)(2,1)S(1)}, bf16[512,256]{1,0:T(8,128)(2,1)S(1)}, u32[]{:S(2)}, u32[]{:S(2)}) collective-permute-start(bf16[512,256]{1,0:T(8,128)(2,1)S(1)} %shard_map.148.refs_2_), channel_id=1, source_target_pairs={{0,4},{4,0},{8,12},{12,8},{1,5},{5,1},{9,13},{13,9},{2,6},{6,2},{1... | collective-permute-start | bytes 786440 | tf_op jit(solution)/shard_map/ppermute | solution.py:476

commit v16 on v13

--- a/solution.py
+++ b/solution.py
@@ -717,14 +717,14 @@
     backs = [exchange(piece, "seq", d) for d, piece in enumerate(away, 1)]
     line.meet(rows)
     mixed.advance()
+    line.enter(step(relay, query_first))
+    dkey, dvalue, dkv_t = step(close_keys, dkv, backs, far_bits, local_levels)
     line.meet(rows)
-    dkey, dvalue, dkv_t = step(close_keys, dkv, backs, far_bits, local_levels)
-    line.enter(step(relay, query_first))
     key_first = step(weight_terms, dkv_t, tokens, inner, 0, 0, pieces)
     line.turn(query_second)
     key_second = step(weight_terms, dkv_t, tokens, inner, 0, 1, pieces)
+    line.turn(key_first)
     line.meet(rows)
-    line.turn(key_first)
     keep, send = step(project_split, rank, [dquery, dkey, dvalue], [w_query, w_key, w_value], "head")
     line.meet(rows)
     value_first = step(weight_terms, dkv_t, tokens, inner, 1, 0, pieces)

time: 98.4 us -> 99.6 us (1.012)
  starting transfers between devices: 35.7 us -> 53.6 us
  waiting for transfers between devices: 27.7 us -> 10.9 us
    ppermute x21, starting transfers between devices: 34.6 us -> 53.1 us  [exchange(): return lax.ppermute(block, axis, [(i, i ^ distance) for i in range(count)])]
    ppermute x21, waiting for transfers between devices: 27.7 us -> 10.9 us  [exchange(): return lax.ppermute(block, axis, [(i, i ^ distance) for i in range(count)])]
  transfers between devices with their start and end apart: 29 -> 29, of which waited for: 14 -> 7; matrix products, arithmetic and copies ran while one was open for 0% -> 0% of each run, Pallas kernels for 23% -> 23%
where the time goes in v16:
time: 99.6 us; the launch traced here: 99.4 us
  starting transfers between devices  53.6 us (54%)
  Pallas kernels  33.7 us (34%)
  waiting for transfers between devices  10.9 us (11%)
  between operations  1.15 us (1%)
    ppermute x21, starting transfers between devices, exchange(): return lax.ppermute(block, axis, [(i, i ^ distance) for i in range(count)])  53.1 us
    pallas_call x41, Pallas kernels, run(): return pl.pallas_call(kernel, in_specs=in_specs, **options)(*ready, *after)  33.7 us
    ppermute x21, waiting for transfers between devices, exchange(): return lax.ppermute(block, axis, [(i, i ^ distance) for i in range(count)])  10.9 us
  transfers between devices with their start and end apart: 29, of which 7 were waited for; matrix products, arithmetic and copies ran while one was open for 0% of the time, Pallas kernels for 23%

profile of v16, /device:TPU:0, one launch (start us, length us, event | category | flops | bytes accessed | tf_op | source)
XLA Modules:
  0.0 99.4 jit_solution(4464929540486827389)
XLA Ops:
  0.7 5.3 %shard_map.110 = (bf16[1024,512]{1,0:T(8,128)(2,1)}, bf16[512,512]{1,0:T(8,128)(2,1)}, bf16[256,512]{1,0:T(8,128)(2,1)}, bf16[128,512]{1,0:T(8,128)(2,1)}, bf16[64,512]{1,0:T(8,128)(2,1)}) custom-call(bf16[1024,1024]{1,0:T(8,128)(2,1)} %refs_1_.17, bf16[1024,256]{1,0:T(8,128)(2,1)} %refs_5_.1, bf16[1024,256]{1,0:T(8,128)(2,1)} %refs_6_.1, ...), custom_call_target="tpu_custom_call" | custom-call | flops 5750000128 | bytes 1 | tf_op jit(solution)/shard_map/pallas_call | solution.py:42
  6.0 4.1 %collective-permute-start.1 = (bf16[64,512]{1,0:T(8,128)(2,1)}, bf16[64,512]{1,0:T(8,128)(2,1)S(1)}, u32[]{:S(2)}, u32[]{:S(2)}) collective-permute-start(bf16[64,512]{1,0:T(8,128)(2,1)} %get-tuple-element.61), channel_id=1, source_target_pairs={{0,8},{4,12},{8,0},{12,4},{1,9},{5,13},{9,1},{13,5},{2,10},{6,14},... | collective-permute-start | bytes 196616 | tf_op jit(solution)/shard_map/ppermute | solution.py:476
  10.1 1.3 %collective-permute-start.2 = (bf16[64,512]{1,0:T(8,128)(2,1)}, bf16[64,512]{1,0:T(8,128)(2,1)S(1)}, u32[]{:S(2)}, u32[]{:S(2)}) collective-permute-start(bf16[64,512]{1,0:T(8,128)(2,1)} %get-tuple-element.61), channel_id=1, source_target_pairs={{0,12},{4,8},{8,4},{12,0},{1,13},{5,9},{9,5},{13,1},{2,14},{6,10},... | collective-permute-start | bytes 196616 | tf_op jit(solution)/shard_map/ppermute | solution.py:476
  11.7 0.7 shard_map.109.refs_0_.refs_4_
  12.5 2.3 %shard_map.111 = (f32[4096,256]{1,0:T(8,128)S(1)}, f32[4,1024]{1,0:T(4,128)S(1)}) custom-call(bf16[1024,256]{1,0:T(8,128)(2,1)S(1)} %shard_map.109.refs_0_.refs_4_, bf16[1024,512]{1,0:T(8,128)(2,1)S(1)} %copy-done.6, bf16[512,512]{1,0:T(8,128)(2,1)S(1)} %copy-done.7, bf16[256,512]{1,0:T(8,128)(2,1)S(1)} %copy-done.8, ...), custom_call_target="tpu_custom_call" | custom-call | flops 2644999936 | bytes 1 | tf_op jit(solution)/shard_map/pallas_call | solution.py:42
  14.9 0.7 shard_map.112.refs_9_.refs_1_
  15.6 1.5 %collective-permute-done.2.refs_8_.refs_10_ = bf16[64,512]{1,0:T(8,128)(2,1)S(1)} collective-permute-done((bf16[64,512]{1,0:T(8,128)(2,1)}, bf16[64,512]{1,0:T(8,128)(2,1)S(1)}, u32[]{:S(2)}, u32[]{:S(2)}) %collective-permute-start.2) | collective-permute-done | bytes 65568 | tf_op jit(solution)/shard_map/ppermute | solution.py:476
  17.1 0.8 collective-permute-done.refs_6_.refs_8_
  17.9 3.9 %shard_map.113 = (bf16[1024,256]{1,0:T(8,128)(2,1)S(1)}, bf16[256,1024]{1,0:T(8,128)(2,1)S(1)}, f32[4,1024]{1,0:T(4,128)S(1)}) custom-call(bf16[1024,256]{1,0:T(8,128)(2,1)S(1)} %shard_map.109.refs_0_.refs_4_, f32[4096,256]{1,0:T(8,128)S(1)} %get-tuple-element.58.refs_2_.refs_1_, f32[4,1024]{1,0:T(4,128)S(1)} %get-tuple-element.59.refs_2_, ...), custom_call_target="tpu_custom_call" | custom-call | flops 4600000000 | bytes 1 | tf_op jit(solution)/shard_map/pallas_call | solution.py:42
  21.8 0.5 shard_map.114.refs_2_.refs_0_
  22.3 0.5 shard_map.115.refs_3_.refs_0_
  22.8 1.0 collective-permute-start.4
  23.8 0.7 shard_map.116
  24.5 1.2 %collective-permute-start.10 = (bf16[512,256]{1,0:T(8,128)(2,1)S(1)}, bf16[512,256]{1,0:T(8,128)(2,1)S(1)}, u32[]{:S(2)}, u32[]{:S(2)}) collective-permute-start(bf16[512,256]{1,0:T(8,128)(2,1)S(1)} %shard_map.115.refs_3_.refs_0_), channel_id=1, source_target_pairs={{0,4},{4,0},{8,12},{12,8},{1,5},{5,1},{9,13},{13,9},{2,6},{6,2},{1... | collective-permute-start | bytes 786440 | tf_op jit(solution)/shard_map/ppermute | solution.py:476
  25.7 6.9 %shard_map.117 = (bf16[1024,256]{1,0:T(8,128)(2,1)S(1)}, f32[1024,512]{1,0:T(8,128)S(1)}, bf16[512,256]{1,0:T(8,128)(2,1)S(1)}, bf16[512,256]{1,0:T(8,128)(2,1)S...) custom-call(bf16[1024,256]{1,0:T(8,128)(2,1)S(1)} %shard_map.109.refs_0_.refs_4_, ...), custom_call_target="tpu_custom_call" | custom-call | flops 9200000000 | bytes 1 | tf_op jit(solution)/shard_map/pallas_call | solution.py:42
  32.7 1.0 collective-permute-start.7
  33.6 2.8 %collective-permute-start.8 = (bf16[64,512]{1,0:T(8,128)(2,1)S(1)}, bf16[64,512]{1,0:T(8,128)(2,1)S(1)}, u32[]{:S(2)}, u32[]{:S(2)}) collective-permute-start(bf16[64,512]{1,0:T(8,128)(2,1)S(1)} %get-tuple-element.73), channel_id=1, source_target_pairs={{0,8},{4,12},{8,0},{12,4},{1,9},{5,13},{9,1},{13,5},{2,10},{6,14},... | collective-permute-start | bytes 196616 | tf_op jit(solution)/shard_map/ppermute | solution.py:476
  36.5 0.6 collective-permute-start.9
  37.5 1.7 %collective-permute-done.8.refs_2_ = bf16[64,512]{1,0:T(8,128)(2,1)S(1)} collective-permute-done((bf16[64,512]{1,0:T(8,128)(2,1)S(1)}, bf16[64,512]{1,0:T(8,128)(2,1)S(1)}, u32[]{:S(2)}, u32[]{:S(2)}) %collective-permute-start.8) | collective-permute-done | bytes 65568 | tf_op jit(solution)/shard_map/ppermute | solution.py:476
  39.2 3.4 %collective-permute-start.12 = (bf16[512,256]{1,0:T(8,128)(2,1)S(1)}, bf16[512,256]{1,0:T(8,128)(2,1)S(1)}, u32[]{:S(2)}, u32[]{:S(2)}) collective-permute-start(bf16[512,256]{1,0:T(8,128)(2,1)S(1)} %shard_map.120.refs_4_.refs_0_), channel_id=1, source_target_pairs={{0,4},{4,0},{8,12},{12,8},{1,5},{5,1},{9,13},{13,9},{2,6},{6,2},{1... | collective-permute-start | bytes 786440 | tf_op jit(solution)/shard_map/ppermute | solution.py:476
  42.7 0.6 collective-permute-done.9.refs_3_
  43.3 1.0 %shard_map.121 = (bf16[1024,256]{1,0:T(8,128)(2,1)S(1)}, bf16[1024,256]{1,0:T(8,128)(2,1)S(1)}, bf16[512,1024]{1,0:T(8,128)(2,1)S(1)}) custom-call(f32[1024,512]{1,0:T(8,128)S(1)} %get-tuple-element.71.refs_0_, bf16[128,512]{1,0:T(8,128)(2,1)S(1)} %collective-permute-done.7.refs_1_, bf16[64,512]{1,0:T(8,128)(2,1)S(1)} %collective-permute-done.8.refs_2_, ...), custom_call_target="tpu_custom_call" | custom-call | flops 230000000 | bytes 1 | tf_op jit(solution)/shard_map/pallas_call | solution.py:42
  44.5 0.5 shard_map.123.refs_4_.refs_3_.refs_0_
  45.2 4.9 %collective-permute-start.11 = (bf16[512,256]{1,0:T(8,128)(2,1)S(1)}, bf16[512,256]{1,0:T(8,128)(2,1)S(1)}, u32[]{:S(2)}, u32[]{:S(2)}) collective-permute-start(bf16[512,256]{1,0:T(8,128)(2,1)S(1)} %get-tuple-element.78), channel_id=1, source_target_pairs={{0,4},{4,0},{8,12},{12,8},{1,5},{5,1},{9,13},{13,9},{2,6},{6,2},{1... | collective-permute-start | bytes 786440 | tf_op jit(solution)/shard_map/ppermute | solution.py:476
  50.1 1.5 %collective-permute-start.5 = (bf16[1024,256]{1,0:T(8,128)(2,1)S(1)}, bf16[1024,256]{1,0:T(8,128)(2,1)S(1)}, u32[]{:S(2)}, u32[]{:S(2)}) collective-permute-start(bf16[1024,256]{1,0:T(8,128)(2,1)S(1)} %get-tuple-element.69), channel_id=1, source_target_pairs={{0,2},{1,3},{2,0},{3,1},{4,6},{5,7},{6,4},{7,5},{8,10},{9,11},{10,... | collective-permute-start | bytes 1572872 | tf_op jit(solution)/shard_map/ppermute | solution.py:476
  51.6 0.5 shard_map.125.refs_4_.refs_3_.refs_0_
  52.1 0.3 shard_map.126
  52.6 4.5 %collective-permute-start.15 = (bf16[512,256]{1,0:T(8,128)(2,1)S(1)}, bf16[512,256]{1,0:T(8,128)(2,1)S(1)}, u32[]{:S(2)}, u32[]{:S(2)}) collective-permute-start(bf16[512,256]{1,0:T(8,128)(2,1)S(1)} %get-tuple-element.84), channel_id=1, source_target_pairs={{0,4},{4,0},{8,12},{12,8},{1,5},{5,1},{9,13},{13,9},{2,6},{6,2},{1... | collective-permute-start | bytes 786440 | tf_op jit(solution)/shard_map/ppermute | solution.py:476
  57.0 1.8 %shard_map.128 = (bf16[1024,512]{1,0:T(8,128)(2,1)S(1)}, bf16[1024,512]{1,0:T(8,128)(2,1)S(1)}) custom-call(s32[1]{0:T(128)} %bitcast.refs_4_.refs_0_, bf16[1024,256]{1,0:T(8,128)(2,1)S(1)} %get-tuple-element.67.refs_2_.refs_1_, bf16[1024,256]{1,0:T(8,128)(2,1)S(1)} %get-tuple-element.77.refs_2_, bf16[1024,256]{1,0:T(8,128)(2,1)S(1)} %get-tuple-element.79.refs_3_, ...), custom_call_target="tpu_custom_call" | custom-call | flops 1150000000 | bytes 1 | tf_op jit(solution)/shard_map/pallas_call | solution.py:42
  59.0 0.5 shard_map.130.refs_4_.refs_3_.refs_0_
  59.7 5.2 %collective-permute-start.20 = (bf16[512,256]{1,0:T(8,128)(2,1)S(1)}, bf16[512,256]{1,0:T(8,128)(2,1)S(1)}, u32[]{:S(2)}, u32[]{:S(2)}) collective-permute-start(bf16[512,256]{1,0:T(8,128)(2,1)S(1)} %get-tuple-element.90), channel_id=1, source_target_pairs={{0,4},{4,0},{8,12},{12,8},{1,5},{5,1},{9,13},{13,9},{2,6},{6,2},{1... | collective-permute-start | bytes 786440 | tf_op jit(solution)/shard_map/ppermute | solution.py:476
  65.1 0.6 collective-permute-start.17
  65.7 4.7 %collective-permute-start.18 = (bf16[512,256]{1,0:T(8,128)(2,1)S(1)}, bf16[512,256]{1,0:T(8,128)(2,1)S(1)}, u32[]{:S(2)}, u32[]{:S(2)}) collective-permute-start(bf16[512,256]{1,0:T(8,128)(2,1)S(1)} %get-tuple-element.88), channel_id=1, source_target_pairs={{0,4},{4,0},{8,12},{12,8},{1,5},{5,1},{9,13},{13,9},{2,6},{6,2},{1... | collective-permute-start | bytes 786440 | tf_op jit(solution)/shard_map/ppermute | solution.py:476
  70.5 0.9 shard_map.135
  71.4 0.5 shard_map.136.refs_2_.refs_3_.refs_0_
  72.2 3.9 %collective-permute-start.22 = (bf16[512,256]{1,0:T(8,128)(2,1)S(1)}, bf16[512,256]{1,0:T(8,128)(2,1)S(1)}, u32[]{:S(2)}, u32[]{:S(2)}) collective-permute-start(bf16[512,256]{1,0:T(8,128)(2,1)S(1)} %get-tuple-element.95), channel_id=1, source_target_pairs={{0,4},{4,0},{8,12},{12,8},{1,5},{5,1},{9,13},{13,9},{2,6},{6,2},{1... | collective-permute-start | bytes 786440 | tf_op jit(solution)/shard_map/ppermute | solution.py:476
  76.1 0.8 shard_map.139
  77.4 4.3 %collective-permute-start.25 = (bf16[512,256]{1,0:T(8,128)(2,1)S(1)}, bf16[512,256]{1,0:T(8,128)(2,1)S(1)}, u32[]{:S(2)}, u32[]{:S(2)}) collective-permute-start(bf16[512,256]{1,0:T(8,128)(2,1)S(1)} %shard_map.142.refs_2_), channel_id=1, source_target_pairs={{0,4},{4,0},{8,12},{12,8},{1,5},{5,1},{9,13},{13,9},{2,6},{6,2},{1... | collective-permute-start | bytes 786440 | tf_op jit(solution)/shard_map/ppermute | solution.py:476
  81.7 1.5 %collective-permute-start.21 = (bf16[1024,256]{1,0:T(8,128)(2,1)S(1)}, bf16[1024,256]{1,0:T(8,128)(2,1)S(1)}, u32[]{:S(2)}, u32[]{:S(2)}) collective-permute-start(bf16[1024,256]{1,0:T(8,128)(2,1)S(1)} %get-tuple-element.94), channel_id=1, source_target_pairs={{0,2},{1,3},{2,0},{3,1},{4,6},{5,7},{6,4},{7,5},{8,10},{9,11},{10,... | collective-permute-start | bytes 1572872 | tf_op jit(solution)/shard_map/ppermute | solution.py:476
  83.3 0.8 shard_map.144
  84.2 3.1 %collective-permute-start.27 = (bf16[512,256]{1,0:T(8,128)(2,1)S(1)}, bf16[512,256]{1,0:T(8,128)(2,1)S(1)}, u32[]{:S(2)}, u32[]{:S(2)}) collective-permute-start(bf16[512,256]{1,0:T(8,128)(2,1)S(1)} %shard_map.145.refs_5_.refs_1_), channel_id=1, source_target_pairs={{0,4},{4,0},{8,12},{12,8},{1,5},{5,1},{9,13},{13,9},{2,6},{6,2},{1... | collective-permute-start | bytes 786440 | tf_op jit(solution)/shard_map/ppermute | solution.py:476
  87.3 0.8 shard_map.146
  88.2 3.3 %collective-permute-start.28 = (bf16[512,256]{1,0:T(8,128)(2,1)S(1)}, bf16[512,256]{1,0:T(8,128)(2,1)S(1)}, u32[]{:S(2)}, u32[]{:S(2)}) collective-permute-start(bf16[512,256]{1,0:T(8,128)(2,1)S(1)} %shard_map.147.refs_2_), channel_id=1, source_target_pairs={{0,4},{4,0},{8,12},{12,8},{1,5},{5,1},{9,13},{13,9},{2,6},{6,2},{1... | collective-permute-start | bytes 786440 | tf_op jit(solution)/shard_map/ppermute | solution.py:476
  91.5 1.0 collective-permute-done.21.refs_1_
  92.4 0.9 shard_map.148
  93.4 1.1 %collective-permute-done.27.refs_3_ = bf16[512,256]{1,0:T(8,128)(2,1)S(1)} collective-permute-done((bf16[512,256]{1,0:T(8,128)(2,1)S(1)}, bf16[512,256]{1,0:T(8,128)(2,1)S(1)}, u32[]{:S(2)}, u32[]{:S(2)}) %collective-permute-start.27) | collective-permute-done | bytes 262176 | tf_op jit(solution)/shard_map/ppermute | solution.py:476
  94.5 4.1 %collective-permute-done.28.refs_4_ = bf16[512,256]{1,0:T(8,128)(2,1)S(1)} collective-permute-done((bf16[512,256]{1,0:T(8,128)(2,1)S(1)}, bf16[512,256]{1,0:T(8,128)(2,1)S(1)}, u32[]{:S(2)}, u32[]{:S(2)}) %collective-permute-start.28) | collective-permute-done | bytes 262176 | tf_op jit(solution)/shard_map/ppermute | solution.py:476
  98.6 0.8 shard_map.149
  (69 shorter events, 2.6 us)
Async XLA Ops:
  0.6 11.1 %copy-start = (bf16[1024,1024]{1,0:T(8,128)(2,1)S(1)}, bf16[1024,1024]{1,0:T(8,128)(2,1)}, u32[]{:S(2)}) copy-start(bf16[1024,1024]{1,0:T(8,128)(2,1)} %refs_1_.17) | copy-start | bytes 6291460
  0.7 11.1 %copy-start.3 = (bf16[1024,256]{1,0:T(8,128)(2,1)S(1)}, bf16[1024,256]{1,0:T(8,128)(2,1)}, u32[]{:S(2)}) copy-start(bf16[1024,256]{1,0:T(8,128)(2,1)} %refs_4_.3) | copy-start | bytes 1572868
  6.0 6.4 %copy-start.6 = (bf16[1024,512]{1,0:T(8,128)(2,1)S(1)}, bf16[1024,512]{1,0:T(8,128)(2,1)}, u32[]{:S(2)}) copy-start(bf16[1024,512]{1,0:T(8,128)(2,1)} %get-tuple-element.55.refs_1_.refs_3_.refs_5_) | copy-start | bytes 3145732
  6.0 6.4 %copy-start.7 = (bf16[512,512]{1,0:T(8,128)(2,1)S(1)}, bf16[512,512]{1,0:T(8,128)(2,1)}, u32[]{:S(2)}) copy-start(bf16[512,512]{1,0:T(8,128)(2,1)} %get-tuple-element.56.refs_2_.refs_4_.refs_6_) | copy-start | bytes 1572868
  6.0 6.4 %copy-start.8 = (bf16[256,512]{1,0:T(8,128)(2,1)S(1)}, bf16[256,512]{1,0:T(8,128)(2,1)}, u32[]{:S(2)}) copy-start(bf16[256,512]{1,0:T(8,128)(2,1)} %get-tuple-element.57.refs_3_.refs_5_.refs_7_) | copy-start | bytes 786436
  6.0 9.5 %collective-permute-start.1 = (bf16[64,512]{1,0:T(8,128)(2,1)}, bf16[64,512]{1,0:T(8,128)(2,1)S(1)}, u32[]{:S(2)}, u32[]{:S(2)}) collective-permute-start(bf16[64,512]{1,0:T(8,128)(2,1)} %get-tuple-element.61), channel_id=1, source_target_pairs={{0,8},{4,12},{8,0},{12,4},{1,9},{5,13},{9,1},{13,5},{2,10},{6,14},... | collective-permute-start | bytes 196616 | tf_op jit(solution)/shard_map/ppermute | solution.py:476
  10.1 7.0 %collective-permute-start.2 = (bf16[64,512]{1,0:T(8,128)(2,1)}, bf16[64,512]{1,0:T(8,128)(2,1)S(1)}, u32[]{:S(2)}, u32[]{:S(2)}) collective-permute-start(bf16[64,512]{1,0:T(8,128)(2,1)} %get-tuple-element.61), channel_id=1, source_target_pairs={{0,12},{4,8},{8,4},{12,0},{1,13},{5,9},{9,5},{13,1},{2,14},{6,10},... | collective-permute-start | bytes 196616 | tf_op jit(solution)/shard_map/ppermute | solution.py:476
  11.5 6.4 %collective-permute-start = (bf16[128,512]{1,0:T(8,128)(2,1)}, bf16[128,512]{1,0:T(8,128)(2,1)S(1)}, u32[]{:S(2)}, u32[]{:S(2)}) collective-permute-start(bf16[128,512]{1,0:T(8,128)(2,1)} %get-tuple-element.60), channel_id=1, source_target_pairs={{0,4},{4,0},{8,12},{12,8},{1,5},{5,1},{9,13},{13,9},{2,6},{6,2},{1... | collective-permute-start | bytes 393224 | tf_op jit(solution)/shard_map/ppermute | solution.py:476
  12.5 2.4 %copy-start.1 = (bf16[1024,1024]{1,0:T(8,128)(2,1)S(1)}, bf16[1024,1024]{1,0:T(8,128)(2,1)}, u32[]{:S(2)}) copy-start(bf16[1024,1024]{1,0:T(8,128)(2,1)} %refs_1_.13) | copy-start | bytes 6291460
  12.5 2.4 %copy-start.2 = (bf16[1024,256]{1,0:T(8,128)(2,1)S(1)}, bf16[1024,256]{1,0:T(8,128)(2,1)}, u32[]{:S(2)}) copy-start(bf16[1024,256]{1,0:T(8,128)(2,1)} %refs_2_.3) | copy-start | bytes 1572868
  22.8 13.7 %collective-permute-start.4 = (bf16[512,256]{1,0:T(8,128)(2,1)S(1)}, bf16[512,256]{1,0:T(8,128)(2,1)S(1)}, u32[]{:S(2)}, u32[]{:S(2)}) collective-permute-start(bf16[512,256]{1,0:T(8,128)(2,1)S(1)} %shard_map.114.refs_2_.refs_0_), channel_id=1, source_target_pairs={{0,4},{4,0},{8,12},{12,8},{1,5},{5,1},{9,13},{13,9},{2,6},{6,2},{1... | collective-permute-start | bytes 786440 | tf_op jit(solution)/shard_map/ppermute | solution.py:476
  24.5 19.8 %collective-permute-start.10 = (bf16[512,256]{1,0:T(8,128)(2,1)S(1)}, bf16[512,256]{1,0:T(8,128)(2,1)S(1)}, u32[]{:S(2)}, u32[]{:S(2)}) collective-permute-start(bf16[512,256]{1,0:T(8,128)(2,1)S(1)} %shard_map.115.refs_3_.refs_0_), channel_id=1, source_target_pairs={{0,4},{4,0},{8,12},{12,8},{1,5},{5,1},{9,13},{13,9},{2,6},{6,2},{1... | collective-permute-start | bytes 786440 | tf_op jit(solution)/shard_map/ppermute | solution.py:476
  25.7 11.5 %collective-permute-start.3 = (bf16[1024,512]{1,0:T(8,128)(2,1)S(1)}, bf16[1024,512]{1,0:T(8,128)(2,1)S(1)}, u32[]{:S(2)}, u32[]{:S(2)}) collective-permute-start(bf16[1024,512]{1,0:T(8,128)(2,1)S(1)} %get-tuple-element.65), channel_id=1, source_target_pairs={{0,1},{1,0},{2,3},{3,2},{4,5},{5,4},{6,7},{7,6},{8,9},{9,8},{10,11... | collective-permute-start | bytes 3145736 | tf_op jit(solution)/shard_map/ppermute | solution.py:476
  32.7 10.7 %collective-permute-start.7 = (bf16[128,512]{1,0:T(8,128)(2,1)S(1)}, bf16[128,512]{1,0:T(8,128)(2,1)S(1)}, u32[]{:S(2)}, u32[]{:S(2)}) collective-permute-start(bf16[128,512]{1,0:T(8,128)(2,1)S(1)} %get-tuple-element.72), channel_id=1, source_target_pairs={{0,4},{4,0},{8,12},{12,8},{1,5},{5,1},{9,13},{13,9},{2,6},{6,2},{1... | collective-permute-start | bytes 393224 | tf_op jit(solution)/shard_map/ppermute | solution.py:476
  33.6 5.6 %collective-permute-start.8 = (bf16[64,512]{1,0:T(8,128)(2,1)S(1)}, bf16[64,512]{1,0:T(8,128)(2,1)S(1)}, u32[]{:S(2)}, u32[]{:S(2)}) collective-permute-start(bf16[64,512]{1,0:T(8,128)(2,1)S(1)} %get-tuple-element.73), channel_id=1, source_target_pairs={{0,8},{4,12},{8,0},{12,4},{1,9},{5,13},{9,1},{13,5},{2,10},{6,14},... | collective-permute-start | bytes 196616 | tf_op jit(solution)/shard_map/ppermute | solution.py:476
  36.5 6.8 %collective-permute-start.9 = (bf16[64,512]{1,0:T(8,128)(2,1)S(1)}, bf16[64,512]{1,0:T(8,128)(2,1)S(1)}, u32[]{:S(2)}, u32[]{:S(2)}) collective-permute-start(bf16[64,512]{1,0:T(8,128)(2,1)S(1)} %get-tuple-element.74), channel_id=1, source_target_pairs={{0,12},{4,8},{8,4},{12,0},{1,13},{5,9},{9,5},{13,1},{2,14},{6,10},... | collective-permute-start | bytes 196616 | tf_op jit(solution)/shard_map/ppermute | solution.py:476
  37.2 7.9 %collective-permute-start.6 = (bf16[512,256]{1,0:T(8,128)(2,1)S(1)}, bf16[512,256]{1,0:T(8,128)(2,1)S(1)}, u32[]{:S(2)}, u32[]{:S(2)}) collective-permute-start(bf16[512,256]{1,0:T(8,128)(2,1)S(1)} %shard_map.118.refs_2_.refs_1_), channel_id=1, source_target_pairs={{0,1},{1,0},{2,3},{3,2},{4,8},{5,9},{6,10},{7,11},{8,4},{9,5},{10,... | collective-permute-start | bytes 786440 | tf_op jit(solution)/shard_map/ppermute | solution.py:633
  39.2 13.2 %collective-permute-start.12 = (bf16[512,256]{1,0:T(8,128)(2,1)S(1)}, bf16[512,256]{1,0:T(8,128)(2,1)S(1)}, u32[]{:S(2)}, u32[]{:S(2)}) collective-permute-start(bf16[512,256]{1,0:T(8,128)(2,1)S(1)} %shard_map.120.refs_4_.refs_0_), channel_id=1, source_target_pairs={{0,4},{4,0},{8,12},{12,8},{1,5},{5,1},{9,13},{13,9},{2,6},{6,2},{1... | collective-permute-start | bytes 786440 | tf_op jit(solution)/shard_map/ppermute | solution.py:476
  44.4 7.7 %collective-permute-start.13 = (bf16[512,256]{1,0:T(8,128)(2,1)S(1)}, bf16[512,256]{1,0:T(8,128)(2,1)S(1)}, u32[]{:S(2)}, u32[]{:S(2)}) collective-permute-start(bf16[512,256]{1,0:T(8,128)(2,1)S(1)} %shard_map.122.refs_2_.refs_1_), channel_id=1, source_target_pairs={{0,1},{1,0},{2,3},{3,2},{4,8},{5,9},{6,10},{7,11},{8,4},{9,5},{10,... | collective-permute-start | bytes 786440 | tf_op jit(solution)/shard_map/ppermute | solution.py:633
  45.2 13.7 %collective-permute-start.11 = (bf16[512,256]{1,0:T(8,128)(2,1)S(1)}, bf16[512,256]{1,0:T(8,128)(2,1)S(1)}, u32[]{:S(2)}, u32[]{:S(2)}) collective-permute-start(bf16[512,256]{1,0:T(8,128)(2,1)S(1)} %get-tuple-element.78), channel_id=1, source_target_pairs={{0,4},{4,0},{8,12},{12,8},{1,5},{5,1},{9,13},{13,9},{2,6},{6,2},{1... | collective-permute-start | bytes 786440 | tf_op jit(solution)/shard_map/ppermute | solution.py:476
  50.1 20.4 %collective-permute-start.5 = (bf16[1024,256]{1,0:T(8,128)(2,1)S(1)}, bf16[1024,256]{1,0:T(8,128)(2,1)S(1)}, u32[]{:S(2)}, u32[]{:S(2)}) collective-permute-start(bf16[1024,256]{1,0:T(8,128)(2,1)S(1)} %get-tuple-element.69), channel_id=1, source_target_pairs={{0,2},{1,3},{2,0},{3,1},{4,6},{5,7},{6,4},{7,5},{8,10},{9,11},{10,... | collective-permute-start | bytes 1572872 | tf_op jit(solution)/shard_map/ppermute | solution.py:476
  52.4 4.6 %copy-start.4 = (bf16[1024,256]{1,0:T(8,128)(2,1)S(1)}, bf16[1024,256]{1,0:T(8,128)(2,1)}, u32[]{:S(2)}) copy-start(bf16[1024,256]{1,0:T(8,128)(2,1)} %refs_5_.1) | copy-start | bytes 1572868
  52.4 4.6 %copy-start.5 = (bf16[1024,256]{1,0:T(8,128)(2,1)S(1)}, bf16[1024,256]{1,0:T(8,128)(2,1)}, u32[]{:S(2)}) copy-start(bf16[1024,256]{1,0:T(8,128)(2,1)} %refs_6_.1) | copy-start | bytes 1572868
  52.5 7.1 %collective-permute-start.16 = (bf16[512,256]{1,0:T(8,128)(2,1)S(1)}, bf16[512,256]{1,0:T(8,128)(2,1)S(1)}, u32[]{:S(2)}, u32[]{:S(2)}) collective-permute-start(bf16[512,256]{1,0:T(8,128)(2,1)S(1)} %shard_map.127.refs_7_.refs_1_), channel_id=1, source_target_pairs={{0,1},{1,0},{2,3},{3,2},{4,8},{5,9},{6,10},{7,11},{8,4},{9,5},{10,... | collective-permute-start | bytes 786440 | tf_op jit(solution)/shard_map/ppermute | solution.py:633
  52.6 12.3 %collective-permute-start.15 = (bf16[512,256]{1,0:T(8,128)(2,1)S(1)}, bf16[512,256]{1,0:T(8,128)(2,1)S(1)}, u32[]{:S(2)}, u32[]{:S(2)}) collective-permute-start(bf16[512,256]{1,0:T(8,128)(2,1)S(1)} %get-tuple-element.84), channel_id=1, source_target_pairs={{0,4},{4,0},{8,12},{12,8},{1,5},{5,1},{9,13},{13,9},{2,6},{6,2},{1... | collective-permute-start | bytes 786440 | tf_op jit(solution)/shard_map/ppermute | solution.py:476
  59.0 6.7 %collective-permute-start.14 = (bf16[512,256]{1,0:T(8,128)(2,1)S(1)}, bf16[512,256]{1,0:T(8,128)(2,1)S(1)}, u32[]{:S(2)}, u32[]{:S(2)}) collective-permute-start(bf16[512,256]{1,0:T(8,128)(2,1)S(1)} %shard_map.129.refs_2_.refs_1_), channel_id=1, source_target_pairs={{0,1},{1,0},{2,3},{3,2},{4,8},{5,9},{6,10},{7,11},{8,4},{9,5},{10,... | collective-permute-start | bytes 786440 | tf_op jit(solution)/shard_map/ppermute | solution.py:633
  59.7 12.2 %collective-permute-start.20 = (bf16[512,256]{1,0:T(8,128)(2,1)S(1)}, bf16[512,256]{1,0:T(8,128)(2,1)S(1)}, u32[]{:S(2)}, u32[]{:S(2)}) collective-permute-start(bf16[512,256]{1,0:T(8,128)(2,1)S(1)} %get-tuple-element.90), channel_id=1, source_target_pairs={{0,4},{4,0},{8,12},{12,8},{1,5},{5,1},{9,13},{13,9},{2,6},{6,2},{1... | collective-permute-start | bytes 786440 | tf_op jit(solution)/shard_map/ppermute | solution.py:476
  64.9 7.2 %collective-permute-start.19 = (bf16[512,256]{1,0:T(8,128)(2,1)S(1)}, bf16[512,256]{1,0:T(8,128)(2,1)S(1)}, u32[]{:S(2)}, u32[]{:S(2)}) collective-permute-start(bf16[512,256]{1,0:T(8,128)(2,1)S(1)} %shard_map.132.refs_1_), channel_id=1, source_target_pairs={{0,1},{1,0},{2,3},{3,2},{4,8},{5,9},{6,10},{7,11},{8,4},{9,5},{10,... | collective-permute-start | bytes 786440 | tf_op jit(solution)/shard_map/ppermute | solution.py:633
  65.1 12.0 %collective-permute-start.17 = (bf16[1024,512]{1,0:T(8,128)(2,1)S(1)}, bf16[1024,512]{1,0:T(8,128)(2,1)S(1)}, u32[]{:S(2)}, u32[]{:S(2)}) collective-permute-start(bf16[1024,512]{1,0:T(8,128)(2,1)S(1)} %shard_map.133.refs_4_), channel_id=1, source_target_pairs={{0,1},{1,0},{2,3},{3,2},{4,5},{5,4},{6,7},{7,6},{8,9},{9,8},{10,11... | collective-permute-start | bytes 3145736 | tf_op jit(solution)/shard_map/ppermute | solution.py:476
  65.7 11.2 %collective-permute-start.18 = (bf16[512,256]{1,0:T(8,128)(2,1)S(1)}, bf16[512,256]{1,0:T(8,128)(2,1)S(1)}, u32[]{:S(2)}, u32[]{:S(2)}) collective-permute-start(bf16[512,256]{1,0:T(8,128)(2,1)S(1)} %get-tuple-element.88), channel_id=1, source_target_pairs={{0,4},{4,0},{8,12},{12,8},{1,5},{5,1},{9,13},{13,9},{2,6},{6,2},{1... | collective-permute-start | bytes 786440 | tf_op jit(solution)/shard_map/ppermute | solution.py:476
  72.0 5.3 %collective-permute-start.23 = (bf16[512,256]{1,0:T(8,128)(2,1)S(1)}, bf16[512,256]{1,0:T(8,128)(2,1)S(1)}, u32[]{:S(2)}, u32[]{:S(2)}) collective-permute-start(bf16[512,256]{1,0:T(8,128)(2,1)S(1)} %shard_map.137.refs_4_.refs_0_), channel_id=1, source_target_pairs={{0,1},{1,0},{2,3},{3,2},{4,8},{5,9},{6,10},{7,11},{8,4},{9,5},{10,... | collective-permute-start | bytes 786440 | tf_op jit(solution)/shard_map/ppermute | solution.py:633
  72.2 11.0 %collective-permute-start.22 = (bf16[512,256]{1,0:T(8,128)(2,1)S(1)}, bf16[512,256]{1,0:T(8,128)(2,1)S(1)}, u32[]{:S(2)}, u32[]{:S(2)}) collective-permute-start(bf16[512,256]{1,0:T(8,128)(2,1)S(1)} %get-tuple-element.95), channel_id=1, source_target_pairs={{0,4},{4,0},{8,12},{12,8},{1,5},{5,1},{9,13},{13,9},{2,6},{6,2},{1... | collective-permute-start | bytes 786440 | tf_op jit(solution)/shard_map/ppermute | solution.py:476
  77.0 7.2 %collective-permute-start.26 = (bf16[512,256]{1,0:T(8,128)(2,1)S(1)}, bf16[512,256]{1,0:T(8,128)(2,1)S(1)}, u32[]{:S(2)}, u32[]{:S(2)}) collective-permute-start(bf16[512,256]{1,0:T(8,128)(2,1)S(1)} %shard_map.140.refs_2_.refs_0_), channel_id=1, source_target_pairs={{0,1},{1,0},{2,3},{3,2},{4,8},{5,9},{6,10},{7,11},{8,4},{9,5},{10,... | collective-permute-start | bytes 786440 | tf_op jit(solution)/shard_map/ppermute | solution.py:633
  77.4 9.9 %collective-permute-start.25 = (bf16[512,256]{1,0:T(8,128)(2,1)S(1)}, bf16[512,256]{1,0:T(8,128)(2,1)S(1)}, u32[]{:S(2)}, u32[]{:S(2)}) collective-permute-start(bf16[512,256]{1,0:T(8,128)(2,1)S(1)} %shard_map.142.refs_2_), channel_id=1, source_target_pairs={{0,4},{4,0},{8,12},{12,8},{1,5},{5,1},{9,13},{13,9},{2,6},{6,2},{1... | collective-permute-start | bytes 786440 | tf_op jit(solution)/shard_map/ppermute | solution.py:476
  81.7 10.8 %collective-permute-start.21 = (bf16[1024,256]{1,0:T(8,128)(2,1)S(1)}, bf16[1024,256]{1,0:T(8,128)(2,1)S(1)}, u32[]{:S(2)}, u32[]{:S(2)}) collective-permute-start(bf16[1024,256]{1,0:T(8,128)(2,1)S(1)} %get-tuple-element.94), channel_id=1, source_target_pairs={{0,2},{1,3},{2,0},{3,1},{4,6},{5,7},{6,4},{7,5},{8,10},{9,11},{10,... | collective-permute-start | bytes 1572872 | tf_op jit(solution)/shard_map/ppermute | solution.py:476
  83.2 4.9 %collective-permute-start.24 = (bf16[512,256]{1,0:T(8,128)(2,1)S(1)}, bf16[512,256]{1,0:T(8,128)(2,1)S(1)}, u32[]{:S(2)}, u32[]{:S(2)}) collective-permute-start(bf16[512,256]{1,0:T(8,128)(2,1)S(1)} %shard_map.143.refs_5_.refs_0_), channel_id=1, source_target_pairs={{0,1},{1,0},{2,3},{3,2},{4,8},{5,9},{6,10},{7,11},{8,4},{9,5},{10,... | collective-permute-start | bytes 786440 | tf_op jit(solution)/shard_map/ppermute | solution.py:633
  84.2 10.3 %collective-permute-start.27 = (bf16[512,256]{1,0:T(8,128)(2,1)S(1)}, bf16[512,256]{1,0:T(8,128)(2,1)S(1)}, u32[]{:S(2)}, u32[]{:S(2)}) collective-permute-start(bf16[512,256]{1,0:T(8,128)(2,1)S(1)} %shard_map.145.refs_5_.refs_1_), channel_id=1, source_target_pairs={{0,4},{4,0},{8,12},{12,8},{1,5},{5,1},{9,13},{13,9},{2,6},{6,2},{1... | collective-permute-start | bytes 786440 | tf_op jit(solution)/shard_map/ppermute | solution.py:476
  88.2 10.4 %collective-permute-start.28 = (bf16[512,256]{1,0:T(8,128)(2,1)S(1)}, bf16[512,256]{1,0:T(8,128)(2,1)S(1)}, u32[]{:S(2)}, u32[]{:S(2)}) collective-permute-start(bf16[512,256]{1,0:T(8,128)(2,1)S(1)} %shard_map.147.refs_2_), channel_id=1, source_target_pairs={{0,4},{4,0},{8,12},{12,8},{1,5},{5,1},{9,13},{13,9},{2,6},{6,2},{1... | collective-permute-start | bytes 786440 | tf_op jit(solution)/shard_map/ppermute | solution.py:476

commit v17 on v15

--- a/solution.py
+++ b/solution.py
@@ -621,8 +621,8 @@
 
 class Line:
     lag = 3
-    half_weights = (3.0, 3.0, 3.0, 3.0, 3.0, 3.0, 3.0, 0.5)
-    turn_weights = (4.0, 4.0, 3.0, 3.0, 4.0, 2.0, 0.5, 0.5)
+    half_weights = (3.0, 4.0, 3.0, 3.0, 3.0, 3.0, 3.0, 0.5)
+    turn_weights = (3.0, 4.0, 3.0, 3.0, 4.0, 2.0, 0.5, 0.5)
 
     def __init__(self, axis, other, end, step):
         self.axis, self.axes, self.step = axis, (axis, other), step
@@ -736,13 +736,13 @@
     away = step(relay_all, away)
     backs = [exchange(piece, "seq", d) for d, piece in enumerate(away, 1)]
     line.meet(rows)
+    line.enter(step(relay, query_first))
+    line.turn(query_second)
     dkey, dvalue, dkv_t = step(close_keys, dkv, backs, far_bits, local_levels)
-    line.enter(step(relay, query_first))
     key_first = step(weight_terms, dkv_t, tokens, inner, 0, 0, pieces)
-    line.turn(query_second)
-    key_second = step(weight_terms, dkv_t, tokens, inner, 0, 1, pieces)
     line.meet(rows)
     line.turn(key_first)
+    key_second = step(weight_terms, dkv_t, tokens, inner, 0, 1, pieces)
     keep, send = step(project_split, rank, [dquery, dkey, dvalue], [w_query, w_key, w_value], "head")
     line.meet(rows)
     value_first = step(weight_terms, dkv_t, tokens, inner, 1, 0, pieces)

time: 102 us -> 98.5 us (0.966)
  waiting for transfers between devices: 27.6 us -> 17.3 us
  starting transfers between devices: 39.7 us -> 46.1 us
    ppermute x21, waiting for transfers between devices: 27.5 us -> 17.2 us  [exchange(): return lax.ppermute(block, axis, [(i, i ^ distance) for i in range(count)])]
    ppermute x21, starting transfers between devices: 38.6 us -> 45 us  [exchange(): return lax.ppermute(block, axis, [(i, i ^ distance) for i in range(count)])]
  transfers between devices with their start and end apart: 29 -> 29, of which waited for: 11 -> 11; matrix products, arithmetic and copies ran while one was open for 0% -> 0% of each run, Pallas kernels for 22% -> 23%
where the time goes in v17:
time: 98.5 us; the launch traced here: 98.3 us
  starting transfers between devices  46.1 us (47%)
  Pallas kernels  33.7 us (34%)
  waiting for transfers between devices  17.3 us (18%)
  between operations  1.15 us (1%)
    ppermute x21, starting transfers between devices, exchange(): return lax.ppermute(block, axis, [(i, i ^ distance) for i in range(count)])  45 us
    pallas_call x42, Pallas kernels, run(): return pl.pallas_call(kernel, in_specs=in_specs, **options)(*ready, *after)  33.7 us
    ppermute x21, waiting for transfers between devices, exchange(): return lax.ppermute(block, axis, [(i, i ^ distance) for i in range(count)])  17.2 us
  transfers between devices with their start and end apart: 29, of which 11 were waited for; matrix products, arithmetic and copies ran while one was open for 0% of the time, Pallas kernels for 23%

profile of v17, /device:TPU:0, one launch (start us, length us, event | category | flops | bytes accessed | tf_op | source)
XLA Modules:
  0.0 98.3 jit_solution(8136759365055834866)
XLA Ops:
  0.7 5.3 %shard_map.110 = (bf16[1024,512]{1,0:T(8,128)(2,1)}, bf16[512,512]{1,0:T(8,128)(2,1)}, bf16[256,512]{1,0:T(8,128)(2,1)}, bf16[128,512]{1,0:T(8,128)(2,1)}, bf16[64,512]{1,0:T(8,128)(2,1)}) custom-call(bf16[1024,1024]{1,0:T(8,128)(2,1)} %refs_1_.17, bf16[1024,256]{1,0:T(8,128)(2,1)} %refs_5_.1, bf16[1024,256]{1,0:T(8,128)(2,1)} %refs_6_.1, ...), custom_call_target="tpu_custom_call" | custom-call | flops 5750000128 | bytes 1 | tf_op jit(solution)/shard_map/pallas_call | solution.py:42
  6.0 4.1 %collective-permute-start.1 = (bf16[64,512]{1,0:T(8,128)(2,1)}, bf16[64,512]{1,0:T(8,128)(2,1)S(1)}, u32[]{:S(2)}, u32[]{:S(2)}) collective-permute-start(bf16[64,512]{1,0:T(8,128)(2,1)} %get-tuple-element.64), channel_id=1, source_target_pairs={{0,8},{4,12},{8,0},{12,4},{1,9},{5,13},{9,1},{13,5},{2,10},{6,14},... | collective-permute-start | bytes 196616 | tf_op jit(solution)/shard_map/ppermute | solution.py:476
  10.1 1.3 %collective-permute-start.2 = (bf16[64,512]{1,0:T(8,128)(2,1)}, bf16[64,512]{1,0:T(8,128)(2,1)S(1)}, u32[]{:S(2)}, u32[]{:S(2)}) collective-permute-start(bf16[64,512]{1,0:T(8,128)(2,1)} %get-tuple-element.64), channel_id=1, source_target_pairs={{0,12},{4,8},{8,4},{12,0},{1,13},{5,9},{9,5},{13,1},{2,14},{6,10},... | collective-permute-start | bytes 196616 | tf_op jit(solution)/shard_map/ppermute | solution.py:476
  11.7 0.7 shard_map.109.refs_0_.refs_4_
  12.5 2.3 %shard_map.111 = (f32[4096,256]{1,0:T(8,128)S(1)}, f32[4,1024]{1,0:T(4,128)S(1)}) custom-call(bf16[1024,256]{1,0:T(8,128)(2,1)S(1)} %shard_map.109.refs_0_.refs_4_, bf16[1024,512]{1,0:T(8,128)(2,1)S(1)} %copy-done.6, bf16[512,512]{1,0:T(8,128)(2,1)S(1)} %copy-done.7, bf16[256,512]{1,0:T(8,128)(2,1)S(1)} %copy-done.8, ...), custom_call_target="tpu_custom_call" | custom-call | flops 2644999936 | bytes 1 | tf_op jit(solution)/shard_map/pallas_call | solution.py:42
  14.9 0.7 shard_map.112.refs_9_.refs_1_
  15.6 1.5 %collective-permute-done.2.refs_8_.refs_10_ = bf16[64,512]{1,0:T(8,128)(2,1)S(1)} collective-permute-done((bf16[64,512]{1,0:T(8,128)(2,1)}, bf16[64,512]{1,0:T(8,128)(2,1)S(1)}, u32[]{:S(2)}, u32[]{:S(2)}) %collective-permute-start.2) | collective-permute-done | bytes 65568 | tf_op jit(solution)/shard_map/ppermute | solution.py:476
  17.1 0.8 collective-permute-done.refs_6_.refs_8_
  17.9 3.9 %shard_map.113 = (bf16[1024,256]{1,0:T(8,128)(2,1)S(1)}, bf16[256,1024]{1,0:T(8,128)(2,1)S(1)}, f32[4,1024]{1,0:T(4,128)S(1)}) custom-call(bf16[1024,256]{1,0:T(8,128)(2,1)S(1)} %shard_map.109.refs_0_.refs_4_, f32[4096,256]{1,0:T(8,128)S(1)} %get-tuple-element.61.refs_2_.refs_1_, f32[4,1024]{1,0:T(4,128)S(1)} %get-tuple-element.62.refs_2_, ...), custom_call_target="tpu_custom_call" | custom-call | flops 4600000000 | bytes 1 | tf_op jit(solution)/shard_map/pallas_call | solution.py:42
  21.8 0.5 shard_map.114.refs_2_.refs_0_
  22.3 0.5 shard_map.115.refs_3_.refs_0_
  22.8 1.0 %collective-permute-start.4 = (bf16[512,256]{1,0:T(8,128)(2,1)S(1)}, bf16[512,256]{1,0:T(8,128)(2,1)S(1)}, u32[]{:S(2)}, u32[]{:S(2)}) collective-permute-start(bf16[512,256]{1,0:T(8,128)(2,1)S(1)} %shard_map.114.refs_2_.refs_0_), channel_id=1, source_target_pairs={{0,4},{4,0},{8,12},{12,8},{1,5},{5,1},{9,13},{13,9},{2,6},{6,2},{1... | collective-permute-start | bytes 786440 | tf_op jit(solution)/shard_map/ppermute | solution.py:476
  23.8 0.7 shard_map.116
  24.5 1.2 %collective-permute-start.7 = (bf16[512,256]{1,0:T(8,128)(2,1)S(1)}, bf16[512,256]{1,0:T(8,128)(2,1)S(1)}, u32[]{:S(2)}, u32[]{:S(2)}) collective-permute-start(bf16[512,256]{1,0:T(8,128)(2,1)S(1)} %shard_map.115.refs_3_.refs_0_), channel_id=1, source_target_pairs={{0,4},{4,0},{8,12},{12,8},{1,5},{5,1},{9,13},{13,9},{2,6},{6,2},{1... | collective-permute-start | bytes 786440 | tf_op jit(solution)/shard_map/ppermute | solution.py:476
  25.7 6.9 %shard_map.117 = (bf16[1024,256]{1,0:T(8,128)(2,1)S(1)}, f32[1024,512]{1,0:T(8,128)S(1)}, bf16[512,256]{1,0:T(8,128)(2,1)S(1)}, bf16[512,256]{1,0:T(8,128)(2,1)S...) custom-call(bf16[1024,256]{1,0:T(8,128)(2,1)S(1)} %shard_map.109.refs_0_.refs_4_, ...), custom_call_target="tpu_custom_call" | custom-call | flops 9200000000 | bytes 1 | tf_op jit(solution)/shard_map/pallas_call | solution.py:42
  32.7 0.6 collective-permute-start.6
  33.6 2.0 %collective-permute-start.9 = (bf16[128,512]{1,0:T(8,128)(2,1)S(1)}, bf16[128,512]{1,0:T(8,128)(2,1)S(1)}, u32[]{:S(2)}, u32[]{:S(2)}) collective-permute-start(bf16[128,512]{1,0:T(8,128)(2,1)S(1)} %get-tuple-element.78.refs_2_), channel_id=1, source_target_pairs={{0,4},{4,0},{8,12},{12,8},{1,5},{5,1},{9,13},{13,9},{2,6},{6,2},{1... | collective-permute-start | bytes 393224 | tf_op jit(solution)/shard_map/ppermute | solution.py:476
  35.5 1.9 %collective-permute-start.10 = (bf16[64,512]{1,0:T(8,128)(2,1)S(1)}, bf16[64,512]{1,0:T(8,128)(2,1)S(1)}, u32[]{:S(2)}, u32[]{:S(2)}) collective-permute-start(bf16[64,512]{1,0:T(8,128)(2,1)S(1)} %get-tuple-element.81), channel_id=1, source_target_pairs={{0,8},{4,12},{8,0},{12,4},{1,9},{5,13},{9,1},{13,5},{2,10},{6,14},... | collective-permute-start | bytes 196616 | tf_op jit(solution)/shard_map/ppermute | solution.py:476
  37.4 0.6 collective-permute-start.11
  38.2 7.4 %collective-permute-start.13 = (bf16[512,256]{1,0:T(8,128)(2,1)S(1)}, bf16[512,256]{1,0:T(8,128)(2,1)S(1)}, u32[]{:S(2)}, u32[]{:S(2)}) collective-permute-start(bf16[512,256]{1,0:T(8,128)(2,1)S(1)} %shard_map.122.refs_4_.refs_0_), channel_id=1, source_target_pairs={{0,4},{4,0},{8,12},{12,8},{1,5},{5,1},{9,13},{13,9},{2,6},{6,2},{1... | collective-permute-start | bytes 786440 | tf_op jit(solution)/shard_map/ppermute | solution.py:476
  45.7 0.8 collective-permute-done.10.refs_2_
  46.5 1.5 %collective-permute-start.5 = (bf16[1024,256]{1,0:T(8,128)(2,1)S(1)}, bf16[1024,256]{1,0:T(8,128)(2,1)S(1)}, u32[]{:S(2)}, u32[]{:S(2)}) collective-permute-start(bf16[1024,256]{1,0:T(8,128)(2,1)S(1)} %get-tuple-element.72), channel_id=1, source_target_pairs={{0,2},{1,3},{2,0},{3,1},{4,6},{5,7},{6,4},{7,5},{8,10},{9,11},{10,... | collective-permute-start | bytes 1572872 | tf_op jit(solution)/shard_map/ppermute | solution.py:476
  48.0 1.0 %shard_map.124 = (bf16[1024,256]{1,0:T(8,128)(2,1)S(1)}, bf16[1024,256]{1,0:T(8,128)(2,1)S(1)}, bf16[512,1024]{1,0:T(8,128)(2,1)S(1)}) custom-call(f32[1024,512]{1,0:T(8,128)S(1)} %get-tuple-element.80.refs_0_, bf16[128,512]{1,0:T(8,128)(2,1)S(1)} %collective-permute-done.9.refs_1_, bf16[64,512]{1,0:T(8,128)(2,1)S(1)} %collective-permute-done.10.refs_2_, ...), custom_call_target="tpu_custom_call" | custom-call | flops 230000000 | bytes 1 | tf_op jit(solution)/shard_map/pallas_call | solution.py:42
  49.0 0.5 shard_map.125.refs_2_.refs_3_.refs_0_
  49.6 3.3 %collective-permute-done.13.refs_1_ = bf16[512,256]{1,0:T(8,128)(2,1)S(1)} collective-permute-done((bf16[512,256]{1,0:T(8,128)(2,1)S(1)}, bf16[512,256]{1,0:T(8,128)(2,1)S(1)}, u32[]{:S(2)}, u32[]{:S(2)}) %collective-permute-start.13) | collective-permute-done | bytes 262176 | tf_op jit(solution)/shard_map/ppermute | solution.py:476
  53.3 3.5 %collective-permute-start.15 = (bf16[512,256]{1,0:T(8,128)(2,1)S(1)}, bf16[512,256]{1,0:T(8,128)(2,1)S(1)}, u32[]{:S(2)}, u32[]{:S(2)}) collective-permute-start(bf16[512,256]{1,0:T(8,128)(2,1)S(1)} %get-tuple-element.90), channel_id=1, source_target_pairs={{0,4},{4,0},{8,12},{12,8},{1,5},{5,1},{9,13},{13,9},{2,6},{6,2},{1... | collective-permute-start | bytes 786440 | tf_op jit(solution)/shard_map/ppermute | solution.py:476
  56.9 0.5 shard_map.128.refs_7_.refs_3_.refs_0_
  57.4 1.8 %shard_map.129 = (bf16[1024,512]{1,0:T(8,128)(2,1)S(1)}, bf16[1024,512]{1,0:T(8,128)(2,1)S(1)}) custom-call(s32[1]{0:T(128)} %bitcast.refs_4_.refs_0_, bf16[1024,256]{1,0:T(8,128)(2,1)S(1)} %get-tuple-element.70.refs_2_.refs_1_, bf16[1024,256]{1,0:T(8,128)(2,1)S(1)} %get-tuple-element.84.refs_2_, bf16[1024,256]{1,0:T(8,128)(2,1)S(1)} %get-tuple-element.85.refs_3_, ...), custom_call_target="tpu_custom_call" | custom-call | flops 1150000000 | bytes 1 | tf_op jit(solution)/shard_map/pallas_call | solution.py:42
  59.4 0.5 shard_map.131.refs_4_.refs_3_.refs_0_
  60.0 2.8 %collective-permute-start.20 = (bf16[512,256]{1,0:T(8,128)(2,1)S(1)}, bf16[512,256]{1,0:T(8,128)(2,1)S(1)}, u32[]{:S(2)}, u32[]{:S(2)}) collective-permute-start(bf16[512,256]{1,0:T(8,128)(2,1)S(1)} %get-tuple-element.96), channel_id=1, source_target_pairs={{0,4},{4,0},{8,12},{12,8},{1,5},{5,1},{9,13},{13,9},{2,6},{6,2},{1... | collective-permute-start | bytes 786440 | tf_op jit(solution)/shard_map/ppermute | solution.py:476
  63.2 0.6 collective-permute-start.17
  63.9 4.7 %collective-permute-start.18 = (bf16[512,256]{1,0:T(8,128)(2,1)S(1)}, bf16[512,256]{1,0:T(8,128)(2,1)S(1)}, u32[]{:S(2)}, u32[]{:S(2)}) collective-permute-start(bf16[512,256]{1,0:T(8,128)(2,1)S(1)} %get-tuple-element.94), channel_id=1, source_target_pairs={{0,4},{4,0},{8,12},{12,8},{1,5},{5,1},{9,13},{13,9},{2,6},{6,2},{1... | collective-permute-start | bytes 786440 | tf_op jit(solution)/shard_map/ppermute | solution.py:476
  68.6 0.9 shard_map.136
  69.5 0.5 shard_map.137.refs_2_.refs_3_.refs_0_
  70.3 2.5 %collective-permute-start.22 = (bf16[512,256]{1,0:T(8,128)(2,1)S(1)}, bf16[512,256]{1,0:T(8,128)(2,1)S(1)}, u32[]{:S(2)}, u32[]{:S(2)}) collective-permute-start(bf16[512,256]{1,0:T(8,128)(2,1)S(1)} %get-tuple-element.101), channel_id=1, source_target_pairs={{0,4},{4,0},{8,12},{12,8},{1,5},{5,1},{9,13},{13,9},{2,6},{6,2},{1... | collective-permute-start | bytes 786440 | tf_op jit(solution)/shard_map/ppermute | solution.py:476
  72.8 0.8 shard_map.140
  73.6 2.1 %collective-permute-done.18.refs_1_.refs_4_ = bf16[512,256]{1,0:T(8,128)(2,1)S(1)} collective-permute-done((bf16[512,256]{1,0:T(8,128)(2,1)S(1)}, bf16[512,256]{1,0:T(8,128)(2,1)S(1)}, u32[]{:S(2)}, u32[]{:S(2)}) %collective-permute-start.18) | collective-permute-done | bytes 262176 | tf_op jit(solution)/shard_map/ppermute | solution.py:476
  76.2 3.2 %collective-permute-start.25 = (bf16[512,256]{1,0:T(8,128)(2,1)S(1)}, bf16[512,256]{1,0:T(8,128)(2,1)S(1)}, u32[]{:S(2)}, u32[]{:S(2)}) collective-permute-start(bf16[512,256]{1,0:T(8,128)(2,1)S(1)} %shard_map.143.refs_2_), channel_id=1, source_target_pairs={{0,4},{4,0},{8,12},{12,8},{1,5},{5,1},{9,13},{13,9},{2,6},{6,2},{1... | collective-permute-start | bytes 786440 | tf_op jit(solution)/shard_map/ppermute | solution.py:476
  79.4 1.5 %collective-permute-start.21 = (bf16[1024,256]{1,0:T(8,128)(2,1)S(1)}, bf16[1024,256]{1,0:T(8,128)(2,1)S(1)}, u32[]{:S(2)}, u32[]{:S(2)}) collective-permute-start(bf16[1024,256]{1,0:T(8,128)(2,1)S(1)} %get-tuple-element.100), channel_id=1, source_target_pairs={{0,2},{1,3},{2,0},{3,1},{4,6},{5,7},{6,4},{7,5},{8,10},{9,11},{10,... | collective-permute-start | bytes 1572872 | tf_op jit(solution)/shard_map/ppermute | solution.py:476
  81.5 0.8 shard_map.145
  82.4 2.9 %collective-permute-start.27 = (bf16[512,256]{1,0:T(8,128)(2,1)S(1)}, bf16[512,256]{1,0:T(8,128)(2,1)S(1)}, u32[]{:S(2)}, u32[]{:S(2)}) collective-permute-start(bf16[512,256]{1,0:T(8,128)(2,1)S(1)} %shard_map.146.refs_5_.refs_1_), channel_id=1, source_target_pairs={{0,4},{4,0},{8,12},{12,8},{1,5},{5,1},{9,13},{13,9},{2,6},{6,2},{1... | collective-permute-start | bytes 786440 | tf_op jit(solution)/shard_map/ppermute | solution.py:476
  85.3 1.6 %collective-permute-done.25.refs_4_ = bf16[512,256]{1,0:T(8,128)(2,1)S(1)} collective-permute-done((bf16[512,256]{1,0:T(8,128)(2,1)S(1)}, bf16[512,256]{1,0:T(8,128)(2,1)S(1)}, u32[]{:S(2)}, u32[]{:S(2)}) %collective-permute-start.25) | collective-permute-done | bytes 262176 | tf_op jit(solution)/shard_map/ppermute | solution.py:476
  86.9 0.8 shard_map.147
  87.8 2.2 %collective-permute-start.28 = (bf16[512,256]{1,0:T(8,128)(2,1)S(1)}, bf16[512,256]{1,0:T(8,128)(2,1)S(1)}, u32[]{:S(2)}, u32[]{:S(2)}) collective-permute-start(bf16[512,256]{1,0:T(8,128)(2,1)S(1)} %shard_map.148.refs_2_), channel_id=1, source_target_pairs={{0,4},{4,0},{8,12},{12,8},{1,5},{5,1},{9,13},{13,9},{2,6},{6,2},{1... | collective-permute-start | bytes 786440 | tf_op jit(solution)/shard_map/ppermute | solution.py:476
  90.0 1.1 %collective-permute-done.21.refs_1_ = bf16[1024,256]{1,0:T(8,128)(2,1)S(1)} collective-permute-done((bf16[1024,256]{1,0:T(8,128)(2,1)S(1)}, bf16[1024,256]{1,0:T(8,128)(2,1)S(1)}, u32[]{:S(2)}, u32[]{:S(2)}) %collective-permute-start.21) | collective-permute-done | bytes 524320 | tf_op jit(solution)/shard_map/ppermute | solution.py:476
  91.1 0.9 shard_map.149
  92.5 4.9 %collective-permute-done.28.refs_4_ = bf16[512,256]{1,0:T(8,128)(2,1)S(1)} collective-permute-done((bf16[512,256]{1,0:T(8,128)(2,1)S(1)}, bf16[512,256]{1,0:T(8,128)(2,1)S(1)}, u32[]{:S(2)}, u32[]{:S(2)}) %collective-permute-start.28) | collective-permute-done | bytes 262176 | tf_op jit(solution)/shard_map/ppermute | solution.py:476
  97.5 0.8 shard_map.150
  (70 shorter events, 3.9 us)
Async XLA Ops:
  0.6 11.1 %copy-start = (bf16[1024,1024]{1,0:T(8,128)(2,1)S(1)}, bf16[1024,1024]{1,0:T(8,128)(2,1)}, u32[]{:S(2)}) copy-start(bf16[1024,1024]{1,0:T(8,128)(2,1)} %refs_1_.17) | copy-start | bytes 6291460
  0.7 11.1 %copy-start.3 = (bf16[1024,256]{1,0:T(8,128)(2,1)S(1)}, bf16[1024,256]{1,0:T(8,128)(2,1)}, u32[]{:S(2)}) copy-start(bf16[1024,256]{1,0:T(8,128)(2,1)} %refs_4_.3) | copy-start | bytes 1572868
  6.0 6.4 %copy-start.6 = (bf16[1024,512]{1,0:T(8,128)(2,1)S(1)}, bf16[1024,512]{1,0:T(8,128)(2,1)}, u32[]{:S(2)}) copy-start(bf16[1024,512]{1,0:T(8,128)(2,1)} %get-tuple-element.58.refs_1_.refs_3_.refs_5_) | copy-start | bytes 3145732
  6.0 6.4 %copy-start.7 = (bf16[512,512]{1,0:T(8,128)(2,1)S(1)}, bf16[512,512]{1,0:T(8,128)(2,1)}, u32[]{:S(2)}) copy-start(bf16[512,512]{1,0:T(8,128)(2,1)} %get-tuple-element.59.refs_2_.refs_4_.refs_6_) | copy-start | bytes 1572868
  6.0 6.4 %copy-start.8 = (bf16[256,512]{1,0:T(8,128)(2,1)S(1)}, bf16[256,512]{1,0:T(8,128)(2,1)}, u32[]{:S(2)}) copy-start(bf16[256,512]{1,0:T(8,128)(2,1)} %get-tuple-element.60.refs_3_.refs_5_.refs_7_) | copy-start | bytes 786436
  6.0 9.5 %collective-permute-start.1 = (bf16[64,512]{1,0:T(8,128)(2,1)}, bf16[64,512]{1,0:T(8,128)(2,1)S(1)}, u32[]{:S(2)}, u32[]{:S(2)}) collective-permute-start(bf16[64,512]{1,0:T(8,128)(2,1)} %get-tuple-element.64), channel_id=1, source_target_pairs={{0,8},{4,12},{8,0},{12,4},{1,9},{5,13},{9,1},{13,5},{2,10},{6,14},... | collective-permute-start | bytes 196616 | tf_op jit(solution)/shard_map/ppermute | solution.py:476
  10.1 7.0 %collective-permute-start.2 = (bf16[64,512]{1,0:T(8,128)(2,1)}, bf16[64,512]{1,0:T(8,128)(2,1)S(1)}, u32[]{:S(2)}, u32[]{:S(2)}) collective-permute-start(bf16[64,512]{1,0:T(8,128)(2,1)} %get-tuple-element.64), channel_id=1, source_target_pairs={{0,12},{4,8},{8,4},{12,0},{1,13},{5,9},{9,5},{13,1},{2,14},{6,10},... | collective-permute-start | bytes 196616 | tf_op jit(solution)/shard_map/ppermute | solution.py:476
  11.5 6.4 %collective-permute-start = (bf16[128,512]{1,0:T(8,128)(2,1)}, bf16[128,512]{1,0:T(8,128)(2,1)S(1)}, u32[]{:S(2)}, u32[]{:S(2)}) collective-permute-start(bf16[128,512]{1,0:T(8,128)(2,1)} %get-tuple-element.63), channel_id=1, source_target_pairs={{0,4},{4,0},{8,12},{12,8},{1,5},{5,1},{9,13},{13,9},{2,6},{6,2},{1... | collective-permute-start | bytes 393224 | tf_op jit(solution)/shard_map/ppermute | solution.py:476
  12.5 2.4 %copy-start.1 = (bf16[1024,1024]{1,0:T(8,128)(2,1)S(1)}, bf16[1024,1024]{1,0:T(8,128)(2,1)}, u32[]{:S(2)}) copy-start(bf16[1024,1024]{1,0:T(8,128)(2,1)} %refs_1_.13) | copy-start | bytes 6291460
  12.5 2.4 %copy-start.2 = (bf16[1024,256]{1,0:T(8,128)(2,1)S(1)}, bf16[1024,256]{1,0:T(8,128)(2,1)}, u32[]{:S(2)}) copy-start(bf16[1024,256]{1,0:T(8,128)(2,1)} %refs_2_.3) | copy-start | bytes 1572868
  22.8 9.9 %collective-permute-start.4 = (bf16[512,256]{1,0:T(8,128)(2,1)S(1)}, bf16[512,256]{1,0:T(8,128)(2,1)S(1)}, u32[]{:S(2)}, u32[]{:S(2)}) collective-permute-start(bf16[512,256]{1,0:T(8,128)(2,1)S(1)} %shard_map.114.refs_2_.refs_0_), channel_id=1, source_target_pairs={{0,4},{4,0},{8,12},{12,8},{1,5},{5,1},{9,13},{13,9},{2,6},{6,2},{1... | collective-permute-start | bytes 786440 | tf_op jit(solution)/shard_map/ppermute | solution.py:476
  24.5 13.5 %collective-permute-start.7 = (bf16[512,256]{1,0:T(8,128)(2,1)S(1)}, bf16[512,256]{1,0:T(8,128)(2,1)S(1)}, u32[]{:S(2)}, u32[]{:S(2)}) collective-permute-start(bf16[512,256]{1,0:T(8,128)(2,1)S(1)} %shard_map.115.refs_3_.refs_0_), channel_id=1, source_target_pairs={{0,4},{4,0},{8,12},{12,8},{1,5},{5,1},{9,13},{13,9},{2,6},{6,2},{1... | collective-permute-start | bytes 786440 | tf_op jit(solution)/shard_map/ppermute | solution.py:476
  25.7 7.6 %collective-permute-start.3 = (bf16[1024,512]{1,0:T(8,128)(2,1)S(1)}, bf16[1024,512]{1,0:T(8,128)(2,1)S(1)}, u32[]{:S(2)}, u32[]{:S(2)}) collective-permute-start(bf16[1024,512]{1,0:T(8,128)(2,1)S(1)} %get-tuple-element.68), channel_id=1, source_target_pairs={{0,1},{1,0},{2,3},{3,2},{4,5},{5,4},{6,7},{7,6},{8,9},{9,8},{10,11... | collective-permute-start | bytes 3145736 | tf_op jit(solution)/shard_map/ppermute | solution.py:476
  32.7 5.5 %collective-permute-start.6 = (bf16[512,256]{1,0:T(8,128)(2,1)S(1)}, bf16[512,256]{1,0:T(8,128)(2,1)S(1)}, u32[]{:S(2)}, u32[]{:S(2)}) collective-permute-start(bf16[512,256]{1,0:T(8,128)(2,1)S(1)} %shard_map.118.refs_2_.refs_1_), channel_id=1, source_target_pairs={{0,1},{1,0},{2,3},{3,2},{4,8},{5,9},{6,10},{7,11},{8,4},{9,5},{10,... | collective-permute-start | bytes 786440 | tf_op jit(solution)/shard_map/ppermute | solution.py:650
  33.6 14.4 %collective-permute-start.9 = (bf16[128,512]{1,0:T(8,128)(2,1)S(1)}, bf16[128,512]{1,0:T(8,128)(2,1)S(1)}, u32[]{:S(2)}, u32[]{:S(2)}) collective-permute-start(bf16[128,512]{1,0:T(8,128)(2,1)S(1)} %get-tuple-element.78.refs_2_), channel_id=1, source_target_pairs={{0,4},{4,0},{8,12},{12,8},{1,5},{5,1},{9,13},{13,9},{2,6},{6,2},{1... | collective-permute-start | bytes 393224 | tf_op jit(solution)/shard_map/ppermute | solution.py:476
  35.5 10.9 %collective-permute-start.10 = (bf16[64,512]{1,0:T(8,128)(2,1)S(1)}, bf16[64,512]{1,0:T(8,128)(2,1)S(1)}, u32[]{:S(2)}, u32[]{:S(2)}) collective-permute-start(bf16[64,512]{1,0:T(8,128)(2,1)S(1)} %get-tuple-element.81), channel_id=1, source_target_pairs={{0,8},{4,12},{8,0},{12,4},{1,9},{5,13},{9,1},{13,5},{2,10},{6,14},... | collective-permute-start | bytes 196616 | tf_op jit(solution)/shard_map/ppermute | solution.py:476
  37.4 9.1 %collective-permute-start.11 = (bf16[64,512]{1,0:T(8,128)(2,1)S(1)}, bf16[64,512]{1,0:T(8,128)(2,1)S(1)}, u32[]{:S(2)}, u32[]{:S(2)}) collective-permute-start(bf16[64,512]{1,0:T(8,128)(2,1)S(1)} %get-tuple-element.82), channel_id=1, source_target_pairs={{0,12},{4,8},{8,4},{12,0},{1,13},{5,9},{9,5},{13,1},{2,14},{6,10},... | collective-permute-start | bytes 196616 | tf_op jit(solution)/shard_map/ppermute | solution.py:476
  38.1 14.9 %collective-permute-start.12 = (bf16[512,256]{1,0:T(8,128)(2,1)S(1)}, bf16[512,256]{1,0:T(8,128)(2,1)S(1)}, u32[]{:S(2)}, u32[]{:S(2)}) collective-permute-start(bf16[512,256]{1,0:T(8,128)(2,1)S(1)} %shard_map.121.refs_1_), channel_id=1, source_target_pairs={{0,1},{1,0},{2,3},{3,2},{4,8},{5,9},{6,10},{7,11},{8,4},{9,5},{10,... | collective-permute-start | bytes 786440 | tf_op jit(solution)/shard_map/ppermute | solution.py:650
  38.2 14.6 %collective-permute-start.13 = (bf16[512,256]{1,0:T(8,128)(2,1)S(1)}, bf16[512,256]{1,0:T(8,128)(2,1)S(1)}, u32[]{:S(2)}, u32[]{:S(2)}) collective-permute-start(bf16[512,256]{1,0:T(8,128)(2,1)S(1)} %shard_map.122.refs_4_.refs_0_), channel_id=1, source_target_pairs={{0,4},{4,0},{8,12},{12,8},{1,5},{5,1},{9,13},{13,9},{2,6},{6,2},{1... | collective-permute-start | bytes 786440 | tf_op jit(solution)/shard_map/ppermute | solution.py:476
  46.5 12.8 %collective-permute-start.8 = (bf16[512,256]{1,0:T(8,128)(2,1)S(1)}, bf16[512,256]{1,0:T(8,128)(2,1)S(1)}, u32[]{:S(2)}, u32[]{:S(2)}) collective-permute-start(bf16[512,256]{1,0:T(8,128)(2,1)S(1)} %get-tuple-element.79), channel_id=1, source_target_pairs={{0,4},{4,0},{8,12},{12,8},{1,5},{5,1},{9,13},{13,9},{2,6},{6,2},{1... | collective-permute-start | bytes 786440 | tf_op jit(solution)/shard_map/ppermute | solution.py:476
  46.5 22.1 %collective-permute-start.5 = (bf16[1024,256]{1,0:T(8,128)(2,1)S(1)}, bf16[1024,256]{1,0:T(8,128)(2,1)S(1)}, u32[]{:S(2)}, u32[]{:S(2)}) collective-permute-start(bf16[1024,256]{1,0:T(8,128)(2,1)S(1)} %get-tuple-element.72), channel_id=1, source_target_pairs={{0,2},{1,3},{2,0},{3,1},{4,6},{5,7},{6,4},{7,5},{8,10},{9,11},{10,... | collective-permute-start | bytes 1572872 | tf_op jit(solution)/shard_map/ppermute | solution.py:476
  52.9 7.0 %collective-permute-start.16 = (bf16[512,256]{1,0:T(8,128)(2,1)S(1)}, bf16[512,256]{1,0:T(8,128)(2,1)S(1)}, u32[]{:S(2)}, u32[]{:S(2)}) collective-permute-start(bf16[512,256]{1,0:T(8,128)(2,1)S(1)} %shard_map.126.refs_4_.refs_1_), channel_id=1, source_target_pairs={{0,1},{1,0},{2,3},{3,2},{4,8},{5,9},{6,10},{7,11},{8,4},{9,5},{10,... | collective-permute-start | bytes 786440 | tf_op jit(solution)/shard_map/ppermute | solution.py:650
  53.3 4.1 %copy-start.4 = (bf16[1024,256]{1,0:T(8,128)(2,1)S(1)}, bf16[1024,256]{1,0:T(8,128)(2,1)}, u32[]{:S(2)}) copy-start(bf16[1024,256]{1,0:T(8,128)(2,1)} %refs_5_.1) | copy-start | bytes 1572868
  53.3 4.1 %copy-start.5 = (bf16[1024,256]{1,0:T(8,128)(2,1)S(1)}, bf16[1024,256]{1,0:T(8,128)(2,1)}, u32[]{:S(2)}) copy-start(bf16[1024,256]{1,0:T(8,128)(2,1)} %refs_6_.1) | copy-start | bytes 1572868
  53.3 9.7 %collective-permute-start.15 = (bf16[512,256]{1,0:T(8,128)(2,1)S(1)}, bf16[512,256]{1,0:T(8,128)(2,1)S(1)}, u32[]{:S(2)}, u32[]{:S(2)}) collective-permute-start(bf16[512,256]{1,0:T(8,128)(2,1)S(1)} %get-tuple-element.90), channel_id=1, source_target_pairs={{0,4},{4,0},{8,12},{12,8},{1,5},{5,1},{9,13},{13,9},{2,6},{6,2},{1... | collective-permute-start | bytes 786440 | tf_op jit(solution)/shard_map/ppermute | solution.py:476
  59.3 4.5 %collective-permute-start.14 = (bf16[512,256]{1,0:T(8,128)(2,1)S(1)}, bf16[512,256]{1,0:T(8,128)(2,1)S(1)}, u32[]{:S(2)}, u32[]{:S(2)}) collective-permute-start(bf16[512,256]{1,0:T(8,128)(2,1)S(1)} %shard_map.130.refs_2_.refs_1_), channel_id=1, source_target_pairs={{0,1},{1,0},{2,3},{3,2},{4,8},{5,9},{6,10},{7,11},{8,4},{9,5},{10,... | collective-permute-start | bytes 786440 | tf_op jit(solution)/shard_map/ppermute | solution.py:650
  60.0 10.0 %collective-permute-start.20 = (bf16[512,256]{1,0:T(8,128)(2,1)S(1)}, bf16[512,256]{1,0:T(8,128)(2,1)S(1)}, u32[]{:S(2)}, u32[]{:S(2)}) collective-permute-start(bf16[512,256]{1,0:T(8,128)(2,1)S(1)} %get-tuple-element.96), channel_id=1, source_target_pairs={{0,4},{4,0},{8,12},{12,8},{1,5},{5,1},{9,13},{13,9},{2,6},{6,2},{1... | collective-permute-start | bytes 786440 | tf_op jit(solution)/shard_map/ppermute | solution.py:476
  63.1 7.1 %collective-permute-start.19 = (bf16[512,256]{1,0:T(8,128)(2,1)S(1)}, bf16[512,256]{1,0:T(8,128)(2,1)S(1)}, u32[]{:S(2)}, u32[]{:S(2)}) collective-permute-start(bf16[512,256]{1,0:T(8,128)(2,1)S(1)} %shard_map.133.refs_1_), channel_id=1, source_target_pairs={{0,1},{1,0},{2,3},{3,2},{4,8},{5,9},{6,10},{7,11},{8,4},{9,5},{10,... | collective-permute-start | bytes 786440 | tf_op jit(solution)/shard_map/ppermute | solution.py:650
  63.2 12.6 %collective-permute-start.17 = (bf16[1024,512]{1,0:T(8,128)(2,1)S(1)}, bf16[1024,512]{1,0:T(8,128)(2,1)S(1)}, u32[]{:S(2)}, u32[]{:S(2)}) collective-permute-start(bf16[1024,512]{1,0:T(8,128)(2,1)S(1)} %shard_map.134.refs_4_), channel_id=1, source_target_pairs={{0,1},{1,0},{2,3},{3,2},{4,5},{5,4},{6,7},{7,6},{8,9},{9,8},{10,11... | collective-permute-start | bytes 3145736 | tf_op jit(solution)/shard_map/ppermute | solution.py:476
  63.9 11.8 %collective-permute-start.18 = (bf16[512,256]{1,0:T(8,128)(2,1)S(1)}, bf16[512,256]{1,0:T(8,128)(2,1)S(1)}, u32[]{:S(2)}, u32[]{:S(2)}) collective-permute-start(bf16[512,256]{1,0:T(8,128)(2,1)S(1)} %get-tuple-element.94), channel_id=1, source_target_pairs={{0,4},{4,0},{8,12},{12,8},{1,5},{5,1},{9,13},{13,9},{2,6},{6,2},{1... | collective-permute-start | bytes 786440 | tf_op jit(solution)/shard_map/ppermute | solution.py:476
  70.1 6.0 %collective-permute-start.23 = (bf16[512,256]{1,0:T(8,128)(2,1)S(1)}, bf16[512,256]{1,0:T(8,128)(2,1)S(1)}, u32[]{:S(2)}, u32[]{:S(2)}) collective-permute-start(bf16[512,256]{1,0:T(8,128)(2,1)S(1)} %shard_map.138.refs_4_.refs_0_), channel_id=1, source_target_pairs={{0,1},{1,0},{2,3},{3,2},{4,8},{5,9},{6,10},{7,11},{8,4},{9,5},{10,... | collective-permute-start | bytes 786440 | tf_op jit(solution)/shard_map/ppermute | solution.py:650
  70.3 11.0 %collective-permute-start.22 = (bf16[512,256]{1,0:T(8,128)(2,1)S(1)}, bf16[512,256]{1,0:T(8,128)(2,1)S(1)}, u32[]{:S(2)}, u32[]{:S(2)}) collective-permute-start(bf16[512,256]{1,0:T(8,128)(2,1)S(1)} %get-tuple-element.101), channel_id=1, source_target_pairs={{0,4},{4,0},{8,12},{12,8},{1,5},{5,1},{9,13},{13,9},{2,6},{6,2},{1... | collective-permute-start | bytes 786440 | tf_op jit(solution)/shard_map/ppermute | solution.py:476
  75.8 6.5 %collective-permute-start.26 = (bf16[512,256]{1,0:T(8,128)(2,1)S(1)}, bf16[512,256]{1,0:T(8,128)(2,1)S(1)}, u32[]{:S(2)}, u32[]{:S(2)}) collective-permute-start(bf16[512,256]{1,0:T(8,128)(2,1)S(1)} %shard_map.141.refs_2_.refs_0_), channel_id=1, source_target_pairs={{0,1},{1,0},{2,3},{3,2},{4,8},{5,9},{6,10},{7,11},{8,4},{9,5},{10,... | collective-permute-start | bytes 786440 | tf_op jit(solution)/shard_map/ppermute | solution.py:650
  76.2 10.8 %collective-permute-start.25 = (bf16[512,256]{1,0:T(8,128)(2,1)S(1)}, bf16[512,256]{1,0:T(8,128)(2,1)S(1)}, u32[]{:S(2)}, u32[]{:S(2)}) collective-permute-start(bf16[512,256]{1,0:T(8,128)(2,1)S(1)} %shard_map.143.refs_2_), channel_id=1, source_target_pairs={{0,4},{4,0},{8,12},{12,8},{1,5},{5,1},{9,13},{13,9},{2,6},{6,2},{1... | collective-permute-start | bytes 786440 | tf_op jit(solution)/shard_map/ppermute | solution.py:476
  79.4 11.8 %collective-permute-start.21 = (bf16[1024,256]{1,0:T(8,128)(2,1)S(1)}, bf16[1024,256]{1,0:T(8,128)(2,1)S(1)}, u32[]{:S(2)}, u32[]{:S(2)}) collective-permute-start(bf16[1024,256]{1,0:T(8,128)(2,1)S(1)} %get-tuple-element.100), channel_id=1, source_target_pairs={{0,2},{1,3},{2,0},{3,1},{4,6},{5,7},{6,4},{7,5},{8,10},{9,11},{10,... | collective-permute-start | bytes 1572872 | tf_op jit(solution)/shard_map/ppermute | solution.py:476
  81.4 6.4 %collective-permute-start.24 = (bf16[512,256]{1,0:T(8,128)(2,1)S(1)}, bf16[512,256]{1,0:T(8,128)(2,1)S(1)}, u32[]{:S(2)}, u32[]{:S(2)}) collective-permute-start(bf16[512,256]{1,0:T(8,128)(2,1)S(1)} %shard_map.144.refs_5_.refs_0_), channel_id=1, source_target_pairs={{0,1},{1,0},{2,3},{3,2},{4,8},{5,9},{6,10},{7,11},{8,4},{9,5},{10,... | collective-permute-start | bytes 786440 | tf_op jit(solution)/shard_map/ppermute | solution.py:650
  82.4 10.2 %collective-permute-start.27 = (bf16[512,256]{1,0:T(8,128)(2,1)S(1)}, bf16[512,256]{1,0:T(8,128)(2,1)S(1)}, u32[]{:S(2)}, u32[]{:S(2)}) collective-permute-start(bf16[512,256]{1,0:T(8,128)(2,1)S(1)} %shard_map.146.refs_5_.refs_1_), channel_id=1, source_target_pairs={{0,4},{4,0},{8,12},{12,8},{1,5},{5,1},{9,13},{13,9},{2,6},{6,2},{1... | collective-permute-start | bytes 786440 | tf_op jit(solution)/shard_map/ppermute | solution.py:476
  87.8 9.6 %collective-permute-start.28 = (bf16[512,256]{1,0:T(8,128)(2,1)S(1)}, bf16[512,256]{1,0:T(8,128)(2,1)S(1)}, u32[]{:S(2)}, u32[]{:S(2)}) collective-permute-start(bf16[512,256]{1,0:T(8,128)(2,1)S(1)} %shard_map.148.refs_2_), channel_id=1, source_target_pairs={{0,4},{4,0},{8,12},{12,8},{1,5},{5,1},{9,13},{13,9},{2,6},{6,2},{1... | collective-permute-start | bytes 786440 | tf_op jit(solution)/shard_map/ppermute | solution.py:476

commit v18 on v10

--- a/solution.py
+++ b/solution.py
@@ -611,8 +611,8 @@
 
 class Line:
     lag = 3
-    half_weights = (3.0, 3.0, 3.0, 2.5, 2.5, 3.0, 3.0, 3.0)
-    turn_weights = (3.0, 2.5, 2.5, 3.0, 3.0, 3.0, 3.0, 3.0)
+    half_weights = (3.0, 3.0, 3.0, 3.0, 3.0, 3.0, 1.0, 0.5)
+    turn_weights = (3.0, 3.0, 3.0, 3.0, 3.0, 0.5, 0.5, 0.5)
 
     def __init__(self, axis, other, end, step):
         self.axis, self.axes, self.step = axis, (axis, other), step
@@ -716,15 +716,12 @@
     rows = tokens.shape[1] // pieces
     line.enter(step(weight_terms, attended_t, cotangent, inner, 0, 0, pieces))
     line.enter(step(weight_terms, attended_t, cotangent, inner, 0, 1, pieces))
-    parts = step(project_split, rank, [attended], [w_out], "head")
-    mixed = Scatter(parts, "head", step)
     dquery, dkv, query_first, query_second, *away = step(
         backward, query, grad, attended_t, stats, tokens, levels, fars, far_bits, pieces
     )
     line.enter(query_first)
     backs = [exchange(piece, "seq", d) for d, piece in enumerate(away, 2)]
     line.meet(rows)
-    mixed.advance()
     line.meet(rows)
     line.turn(query_second)
     dkey, dvalue, dkv_t = step(
@@ -732,6 +729,8 @@
     )
     key_first = step(weight_terms, dkv_t, tokens, inner, 0, 0, pieces)
     line.meet(rows)
+    parts = step(project_split, rank, [attended], [w_out], "head")
+    mixed = Scatter(parts, "head", step)
     line.turn(key_first)
     line.meet(rows)
     key_second = step(weight_terms, dkv_t, tokens, inner, 0, 1, pieces)
@@ -741,17 +740,18 @@
     line.meet(rows)
     tokens_grad = Scatter([keep, step(relay, send)], "head", step)
     line.turn(value_first)
-    mixed = mixed.result()
+    mixed.advance()
     value_second = step(weight_terms, dkv_t, tokens, inner, 1, 1, pieces)
     line.meet(rows)
     line.turn(value_second)
     out_grad = line.output(0, pieces)
     line.meet(rows)
+    line.leave()
     tokens_grad.advance()
-    line.leave()
     line.meet(rows)
     query_grad = line.output(2, pieces)
     line.leave()
+    mixed = mixed.result()
     key_grad = line.output(4, pieces)
     line.leave()
     tokens_grad = tokens_grad.result()

time: 97.7 us -> 96.5 us (0.988)
  starting transfers between devices: 50.6 us -> 40.8 us
  waiting for transfers between devices: 12.1 us -> 20.7 us
    ppermute x20, starting transfers between devices: 49.4 us -> 39.8 us  [exchange(): return lax.ppermute(block, axis, [(i, i ^ distance) for i in range(count)])]
    ppermute x20, waiting for transfers between devices: 11.4 us -> 20.7 us  [exchange(): return lax.ppermute(block, axis, [(i, i ^ distance) for i in range(count)])]
  transfers between devices with their start and end apart: 28 -> 28, of which waited for: 7 -> 10; matrix products, arithmetic and copies ran while one was open for 0% -> 0% of each run, Pallas kernels for 23% -> 23%
where the time goes in v18:
time: 96.5 us; the launch traced here: 96.4 us
  starting transfers between devices  40.8 us (42%)
  Pallas kernels  33.7 us (35%)
  waiting for transfers between devices  20.7 us (21%)
  between operations  1.09 us (1%)
    ppermute x20, starting transfers between devices, exchange(): return lax.ppermute(block, axis, [(i, i ^ distance) for i in range(count)])  39.8 us
    pallas_call x40, Pallas kernels, run(): return pl.pallas_call(kernel, in_specs=in_specs, **options)(*ready, *after)  33.7 us
    ppermute x20, waiting for transfers between devices, exchange(): return lax.ppermute(block, axis, [(i, i ^ distance) for i in range(count)])  20.7 us
  transfers between devices with their start and end apart: 28, of which 10 were waited for; matrix products, arithmetic and copies ran while one was open for 0% of the time, Pallas kernels for 23%

profile of v18, /device:TPU:0, one launch (start us, length us, event | category | flops | bytes accessed | tf_op | source)
XLA Modules:
  0.0 96.4 jit_solution(17693583285681982967)
XLA Ops:
  0.7 5.3 %shard_map.110 = (bf16[1024,512]{1,0:T(8,128)(2,1)}, bf16[512,512]{1,0:T(8,128)(2,1)}, bf16[256,512]{1,0:T(8,128)(2,1)}, bf16[128,512]{1,0:T(8,128)(2,1)}, bf16[64,512]{1,0:T(8,128)(2,1)}) custom-call(bf16[1024,1024]{1,0:T(8,128)(2,1)} %refs_1_.17, bf16[1024,256]{1,0:T(8,128)(2,1)} %refs_5_.1, bf16[1024,256]{1,0:T(8,128)(2,1)} %refs_6_.1, ...), custom_call_target="tpu_custom_call" | custom-call | flops 5750000128 | bytes 1 | tf_op jit(solution)/shard_map/pallas_call | solution.py:42
  6.0 4.1 %collective-permute-start.1 = (bf16[64,512]{1,0:T(8,128)(2,1)}, bf16[64,512]{1,0:T(8,128)(2,1)S(1)}, u32[]{:S(2)}, u32[]{:S(2)}) collective-permute-start(bf16[64,512]{1,0:T(8,128)(2,1)} %get-tuple-element.60), channel_id=1, source_target_pairs={{0,8},{4,12},{8,0},{12,4},{1,9},{5,13},{9,1},{13,5},{2,10},{6,14},... | collective-permute-start | bytes 196616 | tf_op jit(solution)/shard_map/ppermute | solution.py:483
  10.1 1.3 %collective-permute-start.2 = (bf16[64,512]{1,0:T(8,128)(2,1)}, bf16[64,512]{1,0:T(8,128)(2,1)S(1)}, u32[]{:S(2)}, u32[]{:S(2)}) collective-permute-start(bf16[64,512]{1,0:T(8,128)(2,1)} %get-tuple-element.60), channel_id=1, source_target_pairs={{0,12},{4,8},{8,4},{12,0},{1,13},{5,9},{9,5},{13,1},{2,14},{6,10},... | collective-permute-start | bytes 196616 | tf_op jit(solution)/shard_map/ppermute | solution.py:483
  11.7 0.7 shard_map.109.refs_0_.refs_4_
  12.5 2.3 %shard_map.111 = (f32[4096,256]{1,0:T(8,128)S(1)}, f32[4,1024]{1,0:T(4,128)S(1)}) custom-call(bf16[1024,256]{1,0:T(8,128)(2,1)S(1)} %shard_map.109.refs_0_.refs_4_, bf16[1024,512]{1,0:T(8,128)(2,1)S(1)} %copy-done.6, bf16[512,512]{1,0:T(8,128)(2,1)S(1)} %copy-done.7, bf16[256,512]{1,0:T(8,128)(2,1)S(1)} %copy-done.8, ...), custom_call_target="tpu_custom_call" | custom-call | flops 2644999936 | bytes 1 | tf_op jit(solution)/shard_map/pallas_call | solution.py:42
  14.9 0.7 shard_map.112.refs_9_.refs_1_
  15.6 1.5 %collective-permute-done.2.refs_8_.refs_10_ = bf16[64,512]{1,0:T(8,128)(2,1)S(1)} collective-permute-done((bf16[64,512]{1,0:T(8,128)(2,1)}, bf16[64,512]{1,0:T(8,128)(2,1)S(1)}, u32[]{:S(2)}, u32[]{:S(2)}) %collective-permute-start.2) | collective-permute-done | bytes 65568 | tf_op jit(solution)/shard_map/ppermute | solution.py:483
  17.1 0.8 collective-permute-done.refs_6_.refs_8_
  17.9 3.9 %shard_map.113 = (bf16[1024,256]{1,0:T(8,128)(2,1)S(1)}, bf16[256,1024]{1,0:T(8,128)(2,1)S(1)}, f32[4,1024]{1,0:T(4,128)S(1)}) custom-call(bf16[1024,256]{1,0:T(8,128)(2,1)S(1)} %shard_map.109.refs_0_.refs_4_, f32[4096,256]{1,0:T(8,128)S(1)} %get-tuple-element.57.refs_2_.refs_1_, f32[4,1024]{1,0:T(4,128)S(1)} %get-tuple-element.58.refs_2_, ...), custom_call_target="tpu_custom_call" | custom-call | flops 4600000000 | bytes 1 | tf_op jit(solution)/shard_map/pallas_call | solution.py:42
  21.8 0.5 shard_map.114.refs_2_.refs_0_
  22.8 1.0 %collective-permute-start.6 = (bf16[512,256]{1,0:T(8,128)(2,1)S(1)}, bf16[512,256]{1,0:T(8,128)(2,1)S(1)}, u32[]{:S(2)}, u32[]{:S(2)}) collective-permute-start(bf16[512,256]{1,0:T(8,128)(2,1)S(1)} %shard_map.114.refs_2_.refs_0_), channel_id=1, source_target_pairs={{0,4},{4,0},{8,12},{12,8},{1,5},{5,1},{9,13},{13,9},{2,6},{6,2},{1... | collective-permute-start | bytes 786440 | tf_op jit(solution)/shard_map/ppermute | solution.py:483
  23.8 1.1 %collective-permute-start.8 = (bf16[512,256]{1,0:T(8,128)(2,1)S(1)}, bf16[512,256]{1,0:T(8,128)(2,1)S(1)}, u32[]{:S(2)}, u32[]{:S(2)}) collective-permute-start(bf16[512,256]{1,0:T(8,128)(2,1)S(1)} %shard_map.115.refs_11_.refs_0_), channel_id=1, source_target_pairs={{0,4},{4,0},{8,12},{12,8},{1,5},{5,1},{9,13},{13,9},{2,6},{6,2},{1... | collective-permute-start | bytes 786440 | tf_op jit(solution)/shard_map/ppermute | solution.py:483
  24.9 6.9 %shard_map.116 = (bf16[1024,256]{1,0:T(8,128)(2,1)S(1)}, f32[1024,512]{1,0:T(8,128)S(1)}, bf16[768,256]{1,0:T(8,128)(2,1)S(1)}, bf16[512,256]{1,0:T(8,128)(2,1)S...) custom-call(bf16[1024,256]{1,0:T(8,128)(2,1)S(1)} %shard_map.109.refs_0_.refs_4_, ...), custom_call_target="tpu_custom_call" | custom-call | flops 9200000000 | bytes 1 | tf_op jit(solution)/shard_map/pallas_call | solution.py:42
  31.8 1.0 %collective-permute-start.3 = (bf16[768,256]{1,0:T(8,128)(2,1)S(1)}, bf16[768,256]{1,0:T(8,128)(2,1)S(1)}, u32[]{:S(2)}, u32[]{:S(2)}) collective-permute-start(bf16[768,256]{1,0:T(8,128)(2,1)S(1)} %get-tuple-element.64.refs_0_), channel_id=1, source_target_pairs={{0,4},{4,0},{8,12},{12,8},{1,5},{5,1},{9,13},{13,9},{2,6},{6,2},{1... | collective-permute-start | bytes 1179656 | tf_op jit(solution)/shard_map/ppermute | solution.py:483
  32.8 2.8 %collective-permute-start.4 = (bf16[64,512]{1,0:T(8,128)(2,1)S(1)}, bf16[64,512]{1,0:T(8,128)(2,1)S(1)}, u32[]{:S(2)}, u32[]{:S(2)}) collective-permute-start(bf16[64,512]{1,0:T(8,128)(2,1)S(1)} %get-tuple-element.66), channel_id=1, source_target_pairs={{0,8},{4,12},{8,0},{12,4},{1,9},{5,13},{9,1},{13,5},{2,10},{6,14},... | collective-permute-start | bytes 196616 | tf_op jit(solution)/shard_map/ppermute | solution.py:483
  35.7 0.6 collective-permute-start.5
  36.4 2.7 %collective-permute-done.8.refs_1_ = bf16[512,256]{1,0:T(8,128)(2,1)S(1)} collective-permute-done((bf16[512,256]{1,0:T(8,128)(2,1)S(1)}, bf16[512,256]{1,0:T(8,128)(2,1)S(1)}, u32[]{:S(2)}, u32[]{:S(2)}) %collective-permute-start.8) | collective-permute-done | bytes 262176 | tf_op jit(solution)/shard_map/ppermute | solution.py:483
  39.4 8.3 %collective-permute-start.10 = (bf16[512,256]{1,0:T(8,128)(2,1)S(1)}, bf16[512,256]{1,0:T(8,128)(2,1)S(1)}, u32[]{:S(2)}, u32[]{:S(2)}) collective-permute-start(bf16[512,256]{1,0:T(8,128)(2,1)S(1)} %get-tuple-element.75), channel_id=1, source_target_pairs={{0,4},{4,0},{8,12},{12,8},{1,5},{5,1},{9,13},{13,9},{2,6},{6,2},{1... | collective-permute-start | bytes 786440 | tf_op jit(solution)/shard_map/ppermute | solution.py:483
  47.7 2.4 %collective-permute-done.5.refs_3_ = bf16[64,512]{1,0:T(8,128)(2,1)S(1)} collective-permute-done((bf16[64,512]{1,0:T(8,128)(2,1)S(1)}, bf16[64,512]{1,0:T(8,128)(2,1)S(1)}, u32[]{:S(2)}, u32[]{:S(2)}) %collective-permute-start.5) | collective-permute-done | bytes 65568 | tf_op jit(solution)/shard_map/ppermute | solution.py:483
  50.1 1.0 %shard_map.120 = (bf16[1024,256]{1,0:T(8,128)(2,1)S(1)}, bf16[1024,256]{1,0:T(8,128)(2,1)S(1)}, bf16[512,1024]{1,0:T(8,128)(2,1)S(1)}) custom-call(f32[1024,512]{1,0:T(8,128)S(1)} %get-tuple-element.65.refs_0_, bf16[768,256]{1,0:T(8,128)(2,1)S(1)} %collective-permute-done.3.refs_1_, bf16[64,512]{1,0:T(8,128)(2,1)S(1)} %collective-permute-done.4.refs_2_, ...), custom_call_target="tpu_custom_call" | custom-call | flops 230000000 | bytes 1 | tf_op jit(solution)/shard_map/pallas_call | solution.py:42
  51.2 0.5 shard_map.121.refs_2_.refs_3_.refs_0_
  51.8 0.7 shard_map.123
  52.7 2.3 %collective-permute-start.14 = (bf16[512,256]{1,0:T(8,128)(2,1)S(1)}, bf16[512,256]{1,0:T(8,128)(2,1)S(1)}, u32[]{:S(2)}, u32[]{:S(2)}) collective-permute-start(bf16[512,256]{1,0:T(8,128)(2,1)S(1)} %get-tuple-element.80), channel_id=1, source_target_pairs={{0,4},{4,0},{8,12},{12,8},{1,5},{5,1},{9,13},{13,9},{2,6},{6,2},{1... | collective-permute-start | bytes 786440 | tf_op jit(solution)/shard_map/ppermute | solution.py:483
  55.1 0.6 collective-permute-start.12
  55.6 0.5 shard_map.126.refs_3_.refs_4_.refs_0_
  56.5 2.9 %collective-permute-start.18 = (bf16[512,256]{1,0:T(8,128)(2,1)S(1)}, bf16[512,256]{1,0:T(8,128)(2,1)S(1)}, u32[]{:S(2)}, u32[]{:S(2)}) collective-permute-start(bf16[512,256]{1,0:T(8,128)(2,1)S(1)} %get-tuple-element.86), channel_id=1, source_target_pairs={{0,4},{4,0},{8,12},{12,8},{1,5},{5,1},{9,13},{13,9},{2,6},{6,2},{1... | collective-permute-start | bytes 786440 | tf_op jit(solution)/shard_map/ppermute | solution.py:483
  59.4 0.5 shard_map.128.refs_7_.refs_3_.refs_0_
  59.9 1.8 %shard_map.129 = (bf16[1024,512]{1,0:T(8,128)(2,1)S(1)}, bf16[1024,512]{1,0:T(8,128)(2,1)S(1)}) custom-call(s32[1]{0:T(128)} %bitcast.refs_4_.refs_0_, bf16[1024,256]{1,0:T(8,128)(2,1)S(1)} %get-tuple-element.68.refs_2_.refs_1_, bf16[1024,256]{1,0:T(8,128)(2,1)S(1)} %get-tuple-element.72.refs_2_, bf16[1024,256]{1,0:T(8,128)(2,1)S(1)} %get-tuple-element.78.refs_3_, ...), custom_call_target="tpu_custom_call" | custom-call | flops 1150000000 | bytes 1 | tf_op jit(solution)/shard_map/pallas_call | solution.py:42
  62.3 0.6 collective-permute-start.21
  63.0 2.2 %collective-permute-start.16 = (bf16[512,256]{1,0:T(8,128)(2,1)S(1)}, bf16[512,256]{1,0:T(8,128)(2,1)S(1)}, u32[]{:S(2)}, u32[]{:S(2)}) collective-permute-start(bf16[512,256]{1,0:T(8,128)(2,1)S(1)} %get-tuple-element.85), channel_id=1, source_target_pairs={{0,4},{4,0},{8,12},{12,8},{1,5},{5,1},{9,13},{13,9},{2,6},{6,2},{1... | collective-permute-start | bytes 786440 | tf_op jit(solution)/shard_map/ppermute | solution.py:483
  65.4 0.5 shard_map.134.refs_2_.refs_3_.refs_0_
  65.9 1.7 %collective-permute-done.18.refs_1_.refs_3_ = bf16[512,256]{1,0:T(8,128)(2,1)S(1)} collective-permute-done((bf16[512,256]{1,0:T(8,128)(2,1)S(1)}, bf16[512,256]{1,0:T(8,128)(2,1)S(1)}, u32[]{:S(2)}, u32[]{:S(2)}) %collective-permute-start.18) | collective-permute-done | bytes 262176 | tf_op jit(solution)/shard_map/ppermute | solution.py:483
  67.8 1.6 %collective-permute-start.15 = (bf16[1024,256]{1,0:T(8,128)(2,1)S(1)}, bf16[1024,256]{1,0:T(8,128)(2,1)S(1)}, u32[]{:S(2)}, u32[]{:S(2)}) collective-permute-start(bf16[1024,256]{1,0:T(8,128)(2,1)S(1)} %get-tuple-element.84), channel_id=1, source_target_pairs={{0,2},{1,3},{2,0},{3,1},{4,6},{5,7},{6,4},{7,5},{8,10},{9,11},{10,... | collective-permute-start | bytes 1572872 | tf_op jit(solution)/shard_map/ppermute | solution.py:483
  69.4 1.3 %collective-permute-start.20 = (bf16[512,256]{1,0:T(8,128)(2,1)S(1)}, bf16[512,256]{1,0:T(8,128)(2,1)S(1)}, u32[]{:S(2)}, u32[]{:S(2)}) collective-permute-start(bf16[512,256]{1,0:T(8,128)(2,1)S(1)} %get-tuple-element.89), channel_id=1, source_target_pairs={{0,4},{4,0},{8,12},{12,8},{1,5},{5,1},{9,13},{13,9},{2,6},{6,2},{1... | collective-permute-start | bytes 786440 | tf_op jit(solution)/shard_map/ppermute | solution.py:483
  70.8 0.8 shard_map.137
  71.6 1.5 %collective-permute-done.16.refs_1_.refs_4_ = bf16[512,256]{1,0:T(8,128)(2,1)S(1)} collective-permute-done((bf16[512,256]{1,0:T(8,128)(2,1)S(1)}, bf16[512,256]{1,0:T(8,128)(2,1)S(1)}, u32[]{:S(2)}, u32[]{:S(2)}) %collective-permute-start.16) | collective-permute-done | bytes 262176 | tf_op jit(solution)/shard_map/ppermute | solution.py:483
  73.3 2.4 %collective-permute-start.25 = (bf16[512,256]{1,0:T(8,128)(2,1)S(1)}, bf16[512,256]{1,0:T(8,128)(2,1)S(1)}, u32[]{:S(2)}, u32[]{:S(2)}) collective-permute-start(bf16[512,256]{1,0:T(8,128)(2,1)S(1)} %shard_map.139.refs_2_), channel_id=1, source_target_pairs={{0,4},{4,0},{8,12},{12,8},{1,5},{5,1},{9,13},{13,9},{2,6},{6,2},{1... | collective-permute-start | bytes 786440 | tf_op jit(solution)/shard_map/ppermute | solution.py:483
  75.9 2.8 %collective-permute-done.20.refs_1_.refs_3_ = bf16[512,256]{1,0:T(8,128)(2,1)S(1)} collective-permute-done((bf16[512,256]{1,0:T(8,128)(2,1)S(1)}, bf16[512,256]{1,0:T(8,128)(2,1)S(1)}, u32[]{:S(2)}, u32[]{:S(2)}) %collective-permute-start.20) | collective-permute-done | bytes 262176 | tf_op jit(solution)/shard_map/ppermute | solution.py:483
  78.9 1.7 %collective-permute-start.23 = (bf16[1024,256]{1,0:T(8,128)(2,1)S(1)}, bf16[1024,256]{1,0:T(8,128)(2,1)S(1)}, u32[]{:S(2)}, u32[]{:S(2)}) collective-permute-start(bf16[1024,256]{1,0:T(8,128)(2,1)S(1)} %get-tuple-element.93), channel_id=1, source_target_pairs={{0,2},{1,3},{2,0},{3,1},{4,6},{5,7},{6,4},{7,5},{8,10},{9,11},{10,... | collective-permute-start | bytes 1572872 | tf_op jit(solution)/shard_map/ppermute | solution.py:483
  80.6 0.8 shard_map.142
  81.5 2.8 %collective-permute-start.26 = (bf16[512,256]{1,0:T(8,128)(2,1)S(1)}, bf16[512,256]{1,0:T(8,128)(2,1)S(1)}, u32[]{:S(2)}, u32[]{:S(2)}) collective-permute-start(bf16[512,256]{1,0:T(8,128)(2,1)S(1)} %shard_map.143.refs_2_.refs_1_), channel_id=1, source_target_pairs={{0,4},{4,0},{8,12},{12,8},{1,5},{5,1},{9,13},{13,9},{2,6},{6,2},{1... | collective-permute-start | bytes 786440 | tf_op jit(solution)/shard_map/ppermute | solution.py:483
  84.3 0.9 shard_map.144
  85.2 0.8 shard_map.145
  86.1 1.5 %collective-permute-start.27 = (bf16[512,256]{1,0:T(8,128)(2,1)S(1)}, bf16[512,256]{1,0:T(8,128)(2,1)S(1)}, u32[]{:S(2)}, u32[]{:S(2)}) collective-permute-start(bf16[512,256]{1,0:T(8,128)(2,1)S(1)} %shard_map.146.refs_2_), channel_id=1, source_target_pairs={{0,4},{4,0},{8,12},{12,8},{1,5},{5,1},{9,13},{13,9},{2,6},{6,2},{1... | collective-permute-start | bytes 786440 | tf_op jit(solution)/shard_map/ppermute | solution.py:483
  87.6 5.7 %collective-permute-done.23.refs_1_ = bf16[1024,256]{1,0:T(8,128)(2,1)S(1)} collective-permute-done((bf16[1024,256]{1,0:T(8,128)(2,1)S(1)}, bf16[1024,256]{1,0:T(8,128)(2,1)S(1)}, u32[]{:S(2)}, u32[]{:S(2)}) %collective-permute-start.23) | collective-permute-done | bytes 524320 | tf_op jit(solution)/shard_map/ppermute | solution.py:483
  93.3 0.9 shard_map.147
  94.2 1.3 %collective-permute-done.27.refs_4_ = bf16[512,256]{1,0:T(8,128)(2,1)S(1)} collective-permute-done((bf16[512,256]{1,0:T(8,128)(2,1)S(1)}, bf16[512,256]{1,0:T(8,128)(2,1)S(1)}, u32[]{:S(2)}, u32[]{:S(2)}) %collective-permute-start.27) | collective-permute-done | bytes 262176 | tf_op jit(solution)/shard_map/ppermute | solution.py:483
  95.5 0.8 shard_map.148
  (66 shorter events, 3.6 us)
Async XLA Ops:
  0.6 11.1 %copy-start = (bf16[1024,1024]{1,0:T(8,128)(2,1)S(1)}, bf16[1024,1024]{1,0:T(8,128)(2,1)}, u32[]{:S(2)}) copy-start(bf16[1024,1024]{1,0:T(8,128)(2,1)} %refs_1_.17) | copy-start | bytes 6291460
  0.7 11.1 %copy-start.3 = (bf16[1024,256]{1,0:T(8,128)(2,1)S(1)}, bf16[1024,256]{1,0:T(8,128)(2,1)}, u32[]{:S(2)}) copy-start(bf16[1024,256]{1,0:T(8,128)(2,1)} %refs_4_.3) | copy-start | bytes 1572868
  6.0 6.4 %copy-start.6 = (bf16[1024,512]{1,0:T(8,128)(2,1)S(1)}, bf16[1024,512]{1,0:T(8,128)(2,1)}, u32[]{:S(2)}) copy-start(bf16[1024,512]{1,0:T(8,128)(2,1)} %get-tuple-element.54.refs_1_.refs_3_.refs_5_) | copy-start | bytes 3145732
  6.0 6.4 %copy-start.7 = (bf16[512,512]{1,0:T(8,128)(2,1)S(1)}, bf16[512,512]{1,0:T(8,128)(2,1)}, u32[]{:S(2)}) copy-start(bf16[512,512]{1,0:T(8,128)(2,1)} %get-tuple-element.55.refs_2_.refs_4_.refs_6_) | copy-start | bytes 1572868
  6.0 6.4 %copy-start.8 = (bf16[256,512]{1,0:T(8,128)(2,1)S(1)}, bf16[256,512]{1,0:T(8,128)(2,1)}, u32[]{:S(2)}) copy-start(bf16[256,512]{1,0:T(8,128)(2,1)} %get-tuple-element.56.refs_3_.refs_5_.refs_7_) | copy-start | bytes 786436
  6.0 9.5 %collective-permute-start.1 = (bf16[64,512]{1,0:T(8,128)(2,1)}, bf16[64,512]{1,0:T(8,128)(2,1)S(1)}, u32[]{:S(2)}, u32[]{:S(2)}) collective-permute-start(bf16[64,512]{1,0:T(8,128)(2,1)} %get-tuple-element.60), channel_id=1, source_target_pairs={{0,8},{4,12},{8,0},{12,4},{1,9},{5,13},{9,1},{13,5},{2,10},{6,14},... | collective-permute-start | bytes 196616 | tf_op jit(solution)/shard_map/ppermute | solution.py:483
  10.1 7.0 %collective-permute-start.2 = (bf16[64,512]{1,0:T(8,128)(2,1)}, bf16[64,512]{1,0:T(8,128)(2,1)S(1)}, u32[]{:S(2)}, u32[]{:S(2)}) collective-permute-start(bf16[64,512]{1,0:T(8,128)(2,1)} %get-tuple-element.60), channel_id=1, source_target_pairs={{0,12},{4,8},{8,4},{12,0},{1,13},{5,9},{9,5},{13,1},{2,14},{6,10},... | collective-permute-start | bytes 196616 | tf_op jit(solution)/shard_map/ppermute | solution.py:483
  11.5 6.4 %collective-permute-start = (bf16[128,512]{1,0:T(8,128)(2,1)}, bf16[128,512]{1,0:T(8,128)(2,1)S(1)}, u32[]{:S(2)}, u32[]{:S(2)}) collective-permute-start(bf16[128,512]{1,0:T(8,128)(2,1)} %get-tuple-element.59), channel_id=1, source_target_pairs={{0,4},{4,0},{8,12},{12,8},{1,5},{5,1},{9,13},{13,9},{2,6},{6,2},{1... | collective-permute-start | bytes 393224 | tf_op jit(solution)/shard_map/ppermute | solution.py:483
  12.5 2.4 %copy-start.1 = (bf16[1024,1024]{1,0:T(8,128)(2,1)S(1)}, bf16[1024,1024]{1,0:T(8,128)(2,1)}, u32[]{:S(2)}) copy-start(bf16[1024,1024]{1,0:T(8,128)(2,1)} %refs_1_.13) | copy-start | bytes 6291460
  12.5 2.4 %copy-start.2 = (bf16[1024,256]{1,0:T(8,128)(2,1)S(1)}, bf16[1024,256]{1,0:T(8,128)(2,1)}, u32[]{:S(2)}) copy-start(bf16[1024,256]{1,0:T(8,128)(2,1)} %refs_2_.3) | copy-start | bytes 1572868
  22.8 13.5 %collective-permute-start.6 = (bf16[512,256]{1,0:T(8,128)(2,1)S(1)}, bf16[512,256]{1,0:T(8,128)(2,1)S(1)}, u32[]{:S(2)}, u32[]{:S(2)}) collective-permute-start(bf16[512,256]{1,0:T(8,128)(2,1)S(1)} %shard_map.114.refs_2_.refs_0_), channel_id=1, source_target_pairs={{0,4},{4,0},{8,12},{12,8},{1,5},{5,1},{9,13},{13,9},{2,6},{6,2},{1... | collective-permute-start | bytes 786440 | tf_op jit(solution)/shard_map/ppermute | solution.py:483
  23.8 15.3 %collective-permute-start.8 = (bf16[512,256]{1,0:T(8,128)(2,1)S(1)}, bf16[512,256]{1,0:T(8,128)(2,1)S(1)}, u32[]{:S(2)}, u32[]{:S(2)}) collective-permute-start(bf16[512,256]{1,0:T(8,128)(2,1)S(1)} %shard_map.115.refs_11_.refs_0_), channel_id=1, source_target_pairs={{0,4},{4,0},{8,12},{12,8},{1,5},{5,1},{9,13},{13,9},{2,6},{6,2},{1... | collective-permute-start | bytes 786440 | tf_op jit(solution)/shard_map/ppermute | solution.py:483
  31.8 18.3 %collective-permute-start.3 = (bf16[768,256]{1,0:T(8,128)(2,1)S(1)}, bf16[768,256]{1,0:T(8,128)(2,1)S(1)}, u32[]{:S(2)}, u32[]{:S(2)}) collective-permute-start(bf16[768,256]{1,0:T(8,128)(2,1)S(1)} %get-tuple-element.64.refs_0_), channel_id=1, source_target_pairs={{0,4},{4,0},{8,12},{12,8},{1,5},{5,1},{9,13},{13,9},{2,6},{6,2},{1... | collective-permute-start | bytes 1179656 | tf_op jit(solution)/shard_map/ppermute | solution.py:483
  32.8 14.9 %collective-permute-start.4 = (bf16[64,512]{1,0:T(8,128)(2,1)S(1)}, bf16[64,512]{1,0:T(8,128)(2,1)S(1)}, u32[]{:S(2)}, u32[]{:S(2)}) collective-permute-start(bf16[64,512]{1,0:T(8,128)(2,1)S(1)} %get-tuple-element.66), channel_id=1, source_target_pairs={{0,8},{4,12},{8,0},{12,4},{1,9},{5,13},{9,1},{13,5},{2,10},{6,14},... | collective-permute-start | bytes 196616 | tf_op jit(solution)/shard_map/ppermute | solution.py:483
  35.7 14.5 %collective-permute-start.5 = (bf16[64,512]{1,0:T(8,128)(2,1)S(1)}, bf16[64,512]{1,0:T(8,128)(2,1)S(1)}, u32[]{:S(2)}, u32[]{:S(2)}) collective-permute-start(bf16[64,512]{1,0:T(8,128)(2,1)S(1)} %get-tuple-element.67), channel_id=1, source_target_pairs={{0,12},{4,8},{8,4},{12,0},{1,13},{5,9},{9,5},{13,1},{2,14},{6,10},... | collective-permute-start | bytes 196616 | tf_op jit(solution)/shard_map/ppermute | solution.py:483
  36.4 2.9 %collective-permute-start.7 = (bf16[512,256]{1,0:T(8,128)(2,1)S(1)}, bf16[512,256]{1,0:T(8,128)(2,1)S(1)}, u32[]{:S(2)}, u32[]{:S(2)}) collective-permute-start(bf16[512,256]{1,0:T(8,128)(2,1)S(1)} %shard_map.117.refs_2_.refs_1_), channel_id=1, source_target_pairs={{0,1},{1,0},{2,3},{3,2},{4,8},{5,9},{6,10},{7,11},{8,4},{9,5},{10,... | collective-permute-start | bytes 786440 | tf_op jit(solution)/shard_map/ppermute | solution.py:640
  39.2 13.4 %collective-permute-start.11 = (bf16[512,256]{1,0:T(8,128)(2,1)S(1)}, bf16[512,256]{1,0:T(8,128)(2,1)S(1)}, u32[]{:S(2)}, u32[]{:S(2)}) collective-permute-start(bf16[512,256]{1,0:T(8,128)(2,1)S(1)} %shard_map.118.refs_4_.refs_1_), channel_id=1, source_target_pairs={{0,1},{1,0},{2,3},{3,2},{4,8},{5,9},{6,10},{7,11},{8,4},{9,5},{10,... | collective-permute-start | bytes 786440 | tf_op jit(solution)/shard_map/ppermute | solution.py:640
  39.4 15.6 %collective-permute-start.10 = (bf16[512,256]{1,0:T(8,128)(2,1)S(1)}, bf16[512,256]{1,0:T(8,128)(2,1)S(1)}, u32[]{:S(2)}, u32[]{:S(2)}) collective-permute-start(bf16[512,256]{1,0:T(8,128)(2,1)S(1)} %get-tuple-element.75), channel_id=1, source_target_pairs={{0,4},{4,0},{8,12},{12,8},{1,5},{5,1},{9,13},{13,9},{2,6},{6,2},{1... | collective-permute-start | bytes 786440 | tf_op jit(solution)/shard_map/ppermute | solution.py:483
  51.8 4.4 %collective-permute-start.13 = (bf16[512,256]{1,0:T(8,128)(2,1)S(1)}, bf16[512,256]{1,0:T(8,128)(2,1)S(1)}, u32[]{:S(2)}, u32[]{:S(2)}) collective-permute-start(bf16[512,256]{1,0:T(8,128)(2,1)S(1)} %shard_map.122.refs_3_.refs_1_), channel_id=1, source_target_pairs={{0,1},{1,0},{2,3},{3,2},{4,8},{5,9},{6,10},{7,11},{8,4},{9,5},{10,... | collective-permute-start | bytes 786440 | tf_op jit(solution)/shard_map/ppermute | solution.py:640
  52.7 9.4 %collective-permute-start.14 = (bf16[512,256]{1,0:T(8,128)(2,1)S(1)}, bf16[512,256]{1,0:T(8,128)(2,1)S(1)}, u32[]{:S(2)}, u32[]{:S(2)}) collective-permute-start(bf16[512,256]{1,0:T(8,128)(2,1)S(1)} %get-tuple-element.80), channel_id=1, source_target_pairs={{0,4},{4,0},{8,12},{12,8},{1,5},{5,1},{9,13},{13,9},{2,6},{6,2},{1... | collective-permute-start | bytes 786440 | tf_op jit(solution)/shard_map/ppermute | solution.py:483
  55.0 10.2 %collective-permute-start.9 = (bf16[1024,512]{1,0:T(8,128)(2,1)S(1)}, bf16[1024,512]{1,0:T(8,128)(2,1)S(1)}, u32[]{:S(2)}, u32[]{:S(2)}) collective-permute-start(bf16[1024,512]{1,0:T(8,128)(2,1)S(1)} %get-tuple-element.74), channel_id=1, source_target_pairs={{0,1},{1,0},{2,3},{3,2},{4,5},{5,4},{6,7},{7,6},{8,9},{9,8},{10,11... | collective-permute-start | bytes 3145736 | tf_op jit(solution)/shard_map/ppermute | solution.py:483
  55.1 7.8 %collective-permute-start.12 = (bf16[512,256]{1,0:T(8,128)(2,1)S(1)}, bf16[512,256]{1,0:T(8,128)(2,1)S(1)}, u32[]{:S(2)}, u32[]{:S(2)}) collective-permute-start(bf16[512,256]{1,0:T(8,128)(2,1)S(1)} %shard_map.125.refs_2_.refs_1_), channel_id=1, source_target_pairs={{0,1},{1,0},{2,3},{3,2},{4,8},{5,9},{6,10},{7,11},{8,4},{9,5},{10,... | collective-permute-start | bytes 786440 | tf_op jit(solution)/shard_map/ppermute | solution.py:640
  56.4 3.4 %copy-start.4 = (bf16[1024,256]{1,0:T(8,128)(2,1)S(1)}, bf16[1024,256]{1,0:T(8,128)(2,1)}, u32[]{:S(2)}) copy-start(bf16[1024,256]{1,0:T(8,128)(2,1)} %refs_5_.1) | copy-start | bytes 1572868
  56.5 3.4 %copy-start.5 = (bf16[1024,256]{1,0:T(8,128)(2,1)S(1)}, bf16[1024,256]{1,0:T(8,128)(2,1)}, u32[]{:S(2)}) copy-start(bf16[1024,256]{1,0:T(8,128)(2,1)} %refs_6_.1) | copy-start | bytes 1572868
  56.5 11.1 %collective-permute-start.18 = (bf16[512,256]{1,0:T(8,128)(2,1)S(1)}, bf16[512,256]{1,0:T(8,128)(2,1)S(1)}, u32[]{:S(2)}, u32[]{:S(2)}) collective-permute-start(bf16[512,256]{1,0:T(8,128)(2,1)S(1)} %get-tuple-element.86), channel_id=1, source_target_pairs={{0,4},{4,0},{8,12},{12,8},{1,5},{5,1},{9,13},{13,9},{2,6},{6,2},{1... | collective-permute-start | bytes 786440 | tf_op jit(solution)/shard_map/ppermute | solution.py:483
  62.2 7.2 %collective-permute-start.17 = (bf16[512,256]{1,0:T(8,128)(2,1)S(1)}, bf16[512,256]{1,0:T(8,128)(2,1)S(1)}, u32[]{:S(2)}, u32[]{:S(2)}) collective-permute-start(bf16[512,256]{1,0:T(8,128)(2,1)S(1)} %shard_map.130.refs_1_), channel_id=1, source_target_pairs={{0,1},{1,0},{2,3},{3,2},{4,8},{5,9},{6,10},{7,11},{8,4},{9,5},{10,... | collective-permute-start | bytes 786440 | tf_op jit(solution)/shard_map/ppermute | solution.py:640
  62.3 13.3 %collective-permute-start.21 = (bf16[1024,512]{1,0:T(8,128)(2,1)S(1)}, bf16[1024,512]{1,0:T(8,128)(2,1)S(1)}, u32[]{:S(2)}, u32[]{:S(2)}) collective-permute-start(bf16[1024,512]{1,0:T(8,128)(2,1)S(1)} %shard_map.131.refs_4_), channel_id=1, source_target_pairs={{0,1},{1,0},{2,3},{3,2},{4,5},{5,4},{6,7},{7,6},{8,9},{9,8},{10,11... | collective-permute-start | bytes 3145736 | tf_op jit(solution)/shard_map/ppermute | solution.py:483
  63.0 10.1 %collective-permute-start.16 = (bf16[512,256]{1,0:T(8,128)(2,1)S(1)}, bf16[512,256]{1,0:T(8,128)(2,1)S(1)}, u32[]{:S(2)}, u32[]{:S(2)}) collective-permute-start(bf16[512,256]{1,0:T(8,128)(2,1)S(1)} %get-tuple-element.85), channel_id=1, source_target_pairs={{0,4},{4,0},{8,12},{12,8},{1,5},{5,1},{9,13},{13,9},{2,6},{6,2},{1... | collective-permute-start | bytes 786440 | tf_op jit(solution)/shard_map/ppermute | solution.py:483
  67.7 5.6 %collective-permute-start.22 = (bf16[512,256]{1,0:T(8,128)(2,1)S(1)}, bf16[512,256]{1,0:T(8,128)(2,1)S(1)}, u32[]{:S(2)}, u32[]{:S(2)}) collective-permute-start(bf16[512,256]{1,0:T(8,128)(2,1)S(1)} %shard_map.135.refs_4_.refs_0_), channel_id=1, source_target_pairs={{0,1},{1,0},{2,3},{3,2},{4,8},{5,9},{6,10},{7,11},{8,4},{9,5},{10,... | collective-permute-start | bytes 786440 | tf_op jit(solution)/shard_map/ppermute | solution.py:640
  67.8 16.6 %collective-permute-start.15 = (bf16[1024,256]{1,0:T(8,128)(2,1)S(1)}, bf16[1024,256]{1,0:T(8,128)(2,1)S(1)}, u32[]{:S(2)}, u32[]{:S(2)}) collective-permute-start(bf16[1024,256]{1,0:T(8,128)(2,1)S(1)} %get-tuple-element.84), channel_id=1, source_target_pairs={{0,2},{1,3},{2,0},{3,1},{4,6},{5,7},{6,4},{7,5},{8,10},{9,11},{10,... | collective-permute-start | bytes 1572872 | tf_op jit(solution)/shard_map/ppermute | solution.py:483
  69.4 9.3 %collective-permute-start.20 = (bf16[512,256]{1,0:T(8,128)(2,1)S(1)}, bf16[512,256]{1,0:T(8,128)(2,1)S(1)}, u32[]{:S(2)}, u32[]{:S(2)}) collective-permute-start(bf16[512,256]{1,0:T(8,128)(2,1)S(1)} %get-tuple-element.89), channel_id=1, source_target_pairs={{0,4},{4,0},{8,12},{12,8},{1,5},{5,1},{9,13},{13,9},{2,6},{6,2},{1... | collective-permute-start | bytes 786440 | tf_op jit(solution)/shard_map/ppermute | solution.py:483
  73.2 8.2 %collective-permute-start.19 = (bf16[512,256]{1,0:T(8,128)(2,1)S(1)}, bf16[512,256]{1,0:T(8,128)(2,1)S(1)}, u32[]{:S(2)}, u32[]{:S(2)}) collective-permute-start(bf16[512,256]{1,0:T(8,128)(2,1)S(1)} %shard_map.138.refs_2_.refs_0_), channel_id=1, source_target_pairs={{0,1},{1,0},{2,3},{3,2},{4,8},{5,9},{6,10},{7,11},{8,4},{9,5},{10,... | collective-permute-start | bytes 786440 | tf_op jit(solution)/shard_map/ppermute | solution.py:640
  73.3 11.9 %collective-permute-start.25 = (bf16[512,256]{1,0:T(8,128)(2,1)S(1)}, bf16[512,256]{1,0:T(8,128)(2,1)S(1)}, u32[]{:S(2)}, u32[]{:S(2)}) collective-permute-start(bf16[512,256]{1,0:T(8,128)(2,1)S(1)} %shard_map.139.refs_2_), channel_id=1, source_target_pairs={{0,4},{4,0},{8,12},{12,8},{1,5},{5,1},{9,13},{13,9},{2,6},{6,2},{1... | collective-permute-start | bytes 786440 | tf_op jit(solution)/shard_map/ppermute | solution.py:483
  78.8 7.3 %collective-permute-start.24 = (bf16[512,256]{1,0:T(8,128)(2,1)S(1)}, bf16[512,256]{1,0:T(8,128)(2,1)S(1)}, u32[]{:S(2)}, u32[]{:S(2)}) collective-permute-start(bf16[512,256]{1,0:T(8,128)(2,1)S(1)} %shard_map.141.refs_5_.refs_0_), channel_id=1, source_target_pairs={{0,1},{1,0},{2,3},{3,2},{4,8},{5,9},{6,10},{7,11},{8,4},{9,5},{10,... | collective-permute-start | bytes 786440 | tf_op jit(solution)/shard_map/ppermute | solution.py:640
  78.9 14.5 %collective-permute-start.23 = (bf16[1024,256]{1,0:T(8,128)(2,1)S(1)}, bf16[1024,256]{1,0:T(8,128)(2,1)S(1)}, u32[]{:S(2)}, u32[]{:S(2)}) collective-permute-start(bf16[1024,256]{1,0:T(8,128)(2,1)S(1)} %get-tuple-element.93), channel_id=1, source_target_pairs={{0,2},{1,3},{2,0},{3,1},{4,6},{5,7},{6,4},{7,5},{8,10},{9,11},{10,... | collective-permute-start | bytes 1572872 | tf_op jit(solution)/shard_map/ppermute | solution.py:483
  81.5 12.8 %collective-permute-start.26 = (bf16[512,256]{1,0:T(8,128)(2,1)S(1)}, bf16[512,256]{1,0:T(8,128)(2,1)S(1)}, u32[]{:S(2)}, u32[]{:S(2)}) collective-permute-start(bf16[512,256]{1,0:T(8,128)(2,1)S(1)} %shard_map.143.refs_2_.refs_1_), channel_id=1, source_target_pairs={{0,4},{4,0},{8,12},{12,8},{1,5},{5,1},{9,13},{13,9},{2,6},{6,2},{1... | collective-permute-start | bytes 786440 | tf_op jit(solution)/shard_map/ppermute | solution.py:483
  86.1 9.4 %collective-permute-start.27 = (bf16[512,256]{1,0:T(8,128)(2,1)S(1)}, bf16[512,256]{1,0:T(8,128)(2,1)S(1)}, u32[]{:S(2)}, u32[]{:S(2)}) collective-permute-start(bf16[512,256]{1,0:T(8,128)(2,1)S(1)} %shard_map.146.refs_2_), channel_id=1, source_target_pairs={{0,4},{4,0},{8,12},{12,8},{1,5},{5,1},{9,13},{13,9},{2,6},{6,2},{1... | collective-permute-start | bytes 786440 | tf_op jit(solution)/shard_map/ppermute | solution.py:483
